TPU v7x, 32 devices: a whole 2x2x4 slice. The times are simulated.
32 devices in a mesh: ctx: 16 (over z, y, x), head: 2 (over core).
Axes of the slice: x: 2, y: 2, z: 4, core: 2. Of those that a mesh axis runs over, the one named last changes fastest.
Arguments:
- queries: bfloat16 [512, 8192], P('ctx', 'head'), may hold values from -128 to 128
- fresh_span_keys: bfloat16 [512, 1024], P('ctx', 'head'), may hold values from -10 to 10
- fresh_span_values: bfloat16 [512, 1024], P('ctx', 'head'), may hold values from -6 to 6
- context_keys: bfloat16 [65536, 1024], P('ctx', 'head'), may hold values from -6 to 6
- context_values: bfloat16 [65536, 1024], P('ctx', 'head'), may hold values from -12 to 12
- selected: int32 [4, 12], replicated, may hold values from 0 to 15, as said below
- out_weight: bfloat16 [8192, 8192], P('head', 'ctx'), may hold values from -0.0625 to 0.0625
Outputs:
- attended: bfloat16 [512, 8192], P('head', 'ctx')
Inputs may be any that keep to these rules, and one draw needn't show every extreme that they name: `selected`: each row lists 12 different cache blocks, and every row lists the newest block, 15.
All inputs are finite; a program needn't handle non-finite values.
Results may differ from a plain program's by a relative error of at most 0.01345.
Values may be sent and summed in bfloat16 or wider, within the bound.
No kernel may reach another device: no remote copies, remote signals or barrier semaphores. Data moves between devices by JAX's collectives and lax.ppermute only.
A program may use at most 192 MiB of HBM per device.

v0:
```python
import jax
import jax.numpy as jnp
from jax import lax
from jax.sharding import PartitionSpec as P

HEAD_SIZE = 128
GROUP_QUERIES = 8
BLOCK_TOKENS = 4096
QUERY_BLOCK_SIZE = 128
SPAN_TOKENS = 512
BLK_DEV = 1
QUERY_BLOCKS = 4


NEG_FILL = -1e30


def attend_rows(query_matrix, key_matrix, value_rows, keep_mask, carry_state, score_scale):
    row_peak, row_total, row_acc = carry_state
    key_count = key_matrix.shape[0]
    piece_len = min(key_count, 1024)
    for key_start in range(0, key_count, piece_len):
        key_part = key_matrix[key_start : key_start + piece_len]
        value_part = value_rows[key_start : key_start + piece_len]
        scores = (
            jnp.einsum("rhge,khe->rhgk", query_matrix, key_part, preferred_element_type=jnp.float32)
            * score_scale
        )
        if keep_mask is not None:
            scores = jnp.where(
                keep_mask[:, None, None, key_start : key_start + piece_len], scores, NEG_FILL
            )
        new_peak = jnp.maximum(row_peak, jnp.max(scores, axis=-1))
        shrink = jnp.exp(row_peak - new_peak)
        weights = jnp.exp(scores - new_peak[..., None])
        row_total = row_total * shrink + jnp.sum(weights, axis=-1)
        row_acc = row_acc * shrink[..., None] + jnp.einsum(
            "rhgk,khe->rhge",
            weights.astype(jnp.bfloat16),
            value_part,
            preferred_element_type=jnp.float32,
        )
        row_peak = new_peak
    return (row_peak, row_total, row_acc)


def visit_blocks(query_all, key_matrix, value_rows, wanted, carry_state, score_scale):

    def visit_one(block_index, state_now):
        row_start = block_index * QUERY_BLOCK_SIZE
        query_matrix = lax.dynamic_slice_in_dim(query_all, row_start, QUERY_BLOCK_SIZE, 0)
        slice_part = tuple(
            (
                lax.dynamic_slice_in_dim(member, row_start, QUERY_BLOCK_SIZE, 0)
                for member in state_now
            )
        )

        def attend_part(part_now):
            return attend_rows(query_matrix, key_matrix, value_rows, None, part_now, score_scale)

        def keep_part(part_now):
            return part_now

        slice_part = lax.cond(wanted[block_index], attend_part, keep_part, slice_part)
        return tuple(
            (
                lax.dynamic_update_slice_in_dim(member, piece_now, row_start, 0)
                for member, piece_now in zip(state_now, slice_part)
            )
        )

    return lax.fori_loop(0, QUERY_BLOCKS, visit_one, carry_state)


def normalize_rows(numerator, denominator, flat_heads):
    row_count = numerator.shape[0]
    ratio = numerator.reshape(row_count, flat_heads, HEAD_SIZE) / denominator[..., None]
    return ratio.reshape(row_count, flat_heads * HEAD_SIZE).astype(jnp.bfloat16)


def local(
    queries, fresh_span_keys, fresh_span_values, context_keys, context_values, selected, out_weight
):
    ctx_count = lax.axis_size("ctx")
    my_index = lax.axis_index("ctx")
    kv_heads = context_keys.shape[1] // HEAD_SIZE
    own_rows = queries.shape[0]
    flat_heads = kv_heads * GROUP_QUERIES
    score_scale = HEAD_SIZE ** (-0.5)
    whole_q, whole_k, whole_v = (
        lax.all_gather(queries, "ctx", axis=0, tiled=True),
        lax.all_gather(fresh_span_keys, "ctx", axis=0, tiled=True),
        lax.all_gather(fresh_span_values, "ctx", axis=0, tiled=True),
    )
    query_all = whole_q.reshape(SPAN_TOKENS, kv_heads, GROUP_QUERIES, HEAD_SIZE)
    cache_k = context_keys.reshape(BLK_DEV, BLOCK_TOKENS, kv_heads, HEAD_SIZE)
    cache_v = context_values.reshape(BLK_DEV, BLOCK_TOKENS, kv_heads, HEAD_SIZE)
    carry_state = (
        jnp.full((SPAN_TOKENS, kv_heads, GROUP_QUERIES), NEG_FILL, jnp.float32),
        jnp.zeros((SPAN_TOKENS, kv_heads, GROUP_QUERIES), jnp.float32),
        jnp.zeros((SPAN_TOKENS, kv_heads, GROUP_QUERIES, HEAD_SIZE), jnp.float32),
    )
    block_id = my_index * BLK_DEV + 0
    wanted = jnp.any(selected == block_id, axis=1)
    carry_state = visit_blocks(query_all, cache_k[0], cache_v[0], wanted, carry_state, score_scale)
    my_start = my_index * own_rows
    own_q = queries.reshape(own_rows, kv_heads, GROUP_QUERIES, HEAD_SIZE)
    key_pos = jnp.arange(SPAN_TOKENS, dtype=jnp.int32)
    query_pos = my_start + jnp.arange(own_rows, dtype=jnp.int32)
    causal = key_pos[None, :] <= query_pos[:, None]
    own_state = tuple(
        (lax.dynamic_slice_in_dim(member, my_start, own_rows, 0) for member in carry_state)
    )
    own_state = attend_rows(
        own_q,
        whole_k.reshape(SPAN_TOKENS, kv_heads, HEAD_SIZE),
        whole_v.reshape(SPAN_TOKENS, kv_heads, HEAD_SIZE),
        causal,
        own_state,
        score_scale,
    )
    carry_state = tuple(
        (
            lax.dynamic_update_slice_in_dim(member, own_member, my_start, 0)
            for member, own_member in zip(carry_state, own_state)
        )
    )
    row_peak = carry_state[0].reshape(SPAN_TOKENS, flat_heads)
    row_total = carry_state[1].reshape(SPAN_TOKENS, flat_heads)
    row_acc = carry_state[2].reshape(SPAN_TOKENS, flat_heads * HEAD_SIZE)
    got_acc, got_peak, got_total = (
        lax.all_to_all(row_acc, "ctx", split_axis=0, concat_axis=0, tiled=True),
        lax.all_to_all(row_peak, "ctx", split_axis=0, concat_axis=0, tiled=True),
        lax.all_to_all(row_total, "ctx", split_axis=0, concat_axis=0, tiled=True),
    )
    got_peak = got_peak.reshape(ctx_count, own_rows, flat_heads)
    row_top = jnp.max(got_peak, axis=0)
    factor = jnp.exp(got_peak - row_top[None])
    numerator = jnp.sum(
        got_acc.reshape(ctx_count, own_rows, flat_heads, HEAD_SIZE) * factor[..., None], axis=0
    )
    denominator = jnp.sum(got_total.reshape(ctx_count, own_rows, flat_heads) * factor, axis=0)
    attention = normalize_rows(
        numerator.reshape(own_rows, flat_heads * HEAD_SIZE), denominator, flat_heads
    )
    partial_value = jnp.dot(
        lax.all_gather(attention, "ctx", axis=0, tiled=True),
        out_weight,
        preferred_element_type=jnp.float32,
    )
    attended = lax.psum_scatter(
        partial_value.astype(jnp.bfloat16), "head", scatter_dimension=0, tiled=True
    )
    return attended


def solution(mesh):
    return jax.shard_map(
        local,
        mesh=mesh,
        in_specs=(
            P("ctx", "head"),
            P("ctx", "head"),
            P("ctx", "head"),
            P("ctx", "head"),
            P("ctx", "head"),
            P(),
            P("head", "ctx"),
        ),
        out_specs=P("head", "ctx"),
        check_vma=False,
    )
```

profile of v0, /device:TPU:0, one launch (start us, length us, event | category | flops | bytes accessed | tf_op | source)
XLA Modules:
  0.0 854.1 jit_solution(2923158859703972734)
XLA Ops:
  6.5 0.7 all-gather.3.cloned.1.call-update
  7.3 6.5 copy.51
  13.7 6.4 copy.54
  20.1 6.6 copy.52
  26.7 6.4 copy.55
  33.1 49.7 %all_gather.14 = bf16[512,512]{1,0:T(8,128)(2,1)S(1)} all-gather(bf16[32,512]{1,0:T(8,128)(2,1)S(1)} %copy-done.7), channel_id=1, replica_groups=mesh['ctx'=16,'head'=2] {'ctx'}, dimensions={0}, use_global_device_ids=true | all-gather | bytes 557056 | tf_op jit(solution)/shard_map/all_gather | solution.py:94
  82.8 1.0 copy.61
  83.8 39.2 %all_gather.13 = bf16[512,512]{1,0:T(8,128)(2,1)S(1)} all-gather(bf16[32,512]{1,0:T(8,128)(2,1)S(1)} %copy-done.8), channel_id=1, replica_groups=mesh['ctx'=16,'head'=2] {'ctx'}, dimensions={0}, use_global_device_ids=true | all-gather | bytes 557056 | tf_op jit(solution)/shard_map/all_gather | solution.py:93
  123.5 2.4 fusion.72
  126.0 6.5 copy.50
  132.5 6.2 copy.53
  138.7 4.2 broadcast_in_dim.24
  142.9 209.6 %while.17 = (s32[]{:T(128)}, f32[512,4,8]{0,2,1:T(8,128)S(1)}, f32[512,4,8]{0,2,1:T(8,128)S(1)}, f32[512,4,8,128]{3,0,2,1:T(8,128)}, pred[4]{0:T(512)(128)(4,1)S...) while((s32[]{:T(128)}, f32[512,4,8]{0,2,1:T(8,128)S(1)}, ...), condition=%wide.region_12.0_spmd, body=%wide.region_1.0_spmd.sunk | while | flops 8728379392 | bytes 290293120 | solution.py:73
  157.1 3.1 constant_dynamic-slice_fusion.8
  160.2 3.1 constant_dynamic-update-slice_fusion.6
  164.6 3.1 constant_dynamic-slice_fusion.8
  167.8 83.2 %conditional.2 = ((f32[128,4,8]{0,2,1:T(8,128)S(1)}, f32[128,4,8]{0,2,1:T(8,128)S(1)}, f32[128,4,8,128]{3,0,2,1:T(8,128)})) conditional(s32[]{:T(128)} %bitcast.162, (f32[128,4,8]{0,2,1:T(8,128)S(1)}, f32[128,4,8]{0,2,1:T(8,128)S(1)}, f32[128,4,8,128]{3,0,2,1:T(8,128)}) %tuple.62, (bf16[512,4,8,128]{3,0,2,1:T(8,128)(2,1)}, s32[]{:T(128)}, ...), branch_computations={%region_2.0_spmd, %region_3.0_spmd} | conditional | flops 8728379392 | bytes 281772672 | solution.py:65
  167.8 9.7 %bitcast_reduce_fusion.1 = (f32[128,4,8]{0,2,1:T(8,128)S(1)}, f32[4,128,8,1024]{3,1,2,0:T(8,128)}) fusion(bf16[4096,4,128]{2,0,1:T(8,128)(2,1)} %get-tuple-element.173, bf16[512,4,8,128]{3,0,2,1:T(8,128)(2,1)} %get-tuple-element.171, s32[]{:T(128)} %get-tuple-element.172), kind=kOutput, calls=%fused_computation.4 | convolution fusion | flops 1082126336 | bytes 18891264 | tf_op jit(solution)/shard_map/while/body/eval_jaxpr/cond/branch_1_fun/rhge,khe->rhgk/dot_general | solution.py:26
  177.5 8.0 bitcast_reduce_fusion
  185.6 8.1 bitcast_reduce_fusion.2
  193.6 2.4 bitcast_reduce_fusion.3
  196.1 12.7 %fusion.9 = (f32[128,4,8]{0,2,1:T(8,128)S(1)}, f32[128,4,8]{0,2,1:T(8,128)S(1)}) fusion(f32[4,128,8,1024]{3,1,2,0:T(8,128)} %get-tuple-element.251, f32[128,4,8]{0,2,1:T(8,128)S(1)} %get-tuple-element.241, f32[128,4,8]{0,2,1:T(8,128)S(1)} %get-tuple-element.328, f32[4,128,8,1024]{3,1,2,0:T(8,128)} %get-tuple-element.249), kind=kLoop, calls=%fused_computation.17 | loop fusion | flops 25157632 | bytes 33619968 | tf_op jit(solution)/shard_map/while/body/eval_jaxpr/cond/branch_1_fun/reduce_sum | solution.py:36
  208.8 9.7 %fusion.5 = (f32[128,4,8]{0,2,1:T(8,128)S(1)}, f32[128,4,8]{0,2,1:T(8,128)S(1)}) fusion(f32[4,128,8,1024]{3,1,2,0:T(8,128)S(1)} %get-tuple-element.255, f32[128,4,8]{0,2,1:T(8,128)S(1)} %get-tuple-element.243, f32[128,4,8]{0,2,1:T(8,128)S(1)} %get-tuple-element.242, f32[4,128,8,1024]{3,1,2,0:T(8,128)} %get-tuple-element.253), kind=kLoop, calls=%fused_computation.13 | loop fusion | flops 25157632 | bytes 33619968 | tf_op jit(solution)/shard_map/while/body/eval_jaxpr/cond/branch_1_fun/reduce_sum | solution.py:36
  218.6 8.2 fusion.12
  226.8 8.2 fusion.14
  235.0 8.2 fusion.16
  243.3 7.7 bitcast_add_fusion
  251.0 3.1 constant_dynamic-update-slice_fusion.6
  255.4 3.1 constant_dynamic-slice_fusion.8
  258.6 83.2 %conditional.2 = ((f32[128,4,8]{0,2,1:T(8,128)S(1)}, f32[128,4,8]{0,2,1:T(8,128)S(1)}, f32[128,4,8,128]{3,0,2,1:T(8,128)})) conditional(s32[]{:T(128)} %bitcast.162, (f32[128,4,8]{0,2,1:T(8,128)S(1)}, f32[128,4,8]{0,2,1:T(8,128)S(1)}, f32[128,4,8,128]{3,0,2,1:T(8,128)}) %tuple.62, (bf16[512,4,8,128]{3,0,2,1:T(8,128)(2,1)}, s32[]{:T(128)}, ...), branch_computations={%region_2.0_spmd, %region_3.0_spmd} | conditional | flops 8728379392 | bytes 281772672 | solution.py:65
  258.6 9.7 %bitcast_reduce_fusion.1 = (f32[128,4,8]{0,2,1:T(8,128)S(1)}, f32[4,128,8,1024]{3,1,2,0:T(8,128)}) fusion(bf16[4096,4,128]{2,0,1:T(8,128)(2,1)} %get-tuple-element.173, bf16[512,4,8,128]{3,0,2,1:T(8,128)(2,1)} %get-tuple-element.171, s32[]{:T(128)} %get-tuple-element.172), kind=kOutput, calls=%fused_computation.4 | convolution fusion | flops 1082126336 | bytes 18891264 | tf_op jit(solution)/shard_map/while/body/eval_jaxpr/cond/branch_1_fun/rhge,khe->rhgk/dot_general | solution.py:26
  268.3 8.0 bitcast_reduce_fusion
  276.4 8.1 bitcast_reduce_fusion.2
  284.4 2.4 bitcast_reduce_fusion.3
  286.9 12.7 %fusion.9 = (f32[128,4,8]{0,2,1:T(8,128)S(1)}, f32[128,4,8]{0,2,1:T(8,128)S(1)}) fusion(f32[4,128,8,1024]{3,1,2,0:T(8,128)} %get-tuple-element.251, f32[128,4,8]{0,2,1:T(8,128)S(1)} %get-tuple-element.241, f32[128,4,8]{0,2,1:T(8,128)S(1)} %get-tuple-element.328, f32[4,128,8,1024]{3,1,2,0:T(8,128)} %get-tuple-element.249), kind=kLoop, calls=%fused_computation.17 | loop fusion | flops 25157632 | bytes 33619968 | tf_op jit(solution)/shard_map/while/body/eval_jaxpr/cond/branch_1_fun/reduce_sum | solution.py:36
  299.6 9.7 %fusion.5 = (f32[128,4,8]{0,2,1:T(8,128)S(1)}, f32[128,4,8]{0,2,1:T(8,128)S(1)}) fusion(f32[4,128,8,1024]{3,1,2,0:T(8,128)S(1)} %get-tuple-element.255, f32[128,4,8]{0,2,1:T(8,128)S(1)} %get-tuple-element.243, f32[128,4,8]{0,2,1:T(8,128)S(1)} %get-tuple-element.242, f32[4,128,8,1024]{3,1,2,0:T(8,128)} %get-tuple-element.253), kind=kLoop, calls=%fused_computation.13 | loop fusion | flops 25157632 | bytes 33619968 | tf_op jit(solution)/shard_map/while/body/eval_jaxpr/cond/branch_1_fun/reduce_sum | solution.py:36
  309.4 8.2 fusion.12
  317.6 8.2 fusion.14
  325.8 8.2 fusion.16
  334.1 7.7 bitcast_add_fusion
  341.8 3.1 constant_dynamic-update-slice_fusion.6
  346.2 3.1 constant_dynamic-slice_fusion.8
  349.4 3.1 constant_dynamic-update-slice_fusion.6
  352.5 11.6 %copy.56 = f32[512,4,8,128]{3,2,0,1:T(8,128)} copy(f32[512,4,8,128]{3,0,2,1:T(8,128)} %get-tuple-element.192) | data formatting | bytes 16777216 | tf_op jit(solution)/shard_map/while | solution.py:73
  365.4 0.8 reshape.91
  366.2 170.6 %all-to-all-start.1 = ((f32[16,1,1024]{2,1,0:T(1,128)}), f32[16,1,1024]{2,1,0:T(1,128)S(1)}, u32[]{:S(2)}, u32[]{:S(2)}) async-start(f32[16,1,1024]{2,1,0:T(1,128)} %reshape.91), calls=%async_computation.1 | async-start | bytes 131072 | tf_op jit(solution)/shard_map/all_to_all | solution.py:134
  536.8 1.8 fusion.67
  539.1 0.8 reshape.93
  539.9 4.4 all-to-all-done.1
  544.4 3.7 all-to-all-start.2
  548.1 0.9 copy_dynamic-update-slice_fusion
  549.0 11.4 %copy.65 = f32[512,4,8,128]{3,2,1,0:T(8,128)} copy(f32[512,4,8,128]{3,0,2,1:T(8,128)} %copy_dynamic-update-slice_fusion) | data formatting | bytes 16777216 | tf_op jit(solution)/shard_map/dynamic_update_slice | solution.py:125
  560.4 9.4 %all_to_all.18 = f32[16,32,4096]{2,1,0:T(8,128)} reshape(f32[512,4,8,128]{3,2,1,0:T(8,128)} %copy.65) | data formatting | bytes 16777216 | tf_op jit(solution)/shard_map/all_to_all | solution.py:133
  569.8 7.0 all-to-all-start
  577.4 0.8 reduce.2
  578.3 0.8 reduce.3
  579.5 4.6 mul.134
  584.1 9.4 %mul.135 = f32[16,32,4096]{2,1,0:T(8,128)} reshape(f32[16,32,32,128]{3,2,1,0:T(8,128)} %mul.134) | data formatting | bytes 16777216 | tf_op jit(solution)/shard_map/mul | solution.py:141
  593.5 123.4 %all-to-all-done = f32[16,32,4096]{2,1,0:T(8,128)} async-done(((f32[16,32,4096]{2,1,0:T(8,128)}), f32[16,32,4096]{2,1,0:T(8,128)}, u32[]{:S(2)}, u32[]{:S(2)}) %all-to-all-start) | async-done | bytes 8388640 | tf_op jit(solution)/shard_map/all_to_all | solution.py:133
  717.0 6.9 multiply_reduce_fusion
  724.0 1.0 fusion.69
  725.2 108.8 %all-gather.5.cloned.1.call-done = bf16[512,4096]{1,0:T(8,128)(2,1)} async-done(((bf16[32,4096]{1,0:T(8,128)(2,1)}), bf16[512,4096]{1,0:T(8,128)(2,1)}) %all-gather.5.cloned.1.call-update) | async-done | bytes 4194320 | tf_op jit(solution)/shard_map/all_gather | solution.py:148
  834.0 6.6 convolution_convert_fusion
  840.6 6.7 reduce-scatter.2.cloned.1.call-done
  (82 shorter events, 6.3 us)
Async XLA Ops:
  6.5 119.4 %all-gather.3.cloned.1.call-start = ((), (), s32[]{:S(2)}) async-start(), calls=%async_computation.4 | async-start | bytes 4456448 | tf_op jit(solution)/shard_map/all_gather | solution.py:92
  20.1 13.0 %copy-start.7 = (bf16[32,512]{1,0:T(8,128)(2,1)S(1)}, bf16[32,512]{1,0:T(8,128)(2,1)}, u32[]{:S(2)}) copy-start(bf16[32,512]{1,0:T(8,128)(2,1)} %param.13) | copy-start | bytes 98308
  20.1 63.7 %copy-start.8 = (bf16[32,512]{1,0:T(8,128)(2,1)S(1)}, bf16[32,512]{1,0:T(8,128)(2,1)}, u32[]{:S(2)}) copy-start(bf16[32,512]{1,0:T(8,128)(2,1)} %param.12) | copy-start | bytes 98308
  20.1 103.1 %copy-start.5 = (bf16[32,4096]{1,0:T(8,128)(2,1)S(1)}, bf16[32,4096]{1,0:T(8,128)(2,1)}, u32[]{:S(2)}) copy-start(bf16[32,4096]{1,0:T(8,128)(2,1)} %param.11) | copy-start | bytes 786436
  20.1 103.2 %copy-start.9 = (s32[4,12]{1,0:T(4,128)S(1)}, s32[4,12]{1,0:T(4,128)}, u32[]{:S(2)}) copy-start(s32[4,12]{1,0:T(4,128)} %param.16) | copy-start | bytes 580
  167.8 9.8 %copy-start = (bf16[4096,4,128]{2,0,1:T(8,128)(2,1)S(1)}, bf16[4096,4,128]{2,0,1:T(8,128)(2,1)}, u32[]{:S(2)}) copy-start(bf16[4096,4,128]{2,0,1:T(8,128)(2,1)} %get-tuple-element.173) | copy-start | bytes 12582916 | tf_op jit(solution)/shard_map/while/body/eval_jaxpr/cond
  167.8 9.8 %copy-start.1 = (bf16[512,4,8,128]{3,0,2,1:T(8,128)(2,1)S(1)}, bf16[512,4,8,128]{3,0,2,1:T(8,128)(2,1)}, u32[]{:S(2)}) copy-start(bf16[512,4,8,128]{3,0,2,1:T(8,128)(2,1)} %get-tuple-element.171) | copy-start | bytes 12582916 | tf_op jit(solution)/shard_map/while/body/eval_jaxpr/cond
  208.8 9.8 %copy-start.2 = (bf16[4096,4,128]{2,0,1:T(8,128)(2,1)S(1)}, bf16[4096,4,128]{2,0,1:T(8,128)(2,1)}, u32[]{:S(2)}) copy-start(bf16[4096,4,128]{2,0,1:T(8,128)(2,1)} %get-tuple-element.176) | copy-start | bytes 12582916 | tf_op jit(solution)/shard_map/while/body/eval_jaxpr/cond
  258.6 9.8 %copy-start = (bf16[4096,4,128]{2,0,1:T(8,128)(2,1)S(1)}, bf16[4096,4,128]{2,0,1:T(8,128)(2,1)}, u32[]{:S(2)}) copy-start(bf16[4096,4,128]{2,0,1:T(8,128)(2,1)} %get-tuple-element.173) | copy-start | bytes 12582916 | tf_op jit(solution)/shard_map/while/body/eval_jaxpr/cond
  258.6 9.8 %copy-start.1 = (bf16[512,4,8,128]{3,0,2,1:T(8,128)(2,1)S(1)}, bf16[512,4,8,128]{3,0,2,1:T(8,128)(2,1)}, u32[]{:S(2)}) copy-start(bf16[512,4,8,128]{3,0,2,1:T(8,128)(2,1)} %get-tuple-element.171) | copy-start | bytes 12582916 | tf_op jit(solution)/shard_map/while/body/eval_jaxpr/cond
  299.6 9.8 %copy-start.2 = (bf16[4096,4,128]{2,0,1:T(8,128)(2,1)S(1)}, bf16[4096,4,128]{2,0,1:T(8,128)(2,1)}, u32[]{:S(2)}) copy-start(bf16[4096,4,128]{2,0,1:T(8,128)(2,1)} %get-tuple-element.176) | copy-start | bytes 12582916 | tf_op jit(solution)/shard_map/while/body/eval_jaxpr/cond
  352.4 11.6 %copy-start.6 = (f32[32,4,8]{0,2,1:T(8,128)S(1)}, f32[32,4,8]{0,2,1:T(8,128)}, u32[]{:S(2)}) copy-start(f32[32,4,8]{0,2,1:T(8,128)} %get-tuple-element.264) | copy-start | bytes 12292
  352.5 11.7 %copy-start.3 = (f32[32,4,8,512]{3,0,2,1:T(8,128)S(1)}, f32[32,4,8,512]{3,0,2,1:T(8,128)}, u32[]{:S(2)}) copy-start(f32[32,4,8,512]{3,0,2,1:T(8,128)} %get-tuple-element.265) | copy-start | bytes 6291460
  352.5 184.4 %copy-start.4 = (bf16[512,512]{0,1:T(8,128)(2,1)S(1)}, bf16[512,512]{0,1:T(8,128)(2,1)}, u32[]{:S(2)}) copy-start(bf16[512,512]{0,1:T(8,128)(2,1)} %copy.61) | copy-start | bytes 1572868
  366.2 178.1 %all-to-all-start.1 = ((f32[16,1,1024]{2,1,0:T(1,128)}), f32[16,1,1024]{2,1,0:T(1,128)S(1)}, u32[]{:S(2)}, u32[]{:S(2)}) async-start(f32[16,1,1024]{2,1,0:T(1,128)} %reshape.91), calls=%async_computation.1 | async-start | bytes 131072 | tf_op jit(solution)/shard_map/all_to_all | solution.py:134
  544.4 25.5 %all-to-all-start.2 = ((f32[16,1,1024]{2,1,0:T(1,128)}), f32[16,1,1024]{2,1,0:T(1,128)S(1)}, u32[]{:S(2)}, u32[]{:S(2)}) async-start(f32[16,1,1024]{2,1,0:T(1,128)} %reshape.93), calls=%async_computation.2 | async-start | bytes 131072 | tf_op jit(solution)/shard_map/all_to_all | solution.py:135
  569.8 147.2 %all-to-all-start = ((f32[16,32,4096]{2,1,0:T(8,128)}), f32[16,32,4096]{2,1,0:T(8,128)}, u32[]{:S(2)}, u32[]{:S(2)}) async-start(f32[16,32,4096]{2,1,0:T(8,128)} %all_to_all.18), calls=%async_computation | async-start | bytes 16777216 | tf_op jit(solution)/shard_map/all_to_all | solution.py:133
  576.9 257.2 %all-gather.5.cloned.1.call-start = ((), (), s32[]{:S(2)}) async-start(), calls=%async_computation.5 | async-start | bytes 4456448 | tf_op jit(solution)/shard_map/all_gather | solution.py:148
  725.1 122.2 %reduce-scatter.2.cloned.1.call-start = ((), (), s32[]{:S(2)}) async-start(), calls=%async_computation.6 | async-start | bytes 786432 | tf_op jit(solution)/shard_map/reduce_scatter | solution.py:152
Sparse Core Ops, SparseCore 0:
  10.1 88.8 all-gather.2
  725.2 108.7 all-gather.4
  840.7 6.5 reduce-scatter.1
where the time goes:
time: 853 us; the launch traced here: 854 us
  waiting for transfers between devices  244 us (29%)
  starting transfers between devices  181 us (21%)
  matrix products  132 us (15%)
  local copies, waits for them, and re-layouts  123 us (14%)
  blocking collectives  88.9 us (10%)
  other arithmetic  55.5 us (7%)
  loops' own time  15.7 us (2%)
  between operations  13.6 us (2%)
    all_to_all x1, starting transfers between devices, local(): lax.all_to_all(row_peak, 'ctx', split_axis=0, concat_axis=0, tiled=True)  171 us
    all_to_all x1, waiting for transfers between devices, local(): lax.all_to_all(row_acc, 'ctx', split_axis=0, concat_axis=0, tiled=True)  123 us
    all_gather x1, waiting for transfers between devices, local(): lax.all_gather(attention, 'ctx', axis=0, tiled=True)  109 us
    dot_general x9, matrix products, attend_rows(): jnp.einsum('rhgk,khe->rhge', weights.astype(jnp.bfloat16), value_part, pr...  66.6 us
    dot_general x9, matrix products, attend_rows(): jnp.einsum('rhge,khe->rhgk', query_matrix, key_part, preferred_element_ty...  59 us
    all_gather x1, blocking collectives, local(): lax.all_gather(fresh_span_values, 'ctx', axis=0, tiled=True)  49.7 us
    reduce_sum x5, other arithmetic, attend_rows(): row_total = row_total * shrink + jnp.sum(weights, axis=-1)  45.5 us
    all_gather x1, blocking collectives, local(): lax.all_gather(fresh_span_keys, 'ctx', axis=0, tiled=True)  39.2 us
  transfers between devices with their start and end apart: 6, of which 4 were waited for; matrix products, arithmetic and copies ran while one was open for 7% of the time, Pallas kernels for 0%

commit v1 on v0

v1 whole, which is shorter than its diff:
```python
import functools

import jax
import jax.numpy as jnp
import numpy as np
from jax import lax
from jax.experimental import pallas as pl
from jax.experimental.pallas import tpu as pltpu
from jax.sharding import PartitionSpec as P

HEAD_SIZE = 128
GROUP_QUERIES = 8
LANES = 128
LOG2_SCALE = float(HEAD_SIZE**-0.5 * np.log2(np.e))
MASKED = -1e30
LOWEST = -1e20
VMEM_LIMIT = 56 * 1024 * 1024

BF16, F32 = jnp.bfloat16, jnp.float32


def fold_lanes(op, x):
    parts = [x[:, i : i + LANES] for i in range(0, x.shape[1], LANES)]
    while len(parts) > 1:
        parts = [op(*parts[i : i + 2]) if i + 1 < len(parts) else parts[i] for i in range(0, len(parts), 2)]
    return parts[0]


def attend_kernel(
    info, *refs, plane, blocks, rows, group_step, key_chunk, waits
):
    q_refs, refs = refs[:plane], refs[plane:]
    k_ref, v_ref, ks_ref, vs_ref = refs[:4]
    refs = refs[4 + waits :]
    o_refs, refs = refs[:plane], refs[plane:]
    score_ref, peak_ref, aux_ref, pos_ref, ks_pad, vs_pad = refs
    me, my_plane, wanted = info[0], info[1], info[2]
    keys = k_ref.shape[0]
    block_rows = plane * rows
    tile_rows = group_step * block_rows
    steps = GROUP_QUERIES // group_step
    chunks = keys // key_chunk

    ks_pad[...] = jnp.zeros_like(ks_pad)
    vs_pad[...] = jnp.zeros_like(vs_pad)
    ks_pad[0:rows, :] = ks_ref[...]
    vs_pad[0:rows, :] = vs_ref[...]
    row = lax.broadcasted_iota(jnp.int32, (tile_rows, LANES), 0)
    col = lax.broadcasted_iota(jnp.int32, (tile_rows, LANES), 1)
    piece = lax.rem(lax.div(row, rows), plane)
    pos_ref[...] = jnp.where(
        col < rows, (piece ^ my_plane) * rows + lax.rem(row, rows) - me * rows - col, -(1 << 30)
    )
    lane = lax.broadcasted_iota(jnp.int32, (block_rows, LANES), 1)

    def place(tile):
        return info[3 + lax.div(tile, steps)], lax.rem(tile, steps) * group_step

    def load_queries(tile):
        slot, group = place(tile)
        parts = []
        for i in range(group_step):
            cols = pl.ds(pl.multiple_of((group + i) * HEAD_SIZE, HEAD_SIZE), HEAD_SIZE)
            parts += [q[slot, :, cols] for q in q_refs]
        return jnp.concatenate(parts, axis=0)

    def dot_keys(q, k):
        return lax.dot_general(q, k, (((1,), (1,)), ((), ())), preferred_element_type=F32)

    def span_scores(q, tile):
        slot, _ = place(tile)
        start = info[3 + blocks + slot] * block_rows
        return jnp.where(pos_ref[...] + start >= 0, dot_keys(q, ks_pad[...]), MASKED)

    def shift_of(peak):
        top = jnp.max(peak, axis=1, keepdims=True) * LOG2_SCALE
        return jnp.maximum(top, LOWEST).astype(BF16).astype(F32)

    def finish(tile, shift, total, acc):
        slot, group = place(tile)
        total = jnp.sum(total, axis=1, keepdims=True)
        high = total.astype(BF16).astype(F32)
        low = total - high
        aux = jnp.where(group == 0, 0.0, aux_ref[...])
        for i in range(group_step):
            cols = pl.ds(pl.multiple_of((group + i) * HEAD_SIZE, HEAD_SIZE), HEAD_SIZE)
            part = slice(i * block_rows, (i + 1) * block_rows)
            aux = jnp.where(lane == group + i, shift[part], aux)
            aux = jnp.where(lane == group + i + GROUP_QUERIES, high[part], aux)
            aux = jnp.where(lane == group + i + 2 * GROUP_QUERIES, low[part], aux)
            for b, o in enumerate(o_refs):
                start = i * block_rows + b * rows
                o[slot, :, cols] = acc[start : start + rows].astype(BF16)
        aux_ref[...] = aux
        for b, o in enumerate(o_refs):
            o[slot, :, GROUP_QUERIES * HEAD_SIZE :] = aux[b * rows : (b + 1) * rows].astype(BF16)

    def step(now, later):
        if now is not None:
            here = lax.rem(now, 2)
            shift = peak_ref[here][:, 0:1]
            wide_shift = jnp.broadcast_to(shift, (tile_rows, LANES))
            weights = jnp.exp2(score_ref[here, :, keys:] * LOG2_SCALE - wide_shift)
            total = weights
            acc = jnp.dot(weights.astype(BF16), vs_pad[...], preferred_element_type=F32)
        if later is not None:
            there = lax.rem(later, 2)
            q = load_queries(later)
            scores = span_scores(q, later)
            score_ref[there, :, keys:] = scores
            peak = scores
        for j in range(chunks):
            part = slice(j * key_chunk, (j + 1) * key_chunk)
            if later is not None:
                scores = dot_keys(q, k_ref[part])
                score_ref[there, :, part] = scores
                peak = jnp.maximum(peak, fold_lanes(jnp.maximum, scores))
            if now is not None:
                weights = jnp.exp2(score_ref[here, :, part] * LOG2_SCALE - shift)
                total = total + fold_lanes(jnp.add, weights)
                acc = acc + jnp.dot(weights.astype(BF16), v_ref[part], preferred_element_type=F32)
        if later is not None:
            peak_ref[there] = jnp.broadcast_to(shift_of(peak), (tile_rows, LANES))
        if now is not None:
            finish(now, shift, total, acc)

    count = wanted * steps

    @pl.when(count > 0)
    def _():
        step(None, jnp.int32(0))

        def body(t, _):
            step(t, t + 1)
            return 0

        lax.fori_loop(0, count - 1, body, 0)
        step(count - 1, None)

    def span_only(t, _):
        scores = span_scores(load_queries(t), t)
        shift = shift_of(scores)
        weights = jnp.exp2(scores * LOG2_SCALE - shift)
        acc = jnp.dot(weights.astype(BF16), vs_pad[...], preferred_element_type=F32)
        finish(t, shift, weights, acc)
        return 0

    lax.fori_loop(count, blocks * steps, span_only, 0)


def attend_head(info, q_pieces, keys, values, span_keys, span_values, head, after):
    plane = len(q_pieces)
    blocks, rows, cols = q_pieces[0].shape
    key_count = keys.shape[0]
    group_step = 2
    tile_rows = group_step * plane * rows
    out_cols = cols + LANES
    vmem = pltpu.MemorySpace.VMEM
    whole = pl.BlockSpec((blocks, rows, cols), lambda i, s: (0, 0, 0))
    whole_out = pl.BlockSpec((blocks, rows, out_cols), lambda i, s: (0, 0, 0))
    head_block = pl.BlockSpec((key_count, HEAD_SIZE), lambda i, s: (0, head))
    span_block = pl.BlockSpec((rows, HEAD_SIZE), lambda i, s: (0, head))
    scored = blocks * plane * rows * GROUP_QUERIES * key_count
    return pl.pallas_call(
        functools.partial(
            attend_kernel,
            plane=plane,
            blocks=blocks,
            rows=rows,
            group_step=group_step,
            key_chunk=min(key_count, 512),
            waits=len(after),
        ),
        grid_spec=pltpu.PrefetchScalarGridSpec(
            num_scalar_prefetch=1,
            grid=(1,),
            in_specs=[whole] * plane
            + [head_block, head_block, span_block, span_block]
            + [pl.BlockSpec(memory_space=pl.ANY)] * len(after),
            out_specs=[whole_out] * plane,
            scratch_shapes=[
                vmem((2, tile_rows, key_count + LANES), F32),
                vmem((2, tile_rows, LANES), F32),
                vmem((plane * rows, LANES), F32),
                vmem((tile_rows, LANES), jnp.int32),
                vmem((LANES, HEAD_SIZE), BF16),
                vmem((LANES, HEAD_SIZE), BF16),
            ],
        ),
        out_shape=[jax.ShapeDtypeStruct((blocks, rows, out_cols), BF16)] * plane,
        compiler_params=pltpu.CompilerParams(vmem_limit_bytes=VMEM_LIMIT),
        cost_estimate=pl.CostEstimate(
            flops=8 * scored * HEAD_SIZE,
            bytes_accessed=4 * key_count * HEAD_SIZE + 4 * blocks * plane * rows * cols,
            transcendentals=scored,
        ),
        name="attend",
    )(info, *q_pieces, keys, values, span_keys, span_values, *after)


def combine(parts):
    width = GROUP_QUERIES * HEAD_SIZE
    aux = [p[:, width:].astype(F32) for p in parts]
    top = functools.reduce(jnp.maximum, aux)
    factors = [jnp.exp2(jnp.minimum(a - top, 0.0)) for a in aux]
    sums = [
        pltpu.roll(a, LANES - GROUP_QUERIES, 1) + pltpu.roll(a, LANES - 2 * GROUP_QUERIES, 1) for a in aux
    ]
    total = sum(f * s for f, s in zip(factors, sums))
    heads = []
    for g in range(GROUP_QUERIES):
        cols = slice(g * HEAD_SIZE, (g + 1) * HEAD_SIZE)
        heads.append(sum(f[:, g : g + 1] * p[:, cols].astype(F32) for f, p in zip(factors, parts)))
    return heads, top, total


def merge_kernel(*refs, count, waits):
    ins, outs = refs[:count], refs[count + waits :]
    for a, out in enumerate(outs):
        heads, top, total = combine([p[a] for p in ins])
        for g, x in enumerate(heads):
            out[:, g * HEAD_SIZE : (g + 1) * HEAD_SIZE] = x.astype(BF16)
        lane = lax.broadcasted_iota(jnp.int32, top.shape, 1)
        high = total.astype(BF16).astype(F32)
        aux = jnp.where(
            lane < GROUP_QUERIES,
            top,
            jnp.where(
                lane < 2 * GROUP_QUERIES,
                pltpu.roll(high, GROUP_QUERIES, 1),
                pltpu.roll(total - high, 2 * GROUP_QUERIES, 1),
            ),
        )
        aux = jnp.where(lane < 3 * GROUP_QUERIES, aux, 0.0)
        out[:, GROUP_QUERIES * HEAD_SIZE :] = aux.astype(BF16)


def normalize_kernel(*refs, count):
    ins, out = refs[:count], refs[-1]
    heads, _, total = combine([p[...] for p in ins])
    for g, x in enumerate(heads):
        out[:, g * HEAD_SIZE : (g + 1) * HEAD_SIZE] = (x / total[:, g : g + 1]).astype(BF16)


def waiting_specs(pieces, after):
    whole = pl.BlockSpec(memory_space=pltpu.MemorySpace.VMEM)
    return [whole] * len(pieces) + [pl.BlockSpec(memory_space=pl.ANY)] * len(after)


def merge_pieces(pieces, after):
    blocks, rows, cols = pieces[0].shape
    size = blocks * rows * cols
    return pl.pallas_call(
        functools.partial(merge_kernel, count=len(pieces), waits=len(after)),
        in_specs=waiting_specs(pieces, after),
        out_shape=[jax.ShapeDtypeStruct((rows, cols), BF16)] * blocks,
        compiler_params=pltpu.CompilerParams(vmem_limit_bytes=VMEM_LIMIT),
        cost_estimate=pl.CostEstimate(
            flops=2 * size * len(pieces), bytes_accessed=2 * size * (len(pieces) + 1), transcendentals=0
        ),
        name="merge",
    )(*pieces, *after)


def normalize_pieces(pieces, after):
    rows, cols = pieces[0].shape
    size = rows * cols
    return pl.pallas_call(
        functools.partial(normalize_kernel, count=len(pieces)),
        in_specs=waiting_specs(pieces, after),
        out_shape=jax.ShapeDtypeStruct((rows, cols - LANES), BF16),
        compiler_params=pltpu.CompilerParams(vmem_limit_bytes=VMEM_LIMIT),
        cost_estimate=pl.CostEstimate(
            flops=2 * size * len(pieces), bytes_accessed=2 * size * (len(pieces) + 1), transcendentals=0
        ),
        name="normalize",
    )(*pieces, *after)


def project_kernel(info, *refs, plane, blocks, rows, heads):
    ins, w_ref, out = refs[: plane * heads], refs[-2], refs[-1]
    width = GROUP_QUERIES * HEAD_SIZE
    for b in range(plane):
        acc = None
        for h in range(heads):
            x = ins[h * plane + b][...].reshape(blocks * rows, width)
            y = jnp.dot(x, w_ref[h * width : (h + 1) * width], preferred_element_type=F32)
            acc = y if acc is None else acc + y
        for a in range(blocks):
            out[info[3 + blocks + a], b ^ info[1]] = acc[a * rows : (a + 1) * rows].astype(BF16)


def project(info, gathered, weight):
    heads, plane = len(gathered), len(gathered[0])
    blocks, rows, _ = gathered[0][0].shape
    vmem = pltpu.MemorySpace.VMEM
    span = plane * blocks * rows
    return pl.pallas_call(
        functools.partial(project_kernel, plane=plane, blocks=blocks, rows=rows, heads=heads),
        in_specs=[pl.BlockSpec(memory_space=pltpu.MemorySpace.SMEM)]
        + [pl.BlockSpec(memory_space=vmem)] * (heads * plane + 1),
        out_shape=jax.ShapeDtypeStruct((blocks, plane, rows, weight.shape[1]), BF16),
        compiler_params=pltpu.CompilerParams(vmem_limit_bytes=VMEM_LIMIT),
        cost_estimate=pl.CostEstimate(
            flops=2 * span * weight.size, bytes_accessed=2 * (weight.size + span * weight.shape[0]), transcendentals=0
        ),
        name="project",
    )(info, *[x for per_head in gathered for x in per_head], weight)


def exchange(x, axis, distance):
    count = lax.axis_size(axis)
    return lax.ppermute(x, axis, [(i, i ^ distance) for i in range(count)])


def local(queries, span_keys, span_values, context_keys, context_values, selected, out_weight):
    ctx_count, me = lax.axis_size("ctx"), lax.axis_index("ctx")
    head_count, my_head = lax.axis_size("head"), lax.axis_index("head")
    blocks = selected.shape[0]
    plane = ctx_count // blocks
    rows = queries.shape[0]
    heads = context_keys.shape[1] // HEAD_SIZE
    width = GROUP_QUERIES * HEAD_SIZE

    slot_block = lax.div(me, plane) ^ jnp.arange(blocks, dtype=jnp.int32)
    wanted = jnp.any(selected == me, axis=1)[slot_block]
    order = jnp.argsort(jnp.logical_not(wanted), stable=True).astype(jnp.int32)
    info = jnp.concatenate(
        [
            jnp.stack([me, lax.rem(me, plane), jnp.sum(wanted)]).astype(jnp.int32),
            order,
            slot_block.astype(jnp.int32),
        ]
    )

    def stack_blocks(x):
        return jnp.stack([x] + [exchange(x, "ctx", a * plane) for a in range(1, blocks)])

    def gather_plane(stack):
        return [stack] + [exchange(stack, "ctx", b) for b in range(1, plane)]

    def head_queries(h):
        return queries[:, h * width : (h + 1) * width]

    first = stack_blocks(head_queries(0))
    stacks, pieces = [first], [gather_plane(first)]
    for h in range(1, heads):
        held, _ = lax.optimization_barrier((head_queries(h), stacks[h - 1]))
        stacks.append(stack_blocks(held))
    for h in range(1, heads):
        pieces.append(gather_plane(stacks[h]))

    attended, merged, rows_of = [], [], []

    def merge(h, after):
        own = attended[h]
        parts = [own[0]] + [exchange(own[b], "ctx", b) for b in range(1, plane)]
        merged.append(merge_pieces(parts, after))

    def normalize(h, after):
        own = merged[h]
        parts = [own[0]] + [exchange(own[a], "ctx", a * plane) for a in range(1, blocks)]
        rows_of.append(normalize_pieces(parts, after))

    for h in range(heads):
        after = stacks[1:] if h == 0 else []
        if h >= 3:
            normalize(h - 3, [attended[h - 1][0]])
            after.append(rows_of[h - 3])
        if h >= 2:
            merge(h - 2, [attended[h - 1][0]])
            after.append(merged[h - 2][0])
        attended.append(
            attend_head(info, pieces[h], context_keys, context_values, span_keys, span_values, h, after)
        )
    last = [attended[-1][0]]
    for h in range(heads):
        if h >= len(merged):
            merge(h, last)
        if h >= len(rows_of):
            normalize(h, last)
    gathered = [gather_plane(stack_blocks(r)) for r in rows_of]

    partial_out = project(info, gathered, out_weight).reshape(ctx_count * rows, -1)
    share = partial_out.shape[0] // head_count
    total = lax.dynamic_slice_in_dim(partial_out, my_head * share, share, 0).astype(F32)
    for d in range(1, head_count):
        other = lax.dynamic_slice_in_dim(partial_out, (my_head ^ d) * share, share, 0)
        total = total + exchange(other, "head", d).astype(F32)
    return total.astype(BF16)


def solution(mesh):
    return jax.shard_map(
        local,
        mesh=mesh,
        in_specs=(
            P("ctx", "head"),
            P("ctx", "head"),
            P("ctx", "head"),
            P("ctx", "head"),
            P("ctx", "head"),
            P(),
            P("head", "ctx"),
        ),
        out_specs=P("head", "ctx"),
        check_vma=False,
    )
```

time: 853 us -> 393 us (0.46)
  waiting for transfers between devices: 244 us -> 33.4 us
  Pallas kernels: 0 us -> 156 us
  matrix products: 132 us -> 0 us
  local copies, waits for them, and re-layouts: 123 us -> 4.82 us
  blocking collectives: 88.9 us -> 0 us
  other arithmetic: 55.5 us -> 7.51 us
  loops' own time: 15.7 us -> 0 us
  between operations: 13.6 us -> 0.62 us
  starting transfers between devices: 181 us -> 190 us
    ppermute x0 -> x73, starting transfers between devices: none -> 190 us  [exchange(): return lax.ppermute(x, axis, [(i, i ^ distance) for i in range(count)])]
    all_to_all x3 -> x0, starting transfers between devices: 181 us -> none  [the longest x1 171 us: local(): lax.all_to_all(row_peak, 'ctx', split_axis=0, concat_axis=0, tiled=True)]
    pallas_call x0 -> x13, Pallas kernels: none -> 156 us  [the longest x4 131 us: attend_head(): pl.pallas_call(functools.partial(attend_kernel, plane=plane, blocks=block...]
    dot_general x19 -> x0, matrix products: 132 us -> none  [the longest x9 66.6 us: attend_rows(): jnp.einsum('rhgk,khe->rhge', weights.astype(jnp.bfloat16), value_part, pr...]
    all_to_all x3 -> x0, waiting for transfers between devices: 128 us -> none  [the longest x1 123 us: local(): lax.all_to_all(row_acc, 'ctx', split_axis=0, concat_axis=0, tiled=True)]
    all_gather x2 -> x0, waiting for transfers between devices: 109 us -> none  [the longest x1 109 us: local(): lax.all_gather(attention, 'ctx', axis=0, tiled=True)]
    all_gather x2 -> x0, blocking collectives: 88.9 us -> none  [the longest x1 49.7 us: local(): lax.all_gather(fresh_span_values, 'ctx', axis=0, tiled=True)]
    reduce_sum x7 -> x1, other arithmetic: 52.4 us -> 0.66 us  [local(): jnp.sum(wanted)]
  transfers between devices with their start and end apart: 6 -> 73, of which waited for: 4 -> 17; matrix products, arithmetic and copies ran while one was open for 7% -> 2% of each run, Pallas kernels for 0% -> 38%
where the time goes in v1:
time: 393 us
  starting transfers between devices  190 us (48%)
  Pallas kernels  156 us (40%)
  waiting for transfers between devices  33.4 us (8%)
  other arithmetic  7.51 us (2%)
  local copies, waits for them, and re-layouts  4.82 us (1%)
    ppermute x73, starting transfers between devices, exchange(): return lax.ppermute(x, axis, [(i, i ^ distance) for i in range(count)])  190 us
    pallas_call x4, Pallas kernels, attend_head(): pl.pallas_call(functools.partial(attend_kernel, plane=plane, blocks=block...  131 us
    ppermute x73, waiting for transfers between devices, exchange(): return lax.ppermute(x, axis, [(i, i ^ distance) for i in range(count)])  33.4 us
    pallas_call x4, Pallas kernels, merge_pieces(): pl.pallas_call(functools.partial(merge_kernel, count=len(pieces), waits=l...  11 us
  transfers between devices with their start and end apart: 73, of which 17 were waited for; matrix products, arithmetic and copies ran while one was open for 2% of the time, Pallas kernels for 38%

profile of v1, /device:TPU:0, one launch (start us, length us, event | category | flops | bytes accessed | tf_op | source)
XLA Modules:
  0.0 393.0 jit_solution(8904925987879160098)
XLA Ops:
  1.0 3.1 collective-permute-start
  4.1 2.6 collective-permute-start.1
  6.7 4.7 %collective-permute-done.1 = bf16[32,1024]{1,0:T(8,128)(2,1)S(1)} collective-permute-done((bf16[32,1024]{1,0:T(8,128)(2,1)S(1)}, bf16[32,1024]{1,0:T(8,128)(2,1)S(1)}, u32[]{:S(2)}, u32[]{:S(2)}) %collective-permute-start.1) | collective-permute-done | bytes 65568 | tf_op jit(solution)/shard_map/ppermute | solution.py:313
  12.8 1.6 collective-permute-start.7
  16.3 2.4 collective-permute-done.7
  18.8 1.7 collective-permute-done.8
  20.7 2.5 collective-permute-start.10
  23.2 1.8 collective-permute-start.11
  26.4 1.5 collective-permute-start.3
  27.9 1.5 collective-permute-start.4
  31.6 2.6 collective-permute-start.13
  34.5 2.5 collective-permute-start.14
  38.3 1.5 collective-permute-start.18
  40.6 1.5 collective-permute-start.19
  44.8 1.5 collective-permute-start.25
  46.4 32.6 %attend.4 = (bf16[4,32,1152]{2,1,0:T(8,128)(2,1)}, bf16[4,32,1152]{2,1,0:T(8,128)(2,1)}, bf16[4,32,1152]{2,1,0:T(8,128)(2,1)}, bf16[4,32,1152]{2,1,0:T(8,128)(2,1)}) custom-call(s32[11]{0:T(128)} %concatenate.3.info, bf16[4,32,1024]{2,1,0:T(8,128)(2,1)} %copy-done.29, bf16[4,32,1024]{2,1,0:T(8,128)(2,1)} %copy-done.45, bf16[4,32,1024]{2,1,0:T(8,128)(2,1)} %copy-done.46, ...), custom_call_target="tpu_custom_call" | custom-call | flops 17179869184 | bytes 4194304 | tf_op jit(solution)/shard_map/attend/pallas_call | solution.py:164
  79.0 25.5 %collective-permute-start.15 = (bf16[4,32,1152]{2,1,0:T(8,128)(2,1)}, bf16[4,32,1152]{2,1,0:T(8,128)(2,1)S(1)}, u32[]{:S(2)}, u32[]{:S(2)}) collective-permute-start(bf16[4,32,1152]{2,1,0:T(8,128)(2,1)} %get-tuple-element.46), channel_id=1, source_target_pairs={{0,2},{2,0},{4,6},{6,4},{8,10},{10,8},{12,14},{14,12},{16,18},{18,... | collective-permute-start | bytes 884744 | tf_op jit(solution)/shard_map/ppermute | solution.py:313
  104.5 1.6 collective-permute-start.17
  106.1 32.8 %attend.5 = (bf16[4,32,1152]{2,1,0:T(8,128)(2,1)}, bf16[4,32,1152]{2,1,0:T(8,128)(2,1)}, bf16[4,32,1152]{2,1,0:T(8,128)(2,1)}, bf16[4,32,1152]{2,1,0:T(8,128)(2,1)}) custom-call(s32[11]{0:T(128)} %concatenate.3.info, bf16[4,32,1024]{2,1,0:T(8,128)(2,1)} %copy-done.28, bf16[4,32,1024]{2,1,0:T(8,128)(2,1)} %copy-done.52, bf16[4,32,1024]{2,1,0:T(8,128)(2,1)} %copy-done.53, ...), custom_call_target="tpu_custom_call" | custom-call | flops 17179869184 | bytes 4194304 | tf_op jit(solution)/shard_map/attend/pallas_call | solution.py:164
  138.9 25.9 %collective-permute-start.33 = (bf16[4,32,1152]{2,1,0:T(8,128)(2,1)}, bf16[4,32,1152]{2,1,0:T(8,128)(2,1)S(1)}, u32[]{:S(2)}, u32[]{:S(2)}) collective-permute-start(bf16[4,32,1152]{2,1,0:T(8,128)(2,1)} %get-tuple-element.55), channel_id=1, source_target_pairs={{0,2},{2,0},{4,6},{6,4},{8,10},{10,8},{12,14},{14,12},{16,18},{18,... | collective-permute-start | bytes 884744 | tf_op jit(solution)/shard_map/ppermute | solution.py:313
  165.6 2.8 merge.4
  168.4 3.2 collective-permute-start.22
  172.8 5.4 %collective-permute-done.26.refs_3_ = bf16[4,32,1024]{2,1,0:T(8,128)(2,1)S(1)} collective-permute-done((bf16[4,32,1024]{2,1,0:T(8,128)(2,1)S(1)}, bf16[4,32,1024]{2,1,0:T(8,128)(2,1)S(1)}, u32[]{:S(2)}, u32[]{:S(2)}) %collective-permute-start.26) | collective-permute-done | bytes 262176 | tf_op jit(solution)/shard_map/ppermute | solution.py:313
  178.2 4.0 %collective-permute-start.40 = (bf16[4,32,1024]{2,1,0:T(8,128)(2,1)S(1)}, bf16[4,32,1024]{2,1,0:T(8,128)(2,1)S(1)}, u32[]{:S(2)}, u32[]{:S(2)}) collective-permute-start(bf16[4,32,1024]{2,1,0:T(8,128)(2,1)S(1)} %copy-done.25), channel_id=1, source_target_pairs={{0,4},{2,6},{4,0},{6,2},{8,12},{10,14},{12,8},{14,10},{16,20},{18,... | collective-permute-start | bytes 786440 | tf_op jit(solution)/shard_map/ppermute | solution.py:313
  182.2 1.5 collective-permute-start.34
  183.7 1.5 collective-permute-start.35
  185.2 32.6 %attend.6 = (bf16[4,32,1152]{2,1,0:T(8,128)(2,1)}, bf16[4,32,1152]{2,1,0:T(8,128)(2,1)}, bf16[4,32,1152]{2,1,0:T(8,128)(2,1)}, bf16[4,32,1152]{2,1,0:T(8,128)(2,1)}) custom-call(s32[11]{0:T(128)} %concatenate.3.info, bf16[4,32,1024]{2,1,0:T(8,128)(2,1)} %copy-done.26, bf16[4,32,1024]{2,1,0:T(8,128)(2,1)} %copy-done.43, bf16[4,32,1024]{2,1,0:T(8,128)(2,1)} %copy-done.44, ...), custom_call_target="tpu_custom_call" | custom-call | flops 17179869184 | bytes 4194304 | tf_op jit(solution)/shard_map/attend/pallas_call | solution.py:164
  217.8 1.9 normalize.4.refs_8_
  219.7 10.2 %collective-permute-start.27 = (bf16[32,1024]{1,0:T(8,128)(2,1)}, bf16[32,1024]{1,0:T(8,128)(2,1)S(1)}, u32[]{:S(2)}, u32[]{:S(2)}) collective-permute-start(bf16[32,1024]{1,0:T(8,128)(2,1)} %normalize.4.refs_8_), channel_id=1, source_target_pairs={{0,8},{2,10},{4,12},{6,14},{8,0},{10,2},{12,4},{14,6},{16,24},{18,... | collective-permute-start | bytes 196616 | tf_op jit(solution)/shard_map/ppermute | solution.py:313
  229.9 14.4 %collective-permute-start.48 = (bf16[4,32,1152]{2,1,0:T(8,128)(2,1)}, bf16[4,32,1152]{2,1,0:T(8,128)(2,1)S(1)}, u32[]{:S(2)}, u32[]{:S(2)}) collective-permute-start(bf16[4,32,1152]{2,1,0:T(8,128)(2,1)} %get-tuple-element.63), channel_id=1, source_target_pairs={{0,2},{2,0},{4,6},{6,4},{8,10},{10,8},{12,14},{14,12},{16,18},{18,... | collective-permute-start | bytes 884744 | tf_op jit(solution)/shard_map/ppermute | solution.py:313
  244.3 2.8 merge.5
  247.2 2.2 collective-permute-start.50
  249.3 1.9 collective-permute-start.36
  252.4 33.2 %attend.7 = (bf16[4,32,1152]{2,1,0:T(8,128)(2,1)}, bf16[4,32,1152]{2,1,0:T(8,128)(2,1)}, bf16[4,32,1152]{2,1,0:T(8,128)(2,1)}, bf16[4,32,1152]{2,1,0:T(8,128)(2,1)}) custom-call(s32[11]{0:T(128)} %concatenate.3.info, bf16[4,32,1024]{2,1,0:T(8,128)(2,1)} %pad_maximum_fusion.3.refs_10_.refs_0_, bf16[4,32,1024]{2,1,0:T(8,128)(2,1)} %copy-done.47, ...), custom_call_target="tpu_custom_call" | custom-call | flops 17179869184 | bytes 4194304 | tf_op jit(solution)/shard_map/attend/pallas_call | solution.py:164
  285.6 25.2 %collective-permute-start.60 = (bf16[4,32,1152]{2,1,0:T(8,128)(2,1)}, bf16[4,32,1152]{2,1,0:T(8,128)(2,1)S(1)}, u32[]{:S(2)}, u32[]{:S(2)}) collective-permute-start(bf16[4,32,1152]{2,1,0:T(8,128)(2,1)} %get-tuple-element.70), channel_id=1, source_target_pairs={{0,2},{2,0},{4,6},{6,4},{8,10},{10,8},{12,14},{14,12},{16,18},{18,... | collective-permute-start | bytes 884744 | tf_op jit(solution)/shard_map/ppermute | solution.py:313
  310.9 1.5 collective-permute-start.62
  312.4 1.9 collective-permute-start.37
  314.3 2.4 collective-permute-start.38
  316.7 2.7 merge.6
  319.4 2.3 collective-permute-done.37.refs_2_
  321.8 1.7 collective-permute-start.29
  323.5 1.9 normalize.5
  326.6 1.6 collective-permute-start.43
  328.2 1.7 collective-permute-start.44
  329.8 2.7 merge.7
  333.6 1.7 collective-permute-start.53
  336.1 1.9 collective-permute-start.64
  338.0 1.7 collective-permute-start.65
  339.7 2.1 collective-permute-start.30
  343.1 1.9 normalize.6
  345.0 1.9 collective-permute-start.55
  346.9 2.5 collective-permute-start.56
  350.3 2.0 normalize.7
  352.3 1.9 collective-permute-start.67
  354.2 2.5 collective-permute-start.68
  358.0 1.8 collective-permute-start.45
  361.5 1.8 collective-permute-start.57
  367.8 1.9 collective-permute-start.69
  373.5 2.8 collective-permute-done.59.refs_11_
  376.3 2.1 collective-permute-done.69.refs_13_
  379.1 2.9 collective-permute-done.71.refs_15_
  382.1 6.6 %project.1 = bf16[4,4,32,512]{3,2,1,0:T(8,128)(2,1)} custom-call(s32[11]{0:T(128)} %concatenate.3.info, bf16[4,32,1024]{2,1,0:T(8,128)(2,1)} %copy-done, bf16[4,32,1024]{2,1,0:T(8,128)(2,1)} %copy-done.16, bf16[4,32,1024]{2,1,0:T(8,128)(2,1)} %copy-done.17, bf16[4,32,1024]{2,1,0:T(8,128)(2,1)} %copy-done.18, bf16[4,32,1024]{2,1,0:T(8,128)(2,1)} %copy-done.1, ...), custom_call_target="tpu_custom_call" | custom-call | flops 2147483648 | bytes 8388608 | tf_op jit(solution)/shard_map/project/pallas_call | solution.py:298
  389.8 1.5 collective-permute-done.72
  391.3 1.7 add_convert_fusion
  (230 shorter events, 34.9 us)
Async XLA Ops:
  4.1 7.3 %collective-permute-start.1 = (bf16[32,1024]{1,0:T(8,128)(2,1)S(1)}, bf16[32,1024]{1,0:T(8,128)(2,1)S(1)}, u32[]{:S(2)}, u32[]{:S(2)}) collective-permute-start(bf16[32,1024]{1,0:T(8,128)(2,1)S(1)} %get-tuple-element.80), channel_id=1, source_target_pairs={{0,16},{2,18},{4,20},{6,22},{8,24},{10,26},{12,28},{14,30},{16,0},... | collective-permute-start | bytes 196616 | tf_op jit(solution)/shard_map/ppermute | solution.py:313
  20.5 8.9 %collective-permute-start.9 = (bf16[32,1024]{1,0:T(8,128)(2,1)S(1)}, bf16[32,1024]{1,0:T(8,128)(2,1)S(1)}, u32[]{:S(2)}, u32[]{:S(2)}) collective-permute-start(bf16[32,1024]{1,0:T(8,128)(2,1)S(1)} %get-tuple-element.43), channel_id=1, source_target_pairs={{0,8},{2,10},{4,12},{6,14},{8,0},{10,2},{12,4},{14,6},{16,24},{18,... | collective-permute-start | bytes 196616 | tf_op jit(solution)/shard_map/ppermute | solution.py:313
  20.7 9.2 %collective-permute-start.10 = (bf16[32,1024]{1,0:T(8,128)(2,1)S(1)}, bf16[32,1024]{1,0:T(8,128)(2,1)S(1)}, u32[]{:S(2)}, u32[]{:S(2)}) collective-permute-start(bf16[32,1024]{1,0:T(8,128)(2,1)S(1)} %get-tuple-element.43), channel_id=1, source_target_pairs={{0,16},{2,18},{4,20},{6,22},{8,24},{10,26},{12,28},{14,30},{16,0},... | collective-permute-start | bytes 196616 | tf_op jit(solution)/shard_map/ppermute | solution.py:313
  26.4 16.4 %collective-permute-start.3 = (bf16[4,32,1024]{2,1,0:T(8,128)(2,1)S(1)}, bf16[4,32,1024]{2,1,0:T(8,128)(2,1)S(1)}, u32[]{:S(2)}, u32[]{:S(2)}) collective-permute-start(bf16[4,32,1024]{2,1,0:T(8,128)(2,1)S(1)} %pad_maximum_fusion.refs_0_), channel_id=1, source_target_pairs={{0,2},{2,0},{4,6},{6,4},{8,10},{10,8},{12,14},{14,12},{16,18},{18,... | collective-permute-start | bytes 786440 | tf_op jit(solution)/shard_map/ppermute | solution.py:313
  27.9 16.4 %collective-permute-start.4 = (bf16[4,32,1024]{2,1,0:T(8,128)(2,1)S(1)}, bf16[4,32,1024]{2,1,0:T(8,128)(2,1)S(1)}, u32[]{:S(2)}, u32[]{:S(2)}) collective-permute-start(bf16[4,32,1024]{2,1,0:T(8,128)(2,1)S(1)} %pad_maximum_fusion.refs_0_), channel_id=1, source_target_pairs={{0,4},{2,6},{4,0},{6,2},{8,12},{10,14},{12,8},{14,10},{16,20},{18,... | collective-permute-start | bytes 786440 | tf_op jit(solution)/shard_map/ppermute | solution.py:313
  29.4 15.4 %collective-permute-start.5 = (bf16[4,32,1024]{2,1,0:T(8,128)(2,1)S(1)}, bf16[4,32,1024]{2,1,0:T(8,128)(2,1)S(1)}, u32[]{:S(2)}, u32[]{:S(2)}) collective-permute-start(bf16[4,32,1024]{2,1,0:T(8,128)(2,1)S(1)} %pad_maximum_fusion.refs_0_), channel_id=1, source_target_pairs={{0,6},{2,4},{4,2},{6,0},{8,14},{10,12},{12,10},{14,8},{16,22},{18,... | collective-permute-start | bytes 786440 | tf_op jit(solution)/shard_map/ppermute | solution.py:313
  31.6 6.8 %collective-permute-start.13 = (bf16[32,1024]{1,0:T(8,128)(2,1)S(1)}, bf16[32,1024]{1,0:T(8,128)(2,1)S(1)}, u32[]{:S(2)}, u32[]{:S(2)}) collective-permute-start(bf16[32,1024]{1,0:T(8,128)(2,1)S(1)} %get-tuple-element.44), channel_id=1, source_target_pairs={{0,16},{2,18},{4,20},{6,22},{8,24},{10,26},{12,28},{14,30},{16,0},... | collective-permute-start | bytes 196616 | tf_op jit(solution)/shard_map/ppermute | solution.py:313
  38.3 40.6 %collective-permute-start.18 = (bf16[4,32,1024]{2,1,0:T(8,128)(2,1)S(1)}, bf16[4,32,1024]{2,1,0:T(8,128)(2,1)S(1)}, u32[]{:S(2)}, u32[]{:S(2)}) collective-permute-start(bf16[4,32,1024]{2,1,0:T(8,128)(2,1)S(1)} %pad_maximum_fusion.1.refs_8_.refs_0_), channel_id=1, source_target_pairs={{0,2},{2,0},{4,6},{6,4},{8,10},{10,8},{12,14},{14,12},{16,18},{18,... | collective-permute-start | bytes 786440 | tf_op jit(solution)/shard_map/ppermute | solution.py:313
  40.6 63.9 %collective-permute-start.19 = (bf16[4,32,1024]{2,1,0:T(8,128)(2,1)S(1)}, bf16[4,32,1024]{2,1,0:T(8,128)(2,1)S(1)}, u32[]{:S(2)}, u32[]{:S(2)}) collective-permute-start(bf16[4,32,1024]{2,1,0:T(8,128)(2,1)S(1)} %pad_maximum_fusion.1.refs_8_.refs_0_), channel_id=1, source_target_pairs={{0,4},{2,6},{4,0},{6,2},{8,12},{10,14},{12,8},{14,10},{16,20},{18,... | collective-permute-start | bytes 786440 | tf_op jit(solution)/shard_map/ppermute | solution.py:313
  42.8 61.6 %collective-permute-start.20 = (bf16[4,32,1024]{2,1,0:T(8,128)(2,1)S(1)}, bf16[4,32,1024]{2,1,0:T(8,128)(2,1)S(1)}, u32[]{:S(2)}, u32[]{:S(2)}) collective-permute-start(bf16[4,32,1024]{2,1,0:T(8,128)(2,1)S(1)} %pad_maximum_fusion.1.refs_8_.refs_0_), channel_id=1, source_target_pairs={{0,6},{2,4},{4,2},{6,0},{8,14},{10,12},{12,10},{14,8},{16,22},{18,... | collective-permute-start | bytes 786440 | tf_op jit(solution)/shard_map/ppermute | solution.py:313
  44.3 124.1 %collective-permute-start.24 = (bf16[4,32,1024]{2,1,0:T(8,128)(2,1)S(1)}, bf16[4,32,1024]{2,1,0:T(8,128)(2,1)S(1)}, u32[]{:S(2)}, u32[]{:S(2)}) collective-permute-start(bf16[4,32,1024]{2,1,0:T(8,128)(2,1)S(1)} %pad_maximum_fusion.2.refs_9_.refs_0_), channel_id=1, source_target_pairs={{0,2},{2,0},{4,6},{6,4},{8,10},{10,8},{12,14},{14,12},{16,18},{18,... | collective-permute-start | bytes 786440 | tf_op jit(solution)/shard_map/ppermute | solution.py:313
  44.8 126.8 %collective-permute-start.25 = (bf16[4,32,1024]{2,1,0:T(8,128)(2,1)S(1)}, bf16[4,32,1024]{2,1,0:T(8,128)(2,1)S(1)}, u32[]{:S(2)}, u32[]{:S(2)}) collective-permute-start(bf16[4,32,1024]{2,1,0:T(8,128)(2,1)S(1)} %pad_maximum_fusion.2.refs_9_.refs_0_), channel_id=1, source_target_pairs={{0,4},{2,6},{4,0},{6,2},{8,12},{10,14},{12,8},{14,10},{16,20},{18,... | collective-permute-start | bytes 786440 | tf_op jit(solution)/shard_map/ppermute | solution.py:313
  79.0 59.9 %collective-permute-start.15 = (bf16[4,32,1152]{2,1,0:T(8,128)(2,1)}, bf16[4,32,1152]{2,1,0:T(8,128)(2,1)S(1)}, u32[]{:S(2)}, u32[]{:S(2)}) collective-permute-start(bf16[4,32,1152]{2,1,0:T(8,128)(2,1)} %get-tuple-element.46), channel_id=1, source_target_pairs={{0,2},{2,0},{4,6},{6,4},{8,10},{10,8},{12,14},{14,12},{16,18},{18,... | collective-permute-start | bytes 884744 | tf_op jit(solution)/shard_map/ppermute | solution.py:313
  104.4 60.4 %collective-permute-start.16 = (bf16[4,32,1152]{2,1,0:T(8,128)(2,1)}, bf16[4,32,1152]{2,1,0:T(8,128)(2,1)S(1)}, u32[]{:S(2)}, u32[]{:S(2)}) collective-permute-start(bf16[4,32,1152]{2,1,0:T(8,128)(2,1)} %get-tuple-element.47), channel_id=1, source_target_pairs={{0,4},{2,6},{4,0},{6,2},{8,12},{10,14},{12,8},{14,10},{16,20},{18,... | collective-permute-start | bytes 884744 | tf_op jit(solution)/shard_map/ppermute | solution.py:313
  104.5 60.4 %collective-permute-start.17 = (bf16[4,32,1152]{2,1,0:T(8,128)(2,1)}, bf16[4,32,1152]{2,1,0:T(8,128)(2,1)S(1)}, u32[]{:S(2)}, u32[]{:S(2)}) collective-permute-start(bf16[4,32,1152]{2,1,0:T(8,128)(2,1)} %get-tuple-element.48), channel_id=1, source_target_pairs={{0,6},{2,4},{4,2},{6,0},{8,14},{10,12},{12,10},{14,8},{16,22},{18,... | collective-permute-start | bytes 884744 | tf_op jit(solution)/shard_map/ppermute | solution.py:313
  138.9 39.3 %collective-permute-start.33 = (bf16[4,32,1152]{2,1,0:T(8,128)(2,1)}, bf16[4,32,1152]{2,1,0:T(8,128)(2,1)S(1)}, u32[]{:S(2)}, u32[]{:S(2)}) collective-permute-start(bf16[4,32,1152]{2,1,0:T(8,128)(2,1)} %get-tuple-element.55), channel_id=1, source_target_pairs={{0,2},{2,0},{4,6},{6,4},{8,10},{10,8},{12,14},{14,12},{16,18},{18,... | collective-permute-start | bytes 884744 | tf_op jit(solution)/shard_map/ppermute | solution.py:313
  164.8 13.3 %collective-permute-start.26 = (bf16[4,32,1024]{2,1,0:T(8,128)(2,1)S(1)}, bf16[4,32,1024]{2,1,0:T(8,128)(2,1)S(1)}, u32[]{:S(2)}, u32[]{:S(2)}) collective-permute-start(bf16[4,32,1024]{2,1,0:T(8,128)(2,1)S(1)} %copy-done.27), channel_id=1, source_target_pairs={{0,6},{2,4},{4,2},{6,0},{8,14},{10,12},{12,10},{14,8},{16,22},{18,... | collective-permute-start | bytes 786440 | tf_op jit(solution)/shard_map/ppermute | solution.py:313
  168.4 13.8 %collective-permute-start.21 = (bf16[32,1152]{1,0:T(8,128)(2,1)}, bf16[32,1152]{1,0:T(8,128)(2,1)S(1)}, u32[]{:S(2)}, u32[]{:S(2)}) collective-permute-start(bf16[32,1152]{1,0:T(8,128)(2,1)} %get-tuple-element.51), channel_id=1, source_target_pairs={{0,8},{2,10},{4,12},{6,14},{8,0},{10,2},{12,4},{14,6},{16,24},{18,... | collective-permute-start | bytes 221192 | tf_op jit(solution)/shard_map/ppermute | solution.py:313
  168.4 13.8 %collective-permute-start.22 = (bf16[32,1152]{1,0:T(8,128)(2,1)}, bf16[32,1152]{1,0:T(8,128)(2,1)S(1)}, u32[]{:S(2)}, u32[]{:S(2)}) collective-permute-start(bf16[32,1152]{1,0:T(8,128)(2,1)} %get-tuple-element.52), channel_id=1, source_target_pairs={{0,16},{2,18},{4,20},{6,22},{8,24},{10,26},{12,28},{14,30},{16,0},... | collective-permute-start | bytes 221192 | tf_op jit(solution)/shard_map/ppermute | solution.py:313
  171.6 12.1 %collective-permute-start.23 = (bf16[32,1152]{1,0:T(8,128)(2,1)}, bf16[32,1152]{1,0:T(8,128)(2,1)S(1)}, u32[]{:S(2)}, u32[]{:S(2)}) collective-permute-start(bf16[32,1152]{1,0:T(8,128)(2,1)} %get-tuple-element.53), channel_id=1, source_target_pairs={{0,24},{2,26},{4,28},{6,30},{8,16},{10,18},{12,20},{14,22},{16,8},... | collective-permute-start | bytes 221192 | tf_op jit(solution)/shard_map/ppermute | solution.py:313
  178.2 68.9 %collective-permute-start.39 = (bf16[4,32,1024]{2,1,0:T(8,128)(2,1)S(1)}, bf16[4,32,1024]{2,1,0:T(8,128)(2,1)S(1)}, u32[]{:S(2)}, u32[]{:S(2)}) collective-permute-start(bf16[4,32,1024]{2,1,0:T(8,128)(2,1)S(1)} %copy-done.25), channel_id=1, source_target_pairs={{0,2},{2,0},{4,6},{6,4},{8,10},{10,8},{12,14},{14,12},{16,18},{18,... | collective-permute-start | bytes 786440 | tf_op jit(solution)/shard_map/ppermute | solution.py:313
  178.2 69.0 %collective-permute-start.40 = (bf16[4,32,1024]{2,1,0:T(8,128)(2,1)S(1)}, bf16[4,32,1024]{2,1,0:T(8,128)(2,1)S(1)}, u32[]{:S(2)}, u32[]{:S(2)}) collective-permute-start(bf16[4,32,1024]{2,1,0:T(8,128)(2,1)S(1)} %copy-done.25), channel_id=1, source_target_pairs={{0,4},{2,6},{4,0},{6,2},{8,12},{10,14},{12,8},{14,10},{16,20},{18,... | collective-permute-start | bytes 786440 | tf_op jit(solution)/shard_map/ppermute | solution.py:313
  182.2 67.2 %collective-permute-start.41 = (bf16[4,32,1024]{2,1,0:T(8,128)(2,1)S(1)}, bf16[4,32,1024]{2,1,0:T(8,128)(2,1)S(1)}, u32[]{:S(2)}, u32[]{:S(2)}) collective-permute-start(bf16[4,32,1024]{2,1,0:T(8,128)(2,1)S(1)} %copy-done.25), channel_id=1, source_target_pairs={{0,6},{2,4},{4,2},{6,0},{8,14},{10,12},{12,10},{14,8},{16,22},{18,... | collective-permute-start | bytes 786440 | tf_op jit(solution)/shard_map/ppermute | solution.py:313
  182.2 37.5 %collective-permute-start.34 = (bf16[4,32,1152]{2,1,0:T(8,128)(2,1)}, bf16[4,32,1152]{2,1,0:T(8,128)(2,1)S(1)}, u32[]{:S(2)}, u32[]{:S(2)}) collective-permute-start(bf16[4,32,1152]{2,1,0:T(8,128)(2,1)} %get-tuple-element.56), channel_id=1, source_target_pairs={{0,4},{2,6},{4,0},{6,2},{8,12},{10,14},{12,8},{14,10},{16,20},{18,... | collective-permute-start | bytes 884744 | tf_op jit(solution)/shard_map/ppermute | solution.py:313
  183.7 46.2 %collective-permute-start.35 = (bf16[4,32,1152]{2,1,0:T(8,128)(2,1)}, bf16[4,32,1152]{2,1,0:T(8,128)(2,1)S(1)}, u32[]{:S(2)}, u32[]{:S(2)}) collective-permute-start(bf16[4,32,1152]{2,1,0:T(8,128)(2,1)} %get-tuple-element.57), channel_id=1, source_target_pairs={{0,6},{2,4},{4,2},{6,0},{8,14},{10,12},{12,10},{14,8},{16,22},{18,... | collective-permute-start | bytes 884744 | tf_op jit(solution)/shard_map/ppermute | solution.py:313
  219.7 31.5 %collective-permute-start.27 = (bf16[32,1024]{1,0:T(8,128)(2,1)}, bf16[32,1024]{1,0:T(8,128)(2,1)S(1)}, u32[]{:S(2)}, u32[]{:S(2)}) collective-permute-start(bf16[32,1024]{1,0:T(8,128)(2,1)} %normalize.4.refs_8_), channel_id=1, source_target_pairs={{0,8},{2,10},{4,12},{6,14},{8,0},{10,2},{12,4},{14,6},{16,24},{18,... | collective-permute-start | bytes 196616 | tf_op jit(solution)/shard_map/ppermute | solution.py:313
  229.9 81.0 %collective-permute-start.48 = (bf16[4,32,1152]{2,1,0:T(8,128)(2,1)}, bf16[4,32,1152]{2,1,0:T(8,128)(2,1)S(1)}, u32[]{:S(2)}, u32[]{:S(2)}) collective-permute-start(bf16[4,32,1152]{2,1,0:T(8,128)(2,1)} %get-tuple-element.63), channel_id=1, source_target_pairs={{0,2},{2,0},{4,6},{6,4},{8,10},{10,8},{12,14},{14,12},{16,18},{18,... | collective-permute-start | bytes 884744 | tf_op jit(solution)/shard_map/ppermute | solution.py:313
  247.1 65.4 %collective-permute-start.49 = (bf16[4,32,1152]{2,1,0:T(8,128)(2,1)}, bf16[4,32,1152]{2,1,0:T(8,128)(2,1)S(1)}, u32[]{:S(2)}, u32[]{:S(2)}) collective-permute-start(bf16[4,32,1152]{2,1,0:T(8,128)(2,1)} %get-tuple-element.64), channel_id=1, source_target_pairs={{0,4},{2,6},{4,0},{6,2},{8,12},{10,14},{12,8},{14,10},{16,20},{18,... | collective-permute-start | bytes 884744 | tf_op jit(solution)/shard_map/ppermute | solution.py:313
  247.2 67.2 %collective-permute-start.50 = (bf16[4,32,1152]{2,1,0:T(8,128)(2,1)}, bf16[4,32,1152]{2,1,0:T(8,128)(2,1)S(1)}, u32[]{:S(2)}, u32[]{:S(2)}) collective-permute-start(bf16[4,32,1152]{2,1,0:T(8,128)(2,1)} %get-tuple-element.65), channel_id=1, source_target_pairs={{0,6},{2,4},{4,2},{6,0},{8,14},{10,12},{12,10},{14,8},{16,22},{18,... | collective-permute-start | bytes 884744 | tf_op jit(solution)/shard_map/ppermute | solution.py:313
  249.3 61.5 %collective-permute-start.36 = (bf16[32,1152]{1,0:T(8,128)(2,1)}, bf16[32,1152]{1,0:T(8,128)(2,1)S(1)}, u32[]{:S(2)}, u32[]{:S(2)}) collective-permute-start(bf16[32,1152]{1,0:T(8,128)(2,1)} %get-tuple-element.59), channel_id=1, source_target_pairs={{0,8},{2,10},{4,12},{6,14},{8,0},{10,2},{12,4},{14,6},{16,24},{18,... | collective-permute-start | bytes 221192 | tf_op jit(solution)/shard_map/ppermute | solution.py:313
  251.3 34.4 %collective-permute-start.28 = (bf16[32,1024]{1,0:T(8,128)(2,1)}, bf16[32,1024]{1,0:T(8,128)(2,1)S(1)}, u32[]{:S(2)}, u32[]{:S(2)}) collective-permute-start(bf16[32,1024]{1,0:T(8,128)(2,1)} %normalize.4.refs_8_), channel_id=1, source_target_pairs={{0,16},{2,18},{4,20},{6,22},{8,24},{10,26},{12,28},{14,30},{16,0},... | collective-permute-start | bytes 196616 | tf_op jit(solution)/shard_map/ppermute | solution.py:313
  285.6 39.8 %collective-permute-start.60 = (bf16[4,32,1152]{2,1,0:T(8,128)(2,1)}, bf16[4,32,1152]{2,1,0:T(8,128)(2,1)S(1)}, u32[]{:S(2)}, u32[]{:S(2)}) collective-permute-start(bf16[4,32,1152]{2,1,0:T(8,128)(2,1)} %get-tuple-element.70), channel_id=1, source_target_pairs={{0,2},{2,0},{4,6},{6,4},{8,10},{10,8},{12,14},{14,12},{16,18},{18,... | collective-permute-start | bytes 884744 | tf_op jit(solution)/shard_map/ppermute | solution.py:313
  310.9 15.7 %collective-permute-start.61 = (bf16[4,32,1152]{2,1,0:T(8,128)(2,1)}, bf16[4,32,1152]{2,1,0:T(8,128)(2,1)S(1)}, u32[]{:S(2)}, u32[]{:S(2)}) collective-permute-start(bf16[4,32,1152]{2,1,0:T(8,128)(2,1)} %get-tuple-element.71), channel_id=1, source_target_pairs={{0,4},{2,6},{4,0},{6,2},{8,12},{10,14},{12,8},{14,10},{16,20},{18,... | collective-permute-start | bytes 884744 | tf_op jit(solution)/shard_map/ppermute | solution.py:313
  310.9 17.3 %collective-permute-start.62 = (bf16[4,32,1152]{2,1,0:T(8,128)(2,1)}, bf16[4,32,1152]{2,1,0:T(8,128)(2,1)S(1)}, u32[]{:S(2)}, u32[]{:S(2)}) collective-permute-start(bf16[4,32,1152]{2,1,0:T(8,128)(2,1)} %get-tuple-element.72), channel_id=1, source_target_pairs={{0,6},{2,4},{4,2},{6,0},{8,14},{10,12},{12,10},{14,8},{16,22},{18,... | collective-permute-start | bytes 884744 | tf_op jit(solution)/shard_map/ppermute | solution.py:313
  312.4 9.3 %collective-permute-start.37 = (bf16[32,1152]{1,0:T(8,128)(2,1)S(1)}, bf16[32,1152]{1,0:T(8,128)(2,1)S(1)}, u32[]{:S(2)}, u32[]{:S(2)}) collective-permute-start(bf16[32,1152]{1,0:T(8,128)(2,1)S(1)} %copy-done.56), channel_id=1, source_target_pairs={{0,16},{2,18},{4,20},{6,22},{8,24},{10,26},{12,28},{14,30},{16,0},... | collective-permute-start | bytes 221192 | tf_op jit(solution)/shard_map/ppermute | solution.py:313
  314.3 7.4 %collective-permute-start.38 = (bf16[32,1152]{1,0:T(8,128)(2,1)S(1)}, bf16[32,1152]{1,0:T(8,128)(2,1)S(1)}, u32[]{:S(2)}, u32[]{:S(2)}) collective-permute-start(bf16[32,1152]{1,0:T(8,128)(2,1)S(1)} %copy-done.55), channel_id=1, source_target_pairs={{0,24},{2,26},{4,28},{6,30},{8,16},{10,18},{12,20},{14,22},{16,8},... | collective-permute-start | bytes 221192 | tf_op jit(solution)/shard_map/ppermute | solution.py:313
  321.8 16.2 %collective-permute-start.51 = (bf16[32,1152]{1,0:T(8,128)(2,1)}, bf16[32,1152]{1,0:T(8,128)(2,1)S(1)}, u32[]{:S(2)}, u32[]{:S(2)}) collective-permute-start(bf16[32,1152]{1,0:T(8,128)(2,1)} %get-tuple-element.67), channel_id=1, source_target_pairs={{0,8},{2,10},{4,12},{6,14},{8,0},{10,2},{12,4},{14,6},{16,24},{18,... | collective-permute-start | bytes 221192 | tf_op jit(solution)/shard_map/ppermute | solution.py:313
  321.8 10.8 %collective-permute-start.29 = (bf16[32,1024]{1,0:T(8,128)(2,1)S(1)}, bf16[32,1024]{1,0:T(8,128)(2,1)S(1)}, u32[]{:S(2)}, u32[]{:S(2)}) collective-permute-start(bf16[32,1024]{1,0:T(8,128)(2,1)S(1)} %copy-done.30), channel_id=1, source_target_pairs={{0,24},{2,26},{4,28},{6,30},{8,16},{10,18},{12,20},{14,22},{16,8},... | collective-permute-start | bytes 196616 | tf_op jit(solution)/shard_map/ppermute | solution.py:313
  325.4 8.1 %collective-permute-start.42 = (bf16[32,1024]{1,0:T(8,128)(2,1)}, bf16[32,1024]{1,0:T(8,128)(2,1)S(1)}, u32[]{:S(2)}, u32[]{:S(2)}) collective-permute-start(bf16[32,1024]{1,0:T(8,128)(2,1)} %normalize.5), channel_id=1, source_target_pairs={{0,8},{2,10},{4,12},{6,14},{8,0},{10,2},{12,4},{14,6},{16,24},{18,... | collective-permute-start | bytes 196616 | tf_op jit(solution)/shard_map/ppermute | solution.py:313
  326.6 8.6 %collective-permute-start.43 = (bf16[32,1024]{1,0:T(8,128)(2,1)}, bf16[32,1024]{1,0:T(8,128)(2,1)S(1)}, u32[]{:S(2)}, u32[]{:S(2)}) collective-permute-start(bf16[32,1024]{1,0:T(8,128)(2,1)} %normalize.5), channel_id=1, source_target_pairs={{0,16},{2,18},{4,20},{6,22},{8,24},{10,26},{12,28},{14,30},{16,0},... | collective-permute-start | bytes 196616 | tf_op jit(solution)/shard_map/ppermute | solution.py:313
  328.2 7.9 %collective-permute-start.44 = (bf16[32,1024]{1,0:T(8,128)(2,1)}, bf16[32,1024]{1,0:T(8,128)(2,1)S(1)}, u32[]{:S(2)}, u32[]{:S(2)}) collective-permute-start(bf16[32,1024]{1,0:T(8,128)(2,1)} %normalize.5), channel_id=1, source_target_pairs={{0,24},{2,26},{4,28},{6,30},{8,16},{10,18},{12,20},{14,22},{16,8},... | collective-permute-start | bytes 196616 | tf_op jit(solution)/shard_map/ppermute | solution.py:313
  332.6 7.1 %collective-permute-start.52 = (bf16[32,1152]{1,0:T(8,128)(2,1)}, bf16[32,1152]{1,0:T(8,128)(2,1)S(1)}, u32[]{:S(2)}, u32[]{:S(2)}) collective-permute-start(bf16[32,1152]{1,0:T(8,128)(2,1)} %get-tuple-element.68), channel_id=1, source_target_pairs={{0,16},{2,18},{4,20},{6,22},{8,24},{10,26},{12,28},{14,30},{16,0},... | collective-permute-start | bytes 221192 | tf_op jit(solution)/shard_map/ppermute | solution.py:313
  333.6 8.2 %collective-permute-start.53 = (bf16[32,1152]{1,0:T(8,128)(2,1)}, bf16[32,1152]{1,0:T(8,128)(2,1)S(1)}, u32[]{:S(2)}, u32[]{:S(2)}) collective-permute-start(bf16[32,1152]{1,0:T(8,128)(2,1)} %get-tuple-element.69), channel_id=1, source_target_pairs={{0,24},{2,26},{4,28},{6,30},{8,16},{10,18},{12,20},{14,22},{16,8},... | collective-permute-start | bytes 221192 | tf_op jit(solution)/shard_map/ppermute | solution.py:313
  335.2 9.8 %collective-permute-start.63 = (bf16[32,1152]{1,0:T(8,128)(2,1)}, bf16[32,1152]{1,0:T(8,128)(2,1)S(1)}, u32[]{:S(2)}, u32[]{:S(2)}) collective-permute-start(bf16[32,1152]{1,0:T(8,128)(2,1)} %get-tuple-element.74), channel_id=1, source_target_pairs={{0,8},{2,10},{4,12},{6,14},{8,0},{10,2},{12,4},{14,6},{16,24},{18,... | collective-permute-start | bytes 221192 | tf_op jit(solution)/shard_map/ppermute | solution.py:313
  336.1 8.9 %collective-permute-start.64 = (bf16[32,1152]{1,0:T(8,128)(2,1)}, bf16[32,1152]{1,0:T(8,128)(2,1)S(1)}, u32[]{:S(2)}, u32[]{:S(2)}) collective-permute-start(bf16[32,1152]{1,0:T(8,128)(2,1)} %get-tuple-element.75), channel_id=1, source_target_pairs={{0,16},{2,18},{4,20},{6,22},{8,24},{10,26},{12,28},{14,30},{16,0},... | collective-permute-start | bytes 221192 | tf_op jit(solution)/shard_map/ppermute | solution.py:313
  338.0 9.0 %collective-permute-start.65 = (bf16[32,1152]{1,0:T(8,128)(2,1)}, bf16[32,1152]{1,0:T(8,128)(2,1)S(1)}, u32[]{:S(2)}, u32[]{:S(2)}) collective-permute-start(bf16[32,1152]{1,0:T(8,128)(2,1)} %get-tuple-element.76), channel_id=1, source_target_pairs={{0,24},{2,26},{4,28},{6,30},{8,16},{10,18},{12,20},{14,22},{16,8},... | collective-permute-start | bytes 221192 | tf_op jit(solution)/shard_map/ppermute | solution.py:313
  339.7 17.9 %collective-permute-start.30 = (bf16[4,32,1024]{2,1,0:T(8,128)(2,1)S(1)}, bf16[4,32,1024]{2,1,0:T(8,128)(2,1)S(1)}, u32[]{:S(2)}, u32[]{:S(2)}) collective-permute-start(bf16[4,32,1024]{2,1,0:T(8,128)(2,1)S(1)} %pad_maximum_fusion.4.refs_0_), channel_id=1, source_target_pairs={{0,2},{2,0},{4,6},{6,4},{8,10},{10,8},{12,14},{14,12},{16,18},{18,... | collective-permute-start | bytes 786440 | tf_op jit(solution)/shard_map/ppermute | solution.py:313
  341.8 16.2 %collective-permute-start.31 = (bf16[4,32,1024]{2,1,0:T(8,128)(2,1)S(1)}, bf16[4,32,1024]{2,1,0:T(8,128)(2,1)S(1)}, u32[]{:S(2)}, u32[]{:S(2)}) collective-permute-start(bf16[4,32,1024]{2,1,0:T(8,128)(2,1)S(1)} %pad_maximum_fusion.4.refs_0_), channel_id=1, source_target_pairs={{0,4},{2,6},{4,0},{6,2},{8,12},{10,14},{12,8},{14,10},{16,20},{18,... | collective-permute-start | bytes 786440 | tf_op jit(solution)/shard_map/ppermute | solution.py:313
  345.0 7.3 %collective-permute-start.54 = (bf16[32,1024]{1,0:T(8,128)(2,1)}, bf16[32,1024]{1,0:T(8,128)(2,1)S(1)}, u32[]{:S(2)}, u32[]{:S(2)}) collective-permute-start(bf16[32,1024]{1,0:T(8,128)(2,1)} %normalize.6), channel_id=1, source_target_pairs={{0,8},{2,10},{4,12},{6,14},{8,0},{10,2},{12,4},{14,6},{16,24},{18,... | collective-permute-start | bytes 196616 | tf_op jit(solution)/shard_map/ppermute | solution.py:313
  345.0 7.3 %collective-permute-start.55 = (bf16[32,1024]{1,0:T(8,128)(2,1)}, bf16[32,1024]{1,0:T(8,128)(2,1)S(1)}, u32[]{:S(2)}, u32[]{:S(2)}) collective-permute-start(bf16[32,1024]{1,0:T(8,128)(2,1)} %normalize.6), channel_id=1, source_target_pairs={{0,16},{2,18},{4,20},{6,22},{8,24},{10,26},{12,28},{14,30},{16,0},... | collective-permute-start | bytes 196616 | tf_op jit(solution)/shard_map/ppermute | solution.py:313
  346.9 7.3 %collective-permute-start.56 = (bf16[32,1024]{1,0:T(8,128)(2,1)}, bf16[32,1024]{1,0:T(8,128)(2,1)S(1)}, u32[]{:S(2)}, u32[]{:S(2)}) collective-permute-start(bf16[32,1024]{1,0:T(8,128)(2,1)} %normalize.6), channel_id=1, source_target_pairs={{0,24},{2,26},{4,28},{6,30},{8,16},{10,18},{12,20},{14,22},{16,8},... | collective-permute-start | bytes 196616 | tf_op jit(solution)/shard_map/ppermute | solution.py:313
  352.3 7.6 %collective-permute-start.66 = (bf16[32,1024]{1,0:T(8,128)(2,1)}, bf16[32,1024]{1,0:T(8,128)(2,1)S(1)}, u32[]{:S(2)}, u32[]{:S(2)}) collective-permute-start(bf16[32,1024]{1,0:T(8,128)(2,1)} %normalize.7), channel_id=1, source_target_pairs={{0,8},{2,10},{4,12},{6,14},{8,0},{10,2},{12,4},{14,6},{16,24},{18,... | collective-permute-start | bytes 196616 | tf_op jit(solution)/shard_map/ppermute | solution.py:313
  352.3 8.9 %collective-permute-start.67 = (bf16[32,1024]{1,0:T(8,128)(2,1)}, bf16[32,1024]{1,0:T(8,128)(2,1)S(1)}, u32[]{:S(2)}, u32[]{:S(2)}) collective-permute-start(bf16[32,1024]{1,0:T(8,128)(2,1)} %normalize.7), channel_id=1, source_target_pairs={{0,16},{2,18},{4,20},{6,22},{8,24},{10,26},{12,28},{14,30},{16,0},... | collective-permute-start | bytes 196616 | tf_op jit(solution)/shard_map/ppermute | solution.py:313
  354.2 7.3 %collective-permute-start.68 = (bf16[32,1024]{1,0:T(8,128)(2,1)}, bf16[32,1024]{1,0:T(8,128)(2,1)S(1)}, u32[]{:S(2)}, u32[]{:S(2)}) collective-permute-start(bf16[32,1024]{1,0:T(8,128)(2,1)} %normalize.7), channel_id=1, source_target_pairs={{0,24},{2,26},{4,28},{6,30},{8,16},{10,18},{12,20},{14,22},{16,8},... | collective-permute-start | bytes 196616 | tf_op jit(solution)/shard_map/ppermute | solution.py:313
  357.6 7.4 %collective-permute-start.32 = (bf16[4,32,1024]{2,1,0:T(8,128)(2,1)S(1)}, bf16[4,32,1024]{2,1,0:T(8,128)(2,1)S(1)}, u32[]{:S(2)}, u32[]{:S(2)}) collective-permute-start(bf16[4,32,1024]{2,1,0:T(8,128)(2,1)S(1)} %pad_maximum_fusion.4.refs_0_), channel_id=1, source_target_pairs={{0,6},{2,4},{4,2},{6,0},{8,14},{10,12},{12,10},{14,8},{16,22},{18,... | collective-permute-start | bytes 786440 | tf_op jit(solution)/shard_map/ppermute | solution.py:313
  358.0 9.0 %collective-permute-start.45 = (bf16[4,32,1024]{2,1,0:T(8,128)(2,1)S(1)}, bf16[4,32,1024]{2,1,0:T(8,128)(2,1)S(1)}, u32[]{:S(2)}, u32[]{:S(2)}) collective-permute-start(bf16[4,32,1024]{2,1,0:T(8,128)(2,1)S(1)} %pad_maximum_fusion.5.refs_4_), channel_id=1, source_target_pairs={{0,2},{2,0},{4,6},{6,4},{8,10},{10,8},{12,14},{14,12},{16,18},{18,... | collective-permute-start | bytes 786440 | tf_op jit(solution)/shard_map/ppermute | solution.py:313
  359.8 8.0 %collective-permute-start.46 = (bf16[4,32,1024]{2,1,0:T(8,128)(2,1)S(1)}, bf16[4,32,1024]{2,1,0:T(8,128)(2,1)S(1)}, u32[]{:S(2)}, u32[]{:S(2)}) collective-permute-start(bf16[4,32,1024]{2,1,0:T(8,128)(2,1)S(1)} %pad_maximum_fusion.5.refs_4_), channel_id=1, source_target_pairs={{0,4},{2,6},{4,0},{6,2},{8,12},{10,14},{12,8},{14,10},{16,20},{18,... | collective-permute-start | bytes 786440 | tf_op jit(solution)/shard_map/ppermute | solution.py:313
  361.1 9.5 %collective-permute-start.47 = (bf16[4,32,1024]{2,1,0:T(8,128)(2,1)S(1)}, bf16[4,32,1024]{2,1,0:T(8,128)(2,1)S(1)}, u32[]{:S(2)}, u32[]{:S(2)}) collective-permute-start(bf16[4,32,1024]{2,1,0:T(8,128)(2,1)S(1)} %pad_maximum_fusion.5.refs_4_), channel_id=1, source_target_pairs={{0,6},{2,4},{4,2},{6,0},{8,14},{10,12},{12,10},{14,8},{16,22},{18,... | collective-permute-start | bytes 786440 | tf_op jit(solution)/shard_map/ppermute | solution.py:313
  361.5 11.1 %collective-permute-start.57 = (bf16[4,32,1024]{2,1,0:T(8,128)(2,1)S(1)}, bf16[4,32,1024]{2,1,0:T(8,128)(2,1)S(1)}, u32[]{:S(2)}, u32[]{:S(2)}) collective-permute-start(bf16[4,32,1024]{2,1,0:T(8,128)(2,1)S(1)} %pad_maximum_fusion.6.refs_8_), channel_id=1, source_target_pairs={{0,2},{2,0},{4,6},{6,4},{8,10},{10,8},{12,14},{14,12},{16,18},{18,... | collective-permute-start | bytes 786440 | tf_op jit(solution)/shard_map/ppermute | solution.py:313
  365.0 8.5 %collective-permute-start.58 = (bf16[4,32,1024]{2,1,0:T(8,128)(2,1)S(1)}, bf16[4,32,1024]{2,1,0:T(8,128)(2,1)S(1)}, u32[]{:S(2)}, u32[]{:S(2)}) collective-permute-start(bf16[4,32,1024]{2,1,0:T(8,128)(2,1)S(1)} %pad_maximum_fusion.6.refs_8_), channel_id=1, source_target_pairs={{0,4},{2,6},{4,0},{6,2},{8,12},{10,14},{12,8},{14,10},{16,20},{18,... | collective-permute-start | bytes 786440 | tf_op jit(solution)/shard_map/ppermute | solution.py:313
  367.0 9.3 %collective-permute-start.59 = (bf16[4,32,1024]{2,1,0:T(8,128)(2,1)S(1)}, bf16[4,32,1024]{2,1,0:T(8,128)(2,1)S(1)}, u32[]{:S(2)}, u32[]{:S(2)}) collective-permute-start(bf16[4,32,1024]{2,1,0:T(8,128)(2,1)S(1)} %pad_maximum_fusion.6.refs_8_), channel_id=1, source_target_pairs={{0,6},{2,4},{4,2},{6,0},{8,14},{10,12},{12,10},{14,8},{16,22},{18,... | collective-permute-start | bytes 786440 | tf_op jit(solution)/shard_map/ppermute | solution.py:313
  367.8 10.6 %collective-permute-start.69 = (bf16[4,32,1024]{2,1,0:T(8,128)(2,1)S(1)}, bf16[4,32,1024]{2,1,0:T(8,128)(2,1)}, u32[]{:S(2)}, u32[]{:S(2)}) collective-permute-start(bf16[4,32,1024]{2,1,0:T(8,128)(2,1)S(1)} %pad_maximum_fusion.7.refs_12_), channel_id=1, source_target_pairs={{0,2},{2,0},{4,6},{6,4},{8,10},{10,8},{12,14},{14,12},{16,18},{18,... | collective-permute-start | bytes 786440 | tf_op jit(solution)/shard_map/ppermute | solution.py:313
  370.6 8.5 %collective-permute-start.70 = (bf16[4,32,1024]{2,1,0:T(8,128)(2,1)S(1)}, bf16[4,32,1024]{2,1,0:T(8,128)(2,1)}, u32[]{:S(2)}, u32[]{:S(2)}) collective-permute-start(bf16[4,32,1024]{2,1,0:T(8,128)(2,1)S(1)} %pad_maximum_fusion.7.refs_12_), channel_id=1, source_target_pairs={{0,4},{2,6},{4,0},{6,2},{8,12},{10,14},{12,8},{14,10},{16,20},{18,... | collective-permute-start | bytes 786440 | tf_op jit(solution)/shard_map/ppermute | solution.py:313
  372.6 9.3 %collective-permute-start.71 = (bf16[4,32,1024]{2,1,0:T(8,128)(2,1)S(1)}, bf16[4,32,1024]{2,1,0:T(8,128)(2,1)}, u32[]{:S(2)}, u32[]{:S(2)}) collective-permute-start(bf16[4,32,1024]{2,1,0:T(8,128)(2,1)S(1)} %pad_maximum_fusion.7.refs_12_), channel_id=1, source_target_pairs={{0,6},{2,4},{4,2},{6,0},{8,14},{10,12},{12,10},{14,8},{16,22},{18,... | collective-permute-start | bytes 786440 | tf_op jit(solution)/shard_map/ppermute | solution.py:313
  (66 other events, 1057.0 us)

commit v2 on v1

--- a/solution.py
+++ b/solution.py
@@ -26,20 +26,22 @@
     return parts[0]
 
 
-def attend_kernel(
-    info, *refs, plane, blocks, rows, group_step, key_chunk, waits
-):
-    q_refs, refs = refs[:plane], refs[plane:]
-    k_ref, v_ref, ks_ref, vs_ref = refs[:4]
+def attend_kernel(info, *refs, plane, blocks, rows, group_step, key_chunk, pieces, waits):
+    q_refs, refs = refs[:pieces], refs[pieces:]
+    kt_ref, v_ref, ks_ref, vs_ref = refs[:4]
     refs = refs[4 + waits :]
     o_refs, refs = refs[:plane], refs[plane:]
-    score_ref, peak_ref, aux_ref, pos_ref, ks_pad, vs_pad = refs
+    score_refs, refs = refs[:2], refs[2:]
+    weight_refs, refs = refs[:2], refs[2:]
+    shift_refs, refs = refs[:2], refs[2:]
+    aux_ref, pos_ref, ks_pad, vs_pad = refs
     me, my_plane, wanted = info[0], info[1], info[2]
-    keys = k_ref.shape[0]
+    keys = v_ref.shape[0]
     block_rows = plane * rows
     tile_rows = group_step * block_rows
     steps = GROUP_QUERIES // group_step
     chunks = keys // key_chunk
+    strip = min(tile_rows, 64)
 
     ks_pad[...] = jnp.zeros_like(ks_pad)
     vs_pad[...] = jnp.zeros_like(vs_pad)
@@ -58,23 +60,23 @@
 
     def load_queries(tile):
         slot, group = place(tile)
+        block = info[3 + blocks + slot]
         parts = []
         for i in range(group_step):
             cols = pl.ds(pl.multiple_of((group + i) * HEAD_SIZE, HEAD_SIZE), HEAD_SIZE)
-            parts += [q[slot, :, cols] for q in q_refs]
+            for b in range(plane):
+                parts.append(q_refs[b][slot, :, cols] if pieces > 1 else q_refs[0][block, b ^ my_plane, :, cols])
         return jnp.concatenate(parts, axis=0)
-
-    def dot_keys(q, k):
-        return lax.dot_general(q, k, (((1,), (1,)), ((), ())), preferred_element_type=F32)
 
     def span_scores(q, tile):
         slot, _ = place(tile)
         start = info[3 + blocks + slot] * block_rows
-        return jnp.where(pos_ref[...] + start >= 0, dot_keys(q, ks_pad[...]), MASKED)
+        scores = lax.dot_general(q, ks_pad[...], (((1,), (1,)), ((), ())), preferred_element_type=F32)
+        return jnp.where(pos_ref[...] + start >= 0, scores, MASKED)
 
     def shift_of(peak):
         top = jnp.max(peak, axis=1, keepdims=True) * LOG2_SCALE
-        return jnp.maximum(top, LOWEST).astype(BF16).astype(F32)
+        return jnp.broadcast_to(jnp.maximum(top, LOWEST).astype(BF16).astype(F32), (tile_rows, LANES))
 
     def finish(tile, shift, total, acc):
         slot, group = place(tile)
@@ -95,47 +97,62 @@
         for b, o in enumerate(o_refs):
             o[slot, :, GROUP_QUERIES * HEAD_SIZE :] = aux[b * rows : (b + 1) * rows].astype(BF16)
 
-    def step(now, later):
-        if now is not None:
-            here = lax.rem(now, 2)
-            shift = peak_ref[here][:, 0:1]
-            wide_shift = jnp.broadcast_to(shift, (tile_rows, LANES))
-            weights = jnp.exp2(score_ref[here, :, keys:] * LOG2_SCALE - wide_shift)
-            total = weights
-            acc = jnp.dot(weights.astype(BF16), vs_pad[...], preferred_element_type=F32)
-        if later is not None:
-            there = lax.rem(later, 2)
-            q = load_queries(later)
-            scores = span_scores(q, later)
-            score_ref[there, :, keys:] = scores
-            peak = scores
+    def score_span(tile, side):
+        q = load_queries(tile)
+        scores = span_scores(q, tile)
+        score_refs[side][:, keys:] = scores
+        return q, scores
+
+    def score_chunk(q, peak, j, side):
+        part = slice(j * key_chunk, (j + 1) * key_chunk)
+        scores = jnp.dot(q, kt_ref[:, part], preferred_element_type=F32)
+        score_refs[side][:, part] = scores
+        return jnp.maximum(peak, fold_lanes(jnp.maximum, scores))
+
+    def weigh_chunk(totals, j, side):
+        score_ref, shift_ref, weight_ref = score_refs[side], shift_refs[side], weight_refs[j % 2]
+        for n, r in enumerate(range(0, tile_rows, strip)):
+            part = slice(r, r + strip)
+            shift = shift_ref[part]
+            for c in range(0, key_chunk, LANES):
+                start = j * key_chunk + c
+                weights = jnp.exp2(score_ref[part, start : start + LANES] * LOG2_SCALE - shift)
+                totals[n] = totals[n] + weights
+                weight_ref[part, c : c + LANES] = weights.astype(BF16)
+
+    def apply_chunk(acc, j):
+        values = v_ref[j * key_chunk : (j + 1) * key_chunk]
+        return acc + jnp.dot(weight_refs[j % 2][...], values, preferred_element_type=F32)
+
+    def step(now, later, side):
+        q, peak = score_span(later, 1 - side)
+        weights = jnp.exp2(score_refs[side][:, keys:] * LOG2_SCALE - shift_refs[side][...])
+        acc = jnp.dot(weights.astype(BF16), vs_pad[...], preferred_element_type=F32)
+        totals = [weights[r : r + strip] for r in range(0, tile_rows, strip)]
         for j in range(chunks):
-            part = slice(j * key_chunk, (j + 1) * key_chunk)
-            if later is not None:
-                scores = dot_keys(q, k_ref[part])
-                score_ref[there, :, part] = scores
-                peak = jnp.maximum(peak, fold_lanes(jnp.maximum, scores))
-            if now is not None:
-                weights = jnp.exp2(score_ref[here, :, part] * LOG2_SCALE - shift)
-                total = total + fold_lanes(jnp.add, weights)
-                acc = acc + jnp.dot(weights.astype(BF16), v_ref[part], preferred_element_type=F32)
-        if later is not None:
-            peak_ref[there] = jnp.broadcast_to(shift_of(peak), (tile_rows, LANES))
-        if now is not None:
-            finish(now, shift, total, acc)
+            peak = score_chunk(q, peak, j, 1 - side)
+            weigh_chunk(totals, j, side)
+            if j > 0:
+                acc = apply_chunk(acc, j - 1)
+        acc = apply_chunk(acc, chunks - 1)
+        shift_refs[1 - side][...] = shift_of(peak)
+        finish(now, shift_refs[side][...], jnp.concatenate(totals, axis=0), acc)
 
     count = wanted * steps
 
     @pl.when(count > 0)
     def _():
-        step(None, jnp.int32(0))
-
-        def body(t, _):
-            step(t, t + 1)
+        q, peak = score_span(jnp.int32(0), 0)
+        for j in range(chunks):
+            peak = score_chunk(q, peak, j, 0)
+        shift_refs[0][...] = shift_of(peak)
+
+        def body(i, _):
+            step(2 * i, 2 * i + 1, 0)
+            step(2 * i + 1, jnp.minimum(2 * i + 2, count - 1), 1)
             return 0
 
-        lax.fori_loop(0, count - 1, body, 0)
-        step(count - 1, None)
+        lax.fori_loop(0, lax.div(count, 2), body, 0)
 
     def span_only(t, _):
         scores = span_scores(load_queries(t), t)
@@ -148,17 +165,20 @@
     lax.fori_loop(count, blocks * steps, span_only, 0)
 
 
-def attend_head(info, q_pieces, keys, values, span_keys, span_values, head, after):
-    plane = len(q_pieces)
-    blocks, rows, cols = q_pieces[0].shape
-    key_count = keys.shape[0]
+def attend_head(info, q_arrays, q_head, keys_t, values, span_keys, span_values, head, after):
+    shape = q_arrays[0].shape
+    blocks, rows = shape[0], shape[-2]
+    plane = len(q_arrays) if len(q_arrays) > 1 else shape[1]
+    cols = GROUP_QUERIES * HEAD_SIZE
+    key_count = values.shape[0]
     group_step = 2
     tile_rows = group_step * plane * rows
+    key_chunk = min(key_count, 512)
     out_cols = cols + LANES
     vmem = pltpu.MemorySpace.VMEM
-    whole = pl.BlockSpec((blocks, rows, cols), lambda i, s: (0, 0, 0))
+    lead = (0,) * (len(shape) - 1)
+    whole = pl.BlockSpec((*shape[:-1], cols), lambda i, s: (*lead, q_head))
     whole_out = pl.BlockSpec((blocks, rows, out_cols), lambda i, s: (0, 0, 0))
-    head_block = pl.BlockSpec((key_count, HEAD_SIZE), lambda i, s: (0, head))
     span_block = pl.BlockSpec((rows, HEAD_SIZE), lambda i, s: (0, head))
     scored = blocks * plane * rows * GROUP_QUERIES * key_count
     return pl.pallas_call(
@@ -168,19 +188,26 @@
             blocks=blocks,
             rows=rows,
             group_step=group_step,
-            key_chunk=min(key_count, 512),
+            key_chunk=key_chunk,
+            pieces=len(q_arrays),
             waits=len(after),
         ),
         grid_spec=pltpu.PrefetchScalarGridSpec(
             num_scalar_prefetch=1,
             grid=(1,),
-            in_specs=[whole] * plane
-            + [head_block, head_block, span_block, span_block]
+            in_specs=[whole] * len(q_arrays)
+            + [
+                pl.BlockSpec((HEAD_SIZE, key_count), lambda i, s: (head, 0)),
+                pl.BlockSpec((key_count, HEAD_SIZE), lambda i, s: (0, head)),
+                span_block,
+                span_block,
+            ]
             + [pl.BlockSpec(memory_space=pl.ANY)] * len(after),
             out_specs=[whole_out] * plane,
-            scratch_shapes=[
-                vmem((2, tile_rows, key_count + LANES), F32),
-                vmem((2, tile_rows, LANES), F32),
+            scratch_shapes=[vmem((tile_rows, key_count + LANES), F32)] * 2
+            + [vmem((tile_rows, key_chunk), BF16)] * 2
+            + [vmem((tile_rows, LANES), F32)] * 2
+            + [
                 vmem((plane * rows, LANES), F32),
                 vmem((tile_rows, LANES), jnp.int32),
                 vmem((LANES, HEAD_SIZE), BF16),
@@ -195,7 +222,7 @@
             transcendentals=scored,
         ),
         name="attend",
-    )(info, *q_pieces, keys, values, span_keys, span_values, *after)
+    )(info, *q_arrays, keys_t, values, span_keys, span_values, *after)
 
 
 def combine(parts):
@@ -277,35 +304,43 @@
     )(*pieces, *after)
 
 
-def project_kernel(info, *refs, plane, blocks, rows, heads):
-    ins, w_ref, out = refs[: plane * heads], refs[-2], refs[-1]
-    width = GROUP_QUERIES * HEAD_SIZE
+def project_kernel(info, *refs, plane, blocks, rows, width):
+    ins, (w_ref, *base_ref, out) = refs[:plane], refs[plane:]
     for b in range(plane):
-        acc = None
-        for h in range(heads):
-            x = ins[h * plane + b][...].reshape(blocks * rows, width)
-            y = jnp.dot(x, w_ref[h * width : (h + 1) * width], preferred_element_type=F32)
-            acc = y if acc is None else acc + y
+        x = ins[b][...].reshape(blocks * rows, width)
+        y = jnp.dot(x, w_ref[...], preferred_element_type=F32)
         for a in range(blocks):
-            out[info[3 + blocks + a], b ^ info[1]] = acc[a * rows : (a + 1) * rows].astype(BF16)
-
-
-def project(info, gathered, weight):
-    heads, plane = len(gathered), len(gathered[0])
-    blocks, rows, _ = gathered[0][0].shape
-    vmem = pltpu.MemorySpace.VMEM
+            at = (info[3 + blocks + a], b ^ info[1])
+            part = y[a * rows : (a + 1) * rows]
+            out[at] = ((base_ref[0][at] + part) if base_ref else part).astype(BF16)
+
+
+def project_late(info, pieces, weight, base):
+    plane = len(pieces)
+    blocks, rows, width = pieces[0].shape
+    out_cols = weight.shape[1]
     span = plane * blocks * rows
+    whole = pl.BlockSpec((blocks, rows, width), lambda i, s: (0, 0, 0))
+    out_block = pl.BlockSpec((blocks, plane, rows, out_cols), lambda i, s: (0, 0, 0, 0))
     return pl.pallas_call(
-        functools.partial(project_kernel, plane=plane, blocks=blocks, rows=rows, heads=heads),
-        in_specs=[pl.BlockSpec(memory_space=pltpu.MemorySpace.SMEM)]
-        + [pl.BlockSpec(memory_space=vmem)] * (heads * plane + 1),
-        out_shape=jax.ShapeDtypeStruct((blocks, plane, rows, weight.shape[1]), BF16),
+        functools.partial(project_kernel, plane=plane, blocks=blocks, rows=rows, width=width),
+        grid_spec=pltpu.PrefetchScalarGridSpec(
+            num_scalar_prefetch=1,
+            grid=(1,),
+            in_specs=[whole] * plane
+            + [pl.BlockSpec((width, out_cols), lambda i, s: (weight.shape[0] // width - 1, 0))]
+            + [out_block] * len(base),
+            out_specs=out_block,
+        ),
+        out_shape=jax.ShapeDtypeStruct((blocks, plane, rows, out_cols), BF16),
         compiler_params=pltpu.CompilerParams(vmem_limit_bytes=VMEM_LIMIT),
         cost_estimate=pl.CostEstimate(
-            flops=2 * span * weight.size, bytes_accessed=2 * (weight.size + span * weight.shape[0]), transcendentals=0
+            flops=2 * span * width * out_cols,
+            bytes_accessed=2 * (width * out_cols + span * width),
+            transcendentals=0,
         ),
         name="project",
-    )(info, *[x for per_head in gathered for x in per_head], weight)
+    )(info, *pieces, weight, *[x.reshape(blocks, plane, rows, out_cols) for x in base])
 
 
 def exchange(x, axis, distance):
@@ -339,17 +374,18 @@
     def gather_plane(stack):
         return [stack] + [exchange(stack, "ctx", b) for b in range(1, plane)]
 
-    def head_queries(h):
-        return queries[:, h * width : (h + 1) * width]
-
-    first = stack_blocks(head_queries(0))
-    stacks, pieces = [first], [gather_plane(first)]
-    for h in range(1, heads):
-        held, _ = lax.optimization_barrier((head_queries(h), stacks[h - 1]))
-        stacks.append(stack_blocks(held))
-    for h in range(1, heads):
-        pieces.append(gather_plane(stacks[h]))
-
+    def in_span_order(x):
+        return x.reshape(blocks, plane, rows, x.shape[1])
+
+    first = stack_blocks(queries[:, :width])
+    sources = [(gather_plane(first), 0)]
+    for group in [range(1, 2), range(2, heads)]:
+        if len(group) and group[0] < heads:
+            held, _ = lax.optimization_barrier((queries[:, group[0] * width : (group[-1] + 1) * width], first))
+            whole = in_span_order(lax.all_gather(held, "ctx", axis=0, tiled=True))
+            sources += [([whole], i) for i in range(len(group))]
+
+    keys_t = context_keys.T
     attended, merged, rows_of = [], [], []
 
     def merge(h, after):
@@ -363,7 +399,7 @@
         rows_of.append(normalize_pieces(parts, after))
 
     for h in range(heads):
-        after = stacks[1:] if h == 0 else []
+        after = []
         if h >= 3:
             normalize(h - 3, [attended[h - 1][0]])
             after.append(rows_of[h - 3])
@@ -371,17 +407,32 @@
             merge(h - 2, [attended[h - 1][0]])
             after.append(merged[h - 2][0])
         attended.append(
-            attend_head(info, pieces[h], context_keys, context_values, span_keys, span_values, h, after)
+            attend_head(info, *sources[h], keys_t, context_values, span_keys, span_values, h, after)
         )
-    last = [attended[-1][0]]
+    early = max(heads - 2, 0)
+    spread_rows = {}
+
+    def spread(h):
+        spread_rows[h] = lax.all_gather(rows_of[h], "ctx", axis=0, tiled=True)
+        return spread_rows[h]
+
+    last = [attended[-1][0]] + [spread(h) for h in range(min(early, len(rows_of)))]
     for h in range(heads):
         if h >= len(merged):
             merge(h, last)
         if h >= len(rows_of):
             normalize(h, last)
-    gathered = [gather_plane(stack_blocks(r)) for r in rows_of]
-
-    partial_out = project(info, gathered, out_weight).reshape(ctx_count * rows, -1)
+    base = [
+        jnp.dot(
+            spread_rows[h] if h in spread_rows else spread(h),
+            out_weight[h * width : (h + 1) * width],
+            preferred_element_type=F32,
+        )
+        for h in range(early)
+    ]
+    base = [functools.reduce(jnp.add, base)] if base else []
+    late = gather_plane(stack_blocks(jnp.concatenate(rows_of[early:], axis=1)))
+    partial_out = project_late(info, late, out_weight, base).reshape(ctx_count * rows, -1)
     share = partial_out.shape[0] // head_count
     total = lax.dynamic_slice_in_dim(partial_out, my_head * share, share, 0).astype(F32)
     for d in range(1, head_count):

time: 393 us -> 342 us (0.87); the launches traced: 393 us -> 338 us
  starting transfers between devices: 190 us -> 62.7 us
  waiting for transfers between devices: 33.4 us -> 90 us
  local copies, waits for them, and re-layouts: 4.82 us -> 20.4 us
  Pallas kernels: 156 us -> 141 us
  between operations: 0.62 us -> 13.4 us
  matrix products: 0 us -> 5.16 us
    ppermute x73 -> x37, starting transfers between devices: 190 us -> 62.5 us  [exchange(): return lax.ppermute(x, axis, [(i, i ^ distance) for i in range(count)])]
    all_gather x0 -> x4, waiting for transfers between devices: none -> 33.2 us  [the longest x2 29.1 us: local(): whole = in_span_order(lax.all_gather(held, 'ctx', axis=0, tiled=True))]
    ppermute x73 -> x37, waiting for transfers between devices: 33.4 us -> 56.7 us  [exchange(): return lax.ppermute(x, axis, [(i, i ^ distance) for i in range(count)])]
    pallas_call x4, Pallas kernels: 131 us -> 117 us  [attend_head(): pl.pallas_call(functools.partial(attend_kernel, plane=plane, blocks=block...]
    unnamed x114 -> x79, local copies, waits for them, and re-layouts: 0.94 us -> 14.4 us
    dot_general x0 -> x2, matrix products: none -> 5.16 us  [local(): jnp.dot(spread_rows[h] if h in spread_rows else spread(h), out_weight[h *...]
  transfers between devices with their start and end apart: 73 -> 41, of which waited for: 17 -> 17; matrix products, arithmetic and copies ran while one was open for 2% -> 5% of each run, Pallas kernels for 38% -> 39%
where the time goes in v2:
time: 342 us; the launch traced here: 338 us
  Pallas kernels  141 us (41%)
  waiting for transfers between devices  90 us (26%)
  starting transfers between devices  62.7 us (18%)
  local copies, waits for them, and re-layouts  20.4 us (6%)
  between operations  13.4 us (4%)
  matrix products  5.16 us (2%)
  other arithmetic  5.03 us (1%)
    pallas_call x4, Pallas kernels, attend_head(): pl.pallas_call(functools.partial(attend_kernel, plane=plane, blocks=block...  117 us
    ppermute x37, starting transfers between devices, exchange(): return lax.ppermute(x, axis, [(i, i ^ distance) for i in range(count)])  62.5 us
    ppermute x37, waiting for transfers between devices, exchange(): return lax.ppermute(x, axis, [(i, i ^ distance) for i in range(count)])  56.7 us
    all_gather x2, waiting for transfers between devices, local(): whole = in_span_order(lax.all_gather(held, 'ctx', axis=0, tiled=True))  29.1 us
    unnamed x79, local copies, waits for them, and re-layouts  14.4 us
    pallas_call x4, Pallas kernels, merge_pieces(): pl.pallas_call(functools.partial(merge_kernel, count=len(pieces), waits=l...  10.9 us
    pallas_call x4, Pallas kernels, normalize_pieces(): pl.pallas_call(functools.partial(normalize_kernel, count=len(pieces)), in...  7.58 us
  transfers between devices with their start and end apart: 41, of which 17 were waited for; matrix products, arithmetic and copies ran while one was open for 5% of the time, Pallas kernels for 39%

profile of v2, /device:TPU:0, one launch (start us, length us, event | category | flops | bytes accessed | tf_op | source)
XLA Modules:
  0.0 337.7 jit_solution(18428141606209872444)
XLA Ops:
  6.5 1.5 fusion.5
  8.1 3.0 collective-permute-start
  11.1 2.6 collective-permute-start.1
  13.7 4.7 %collective-permute-done.1 = bf16[32,1024]{1,0:T(8,128)(2,1)S(1)} collective-permute-done((bf16[32,1024]{1,0:T(8,128)(2,1)S(1)}, bf16[32,1024]{1,0:T(8,128)(2,1)S(1)}, u32[]{:S(2)}, u32[]{:S(2)}) %collective-permute-start.1) | collective-permute-done | bytes 65568 | tf_op jit(solution)/shard_map/ppermute | solution.py:348
  18.3 1.4 collective-permute-done.2
  19.9 1.6 slice.15
  21.6 1.6 collective-permute-start.3
  23.1 1.5 collective-permute-start.4
  25.1 0.8 compare_reduce_fusion
  26.6 6.4 %copy.9 = bf16[4096,512]{0,1:T(8,128)(2,1)} copy(bf16[4096,512]{1,0:T(8,128)(2,1)} %param.10) | data formatting | bytes 8388608 | tf_op args[3]
  33.0 0.8 sort.17
  34.5 1.4 concatenate.6.info
  36.8 29.2 %attend.4 = (bf16[4,32,1152]{2,1,0:T(8,128)(2,1)}, bf16[4,32,1152]{2,1,0:T(8,128)(2,1)}, bf16[4,32,1152]{2,1,0:T(8,128)(2,1)}, bf16[4,32,1152]{2,1,0:T(8,128)(2,1)}) custom-call(s32[11]{0:T(128)} %concatenate.6.info, bf16[4,32,1024]{2,1,0:T(8,128)(2,1)} %copy-done.17, bf16[4,32,1024]{2,1,0:T(8,128)(2,1)} %copy-done.36, bf16[4,32,1024]{2,1,0:T(8,128)(2,1)} %copy-done.37, ...), custom_call_target="tpu_custom_call" | custom-call | flops 17179869184 | bytes 4194304 | tf_op jit(solution)/shard_map/attend/pallas_call | solution.py:184
  65.9 1.5 collective-permute-start.6
  67.4 1.5 collective-permute-start.7
  69.4 6.5 %all-gather.7.cloned.1.call-done = bf16[512,1024]{1,0:T(8,128)(2,1)} async-done(((bf16[32,1024]{1,0:T(8,128)(2,1)}), bf16[512,1024]{1,0:T(8,128)(2,1)}) %all-gather.7.cloned.1.call-update) | async-done | bytes 1048592 | tf_op jit(solution)/shard_map/all_gather | solution.py:385
  75.9 29.3 %attend.5 = (bf16[4,32,1152]{2,1,0:T(8,128)(2,1)}, bf16[4,32,1152]{2,1,0:T(8,128)(2,1)}, bf16[4,32,1152]{2,1,0:T(8,128)(2,1)}, bf16[4,32,1152]{2,1,0:T(8,128)(2,1)}) custom-call(s32[11]{0:T(128)} %concatenate.6.info, bf16[4,4,32,1024]{3,2,1,0:T(8,128)(2,1)} %bitcast.37, bf16[512,4096]{1,0:T(8,128)(2,1)} %bitcast.23, bf16[4096,512]{1,0:T(8,128)(2,1)} %refs_2_.5, ...), custom_call_target="tpu_custom_call" | custom-call | flops 17179869184 | bytes 4194304 | tf_op jit(solution)/shard_map/attend/pallas_call | solution.py:184
  106.2 2.7 merge.4
  109.4 8.3 %collective-permute-start.13 = (bf16[32,1152]{1,0:T(8,128)(2,1)}, bf16[32,1152]{1,0:T(8,128)(2,1)S(1)}, u32[]{:S(2)}, u32[]{:S(2)}) collective-permute-start(bf16[32,1152]{1,0:T(8,128)(2,1)} %get-tuple-element.54), channel_id=1, source_target_pairs={{0,16},{2,18},{4,20},{6,22},{8,24},{10,26},{12,28},{14,30},{16,0},... | collective-permute-start | bytes 221192 | tf_op jit(solution)/shard_map/ppermute | solution.py:348
  117.7 22.6 %all-gather.5.cloned.1.call-done = bf16[512,2048]{1,0:T(8,128)(2,1)} async-done(((bf16[32,2048]{1,0:T(8,128)(2,1)}), bf16[512,2048]{1,0:T(8,128)(2,1)}) %all-gather.5.cloned.1.call-update) | async-done | bytes 2097168 | tf_op jit(solution)/shard_map/all_gather | solution.py:385
  140.2 29.3 %attend.6 = (bf16[4,32,1152]{2,1,0:T(8,128)(2,1)}, bf16[4,32,1152]{2,1,0:T(8,128)(2,1)}, bf16[4,32,1152]{2,1,0:T(8,128)(2,1)}, bf16[4,32,1152]{2,1,0:T(8,128)(2,1)}) custom-call(s32[11]{0:T(128)} %concatenate.6.info, bf16[4,4,32,2048]{3,2,1,0:T(8,128)(2,1)} %bitcast.35, bf16[512,4096]{1,0:T(8,128)(2,1)} %bitcast.24, bf16[4096,512]{1,0:T(8,128)(2,1)} %refs_2_.5, ...), custom_call_target="tpu_custom_call" | custom-call | flops 17179869184 | bytes 4194304 | tf_op jit(solution)/shard_map/attend/pallas_call | solution.py:184
  170.2 1.9 normalize.4.refs_5_
  172.2 1.3 collective-permute-start.15
  174.3 1.5 collective-permute-start.17
  175.7 6.5 %collective-permute-done.15.refs_1_ = bf16[4,32,1152]{2,1,0:T(8,128)(2,1)S(1)} collective-permute-done((bf16[4,32,1152]{2,1,0:T(8,128)(2,1)S(1)}, bf16[4,32,1152]{2,1,0:T(8,128)(2,1)S(1)}, u32[]{:S(2)}, u32[]{:S(2)}) %collective-permute-start.15) | collective-permute-done | bytes 294944 | tf_op jit(solution)/shard_map/ppermute | solution.py:348
  182.2 4.0 %collective-permute-done.16.refs_2_ = bf16[4,32,1152]{2,1,0:T(8,128)(2,1)S(1)} collective-permute-done((bf16[4,32,1152]{2,1,0:T(8,128)(2,1)S(1)}, bf16[4,32,1152]{2,1,0:T(8,128)(2,1)S(1)}, u32[]{:S(2)}, u32[]{:S(2)}) %collective-permute-start.16) | collective-permute-done | bytes 294944 | tf_op jit(solution)/shard_map/ppermute | solution.py:348
  186.2 1.7 collective-permute-done.17.refs_3_
  188.6 2.7 merge.5
  191.3 8.7 %collective-permute-start.33 = (bf16[32,1152]{1,0:T(8,128)(2,1)}, bf16[32,1152]{1,0:T(8,128)(2,1)S(1)}, u32[]{:S(2)}, u32[]{:S(2)}) collective-permute-start(bf16[32,1152]{1,0:T(8,128)(2,1)} %get-tuple-element.72), channel_id=1, source_target_pairs={{0,8},{2,10},{4,12},{6,14},{8,0},{10,2},{12,4},{14,6},{16,24},{18,... | collective-permute-start | bytes 221192 | tf_op jit(solution)/shard_map/ppermute | solution.py:348
  200.4 1.9 collective-permute-start.35
  202.4 29.5 %attend.7 = (bf16[4,32,1152]{2,1,0:T(8,128)(2,1)}, bf16[4,32,1152]{2,1,0:T(8,128)(2,1)}, bf16[4,32,1152]{2,1,0:T(8,128)(2,1)}, bf16[4,32,1152]{2,1,0:T(8,128)(2,1)}) custom-call(s32[11]{0:T(128)} %concatenate.6.info, bf16[4,4,32,2048]{3,2,1,0:T(8,128)(2,1)} %bitcast.36, bf16[512,4096]{1,0:T(8,128)(2,1)} %bitcast.25, bf16[4096,512]{1,0:T(8,128)(2,1)} %refs_2_.5, ...), custom_call_target="tpu_custom_call" | custom-call | flops 17179869184 | bytes 4194304 | tf_op jit(solution)/shard_map/attend/pallas_call | solution.py:184
  231.9 4.1 %all-gather.9.cloned.1.call-done.refs_5_ = bf16[512,1024]{1,0:T(8,128)(2,1)} async-done(((bf16[32,1024]{1,0:T(8,128)(2,1)}), bf16[512,1024]{1,0:T(8,128)(2,1)}) %all-gather.9.cloned.1.call-update) | async-done | bytes 1048592 | tf_op jit(solution)/shard_map/all_gather | solution.py:416
  236.0 1.9 normalize.7
  238.0 1.5 collective-permute-start.10
  239.5 1.4 collective-permute-start.11
  241.5 1.4 collective-permute-start.21
  243.5 11.0 %collective-permute-done.10.refs_2_ = bf16[4,32,1152]{2,1,0:T(8,128)(2,1)S(1)} collective-permute-done((bf16[4,32,1152]{2,1,0:T(8,128)(2,1)S(1)}, bf16[4,32,1152]{2,1,0:T(8,128)(2,1)S(1)}, u32[]{:S(2)}, u32[]{:S(2)}) %collective-permute-start.10) | collective-permute-done | bytes 294944 | tf_op jit(solution)/shard_map/ppermute | solution.py:348
  254.5 1.4 collective-permute-start.23
  257.4 2.7 merge.6
  260.1 1.4 collective-permute-start.18
  261.5 3.3 collective-permute-start.19
  264.8 2.3 collective-permute-start.20
  268.6 2.7 merge.7
  271.7 2.9 collective-permute-start.25
  274.6 1.1 collective-permute-start.26
  276.3 1.9 normalize.5
  278.8 2.2 collective-permute-done.26.refs_3_
  281.6 1.9 normalize.6
  283.5 0.9 fusion.4
  284.5 1.7 collective-permute-start.28
  286.2 2.7 collective-permute-start.29
  288.8 6.7 %collective-permute-done.27 = bf16[32,2048]{1,0:T(8,128)(2,1)S(1)} collective-permute-done((bf16[32,2048]{1,0:T(8,128)(2,1)S(1)}, bf16[32,2048]{1,0:T(8,128)(2,1)S(1)}, u32[]{:S(2)}, u32[]{:S(2)}) %collective-permute-start.27) | collective-permute-done | bytes 131104 | tf_op jit(solution)/shard_map/ppermute | solution.py:348
  295.6 4.1 %collective-permute-done.28 = bf16[32,2048]{1,0:T(8,128)(2,1)S(1)} collective-permute-done((bf16[32,2048]{1,0:T(8,128)(2,1)S(1)}, bf16[32,2048]{1,0:T(8,128)(2,1)S(1)}, u32[]{:S(2)}, u32[]{:S(2)}) %collective-permute-start.28) | collective-permute-done | bytes 131104 | tf_op jit(solution)/shard_map/ppermute | solution.py:348
  300.4 1.1 collective-permute-start.31
  301.5 1.8 collective-permute-start.32
  303.3 2.2 fusion
  305.6 2.9 convolution_add_fusion
  308.5 6.2 %collective-permute-done.30.refs_1_ = bf16[4,32,2048]{2,1,0:T(8,128)(2,1)S(1)} collective-permute-done((bf16[4,32,2048]{2,1,0:T(8,128)(2,1)S(1)}, bf16[4,32,2048]{2,1,0:T(8,128)(2,1)S(1)}, u32[]{:S(2)}, u32[]{:S(2)}) %collective-permute-start.30) | collective-permute-done | bytes 524320 | tf_op jit(solution)/shard_map/ppermute | solution.py:348
  314.7 5.9 %collective-permute-done.31.refs_2_ = bf16[4,32,2048]{2,1,0:T(8,128)(2,1)S(1)} collective-permute-done((bf16[4,32,2048]{2,1,0:T(8,128)(2,1)S(1)}, bf16[4,32,2048]{2,1,0:T(8,128)(2,1)S(1)}, u32[]{:S(2)}, u32[]{:S(2)}) %collective-permute-start.31) | collective-permute-done | bytes 524320 | tf_op jit(solution)/shard_map/ppermute | solution.py:348
  320.6 0.8 copy-done.3
  321.6 5.2 %project.1 = bf16[4,4,32,512]{3,2,1,0:T(8,128)(2,1)} custom-call(s32[11]{0:T(128)} %concatenate.6.info, bf16[4,32,2048]{2,1,0:T(8,128)(2,1)} %copy-done.1, bf16[4,32,2048]{2,1,0:T(8,128)(2,1)} %copy-done.2, bf16[4,32,2048]{2,1,0:T(8,128)(2,1)} %copy-done.3, bf16[4,32,2048]{2,1,0:T(8,128)(2,1)} %copy-done.4, bf16[4096,512]{1,0:T(8,128)(2,1)} %refs_4_.7, ...), custom_call_target="tpu_custom_call" | custom-call | flops 1073741824 | bytes 4194304 | tf_op jit(solution)/shard_map/project/pallas_call | solution.py:325
  326.8 1.0 constant_dynamic-slice_fusion
  327.9 1.5 collective-permute-done.36
  329.4 1.7 add_convert_fusion
  (133 shorter events, 14.9 us)
Async XLA Ops:
  6.5 69.4 %all-gather.7.cloned.1.call-start = ((), (), s32[]{:S(2)}) async-start(), calls=%async_computation.1 | async-start | bytes 1114112 | tf_op jit(solution)/shard_map/all_gather | solution.py:385
  8.1 5.6 %collective-permute-start = (bf16[32,1024]{1,0:T(8,128)(2,1)S(1)}, bf16[32,1024]{1,0:T(8,128)(2,1)S(1)}, u32[]{:S(2)}, u32[]{:S(2)}) collective-permute-start(bf16[32,1024]{1,0:T(8,128)(2,1)S(1)} %get-tuple-element.77), channel_id=1, source_target_pairs={{0,8},{2,10},{4,12},{6,14},{8,0},{10,2},{12,4},{14,6},{16,24},{18,... | collective-permute-start | bytes 196616 | tf_op jit(solution)/shard_map/ppermute | solution.py:348
  11.1 7.3 %collective-permute-start.1 = (bf16[32,1024]{1,0:T(8,128)(2,1)S(1)}, bf16[32,1024]{1,0:T(8,128)(2,1)S(1)}, u32[]{:S(2)}, u32[]{:S(2)}) collective-permute-start(bf16[32,1024]{1,0:T(8,128)(2,1)S(1)} %get-tuple-element.77), channel_id=1, source_target_pairs={{0,16},{2,18},{4,20},{6,22},{8,24},{10,26},{12,28},{14,30},{16,0},... | collective-permute-start | bytes 196616 | tf_op jit(solution)/shard_map/ppermute | solution.py:348
  13.7 6.1 %collective-permute-start.2 = (bf16[32,1024]{1,0:T(8,128)(2,1)S(1)}, bf16[32,1024]{1,0:T(8,128)(2,1)S(1)}, u32[]{:S(2)}, u32[]{:S(2)}) collective-permute-start(bf16[32,1024]{1,0:T(8,128)(2,1)S(1)} %get-tuple-element.77), channel_id=1, source_target_pairs={{0,24},{2,26},{4,28},{6,30},{8,16},{10,18},{12,20},{14,22},{16,8},... | collective-permute-start | bytes 196616 | tf_op jit(solution)/shard_map/ppermute | solution.py:348
  19.8 13.2 %copy-start.17 = (bf16[4,32,1024]{2,1,0:T(8,128)(2,1)}, bf16[4,32,1024]{2,1,0:T(8,128)(2,1)S(1)}, u32[]{:S(2)}) copy-start(bf16[4,32,1024]{2,1,0:T(8,128)(2,1)S(1)} %pad_maximum_fusion.1.refs_0_) | copy-start | bytes 786436
  19.8 120.4 %all-gather.5.cloned.1.call-start = ((), (), s32[]{:S(2)}) async-start(), calls=%async_computation | async-start | bytes 2228224 | tf_op jit(solution)/shard_map/all_gather | solution.py:385
  21.5 214.5 %all-gather.9.cloned.1.call-start = ((), (), s32[]{:S(2)}) async-start(), calls=%async_computation.2 | async-start | bytes 1114112 | tf_op jit(solution)/shard_map/all_gather | solution.py:416
  21.6 14.3 %collective-permute-start.3 = (bf16[4,32,1024]{2,1,0:T(8,128)(2,1)S(1)}, bf16[4,32,1024]{2,1,0:T(8,128)(2,1)S(1)}, u32[]{:S(2)}, u32[]{:S(2)}) collective-permute-start(bf16[4,32,1024]{2,1,0:T(8,128)(2,1)S(1)} %pad_maximum_fusion.1.refs_0_), channel_id=1, source_target_pairs={{0,2},{2,0},{4,6},{6,4},{8,10},{10,8},{12,14},{14,12},{16,18},{18,... | collective-permute-start | bytes 786440 | tf_op jit(solution)/shard_map/ppermute | solution.py:348
  23.1 12.7 %collective-permute-start.4 = (bf16[4,32,1024]{2,1,0:T(8,128)(2,1)S(1)}, bf16[4,32,1024]{2,1,0:T(8,128)(2,1)S(1)}, u32[]{:S(2)}, u32[]{:S(2)}) collective-permute-start(bf16[4,32,1024]{2,1,0:T(8,128)(2,1)S(1)} %pad_maximum_fusion.1.refs_0_), channel_id=1, source_target_pairs={{0,4},{2,6},{4,0},{6,2},{8,12},{10,14},{12,8},{14,10},{16,20},{18,... | collective-permute-start | bytes 786440 | tf_op jit(solution)/shard_map/ppermute | solution.py:348
  24.6 11.2 %collective-permute-start.5 = (bf16[4,32,1024]{2,1,0:T(8,128)(2,1)S(1)}, bf16[4,32,1024]{2,1,0:T(8,128)(2,1)S(1)}, u32[]{:S(2)}, u32[]{:S(2)}) collective-permute-start(bf16[4,32,1024]{2,1,0:T(8,128)(2,1)S(1)} %pad_maximum_fusion.1.refs_0_), channel_id=1, source_target_pairs={{0,6},{2,4},{4,2},{6,0},{8,14},{10,12},{12,10},{14,8},{16,22},{18,... | collective-permute-start | bytes 786440 | tf_op jit(solution)/shard_map/ppermute | solution.py:348
  35.9 0.9 copy-start.38
  65.9 39.3 %collective-permute-start.6 = (bf16[4,32,1152]{2,1,0:T(8,128)(2,1)}, bf16[4,32,1152]{2,1,0:T(8,128)(2,1)S(1)}, u32[]{:S(2)}, u32[]{:S(2)}) collective-permute-start(bf16[4,32,1152]{2,1,0:T(8,128)(2,1)} %get-tuple-element.43), channel_id=1, source_target_pairs={{0,2},{2,0},{4,6},{6,4},{8,10},{10,8},{12,14},{14,12},{16,18},{18,... | collective-permute-start | bytes 884744 | tf_op jit(solution)/shard_map/ppermute | solution.py:348
  67.4 37.8 %collective-permute-start.7 = (bf16[4,32,1152]{2,1,0:T(8,128)(2,1)}, bf16[4,32,1152]{2,1,0:T(8,128)(2,1)S(1)}, u32[]{:S(2)}, u32[]{:S(2)}) collective-permute-start(bf16[4,32,1152]{2,1,0:T(8,128)(2,1)} %get-tuple-element.44), channel_id=1, source_target_pairs={{0,4},{2,6},{4,0},{6,2},{8,12},{10,14},{12,8},{14,10},{16,20},{18,... | collective-permute-start | bytes 884744 | tf_op jit(solution)/shard_map/ppermute | solution.py:348
  68.9 36.3 %collective-permute-start.8 = (bf16[4,32,1152]{2,1,0:T(8,128)(2,1)}, bf16[4,32,1152]{2,1,0:T(8,128)(2,1)S(1)}, u32[]{:S(2)}, u32[]{:S(2)}) collective-permute-start(bf16[4,32,1152]{2,1,0:T(8,128)(2,1)} %get-tuple-element.45), channel_id=1, source_target_pairs={{0,6},{2,4},{4,2},{6,0},{8,14},{10,12},{12,10},{14,8},{16,22},{18,... | collective-permute-start | bytes 884744 | tf_op jit(solution)/shard_map/ppermute | solution.py:348
  105.3 0.9 copy-start.13
  108.9 60.6 %collective-permute-start.12 = (bf16[32,1152]{1,0:T(8,128)(2,1)}, bf16[32,1152]{1,0:T(8,128)(2,1)S(1)}, u32[]{:S(2)}, u32[]{:S(2)}) collective-permute-start(bf16[32,1152]{1,0:T(8,128)(2,1)} %get-tuple-element.53), channel_id=1, source_target_pairs={{0,8},{2,10},{4,12},{6,14},{8,0},{10,2},{12,4},{14,6},{16,24},{18,... | collective-permute-start | bytes 221192 | tf_op jit(solution)/shard_map/ppermute | solution.py:348
  109.4 60.1 %collective-permute-start.13 = (bf16[32,1152]{1,0:T(8,128)(2,1)}, bf16[32,1152]{1,0:T(8,128)(2,1)S(1)}, u32[]{:S(2)}, u32[]{:S(2)}) collective-permute-start(bf16[32,1152]{1,0:T(8,128)(2,1)} %get-tuple-element.54), channel_id=1, source_target_pairs={{0,16},{2,18},{4,20},{6,22},{8,24},{10,26},{12,28},{14,30},{16,0},... | collective-permute-start | bytes 221192 | tf_op jit(solution)/shard_map/ppermute | solution.py:348
  117.6 51.9 %collective-permute-start.14 = (bf16[32,1152]{1,0:T(8,128)(2,1)}, bf16[32,1152]{1,0:T(8,128)(2,1)S(1)}, u32[]{:S(2)}, u32[]{:S(2)}) collective-permute-start(bf16[32,1152]{1,0:T(8,128)(2,1)} %get-tuple-element.55), channel_id=1, source_target_pairs={{0,24},{2,26},{4,28},{6,30},{8,16},{10,18},{12,20},{14,22},{16,8},... | collective-permute-start | bytes 221192 | tf_op jit(solution)/shard_map/ppermute | solution.py:348
  140.2 32.0 %copy-start.35 = (bf16[4,32,1152]{2,1,0:T(8,128)(2,1)S(1)}, bf16[4,32,1152]{2,1,0:T(8,128)(2,1)}, u32[]{:S(2)}) copy-start(bf16[4,32,1152]{2,1,0:T(8,128)(2,1)} %get-tuple-element.56) | copy-start | bytes 884740
  140.2 33.3 %copy-start.34 = (bf16[4,32,1152]{2,1,0:T(8,128)(2,1)S(1)}, bf16[4,32,1152]{2,1,0:T(8,128)(2,1)}, u32[]{:S(2)}) copy-start(bf16[4,32,1152]{2,1,0:T(8,128)(2,1)} %get-tuple-element.57) | copy-start | bytes 884740
  140.2 34.1 %copy-start.33 = (bf16[4,32,1152]{2,1,0:T(8,128)(2,1)S(1)}, bf16[4,32,1152]{2,1,0:T(8,128)(2,1)}, u32[]{:S(2)}) copy-start(bf16[4,32,1152]{2,1,0:T(8,128)(2,1)} %get-tuple-element.58) | copy-start | bytes 884740
  172.1 131.2 %all-gather.11.cloned.1.call-start = ((), (), s32[]{:S(2)}) async-start(), calls=%async_computation.3 | async-start | bytes 1114112 | tf_op jit(solution)/shard_map/all_gather | solution.py:416
  172.2 10.0 %collective-permute-start.15 = (bf16[4,32,1152]{2,1,0:T(8,128)(2,1)S(1)}, bf16[4,32,1152]{2,1,0:T(8,128)(2,1)S(1)}, u32[]{:S(2)}, u32[]{:S(2)}) collective-permute-start(bf16[4,32,1152]{2,1,0:T(8,128)(2,1)S(1)} %copy-done.35), channel_id=1, source_target_pairs={{0,2},{2,0},{4,6},{6,4},{8,10},{10,8},{12,14},{14,12},{16,18},{18,... | collective-permute-start | bytes 884744 | tf_op jit(solution)/shard_map/ppermute | solution.py:348
  173.5 12.6 %collective-permute-start.16 = (bf16[4,32,1152]{2,1,0:T(8,128)(2,1)S(1)}, bf16[4,32,1152]{2,1,0:T(8,128)(2,1)S(1)}, u32[]{:S(2)}, u32[]{:S(2)}) collective-permute-start(bf16[4,32,1152]{2,1,0:T(8,128)(2,1)S(1)} %copy-done.34), channel_id=1, source_target_pairs={{0,4},{2,6},{4,0},{6,2},{8,12},{10,14},{12,8},{14,10},{16,20},{18,... | collective-permute-start | bytes 884744 | tf_op jit(solution)/shard_map/ppermute | solution.py:348
  174.3 13.6 %collective-permute-start.17 = (bf16[4,32,1152]{2,1,0:T(8,128)(2,1)S(1)}, bf16[4,32,1152]{2,1,0:T(8,128)(2,1)S(1)}, u32[]{:S(2)}, u32[]{:S(2)}) collective-permute-start(bf16[4,32,1152]{2,1,0:T(8,128)(2,1)S(1)} %copy-done.33), channel_id=1, source_target_pairs={{0,6},{2,4},{4,2},{6,0},{8,14},{10,12},{12,10},{14,8},{16,22},{18,... | collective-permute-start | bytes 884744 | tf_op jit(solution)/shard_map/ppermute | solution.py:348
  182.2 5.7 %copy-start.14 = (bf16[4,32,1152]{2,1,0:T(8,128)(2,1)}, bf16[4,32,1152]{2,1,0:T(8,128)(2,1)S(1)}, u32[]{:S(2)}) copy-start(bf16[4,32,1152]{2,1,0:T(8,128)(2,1)S(1)} %collective-permute-done.15.refs_1_) | copy-start | bytes 884740
  186.2 1.7 copy-start.15
  191.3 40.6 %collective-permute-start.33 = (bf16[32,1152]{1,0:T(8,128)(2,1)}, bf16[32,1152]{1,0:T(8,128)(2,1)S(1)}, u32[]{:S(2)}, u32[]{:S(2)}) collective-permute-start(bf16[32,1152]{1,0:T(8,128)(2,1)} %get-tuple-element.72), channel_id=1, source_target_pairs={{0,8},{2,10},{4,12},{6,14},{8,0},{10,2},{12,4},{14,6},{16,24},{18,... | collective-permute-start | bytes 221192 | tf_op jit(solution)/shard_map/ppermute | solution.py:348
  200.0 31.9 %collective-permute-start.34 = (bf16[32,1152]{1,0:T(8,128)(2,1)}, bf16[32,1152]{1,0:T(8,128)(2,1)S(1)}, u32[]{:S(2)}, u32[]{:S(2)}) collective-permute-start(bf16[32,1152]{1,0:T(8,128)(2,1)} %get-tuple-element.73), channel_id=1, source_target_pairs={{0,16},{2,18},{4,20},{6,22},{8,24},{10,26},{12,28},{14,30},{16,0},... | collective-permute-start | bytes 221192 | tf_op jit(solution)/shard_map/ppermute | solution.py:348
  200.4 31.5 %collective-permute-start.35 = (bf16[32,1152]{1,0:T(8,128)(2,1)}, bf16[32,1152]{1,0:T(8,128)(2,1)S(1)}, u32[]{:S(2)}, u32[]{:S(2)}) collective-permute-start(bf16[32,1152]{1,0:T(8,128)(2,1)} %get-tuple-element.74), channel_id=1, source_target_pairs={{0,24},{2,26},{4,28},{6,30},{8,16},{10,18},{12,20},{14,22},{16,8},... | collective-permute-start | bytes 221192 | tf_op jit(solution)/shard_map/ppermute | solution.py:348
  202.4 35.6 %copy-start.32 = (bf16[4,32,1152]{2,1,0:T(8,128)(2,1)S(1)}, bf16[4,32,1152]{2,1,0:T(8,128)(2,1)}, u32[]{:S(2)}) copy-start(bf16[4,32,1152]{2,1,0:T(8,128)(2,1)} %get-tuple-element.51) | copy-start | bytes 884740
  202.4 37.1 %copy-start.31 = (bf16[4,32,1152]{2,1,0:T(8,128)(2,1)S(1)}, bf16[4,32,1152]{2,1,0:T(8,128)(2,1)}, u32[]{:S(2)}) copy-start(bf16[4,32,1152]{2,1,0:T(8,128)(2,1)} %get-tuple-element.52) | copy-start | bytes 884740
  202.4 38.6 %copy-start.30 = (bf16[4,32,1152]{2,1,0:T(8,128)(2,1)S(1)}, bf16[4,32,1152]{2,1,0:T(8,128)(2,1)}, u32[]{:S(2)}) copy-start(bf16[4,32,1152]{2,1,0:T(8,128)(2,1)} %get-tuple-element.50) | copy-start | bytes 884740
  231.9 4.2 %copy-start.26 = (bf16[32,1152]{1,0:T(8,128)(2,1)}, bf16[32,1152]{1,0:T(8,128)(2,1)S(1)}, u32[]{:S(2)}) copy-start(bf16[32,1152]{1,0:T(8,128)(2,1)S(1)} %collective-permute-done.33.refs_1_) | copy-start | bytes 221188
  231.9 4.2 %copy-start.28 = (bf16[32,1152]{1,0:T(8,128)(2,1)}, bf16[32,1152]{1,0:T(8,128)(2,1)S(1)}, u32[]{:S(2)}) copy-start(bf16[32,1152]{1,0:T(8,128)(2,1)S(1)} %collective-permute-done.34.refs_2_) | copy-start | bytes 221188
  231.9 4.1 %copy-start.29 = (bf16[32,1152]{1,0:T(8,128)(2,1)}, bf16[32,1152]{1,0:T(8,128)(2,1)S(1)}, u32[]{:S(2)}) copy-start(bf16[32,1152]{1,0:T(8,128)(2,1)S(1)} %collective-permute-done.35.refs_3_) | copy-start | bytes 221188
  238.0 16.5 %collective-permute-start.10 = (bf16[4,32,1152]{2,1,0:T(8,128)(2,1)S(1)}, bf16[4,32,1152]{2,1,0:T(8,128)(2,1)S(1)}, u32[]{:S(2)}, u32[]{:S(2)}) collective-permute-start(bf16[4,32,1152]{2,1,0:T(8,128)(2,1)S(1)} %copy-done.32), channel_id=1, source_target_pairs={{0,4},{2,6},{4,0},{6,2},{8,12},{10,14},{12,8},{14,10},{16,20},{18,... | collective-permute-start | bytes 884744 | tf_op jit(solution)/shard_map/ppermute | solution.py:348
  239.5 16.5 %collective-permute-start.11 = (bf16[4,32,1152]{2,1,0:T(8,128)(2,1)S(1)}, bf16[4,32,1152]{2,1,0:T(8,128)(2,1)S(1)}, u32[]{:S(2)}, u32[]{:S(2)}) collective-permute-start(bf16[4,32,1152]{2,1,0:T(8,128)(2,1)S(1)} %copy-done.31), channel_id=1, source_target_pairs={{0,6},{2,4},{4,2},{6,0},{8,14},{10,12},{12,10},{14,8},{16,22},{18,... | collective-permute-start | bytes 884744 | tf_op jit(solution)/shard_map/ppermute | solution.py:348
  240.9 15.3 %collective-permute-start.9 = (bf16[4,32,1152]{2,1,0:T(8,128)(2,1)S(1)}, bf16[4,32,1152]{2,1,0:T(8,128)(2,1)S(1)}, u32[]{:S(2)}, u32[]{:S(2)}) collective-permute-start(bf16[4,32,1152]{2,1,0:T(8,128)(2,1)S(1)} %copy-done.30), channel_id=1, source_target_pairs={{0,2},{2,0},{4,6},{6,4},{8,10},{10,8},{12,14},{14,12},{16,18},{18,... | collective-permute-start | bytes 884744 | tf_op jit(solution)/shard_map/ppermute | solution.py:348
  241.5 23.3 %collective-permute-start.21 = (bf16[4,32,1152]{2,1,0:T(8,128)(2,1)}, bf16[4,32,1152]{2,1,0:T(8,128)(2,1)S(1)}, u32[]{:S(2)}, u32[]{:S(2)}) collective-permute-start(bf16[4,32,1152]{2,1,0:T(8,128)(2,1)} %get-tuple-element.65), channel_id=1, source_target_pairs={{0,2},{2,0},{4,6},{6,4},{8,10},{10,8},{12,14},{14,12},{16,18},{18,... | collective-permute-start | bytes 884744 | tf_op jit(solution)/shard_map/ppermute | solution.py:348
  243.0 24.2 %collective-permute-start.22 = (bf16[4,32,1152]{2,1,0:T(8,128)(2,1)}, bf16[4,32,1152]{2,1,0:T(8,128)(2,1)S(1)}, u32[]{:S(2)}, u32[]{:S(2)}) collective-permute-start(bf16[4,32,1152]{2,1,0:T(8,128)(2,1)} %get-tuple-element.66), channel_id=1, source_target_pairs={{0,4},{2,6},{4,0},{6,2},{8,12},{10,14},{12,8},{14,10},{16,20},{18,... | collective-permute-start | bytes 884744 | tf_op jit(solution)/shard_map/ppermute | solution.py:348
  254.5 1.7 copy-start.8
  254.5 12.6 %collective-permute-start.23 = (bf16[4,32,1152]{2,1,0:T(8,128)(2,1)}, bf16[4,32,1152]{2,1,0:T(8,128)(2,1)S(1)}, u32[]{:S(2)}, u32[]{:S(2)}) collective-permute-start(bf16[4,32,1152]{2,1,0:T(8,128)(2,1)} %get-tuple-element.67), channel_id=1, source_target_pairs={{0,6},{2,4},{4,2},{6,0},{8,14},{10,12},{12,10},{14,8},{16,22},{18,... | collective-permute-start | bytes 884744 | tf_op jit(solution)/shard_map/ppermute | solution.py:348
  260.1 14.5 %collective-permute-start.18 = (bf16[32,1152]{1,0:T(8,128)(2,1)}, bf16[32,1152]{1,0:T(8,128)(2,1)S(1)}, u32[]{:S(2)}, u32[]{:S(2)}) collective-permute-start(bf16[32,1152]{1,0:T(8,128)(2,1)} %get-tuple-element.62), channel_id=1, source_target_pairs={{0,8},{2,10},{4,12},{6,14},{8,0},{10,2},{12,4},{14,6},{16,24},{18,... | collective-permute-start | bytes 221192 | tf_op jit(solution)/shard_map/ppermute | solution.py:348
  261.5 14.1 %collective-permute-start.19 = (bf16[32,1152]{1,0:T(8,128)(2,1)}, bf16[32,1152]{1,0:T(8,128)(2,1)S(1)}, u32[]{:S(2)}, u32[]{:S(2)}) collective-permute-start(bf16[32,1152]{1,0:T(8,128)(2,1)} %get-tuple-element.63), channel_id=1, source_target_pairs={{0,16},{2,18},{4,20},{6,22},{8,24},{10,26},{12,28},{14,30},{16,0},... | collective-permute-start | bytes 221192 | tf_op jit(solution)/shard_map/ppermute | solution.py:348
  264.8 2.3 copy-start.5
  264.8 10.9 %collective-permute-start.20 = (bf16[32,1152]{1,0:T(8,128)(2,1)}, bf16[32,1152]{1,0:T(8,128)(2,1)S(1)}, u32[]{:S(2)}, u32[]{:S(2)}) collective-permute-start(bf16[32,1152]{1,0:T(8,128)(2,1)} %get-tuple-element.64), channel_id=1, source_target_pairs={{0,24},{2,26},{4,28},{6,30},{8,16},{10,18},{12,20},{14,22},{16,8},... | collective-permute-start | bytes 221192 | tf_op jit(solution)/shard_map/ppermute | solution.py:348
  271.3 34.3 %copy-start = (bf16[512,1024]{1,0:T(8,128)(2,1)S(1)}, bf16[512,1024]{1,0:T(8,128)(2,1)}, u32[]{:S(2)}) copy-start(bf16[512,1024]{1,0:T(8,128)(2,1)} %all-gather.9.cloned.1.call-done.refs_5_) | copy-start | bytes 3145732
  271.3 7.0 %collective-permute-start.24 = (bf16[32,1152]{1,0:T(8,128)(2,1)}, bf16[32,1152]{1,0:T(8,128)(2,1)S(1)}, u32[]{:S(2)}, u32[]{:S(2)}) collective-permute-start(bf16[32,1152]{1,0:T(8,128)(2,1)} %get-tuple-element.69), channel_id=1, source_target_pairs={{0,8},{2,10},{4,12},{6,14},{8,0},{10,2},{12,4},{14,6},{16,24},{18,... | collective-permute-start | bytes 221192 | tf_op jit(solution)/shard_map/ppermute | solution.py:348
  271.7 7.1 %collective-permute-start.25 = (bf16[32,1152]{1,0:T(8,128)(2,1)}, bf16[32,1152]{1,0:T(8,128)(2,1)S(1)}, u32[]{:S(2)}, u32[]{:S(2)}) collective-permute-start(bf16[32,1152]{1,0:T(8,128)(2,1)} %get-tuple-element.70), channel_id=1, source_target_pairs={{0,16},{2,18},{4,20},{6,22},{8,24},{10,26},{12,28},{14,30},{16,0},... | collective-permute-start | bytes 221192 | tf_op jit(solution)/shard_map/ppermute | solution.py:348
  274.6 1.1 copy-start.21
  274.6 6.4 %collective-permute-start.26 = (bf16[32,1152]{1,0:T(8,128)(2,1)}, bf16[32,1152]{1,0:T(8,128)(2,1)S(1)}, u32[]{:S(2)}, u32[]{:S(2)}) collective-permute-start(bf16[32,1152]{1,0:T(8,128)(2,1)} %get-tuple-element.71), channel_id=1, source_target_pairs={{0,24},{2,26},{4,28},{6,30},{8,16},{10,18},{12,20},{14,22},{16,8},... | collective-permute-start | bytes 221192 | tf_op jit(solution)/shard_map/ppermute | solution.py:348
  278.2 2.7 copy-start.24
  278.8 2.2 copy-start.25
  284.4 11.2 %collective-permute-start.27 = (bf16[32,2048]{1,0:T(8,128)(2,1)S(1)}, bf16[32,2048]{1,0:T(8,128)(2,1)S(1)}, u32[]{:S(2)}, u32[]{:S(2)}) collective-permute-start(bf16[32,2048]{1,0:T(8,128)(2,1)S(1)} %get-tuple-element.79), channel_id=1, source_target_pairs={{0,8},{2,10},{4,12},{6,14},{8,0},{10,2},{12,4},{14,6},{16,24},{18,... | collective-permute-start | bytes 393224 | tf_op jit(solution)/shard_map/ppermute | solution.py:348
  284.5 15.2 %collective-permute-start.28 = (bf16[32,2048]{1,0:T(8,128)(2,1)S(1)}, bf16[32,2048]{1,0:T(8,128)(2,1)S(1)}, u32[]{:S(2)}, u32[]{:S(2)}) collective-permute-start(bf16[32,2048]{1,0:T(8,128)(2,1)S(1)} %get-tuple-element.79), channel_id=1, source_target_pairs={{0,16},{2,18},{4,20},{6,22},{8,24},{10,26},{12,28},{14,30},{16,0},... | collective-permute-start | bytes 393224 | tf_op jit(solution)/shard_map/ppermute | solution.py:348
  286.2 13.5 %collective-permute-start.29 = (bf16[32,2048]{1,0:T(8,128)(2,1)S(1)}, bf16[32,2048]{1,0:T(8,128)(2,1)S(1)}, u32[]{:S(2)}, u32[]{:S(2)}) collective-permute-start(bf16[32,2048]{1,0:T(8,128)(2,1)S(1)} %get-tuple-element.79), channel_id=1, source_target_pairs={{0,24},{2,26},{4,28},{6,30},{8,16},{10,18},{12,20},{14,22},{16,8},... | collective-permute-start | bytes 393224 | tf_op jit(solution)/shard_map/ppermute | solution.py:348
  299.7 20.9 %copy-start.1 = (bf16[4,32,2048]{2,1,0:T(8,128)(2,1)}, bf16[4,32,2048]{2,1,0:T(8,128)(2,1)S(1)}, u32[]{:S(2)}) copy-start(bf16[4,32,2048]{2,1,0:T(8,128)(2,1)S(1)} %pad_maximum_fusion.refs_0_) | copy-start | bytes 1572868
  299.8 14.9 %collective-permute-start.30 = (bf16[4,32,2048]{2,1,0:T(8,128)(2,1)S(1)}, bf16[4,32,2048]{2,1,0:T(8,128)(2,1)S(1)}, u32[]{:S(2)}, u32[]{:S(2)}) collective-permute-start(bf16[4,32,2048]{2,1,0:T(8,128)(2,1)S(1)} %pad_maximum_fusion.refs_0_), channel_id=1, source_target_pairs={{0,2},{2,0},{4,6},{6,4},{8,10},{10,8},{12,14},{14,12},{16,18},{18,... | collective-permute-start | bytes 1572872 | tf_op jit(solution)/shard_map/ppermute | solution.py:348
  300.4 20.2 %collective-permute-start.31 = (bf16[4,32,2048]{2,1,0:T(8,128)(2,1)S(1)}, bf16[4,32,2048]{2,1,0:T(8,128)(2,1)S(1)}, u32[]{:S(2)}, u32[]{:S(2)}) collective-permute-start(bf16[4,32,2048]{2,1,0:T(8,128)(2,1)S(1)} %pad_maximum_fusion.refs_0_), channel_id=1, source_target_pairs={{0,4},{2,6},{4,0},{6,2},{8,12},{10,14},{12,8},{14,10},{16,20},{18,... | collective-permute-start | bytes 1572872 | tf_op jit(solution)/shard_map/ppermute | solution.py:348
  301.5 19.1 %collective-permute-start.32 = (bf16[4,32,2048]{2,1,0:T(8,128)(2,1)S(1)}, bf16[4,32,2048]{2,1,0:T(8,128)(2,1)S(1)}, u32[]{:S(2)}, u32[]{:S(2)}) collective-permute-start(bf16[4,32,2048]{2,1,0:T(8,128)(2,1)S(1)} %pad_maximum_fusion.refs_0_), channel_id=1, source_target_pairs={{0,6},{2,4},{4,2},{6,0},{8,14},{10,12},{12,10},{14,8},{16,22},{18,... | collective-permute-start | bytes 1572872 | tf_op jit(solution)/shard_map/ppermute | solution.py:348
  314.7 5.9 %copy-start.2 = (bf16[4,32,2048]{2,1,0:T(8,128)(2,1)}, bf16[4,32,2048]{2,1,0:T(8,128)(2,1)S(1)}, u32[]{:S(2)}) copy-start(bf16[4,32,2048]{2,1,0:T(8,128)(2,1)S(1)} %collective-permute-done.30.refs_1_) | copy-start | bytes 1572868
  320.6 1.0 copy-start.4
  327.8 1.6 collective-permute-start.36
  (16 other events, 11.2 us)
Sparse Core Ops, SparseCore 0:
  19.9 55.9 all-gather.6
  78.7 61.5 all-gather.4
  172.2 63.7 all-gather.8
  238.6 60.7 all-gather.10

commit v3 on v2

--- a/solution.py
+++ b/solution.py
@@ -17,6 +17,7 @@
 VMEM_LIMIT = 56 * 1024 * 1024
 
 BF16, F32 = jnp.bfloat16, jnp.float32
+SHORT = pl.CostEstimate(flops=0, bytes_accessed=0, transcendentals=0)
 
 
 def fold_lanes(op, x):
@@ -26,15 +27,13 @@
     return parts[0]
 
 
-def attend_kernel(info, *refs, plane, blocks, rows, group_step, key_chunk, pieces, waits):
-    q_refs, refs = refs[:pieces], refs[pieces:]
+def attend_kernel(info, *refs, plane, blocks, rows, group_step, key_chunk, waits):
+    q_refs, refs = refs[:plane], refs[plane:]
     kt_ref, v_ref, ks_ref, vs_ref = refs[:4]
     refs = refs[4 + waits :]
     o_refs, refs = refs[:plane], refs[plane:]
-    score_refs, refs = refs[:2], refs[2:]
     weight_refs, refs = refs[:2], refs[2:]
-    shift_refs, refs = refs[:2], refs[2:]
-    aux_ref, pos_ref, ks_pad, vs_pad = refs
+    score_ref, shift_ref, aux_ref, pos_ref, ks_pad, vs_pad = refs
     me, my_plane, wanted = info[0], info[1], info[2]
     keys = v_ref.shape[0]
     block_rows = plane * rows
@@ -60,12 +59,10 @@
 
     def load_queries(tile):
         slot, group = place(tile)
-        block = info[3 + blocks + slot]
         parts = []
         for i in range(group_step):
             cols = pl.ds(pl.multiple_of((group + i) * HEAD_SIZE, HEAD_SIZE), HEAD_SIZE)
-            for b in range(plane):
-                parts.append(q_refs[b][slot, :, cols] if pieces > 1 else q_refs[0][block, b ^ my_plane, :, cols])
+            parts += [q[slot, :, cols] for q in q_refs]
         return jnp.concatenate(parts, axis=0)
 
     def span_scores(q, tile):
@@ -97,20 +94,14 @@
         for b, o in enumerate(o_refs):
             o[slot, :, GROUP_QUERIES * HEAD_SIZE :] = aux[b * rows : (b + 1) * rows].astype(BF16)
 
-    def score_span(tile, side):
-        q = load_queries(tile)
-        scores = span_scores(q, tile)
-        score_refs[side][:, keys:] = scores
-        return q, scores
-
-    def score_chunk(q, peak, j, side):
+    def score_chunk(q, peak, j):
         part = slice(j * key_chunk, (j + 1) * key_chunk)
         scores = jnp.dot(q, kt_ref[:, part], preferred_element_type=F32)
-        score_refs[side][:, part] = scores
+        score_ref[:, part] = scores
         return jnp.maximum(peak, fold_lanes(jnp.maximum, scores))
 
-    def weigh_chunk(totals, j, side):
-        score_ref, shift_ref, weight_ref = score_refs[side], shift_refs[side], weight_refs[j % 2]
+    def weigh_chunk(totals, j):
+        weight_ref = weight_refs[j % 2]
         for n, r in enumerate(range(0, tile_rows, strip)):
             part = slice(r, r + strip)
             shift = shift_ref[part]
@@ -124,35 +115,38 @@
         values = v_ref[j * key_chunk : (j + 1) * key_chunk]
         return acc + jnp.dot(weight_refs[j % 2][...], values, preferred_element_type=F32)
 
-    def step(now, later, side):
-        q, peak = score_span(later, 1 - side)
-        weights = jnp.exp2(score_refs[side][:, keys:] * LOG2_SCALE - shift_refs[side][...])
+    def step(now, later):
+        weights = jnp.exp2(score_ref[:, keys:] * LOG2_SCALE - shift_ref[...])
         acc = jnp.dot(weights.astype(BF16), vs_pad[...], preferred_element_type=F32)
         totals = [weights[r : r + strip] for r in range(0, tile_rows, strip)]
+        q = load_queries(later)
+        peak = span_scores(q, later)
+        score_ref[:, keys:] = peak
         for j in range(chunks):
-            peak = score_chunk(q, peak, j, 1 - side)
-            weigh_chunk(totals, j, side)
+            weigh_chunk(totals, j)
+            peak = score_chunk(q, peak, j)
             if j > 0:
                 acc = apply_chunk(acc, j - 1)
         acc = apply_chunk(acc, chunks - 1)
-        shift_refs[1 - side][...] = shift_of(peak)
-        finish(now, shift_refs[side][...], jnp.concatenate(totals, axis=0), acc)
+        finish(now, shift_ref[...], jnp.concatenate(totals, axis=0), acc)
+        shift_ref[...] = shift_of(peak)
 
     count = wanted * steps
 
     @pl.when(count > 0)
     def _():
-        q, peak = score_span(jnp.int32(0), 0)
+        q = load_queries(jnp.int32(0))
+        peak = span_scores(q, jnp.int32(0))
+        score_ref[:, keys:] = peak
         for j in range(chunks):
-            peak = score_chunk(q, peak, j, 0)
-        shift_refs[0][...] = shift_of(peak)
-
-        def body(i, _):
-            step(2 * i, 2 * i + 1, 0)
-            step(2 * i + 1, jnp.minimum(2 * i + 2, count - 1), 1)
+            peak = score_chunk(q, peak, j)
+        shift_ref[...] = shift_of(peak)
+
+        def body(t, _):
+            step(t, jnp.minimum(t + 1, count - 1))
             return 0
 
-        lax.fori_loop(0, lax.div(count, 2), body, 0)
+        lax.fori_loop(0, count, body, 0)
 
     def span_only(t, _):
         scores = span_scores(load_queries(t), t)
@@ -165,10 +159,9 @@
     lax.fori_loop(count, blocks * steps, span_only, 0)
 
 
-def attend_head(info, q_arrays, q_head, keys_t, values, span_keys, span_values, head, after):
-    shape = q_arrays[0].shape
-    blocks, rows = shape[0], shape[-2]
-    plane = len(q_arrays) if len(q_arrays) > 1 else shape[1]
+def attend_head(info, q_pieces, q_head, keys_t, values, span_keys, span_values, head, after):
+    plane = len(q_pieces)
+    blocks, rows, _ = q_pieces[0].shape
     cols = GROUP_QUERIES * HEAD_SIZE
     key_count = values.shape[0]
     group_step = 2
@@ -176,8 +169,7 @@
     key_chunk = min(key_count, 512)
     out_cols = cols + LANES
     vmem = pltpu.MemorySpace.VMEM
-    lead = (0,) * (len(shape) - 1)
-    whole = pl.BlockSpec((*shape[:-1], cols), lambda i, s: (*lead, q_head))
+    whole = pl.BlockSpec((blocks, rows, cols), lambda i, s: (0, 0, q_head))
     whole_out = pl.BlockSpec((blocks, rows, out_cols), lambda i, s: (0, 0, 0))
     span_block = pl.BlockSpec((rows, HEAD_SIZE), lambda i, s: (0, head))
     scored = blocks * plane * rows * GROUP_QUERIES * key_count
@@ -189,13 +181,12 @@
             rows=rows,
             group_step=group_step,
             key_chunk=key_chunk,
-            pieces=len(q_arrays),
             waits=len(after),
         ),
         grid_spec=pltpu.PrefetchScalarGridSpec(
             num_scalar_prefetch=1,
             grid=(1,),
-            in_specs=[whole] * len(q_arrays)
+            in_specs=[whole] * plane
             + [
                 pl.BlockSpec((HEAD_SIZE, key_count), lambda i, s: (head, 0)),
                 pl.BlockSpec((key_count, HEAD_SIZE), lambda i, s: (0, head)),
@@ -204,10 +195,10 @@
             ]
             + [pl.BlockSpec(memory_space=pl.ANY)] * len(after),
             out_specs=[whole_out] * plane,
-            scratch_shapes=[vmem((tile_rows, key_count + LANES), F32)] * 2
-            + [vmem((tile_rows, key_chunk), BF16)] * 2
-            + [vmem((tile_rows, LANES), F32)] * 2
+            scratch_shapes=[vmem((tile_rows, key_chunk), BF16)] * 2
             + [
+                vmem((tile_rows, key_count + LANES), F32),
+                vmem((tile_rows, LANES), F32),
                 vmem((plane * rows, LANES), F32),
                 vmem((tile_rows, LANES), jnp.int32),
                 vmem((LANES, HEAD_SIZE), BF16),
@@ -222,7 +213,7 @@
             transcendentals=scored,
         ),
         name="attend",
-    )(info, *q_arrays, keys_t, values, span_keys, span_values, *after)
+    )(info, *q_pieces, keys_t, values, span_keys, span_values, *after)
 
 
 def combine(parts):
@@ -276,30 +267,24 @@
 
 def merge_pieces(pieces, after):
     blocks, rows, cols = pieces[0].shape
-    size = blocks * rows * cols
     return pl.pallas_call(
         functools.partial(merge_kernel, count=len(pieces), waits=len(after)),
         in_specs=waiting_specs(pieces, after),
         out_shape=[jax.ShapeDtypeStruct((rows, cols), BF16)] * blocks,
         compiler_params=pltpu.CompilerParams(vmem_limit_bytes=VMEM_LIMIT),
-        cost_estimate=pl.CostEstimate(
-            flops=2 * size * len(pieces), bytes_accessed=2 * size * (len(pieces) + 1), transcendentals=0
-        ),
+        cost_estimate=SHORT,
         name="merge",
     )(*pieces, *after)
 
 
 def normalize_pieces(pieces, after):
     rows, cols = pieces[0].shape
-    size = rows * cols
     return pl.pallas_call(
         functools.partial(normalize_kernel, count=len(pieces)),
         in_specs=waiting_specs(pieces, after),
         out_shape=jax.ShapeDtypeStruct((rows, cols - LANES), BF16),
         compiler_params=pltpu.CompilerParams(vmem_limit_bytes=VMEM_LIMIT),
-        cost_estimate=pl.CostEstimate(
-            flops=2 * size * len(pieces), bytes_accessed=2 * size * (len(pieces) + 1), transcendentals=0
-        ),
+        cost_estimate=SHORT,
         name="normalize",
     )(*pieces, *after)
 
@@ -312,10 +297,10 @@
         for a in range(blocks):
             at = (info[3 + blocks + a], b ^ info[1])
             part = y[a * rows : (a + 1) * rows]
-            out[at] = ((base_ref[0][at] + part) if base_ref else part).astype(BF16)
-
-
-def project_late(info, pieces, weight, base):
+            out[at] = ((base_ref[0][at] + part) if base_ref else part).astype(out.dtype)
+
+
+def project(info, pieces, weight, group, base, dtype):
     plane = len(pieces)
     blocks, rows, width = pieces[0].shape
     out_cols = weight.shape[1]
@@ -328,11 +313,11 @@
             num_scalar_prefetch=1,
             grid=(1,),
             in_specs=[whole] * plane
-            + [pl.BlockSpec((width, out_cols), lambda i, s: (weight.shape[0] // width - 1, 0))]
+            + [pl.BlockSpec((width, out_cols), lambda i, s: (group, 0))]
             + [out_block] * len(base),
             out_specs=out_block,
         ),
-        out_shape=jax.ShapeDtypeStruct((blocks, plane, rows, out_cols), BF16),
+        out_shape=jax.ShapeDtypeStruct((blocks, plane, rows, out_cols), dtype),
         compiler_params=pltpu.CompilerParams(vmem_limit_bytes=VMEM_LIMIT),
         cost_estimate=pl.CostEstimate(
             flops=2 * span * width * out_cols,
@@ -340,7 +325,7 @@
             transcendentals=0,
         ),
         name="project",
-    )(info, *pieces, weight, *[x.reshape(blocks, plane, rows, out_cols) for x in base])
+    )(info, *pieces, weight, *base)
 
 
 def exchange(x, axis, distance):
@@ -374,19 +359,22 @@
     def gather_plane(stack):
         return [stack] + [exchange(stack, "ctx", b) for b in range(1, plane)]
 
-    def in_span_order(x):
-        return x.reshape(blocks, plane, rows, x.shape[1])
-
     first = stack_blocks(queries[:, :width])
-    sources = [(gather_plane(first), 0)]
-    for group in [range(1, 2), range(2, heads)]:
-        if len(group) and group[0] < heads:
-            held, _ = lax.optimization_barrier((queries[:, group[0] * width : (group[-1] + 1) * width], first))
-            whole = in_span_order(lax.all_gather(held, "ctx", axis=0, tiled=True))
-            sources += [([whole], i) for i in range(len(group))]
+    sources, stacks = [(gather_plane(first), 0)], []
+    if heads > 1:
+        held, _ = lax.optimization_barrier((queries[:, width:], first))
+        stacks = [stack_blocks(held)]
+        pieces = gather_plane(stacks[0])
+        sources += [(pieces, i) for i in range(heads - 1)]
 
     keys_t = context_keys.T
+
     attended, merged, rows_of = [], [], []
+
+    def attend(h, after):
+        attended.append(
+            attend_head(info, *sources[h], keys_t, context_values, span_keys, span_values, h, after)
+        )
 
     def merge(h, after):
         own = attended[h]
@@ -398,41 +386,31 @@
         parts = [own[0]] + [exchange(own[a], "ctx", a * plane) for a in range(1, blocks)]
         rows_of.append(normalize_pieces(parts, after))
 
+    latest = stacks
     for h in range(heads):
-        after = []
-        if h >= 3:
-            normalize(h - 3, [attended[h - 1][0]])
-            after.append(rows_of[h - 3])
+        attend(h, latest)
+        latest = [attended[h][0]]
+        if h >= 1:
+            merge(h - 1, latest)
+            latest = [merged[h - 1][0]]
         if h >= 2:
-            merge(h - 2, [attended[h - 1][0]])
-            after.append(merged[h - 2][0])
-        attended.append(
-            attend_head(info, *sources[h], keys_t, context_values, span_keys, span_values, h, after)
-        )
-    early = max(heads - 2, 0)
-    spread_rows = {}
-
-    def spread(h):
-        spread_rows[h] = lax.all_gather(rows_of[h], "ctx", axis=0, tiled=True)
-        return spread_rows[h]
-
-    last = [attended[-1][0]] + [spread(h) for h in range(min(early, len(rows_of)))]
-    for h in range(heads):
-        if h >= len(merged):
-            merge(h, last)
-        if h >= len(rows_of):
-            normalize(h, last)
-    base = [
-        jnp.dot(
-            spread_rows[h] if h in spread_rows else spread(h),
-            out_weight[h * width : (h + 1) * width],
-            preferred_element_type=F32,
-        )
-        for h in range(early)
-    ]
-    base = [functools.reduce(jnp.add, base)] if base else []
-    late = gather_plane(stack_blocks(jnp.concatenate(rows_of[early:], axis=1)))
-    partial_out = project_late(info, late, out_weight, base).reshape(ctx_count * rows, -1)
+            normalize(h - 2, latest)
+            latest = [rows_of[h - 2]]
+    merge(heads - 1, latest)
+    held, _ = lax.optimization_barrier((rows_of, merged[-1][0]))
+    rows_of = list(held)
+    for h in range(len(rows_of), heads):
+        normalize(h, [merged[-1][0]])
+    size = 2 if heads % 2 == 0 else 1
+    groups = [list(range(h, h + size)) for h in range(0, heads, size)]
+    total = []
+    for g, group in enumerate(groups):
+        stack = stack_blocks(jnp.concatenate([rows_of[h] for h in group], axis=1))
+        if total:
+            stack, _ = lax.optimization_barrier((stack, total[0]))
+        dtype = BF16 if g == len(groups) - 1 else F32
+        total = [project(info, gather_plane(stack), out_weight, g, total, dtype)]
+    partial_out = total[0].reshape(ctx_count * rows, -1)
     share = partial_out.shape[0] // head_count
     total = lax.dynamic_slice_in_dim(partial_out, my_head * share, share, 0).astype(F32)
     for d in range(1, head_count):

time: 342 us -> 282 us (0.82)
  waiting for transfers between devices: 90 us -> 45.8 us
  starting transfers between devices: 62.7 us -> 84.9 us
  Pallas kernels: 141 us -> 123 us
  between operations: 13.4 us -> 0.42 us
  matrix products: 5.16 us -> 0 us
    all_gather x4 -> x0, waiting for transfers between devices: 33.2 us -> none  [the longest x2 29.1 us: local(): whole = in_span_order(lax.all_gather(held, 'ctx', axis=0, tiled=True))]
    pallas_call x4, Pallas kernels: 117 us -> 94 us  [attend_head(): pl.pallas_call(functools.partial(attend_kernel, plane=plane, blocks=block...]
    ppermute x37 -> x49, starting transfers between devices: 62.5 us -> 84.9 us  [exchange(): return lax.ppermute(x, axis, [(i, i ^ distance) for i in range(count)])]
    ppermute x37 -> x49, waiting for transfers between devices: 56.7 us -> 45.8 us  [exchange(): return lax.ppermute(x, axis, [(i, i ^ distance) for i in range(count)])]
    dot_general x2 -> x0, matrix products: 5.16 us -> none  [local(): jnp.dot(spread_rows[h] if h in spread_rows else spread(h), out_weight[h *...]
    pallas_call x1 -> x2, Pallas kernels: 5.22 us -> 10.4 us  [project(): pl.pallas_call(functools.partial(project_kernel, plane=plane, blocks=bloc...]
    unnamed x79 -> x90, local copies, waits for them, and re-layouts: 14.4 us -> 14.8 us
  transfers between devices with their start and end apart: 41 -> 49, of which waited for: 17 -> 14; matrix products, arithmetic and copies ran while one was open for 5% -> 5% of each run, Pallas kernels for 39% -> 40%
where the time goes in v3:
time: 282 us; the launch traced here: 279 us
  Pallas kernels  123 us (44%)
  starting transfers between devices  84.9 us (30%)
  waiting for transfers between devices  45.8 us (16%)
  local copies, waits for them, and re-layouts  20.4 us (7%)
  other arithmetic  5.1 us (2%)
    pallas_call x4, Pallas kernels, attend_head(): pl.pallas_call(functools.partial(attend_kernel, plane=plane, blocks=block...  94 us
    ppermute x49, starting transfers between devices, exchange(): return lax.ppermute(x, axis, [(i, i ^ distance) for i in range(count)])  84.9 us
    ppermute x49, waiting for transfers between devices, exchange(): return lax.ppermute(x, axis, [(i, i ^ distance) for i in range(count)])  45.8 us
    unnamed x90, local copies, waits for them, and re-layouts  14.8 us
    pallas_call x4, Pallas kernels, merge_pieces(): pl.pallas_call(functools.partial(merge_kernel, count=len(pieces), waits=l...  11 us
    pallas_call x2, Pallas kernels, project(): pl.pallas_call(functools.partial(project_kernel, plane=plane, blocks=bloc...  10.4 us
    pallas_call x4, Pallas kernels, normalize_pieces(): pl.pallas_call(functools.partial(normalize_kernel, count=len(pieces)), in...  7.59 us
  transfers between devices with their start and end apart: 49, of which 14 were waited for; matrix products, arithmetic and copies ran while one was open for 5% of the time, Pallas kernels for 40%

profile of v3, /device:TPU:0, one launch (start us, length us, event | category | flops | bytes accessed | tf_op | source)
XLA Modules:
  0.0 279.4 jit_solution(8282289816133478998)
XLA Ops:
  0.0 0.8 slice_bitcast_fusion
  0.9 5.1 %collective-permute-start.2 = (bf16[32,1024]{1,0:T(8,128)(2,1)S(1)}, bf16[32,1024]{1,0:T(8,128)(2,1)S(1)}, u32[]{:S(2)}, u32[]{:S(2)}) collective-permute-start(bf16[32,1024]{1,0:T(8,128)(2,1)S(1)} %get-tuple-element.80), channel_id=1, source_target_pairs={{0,24},{2,26},{4,28},{6,30},{8,16},{10,18},{12,20},{14,22},{16,8},... | collective-permute-start | bytes 196616 | tf_op jit(solution)/shard_map/ppermute | solution.py:333
  6.6 0.9 slice.6
  9.0 6.4 %copy.9 = bf16[4096,512]{0,1:T(8,128)(2,1)} copy(bf16[4096,512]{1,0:T(8,128)(2,1)} %param.10) | data formatting | bytes 8388608 | tf_op args[3]
  16.3 3.8 %collective-permute-start.5 = (bf16[32,3072]{1,0:T(8,128)(2,1)S(1)}, bf16[32,3072]{1,0:T(8,128)(2,1)S(1)}, u32[]{:S(2)}, u32[]{:S(2)}) collective-permute-start(bf16[32,3072]{1,0:T(8,128)(2,1)S(1)} %slice.6), channel_id=1, source_target_pairs={{0,24},{2,26},{4,28},{6,30},{8,16},{10,18},{12,20},{14,22},{16,8},... | collective-permute-start | bytes 589832 | tf_op jit(solution)/shard_map/ppermute | solution.py:333
  21.4 1.3 concatenate.9.info
  22.7 1.6 collective-permute-start.9
  24.3 1.5 collective-permute-start.10
  26.1 2.6 collective-permute-start.11
  28.6 7.3 %collective-permute-done.4 = bf16[32,3072]{1,0:T(8,128)(2,1)S(1)} collective-permute-done((bf16[32,3072]{1,0:T(8,128)(2,1)S(1)}, bf16[32,3072]{1,0:T(8,128)(2,1)S(1)}, u32[]{:S(2)}, u32[]{:S(2)}) %collective-permute-start.4) | collective-permute-done | bytes 196640 | tf_op jit(solution)/shard_map/ppermute | solution.py:333
  36.0 1.6 collective-permute-start.6
  37.6 1.5 collective-permute-start.7
  40.4 23.4 %attend.4 = (bf16[4,32,1152]{2,1,0:T(8,128)(2,1)}, bf16[4,32,1152]{2,1,0:T(8,128)(2,1)}, bf16[4,32,1152]{2,1,0:T(8,128)(2,1)}, bf16[4,32,1152]{2,1,0:T(8,128)(2,1)}) custom-call(s32[11]{0:T(128)} %concatenate.9.info, bf16[4,32,1024]{2,1,0:T(8,128)(2,1)} %copy-done.21, bf16[4,32,1024]{2,1,0:T(8,128)(2,1)} %copy-done.38, bf16[4,32,1024]{2,1,0:T(8,128)(2,1)} %copy-done.39, ...), custom_call_target="tpu_custom_call" | custom-call | flops 17179869184 | bytes 4194304 | tf_op jit(solution)/shard_map/attend/pallas_call | solution.py:176
  63.8 7.2 %collective-permute-start.13 = (bf16[4,32,1152]{2,1,0:T(8,128)(2,1)}, bf16[4,32,1152]{2,1,0:T(8,128)(2,1)S(1)}, u32[]{:S(2)}, u32[]{:S(2)}) collective-permute-start(bf16[4,32,1152]{2,1,0:T(8,128)(2,1)} %get-tuple-element.46), channel_id=1, source_target_pairs={{0,4},{2,6},{4,0},{6,2},{8,12},{10,14},{12,8},{14,10},{16,20},{18,... | collective-permute-start | bytes 884744 | tf_op jit(solution)/shard_map/ppermute | solution.py:333
  71.7 2.7 collective-permute-done.8.refs_3_
  74.4 1.0 copy-done.37
  75.4 23.4 %attend.5 = (bf16[4,32,1152]{2,1,0:T(8,128)(2,1)}, bf16[4,32,1152]{2,1,0:T(8,128)(2,1)}, bf16[4,32,1152]{2,1,0:T(8,128)(2,1)}, bf16[4,32,1152]{2,1,0:T(8,128)(2,1)}) custom-call(s32[11]{0:T(128)} %concatenate.9.info, bf16[4,32,3072]{2,1,0:T(8,128)(2,1)} %copy-done.2, bf16[4,32,3072]{2,1,0:T(8,128)(2,1)} %copy-done.35, bf16[4,32,3072]{2,1,0:T(8,128)(2,1)} %copy-done.36, ...), custom_call_target="tpu_custom_call" | custom-call | flops 17179869184 | bytes 4194304 | tf_op jit(solution)/shard_map/attend/pallas_call | solution.py:176
  99.7 2.7 merge.4
  102.4 2.8 %collective-permute-start.18 = (bf16[32,1152]{1,0:T(8,128)(2,1)}, bf16[32,1152]{1,0:T(8,128)(2,1)S(1)}, u32[]{:S(2)}, u32[]{:S(2)}) collective-permute-start(bf16[32,1152]{1,0:T(8,128)(2,1)} %get-tuple-element.54), channel_id=1, source_target_pairs={{0,8},{2,10},{4,12},{6,14},{8,0},{10,2},{12,4},{14,6},{16,24},{18,... | collective-permute-start | bytes 221192 | tf_op jit(solution)/shard_map/ppermute | solution.py:333
  105.2 3.1 %collective-permute-start.19 = (bf16[32,1152]{1,0:T(8,128)(2,1)}, bf16[32,1152]{1,0:T(8,128)(2,1)S(1)}, u32[]{:S(2)}, u32[]{:S(2)}) collective-permute-start(bf16[32,1152]{1,0:T(8,128)(2,1)} %get-tuple-element.55), channel_id=1, source_target_pairs={{0,16},{2,18},{4,20},{6,22},{8,24},{10,26},{12,28},{14,30},{16,0},... | collective-permute-start | bytes 221192 | tf_op jit(solution)/shard_map/ppermute | solution.py:333
  108.4 1.4 collective-permute-start.20
  109.8 5.8 %collective-permute-start.22 = (bf16[4,32,1152]{2,1,0:T(8,128)(2,1)}, bf16[4,32,1152]{2,1,0:T(8,128)(2,1)S(1)}, u32[]{:S(2)}, u32[]{:S(2)}) collective-permute-start(bf16[4,32,1152]{2,1,0:T(8,128)(2,1)} %get-tuple-element.58), channel_id=1, source_target_pairs={{0,4},{2,6},{4,0},{6,2},{8,12},{10,14},{12,8},{14,10},{16,20},{18,... | collective-permute-start | bytes 884744 | tf_op jit(solution)/shard_map/ppermute | solution.py:333
  115.6 23.6 %attend.6 = (bf16[4,32,1152]{2,1,0:T(8,128)(2,1)}, bf16[4,32,1152]{2,1,0:T(8,128)(2,1)}, bf16[4,32,1152]{2,1,0:T(8,128)(2,1)}, bf16[4,32,1152]{2,1,0:T(8,128)(2,1)}) custom-call(s32[11]{0:T(128)} %concatenate.9.info, bf16[4,32,3072]{2,1,0:T(8,128)(2,1)} %copy-done.2, bf16[4,32,3072]{2,1,0:T(8,128)(2,1)} %copy-done.35, bf16[4,32,3072]{2,1,0:T(8,128)(2,1)} %copy-done.36, ...), custom_call_target="tpu_custom_call" | custom-call | flops 17179869184 | bytes 4194304 | tf_op jit(solution)/shard_map/attend/pallas_call | solution.py:176
  139.4 7.7 %collective-permute-start.16 = (bf16[4,32,1152]{2,1,0:T(8,128)(2,1)}, bf16[4,32,1152]{2,1,0:T(8,128)(2,1)S(1)}, u32[]{:S(2)}, u32[]{:S(2)}) collective-permute-start(bf16[4,32,1152]{2,1,0:T(8,128)(2,1)} %get-tuple-element.52), channel_id=1, source_target_pairs={{0,4},{2,6},{4,0},{6,2},{8,12},{10,14},{12,8},{14,10},{16,20},{18,... | collective-permute-start | bytes 884744 | tf_op jit(solution)/shard_map/ppermute | solution.py:333
  147.0 2.8 merge.5
  150.7 1.9 normalize.4.refs_8_
  152.6 23.5 %attend.7 = (bf16[4,32,1152]{2,1,0:T(8,128)(2,1)}, bf16[4,32,1152]{2,1,0:T(8,128)(2,1)}, bf16[4,32,1152]{2,1,0:T(8,128)(2,1)}, bf16[4,32,1152]{2,1,0:T(8,128)(2,1)}) custom-call(s32[11]{0:T(128)} %concatenate.9.info, bf16[4,32,3072]{2,1,0:T(8,128)(2,1)} %copy-done.2, bf16[4,32,3072]{2,1,0:T(8,128)(2,1)} %copy-done.35, bf16[4,32,3072]{2,1,0:T(8,128)(2,1)} %copy-done.36, ...), custom_call_target="tpu_custom_call" | custom-call | flops 17179869184 | bytes 4194304 | tf_op jit(solution)/shard_map/attend/pallas_call | solution.py:176
  176.2 7.5 %collective-permute-start.28 = (bf16[4,32,1152]{2,1,0:T(8,128)(2,1)}, bf16[4,32,1152]{2,1,0:T(8,128)(2,1)S(1)}, u32[]{:S(2)}, u32[]{:S(2)}) collective-permute-start(bf16[4,32,1152]{2,1,0:T(8,128)(2,1)} %get-tuple-element.67), channel_id=1, source_target_pairs={{0,4},{2,6},{4,0},{6,2},{8,12},{10,14},{12,8},{14,10},{16,20},{18,... | collective-permute-start | bytes 884744 | tf_op jit(solution)/shard_map/ppermute | solution.py:333
  184.4 2.4 collective-permute-start.31
  186.8 1.7 collective-permute-done.30.refs_1_
  188.5 2.1 collective-permute-start.32
  190.6 2.7 merge.6
  193.6 1.3 collective-permute-done.32.refs_3_
  194.9 0.8 collective-permute-start.25
  195.7 1.9 normalize.5.refs_4_
  197.6 2.3 collective-permute-start.26
  201.4 2.7 merge.7
  204.5 0.8 constant_dynamic-update-slice_fusion
  205.3 2.5 collective-permute-start.41
  208.5 1.3 collective-permute-start.39
  209.7 1.1 collective-permute-start.34
  210.9 2.0 collective-permute-start.35
  212.9 1.9 normalize.6
  214.8 6.8 %collective-permute-done.34.refs_2_ = bf16[32,1152]{1,0:T(8,128)(2,1)S(1)} collective-permute-done((bf16[32,1152]{1,0:T(8,128)(2,1)}, bf16[32,1152]{1,0:T(8,128)(2,1)S(1)}, u32[]{:S(2)}, u32[]{:S(2)}) %collective-permute-start.34) | collective-permute-done | bytes 73760 | tf_op jit(solution)/shard_map/ppermute | solution.py:333
  222.9 1.9 normalize.7
  224.9 1.6 collective-permute-start.42
  226.4 2.2 collective-permute-start.43
  228.7 0.9 fusion.1
  229.6 1.3 collective-permute-start.38
  230.9 1.7 collective-permute-start.37
  232.6 3.9 %collective-permute-done.38 = bf16[32,2048]{1,0:T(8,128)(2,1)S(1)} collective-permute-done((bf16[32,2048]{1,0:T(8,128)(2,1)S(1)}, bf16[32,2048]{1,0:T(8,128)(2,1)S(1)}, u32[]{:S(2)}, u32[]{:S(2)}) %collective-permute-start.38) | collective-permute-done | bytes 131104 | tf_op jit(solution)/shard_map/ppermute | solution.py:333
  236.5 2.4 collective-permute-start.36
  238.9 0.8 collective-permute-done.37
  239.8 2.1 collective-permute-done.36
  242.0 3.4 %collective-permute-done.44.refs_3_ = bf16[4,32,2048]{2,1,0:T(8,128)(2,1)S(1)} collective-permute-done((bf16[4,32,2048]{2,1,0:T(8,128)(2,1)S(1)}, bf16[4,32,2048]{2,1,0:T(8,128)(2,1)S(1)}, u32[]{:S(2)}, u32[]{:S(2)}) %collective-permute-start.44) | collective-permute-done | bytes 524320 | tf_op jit(solution)/shard_map/ppermute | solution.py:333
  246.2 5.1 %project.2.refs_5_ = f32[4,4,32,512]{3,2,1,0:T(8,128)} custom-call(s32[11]{0:T(128)} %concatenate.9.info, bf16[4,32,2048]{2,1,0:T(8,128)(2,1)} %copy-done.1, bf16[4,32,2048]{2,1,0:T(8,128)(2,1)} %copy-done.6, bf16[4,32,2048]{2,1,0:T(8,128)(2,1)} %copy-done.7, bf16[4,32,2048]{2,1,0:T(8,128)(2,1)} %copy-done.8, bf16[4096,512]{1,0:T(8,128)(2,1)} %refs_4_.3), custom_call_target="tpu_custom_call" | custom-call | flops 1073741824 | bytes 4194304 | tf_op jit(solution)/shard_map/project/pallas_call | solution.py:310
  251.3 2.2 collective-permute-start.45
  253.5 1.5 collective-permute-start.47
  255.0 5.7 %collective-permute-done.45.refs_1_ = bf16[4,32,2048]{2,1,0:T(8,128)(2,1)S(1)} collective-permute-done((bf16[4,32,2048]{2,1,0:T(8,128)(2,1)S(1)}, bf16[4,32,2048]{2,1,0:T(8,128)(2,1)S(1)}, u32[]{:S(2)}, u32[]{:S(2)}) %collective-permute-start.45) | collective-permute-done | bytes 524320 | tf_op jit(solution)/shard_map/ppermute | solution.py:333
  260.7 7.6 %collective-permute-done.46.refs_2_ = bf16[4,32,2048]{2,1,0:T(8,128)(2,1)S(1)} collective-permute-done((bf16[4,32,2048]{2,1,0:T(8,128)(2,1)S(1)}, bf16[4,32,2048]{2,1,0:T(8,128)(2,1)S(1)}, u32[]{:S(2)}, u32[]{:S(2)}) %collective-permute-start.46) | collective-permute-done | bytes 524320 | tf_op jit(solution)/shard_map/ppermute | solution.py:333
  269.9 5.2 %project.3 = bf16[4,4,32,512]{3,2,1,0:T(8,128)(2,1)} custom-call(s32[11]{0:T(128)} %concatenate.9.info, bf16[4,32,2048]{2,1,0:T(8,128)(2,1)} %copy-done, bf16[4,32,2048]{2,1,0:T(8,128)(2,1)} %copy-done.3, bf16[4,32,2048]{2,1,0:T(8,128)(2,1)} %copy-done.4, bf16[4,32,2048]{2,1,0:T(8,128)(2,1)} %copy-done.5, bf16[4096,512]{1,0:T(8,128)(2,1)} %refs_4_.3, ...), custom_call_target="tpu_custom_call" | custom-call | flops 1073741824 | bytes 4194304 | tf_op jit(solution)/shard_map/project/pallas_call | solution.py:310
  275.1 1.0 constant_dynamic-slice_fusion
  276.2 1.5 collective-permute-done.48
  277.7 1.7 add_convert_fusion
  (158 shorter events, 15.6 us)
Async XLA Ops:
  0.9 15.4 %collective-permute-start.2 = (bf16[32,1024]{1,0:T(8,128)(2,1)S(1)}, bf16[32,1024]{1,0:T(8,128)(2,1)S(1)}, u32[]{:S(2)}, u32[]{:S(2)}) collective-permute-start(bf16[32,1024]{1,0:T(8,128)(2,1)S(1)} %get-tuple-element.80), channel_id=1, source_target_pairs={{0,24},{2,26},{4,28},{6,30},{8,16},{10,18},{12,20},{14,22},{16,8},... | collective-permute-start | bytes 196616 | tf_op jit(solution)/shard_map/ppermute | solution.py:333
  6.0 10.3 %collective-permute-start.1 = (bf16[32,1024]{1,0:T(8,128)(2,1)S(1)}, bf16[32,1024]{1,0:T(8,128)(2,1)S(1)}, u32[]{:S(2)}, u32[]{:S(2)}) collective-permute-start(bf16[32,1024]{1,0:T(8,128)(2,1)S(1)} %get-tuple-element.80), channel_id=1, source_target_pairs={{0,16},{2,18},{4,20},{6,22},{8,24},{10,26},{12,28},{14,30},{16,0},... | collective-permute-start | bytes 196616 | tf_op jit(solution)/shard_map/ppermute | solution.py:333
  6.0 10.3 %collective-permute-start = (bf16[32,1024]{1,0:T(8,128)(2,1)S(1)}, bf16[32,1024]{1,0:T(8,128)(2,1)S(1)}, u32[]{:S(2)}, u32[]{:S(2)}) collective-permute-start(bf16[32,1024]{1,0:T(8,128)(2,1)S(1)} %get-tuple-element.80), channel_id=1, source_target_pairs={{0,8},{2,10},{4,12},{6,14},{8,0},{10,2},{12,4},{14,6},{16,24},{18,... | collective-permute-start | bytes 196616 | tf_op jit(solution)/shard_map/ppermute | solution.py:333
  16.3 23.3 %copy-start.21 = (bf16[4,32,1024]{2,1,0:T(8,128)(2,1)}, bf16[4,32,1024]{2,1,0:T(8,128)(2,1)S(1)}, u32[]{:S(2)}) copy-start(bf16[4,32,1024]{2,1,0:T(8,128)(2,1)S(1)} %pad_maximum_fusion.3.refs_0_) | copy-start | bytes 786436
  16.3 9.8 %collective-permute-start.5 = (bf16[32,3072]{1,0:T(8,128)(2,1)S(1)}, bf16[32,3072]{1,0:T(8,128)(2,1)S(1)}, u32[]{:S(2)}, u32[]{:S(2)}) collective-permute-start(bf16[32,3072]{1,0:T(8,128)(2,1)S(1)} %slice.6), channel_id=1, source_target_pairs={{0,24},{2,26},{4,28},{6,30},{8,16},{10,18},{12,20},{14,22},{16,8},... | collective-permute-start | bytes 589832 | tf_op jit(solution)/shard_map/ppermute | solution.py:333
  20.1 15.8 %collective-permute-start.4 = (bf16[32,3072]{1,0:T(8,128)(2,1)S(1)}, bf16[32,3072]{1,0:T(8,128)(2,1)S(1)}, u32[]{:S(2)}, u32[]{:S(2)}) collective-permute-start(bf16[32,3072]{1,0:T(8,128)(2,1)S(1)} %slice.6), channel_id=1, source_target_pairs={{0,16},{2,18},{4,20},{6,22},{8,24},{10,26},{12,28},{14,30},{16,0},... | collective-permute-start | bytes 589832 | tf_op jit(solution)/shard_map/ppermute | solution.py:333
  20.1 15.8 %collective-permute-start.3 = (bf16[32,3072]{1,0:T(8,128)(2,1)S(1)}, bf16[32,3072]{1,0:T(8,128)(2,1)S(1)}, u32[]{:S(2)}, u32[]{:S(2)}) collective-permute-start(bf16[32,3072]{1,0:T(8,128)(2,1)S(1)} %slice.6), channel_id=1, source_target_pairs={{0,8},{2,10},{4,12},{6,14},{8,0},{10,2},{12,4},{14,6},{16,24},{18,... | collective-permute-start | bytes 589832 | tf_op jit(solution)/shard_map/ppermute | solution.py:333
  22.7 16.4 %collective-permute-start.9 = (bf16[4,32,1024]{2,1,0:T(8,128)(2,1)S(1)}, bf16[4,32,1024]{2,1,0:T(8,128)(2,1)S(1)}, u32[]{:S(2)}, u32[]{:S(2)}) collective-permute-start(bf16[4,32,1024]{2,1,0:T(8,128)(2,1)S(1)} %pad_maximum_fusion.3.refs_0_), channel_id=1, source_target_pairs={{0,2},{2,0},{4,6},{6,4},{8,10},{10,8},{12,14},{14,12},{16,18},{18,... | collective-permute-start | bytes 786440 | tf_op jit(solution)/shard_map/ppermute | solution.py:333
  24.3 15.3 %collective-permute-start.10 = (bf16[4,32,1024]{2,1,0:T(8,128)(2,1)S(1)}, bf16[4,32,1024]{2,1,0:T(8,128)(2,1)S(1)}, u32[]{:S(2)}, u32[]{:S(2)}) collective-permute-start(bf16[4,32,1024]{2,1,0:T(8,128)(2,1)S(1)} %pad_maximum_fusion.3.refs_0_), channel_id=1, source_target_pairs={{0,4},{2,6},{4,0},{6,2},{8,12},{10,14},{12,8},{14,10},{16,20},{18,... | collective-permute-start | bytes 786440 | tf_op jit(solution)/shard_map/ppermute | solution.py:333
  26.1 13.5 %collective-permute-start.11 = (bf16[4,32,1024]{2,1,0:T(8,128)(2,1)S(1)}, bf16[4,32,1024]{2,1,0:T(8,128)(2,1)S(1)}, u32[]{:S(2)}, u32[]{:S(2)}) collective-permute-start(bf16[4,32,1024]{2,1,0:T(8,128)(2,1)S(1)} %pad_maximum_fusion.3.refs_0_), channel_id=1, source_target_pairs={{0,6},{2,4},{4,2},{6,0},{8,14},{10,12},{12,10},{14,8},{16,22},{18,... | collective-permute-start | bytes 786440 | tf_op jit(solution)/shard_map/ppermute | solution.py:333
  36.0 35.0 %collective-permute-start.6 = (bf16[4,32,3072]{2,1,0:T(8,128)(2,1)S(1)}, bf16[4,32,3072]{2,1,0:T(8,128)(2,1)S(1)}, u32[]{:S(2)}, u32[]{:S(2)}) collective-permute-start(bf16[4,32,3072]{2,1,0:T(8,128)(2,1)S(1)} %pad_maximum_fusion.refs_8_.refs_0_), channel_id=1, source_target_pairs={{0,2},{2,0},{4,6},{6,4},{8,10},{10,8},{12,14},{14,12},{16,18},{18,... | collective-permute-start | bytes 2359304 | tf_op jit(solution)/shard_map/ppermute | solution.py:333
  37.6 34.1 %collective-permute-start.7 = (bf16[4,32,3072]{2,1,0:T(8,128)(2,1)S(1)}, bf16[4,32,3072]{2,1,0:T(8,128)(2,1)S(1)}, u32[]{:S(2)}, u32[]{:S(2)}) collective-permute-start(bf16[4,32,3072]{2,1,0:T(8,128)(2,1)S(1)} %pad_maximum_fusion.refs_8_.refs_0_), channel_id=1, source_target_pairs={{0,4},{2,6},{4,0},{6,2},{8,12},{10,14},{12,8},{14,10},{16,20},{18,... | collective-permute-start | bytes 2359304 | tf_op jit(solution)/shard_map/ppermute | solution.py:333
  39.1 35.3 %collective-permute-start.8 = (bf16[4,32,3072]{2,1,0:T(8,128)(2,1)S(1)}, bf16[4,32,3072]{2,1,0:T(8,128)(2,1)S(1)}, u32[]{:S(2)}, u32[]{:S(2)}) collective-permute-start(bf16[4,32,3072]{2,1,0:T(8,128)(2,1)S(1)} %pad_maximum_fusion.refs_8_.refs_0_), channel_id=1, source_target_pairs={{0,6},{2,4},{4,2},{6,0},{8,14},{10,12},{12,10},{14,8},{16,22},{18,... | collective-permute-start | bytes 2359304 | tf_op jit(solution)/shard_map/ppermute | solution.py:333
  63.8 35.0 %collective-permute-start.12 = (bf16[4,32,1152]{2,1,0:T(8,128)(2,1)}, bf16[4,32,1152]{2,1,0:T(8,128)(2,1)S(1)}, u32[]{:S(2)}, u32[]{:S(2)}) collective-permute-start(bf16[4,32,1152]{2,1,0:T(8,128)(2,1)} %get-tuple-element.45), channel_id=1, source_target_pairs={{0,2},{2,0},{4,6},{6,4},{8,10},{10,8},{12,14},{14,12},{16,18},{18,... | collective-permute-start | bytes 884744 | tf_op jit(solution)/shard_map/ppermute | solution.py:333
  63.8 35.1 %collective-permute-start.13 = (bf16[4,32,1152]{2,1,0:T(8,128)(2,1)}, bf16[4,32,1152]{2,1,0:T(8,128)(2,1)S(1)}, u32[]{:S(2)}, u32[]{:S(2)}) collective-permute-start(bf16[4,32,1152]{2,1,0:T(8,128)(2,1)} %get-tuple-element.46), channel_id=1, source_target_pairs={{0,4},{2,6},{4,0},{6,2},{8,12},{10,14},{12,8},{14,10},{16,20},{18,... | collective-permute-start | bytes 884744 | tf_op jit(solution)/shard_map/ppermute | solution.py:333
  71.0 27.8 %collective-permute-start.14 = (bf16[4,32,1152]{2,1,0:T(8,128)(2,1)}, bf16[4,32,1152]{2,1,0:T(8,128)(2,1)S(1)}, u32[]{:S(2)}, u32[]{:S(2)}) collective-permute-start(bf16[4,32,1152]{2,1,0:T(8,128)(2,1)} %get-tuple-element.47), channel_id=1, source_target_pairs={{0,6},{2,4},{4,2},{6,0},{8,14},{10,12},{12,10},{14,8},{16,22},{18,... | collective-permute-start | bytes 884744 | tf_op jit(solution)/shard_map/ppermute | solution.py:333
  98.8 16.8 %collective-permute-start.21 = (bf16[4,32,1152]{2,1,0:T(8,128)(2,1)}, bf16[4,32,1152]{2,1,0:T(8,128)(2,1)S(1)}, u32[]{:S(2)}, u32[]{:S(2)}) collective-permute-start(bf16[4,32,1152]{2,1,0:T(8,128)(2,1)} %get-tuple-element.57), channel_id=1, source_target_pairs={{0,2},{2,0},{4,6},{6,4},{8,10},{10,8},{12,14},{14,12},{16,18},{18,... | collective-permute-start | bytes 884744 | tf_op jit(solution)/shard_map/ppermute | solution.py:333
  102.4 47.4 %collective-permute-start.18 = (bf16[32,1152]{1,0:T(8,128)(2,1)}, bf16[32,1152]{1,0:T(8,128)(2,1)S(1)}, u32[]{:S(2)}, u32[]{:S(2)}) collective-permute-start(bf16[32,1152]{1,0:T(8,128)(2,1)} %get-tuple-element.54), channel_id=1, source_target_pairs={{0,8},{2,10},{4,12},{6,14},{8,0},{10,2},{12,4},{14,6},{16,24},{18,... | collective-permute-start | bytes 221192 | tf_op jit(solution)/shard_map/ppermute | solution.py:333
  105.2 44.8 %collective-permute-start.19 = (bf16[32,1152]{1,0:T(8,128)(2,1)}, bf16[32,1152]{1,0:T(8,128)(2,1)S(1)}, u32[]{:S(2)}, u32[]{:S(2)}) collective-permute-start(bf16[32,1152]{1,0:T(8,128)(2,1)} %get-tuple-element.55), channel_id=1, source_target_pairs={{0,16},{2,18},{4,20},{6,22},{8,24},{10,26},{12,28},{14,30},{16,0},... | collective-permute-start | bytes 221192 | tf_op jit(solution)/shard_map/ppermute | solution.py:333
  108.4 41.7 %collective-permute-start.20 = (bf16[32,1152]{1,0:T(8,128)(2,1)}, bf16[32,1152]{1,0:T(8,128)(2,1)S(1)}, u32[]{:S(2)}, u32[]{:S(2)}) collective-permute-start(bf16[32,1152]{1,0:T(8,128)(2,1)} %get-tuple-element.56), channel_id=1, source_target_pairs={{0,24},{2,26},{4,28},{6,30},{8,16},{10,18},{12,20},{14,22},{16,8},... | collective-permute-start | bytes 221192 | tf_op jit(solution)/shard_map/ppermute | solution.py:333
  109.8 29.5 %collective-permute-start.22 = (bf16[4,32,1152]{2,1,0:T(8,128)(2,1)}, bf16[4,32,1152]{2,1,0:T(8,128)(2,1)S(1)}, u32[]{:S(2)}, u32[]{:S(2)}) collective-permute-start(bf16[4,32,1152]{2,1,0:T(8,128)(2,1)} %get-tuple-element.58), channel_id=1, source_target_pairs={{0,4},{2,6},{4,0},{6,2},{8,12},{10,14},{12,8},{14,10},{16,20},{18,... | collective-permute-start | bytes 884744 | tf_op jit(solution)/shard_map/ppermute | solution.py:333
  115.6 23.7 %copy-start.14 = (bf16[4,32,1152]{2,1,0:T(8,128)(2,1)}, bf16[4,32,1152]{2,1,0:T(8,128)(2,1)S(1)}, u32[]{:S(2)}) copy-start(bf16[4,32,1152]{2,1,0:T(8,128)(2,1)S(1)} %collective-permute-done.21.refs_1_) | copy-start | bytes 884740
  115.6 23.8 %collective-permute-start.23 = (bf16[4,32,1152]{2,1,0:T(8,128)(2,1)}, bf16[4,32,1152]{2,1,0:T(8,128)(2,1)S(1)}, u32[]{:S(2)}, u32[]{:S(2)}) collective-permute-start(bf16[4,32,1152]{2,1,0:T(8,128)(2,1)} %get-tuple-element.59), channel_id=1, source_target_pairs={{0,6},{2,4},{4,2},{6,0},{8,14},{10,12},{12,10},{14,8},{16,22},{18,... | collective-permute-start | bytes 884744 | tf_op jit(solution)/shard_map/ppermute | solution.py:333
  139.3 7.8 %copy-start.18 = (bf16[4,32,1152]{2,1,0:T(8,128)(2,1)}, bf16[4,32,1152]{2,1,0:T(8,128)(2,1)S(1)}, u32[]{:S(2)}) copy-start(bf16[4,32,1152]{2,1,0:T(8,128)(2,1)S(1)} %collective-permute-done.22.refs_2_) | copy-start | bytes 884740
  139.3 44.4 %collective-permute-start.15 = (bf16[4,32,1152]{2,1,0:T(8,128)(2,1)}, bf16[4,32,1152]{2,1,0:T(8,128)(2,1)S(1)}, u32[]{:S(2)}, u32[]{:S(2)}) collective-permute-start(bf16[4,32,1152]{2,1,0:T(8,128)(2,1)} %get-tuple-element.51), channel_id=1, source_target_pairs={{0,2},{2,0},{4,6},{6,4},{8,10},{10,8},{12,14},{14,12},{16,18},{18,... | collective-permute-start | bytes 884744 | tf_op jit(solution)/shard_map/ppermute | solution.py:333
  139.4 7.7 %copy-start.20 = (bf16[4,32,1152]{2,1,0:T(8,128)(2,1)}, bf16[4,32,1152]{2,1,0:T(8,128)(2,1)S(1)}, u32[]{:S(2)}) copy-start(bf16[4,32,1152]{2,1,0:T(8,128)(2,1)S(1)} %collective-permute-done.23.refs_3_) | copy-start | bytes 884740
  139.4 44.3 %collective-permute-start.16 = (bf16[4,32,1152]{2,1,0:T(8,128)(2,1)}, bf16[4,32,1152]{2,1,0:T(8,128)(2,1)S(1)}, u32[]{:S(2)}, u32[]{:S(2)}) collective-permute-start(bf16[4,32,1152]{2,1,0:T(8,128)(2,1)} %get-tuple-element.52), channel_id=1, source_target_pairs={{0,4},{2,6},{4,0},{6,2},{8,12},{10,14},{12,8},{14,10},{16,20},{18,... | collective-permute-start | bytes 884744 | tf_op jit(solution)/shard_map/ppermute | solution.py:333
  149.8 34.6 %collective-permute-start.17 = (bf16[4,32,1152]{2,1,0:T(8,128)(2,1)}, bf16[4,32,1152]{2,1,0:T(8,128)(2,1)S(1)}, u32[]{:S(2)}, u32[]{:S(2)}) collective-permute-start(bf16[4,32,1152]{2,1,0:T(8,128)(2,1)} %get-tuple-element.53), channel_id=1, source_target_pairs={{0,6},{2,4},{4,2},{6,0},{8,14},{10,12},{12,10},{14,8},{16,22},{18,... | collective-permute-start | bytes 884744 | tf_op jit(solution)/shard_map/ppermute | solution.py:333
  152.6 31.1 %copy-start.43 = (bf16[32,1152]{1,0:T(8,128)(2,1)S(1)}, bf16[32,1152]{1,0:T(8,128)(2,1)}, u32[]{:S(2)}) copy-start(bf16[32,1152]{1,0:T(8,128)(2,1)} %get-tuple-element.69) | copy-start | bytes 221188
  152.6 31.8 %copy-start.42 = (bf16[32,1152]{1,0:T(8,128)(2,1)S(1)}, bf16[32,1152]{1,0:T(8,128)(2,1)}, u32[]{:S(2)}) copy-start(bf16[32,1152]{1,0:T(8,128)(2,1)} %get-tuple-element.70) | copy-start | bytes 221188
  152.6 35.9 %copy-start.41 = (bf16[32,1152]{1,0:T(8,128)(2,1)S(1)}, bf16[32,1152]{1,0:T(8,128)(2,1)}, u32[]{:S(2)}) copy-start(bf16[32,1152]{1,0:T(8,128)(2,1)} %get-tuple-element.71) | copy-start | bytes 221188
  152.6 51.8 %copy-start.22 = (bf16[32,1024]{1,0:T(8,128)(2,1)S(1)}, bf16[32,1024]{1,0:T(8,128)(2,1)}, u32[]{:S(2)}) copy-start(bf16[32,1024]{1,0:T(8,128)(2,1)} %normalize.4.refs_8_) | copy-start | bytes 196612
  176.2 21.4 %collective-permute-start.27 = (bf16[4,32,1152]{2,1,0:T(8,128)(2,1)}, bf16[4,32,1152]{2,1,0:T(8,128)(2,1)S(1)}, u32[]{:S(2)}, u32[]{:S(2)}) collective-permute-start(bf16[4,32,1152]{2,1,0:T(8,128)(2,1)} %get-tuple-element.66), channel_id=1, source_target_pairs={{0,2},{2,0},{4,6},{6,4},{8,10},{10,8},{12,14},{14,12},{16,18},{18,... | collective-permute-start | bytes 884744 | tf_op jit(solution)/shard_map/ppermute | solution.py:333
  176.2 23.7 %collective-permute-start.28 = (bf16[4,32,1152]{2,1,0:T(8,128)(2,1)}, bf16[4,32,1152]{2,1,0:T(8,128)(2,1)S(1)}, u32[]{:S(2)}, u32[]{:S(2)}) collective-permute-start(bf16[4,32,1152]{2,1,0:T(8,128)(2,1)} %get-tuple-element.67), channel_id=1, source_target_pairs={{0,4},{2,6},{4,0},{6,2},{8,12},{10,14},{12,8},{14,10},{16,20},{18,... | collective-permute-start | bytes 884744 | tf_op jit(solution)/shard_map/ppermute | solution.py:333
  183.7 6.8 %copy-start.12 = (bf16[4,32,1152]{2,1,0:T(8,128)(2,1)}, bf16[4,32,1152]{2,1,0:T(8,128)(2,1)S(1)}, u32[]{:S(2)}) copy-start(bf16[4,32,1152]{2,1,0:T(8,128)(2,1)S(1)} %collective-permute-done.15.refs_1_) | copy-start | bytes 884740
  183.7 16.2 %collective-permute-start.29 = (bf16[4,32,1152]{2,1,0:T(8,128)(2,1)}, bf16[4,32,1152]{2,1,0:T(8,128)(2,1)S(1)}, u32[]{:S(2)}, u32[]{:S(2)}) collective-permute-start(bf16[4,32,1152]{2,1,0:T(8,128)(2,1)} %get-tuple-element.68), channel_id=1, source_target_pairs={{0,6},{2,4},{4,2},{6,0},{8,14},{10,12},{12,10},{14,8},{16,22},{18,... | collective-permute-start | bytes 884744 | tf_op jit(solution)/shard_map/ppermute | solution.py:333
  183.7 6.8 %copy-start.13 = (bf16[4,32,1152]{2,1,0:T(8,128)(2,1)}, bf16[4,32,1152]{2,1,0:T(8,128)(2,1)S(1)}, u32[]{:S(2)}) copy-start(bf16[4,32,1152]{2,1,0:T(8,128)(2,1)S(1)} %collective-permute-done.16.refs_2_) | copy-start | bytes 884740
  183.8 4.7 %collective-permute-start.30 = (bf16[32,1152]{1,0:T(8,128)(2,1)S(1)}, bf16[32,1152]{1,0:T(8,128)(2,1)S(1)}, u32[]{:S(2)}, u32[]{:S(2)}) collective-permute-start(bf16[32,1152]{1,0:T(8,128)(2,1)S(1)} %copy-done.43), channel_id=1, source_target_pairs={{0,8},{2,10},{4,12},{6,14},{8,0},{10,2},{12,4},{14,6},{16,24},{18,... | collective-permute-start | bytes 221192 | tf_op jit(solution)/shard_map/ppermute | solution.py:333
  184.4 8.9 %collective-permute-start.31 = (bf16[32,1152]{1,0:T(8,128)(2,1)S(1)}, bf16[32,1152]{1,0:T(8,128)(2,1)S(1)}, u32[]{:S(2)}, u32[]{:S(2)}) collective-permute-start(bf16[32,1152]{1,0:T(8,128)(2,1)S(1)} %copy-done.42), channel_id=1, source_target_pairs={{0,16},{2,18},{4,20},{6,22},{8,24},{10,26},{12,28},{14,30},{16,0},... | collective-permute-start | bytes 221192 | tf_op jit(solution)/shard_map/ppermute | solution.py:333
  188.5 7.2 %copy-start.30 = (bf16[32,1152]{1,0:T(8,128)(2,1)}, bf16[32,1152]{1,0:T(8,128)(2,1)S(1)}, u32[]{:S(2)}) copy-start(bf16[32,1152]{1,0:T(8,128)(2,1)S(1)} %collective-permute-done.30.refs_1_) | copy-start | bytes 221188
  188.5 6.4 %collective-permute-start.32 = (bf16[32,1152]{1,0:T(8,128)(2,1)S(1)}, bf16[32,1152]{1,0:T(8,128)(2,1)S(1)}, u32[]{:S(2)}, u32[]{:S(2)}) collective-permute-start(bf16[32,1152]{1,0:T(8,128)(2,1)S(1)} %copy-done.41), channel_id=1, source_target_pairs={{0,24},{2,26},{4,28},{6,30},{8,16},{10,18},{12,20},{14,22},{16,8},... | collective-permute-start | bytes 221192 | tf_op jit(solution)/shard_map/ppermute | solution.py:333
  193.3 14.5 %collective-permute-start.24 = (bf16[32,1152]{1,0:T(8,128)(2,1)}, bf16[32,1152]{1,0:T(8,128)(2,1)S(1)}, u32[]{:S(2)}, u32[]{:S(2)}) collective-permute-start(bf16[32,1152]{1,0:T(8,128)(2,1)} %get-tuple-element.63), channel_id=1, source_target_pairs={{0,8},{2,10},{4,12},{6,14},{8,0},{10,2},{12,4},{14,6},{16,24},{18,... | collective-permute-start | bytes 221192 | tf_op jit(solution)/shard_map/ppermute | solution.py:333
  194.9 13.6 %collective-permute-start.25 = (bf16[32,1152]{1,0:T(8,128)(2,1)}, bf16[32,1152]{1,0:T(8,128)(2,1)S(1)}, u32[]{:S(2)}, u32[]{:S(2)}) collective-permute-start(bf16[32,1152]{1,0:T(8,128)(2,1)} %get-tuple-element.64), channel_id=1, source_target_pairs={{0,16},{2,18},{4,20},{6,22},{8,24},{10,26},{12,28},{14,30},{16,0},... | collective-permute-start | bytes 221192 | tf_op jit(solution)/shard_map/ppermute | solution.py:333
  197.6 12.1 %collective-permute-start.26 = (bf16[32,1152]{1,0:T(8,128)(2,1)}, bf16[32,1152]{1,0:T(8,128)(2,1)S(1)}, u32[]{:S(2)}, u32[]{:S(2)}) collective-permute-start(bf16[32,1152]{1,0:T(8,128)(2,1)} %get-tuple-element.65), channel_id=1, source_target_pairs={{0,24},{2,26},{4,28},{6,30},{8,16},{10,18},{12,20},{14,22},{16,8},... | collective-permute-start | bytes 221192 | tf_op jit(solution)/shard_map/ppermute | solution.py:333
  204.1 6.8 %collective-permute-start.33 = (bf16[32,1152]{1,0:T(8,128)(2,1)}, bf16[32,1152]{1,0:T(8,128)(2,1)S(1)}, u32[]{:S(2)}, u32[]{:S(2)}) collective-permute-start(bf16[32,1152]{1,0:T(8,128)(2,1)} %get-tuple-element.73), channel_id=1, source_target_pairs={{0,8},{2,10},{4,12},{6,14},{8,0},{10,2},{12,4},{14,6},{16,24},{18,... | collective-permute-start | bytes 221192 | tf_op jit(solution)/shard_map/ppermute | solution.py:333
  205.3 19.5 %collective-permute-start.41 = (bf16[32,2048]{1,0:T(8,128)(2,1)S(1)}, bf16[32,2048]{1,0:T(8,128)(2,1)S(1)}, u32[]{:S(2)}, u32[]{:S(2)}) collective-permute-start(bf16[32,2048]{1,0:T(8,128)(2,1)S(1)} %constant_dynamic-update-slice_fusion), channel_id=1, source_target_pairs={{0,24},{2,26},{4,28},{6,30},{8,16},{10,18},{12,20},{14,22},{16,8},... | collective-permute-start | bytes 393224 | tf_op jit(solution)/shard_map/ppermute | solution.py:333
  207.8 16.9 %collective-permute-start.40 = (bf16[32,2048]{1,0:T(8,128)(2,1)S(1)}, bf16[32,2048]{1,0:T(8,128)(2,1)S(1)}, u32[]{:S(2)}, u32[]{:S(2)}) collective-permute-start(bf16[32,2048]{1,0:T(8,128)(2,1)S(1)} %constant_dynamic-update-slice_fusion), channel_id=1, source_target_pairs={{0,16},{2,18},{4,20},{6,22},{8,24},{10,26},{12,28},{14,30},{16,0},... | collective-permute-start | bytes 393224 | tf_op jit(solution)/shard_map/ppermute | solution.py:333
  208.5 16.3 %collective-permute-start.39 = (bf16[32,2048]{1,0:T(8,128)(2,1)S(1)}, bf16[32,2048]{1,0:T(8,128)(2,1)S(1)}, u32[]{:S(2)}, u32[]{:S(2)}) collective-permute-start(bf16[32,2048]{1,0:T(8,128)(2,1)S(1)} %constant_dynamic-update-slice_fusion), channel_id=1, source_target_pairs={{0,8},{2,10},{4,12},{6,14},{8,0},{10,2},{12,4},{14,6},{16,24},{18,... | collective-permute-start | bytes 393224 | tf_op jit(solution)/shard_map/ppermute | solution.py:333
  209.7 11.9 %collective-permute-start.34 = (bf16[32,1152]{1,0:T(8,128)(2,1)}, bf16[32,1152]{1,0:T(8,128)(2,1)S(1)}, u32[]{:S(2)}, u32[]{:S(2)}) collective-permute-start(bf16[32,1152]{1,0:T(8,128)(2,1)} %get-tuple-element.74), channel_id=1, source_target_pairs={{0,16},{2,18},{4,20},{6,22},{8,24},{10,26},{12,28},{14,30},{16,0},... | collective-permute-start | bytes 221192 | tf_op jit(solution)/shard_map/ppermute | solution.py:333
  210.9 10.7 %copy-start.29 = (bf16[32,1152]{1,0:T(8,128)(2,1)}, bf16[32,1152]{1,0:T(8,128)(2,1)S(1)}, u32[]{:S(2)}) copy-start(bf16[32,1152]{1,0:T(8,128)(2,1)S(1)} %collective-permute-done.33.refs_1_) | copy-start | bytes 221188
  210.9 10.7 %collective-permute-start.35 = (bf16[32,1152]{1,0:T(8,128)(2,1)}, bf16[32,1152]{1,0:T(8,128)(2,1)S(1)}, u32[]{:S(2)}, u32[]{:S(2)}) collective-permute-start(bf16[32,1152]{1,0:T(8,128)(2,1)} %get-tuple-element.75), channel_id=1, source_target_pairs={{0,24},{2,26},{4,28},{6,30},{8,16},{10,18},{12,20},{14,22},{16,8},... | collective-permute-start | bytes 221192 | tf_op jit(solution)/shard_map/ppermute | solution.py:333
  224.9 20.5 %copy-start.1 = (bf16[4,32,2048]{2,1,0:T(8,128)(2,1)}, bf16[4,32,2048]{2,1,0:T(8,128)(2,1)S(1)}, u32[]{:S(2)}) copy-start(bf16[4,32,2048]{2,1,0:T(8,128)(2,1)S(1)} %pad_maximum_fusion.2.refs_0_) | copy-start | bytes 1572868
  224.9 17.1 %collective-permute-start.42 = (bf16[4,32,2048]{2,1,0:T(8,128)(2,1)S(1)}, bf16[4,32,2048]{2,1,0:T(8,128)(2,1)S(1)}, u32[]{:S(2)}, u32[]{:S(2)}) collective-permute-start(bf16[4,32,2048]{2,1,0:T(8,128)(2,1)S(1)} %pad_maximum_fusion.2.refs_0_), channel_id=1, source_target_pairs={{0,2},{2,0},{4,6},{6,4},{8,10},{10,8},{12,14},{14,12},{16,18},{18,... | collective-permute-start | bytes 1572872 | tf_op jit(solution)/shard_map/ppermute | solution.py:333
  226.4 15.5 %collective-permute-start.43 = (bf16[4,32,2048]{2,1,0:T(8,128)(2,1)S(1)}, bf16[4,32,2048]{2,1,0:T(8,128)(2,1)S(1)}, u32[]{:S(2)}, u32[]{:S(2)}) collective-permute-start(bf16[4,32,2048]{2,1,0:T(8,128)(2,1)S(1)} %pad_maximum_fusion.2.refs_0_), channel_id=1, source_target_pairs={{0,4},{2,6},{4,0},{6,2},{8,12},{10,14},{12,8},{14,10},{16,20},{18,... | collective-permute-start | bytes 1572872 | tf_op jit(solution)/shard_map/ppermute | solution.py:333
  228.7 16.7 %collective-permute-start.44 = (bf16[4,32,2048]{2,1,0:T(8,128)(2,1)S(1)}, bf16[4,32,2048]{2,1,0:T(8,128)(2,1)S(1)}, u32[]{:S(2)}, u32[]{:S(2)}) collective-permute-start(bf16[4,32,2048]{2,1,0:T(8,128)(2,1)S(1)} %pad_maximum_fusion.2.refs_0_), channel_id=1, source_target_pairs={{0,6},{2,4},{4,2},{6,0},{8,14},{10,12},{12,10},{14,8},{16,22},{18,... | collective-permute-start | bytes 1572872 | tf_op jit(solution)/shard_map/ppermute | solution.py:333
  229.6 6.9 %collective-permute-start.38 = (bf16[32,2048]{1,0:T(8,128)(2,1)S(1)}, bf16[32,2048]{1,0:T(8,128)(2,1)S(1)}, u32[]{:S(2)}, u32[]{:S(2)}) collective-permute-start(bf16[32,2048]{1,0:T(8,128)(2,1)S(1)} %get-tuple-element.82), channel_id=1, source_target_pairs={{0,24},{2,26},{4,28},{6,30},{8,16},{10,18},{12,20},{14,22},{16,8},... | collective-permute-start | bytes 393224 | tf_op jit(solution)/shard_map/ppermute | solution.py:333
  230.9 8.8 %collective-permute-start.37 = (bf16[32,2048]{1,0:T(8,128)(2,1)S(1)}, bf16[32,2048]{1,0:T(8,128)(2,1)S(1)}, u32[]{:S(2)}, u32[]{:S(2)}) collective-permute-start(bf16[32,2048]{1,0:T(8,128)(2,1)S(1)} %get-tuple-element.82), channel_id=1, source_target_pairs={{0,16},{2,18},{4,20},{6,22},{8,24},{10,26},{12,28},{14,30},{16,0},... | collective-permute-start | bytes 393224 | tf_op jit(solution)/shard_map/ppermute | solution.py:333
  236.5 5.4 %collective-permute-start.36 = (bf16[32,2048]{1,0:T(8,128)(2,1)S(1)}, bf16[32,2048]{1,0:T(8,128)(2,1)S(1)}, u32[]{:S(2)}, u32[]{:S(2)}) collective-permute-start(bf16[32,2048]{1,0:T(8,128)(2,1)S(1)} %get-tuple-element.82), channel_id=1, source_target_pairs={{0,8},{2,10},{4,12},{6,14},{8,0},{10,2},{12,4},{14,6},{16,24},{18,... | collective-permute-start | bytes 393224 | tf_op jit(solution)/shard_map/ppermute | solution.py:333
  241.9 26.4 %copy-start = (bf16[4,32,2048]{2,1,0:T(8,128)(2,1)}, bf16[4,32,2048]{2,1,0:T(8,128)(2,1)S(1)}, u32[]{:S(2)}) copy-start(bf16[4,32,2048]{2,1,0:T(8,128)(2,1)S(1)} %pad_maximum_fusion.1.refs_0_) | copy-start | bytes 1572868
  251.3 9.4 %collective-permute-start.45 = (bf16[4,32,2048]{2,1,0:T(8,128)(2,1)S(1)}, bf16[4,32,2048]{2,1,0:T(8,128)(2,1)S(1)}, u32[]{:S(2)}, u32[]{:S(2)}) collective-permute-start(bf16[4,32,2048]{2,1,0:T(8,128)(2,1)S(1)} %pad_maximum_fusion.1.refs_0_), channel_id=1, source_target_pairs={{0,2},{2,0},{4,6},{6,4},{8,10},{10,8},{12,14},{14,12},{16,18},{18,... | collective-permute-start | bytes 1572872 | tf_op jit(solution)/shard_map/ppermute | solution.py:333
  253.5 14.8 %collective-permute-start.46 = (bf16[4,32,2048]{2,1,0:T(8,128)(2,1)S(1)}, bf16[4,32,2048]{2,1,0:T(8,128)(2,1)S(1)}, u32[]{:S(2)}, u32[]{:S(2)}) collective-permute-start(bf16[4,32,2048]{2,1,0:T(8,128)(2,1)S(1)} %pad_maximum_fusion.1.refs_0_), channel_id=1, source_target_pairs={{0,4},{2,6},{4,0},{6,2},{8,12},{10,14},{12,8},{14,10},{16,20},{18,... | collective-permute-start | bytes 1572872 | tf_op jit(solution)/shard_map/ppermute | solution.py:333
  253.5 14.8 %collective-permute-start.47 = (bf16[4,32,2048]{2,1,0:T(8,128)(2,1)S(1)}, bf16[4,32,2048]{2,1,0:T(8,128)(2,1)S(1)}, u32[]{:S(2)}, u32[]{:S(2)}) collective-permute-start(bf16[4,32,2048]{2,1,0:T(8,128)(2,1)S(1)} %pad_maximum_fusion.1.refs_0_), channel_id=1, source_target_pairs={{0,6},{2,4},{4,2},{6,0},{8,14},{10,12},{12,10},{14,8},{16,22},{18,... | collective-permute-start | bytes 1572872 | tf_op jit(solution)/shard_map/ppermute | solution.py:333
  260.7 7.7 %copy-start.3 = (bf16[4,32,2048]{2,1,0:T(8,128)(2,1)}, bf16[4,32,2048]{2,1,0:T(8,128)(2,1)S(1)}, u32[]{:S(2)}) copy-start(bf16[4,32,2048]{2,1,0:T(8,128)(2,1)S(1)} %collective-permute-done.45.refs_1_) | copy-start | bytes 1572868
  276.1 1.6 collective-permute-start.48
  (29 other events, 53.4 us)

commit v4 on v3

--- a/solution.py
+++ b/solution.py
@@ -14,7 +14,8 @@
 LOG2_SCALE = float(HEAD_SIZE**-0.5 * np.log2(np.e))
 MASKED = -1e30
 LOWEST = -1e20
-VMEM_LIMIT = 56 * 1024 * 1024
+ATTEND_VMEM = 28 * 1024 * 1024
+SHORT_VMEM = 16 * 1024 * 1024
 
 BF16, F32 = jnp.bfloat16, jnp.float32
 SHORT = pl.CostEstimate(flops=0, bytes_accessed=0, transcendentals=0)
@@ -46,12 +47,13 @@
     vs_pad[...] = jnp.zeros_like(vs_pad)
     ks_pad[0:rows, :] = ks_ref[...]
     vs_pad[0:rows, :] = vs_ref[...]
-    row = lax.broadcasted_iota(jnp.int32, (tile_rows, LANES), 0)
-    col = lax.broadcasted_iota(jnp.int32, (tile_rows, LANES), 1)
-    piece = lax.rem(lax.div(row, rows), plane)
-    pos_ref[...] = jnp.where(
-        col < rows, (piece ^ my_plane) * rows + lax.rem(row, rows) - me * rows - col, -(1 << 30)
-    )
+    row = lax.broadcasted_iota(jnp.int32, (rows, LANES), 0)
+    col = lax.broadcasted_iota(jnp.int32, (rows, LANES), 1)
+    for i in range(group_step):
+        for b in range(plane):
+            start = (i * plane + b) * rows
+            base = ((b ^ my_plane) - me) * rows
+            pos_ref[start : start + rows] = jnp.where(col < rows, row - col + base, -(1 << 30))
     lane = lax.broadcasted_iota(jnp.int32, (block_rows, LANES), 1)
 
     def place(tile):
@@ -206,7 +208,7 @@
             ],
         ),
         out_shape=[jax.ShapeDtypeStruct((blocks, rows, out_cols), BF16)] * plane,
-        compiler_params=pltpu.CompilerParams(vmem_limit_bytes=VMEM_LIMIT),
+        compiler_params=pltpu.CompilerParams(vmem_limit_bytes=ATTEND_VMEM),
         cost_estimate=pl.CostEstimate(
             flops=8 * scored * HEAD_SIZE,
             bytes_accessed=4 * key_count * HEAD_SIZE + 4 * blocks * plane * rows * cols,
@@ -232,67 +234,78 @@
     return heads, top, total
 
 
-def merge_kernel(*refs, count, waits):
-    ins, outs = refs[:count], refs[count + waits :]
-    for a, out in enumerate(outs):
-        heads, top, total = combine([p[a] for p in ins])
-        for g, x in enumerate(heads):
-            out[:, g * HEAD_SIZE : (g + 1) * HEAD_SIZE] = x.astype(BF16)
-        lane = lax.broadcasted_iota(jnp.int32, top.shape, 1)
-        high = total.astype(BF16).astype(F32)
-        aux = jnp.where(
-            lane < GROUP_QUERIES,
-            top,
-            jnp.where(
-                lane < 2 * GROUP_QUERIES,
-                pltpu.roll(high, GROUP_QUERIES, 1),
-                pltpu.roll(total - high, 2 * GROUP_QUERIES, 1),
-            ),
-        )
-        aux = jnp.where(lane < 3 * GROUP_QUERIES, aux, 0.0)
-        out[:, GROUP_QUERIES * HEAD_SIZE :] = aux.astype(BF16)
-
-
-def normalize_kernel(*refs, count):
+def merge_kernel(*refs, heads, plane, waits):
+    ins, outs = refs[: heads * plane], refs[heads * plane + waits :]
+    width = GROUP_QUERIES * HEAD_SIZE
+    for h in range(heads):
+        first = h * (width + LANES)
+        for a, out in enumerate(outs):
+            parts, top, total = combine([p[a] for p in ins[h * plane : (h + 1) * plane]])
+            for g, x in enumerate(parts):
+                out[:, first + g * HEAD_SIZE : first + (g + 1) * HEAD_SIZE] = x.astype(BF16)
+            lane = lax.broadcasted_iota(jnp.int32, top.shape, 1)
+            high = total.astype(BF16).astype(F32)
+            aux = jnp.where(
+                lane < GROUP_QUERIES,
+                top,
+                jnp.where(
+                    lane < 2 * GROUP_QUERIES,
+                    pltpu.roll(high, GROUP_QUERIES, 1),
+                    pltpu.roll(total - high, 2 * GROUP_QUERIES, 1),
+                ),
+            )
+            aux = jnp.where(lane < 3 * GROUP_QUERIES, aux, 0.0)
+            out[:, first + width : first + width + LANES] = aux.astype(BF16)
+
+
+def normalize_kernel(*refs, heads, count):
     ins, out = refs[:count], refs[-1]
-    heads, _, total = combine([p[...] for p in ins])
-    for g, x in enumerate(heads):
-        out[:, g * HEAD_SIZE : (g + 1) * HEAD_SIZE] = (x / total[:, g : g + 1]).astype(BF16)
-
-
-def waiting_specs(pieces, after):
+    width = GROUP_QUERIES * HEAD_SIZE
+    for h in range(heads):
+        first = h * (width + LANES)
+        parts, _, total = combine([p[:, first : first + width + LANES] for p in ins])
+        for g, x in enumerate(parts):
+            start = h * width + g * HEAD_SIZE
+            out[:, start : start + HEAD_SIZE] = (x / total[:, g : g + 1]).astype(BF16)
+
+
+def waiting_specs(count, waits):
     whole = pl.BlockSpec(memory_space=pltpu.MemorySpace.VMEM)
-    return [whole] * len(pieces) + [pl.BlockSpec(memory_space=pl.ANY)] * len(after)
+    return [whole] * count + [pl.BlockSpec(memory_space=pl.ANY)] * waits
 
 
 def merge_pieces(pieces, after):
-    blocks, rows, cols = pieces[0].shape
+    heads, plane = len(pieces), len(pieces[0])
+    blocks, rows, cols = pieces[0][0].shape
     return pl.pallas_call(
-        functools.partial(merge_kernel, count=len(pieces), waits=len(after)),
-        in_specs=waiting_specs(pieces, after),
-        out_shape=[jax.ShapeDtypeStruct((rows, cols), BF16)] * blocks,
-        compiler_params=pltpu.CompilerParams(vmem_limit_bytes=VMEM_LIMIT),
+        functools.partial(merge_kernel, heads=heads, plane=plane, waits=len(after)),
+        in_specs=waiting_specs(heads * plane, len(after)),
+        out_shape=[jax.ShapeDtypeStruct((rows, heads * cols), BF16)] * blocks,
+        compiler_params=pltpu.CompilerParams(vmem_limit_bytes=SHORT_VMEM),
         cost_estimate=SHORT,
         name="merge",
-    )(*pieces, *after)
+    )(*[p for own in pieces for p in own], *after)
 
 
 def normalize_pieces(pieces, after):
     rows, cols = pieces[0].shape
+    heads = cols // (GROUP_QUERIES * HEAD_SIZE + LANES)
     return pl.pallas_call(
-        functools.partial(normalize_kernel, count=len(pieces)),
-        in_specs=waiting_specs(pieces, after),
-        out_shape=jax.ShapeDtypeStruct((rows, cols - LANES), BF16),
-        compiler_params=pltpu.CompilerParams(vmem_limit_bytes=VMEM_LIMIT),
+        functools.partial(normalize_kernel, heads=heads, count=len(pieces)),
+        in_specs=waiting_specs(len(pieces), len(after)),
+        out_shape=jax.ShapeDtypeStruct((rows, cols - heads * LANES), BF16),
+        compiler_params=pltpu.CompilerParams(vmem_limit_bytes=SHORT_VMEM),
         cost_estimate=SHORT,
         name="normalize",
     )(*pieces, *after)
 
 
-def project_kernel(info, *refs, plane, blocks, rows, width):
-    ins, (w_ref, *base_ref, out) = refs[:plane], refs[plane:]
-    for b in range(plane):
-        x = ins[b][...].reshape(blocks * rows, width)
+def project_kernel(info, *refs, chosen, blocks, rows, width):
+    ins, (w_ref, *base_ref, out) = refs[: len(chosen)], refs[len(chosen) :]
+    if base_ref:
+        out[...] = base_ref[0][...].astype(out.dtype)
+    for x_ref, b in zip(ins, chosen):
+        x = x_ref[...].reshape(blocks * rows, width)
         y = jnp.dot(x, w_ref[...], preferred_element_type=F32)
         for a in range(blocks):
             at = (info[3 + blocks + a], b ^ info[1])
@@ -300,32 +313,32 @@
             out[at] = ((base_ref[0][at] + part) if base_ref else part).astype(out.dtype)
 
 
-def project(info, pieces, weight, group, base, dtype):
+def project(info, pieces, chosen, weight, group, base, dtype):
     plane = len(pieces)
     blocks, rows, width = pieces[0].shape
     out_cols = weight.shape[1]
-    span = plane * blocks * rows
+    span = len(chosen) * blocks * rows
     whole = pl.BlockSpec((blocks, rows, width), lambda i, s: (0, 0, 0))
     out_block = pl.BlockSpec((blocks, plane, rows, out_cols), lambda i, s: (0, 0, 0, 0))
     return pl.pallas_call(
-        functools.partial(project_kernel, plane=plane, blocks=blocks, rows=rows, width=width),
+        functools.partial(project_kernel, chosen=chosen, blocks=blocks, rows=rows, width=width),
         grid_spec=pltpu.PrefetchScalarGridSpec(
             num_scalar_prefetch=1,
             grid=(1,),
-            in_specs=[whole] * plane
+            in_specs=[whole] * len(chosen)
             + [pl.BlockSpec((width, out_cols), lambda i, s: (group, 0))]
             + [out_block] * len(base),
             out_specs=out_block,
         ),
         out_shape=jax.ShapeDtypeStruct((blocks, plane, rows, out_cols), dtype),
-        compiler_params=pltpu.CompilerParams(vmem_limit_bytes=VMEM_LIMIT),
+        compiler_params=pltpu.CompilerParams(vmem_limit_bytes=SHORT_VMEM),
         cost_estimate=pl.CostEstimate(
             flops=2 * span * width * out_cols,
             bytes_accessed=2 * (width * out_cols + span * width),
             transcendentals=0,
         ),
         name="project",
-    )(info, *pieces, weight, *base)
+    )(info, *[pieces[b] for b in chosen], weight, *base)
 
 
 def exchange(x, axis, distance):
@@ -361,55 +374,56 @@
 
     first = stack_blocks(queries[:, :width])
     sources, stacks = [(gather_plane(first), 0)], []
+    keys, _ = lax.optimization_barrier((context_keys, first))
+    keys_t = keys.T
     if heads > 1:
         held, _ = lax.optimization_barrier((queries[:, width:], first))
         stacks = [stack_blocks(held)]
         pieces = gather_plane(stacks[0])
         sources += [(pieces, i) for i in range(heads - 1)]
 
-    keys_t = context_keys.T
-
+    size = 2 if heads % 2 == 0 else 1
     attended, merged, rows_of = [], [], []
 
-    def attend(h, after):
-        attended.append(
-            attend_head(info, *sources[h], keys_t, context_values, span_keys, span_values, h, after)
-        )
-
-    def merge(h, after):
-        own = attended[h]
-        parts = [own[0]] + [exchange(own[b], "ctx", b) for b in range(1, plane)]
+    def merge(after):
+        group = range(len(merged) * size, (len(merged) + 1) * size)
+        parts = [
+            [attended[h][0]] + [exchange(attended[h][b], "ctx", b) for b in range(1, plane)] for h in group
+        ]
         merged.append(merge_pieces(parts, after))
-
-    def normalize(h, after):
-        own = merged[h]
+        return [merged[-1][0]]
+
+    def normalize(after):
+        own = merged[len(rows_of)]
         parts = [own[0]] + [exchange(own[a], "ctx", a * plane) for a in range(1, blocks)]
         rows_of.append(normalize_pieces(parts, after))
+        return [rows_of[-1]]
 
     latest = stacks
     for h in range(heads):
-        attend(h, latest)
+        attended.append(
+            attend_head(info, *sources[h], keys_t, context_values, span_keys, span_values, h, latest)
+        )
         latest = [attended[h][0]]
-        if h >= 1:
-            merge(h - 1, latest)
-            latest = [merged[h - 1][0]]
-        if h >= 2:
-            normalize(h - 2, latest)
-            latest = [rows_of[h - 2]]
-    merge(heads - 1, latest)
-    held, _ = lax.optimization_barrier((rows_of, merged[-1][0]))
-    rows_of = list(held)
-    for h in range(len(rows_of), heads):
-        normalize(h, [merged[-1][0]])
-    size = 2 if heads % 2 == 0 else 1
-    groups = [list(range(h, h + size)) for h in range(0, heads, size)]
+        if len(rows_of) < len(merged):
+            latest = normalize(latest)
+        if h >= (len(merged) + 1) * size:
+            latest = merge(latest)
+    while len(merged) < heads // size:
+        latest = merge(latest)
+    while len(rows_of) < heads // size:
+        latest = normalize(latest)
+
     total = []
-    for g, group in enumerate(groups):
-        stack = stack_blocks(jnp.concatenate([rows_of[h] for h in group], axis=1))
-        if total:
-            stack, _ = lax.optimization_barrier((stack, total[0]))
-        dtype = BF16 if g == len(groups) - 1 else F32
-        total = [project(info, gather_plane(stack), out_weight, g, total, dtype)]
+    for g, rows_now in enumerate(rows_of):
+        if g < len(rows_of) - 1:
+            rows_now, _ = lax.optimization_barrier((rows_now, merged[-1][0]))
+        pieces = gather_plane(stack_blocks(rows_now))
+        if g < len(rows_of) - 1:
+            total = [project(info, pieces, range(plane), out_weight, g, total, F32)]
+        else:
+            total = [project(info, pieces, range(plane // 2), out_weight, g, total, F32)]
+            total = [project(info, pieces, range(plane // 2, plane), out_weight, g, total, BF16)]
     partial_out = total[0].reshape(ctx_count * rows, -1)
     share = partial_out.shape[0] // head_count
     total = lax.dynamic_slice_in_dim(partial_out, my_head * share, share, 0).astype(F32)

time: 282 us -> 243 us (0.86)
  starting transfers between devices: 84.9 us -> 64.2 us
  Pallas kernels: 123 us -> 113 us
  local copies, waits for them, and re-layouts: 20.4 us -> 16.6 us
    ppermute x49 -> x43, starting transfers between devices: 84.9 us -> 64.2 us  [exchange(): return lax.ppermute(x, axis, [(i, i ^ distance) for i in range(count)])]
    pallas_call x10 -> x7, Pallas kernels: 28.9 us -> 11.2 us  [the longest x3 6.56 us: project(): pl.pallas_call(functools.partial(project_kernel, chosen=chosen, blocks=bl...]
    unnamed x90 -> x16, local copies, waits for them, and re-layouts: 14.8 us -> 6.96 us
    pallas_call x4, Pallas kernels: 94 us -> 102 us  [attend_head(): pl.pallas_call(functools.partial(attend_kernel, plane=plane, blocks=block...]
    optimization_barrier x0 -> x1, local copies, waits for them, and re-layouts: none -> 6.41 us  [local(): keys, _ = lax.optimization_barrier((context_keys, first))]
    ppermute x49 -> x43, waiting for transfers between devices: 45.8 us -> 44.6 us  [exchange(): return lax.ppermute(x, axis, [(i, i ^ distance) for i in range(count)])]
  transfers between devices with their start and end apart: 49 -> 43, of which waited for: 14 -> 13; matrix products, arithmetic and copies ran while one was open for 5% -> 5% of each run, Pallas kernels for 40% -> 45%
where the time goes in v4:
time: 243 us; the launch traced here: 242 us
  Pallas kernels  113 us (47%)
  starting transfers between devices  64.2 us (26%)
  waiting for transfers between devices  44.6 us (18%)
  local copies, waits for them, and re-layouts  16.6 us (7%)
  other arithmetic  3.37 us (1%)
    pallas_call x4, Pallas kernels, attend_head(): pl.pallas_call(functools.partial(attend_kernel, plane=plane, blocks=block...  102 us
    ppermute x43, starting transfers between devices, exchange(): return lax.ppermute(x, axis, [(i, i ^ distance) for i in range(count)])  64.2 us
    ppermute x43, waiting for transfers between devices, exchange(): return lax.ppermute(x, axis, [(i, i ^ distance) for i in range(count)])  44.6 us
    unnamed x16, local copies, waits for them, and re-layouts  6.96 us
    pallas_call x3, Pallas kernels, project(): pl.pallas_call(functools.partial(project_kernel, chosen=chosen, blocks=bl...  6.56 us
    optimization_barrier x1, local copies, waits for them, and re-layouts, local(): keys, _ = lax.optimization_barrier((context_keys, first))  6.41 us
  transfers between devices with their start and end apart: 43, of which 13 were waited for; matrix products, arithmetic and copies ran while one was open for 5% of the time, Pallas kernels for 45%

profile of v4, /device:TPU:0, one launch (start us, length us, event | category | flops | bytes accessed | tf_op | source)
XLA Modules:
  0.0 241.8 jit_solution(6470701332788143868)
XLA Ops:
  0.0 0.8 slice_bitcast_fusion
  0.9 5.1 %collective-permute-start.2 = (bf16[32,1024]{1,0:T(8,128)(2,1)S(1)}, bf16[32,1024]{1,0:T(8,128)(2,1)S(1)}, u32[]{:S(2)}, u32[]{:S(2)}) collective-permute-start(bf16[32,1024]{1,0:T(8,128)(2,1)S(1)} %get-tuple-element.62), channel_id=1, source_target_pairs={{0,24},{2,26},{4,28},{6,30},{8,16},{10,18},{12,20},{14,22},{16,8},... | collective-permute-start | bytes 196616 | tf_op jit(solution)/shard_map/ppermute | solution.py:346
  6.0 0.6 collective-permute-start
  6.6 0.9 slice.6
  7.6 0.8 compare_reduce_fusion
  8.4 0.6 gather_fusion
  9.0 0.8 sort.17
  9.9 1.7 collective-permute-done.1
  11.6 2.8 %collective-permute-start.5 = (bf16[32,3072]{1,0:T(8,128)(2,1)S(1)}, bf16[32,3072]{1,0:T(8,128)(2,1)S(1)}, u32[]{:S(2)}, u32[]{:S(2)}) collective-permute-start(bf16[32,3072]{1,0:T(8,128)(2,1)S(1)} %slice.6), channel_id=1, source_target_pairs={{0,24},{2,26},{4,28},{6,30},{8,16},{10,18},{12,20},{14,22},{16,8},... | collective-permute-start | bytes 589832 | tf_op jit(solution)/shard_map/ppermute | solution.py:346
  14.4 1.7 collective-permute-start.3
  16.1 0.7 convert_reduce_fusion
  16.8 0.7 concatenate.3.info
  17.5 1.6 collective-permute-start.9
  19.1 1.5 collective-permute-start.10
  20.6 6.4 %copy.9 = bf16[4096,512]{0,1:T(8,128)(2,1)} copy(bf16[4096,512]{1,0:T(8,128)(2,1)} %param.10) | data formatting | bytes 8388608 | tf_op jit(solution)/shard_map/optimization_barrier | solution.py:377
  27.5 3.0 %collective-permute-done.4 = bf16[32,3072]{1,0:T(8,128)(2,1)S(1)} collective-permute-done((bf16[32,3072]{1,0:T(8,128)(2,1)S(1)}, bf16[32,3072]{1,0:T(8,128)(2,1)S(1)}, u32[]{:S(2)}, u32[]{:S(2)}) %collective-permute-start.4) | collective-permute-done | bytes 196640 | tf_op jit(solution)/shard_map/ppermute | solution.py:346
  30.6 1.6 collective-permute-start.6
  32.2 1.5 collective-permute-start.7
  34.2 2.4 %collective-permute-done.11.refs_3_ = bf16[4,32,1024]{2,1,0:T(8,128)(2,1)S(1)} collective-permute-done((bf16[4,32,1024]{2,1,0:T(8,128)(2,1)S(1)}, bf16[4,32,1024]{2,1,0:T(8,128)(2,1)S(1)}, u32[]{:S(2)}, u32[]{:S(2)}) %collective-permute-start.11) | collective-permute-done | bytes 262176 | tf_op jit(solution)/shard_map/ppermute | solution.py:346
  36.6 2.2 copy-done.2
  38.8 2.2 copy-done.4
  41.0 25.3 %attend.4 = (bf16[4,32,1152]{2,1,0:T(8,128)(2,1)S(1)}, bf16[4,32,1152]{2,1,0:T(8,128)(2,1)S(1)}, bf16[4,32,1152]{2,1,0:T(8,128)(2,1)S(1)}, bf16[4,32,1152]{2,1,0:T(8,128)(2,1)S(1)}) custom-call(s32[11]{0:T(128)S(1)} %concatenate.3.info, bf16[4,32,1024]{2,1,0:T(8,128)(2,1)S(1)} %pad_maximum_fusion.3.refs_0_, ...), custom_call_target="tpu_custom_call" | custom-call | flops 17179869184 | bytes 4194304 | tf_op jit(solution)/shard_map/attend/pallas_call | solution.py:178
  66.4 0.9 collective-permute-start.16
  67.2 2.6 %collective-permute-start.17 = (bf16[4,32,1152]{2,1,0:T(8,128)(2,1)S(1)}, bf16[4,32,1152]{2,1,0:T(8,128)(2,1)S(1)}, u32[]{:S(2)}, u32[]{:S(2)}) collective-permute-start(bf16[4,32,1152]{2,1,0:T(8,128)(2,1)S(1)} %get-tuple-element.44), channel_id=1, source_target_pairs={{0,6},{2,4},{4,2},{6,0},{8,14},{10,12},{12,10},{14,8},{16,22},{18,... | collective-permute-start | bytes 884744 | tf_op jit(solution)/shard_map/ppermute | solution.py:346
  70.3 25.4 %attend.5 = (bf16[4,32,1152]{2,1,0:T(8,128)(2,1)S(1)}, bf16[4,32,1152]{2,1,0:T(8,128)(2,1)S(1)}, bf16[4,32,1152]{2,1,0:T(8,128)(2,1)S(1)}, bf16[4,32,1152]{2,1,0:T(8,128)(2,1)S(1)}) custom-call(s32[11]{0:T(128)S(1)} %concatenate.3.info, bf16[4,32,3072]{2,1,0:T(8,128)(2,1)S(1)} %pad_maximum_fusion.refs_8_.refs_0_, ...), custom_call_target="tpu_custom_call" | custom-call | flops 17179869184 | bytes 4194304 | tf_op jit(solution)/shard_map/attend/pallas_call | solution.py:178
  95.8 0.9 collective-permute-start.19
  96.7 2.6 %collective-permute-start.20 = (bf16[4,32,1152]{2,1,0:T(8,128)(2,1)S(1)}, bf16[4,32,1152]{2,1,0:T(8,128)(2,1)S(1)}, u32[]{:S(2)}, u32[]{:S(2)}) collective-permute-start(bf16[4,32,1152]{2,1,0:T(8,128)(2,1)S(1)} %get-tuple-element.47), channel_id=1, source_target_pairs={{0,6},{2,4},{4,2},{6,0},{8,14},{10,12},{12,10},{14,8},{16,22},{18,... | collective-permute-start | bytes 884744 | tf_op jit(solution)/shard_map/ppermute | solution.py:346
  99.3 25.6 %attend.6 = (bf16[4,32,1152]{2,1,0:T(8,128)(2,1)S(1)}, bf16[4,32,1152]{2,1,0:T(8,128)(2,1)S(1)}, bf16[4,32,1152]{2,1,0:T(8,128)(2,1)S(1)}, bf16[4,32,1152]{2,1,0:T(8,128)(2,1)S(1)}) custom-call(s32[11]{0:T(128)S(1)} %concatenate.3.info, bf16[4,32,3072]{2,1,0:T(8,128)(2,1)S(1)} %pad_maximum_fusion.refs_8_.refs_0_, ...), custom_call_target="tpu_custom_call" | custom-call | flops 17179869184 | bytes 4194304 | tf_op jit(solution)/shard_map/attend/pallas_call | solution.py:178
  124.9 0.9 collective-permute-start.13
  125.8 1.7 merge.2
  127.5 4.0 %collective-permute-start.24 = (bf16[32,2304]{1,0:T(8,128)(2,1)S(1)}, bf16[32,2304]{1,0:T(8,128)(2,1)S(1)}, u32[]{:S(2)}, u32[]{:S(2)}) collective-permute-start(bf16[32,2304]{1,0:T(8,128)(2,1)S(1)} %get-tuple-element.53), channel_id=1, source_target_pairs={{0,8},{2,10},{4,12},{6,14},{8,0},{10,2},{12,4},{14,6},{16,24},{18,... | collective-permute-start | bytes 442376 | tf_op jit(solution)/shard_map/ppermute | solution.py:346
  131.6 2.4 %collective-permute-start.26 = (bf16[32,2304]{1,0:T(8,128)(2,1)S(1)}, bf16[32,2304]{1,0:T(8,128)(2,1)S(1)}, u32[]{:S(2)}, u32[]{:S(2)}) collective-permute-start(bf16[32,2304]{1,0:T(8,128)(2,1)S(1)} %get-tuple-element.55), channel_id=1, source_target_pairs={{0,24},{2,26},{4,28},{6,30},{8,16},{10,18},{12,20},{14,22},{16,8},... | collective-permute-start | bytes 442376 | tf_op jit(solution)/shard_map/ppermute | solution.py:346
  134.0 25.4 %attend.7 = (bf16[4,32,1152]{2,1,0:T(8,128)(2,1)S(1)}, bf16[4,32,1152]{2,1,0:T(8,128)(2,1)S(1)}, bf16[4,32,1152]{2,1,0:T(8,128)(2,1)S(1)}, bf16[4,32,1152]{2,1,0:T(8,128)(2,1)S(1)}) custom-call(s32[11]{0:T(128)S(1)} %concatenate.3.info, bf16[4,32,3072]{2,1,0:T(8,128)(2,1)S(1)} %pad_maximum_fusion.refs_8_.refs_0_, ...), custom_call_target="tpu_custom_call" | custom-call | flops 17179869184 | bytes 4194304 | tf_op jit(solution)/shard_map/attend/pallas_call | solution.py:178
  159.5 2.0 collective-permute-start.21
  161.5 1.5 collective-permute-start.22
  163.1 0.6 normalize.2.refs_8_
  163.7 3.6 %collective-permute-done.14.refs_3_ = bf16[4,32,1152]{2,1,0:T(8,128)(2,1)S(1)} collective-permute-done((bf16[4,32,1152]{2,1,0:T(8,128)(2,1)S(1)}, bf16[4,32,1152]{2,1,0:T(8,128)(2,1)S(1)}, u32[]{:S(2)}, u32[]{:S(2)}) %collective-permute-start.14) | collective-permute-done | bytes 294944 | tf_op jit(solution)/shard_map/ppermute | solution.py:346
  167.3 3.4 %collective-permute-done.21.refs_5_ = bf16[4,32,1152]{2,1,0:T(8,128)(2,1)S(1)} collective-permute-done((bf16[4,32,1152]{2,1,0:T(8,128)(2,1)S(1)}, bf16[4,32,1152]{2,1,0:T(8,128)(2,1)S(1)}, u32[]{:S(2)}, u32[]{:S(2)}) %collective-permute-start.21) | collective-permute-done | bytes 294944 | tf_op jit(solution)/shard_map/ppermute | solution.py:346
  170.7 2.9 %collective-permute-done.23.refs_7_ = bf16[4,32,1152]{2,1,0:T(8,128)(2,1)S(1)} collective-permute-done((bf16[4,32,1152]{2,1,0:T(8,128)(2,1)S(1)}, bf16[4,32,1152]{2,1,0:T(8,128)(2,1)S(1)}, u32[]{:S(2)}, u32[]{:S(2)}) %collective-permute-start.23) | collective-permute-done | bytes 294944 | tf_op jit(solution)/shard_map/ppermute | solution.py:346
  173.5 1.7 merge.3
  175.2 2.8 %collective-permute-start.38 = (bf16[32,2048]{1,0:T(8,128)(2,1)S(1)}, bf16[32,2048]{1,0:T(8,128)(2,1)S(1)}, u32[]{:S(2)}, u32[]{:S(2)}) collective-permute-start(bf16[32,2048]{1,0:T(8,128)(2,1)S(1)} %normalize.2.refs_8_), channel_id=1, source_target_pairs={{0,24},{2,26},{4,28},{6,30},{8,16},{10,18},{12,20},{14,22},{16,8},... | collective-permute-start | bytes 393224 | tf_op jit(solution)/shard_map/ppermute | solution.py:346
  178.0 1.7 collective-permute-start.36
  180.1 2.9 %collective-permute-start.28 = (bf16[32,2304]{1,0:T(8,128)(2,1)S(1)}, bf16[32,2304]{1,0:T(8,128)(2,1)S(1)}, u32[]{:S(2)}, u32[]{:S(2)}) collective-permute-start(bf16[32,2304]{1,0:T(8,128)(2,1)S(1)} %get-tuple-element.58), channel_id=1, source_target_pairs={{0,16},{2,18},{4,20},{6,22},{8,24},{10,26},{12,28},{14,30},{16,0},... | collective-permute-start | bytes 442376 | tf_op jit(solution)/shard_map/ppermute | solution.py:346
  183.0 2.0 collective-permute-start.29
  185.0 3.4 %collective-permute-done.37 = bf16[32,2048]{1,0:T(8,128)(2,1)S(1)} collective-permute-done((bf16[32,2048]{1,0:T(8,128)(2,1)S(1)}, bf16[32,2048]{1,0:T(8,128)(2,1)S(1)}, u32[]{:S(2)}, u32[]{:S(2)}) %collective-permute-start.37) | collective-permute-done | bytes 131104 | tf_op jit(solution)/shard_map/ppermute | solution.py:346
  188.5 6.3 %collective-permute-start.39 = (bf16[4,32,2048]{2,1,0:T(8,128)(2,1)S(1)}, bf16[4,32,2048]{2,1,0:T(8,128)(2,1)S(1)}, u32[]{:S(2)}, u32[]{:S(2)}) collective-permute-start(bf16[4,32,2048]{2,1,0:T(8,128)(2,1)S(1)} %pad_maximum_fusion.2.refs_0_), channel_id=1, source_target_pairs={{0,2},{2,0},{4,6},{6,4},{8,10},{10,8},{12,14},{14,12},{16,18},{18,... | collective-permute-start | bytes 1572872 | tf_op jit(solution)/shard_map/ppermute | solution.py:346
  194.7 1.4 collective-permute-done.28.refs_2_
  196.1 0.6 normalize.3
  196.7 3.2 %collective-permute-start.32 = (bf16[32,2048]{1,0:T(8,128)(2,1)S(1)}, bf16[32,2048]{1,0:T(8,128)(2,1)S(1)}, u32[]{:S(2)}, u32[]{:S(2)}) collective-permute-start(bf16[32,2048]{1,0:T(8,128)(2,1)S(1)} %normalize.3), channel_id=1, source_target_pairs={{0,24},{2,26},{4,28},{6,30},{8,16},{10,18},{12,20},{14,22},{16,8},... | collective-permute-start | bytes 393224 | tf_op jit(solution)/shard_map/ppermute | solution.py:346
  200.0 1.7 collective-permute-start.31
  202.1 1.5 collective-permute-start.40
  203.6 1.8 collective-permute-start.41
  205.4 2.4 collective-permute-done.31
  207.9 1.7 collective-permute-start.35
  209.6 0.9 collective-permute-start.33
  210.4 1.4 collective-permute-start.34
  211.8 14.0 %collective-permute-done.40.refs_2_ = bf16[4,32,2048]{2,1,0:T(8,128)(2,1)S(1)} collective-permute-done((bf16[4,32,2048]{2,1,0:T(8,128)(2,1)S(1)}, bf16[4,32,2048]{2,1,0:T(8,128)(2,1)S(1)}, u32[]{:S(2)}, u32[]{:S(2)}) %collective-permute-start.40) | collective-permute-done | bytes 524320 | tf_op jit(solution)/shard_map/ppermute | solution.py:346
  225.8 2.2 copy-done
  228.0 1.8 project.3.refs_3_
  230.2 2.4 project.4.refs_3_
  232.6 4.4 %collective-permute-done.33.refs_0_ = bf16[4,32,2048]{2,1,0:T(8,128)(2,1)S(1)} collective-permute-done((bf16[4,32,2048]{2,1,0:T(8,128)(2,1)S(1)}, bf16[4,32,2048]{2,1,0:T(8,128)(2,1)S(1)}, u32[]{:S(2)}, u32[]{:S(2)}) %collective-permute-start.33) | collective-permute-done | bytes 524320 | tf_op jit(solution)/shard_map/ppermute | solution.py:346
  237.0 2.4 project.5
  239.5 1.5 collective-permute-done.42
  241.1 0.8 add_convert_fusion
  (68 shorter events, 3.3 us)
Async XLA Ops:
  0.9 9.0 %collective-permute-start.2 = (bf16[32,1024]{1,0:T(8,128)(2,1)S(1)}, bf16[32,1024]{1,0:T(8,128)(2,1)S(1)}, u32[]{:S(2)}, u32[]{:S(2)}) collective-permute-start(bf16[32,1024]{1,0:T(8,128)(2,1)S(1)} %get-tuple-element.62), channel_id=1, source_target_pairs={{0,24},{2,26},{4,28},{6,30},{8,16},{10,18},{12,20},{14,22},{16,8},... | collective-permute-start | bytes 196616 | tf_op jit(solution)/shard_map/ppermute | solution.py:346
  6.0 5.6 %collective-permute-start.1 = (bf16[32,1024]{1,0:T(8,128)(2,1)S(1)}, bf16[32,1024]{1,0:T(8,128)(2,1)S(1)}, u32[]{:S(2)}, u32[]{:S(2)}) collective-permute-start(bf16[32,1024]{1,0:T(8,128)(2,1)S(1)} %get-tuple-element.62), channel_id=1, source_target_pairs={{0,16},{2,18},{4,20},{6,22},{8,24},{10,26},{12,28},{14,30},{16,0},... | collective-permute-start | bytes 196616 | tf_op jit(solution)/shard_map/ppermute | solution.py:346
  6.0 5.6 %collective-permute-start = (bf16[32,1024]{1,0:T(8,128)(2,1)S(1)}, bf16[32,1024]{1,0:T(8,128)(2,1)S(1)}, u32[]{:S(2)}, u32[]{:S(2)}) collective-permute-start(bf16[32,1024]{1,0:T(8,128)(2,1)S(1)} %get-tuple-element.62), channel_id=1, source_target_pairs={{0,8},{2,10},{4,12},{6,14},{8,0},{10,2},{12,4},{14,6},{16,24},{18,... | collective-permute-start | bytes 196616 | tf_op jit(solution)/shard_map/ppermute | solution.py:346
  11.6 15.4 %collective-permute-start.5 = (bf16[32,3072]{1,0:T(8,128)(2,1)S(1)}, bf16[32,3072]{1,0:T(8,128)(2,1)S(1)}, u32[]{:S(2)}, u32[]{:S(2)}) collective-permute-start(bf16[32,3072]{1,0:T(8,128)(2,1)S(1)} %slice.6), channel_id=1, source_target_pairs={{0,24},{2,26},{4,28},{6,30},{8,16},{10,18},{12,20},{14,22},{16,8},... | collective-permute-start | bytes 589832 | tf_op jit(solution)/shard_map/ppermute | solution.py:346
  14.4 16.1 %collective-permute-start.4 = (bf16[32,3072]{1,0:T(8,128)(2,1)S(1)}, bf16[32,3072]{1,0:T(8,128)(2,1)S(1)}, u32[]{:S(2)}, u32[]{:S(2)}) collective-permute-start(bf16[32,3072]{1,0:T(8,128)(2,1)S(1)} %slice.6), channel_id=1, source_target_pairs={{0,16},{2,18},{4,20},{6,22},{8,24},{10,26},{12,28},{14,30},{16,0},... | collective-permute-start | bytes 589832 | tf_op jit(solution)/shard_map/ppermute | solution.py:346
  14.4 16.1 %collective-permute-start.3 = (bf16[32,3072]{1,0:T(8,128)(2,1)S(1)}, bf16[32,3072]{1,0:T(8,128)(2,1)S(1)}, u32[]{:S(2)}, u32[]{:S(2)}) collective-permute-start(bf16[32,3072]{1,0:T(8,128)(2,1)S(1)} %slice.6), channel_id=1, source_target_pairs={{0,8},{2,10},{4,12},{6,14},{8,0},{10,2},{12,4},{14,6},{16,24},{18,... | collective-permute-start | bytes 589832 | tf_op jit(solution)/shard_map/ppermute | solution.py:346
  17.5 19.1 %copy-start.6 = (bf16[32,512]{1,0:T(8,128)(2,1)S(1)}, bf16[32,512]{1,0:T(8,128)(2,1)}, u32[]{:S(2)}) copy-start(bf16[32,512]{1,0:T(8,128)(2,1)} %refs_6_.7) | copy-start | bytes 98308
  17.5 19.1 %copy-start.7 = (bf16[32,512]{1,0:T(8,128)(2,1)S(1)}, bf16[32,512]{1,0:T(8,128)(2,1)}, u32[]{:S(2)}) copy-start(bf16[32,512]{1,0:T(8,128)(2,1)} %refs_7_.7) | copy-start | bytes 98308
  17.5 16.2 %collective-permute-start.9 = (bf16[4,32,1024]{2,1,0:T(8,128)(2,1)S(1)}, bf16[4,32,1024]{2,1,0:T(8,128)(2,1)S(1)}, u32[]{:S(2)}, u32[]{:S(2)}) collective-permute-start(bf16[4,32,1024]{2,1,0:T(8,128)(2,1)S(1)} %pad_maximum_fusion.3.refs_0_), channel_id=1, source_target_pairs={{0,2},{2,0},{4,6},{6,4},{8,10},{10,8},{12,14},{14,12},{16,18},{18,... | collective-permute-start | bytes 786440 | tf_op jit(solution)/shard_map/ppermute | solution.py:346
  19.1 15.1 %collective-permute-start.10 = (bf16[4,32,1024]{2,1,0:T(8,128)(2,1)S(1)}, bf16[4,32,1024]{2,1,0:T(8,128)(2,1)S(1)}, u32[]{:S(2)}, u32[]{:S(2)}) collective-permute-start(bf16[4,32,1024]{2,1,0:T(8,128)(2,1)S(1)} %pad_maximum_fusion.3.refs_0_), channel_id=1, source_target_pairs={{0,4},{2,6},{4,0},{6,2},{8,12},{10,14},{12,8},{14,10},{16,20},{18,... | collective-permute-start | bytes 786440 | tf_op jit(solution)/shard_map/ppermute | solution.py:346
  27.0 9.6 %collective-permute-start.11 = (bf16[4,32,1024]{2,1,0:T(8,128)(2,1)S(1)}, bf16[4,32,1024]{2,1,0:T(8,128)(2,1)S(1)}, u32[]{:S(2)}, u32[]{:S(2)}) collective-permute-start(bf16[4,32,1024]{2,1,0:T(8,128)(2,1)S(1)} %pad_maximum_fusion.3.refs_0_), channel_id=1, source_target_pairs={{0,6},{2,4},{4,2},{6,0},{8,14},{10,12},{12,10},{14,8},{16,22},{18,... | collective-permute-start | bytes 786440 | tf_op jit(solution)/shard_map/ppermute | solution.py:346
  30.6 36.7 %collective-permute-start.6 = (bf16[4,32,3072]{2,1,0:T(8,128)(2,1)S(1)}, bf16[4,32,3072]{2,1,0:T(8,128)(2,1)S(1)}, u32[]{:S(2)}, u32[]{:S(2)}) collective-permute-start(bf16[4,32,3072]{2,1,0:T(8,128)(2,1)S(1)} %pad_maximum_fusion.refs_8_.refs_0_), channel_id=1, source_target_pairs={{0,2},{2,0},{4,6},{6,4},{8,10},{10,8},{12,14},{14,12},{16,18},{18,... | collective-permute-start | bytes 2359304 | tf_op jit(solution)/shard_map/ppermute | solution.py:346
  32.2 37.6 %collective-permute-start.7 = (bf16[4,32,3072]{2,1,0:T(8,128)(2,1)S(1)}, bf16[4,32,3072]{2,1,0:T(8,128)(2,1)S(1)}, u32[]{:S(2)}, u32[]{:S(2)}) collective-permute-start(bf16[4,32,3072]{2,1,0:T(8,128)(2,1)S(1)} %pad_maximum_fusion.refs_8_.refs_0_), channel_id=1, source_target_pairs={{0,4},{2,6},{4,0},{6,2},{8,12},{10,14},{12,8},{14,10},{16,20},{18,... | collective-permute-start | bytes 2359304 | tf_op jit(solution)/shard_map/ppermute | solution.py:346
  33.7 36.6 %collective-permute-start.8 = (bf16[4,32,3072]{2,1,0:T(8,128)(2,1)S(1)}, bf16[4,32,3072]{2,1,0:T(8,128)(2,1)S(1)}, u32[]{:S(2)}, u32[]{:S(2)}) collective-permute-start(bf16[4,32,3072]{2,1,0:T(8,128)(2,1)S(1)} %pad_maximum_fusion.refs_8_.refs_0_), channel_id=1, source_target_pairs={{0,6},{2,4},{4,2},{6,0},{8,14},{10,12},{12,10},{14,8},{16,22},{18,... | collective-permute-start | bytes 2359304 | tf_op jit(solution)/shard_map/ppermute | solution.py:346
  36.6 2.2 copy-start.2
  38.8 2.2 copy-start.4
  41.0 29.4 %copy-start.3 = (bf16[4096,512]{0,1:T(8,128)(2,1)S(1)}, bf16[4096,512]{0,1:T(8,128)(2,1)}, u32[]{:S(2)}) copy-start(bf16[4096,512]{0,1:T(8,128)(2,1)} %copy.9) | copy-start | bytes 12582916
  41.0 29.4 %copy-start.5 = (bf16[4096,512]{1,0:T(8,128)(2,1)S(1)}, bf16[4096,512]{1,0:T(8,128)(2,1)}, u32[]{:S(2)}) copy-start(bf16[4096,512]{1,0:T(8,128)(2,1)} %refs_5_.7) | copy-start | bytes 12582916
  66.3 30.4 %collective-permute-start.15 = (bf16[4,32,1152]{2,1,0:T(8,128)(2,1)S(1)}, bf16[4,32,1152]{2,1,0:T(8,128)(2,1)S(1)}, u32[]{:S(2)}, u32[]{:S(2)}) collective-permute-start(bf16[4,32,1152]{2,1,0:T(8,128)(2,1)S(1)} %get-tuple-element.42), channel_id=1, source_target_pairs={{0,2},{2,0},{4,6},{6,4},{8,10},{10,8},{12,14},{14,12},{16,18},{18,... | collective-permute-start | bytes 884744 | tf_op jit(solution)/shard_map/ppermute | solution.py:346
  66.4 58.5 %collective-permute-start.16 = (bf16[4,32,1152]{2,1,0:T(8,128)(2,1)S(1)}, bf16[4,32,1152]{2,1,0:T(8,128)(2,1)S(1)}, u32[]{:S(2)}, u32[]{:S(2)}) collective-permute-start(bf16[4,32,1152]{2,1,0:T(8,128)(2,1)S(1)} %get-tuple-element.43), channel_id=1, source_target_pairs={{0,4},{2,6},{4,0},{6,2},{8,12},{10,14},{12,8},{14,10},{16,20},{18,... | collective-permute-start | bytes 884744 | tf_op jit(solution)/shard_map/ppermute | solution.py:346
  67.2 57.7 %collective-permute-start.17 = (bf16[4,32,1152]{2,1,0:T(8,128)(2,1)S(1)}, bf16[4,32,1152]{2,1,0:T(8,128)(2,1)S(1)}, u32[]{:S(2)}, u32[]{:S(2)}) collective-permute-start(bf16[4,32,1152]{2,1,0:T(8,128)(2,1)S(1)} %get-tuple-element.44), channel_id=1, source_target_pairs={{0,6},{2,4},{4,2},{6,0},{8,14},{10,12},{12,10},{14,8},{16,22},{18,... | collective-permute-start | bytes 884744 | tf_op jit(solution)/shard_map/ppermute | solution.py:346
  95.7 30.1 %collective-permute-start.18 = (bf16[4,32,1152]{2,1,0:T(8,128)(2,1)S(1)}, bf16[4,32,1152]{2,1,0:T(8,128)(2,1)S(1)}, u32[]{:S(2)}, u32[]{:S(2)}) collective-permute-start(bf16[4,32,1152]{2,1,0:T(8,128)(2,1)S(1)} %get-tuple-element.45), channel_id=1, source_target_pairs={{0,2},{2,0},{4,6},{6,4},{8,10},{10,8},{12,14},{14,12},{16,18},{18,... | collective-permute-start | bytes 884744 | tf_op jit(solution)/shard_map/ppermute | solution.py:346
  95.8 30.0 %collective-permute-start.19 = (bf16[4,32,1152]{2,1,0:T(8,128)(2,1)S(1)}, bf16[4,32,1152]{2,1,0:T(8,128)(2,1)S(1)}, u32[]{:S(2)}, u32[]{:S(2)}) collective-permute-start(bf16[4,32,1152]{2,1,0:T(8,128)(2,1)S(1)} %get-tuple-element.46), channel_id=1, source_target_pairs={{0,4},{2,6},{4,0},{6,2},{8,12},{10,14},{12,8},{14,10},{16,20},{18,... | collective-permute-start | bytes 884744 | tf_op jit(solution)/shard_map/ppermute | solution.py:346
  96.7 29.2 %collective-permute-start.20 = (bf16[4,32,1152]{2,1,0:T(8,128)(2,1)S(1)}, bf16[4,32,1152]{2,1,0:T(8,128)(2,1)S(1)}, u32[]{:S(2)}, u32[]{:S(2)}) collective-permute-start(bf16[4,32,1152]{2,1,0:T(8,128)(2,1)S(1)} %get-tuple-element.47), channel_id=1, source_target_pairs={{0,6},{2,4},{4,2},{6,0},{8,14},{10,12},{12,10},{14,8},{16,22},{18,... | collective-permute-start | bytes 884744 | tf_op jit(solution)/shard_map/ppermute | solution.py:346
  124.8 34.6 %collective-permute-start.12 = (bf16[4,32,1152]{2,1,0:T(8,128)(2,1)S(1)}, bf16[4,32,1152]{2,1,0:T(8,128)(2,1)S(1)}, u32[]{:S(2)}, u32[]{:S(2)}) collective-permute-start(bf16[4,32,1152]{2,1,0:T(8,128)(2,1)S(1)} %get-tuple-element.39), channel_id=1, source_target_pairs={{0,2},{2,0},{4,6},{6,4},{8,10},{10,8},{12,14},{14,12},{16,18},{18,... | collective-permute-start | bytes 884744 | tf_op jit(solution)/shard_map/ppermute | solution.py:346
  124.9 38.8 %collective-permute-start.13 = (bf16[4,32,1152]{2,1,0:T(8,128)(2,1)S(1)}, bf16[4,32,1152]{2,1,0:T(8,128)(2,1)S(1)}, u32[]{:S(2)}, u32[]{:S(2)}) collective-permute-start(bf16[4,32,1152]{2,1,0:T(8,128)(2,1)S(1)} %get-tuple-element.40), channel_id=1, source_target_pairs={{0,4},{2,6},{4,0},{6,2},{8,12},{10,14},{12,8},{14,10},{16,20},{18,... | collective-permute-start | bytes 884744 | tf_op jit(solution)/shard_map/ppermute | solution.py:346
  127.5 32.0 %collective-permute-start.24 = (bf16[32,2304]{1,0:T(8,128)(2,1)S(1)}, bf16[32,2304]{1,0:T(8,128)(2,1)S(1)}, u32[]{:S(2)}, u32[]{:S(2)}) collective-permute-start(bf16[32,2304]{1,0:T(8,128)(2,1)S(1)} %get-tuple-element.53), channel_id=1, source_target_pairs={{0,8},{2,10},{4,12},{6,14},{8,0},{10,2},{12,4},{14,6},{16,24},{18,... | collective-permute-start | bytes 442376 | tf_op jit(solution)/shard_map/ppermute | solution.py:346
  131.6 29.9 %collective-permute-start.25 = (bf16[32,2304]{1,0:T(8,128)(2,1)S(1)}, bf16[32,2304]{1,0:T(8,128)(2,1)S(1)}, u32[]{:S(2)}, u32[]{:S(2)}) collective-permute-start(bf16[32,2304]{1,0:T(8,128)(2,1)S(1)} %get-tuple-element.54), channel_id=1, source_target_pairs={{0,16},{2,18},{4,20},{6,22},{8,24},{10,26},{12,28},{14,30},{16,0},... | collective-permute-start | bytes 442376 | tf_op jit(solution)/shard_map/ppermute | solution.py:346
  131.6 31.4 %collective-permute-start.26 = (bf16[32,2304]{1,0:T(8,128)(2,1)S(1)}, bf16[32,2304]{1,0:T(8,128)(2,1)S(1)}, u32[]{:S(2)}, u32[]{:S(2)}) collective-permute-start(bf16[32,2304]{1,0:T(8,128)(2,1)S(1)} %get-tuple-element.55), channel_id=1, source_target_pairs={{0,24},{2,26},{4,28},{6,30},{8,16},{10,18},{12,20},{14,22},{16,8},... | collective-permute-start | bytes 442376 | tf_op jit(solution)/shard_map/ppermute | solution.py:346
  159.4 7.9 %collective-permute-start.14 = (bf16[4,32,1152]{2,1,0:T(8,128)(2,1)S(1)}, bf16[4,32,1152]{2,1,0:T(8,128)(2,1)S(1)}, u32[]{:S(2)}, u32[]{:S(2)}) collective-permute-start(bf16[4,32,1152]{2,1,0:T(8,128)(2,1)S(1)} %get-tuple-element.41), channel_id=1, source_target_pairs={{0,6},{2,4},{4,2},{6,0},{8,14},{10,12},{12,10},{14,8},{16,22},{18,... | collective-permute-start | bytes 884744 | tf_op jit(solution)/shard_map/ppermute | solution.py:346
  159.5 11.2 %collective-permute-start.21 = (bf16[4,32,1152]{2,1,0:T(8,128)(2,1)S(1)}, bf16[4,32,1152]{2,1,0:T(8,128)(2,1)S(1)}, u32[]{:S(2)}, u32[]{:S(2)}) collective-permute-start(bf16[4,32,1152]{2,1,0:T(8,128)(2,1)S(1)} %get-tuple-element.50), channel_id=1, source_target_pairs={{0,2},{2,0},{4,6},{6,4},{8,10},{10,8},{12,14},{14,12},{16,18},{18,... | collective-permute-start | bytes 884744 | tf_op jit(solution)/shard_map/ppermute | solution.py:346
  161.5 9.2 %collective-permute-start.22 = (bf16[4,32,1152]{2,1,0:T(8,128)(2,1)S(1)}, bf16[4,32,1152]{2,1,0:T(8,128)(2,1)S(1)}, u32[]{:S(2)}, u32[]{:S(2)}) collective-permute-start(bf16[4,32,1152]{2,1,0:T(8,128)(2,1)S(1)} %get-tuple-element.51), channel_id=1, source_target_pairs={{0,4},{2,6},{4,0},{6,2},{8,12},{10,14},{12,8},{14,10},{16,20},{18,... | collective-permute-start | bytes 884744 | tf_op jit(solution)/shard_map/ppermute | solution.py:346
  163.0 10.6 %collective-permute-start.23 = (bf16[4,32,1152]{2,1,0:T(8,128)(2,1)S(1)}, bf16[4,32,1152]{2,1,0:T(8,128)(2,1)S(1)}, u32[]{:S(2)}, u32[]{:S(2)}) collective-permute-start(bf16[4,32,1152]{2,1,0:T(8,128)(2,1)S(1)} %get-tuple-element.52), channel_id=1, source_target_pairs={{0,6},{2,4},{4,2},{6,0},{8,14},{10,12},{12,10},{14,8},{16,22},{18,... | collective-permute-start | bytes 884744 | tf_op jit(solution)/shard_map/ppermute | solution.py:346
  175.2 7.8 %collective-permute-start.38 = (bf16[32,2048]{1,0:T(8,128)(2,1)S(1)}, bf16[32,2048]{1,0:T(8,128)(2,1)S(1)}, u32[]{:S(2)}, u32[]{:S(2)}) collective-permute-start(bf16[32,2048]{1,0:T(8,128)(2,1)S(1)} %normalize.2.refs_8_), channel_id=1, source_target_pairs={{0,24},{2,26},{4,28},{6,30},{8,16},{10,18},{12,20},{14,22},{16,8},... | collective-permute-start | bytes 393224 | tf_op jit(solution)/shard_map/ppermute | solution.py:346
  178.0 10.3 %collective-permute-start.37 = (bf16[32,2048]{1,0:T(8,128)(2,1)S(1)}, bf16[32,2048]{1,0:T(8,128)(2,1)S(1)}, u32[]{:S(2)}, u32[]{:S(2)}) collective-permute-start(bf16[32,2048]{1,0:T(8,128)(2,1)S(1)} %normalize.2.refs_8_), channel_id=1, source_target_pairs={{0,16},{2,18},{4,20},{6,22},{8,24},{10,26},{12,28},{14,30},{16,0},... | collective-permute-start | bytes 393224 | tf_op jit(solution)/shard_map/ppermute | solution.py:346
  178.0 10.3 %collective-permute-start.36 = (bf16[32,2048]{1,0:T(8,128)(2,1)S(1)}, bf16[32,2048]{1,0:T(8,128)(2,1)S(1)}, u32[]{:S(2)}, u32[]{:S(2)}) collective-permute-start(bf16[32,2048]{1,0:T(8,128)(2,1)S(1)} %normalize.2.refs_8_), channel_id=1, source_target_pairs={{0,8},{2,10},{4,12},{6,14},{8,0},{10,2},{12,4},{14,6},{16,24},{18,... | collective-permute-start | bytes 393224 | tf_op jit(solution)/shard_map/ppermute | solution.py:346
  179.7 15.0 %collective-permute-start.27 = (bf16[32,2304]{1,0:T(8,128)(2,1)S(1)}, bf16[32,2304]{1,0:T(8,128)(2,1)S(1)}, u32[]{:S(2)}, u32[]{:S(2)}) collective-permute-start(bf16[32,2304]{1,0:T(8,128)(2,1)S(1)} %get-tuple-element.57), channel_id=1, source_target_pairs={{0,8},{2,10},{4,12},{6,14},{8,0},{10,2},{12,4},{14,6},{16,24},{18,... | collective-permute-start | bytes 442376 | tf_op jit(solution)/shard_map/ppermute | solution.py:346
  180.1 16.0 %collective-permute-start.28 = (bf16[32,2304]{1,0:T(8,128)(2,1)S(1)}, bf16[32,2304]{1,0:T(8,128)(2,1)S(1)}, u32[]{:S(2)}, u32[]{:S(2)}) collective-permute-start(bf16[32,2304]{1,0:T(8,128)(2,1)S(1)} %get-tuple-element.58), channel_id=1, source_target_pairs={{0,16},{2,18},{4,20},{6,22},{8,24},{10,26},{12,28},{14,30},{16,0},... | collective-permute-start | bytes 442376 | tf_op jit(solution)/shard_map/ppermute | solution.py:346
  183.0 13.1 %collective-permute-start.29 = (bf16[32,2304]{1,0:T(8,128)(2,1)S(1)}, bf16[32,2304]{1,0:T(8,128)(2,1)S(1)}, u32[]{:S(2)}, u32[]{:S(2)}) collective-permute-start(bf16[32,2304]{1,0:T(8,128)(2,1)S(1)} %get-tuple-element.59), channel_id=1, source_target_pairs={{0,24},{2,26},{4,28},{6,30},{8,16},{10,18},{12,20},{14,22},{16,8},... | collective-permute-start | bytes 442376 | tf_op jit(solution)/shard_map/ppermute | solution.py:346
  188.5 22.0 %collective-permute-start.39 = (bf16[4,32,2048]{2,1,0:T(8,128)(2,1)S(1)}, bf16[4,32,2048]{2,1,0:T(8,128)(2,1)S(1)}, u32[]{:S(2)}, u32[]{:S(2)}) collective-permute-start(bf16[4,32,2048]{2,1,0:T(8,128)(2,1)S(1)} %pad_maximum_fusion.2.refs_0_), channel_id=1, source_target_pairs={{0,2},{2,0},{4,6},{6,4},{8,10},{10,8},{12,14},{14,12},{16,18},{18,... | collective-permute-start | bytes 1572872 | tf_op jit(solution)/shard_map/ppermute | solution.py:346
  196.7 6.9 %collective-permute-start.32 = (bf16[32,2048]{1,0:T(8,128)(2,1)S(1)}, bf16[32,2048]{1,0:T(8,128)(2,1)S(1)}, u32[]{:S(2)}, u32[]{:S(2)}) collective-permute-start(bf16[32,2048]{1,0:T(8,128)(2,1)S(1)} %normalize.3), channel_id=1, source_target_pairs={{0,24},{2,26},{4,28},{6,30},{8,16},{10,18},{12,20},{14,22},{16,8},... | collective-permute-start | bytes 393224 | tf_op jit(solution)/shard_map/ppermute | solution.py:346
  200.0 7.8 %collective-permute-start.31 = (bf16[32,2048]{1,0:T(8,128)(2,1)S(1)}, bf16[32,2048]{1,0:T(8,128)(2,1)S(1)}, u32[]{:S(2)}, u32[]{:S(2)}) collective-permute-start(bf16[32,2048]{1,0:T(8,128)(2,1)S(1)} %normalize.3), channel_id=1, source_target_pairs={{0,16},{2,18},{4,20},{6,22},{8,24},{10,26},{12,28},{14,30},{16,0},... | collective-permute-start | bytes 393224 | tf_op jit(solution)/shard_map/ppermute | solution.py:346
  201.7 6.1 %collective-permute-start.30 = (bf16[32,2048]{1,0:T(8,128)(2,1)S(1)}, bf16[32,2048]{1,0:T(8,128)(2,1)S(1)}, u32[]{:S(2)}, u32[]{:S(2)}) collective-permute-start(bf16[32,2048]{1,0:T(8,128)(2,1)S(1)} %normalize.3), channel_id=1, source_target_pairs={{0,8},{2,10},{4,12},{6,14},{8,0},{10,2},{12,4},{14,6},{16,24},{18,... | collective-permute-start | bytes 393224 | tf_op jit(solution)/shard_map/ppermute | solution.py:346
  202.1 23.7 %collective-permute-start.40 = (bf16[4,32,2048]{2,1,0:T(8,128)(2,1)S(1)}, bf16[4,32,2048]{2,1,0:T(8,128)(2,1)S(1)}, u32[]{:S(2)}, u32[]{:S(2)}) collective-permute-start(bf16[4,32,2048]{2,1,0:T(8,128)(2,1)S(1)} %pad_maximum_fusion.2.refs_0_), channel_id=1, source_target_pairs={{0,4},{2,6},{4,0},{6,2},{8,12},{10,14},{12,8},{14,10},{16,20},{18,... | collective-permute-start | bytes 1572872 | tf_op jit(solution)/shard_map/ppermute | solution.py:346
  203.6 22.2 %collective-permute-start.41 = (bf16[4,32,2048]{2,1,0:T(8,128)(2,1)S(1)}, bf16[4,32,2048]{2,1,0:T(8,128)(2,1)S(1)}, u32[]{:S(2)}, u32[]{:S(2)}) collective-permute-start(bf16[4,32,2048]{2,1,0:T(8,128)(2,1)S(1)} %pad_maximum_fusion.2.refs_0_), channel_id=1, source_target_pairs={{0,6},{2,4},{4,2},{6,0},{8,14},{10,12},{12,10},{14,8},{16,22},{18,... | collective-permute-start | bytes 1572872 | tf_op jit(solution)/shard_map/ppermute | solution.py:346
  207.9 21.9 %collective-permute-start.35 = (bf16[4,32,2048]{2,1,0:T(8,128)(2,1)S(1)}, bf16[4,32,2048]{2,1,0:T(8,128)(2,1)}, u32[]{:S(2)}, u32[]{:S(2)}) collective-permute-start(bf16[4,32,2048]{2,1,0:T(8,128)(2,1)S(1)} %pad_maximum_fusion.1.refs_0_), channel_id=1, source_target_pairs={{0,2},{2,0},{4,6},{6,4},{8,10},{10,8},{12,14},{14,12},{16,18},{18,... | collective-permute-start | bytes 1572872 | tf_op jit(solution)/shard_map/ppermute | solution.py:346
  209.6 27.5 %collective-permute-start.33 = (bf16[4,32,2048]{2,1,0:T(8,128)(2,1)S(1)}, bf16[4,32,2048]{2,1,0:T(8,128)(2,1)S(1)}, u32[]{:S(2)}, u32[]{:S(2)}) collective-permute-start(bf16[4,32,2048]{2,1,0:T(8,128)(2,1)S(1)} %pad_maximum_fusion.1.refs_0_), channel_id=1, source_target_pairs={{0,4},{2,6},{4,0},{6,2},{8,12},{10,14},{12,8},{14,10},{16,20},{18,... | collective-permute-start | bytes 1572872 | tf_op jit(solution)/shard_map/ppermute | solution.py:346
  210.4 26.6 %collective-permute-start.34 = (bf16[4,32,2048]{2,1,0:T(8,128)(2,1)S(1)}, bf16[4,32,2048]{2,1,0:T(8,128)(2,1)}, u32[]{:S(2)}, u32[]{:S(2)}) collective-permute-start(bf16[4,32,2048]{2,1,0:T(8,128)(2,1)S(1)} %pad_maximum_fusion.1.refs_0_), channel_id=1, source_target_pairs={{0,6},{2,4},{4,2},{6,0},{8,14},{10,12},{12,10},{14,8},{16,22},{18,... | collective-permute-start | bytes 1572872 | tf_op jit(solution)/shard_map/ppermute | solution.py:346
  225.8 2.2 copy-start
  228.0 2.2 copy-start.1
  239.5 1.6 collective-permute-start.42

commit v5 on v4

--- a/solution.py
+++ b/solution.py
@@ -1,4 +1,5 @@
 import functools
+import math
 
 import jax
 import jax.numpy as jnp
@@ -28,30 +29,33 @@
     return parts[0]
 
 
-def attend_kernel(info, *refs, plane, blocks, rows, group_step, key_chunk, waits):
-    q_refs, refs = refs[:plane], refs[plane:]
+def attend_kernel(info, *refs, chosen, blocks, plane, rows, head, q_head, group_step, key_chunk, waits):
+    count = len(chosen)
+    q_refs, refs = refs[:count], refs[count:]
     kt_ref, v_ref, ks_ref, vs_ref = refs[:4]
     refs = refs[4 + waits :]
-    o_refs, refs = refs[:plane], refs[plane:]
+    o_refs, refs = refs[:count], refs[count:]
     weight_refs, refs = refs[:2], refs[2:]
     score_ref, shift_ref, aux_ref, pos_ref, ks_pad, vs_pad = refs
     me, my_plane, wanted = info[0], info[1], info[2]
     keys = v_ref.shape[0]
-    block_rows = plane * rows
+    block_rows = count * rows
     tile_rows = group_step * block_rows
     steps = GROUP_QUERIES // group_step
     chunks = keys // key_chunk
-    strip = min(tile_rows, 64)
+    strip = math.gcd(tile_rows, 64)
+    own = slice(head * HEAD_SIZE, (head + 1) * HEAD_SIZE)
+    q_first = q_head * GROUP_QUERIES
 
     ks_pad[...] = jnp.zeros_like(ks_pad)
     vs_pad[...] = jnp.zeros_like(vs_pad)
-    ks_pad[0:rows, :] = ks_ref[...]
-    vs_pad[0:rows, :] = vs_ref[...]
+    ks_pad[0:rows, :] = ks_ref[:, own]
+    vs_pad[0:rows, :] = vs_ref[:, own]
     row = lax.broadcasted_iota(jnp.int32, (rows, LANES), 0)
     col = lax.broadcasted_iota(jnp.int32, (rows, LANES), 1)
     for i in range(group_step):
-        for b in range(plane):
-            start = (i * plane + b) * rows
+        for n, b in enumerate(chosen):
+            start = (i * count + n) * rows
             base = ((b ^ my_plane) - me) * rows
             pos_ref[start : start + rows] = jnp.where(col < rows, row - col + base, -(1 << 30))
     lane = lax.broadcasted_iota(jnp.int32, (block_rows, LANES), 1)
@@ -63,13 +67,13 @@
         slot, group = place(tile)
         parts = []
         for i in range(group_step):
-            cols = pl.ds(pl.multiple_of((group + i) * HEAD_SIZE, HEAD_SIZE), HEAD_SIZE)
+            cols = pl.ds(pl.multiple_of((q_first + group + i) * HEAD_SIZE, HEAD_SIZE), HEAD_SIZE)
             parts += [q[slot, :, cols] for q in q_refs]
         return jnp.concatenate(parts, axis=0)
 
     def span_scores(q, tile):
         slot, _ = place(tile)
-        start = info[3 + blocks + slot] * block_rows
+        start = info[3 + blocks + slot] * (plane * rows)
         scores = lax.dot_general(q, ks_pad[...], (((1,), (1,)), ((), ())), preferred_element_type=F32)
         return jnp.where(pos_ref[...] + start >= 0, scores, MASKED)
 
@@ -114,7 +118,7 @@
                 weight_ref[part, c : c + LANES] = weights.astype(BF16)
 
     def apply_chunk(acc, j):
-        values = v_ref[j * key_chunk : (j + 1) * key_chunk]
+        values = v_ref[j * key_chunk : (j + 1) * key_chunk, own]
         return acc + jnp.dot(weight_refs[j % 2][...], values, preferred_element_type=F32)
 
     def step(now, later):
@@ -133,9 +137,9 @@
         finish(now, shift_ref[...], jnp.concatenate(totals, axis=0), acc)
         shift_ref[...] = shift_of(peak)
 
-    count = wanted * steps
-
-    @pl.when(count > 0)
+    tiles = wanted * steps
+
+    @pl.when(tiles > 0)
     def _():
         q = load_queries(jnp.int32(0))
         peak = span_scores(q, jnp.int32(0))
@@ -145,10 +149,10 @@
         shift_ref[...] = shift_of(peak)
 
         def body(t, _):
-            step(t, jnp.minimum(t + 1, count - 1))
+            step(t, jnp.minimum(t + 1, tiles - 1))
             return 0
 
-        lax.fori_loop(0, count, body, 0)
+        lax.fori_loop(0, tiles, body, 0)
 
     def span_only(t, _):
         scores = span_scores(load_queries(t), t)
@@ -158,64 +162,54 @@
         finish(t, shift, weights, acc)
         return 0
 
-    lax.fori_loop(count, blocks * steps, span_only, 0)
-
-
-def attend_head(info, q_pieces, q_head, keys_t, values, span_keys, span_values, head, after):
-    plane = len(q_pieces)
+    lax.fori_loop(tiles, blocks * steps, span_only, 0)
+
+
+def attend_head(info, q_pieces, chosen, q_head, keys_t, values, span_keys, span_values, head, after):
     blocks, rows, _ = q_pieces[0].shape
+    plane, count = len(q_pieces), len(chosen)
     cols = GROUP_QUERIES * HEAD_SIZE
     key_count = values.shape[0]
-    group_step = 2
-    tile_rows = group_step * plane * rows
+    group_step = min(GROUP_QUERIES, 2 * (plane // count))
+    tile_rows = group_step * count * rows
     key_chunk = min(key_count, 512)
-    out_cols = cols + LANES
-    vmem = pltpu.MemorySpace.VMEM
-    whole = pl.BlockSpec((blocks, rows, cols), lambda i, s: (0, 0, q_head))
-    whole_out = pl.BlockSpec((blocks, rows, out_cols), lambda i, s: (0, 0, 0))
-    span_block = pl.BlockSpec((rows, HEAD_SIZE), lambda i, s: (0, head))
-    scored = blocks * plane * rows * GROUP_QUERIES * key_count
+    vmem, smem = pltpu.MemorySpace.VMEM, pltpu.MemorySpace.SMEM
+    scored = blocks * count * rows * GROUP_QUERIES * key_count
     return pl.pallas_call(
         functools.partial(
             attend_kernel,
+            chosen=chosen,
+            blocks=blocks,
             plane=plane,
-            blocks=blocks,
             rows=rows,
+            head=head,
+            q_head=q_head,
             group_step=group_step,
             key_chunk=key_chunk,
             waits=len(after),
         ),
-        grid_spec=pltpu.PrefetchScalarGridSpec(
-            num_scalar_prefetch=1,
-            grid=(1,),
-            in_specs=[whole] * plane
-            + [
-                pl.BlockSpec((HEAD_SIZE, key_count), lambda i, s: (head, 0)),
-                pl.BlockSpec((key_count, HEAD_SIZE), lambda i, s: (0, head)),
-                span_block,
-                span_block,
-            ]
-            + [pl.BlockSpec(memory_space=pl.ANY)] * len(after),
-            out_specs=[whole_out] * plane,
-            scratch_shapes=[vmem((tile_rows, key_chunk), BF16)] * 2
-            + [
-                vmem((tile_rows, key_count + LANES), F32),
-                vmem((tile_rows, LANES), F32),
-                vmem((plane * rows, LANES), F32),
-                vmem((tile_rows, LANES), jnp.int32),
-                vmem((LANES, HEAD_SIZE), BF16),
-                vmem((LANES, HEAD_SIZE), BF16),
-            ],
-        ),
-        out_shape=[jax.ShapeDtypeStruct((blocks, rows, out_cols), BF16)] * plane,
+        in_specs=[pl.BlockSpec(memory_space=smem)]
+        + [pl.BlockSpec(memory_space=vmem)] * (count + 4)
+        + [pl.BlockSpec(memory_space=pl.ANY)] * len(after),
+        out_specs=[pl.BlockSpec(memory_space=vmem)] * count,
+        scratch_shapes=[vmem((tile_rows, key_chunk), BF16)] * 2
+        + [
+            vmem((tile_rows, key_count + LANES), F32),
+            vmem((tile_rows, LANES), F32),
+            vmem((count * rows, LANES), F32),
+            vmem((tile_rows, LANES), jnp.int32),
+            vmem((LANES, HEAD_SIZE), BF16),
+            vmem((LANES, HEAD_SIZE), BF16),
+        ],
+        out_shape=[jax.ShapeDtypeStruct((blocks, rows, cols + LANES), BF16)] * count,
         compiler_params=pltpu.CompilerParams(vmem_limit_bytes=ATTEND_VMEM),
         cost_estimate=pl.CostEstimate(
             flops=8 * scored * HEAD_SIZE,
-            bytes_accessed=4 * key_count * HEAD_SIZE + 4 * blocks * plane * rows * cols,
+            bytes_accessed=4 * key_count * HEAD_SIZE + 4 * blocks * count * rows * cols,
             transcendentals=scored,
         ),
         name="attend",
-    )(info, *q_pieces, keys_t, values, span_keys, span_values, *after)
+    )(info, *[q_pieces[b] for b in chosen], keys_t, values, span_keys, span_values, *after)
 
 
 def combine(parts):
@@ -302,8 +296,7 @@
 
 def project_kernel(info, *refs, chosen, blocks, rows, width):
     ins, (w_ref, *base_ref, out) = refs[: len(chosen)], refs[len(chosen) :]
-    if base_ref:
-        out[...] = base_ref[0][...].astype(out.dtype)
+    out[...] = base_ref[0][...].astype(out.dtype) if base_ref else jnp.zeros_like(out)
     for x_ref, b in zip(ins, chosen):
         x = x_ref[...].reshape(blocks * rows, width)
         y = jnp.dot(x, w_ref[...], preferred_element_type=F32)
@@ -375,10 +368,11 @@
     first = stack_blocks(queries[:, :width])
     sources, stacks = [(gather_plane(first), 0)], []
     keys, _ = lax.optimization_barrier((context_keys, first))
-    keys_t = keys.T
+    keys_t = [
+        (keys if h else context_keys)[:, h * HEAD_SIZE : (h + 1) * HEAD_SIZE].T for h in range(heads)
+    ]
     if heads > 1:
-        held, _ = lax.optimization_barrier((queries[:, width:], first))
-        stacks = [stack_blocks(held)]
+        stacks = [stack_blocks(queries[:, width:])]
         pieces = gather_plane(stacks[0])
         sources += [(pieces, i) for i in range(heads - 1)]
 
@@ -399,14 +393,22 @@
         rows_of.append(normalize_pieces(parts, after))
         return [rows_of[-1]]
 
+    def attend(h, chosen, after):
+        pieces, q_head = sources[h]
+        return attend_head(
+            info, pieces, chosen, q_head, keys_t[h], context_values, span_keys, span_values, h, after
+        )
+
     latest = stacks
     for h in range(heads):
-        attended.append(
-            attend_head(info, *sources[h], keys_t, context_values, span_keys, span_values, h, latest)
-        )
+        start = 1 if h == heads - 1 else 0
+        attended.append(attend(h, range(start, plane), latest))
         latest = [attended[h][0]]
         if len(rows_of) < len(merged):
             latest = normalize(latest)
+        if start:
+            attended[h] = attend(h, [0], latest) + attended[h]
+            latest = [attended[h][0]]
         if h >= (len(merged) + 1) * size:
             latest = merge(latest)
     while len(merged) < heads // size:
@@ -417,7 +419,7 @@
     total = []
     for g, rows_now in enumerate(rows_of):
         if g < len(rows_of) - 1:
-            rows_now, _ = lax.optimization_barrier((rows_now, merged[-1][0]))
+            rows_now, _ = lax.optimization_barrier((rows_now, attended[-1][0]))
         pieces = gather_plane(stack_blocks(rows_now))
         if g < len(rows_of) - 1:
             total = [project(info, pieces, range(plane), out_weight, g, total, F32)]

time: 243 us -> 251 us (1.033)
  Pallas kernels: 113 us -> 101 us
  starting transfers between devices: 64.2 us -> 76.1 us
  waiting for transfers between devices: 44.6 us -> 51 us
    ppermute x43, starting transfers between devices: 64.2 us -> 76.1 us  [exchange(): return lax.ppermute(x, axis, [(i, i ^ distance) for i in range(count)])]
    pallas_call x4 -> x5, Pallas kernels: 102 us -> 89.9 us  [attend_head(): pl.pallas_call(functools.partial(attend_kernel, chosen=chosen, blocks=blo...]
    ppermute x43, waiting for transfers between devices: 44.6 us -> 51 us  [exchange(): return lax.ppermute(x, axis, [(i, i ^ distance) for i in range(count)])]
    unnamed x16 -> x11, local copies, waits for them, and re-layouts: 6.96 us -> 2.74 us
  transfers between devices with their start and end apart: 43 -> 43, of which waited for: 13 -> 12; matrix products, arithmetic and copies ran while one was open for 5% -> 6% of each run, Pallas kernels for 45% -> 40%
where the time goes in v5:
time: 251 us; the launch traced here: 248 us
  Pallas kernels  101 us (40%)
  starting transfers between devices  76.1 us (30%)
  waiting for transfers between devices  51 us (20%)
  local copies, waits for them, and re-layouts  16 us (6%)
  other arithmetic  3.32 us (1%)
    pallas_call x5, Pallas kernels, attend_head(): pl.pallas_call(functools.partial(attend_kernel, chosen=chosen, blocks=blo...  89.9 us
    ppermute x43, starting transfers between devices, exchange(): return lax.ppermute(x, axis, [(i, i ^ distance) for i in range(count)])  76.1 us
    ppermute x43, waiting for transfers between devices, exchange(): return lax.ppermute(x, axis, [(i, i ^ distance) for i in range(count)])  51 us
    pallas_call x3, Pallas kernels, project(): pl.pallas_call(functools.partial(project_kernel, chosen=chosen, blocks=bl...  6.59 us
    optimization_barrier x1, local copies, waits for them, and re-layouts, local(): keys, _ = lax.optimization_barrier((context_keys, first))  6.45 us
  transfers between devices with their start and end apart: 43, of which 12 were waited for; matrix products, arithmetic and copies ran while one was open for 6% of the time, Pallas kernels for 40%

profile of v5, /device:TPU:0, one launch (start us, length us, event | category | flops | bytes accessed | tf_op | source)
XLA Modules:
  0.0 247.9 jit_solution(14720356541764949784)
XLA Ops:
  0.0 1.0 slice_bitcast_fusion.4
  1.0 5.1 %collective-permute-start.2 = (bf16[32,3072]{1,0:T(8,128)(2,1)S(1)}, bf16[32,3072]{1,0:T(8,128)(2,1)S(1)}, u32[]{:S(2)}, u32[]{:S(2)}) collective-permute-start(bf16[32,3072]{1,0:T(8,128)(2,1)S(1)} %get-tuple-element.63), channel_id=1, source_target_pairs={{0,24},{2,26},{4,28},{6,30},{8,16},{10,18},{12,20},{14,22},{16,8},... | collective-permute-start | bytes 589832 | tf_op jit(solution)/shard_map/ppermute | solution.py:339
  6.1 0.8 slice_bitcast_fusion.3
  6.9 2.0 collective-permute-start.8
  8.9 1.1 collective-permute-start.7
  10.0 1.4 collective-permute-start.6
  11.4 0.8 compare_reduce_fusion
  12.2 0.6 gather_fusion
  12.8 0.6 convert_reduce_fusion
  13.5 1.3 slice.22
  15.3 0.8 sort.17
  16.2 0.7 concatenate.3.info
  16.8 0.6 collective-permute-done.8
  17.5 10.8 %collective-permute-start = (bf16[32,3072]{1,0:T(8,128)(2,1)S(1)}, bf16[32,3072]{1,0:T(8,128)(2,1)S(1)}, u32[]{:S(2)}, u32[]{:S(2)}) collective-permute-start(bf16[32,3072]{1,0:T(8,128)(2,1)S(1)} %get-tuple-element.63), channel_id=1, source_target_pairs={{0,8},{2,10},{4,12},{6,14},{8,0},{10,2},{12,4},{14,6},{16,24},{18,... | collective-permute-start | bytes 589832 | tf_op jit(solution)/shard_map/ppermute | solution.py:339
  28.5 1.6 collective-permute-start.9
  30.1 1.5 collective-permute-start.10
  31.6 6.5 %copy.12 = bf16[4096,512]{0,1:T(8,128)(2,1)} copy(bf16[4096,512]{1,0:T(8,128)(2,1)} %param.10) | data formatting | bytes 8388608 | tf_op jit(solution)/shard_map/optimization_barrier | solution.py:370
  38.1 2.3 slice_bitcast_fusion
  40.4 0.5 collective-permute-start.11
  41.1 1.6 collective-permute-start.3
  42.6 1.5 collective-permute-start.4
  44.6 6.0 %collective-permute-done.11.refs_3_ = bf16[4,32,1024]{2,1,0:T(8,128)(2,1)S(1)} collective-permute-done((bf16[4,32,1024]{2,1,0:T(8,128)(2,1)S(1)}, bf16[4,32,1024]{2,1,0:T(8,128)(2,1)S(1)}, u32[]{:S(2)}, u32[]{:S(2)}) %collective-permute-start.11) | collective-permute-done | bytes 262176 | tf_op jit(solution)/shard_map/ppermute | solution.py:339
  50.7 21.8 %attend.5 = (bf16[4,32,1152]{2,1,0:T(8,128)(2,1)S(1)}, bf16[4,32,1152]{2,1,0:T(8,128)(2,1)S(1)}, bf16[4,32,1152]{2,1,0:T(8,128)(2,1)S(1)}, bf16[4,32,1152]{2,1,0:T(8,128)(2,1)S(1)}) custom-call(s32[11]{0:T(128)S(1)} %concatenate.3.info, bf16[4,32,1024]{2,1,0:T(8,128)(2,1)S(1)} %pad_maximum_fusion.3.refs_0_, ...), custom_call_target="tpu_custom_call" | custom-call | flops 17179869184 | bytes 4194304 | tf_op jit(solution)/shard_map/attend/pallas_call | solution.py:178
  72.5 0.6 collective-permute-start.15
  73.1 5.2 %collective-permute-start.16 = (bf16[4,32,1152]{2,1,0:T(8,128)(2,1)S(1)}, bf16[4,32,1152]{2,1,0:T(8,128)(2,1)S(1)}, u32[]{:S(2)}, u32[]{:S(2)}) collective-permute-start(bf16[4,32,1152]{2,1,0:T(8,128)(2,1)S(1)} %get-tuple-element.40), channel_id=1, source_target_pairs={{0,4},{2,6},{4,0},{6,2},{8,12},{10,14},{12,8},{14,10},{16,20},{18,... | collective-permute-start | bytes 884744 | tf_op jit(solution)/shard_map/ppermute | solution.py:339
  78.3 6.1 %collective-permute-done.5.refs_3_.refs_2_ = bf16[4,32,3072]{2,1,0:T(8,128)(2,1)S(1)} collective-permute-done((bf16[4,32,3072]{2,1,0:T(8,128)(2,1)S(1)}, bf16[4,32,3072]{2,1,0:T(8,128)(2,1)S(1)}, u32[]{:S(2)}, u32[]{:S(2)}) %collective-permute-start.5) | collective-permute-done | bytes 786464 | tf_op jit(solution)/shard_map/ppermute | solution.py:339
  84.4 21.8 %attend.6 = (bf16[4,32,1152]{2,1,0:T(8,128)(2,1)S(1)}, bf16[4,32,1152]{2,1,0:T(8,128)(2,1)S(1)}, bf16[4,32,1152]{2,1,0:T(8,128)(2,1)S(1)}, bf16[4,32,1152]{2,1,0:T(8,128)(2,1)S(1)}) custom-call(s32[11]{0:T(128)S(1)} %concatenate.3.info, bf16[4,32,3072]{2,1,0:T(8,128)(2,1)S(1)} %pad_maximum_fusion.refs_8_.refs_0_, ...), custom_call_target="tpu_custom_call" | custom-call | flops 17179869184 | bytes 4194304 | tf_op jit(solution)/shard_map/attend/pallas_call | solution.py:178
  106.2 0.6 collective-permute-start.18
  106.8 5.2 %collective-permute-start.19 = (bf16[4,32,1152]{2,1,0:T(8,128)(2,1)S(1)}, bf16[4,32,1152]{2,1,0:T(8,128)(2,1)S(1)}, u32[]{:S(2)}, u32[]{:S(2)}) collective-permute-start(bf16[4,32,1152]{2,1,0:T(8,128)(2,1)S(1)} %get-tuple-element.43), channel_id=1, source_target_pairs={{0,4},{2,6},{4,0},{6,2},{8,12},{10,14},{12,8},{14,10},{16,20},{18,... | collective-permute-start | bytes 884744 | tf_op jit(solution)/shard_map/ppermute | solution.py:339
  112.1 22.1 %attend.7 = (bf16[4,32,1152]{2,1,0:T(8,128)(2,1)S(1)}, bf16[4,32,1152]{2,1,0:T(8,128)(2,1)S(1)}, bf16[4,32,1152]{2,1,0:T(8,128)(2,1)S(1)}, bf16[4,32,1152]{2,1,0:T(8,128)(2,1)S(1)}) custom-call(s32[11]{0:T(128)S(1)} %concatenate.3.info, bf16[4,32,3072]{2,1,0:T(8,128)(2,1)S(1)} %pad_maximum_fusion.refs_8_.refs_0_, ...), custom_call_target="tpu_custom_call" | custom-call | flops 17179869184 | bytes 4194304 | tf_op jit(solution)/shard_map/attend/pallas_call | solution.py:178
  134.1 1.5 collective-permute-start.12
  135.7 6.8 %collective-permute-start.13 = (bf16[4,32,1152]{2,1,0:T(8,128)(2,1)S(1)}, bf16[4,32,1152]{2,1,0:T(8,128)(2,1)S(1)}, u32[]{:S(2)}, u32[]{:S(2)}) collective-permute-start(bf16[4,32,1152]{2,1,0:T(8,128)(2,1)S(1)} %get-tuple-element.37), channel_id=1, source_target_pairs={{0,4},{2,6},{4,0},{6,2},{8,12},{10,14},{12,8},{14,10},{16,20},{18,... | collective-permute-start | bytes 884744 | tf_op jit(solution)/shard_map/ppermute | solution.py:339
  142.5 1.7 merge.2
  144.2 3.0 %collective-permute-start.22 = (bf16[32,2304]{1,0:T(8,128)(2,1)S(1)}, bf16[32,2304]{1,0:T(8,128)(2,1)S(1)}, u32[]{:S(2)}, u32[]{:S(2)}) collective-permute-start(bf16[32,2304]{1,0:T(8,128)(2,1)S(1)} %get-tuple-element.47), channel_id=1, source_target_pairs={{0,16},{2,18},{4,20},{6,22},{8,24},{10,26},{12,28},{14,30},{16,0},... | collective-permute-start | bytes 442376 | tf_op jit(solution)/shard_map/ppermute | solution.py:339
  147.3 1.4 collective-permute-start.23
  148.6 17.5 %attend.8 = (bf16[4,32,1152]{2,1,0:T(8,128)(2,1)S(1)}, bf16[4,32,1152]{2,1,0:T(8,128)(2,1)S(1)}, bf16[4,32,1152]{2,1,0:T(8,128)(2,1)S(1)}) custom-call(s32[11]{0:T(128)S(1)} %concatenate.3.info, bf16[4,32,3072]{2,1,0:T(8,128)(2,1)S(1)} %collective-permute-done.3.refs_1_.refs_0_, bf16[4,32,3072]{2,1,0:T(8,128)(2,1)S(1)} %collective-permute-done.4.refs_2_.refs_1_, ...), custom_call_target="tpu_custom_call" | custom-call | flops 12884901888 | bytes 3670016 | tf_op jit(solution)/shard_map/attend/pallas_call | solution.py:178
  166.2 3.0 %collective-permute-start.14 = (bf16[4,32,1152]{2,1,0:T(8,128)(2,1)S(1)}, bf16[4,32,1152]{2,1,0:T(8,128)(2,1)S(1)}, u32[]{:S(2)}, u32[]{:S(2)}) collective-permute-start(bf16[4,32,1152]{2,1,0:T(8,128)(2,1)S(1)} %get-tuple-element.38), channel_id=1, source_target_pairs={{0,6},{2,4},{4,2},{6,0},{8,14},{10,12},{12,10},{14,8},{16,22},{18,... | collective-permute-start | bytes 884744 | tf_op jit(solution)/shard_map/ppermute | solution.py:339
  169.2 0.6 collective-permute-start.25
  169.9 0.6 normalize.2.refs_5_
  170.5 2.9 %collective-permute-start.26 = (bf16[4,32,1152]{2,1,0:T(8,128)(2,1)S(1)}, bf16[4,32,1152]{2,1,0:T(8,128)(2,1)S(1)}, u32[]{:S(2)}, u32[]{:S(2)}) collective-permute-start(bf16[4,32,1152]{2,1,0:T(8,128)(2,1)S(1)} %get-tuple-element.51), channel_id=1, source_target_pairs={{0,6},{2,4},{4,2},{6,0},{8,14},{10,12},{12,10},{14,8},{16,22},{18,... | collective-permute-start | bytes 884744 | tf_op jit(solution)/shard_map/ppermute | solution.py:339
  173.4 6.7 %attend.9.refs_4_.refs_8_ = bf16[4,32,1152]{2,1,0:T(8,128)(2,1)S(1)} custom-call(s32[11]{0:T(128)S(1)} %concatenate.3.info, bf16[4,32,3072]{2,1,0:T(8,128)(2,1)S(1)} %pad_maximum_fusion.refs_8_.refs_0_, bf16[128,4096]{1,0:T(8,128)(2,1)S(1)} %get-tuple-element.57.refs_3_.refs_1_, bf16[4096,512]{1,0:T(8,128)(2,1)S(1)} %copy-done.2, ...), custom_call_target="tpu_custom_call" | custom-call | flops 4294967296 | bytes 2621440 | tf_op jit(solution)/shard_map/attend/pallas_call | solution.py:178
  180.1 1.4 collective-permute-start.38
  181.5 3.1 %collective-permute-start.36 = (bf16[32,2048]{1,0:T(8,128)(2,1)S(1)}, bf16[32,2048]{1,0:T(8,128)(2,1)S(1)}, u32[]{:S(2)}, u32[]{:S(2)}) collective-permute-start(bf16[32,2048]{1,0:T(8,128)(2,1)S(1)} %normalize.2.refs_5_), channel_id=1, source_target_pairs={{0,8},{2,10},{4,12},{6,14},{8,0},{10,2},{12,4},{14,6},{16,24},{18,... | collective-permute-start | bytes 393224 | tf_op jit(solution)/shard_map/ppermute | solution.py:339
  184.6 1.7 merge.3
  186.4 1.8 collective-permute-start.28
  188.2 2.5 %collective-permute-start.29 = (bf16[32,2304]{1,0:T(8,128)(2,1)S(1)}, bf16[32,2304]{1,0:T(8,128)(2,1)S(1)}, u32[]{:S(2)}, u32[]{:S(2)}) collective-permute-start(bf16[32,2304]{1,0:T(8,128)(2,1)S(1)} %get-tuple-element.55), channel_id=1, source_target_pairs={{0,24},{2,26},{4,28},{6,30},{8,16},{10,18},{12,20},{14,22},{16,8},... | collective-permute-start | bytes 442376 | tf_op jit(solution)/shard_map/ppermute | solution.py:339
  190.7 8.2 %collective-permute-done.37 = bf16[32,2048]{1,0:T(8,128)(2,1)S(1)} collective-permute-done((bf16[32,2048]{1,0:T(8,128)(2,1)S(1)}, bf16[32,2048]{1,0:T(8,128)(2,1)S(1)}, u32[]{:S(2)}, u32[]{:S(2)}) %collective-permute-start.37) | collective-permute-done | bytes 131104 | tf_op jit(solution)/shard_map/ppermute | solution.py:339
  199.1 3.0 %collective-permute-done.28.refs_2_ = bf16[32,2304]{1,0:T(8,128)(2,1)S(1)} collective-permute-done((bf16[32,2304]{1,0:T(8,128)(2,1)S(1)}, bf16[32,2304]{1,0:T(8,128)(2,1)S(1)}, u32[]{:S(2)}, u32[]{:S(2)}) %collective-permute-start.28) | collective-permute-done | bytes 147488 | tf_op jit(solution)/shard_map/ppermute | solution.py:339
  202.1 0.6 normalize.3
  202.7 1.7 collective-permute-start.32
  204.4 3.0 %collective-permute-start.31 = (bf16[32,2048]{1,0:T(8,128)(2,1)S(1)}, bf16[32,2048]{1,0:T(8,128)(2,1)S(1)}, u32[]{:S(2)}, u32[]{:S(2)}) collective-permute-start(bf16[32,2048]{1,0:T(8,128)(2,1)S(1)} %normalize.3), channel_id=1, source_target_pairs={{0,16},{2,18},{4,20},{6,22},{8,24},{10,26},{12,28},{14,30},{16,0},... | collective-permute-start | bytes 393224 | tf_op jit(solution)/shard_map/ppermute | solution.py:339
  207.6 2.0 collective-permute-done.32
  209.6 4.1 %collective-permute-done.31 = bf16[32,2048]{1,0:T(8,128)(2,1)S(1)} collective-permute-done((bf16[32,2048]{1,0:T(8,128)(2,1)S(1)}, bf16[32,2048]{1,0:T(8,128)(2,1)S(1)}, u32[]{:S(2)}, u32[]{:S(2)}) %collective-permute-start.31) | collective-permute-done | bytes 131104 | tf_op jit(solution)/shard_map/ppermute | solution.py:339
  213.8 0.9 collective-permute-start.35
  214.7 2.6 %collective-permute-start.34 = (bf16[4,32,2048]{2,1,0:T(8,128)(2,1)S(1)}, bf16[4,32,2048]{2,1,0:T(8,128)(2,1)}, u32[]{:S(2)}, u32[]{:S(2)}) collective-permute-start(bf16[4,32,2048]{2,1,0:T(8,128)(2,1)S(1)} %pad_maximum_fusion.1.refs_0_), channel_id=1, source_target_pairs={{0,6},{2,4},{4,2},{6,0},{8,14},{10,12},{12,10},{14,8},{16,22},{18,... | collective-permute-start | bytes 1572872 | tf_op jit(solution)/shard_map/ppermute | solution.py:339
  217.4 12.6 %collective-permute-done.40.refs_2_ = bf16[4,32,2048]{2,1,0:T(8,128)(2,1)S(1)} collective-permute-done((bf16[4,32,2048]{2,1,0:T(8,128)(2,1)S(1)}, bf16[4,32,2048]{2,1,0:T(8,128)(2,1)S(1)}, u32[]{:S(2)}, u32[]{:S(2)}) %collective-permute-start.40) | collective-permute-done | bytes 524320 | tf_op jit(solution)/shard_map/ppermute | solution.py:339
  230.0 2.2 copy-done
  232.2 1.8 project.3.refs_3_
  234.0 1.4 collective-permute-done.35.refs_1_
  235.5 2.4 project.4.refs_3_
  237.9 5.2 %collective-permute-done.33.refs_0_ = bf16[4,32,2048]{2,1,0:T(8,128)(2,1)S(1)} collective-permute-done((bf16[4,32,2048]{2,1,0:T(8,128)(2,1)S(1)}, bf16[4,32,2048]{2,1,0:T(8,128)(2,1)S(1)}, u32[]{:S(2)}, u32[]{:S(2)}) %collective-permute-start.33) | collective-permute-done | bytes 524320 | tf_op jit(solution)/shard_map/ppermute | solution.py:339
  243.1 2.4 project.5
  245.6 1.5 collective-permute-done.42
  247.1 0.8 add_convert_fusion
  (66 shorter events, 2.2 us)
Async XLA Ops:
  1.0 39.5 %collective-permute-start.2 = (bf16[32,3072]{1,0:T(8,128)(2,1)S(1)}, bf16[32,3072]{1,0:T(8,128)(2,1)S(1)}, u32[]{:S(2)}, u32[]{:S(2)}) collective-permute-start(bf16[32,3072]{1,0:T(8,128)(2,1)S(1)} %get-tuple-element.63), channel_id=1, source_target_pairs={{0,24},{2,26},{4,28},{6,30},{8,16},{10,18},{12,20},{14,22},{16,8},... | collective-permute-start | bytes 589832 | tf_op jit(solution)/shard_map/ppermute | solution.py:339
  6.1 34.9 %collective-permute-start.1 = (bf16[32,3072]{1,0:T(8,128)(2,1)S(1)}, bf16[32,3072]{1,0:T(8,128)(2,1)S(1)}, u32[]{:S(2)}, u32[]{:S(2)}) collective-permute-start(bf16[32,3072]{1,0:T(8,128)(2,1)S(1)} %get-tuple-element.63), channel_id=1, source_target_pairs={{0,16},{2,18},{4,20},{6,22},{8,24},{10,26},{12,28},{14,30},{16,0},... | collective-permute-start | bytes 589832 | tf_op jit(solution)/shard_map/ppermute | solution.py:339
  6.9 10.5 %collective-permute-start.8 = (bf16[32,1024]{1,0:T(8,128)(2,1)S(1)}, bf16[32,1024]{1,0:T(8,128)(2,1)S(1)}, u32[]{:S(2)}, u32[]{:S(2)}) collective-permute-start(bf16[32,1024]{1,0:T(8,128)(2,1)S(1)} %get-tuple-element.61), channel_id=1, source_target_pairs={{0,24},{2,26},{4,28},{6,30},{8,16},{10,18},{12,20},{14,22},{16,8},... | collective-permute-start | bytes 196616 | tf_op jit(solution)/shard_map/ppermute | solution.py:339
  8.9 19.6 %collective-permute-start.7 = (bf16[32,1024]{1,0:T(8,128)(2,1)S(1)}, bf16[32,1024]{1,0:T(8,128)(2,1)S(1)}, u32[]{:S(2)}, u32[]{:S(2)}) collective-permute-start(bf16[32,1024]{1,0:T(8,128)(2,1)S(1)} %get-tuple-element.61), channel_id=1, source_target_pairs={{0,16},{2,18},{4,20},{6,22},{8,24},{10,26},{12,28},{14,30},{16,0},... | collective-permute-start | bytes 196616 | tf_op jit(solution)/shard_map/ppermute | solution.py:339
  10.0 18.5 %collective-permute-start.6 = (bf16[32,1024]{1,0:T(8,128)(2,1)S(1)}, bf16[32,1024]{1,0:T(8,128)(2,1)S(1)}, u32[]{:S(2)}, u32[]{:S(2)}) collective-permute-start(bf16[32,1024]{1,0:T(8,128)(2,1)S(1)} %get-tuple-element.61), channel_id=1, source_target_pairs={{0,8},{2,10},{4,12},{6,14},{8,0},{10,2},{12,4},{14,6},{16,24},{18,... | collective-permute-start | bytes 196616 | tf_op jit(solution)/shard_map/ppermute | solution.py:339
  17.5 23.5 %collective-permute-start = (bf16[32,3072]{1,0:T(8,128)(2,1)S(1)}, bf16[32,3072]{1,0:T(8,128)(2,1)S(1)}, u32[]{:S(2)}, u32[]{:S(2)}) collective-permute-start(bf16[32,3072]{1,0:T(8,128)(2,1)S(1)} %get-tuple-element.63), channel_id=1, source_target_pairs={{0,8},{2,10},{4,12},{6,14},{8,0},{10,2},{12,4},{14,6},{16,24},{18,... | collective-permute-start | bytes 589832 | tf_op jit(solution)/shard_map/ppermute | solution.py:339
  28.5 15.6 %collective-permute-start.9 = (bf16[4,32,1024]{2,1,0:T(8,128)(2,1)S(1)}, bf16[4,32,1024]{2,1,0:T(8,128)(2,1)S(1)}, u32[]{:S(2)}, u32[]{:S(2)}) collective-permute-start(bf16[4,32,1024]{2,1,0:T(8,128)(2,1)S(1)} %pad_maximum_fusion.3.refs_0_), channel_id=1, source_target_pairs={{0,2},{2,0},{4,6},{6,4},{8,10},{10,8},{12,14},{14,12},{16,18},{18,... | collective-permute-start | bytes 786440 | tf_op jit(solution)/shard_map/ppermute | solution.py:339
  30.1 14.6 %collective-permute-start.10 = (bf16[4,32,1024]{2,1,0:T(8,128)(2,1)S(1)}, bf16[4,32,1024]{2,1,0:T(8,128)(2,1)S(1)}, u32[]{:S(2)}, u32[]{:S(2)}) collective-permute-start(bf16[4,32,1024]{2,1,0:T(8,128)(2,1)S(1)} %pad_maximum_fusion.3.refs_0_), channel_id=1, source_target_pairs={{0,4},{2,6},{4,0},{6,2},{8,12},{10,14},{12,8},{14,10},{16,20},{18,... | collective-permute-start | bytes 786440 | tf_op jit(solution)/shard_map/ppermute | solution.py:339
  38.1 12.6 %copy-start.2 = (bf16[4096,512]{1,0:T(8,128)(2,1)S(1)}, bf16[4096,512]{1,0:T(8,128)(2,1)}, u32[]{:S(2)}) copy-start(bf16[4096,512]{1,0:T(8,128)(2,1)} %refs_2_.3) | copy-start | bytes 12582916
  38.1 12.6 %copy-start.3 = (bf16[32,512]{1,0:T(8,128)(2,1)S(1)}, bf16[32,512]{1,0:T(8,128)(2,1)}, u32[]{:S(2)}) copy-start(bf16[32,512]{1,0:T(8,128)(2,1)} %refs_3_.1) | copy-start | bytes 98308
  38.1 12.6 %copy-start.4 = (bf16[32,512]{1,0:T(8,128)(2,1)S(1)}, bf16[32,512]{1,0:T(8,128)(2,1)}, u32[]{:S(2)}) copy-start(bf16[32,512]{1,0:T(8,128)(2,1)} %refs_4_.4) | copy-start | bytes 98308
  40.4 10.2 %collective-permute-start.11 = (bf16[4,32,1024]{2,1,0:T(8,128)(2,1)S(1)}, bf16[4,32,1024]{2,1,0:T(8,128)(2,1)S(1)}, u32[]{:S(2)}, u32[]{:S(2)}) collective-permute-start(bf16[4,32,1024]{2,1,0:T(8,128)(2,1)S(1)} %pad_maximum_fusion.3.refs_0_), channel_id=1, source_target_pairs={{0,6},{2,4},{4,2},{6,0},{8,14},{10,12},{12,10},{14,8},{16,22},{18,... | collective-permute-start | bytes 786440 | tf_op jit(solution)/shard_map/ppermute | solution.py:339
  41.1 37.2 %collective-permute-start.3 = (bf16[4,32,3072]{2,1,0:T(8,128)(2,1)S(1)}, bf16[4,32,3072]{2,1,0:T(8,128)(2,1)S(1)}, u32[]{:S(2)}, u32[]{:S(2)}) collective-permute-start(bf16[4,32,3072]{2,1,0:T(8,128)(2,1)S(1)} %pad_maximum_fusion.refs_8_.refs_0_), channel_id=1, source_target_pairs={{0,2},{2,0},{4,6},{6,4},{8,10},{10,8},{12,14},{14,12},{16,18},{18,... | collective-permute-start | bytes 2359304 | tf_op jit(solution)/shard_map/ppermute | solution.py:339
  42.6 35.7 %collective-permute-start.4 = (bf16[4,32,3072]{2,1,0:T(8,128)(2,1)S(1)}, bf16[4,32,3072]{2,1,0:T(8,128)(2,1)S(1)}, u32[]{:S(2)}, u32[]{:S(2)}) collective-permute-start(bf16[4,32,3072]{2,1,0:T(8,128)(2,1)S(1)} %pad_maximum_fusion.refs_8_.refs_0_), channel_id=1, source_target_pairs={{0,4},{2,6},{4,0},{6,2},{8,12},{10,14},{12,8},{14,10},{16,20},{18,... | collective-permute-start | bytes 2359304 | tf_op jit(solution)/shard_map/ppermute | solution.py:339
  44.2 40.2 %collective-permute-start.5 = (bf16[4,32,3072]{2,1,0:T(8,128)(2,1)S(1)}, bf16[4,32,3072]{2,1,0:T(8,128)(2,1)S(1)}, u32[]{:S(2)}, u32[]{:S(2)}) collective-permute-start(bf16[4,32,3072]{2,1,0:T(8,128)(2,1)S(1)} %pad_maximum_fusion.refs_8_.refs_0_), channel_id=1, source_target_pairs={{0,6},{2,4},{4,2},{6,0},{8,14},{10,12},{12,10},{14,8},{16,22},{18,... | collective-permute-start | bytes 2359304 | tf_op jit(solution)/shard_map/ppermute | solution.py:339
  72.5 39.6 %collective-permute-start.15 = (bf16[4,32,1152]{2,1,0:T(8,128)(2,1)S(1)}, bf16[4,32,1152]{2,1,0:T(8,128)(2,1)S(1)}, u32[]{:S(2)}, u32[]{:S(2)}) collective-permute-start(bf16[4,32,1152]{2,1,0:T(8,128)(2,1)S(1)} %get-tuple-element.39), channel_id=1, source_target_pairs={{0,2},{2,0},{4,6},{6,4},{8,10},{10,8},{12,14},{14,12},{16,18},{18,... | collective-permute-start | bytes 884744 | tf_op jit(solution)/shard_map/ppermute | solution.py:339
  73.1 61.1 %collective-permute-start.16 = (bf16[4,32,1152]{2,1,0:T(8,128)(2,1)S(1)}, bf16[4,32,1152]{2,1,0:T(8,128)(2,1)S(1)}, u32[]{:S(2)}, u32[]{:S(2)}) collective-permute-start(bf16[4,32,1152]{2,1,0:T(8,128)(2,1)S(1)} %get-tuple-element.40), channel_id=1, source_target_pairs={{0,4},{2,6},{4,0},{6,2},{8,12},{10,14},{12,8},{14,10},{16,20},{18,... | collective-permute-start | bytes 884744 | tf_op jit(solution)/shard_map/ppermute | solution.py:339
  78.3 57.4 %collective-permute-start.17 = (bf16[4,32,1152]{2,1,0:T(8,128)(2,1)S(1)}, bf16[4,32,1152]{2,1,0:T(8,128)(2,1)S(1)}, u32[]{:S(2)}, u32[]{:S(2)}) collective-permute-start(bf16[4,32,1152]{2,1,0:T(8,128)(2,1)S(1)} %get-tuple-element.41), channel_id=1, source_target_pairs={{0,6},{2,4},{4,2},{6,0},{8,14},{10,12},{12,10},{14,8},{16,22},{18,... | collective-permute-start | bytes 884744 | tf_op jit(solution)/shard_map/ppermute | solution.py:339
  106.2 36.2 %collective-permute-start.18 = (bf16[4,32,1152]{2,1,0:T(8,128)(2,1)S(1)}, bf16[4,32,1152]{2,1,0:T(8,128)(2,1)S(1)}, u32[]{:S(2)}, u32[]{:S(2)}) collective-permute-start(bf16[4,32,1152]{2,1,0:T(8,128)(2,1)S(1)} %get-tuple-element.42), channel_id=1, source_target_pairs={{0,2},{2,0},{4,6},{6,4},{8,10},{10,8},{12,14},{14,12},{16,18},{18,... | collective-permute-start | bytes 884744 | tf_op jit(solution)/shard_map/ppermute | solution.py:339
  106.8 35.6 %collective-permute-start.19 = (bf16[4,32,1152]{2,1,0:T(8,128)(2,1)S(1)}, bf16[4,32,1152]{2,1,0:T(8,128)(2,1)S(1)}, u32[]{:S(2)}, u32[]{:S(2)}) collective-permute-start(bf16[4,32,1152]{2,1,0:T(8,128)(2,1)S(1)} %get-tuple-element.43), channel_id=1, source_target_pairs={{0,4},{2,6},{4,0},{6,2},{8,12},{10,14},{12,8},{14,10},{16,20},{18,... | collective-permute-start | bytes 884744 | tf_op jit(solution)/shard_map/ppermute | solution.py:339
  112.1 30.4 %collective-permute-start.20 = (bf16[4,32,1152]{2,1,0:T(8,128)(2,1)S(1)}, bf16[4,32,1152]{2,1,0:T(8,128)(2,1)S(1)}, u32[]{:S(2)}, u32[]{:S(2)}) collective-permute-start(bf16[4,32,1152]{2,1,0:T(8,128)(2,1)S(1)} %get-tuple-element.44), channel_id=1, source_target_pairs={{0,6},{2,4},{4,2},{6,0},{8,14},{10,12},{12,10},{14,8},{16,22},{18,... | collective-permute-start | bytes 884744 | tf_op jit(solution)/shard_map/ppermute | solution.py:339
  134.1 36.4 %collective-permute-start.12 = (bf16[4,32,1152]{2,1,0:T(8,128)(2,1)S(1)}, bf16[4,32,1152]{2,1,0:T(8,128)(2,1)S(1)}, u32[]{:S(2)}, u32[]{:S(2)}) collective-permute-start(bf16[4,32,1152]{2,1,0:T(8,128)(2,1)S(1)} %get-tuple-element.36), channel_id=1, source_target_pairs={{0,2},{2,0},{4,6},{6,4},{8,10},{10,8},{12,14},{14,12},{16,18},{18,... | collective-permute-start | bytes 884744 | tf_op jit(solution)/shard_map/ppermute | solution.py:339
  135.7 44.4 %collective-permute-start.13 = (bf16[4,32,1152]{2,1,0:T(8,128)(2,1)S(1)}, bf16[4,32,1152]{2,1,0:T(8,128)(2,1)S(1)}, u32[]{:S(2)}, u32[]{:S(2)}) collective-permute-start(bf16[4,32,1152]{2,1,0:T(8,128)(2,1)S(1)} %get-tuple-element.37), channel_id=1, source_target_pairs={{0,4},{2,6},{4,0},{6,2},{8,12},{10,14},{12,8},{14,10},{16,20},{18,... | collective-permute-start | bytes 884744 | tf_op jit(solution)/shard_map/ppermute | solution.py:339
  144.2 22.0 %collective-permute-start.21 = (bf16[32,2304]{1,0:T(8,128)(2,1)S(1)}, bf16[32,2304]{1,0:T(8,128)(2,1)S(1)}, u32[]{:S(2)}, u32[]{:S(2)}) collective-permute-start(bf16[32,2304]{1,0:T(8,128)(2,1)S(1)} %get-tuple-element.46), channel_id=1, source_target_pairs={{0,8},{2,10},{4,12},{6,14},{8,0},{10,2},{12,4},{14,6},{16,24},{18,... | collective-permute-start | bytes 442376 | tf_op jit(solution)/shard_map/ppermute | solution.py:339
  144.2 25.0 %collective-permute-start.22 = (bf16[32,2304]{1,0:T(8,128)(2,1)S(1)}, bf16[32,2304]{1,0:T(8,128)(2,1)S(1)}, u32[]{:S(2)}, u32[]{:S(2)}) collective-permute-start(bf16[32,2304]{1,0:T(8,128)(2,1)S(1)} %get-tuple-element.47), channel_id=1, source_target_pairs={{0,16},{2,18},{4,20},{6,22},{8,24},{10,26},{12,28},{14,30},{16,0},... | collective-permute-start | bytes 442376 | tf_op jit(solution)/shard_map/ppermute | solution.py:339
  147.3 21.9 %collective-permute-start.23 = (bf16[32,2304]{1,0:T(8,128)(2,1)S(1)}, bf16[32,2304]{1,0:T(8,128)(2,1)S(1)}, u32[]{:S(2)}, u32[]{:S(2)}) collective-permute-start(bf16[32,2304]{1,0:T(8,128)(2,1)S(1)} %get-tuple-element.48), channel_id=1, source_target_pairs={{0,24},{2,26},{4,28},{6,30},{8,16},{10,18},{12,20},{14,22},{16,8},... | collective-permute-start | bytes 442376 | tf_op jit(solution)/shard_map/ppermute | solution.py:339
  166.2 15.3 %collective-permute-start.14 = (bf16[4,32,1152]{2,1,0:T(8,128)(2,1)S(1)}, bf16[4,32,1152]{2,1,0:T(8,128)(2,1)S(1)}, u32[]{:S(2)}, u32[]{:S(2)}) collective-permute-start(bf16[4,32,1152]{2,1,0:T(8,128)(2,1)S(1)} %get-tuple-element.38), channel_id=1, source_target_pairs={{0,6},{2,4},{4,2},{6,0},{8,14},{10,12},{12,10},{14,8},{16,22},{18,... | collective-permute-start | bytes 884744 | tf_op jit(solution)/shard_map/ppermute | solution.py:339
  169.2 12.3 %collective-permute-start.24 = (bf16[4,32,1152]{2,1,0:T(8,128)(2,1)S(1)}, bf16[4,32,1152]{2,1,0:T(8,128)(2,1)S(1)}, u32[]{:S(2)}, u32[]{:S(2)}) collective-permute-start(bf16[4,32,1152]{2,1,0:T(8,128)(2,1)S(1)} %get-tuple-element.49.refs_4_), channel_id=1, source_target_pairs={{0,2},{2,0},{4,6},{6,4},{8,10},{10,8},{12,14},{14,12},{16,18},{18,... | collective-permute-start | bytes 884744 | tf_op jit(solution)/shard_map/ppermute | solution.py:339
  169.2 15.4 %collective-permute-start.25 = (bf16[4,32,1152]{2,1,0:T(8,128)(2,1)S(1)}, bf16[4,32,1152]{2,1,0:T(8,128)(2,1)S(1)}, u32[]{:S(2)}, u32[]{:S(2)}) collective-permute-start(bf16[4,32,1152]{2,1,0:T(8,128)(2,1)S(1)} %get-tuple-element.50), channel_id=1, source_target_pairs={{0,4},{2,6},{4,0},{6,2},{8,12},{10,14},{12,8},{14,10},{16,20},{18,... | collective-permute-start | bytes 884744 | tf_op jit(solution)/shard_map/ppermute | solution.py:339
  170.5 14.1 %collective-permute-start.26 = (bf16[4,32,1152]{2,1,0:T(8,128)(2,1)S(1)}, bf16[4,32,1152]{2,1,0:T(8,128)(2,1)S(1)}, u32[]{:S(2)}, u32[]{:S(2)}) collective-permute-start(bf16[4,32,1152]{2,1,0:T(8,128)(2,1)S(1)} %get-tuple-element.51), channel_id=1, source_target_pairs={{0,6},{2,4},{4,2},{6,0},{8,14},{10,12},{12,10},{14,8},{16,22},{18,... | collective-permute-start | bytes 884744 | tf_op jit(solution)/shard_map/ppermute | solution.py:339
  180.1 8.1 %collective-permute-start.38 = (bf16[32,2048]{1,0:T(8,128)(2,1)S(1)}, bf16[32,2048]{1,0:T(8,128)(2,1)S(1)}, u32[]{:S(2)}, u32[]{:S(2)}) collective-permute-start(bf16[32,2048]{1,0:T(8,128)(2,1)S(1)} %normalize.2.refs_5_), channel_id=1, source_target_pairs={{0,24},{2,26},{4,28},{6,30},{8,16},{10,18},{12,20},{14,22},{16,8},... | collective-permute-start | bytes 393224 | tf_op jit(solution)/shard_map/ppermute | solution.py:339
  181.5 17.4 %collective-permute-start.37 = (bf16[32,2048]{1,0:T(8,128)(2,1)S(1)}, bf16[32,2048]{1,0:T(8,128)(2,1)S(1)}, u32[]{:S(2)}, u32[]{:S(2)}) collective-permute-start(bf16[32,2048]{1,0:T(8,128)(2,1)S(1)} %normalize.2.refs_5_), channel_id=1, source_target_pairs={{0,16},{2,18},{4,20},{6,22},{8,24},{10,26},{12,28},{14,30},{16,0},... | collective-permute-start | bytes 393224 | tf_op jit(solution)/shard_map/ppermute | solution.py:339
  181.5 17.4 %collective-permute-start.36 = (bf16[32,2048]{1,0:T(8,128)(2,1)S(1)}, bf16[32,2048]{1,0:T(8,128)(2,1)S(1)}, u32[]{:S(2)}, u32[]{:S(2)}) collective-permute-start(bf16[32,2048]{1,0:T(8,128)(2,1)S(1)} %normalize.2.refs_5_), channel_id=1, source_target_pairs={{0,8},{2,10},{4,12},{6,14},{8,0},{10,2},{12,4},{14,6},{16,24},{18,... | collective-permute-start | bytes 393224 | tf_op jit(solution)/shard_map/ppermute | solution.py:339
  186.3 12.8 %collective-permute-start.27 = (bf16[32,2304]{1,0:T(8,128)(2,1)S(1)}, bf16[32,2304]{1,0:T(8,128)(2,1)S(1)}, u32[]{:S(2)}, u32[]{:S(2)}) collective-permute-start(bf16[32,2304]{1,0:T(8,128)(2,1)S(1)} %get-tuple-element.53), channel_id=1, source_target_pairs={{0,8},{2,10},{4,12},{6,14},{8,0},{10,2},{12,4},{14,6},{16,24},{18,... | collective-permute-start | bytes 442376 | tf_op jit(solution)/shard_map/ppermute | solution.py:339
  186.4 15.7 %collective-permute-start.28 = (bf16[32,2304]{1,0:T(8,128)(2,1)S(1)}, bf16[32,2304]{1,0:T(8,128)(2,1)S(1)}, u32[]{:S(2)}, u32[]{:S(2)}) collective-permute-start(bf16[32,2304]{1,0:T(8,128)(2,1)S(1)} %get-tuple-element.54), channel_id=1, source_target_pairs={{0,16},{2,18},{4,20},{6,22},{8,24},{10,26},{12,28},{14,30},{16,0},... | collective-permute-start | bytes 442376 | tf_op jit(solution)/shard_map/ppermute | solution.py:339
  188.2 13.9 %collective-permute-start.29 = (bf16[32,2304]{1,0:T(8,128)(2,1)S(1)}, bf16[32,2304]{1,0:T(8,128)(2,1)S(1)}, u32[]{:S(2)}, u32[]{:S(2)}) collective-permute-start(bf16[32,2304]{1,0:T(8,128)(2,1)S(1)} %get-tuple-element.55), channel_id=1, source_target_pairs={{0,24},{2,26},{4,28},{6,30},{8,16},{10,18},{12,20},{14,22},{16,8},... | collective-permute-start | bytes 442376 | tf_op jit(solution)/shard_map/ppermute | solution.py:339
  199.0 15.8 %collective-permute-start.39 = (bf16[4,32,2048]{2,1,0:T(8,128)(2,1)S(1)}, bf16[4,32,2048]{2,1,0:T(8,128)(2,1)S(1)}, u32[]{:S(2)}, u32[]{:S(2)}) collective-permute-start(bf16[4,32,2048]{2,1,0:T(8,128)(2,1)S(1)} %pad_maximum_fusion.2.refs_0_), channel_id=1, source_target_pairs={{0,2},{2,0},{4,6},{6,4},{8,10},{10,8},{12,14},{14,12},{16,18},{18,... | collective-permute-start | bytes 1572872 | tf_op jit(solution)/shard_map/ppermute | solution.py:339
  202.7 6.9 %collective-permute-start.32 = (bf16[32,2048]{1,0:T(8,128)(2,1)S(1)}, bf16[32,2048]{1,0:T(8,128)(2,1)S(1)}, u32[]{:S(2)}, u32[]{:S(2)}) collective-permute-start(bf16[32,2048]{1,0:T(8,128)(2,1)S(1)} %normalize.3), channel_id=1, source_target_pairs={{0,24},{2,26},{4,28},{6,30},{8,16},{10,18},{12,20},{14,22},{16,8},... | collective-permute-start | bytes 393224 | tf_op jit(solution)/shard_map/ppermute | solution.py:339
  204.4 9.4 %collective-permute-start.31 = (bf16[32,2048]{1,0:T(8,128)(2,1)S(1)}, bf16[32,2048]{1,0:T(8,128)(2,1)S(1)}, u32[]{:S(2)}, u32[]{:S(2)}) collective-permute-start(bf16[32,2048]{1,0:T(8,128)(2,1)S(1)} %normalize.3), channel_id=1, source_target_pairs={{0,16},{2,18},{4,20},{6,22},{8,24},{10,26},{12,28},{14,30},{16,0},... | collective-permute-start | bytes 393224 | tf_op jit(solution)/shard_map/ppermute | solution.py:339
  207.4 6.4 %collective-permute-start.30 = (bf16[32,2048]{1,0:T(8,128)(2,1)S(1)}, bf16[32,2048]{1,0:T(8,128)(2,1)S(1)}, u32[]{:S(2)}, u32[]{:S(2)}) collective-permute-start(bf16[32,2048]{1,0:T(8,128)(2,1)S(1)} %normalize.3), channel_id=1, source_target_pairs={{0,8},{2,10},{4,12},{6,14},{8,0},{10,2},{12,4},{14,6},{16,24},{18,... | collective-permute-start | bytes 393224 | tf_op jit(solution)/shard_map/ppermute | solution.py:339
  207.4 22.7 %collective-permute-start.40 = (bf16[4,32,2048]{2,1,0:T(8,128)(2,1)S(1)}, bf16[4,32,2048]{2,1,0:T(8,128)(2,1)S(1)}, u32[]{:S(2)}, u32[]{:S(2)}) collective-permute-start(bf16[4,32,2048]{2,1,0:T(8,128)(2,1)S(1)} %pad_maximum_fusion.2.refs_0_), channel_id=1, source_target_pairs={{0,4},{2,6},{4,0},{6,2},{8,12},{10,14},{12,8},{14,10},{16,20},{18,... | collective-permute-start | bytes 1572872 | tf_op jit(solution)/shard_map/ppermute | solution.py:339
  209.6 20.4 %collective-permute-start.41 = (bf16[4,32,2048]{2,1,0:T(8,128)(2,1)S(1)}, bf16[4,32,2048]{2,1,0:T(8,128)(2,1)S(1)}, u32[]{:S(2)}, u32[]{:S(2)}) collective-permute-start(bf16[4,32,2048]{2,1,0:T(8,128)(2,1)S(1)} %pad_maximum_fusion.2.refs_0_), channel_id=1, source_target_pairs={{0,6},{2,4},{4,2},{6,0},{8,14},{10,12},{12,10},{14,8},{16,22},{18,... | collective-permute-start | bytes 1572872 | tf_op jit(solution)/shard_map/ppermute | solution.py:339
  213.8 21.7 %collective-permute-start.35 = (bf16[4,32,2048]{2,1,0:T(8,128)(2,1)S(1)}, bf16[4,32,2048]{2,1,0:T(8,128)(2,1)}, u32[]{:S(2)}, u32[]{:S(2)}) collective-permute-start(bf16[4,32,2048]{2,1,0:T(8,128)(2,1)S(1)} %pad_maximum_fusion.1.refs_0_), channel_id=1, source_target_pairs={{0,2},{2,0},{4,6},{6,4},{8,10},{10,8},{12,14},{14,12},{16,18},{18,... | collective-permute-start | bytes 1572872 | tf_op jit(solution)/shard_map/ppermute | solution.py:339
  214.7 28.3 %collective-permute-start.33 = (bf16[4,32,2048]{2,1,0:T(8,128)(2,1)S(1)}, bf16[4,32,2048]{2,1,0:T(8,128)(2,1)S(1)}, u32[]{:S(2)}, u32[]{:S(2)}) collective-permute-start(bf16[4,32,2048]{2,1,0:T(8,128)(2,1)S(1)} %pad_maximum_fusion.1.refs_0_), channel_id=1, source_target_pairs={{0,4},{2,6},{4,0},{6,2},{8,12},{10,14},{12,8},{14,10},{16,20},{18,... | collective-permute-start | bytes 1572872 | tf_op jit(solution)/shard_map/ppermute | solution.py:339
  214.7 28.3 %collective-permute-start.34 = (bf16[4,32,2048]{2,1,0:T(8,128)(2,1)S(1)}, bf16[4,32,2048]{2,1,0:T(8,128)(2,1)}, u32[]{:S(2)}, u32[]{:S(2)}) collective-permute-start(bf16[4,32,2048]{2,1,0:T(8,128)(2,1)S(1)} %pad_maximum_fusion.1.refs_0_), channel_id=1, source_target_pairs={{0,6},{2,4},{4,2},{6,0},{8,14},{10,12},{12,10},{14,8},{16,22},{18,... | collective-permute-start | bytes 1572872 | tf_op jit(solution)/shard_map/ppermute | solution.py:339
  230.0 2.2 copy-start
  232.2 3.3 %copy-start.1 = (bf16[4096,512]{1,0:T(8,128)(2,1)S(1)}, bf16[4096,512]{1,0:T(8,128)(2,1)}, u32[]{:S(2)}) copy-start(bf16[4096,512]{1,0:T(8,128)(2,1)} %refs_2_.5) | copy-start | bytes 12582916
  245.5 1.6 collective-permute-start.42

commit v6 on v5

--- a/solution.py
+++ b/solution.py
@@ -29,12 +29,12 @@
     return parts[0]
 
 
-def attend_kernel(info, *refs, chosen, blocks, plane, rows, head, q_head, group_step, key_chunk, waits):
+def attend_kernel(info, *refs, chosen, blocks, plane, rows, group_step, key_chunk, waits):
     count = len(chosen)
     q_refs, refs = refs[:count], refs[count:]
     kt_ref, v_ref, ks_ref, vs_ref = refs[:4]
     refs = refs[4 + waits :]
-    o_refs, refs = refs[:count], refs[count:]
+    o_ref, refs = refs[0], refs[1:]
     weight_refs, refs = refs[:2], refs[2:]
     score_ref, shift_ref, aux_ref, pos_ref, ks_pad, vs_pad = refs
     me, my_plane, wanted = info[0], info[1], info[2]
@@ -44,13 +44,12 @@
     steps = GROUP_QUERIES // group_step
     chunks = keys // key_chunk
     strip = math.gcd(tile_rows, 64)
-    own = slice(head * HEAD_SIZE, (head + 1) * HEAD_SIZE)
-    q_first = q_head * GROUP_QUERIES
+    spots = [b ^ my_plane if o_ref.shape[0] == plane else n for n, b in enumerate(chosen)]
 
     ks_pad[...] = jnp.zeros_like(ks_pad)
     vs_pad[...] = jnp.zeros_like(vs_pad)
-    ks_pad[0:rows, :] = ks_ref[:, own]
-    vs_pad[0:rows, :] = vs_ref[:, own]
+    ks_pad[0:rows, :] = ks_ref[...]
+    vs_pad[0:rows, :] = vs_ref[...]
     row = lax.broadcasted_iota(jnp.int32, (rows, LANES), 0)
     col = lax.broadcasted_iota(jnp.int32, (rows, LANES), 1)
     for i in range(group_step):
@@ -67,7 +66,7 @@
         slot, group = place(tile)
         parts = []
         for i in range(group_step):
-            cols = pl.ds(pl.multiple_of((q_first + group + i) * HEAD_SIZE, HEAD_SIZE), HEAD_SIZE)
+            cols = pl.ds(pl.multiple_of((group + i) * HEAD_SIZE, HEAD_SIZE), HEAD_SIZE)
             parts += [q[slot, :, cols] for q in q_refs]
         return jnp.concatenate(parts, axis=0)
 
@@ -93,12 +92,12 @@
             aux = jnp.where(lane == group + i, shift[part], aux)
             aux = jnp.where(lane == group + i + GROUP_QUERIES, high[part], aux)
             aux = jnp.where(lane == group + i + 2 * GROUP_QUERIES, low[part], aux)
-            for b, o in enumerate(o_refs):
-                start = i * block_rows + b * rows
-                o[slot, :, cols] = acc[start : start + rows].astype(BF16)
+            for n, spot in enumerate(spots):
+                start = i * block_rows + n * rows
+                o_ref[spot, slot, :, cols] = acc[start : start + rows].astype(BF16)
         aux_ref[...] = aux
-        for b, o in enumerate(o_refs):
-            o[slot, :, GROUP_QUERIES * HEAD_SIZE :] = aux[b * rows : (b + 1) * rows].astype(BF16)
+        for n, spot in enumerate(spots):
+            o_ref[spot, slot, :, GROUP_QUERIES * HEAD_SIZE :] = aux[n * rows : (n + 1) * rows].astype(BF16)
 
     def score_chunk(q, peak, j):
         part = slice(j * key_chunk, (j + 1) * key_chunk)
@@ -118,7 +117,7 @@
                 weight_ref[part, c : c + LANES] = weights.astype(BF16)
 
     def apply_chunk(acc, j):
-        values = v_ref[j * key_chunk : (j + 1) * key_chunk, own]
+        values = v_ref[j * key_chunk : (j + 1) * key_chunk]
         return acc + jnp.dot(weight_refs[j % 2][...], values, preferred_element_type=F32)
 
     def step(now, later):
@@ -173,7 +172,9 @@
     group_step = min(GROUP_QUERIES, 2 * (plane // count))
     tile_rows = group_step * count * rows
     key_chunk = min(key_count, 512)
-    vmem, smem = pltpu.MemorySpace.VMEM, pltpu.MemorySpace.SMEM
+    vmem = pltpu.MemorySpace.VMEM
+    out_shape = (plane if count > 1 else 1, blocks, rows, cols + LANES)
+    span_block = pl.BlockSpec((rows, HEAD_SIZE), lambda i, s: (0, head))
     scored = blocks * count * rows * GROUP_QUERIES * key_count
     return pl.pallas_call(
         functools.partial(
@@ -182,26 +183,33 @@
             blocks=blocks,
             plane=plane,
             rows=rows,
-            head=head,
-            q_head=q_head,
             group_step=group_step,
             key_chunk=key_chunk,
             waits=len(after),
         ),
-        in_specs=[pl.BlockSpec(memory_space=smem)]
-        + [pl.BlockSpec(memory_space=vmem)] * (count + 4)
-        + [pl.BlockSpec(memory_space=pl.ANY)] * len(after),
-        out_specs=[pl.BlockSpec(memory_space=vmem)] * count,
-        scratch_shapes=[vmem((tile_rows, key_chunk), BF16)] * 2
-        + [
-            vmem((tile_rows, key_count + LANES), F32),
-            vmem((tile_rows, LANES), F32),
-            vmem((count * rows, LANES), F32),
-            vmem((tile_rows, LANES), jnp.int32),
-            vmem((LANES, HEAD_SIZE), BF16),
-            vmem((LANES, HEAD_SIZE), BF16),
-        ],
-        out_shape=[jax.ShapeDtypeStruct((blocks, rows, cols + LANES), BF16)] * count,
+        grid_spec=pltpu.PrefetchScalarGridSpec(
+            num_scalar_prefetch=1,
+            grid=(1,),
+            in_specs=[pl.BlockSpec((blocks, rows, cols), lambda i, s: (0, 0, q_head))] * count
+            + [
+                pl.BlockSpec((HEAD_SIZE, key_count), lambda i, s: (0, 0)),
+                pl.BlockSpec((key_count, HEAD_SIZE), lambda i, s: (0, head)),
+                span_block,
+                span_block,
+            ]
+            + [pl.BlockSpec(memory_space=pl.ANY)] * len(after),
+            out_specs=pl.BlockSpec(out_shape, lambda i, s: (0, 0, 0, 0)),
+            scratch_shapes=[vmem((tile_rows, key_chunk), BF16)] * 2
+            + [
+                vmem((tile_rows, key_count + LANES), F32),
+                vmem((tile_rows, LANES), F32),
+                vmem((count * rows, LANES), F32),
+                vmem((tile_rows, LANES), jnp.int32),
+                vmem((LANES, HEAD_SIZE), BF16),
+                vmem((LANES, HEAD_SIZE), BF16),
+            ],
+        ),
+        out_shape=jax.ShapeDtypeStruct(out_shape, BF16),
         compiler_params=pltpu.CompilerParams(vmem_limit_bytes=ATTEND_VMEM),
         cost_estimate=pl.CostEstimate(
             flops=8 * scored * HEAD_SIZE,
@@ -228,15 +236,20 @@
     return heads, top, total
 
 
-def merge_kernel(*refs, heads, plane, waits):
-    ins, outs = refs[: heads * plane], refs[heads * plane + waits :]
+def merge_kernel(info, *refs, owned, waits):
+    refs, out = list(refs[:-1]), refs[-1]
     width = GROUP_QUERIES * HEAD_SIZE
-    for h in range(heads):
+    blocks = out.shape[0]
+    for h, alone in enumerate(owned):
+        got = refs.pop(0)
+        own = refs.pop(0) if alone else None
         first = h * (width + LANES)
-        for a, out in enumerate(outs):
-            parts, top, total = combine([p[a] for p in ins[h * plane : (h + 1) * plane]])
+        for a in range(blocks):
+            at = info[3 + blocks + a]
+            pieces = [got[b ^ info[1], a] for b in range(1 if alone else 0, got.shape[0])]
+            parts, top, total = combine(pieces + ([own[0, a]] if alone else []))
             for g, x in enumerate(parts):
-                out[:, first + g * HEAD_SIZE : first + (g + 1) * HEAD_SIZE] = x.astype(BF16)
+                out[at, :, first + g * HEAD_SIZE : first + (g + 1) * HEAD_SIZE] = x.astype(BF16)
             lane = lax.broadcasted_iota(jnp.int32, top.shape, 1)
             high = total.astype(BF16).astype(F32)
             aux = jnp.where(
@@ -249,80 +262,75 @@
                 ),
             )
             aux = jnp.where(lane < 3 * GROUP_QUERIES, aux, 0.0)
-            out[:, first + width : first + width + LANES] = aux.astype(BF16)
-
-
-def normalize_kernel(*refs, heads, count):
-    ins, out = refs[:count], refs[-1]
+            out[at, :, first + width : first + width + LANES] = aux.astype(BF16)
+
+
+def normalize_kernel(got, *refs, heads):
+    out = refs[-1]
     width = GROUP_QUERIES * HEAD_SIZE
     for h in range(heads):
         first = h * (width + LANES)
-        parts, _, total = combine([p[:, first : first + width + LANES] for p in ins])
+        parts, _, total = combine([got[a, :, first : first + width + LANES] for a in range(got.shape[0])])
         for g, x in enumerate(parts):
             start = h * width + g * HEAD_SIZE
-            out[:, start : start + HEAD_SIZE] = (x / total[:, g : g + 1]).astype(BF16)
-
-
-def waiting_specs(count, waits):
-    whole = pl.BlockSpec(memory_space=pltpu.MemorySpace.VMEM)
-    return [whole] * count + [pl.BlockSpec(memory_space=pl.ANY)] * waits
-
-
-def merge_pieces(pieces, after):
-    heads, plane = len(pieces), len(pieces[0])
-    blocks, rows, cols = pieces[0][0].shape
+            row = (x / total[:, g : g + 1]).astype(BF16)
+            for a in range(out.shape[0]):
+                out[a, :, start : start + HEAD_SIZE] = row
+
+
+def merge_pieces(info, pieces, after):
+    _, blocks, rows, cols = pieces[0][0].shape
+    arrays = [p for parts in pieces for p in parts]
     return pl.pallas_call(
-        functools.partial(merge_kernel, heads=heads, plane=plane, waits=len(after)),
-        in_specs=waiting_specs(heads * plane, len(after)),
-        out_shape=[jax.ShapeDtypeStruct((rows, heads * cols), BF16)] * blocks,
+        functools.partial(merge_kernel, owned=[len(parts) > 1 for parts in pieces], waits=len(after)),
+        in_specs=[pl.BlockSpec(memory_space=pltpu.MemorySpace.SMEM)]
+        + [pl.BlockSpec(memory_space=pltpu.MemorySpace.VMEM)] * len(arrays)
+        + [pl.BlockSpec(memory_space=pl.ANY)] * len(after),
+        out_shape=jax.ShapeDtypeStruct((blocks, rows, len(pieces) * cols), BF16),
         compiler_params=pltpu.CompilerParams(vmem_limit_bytes=SHORT_VMEM),
         cost_estimate=SHORT,
         name="merge",
-    )(*[p for own in pieces for p in own], *after)
-
-
-def normalize_pieces(pieces, after):
-    rows, cols = pieces[0].shape
+    )(info, *arrays, *after)
+
+
+def normalize_pieces(got, after):
+    blocks, rows, cols = got.shape
     heads = cols // (GROUP_QUERIES * HEAD_SIZE + LANES)
     return pl.pallas_call(
-        functools.partial(normalize_kernel, heads=heads, count=len(pieces)),
-        in_specs=waiting_specs(len(pieces), len(after)),
-        out_shape=jax.ShapeDtypeStruct((rows, cols - heads * LANES), BF16),
+        functools.partial(normalize_kernel, heads=heads),
+        in_specs=[pl.BlockSpec(memory_space=pltpu.MemorySpace.VMEM)]
+        + [pl.BlockSpec(memory_space=pl.ANY)] * len(after),
+        out_shape=jax.ShapeDtypeStruct((blocks, rows, cols - heads * LANES), BF16),
         compiler_params=pltpu.CompilerParams(vmem_limit_bytes=SHORT_VMEM),
         cost_estimate=SHORT,
         name="normalize",
-    )(*pieces, *after)
-
-
-def project_kernel(info, *refs, chosen, blocks, rows, width):
-    ins, (w_ref, *base_ref, out) = refs[: len(chosen)], refs[len(chosen) :]
-    out[...] = base_ref[0][...].astype(out.dtype) if base_ref else jnp.zeros_like(out)
-    for x_ref, b in zip(ins, chosen):
-        x = x_ref[...].reshape(blocks * rows, width)
-        y = jnp.dot(x, w_ref[...], preferred_element_type=F32)
+    )(got, *after)
+
+
+def project_kernel(x_ref, w_ref, *refs):
+    *base_ref, out = refs
+    plane, blocks, rows, width = x_ref.shape
+    for b in range(plane):
+        y = jnp.dot(x_ref[b].reshape(blocks * rows, width), w_ref[...], preferred_element_type=F32)
         for a in range(blocks):
-            at = (info[3 + blocks + a], b ^ info[1])
             part = y[a * rows : (a + 1) * rows]
-            out[at] = ((base_ref[0][at] + part) if base_ref else part).astype(out.dtype)
-
-
-def project(info, pieces, chosen, weight, group, base, dtype):
-    plane = len(pieces)
-    blocks, rows, width = pieces[0].shape
+            out[a, b] = ((base_ref[0][a, b] + part) if base_ref else part).astype(out.dtype)
+
+
+def project(gathered, weight, group, base, dtype):
+    plane, blocks, rows, width = gathered.shape
     out_cols = weight.shape[1]
-    span = len(chosen) * blocks * rows
-    whole = pl.BlockSpec((blocks, rows, width), lambda i, s: (0, 0, 0))
-    out_block = pl.BlockSpec((blocks, plane, rows, out_cols), lambda i, s: (0, 0, 0, 0))
+    span = plane * blocks * rows
+    out_block = pl.BlockSpec((blocks, plane, rows, out_cols), lambda i: (0, 0, 0, 0))
     return pl.pallas_call(
-        functools.partial(project_kernel, chosen=chosen, blocks=blocks, rows=rows, width=width),
-        grid_spec=pltpu.PrefetchScalarGridSpec(
-            num_scalar_prefetch=1,
-            grid=(1,),
-            in_specs=[whole] * len(chosen)
-            + [pl.BlockSpec((width, out_cols), lambda i, s: (group, 0))]
-            + [out_block] * len(base),
-            out_specs=out_block,
-        ),
+        project_kernel,
+        grid=(1,),
+        in_specs=[
+            pl.BlockSpec((plane, blocks, rows, width), lambda i: (0, 0, 0, 0)),
+            pl.BlockSpec((width, out_cols), lambda i: (group, 0)),
+        ]
+        + [out_block] * len(base),
+        out_specs=out_block,
         out_shape=jax.ShapeDtypeStruct((blocks, plane, rows, out_cols), dtype),
         compiler_params=pltpu.CompilerParams(vmem_limit_bytes=SHORT_VMEM),
         cost_estimate=pl.CostEstimate(
@@ -331,7 +339,7 @@
             transcendentals=0,
         ),
         name="project",
-    )(info, *[pieces[b] for b in chosen], weight, *base)
+    )(gathered, weight, *base)
 
 
 def exchange(x, axis, distance):
@@ -362,6 +370,12 @@
     def stack_blocks(x):
         return jnp.stack([x] + [exchange(x, "ctx", a * plane) for a in range(1, blocks)])
 
+    planes = [[z * plane + p for p in range(plane)] for z in range(blocks)]
+    columns = [[z * plane + p for z in range(blocks)] for p in range(plane)]
+
+    def swap(x, groups):
+        return lax.all_to_all(x, "ctx", 0, 0, axis_index_groups=groups, tiled=True)
+
     def gather_plane(stack):
         return [stack] + [exchange(stack, "ctx", b) for b in range(1, plane)]
 
@@ -372,7 +386,8 @@
         (keys if h else context_keys)[:, h * HEAD_SIZE : (h + 1) * HEAD_SIZE].T for h in range(heads)
     ]
     if heads > 1:
-        stacks = [stack_blocks(queries[:, width:])]
+        held, _ = lax.optimization_barrier((queries[:, width:], first))
+        stacks = [stack_blocks(held)]
         pieces = gather_plane(stacks[0])
         sources += [(pieces, i) for i in range(heads - 1)]
 
@@ -381,16 +396,12 @@
 
     def merge(after):
         group = range(len(merged) * size, (len(merged) + 1) * size)
-        parts = [
-            [attended[h][0]] + [exchange(attended[h][b], "ctx", b) for b in range(1, plane)] for h in group
-        ]
-        merged.append(merge_pieces(parts, after))
-        return [merged[-1][0]]
+        parts = [[swap(attended[h][0], planes)] + attended[h][1:] for h in group]
+        merged.append(merge_pieces(info, parts, after))
+        return [merged[-1]]
 
     def normalize(after):
-        own = merged[len(rows_of)]
-        parts = [own[0]] + [exchange(own[a], "ctx", a * plane) for a in range(1, blocks)]
-        rows_of.append(normalize_pieces(parts, after))
+        rows_of.append(normalize_pieces(swap(merged[len(rows_of)], columns), after))
         return [rows_of[-1]]
 
     def attend(h, chosen, after):
@@ -402,13 +413,13 @@
     latest = stacks
     for h in range(heads):
         start = 1 if h == heads - 1 else 0
-        attended.append(attend(h, range(start, plane), latest))
-        latest = [attended[h][0]]
+        attended.append([attend(h, range(start, plane), latest)])
+        latest = attended[h]
         if len(rows_of) < len(merged):
             latest = normalize(latest)
         if start:
-            attended[h] = attend(h, [0], latest) + attended[h]
-            latest = [attended[h][0]]
+            attended[h] = attended[h] + [attend(h, [0], latest)]
+            latest = attended[h][1:]
         if h >= (len(merged) + 1) * size:
             latest = merge(latest)
     while len(merged) < heads // size:
@@ -419,13 +430,10 @@
     total = []
     for g, rows_now in enumerate(rows_of):
         if g < len(rows_of) - 1:
-            rows_now, _ = lax.optimization_barrier((rows_now, attended[-1][0]))
-        pieces = gather_plane(stack_blocks(rows_now))
-        if g < len(rows_of) - 1:
-            total = [project(info, pieces, range(plane), out_weight, g, total, F32)]
-        else:
-            total = [project(info, pieces, range(plane // 2), out_weight, g, total, F32)]
-            total = [project(info, pieces, range(plane // 2, plane), out_weight, g, total, BF16)]
+            rows_now, _ = lax.optimization_barrier((rows_now, attended[-1][-1]))
+        column = swap(rows_now, columns)
+        gathered = swap(jnp.broadcast_to(column, (plane, *column.shape)), planes)
+        total = [project(gathered, out_weight, g, total, BF16 if g == len(rows_of) - 1 else F32)]
     partial_out = total[0].reshape(ctx_count * rows, -1)
     share = partial_out.shape[0] // head_count
     total = lax.dynamic_slice_in_dim(partial_out, my_head * share, share, 0).astype(F32)

time: 251 us -> 313 us (1.25)
  blocking collectives: 0 us -> 42.2 us
  local copies, waits for them, and re-layouts: 16 us -> 40.5 us
  starting transfers between devices: 76.1 us -> 60.4 us
  waiting for transfers between devices: 51 us -> 62.3 us
    ppermute x43 -> x13, starting transfers between devices: 76.1 us -> 17.3 us  [exchange(): return lax.ppermute(x, axis, [(i, i ^ distance) for i in range(count)])]
    all_to_all x0 -> x8, waiting for transfers between devices: none -> 51.7 us  [swap(): return lax.all_to_all(x, 'ctx', 0, 0, axis_index_groups=groups, tiled=True)]
    all_to_all x0 -> x8, starting transfers between devices: none -> 43.1 us  [swap(): return lax.all_to_all(x, 'ctx', 0, 0, axis_index_groups=groups, tiled=True)]
    all_to_all x0 -> x2, blocking collectives: none -> 42.2 us  [swap(): return lax.all_to_all(x, 'ctx', 0, 0, axis_index_groups=groups, tiled=True)]
    ppermute x43 -> x13, waiting for transfers between devices: 51 us -> 10.6 us  [exchange(): return lax.ppermute(x, axis, [(i, i ^ distance) for i in range(count)])]
    unnamed x11 -> x65, local copies, waits for them, and re-layouts: 2.74 us -> 25.3 us
    pallas_call x7 -> x6, Pallas kernels: 11.3 us -> 11.6 us  [the longest x2 5.46 us: merge_pieces(): pl.pallas_call(functools.partial(merge_kernel, owned=[len(parts) > 1 for...]
  transfers between devices with their start and end apart: 43 -> 21, of which waited for: 12 -> 9; matrix products, arithmetic and copies ran while one was open for 6% -> 5% of each run, Pallas kernels for 40% -> 31%
where the time goes in v6:
time: 313 us
  Pallas kernels  103 us (33%)
  waiting for transfers between devices  62.3 us (20%)
  starting transfers between devices  60.4 us (19%)
  blocking collectives  42.2 us (13%)
  local copies, waits for them, and re-layouts  40.5 us (13%)
  other arithmetic  4.24 us (1%)
    pallas_call x5, Pallas kernels, attend_head(): pl.pallas_call(functools.partial(attend_kernel, chosen=chosen, blocks=blo...  91.1 us
    all_to_all x8, waiting for transfers between devices, swap(): return lax.all_to_all(x, 'ctx', 0, 0, axis_index_groups=groups, tiled=True)  51.7 us
    all_to_all x8, starting transfers between devices, swap(): return lax.all_to_all(x, 'ctx', 0, 0, axis_index_groups=groups, tiled=True)  43.1 us
    all_to_all x2, blocking collectives, swap(): return lax.all_to_all(x, 'ctx', 0, 0, axis_index_groups=groups, tiled=True)  42.2 us
    unnamed x65, local copies, waits for them, and re-layouts  25.3 us
    ppermute x13, starting transfers between devices, exchange(): return lax.ppermute(x, axis, [(i, i ^ distance) for i in range(count)])  17.3 us
    ppermute x13, waiting for transfers between devices, exchange(): return lax.ppermute(x, axis, [(i, i ^ distance) for i in range(count)])  10.6 us
    optimization_barrier x1, local copies, waits for them, and re-layouts, local(): keys, _ = lax.optimization_barrier((context_keys, first))  6.4 us
  transfers between devices with their start and end apart: 21, of which 9 were waited for; matrix products, arithmetic and copies ran while one was open for 5% of the time, Pallas kernels for 31%

profile of v6, /device:TPU:0, one launch (start us, length us, event | category | flops | bytes accessed | tf_op | source)
XLA Modules:
  0.0 312.7 jit_solution(14044705017143984410)
XLA Ops:
  0.0 0.9 slice_bitcast_fusion.3
  0.9 5.1 %collective-permute-start.2 = (bf16[32,1024]{1,0:T(8,128)(2,1)S(1)}, bf16[32,1024]{1,0:T(8,128)(2,1)S(1)}, u32[]{:S(2)}, u32[]{:S(2)}) collective-permute-start(bf16[32,1024]{1,0:T(8,128)(2,1)S(1)} %get-tuple-element.17), channel_id=1, source_target_pairs={{0,24},{2,26},{4,28},{6,30},{8,16},{10,18},{12,20},{14,22},{16,8},... | collective-permute-start | bytes 196616 | tf_op jit(solution)/shard_map/ppermute | solution.py:347
  6.7 0.8 compare_reduce_fusion
  8.2 0.7 convert_reduce_fusion
  8.8 0.9 slice.18
  10.3 0.7 sort.17
  11.1 0.7 concatenate.3.info
  11.9 3.8 %collective-permute-start.5 = (bf16[32,3072]{1,0:T(8,128)(2,1)S(1)}, bf16[32,3072]{1,0:T(8,128)(2,1)S(1)}, u32[]{:S(2)}, u32[]{:S(2)}) collective-permute-start(bf16[32,3072]{1,0:T(8,128)(2,1)S(1)} %slice.18), channel_id=1, source_target_pairs={{0,24},{2,26},{4,28},{6,30},{8,16},{10,18},{12,20},{14,22},{16,8},... | collective-permute-start | bytes 589832 | tf_op jit(solution)/shard_map/ppermute | solution.py:347
  16.3 1.6 collective-permute-start.9
  18.0 1.5 collective-permute-start.10
  19.5 6.4 %copy.12 = bf16[4096,512]{0,1:T(8,128)(2,1)} copy(bf16[4096,512]{1,0:T(8,128)(2,1)} %param.10) | data formatting | bytes 8388608 | tf_op jit(solution)/shard_map/optimization_barrier | solution.py:384
  25.9 3.7 %slice_bitcast_fusion = (bf16[128,4096]{1,0:T(8,128)(2,1)}, bf16[128,4096]{1,0:T(8,128)(2,1)S(1)}, bf16[128,4096]{1,0:T(8,128)(2,1)}) fusion(bf16[4096,512]{0,1:T(8,128)(2,1)} %copy.12), kind=kLoop, calls=%fused_computation.1 | loop fusion | bytes 6291456 | tf_op jit(solution)/shard_map/transpose | solution.py:386
  29.9 1.6 collective-permute-done.4
  31.5 0.7 copy-done.30
  32.2 1.2 pad_maximum_fusion.refs_8_.refs_0_
  33.5 1.6 collective-permute-start.6
  35.0 1.5 collective-permute-start.7
  37.0 0.9 collective-permute-done.11.refs_3_
  38.0 22.5 %attend.5.refs_8_ = bf16[4,4,32,1152]{3,2,1,0:T(8,128)(2,1)} custom-call(s32[11]{0:T(128)S(1)} %concatenate.3.info, bf16[4,32,1024]{2,1,0:T(8,128)(2,1)S(1)} %pad_maximum_fusion.1.refs_0_, bf16[4,32,1024]{2,1,0:T(8,128)(2,1)S(1)} %collective-permute-done.9.refs_1_, bf16[4,32,1024]{2,1,0:T(8,128)(2,1)} %collective-permute-done.10.refs_2_, ...), custom_call_target="tpu_custom_call" | custom-call | flops 17179869184 | bytes 4194304 | tf_op jit(solution)/shard_map/attend/pallas_call | solution.py:179
  60.4 7.2 %all-to-all-start.1 = ((bf16[4,4,32,1152]{3,2,1,0:T(8,128)(2,1)}), bf16[4,4,32,1152]{3,2,1,0:T(8,128)(2,1)S(1)}, u32[]{:S(2)}, u32[]{:S(2)}) async-start(bf16[4,4,32,1152]{3,2,1,0:T(8,128)(2,1)} %attend.5.refs_8_), calls=%async_computation.1 | async-start | bytes 2359296 | tf_op jit(solution)/shard_map/all_to_all | solution.py:377
  67.6 6.5 %collective-permute-done.7.refs_2_.refs_1_ = bf16[4,32,3072]{2,1,0:T(8,128)(2,1)} collective-permute-done((bf16[4,32,3072]{2,1,0:T(8,128)(2,1)S(1)}, bf16[4,32,3072]{2,1,0:T(8,128)(2,1)}, u32[]{:S(2)}, u32[]{:S(2)}) %collective-permute-start.7) | collective-permute-done | bytes 786464 | tf_op jit(solution)/shard_map/ppermute | solution.py:347
  74.2 2.2 copy-done.13
  76.4 22.6 %attend.6.refs_8_ = bf16[4,4,32,1152]{3,2,1,0:T(8,128)(2,1)} custom-call(s32[11]{0:T(128)S(1)} %concatenate.3.info, bf16[4,32,3072]{2,1,0:T(8,128)(2,1)S(1)} %pad_maximum_fusion.refs_8_.refs_0_, bf16[4,32,3072]{2,1,0:T(8,128)(2,1)} %collective-permute-done.6.refs_1_.refs_0_, bf16[4,32,3072]{2,1,0:T(8,128)(2,1)} %collective-permute-done.7.refs_2_.refs_1_, ...), custom_call_target="tpu_custom_call" | custom-call | flops 17179869184 | bytes 4194304 | tf_op jit(solution)/shard_map/attend/pallas_call | solution.py:179
  99.0 4.4 %all-to-all-start.2 = ((bf16[4,4,32,1152]{3,2,1,0:T(8,128)(2,1)}), bf16[4,4,32,1152]{3,2,1,0:T(8,128)(2,1)S(1)}, u32[]{:S(2)}, u32[]{:S(2)}) async-start(bf16[4,4,32,1152]{3,2,1,0:T(8,128)(2,1)} %attend.6.refs_8_), calls=%async_computation.2 | async-start | bytes 2359296 | tf_op jit(solution)/shard_map/all_to_all | solution.py:377
  103.3 1.2 copy-done.8
  104.6 1.1 copy-done.10
  105.7 2.2 copy-done.14
  107.9 0.8 copy-done.19
  108.6 0.8 copy-done.24
  109.4 21.5 %attend.7.refs_2_ = bf16[4,4,32,1152]{3,2,1,0:T(8,128)(2,1)S(1)} custom-call(s32[11]{0:T(128)S(1)} %concatenate.3.info, bf16[4,32,3072]{2,1,0:T(8,128)(2,1)S(1)} %copy-done.10, bf16[4,32,3072]{2,1,0:T(8,128)(2,1)} %collective-permute-done.6.refs_1_.refs_0_, bf16[4,32,3072]{2,1,0:T(8,128)(2,1)} %collective-permute-done.7.refs_2_.refs_1_, ...), custom_call_target="tpu_custom_call" | custom-call | flops 17179869184 | bytes 4194304 | tf_op jit(solution)/shard_map/attend/pallas_call | solution.py:179
  130.9 1.0 copy-done.2
  132.0 8.4 %all-to-all-start = ((bf16[4,4,32,1152]{3,2,1,0:T(8,128)(2,1)}), bf16[4,4,32,1152]{3,2,1,0:T(8,128)(2,1)S(1)}, u32[]{:S(2)}, u32[]{:S(2)}) async-start(bf16[4,4,32,1152]{3,2,1,0:T(8,128)(2,1)} %copy-done.2), calls=%async_computation | async-start | bytes 2359296 | tf_op jit(solution)/shard_map/all_to_all | solution.py:377
  140.4 1.3 copy-done.3
  141.7 2.3 merge.2.refs_7_
  144.1 0.8 copy-done.4
  144.9 7.1 %all-to-all-done.refs_0_ = bf16[4,4,32,1152]{3,2,1,0:T(8,128)(2,1)S(1)} async-done(((bf16[4,4,32,1152]{3,2,1,0:T(8,128)(2,1)}), bf16[4,4,32,1152]{3,2,1,0:T(8,128)(2,1)S(1)}, u32[]{:S(2)}, u32[]{:S(2)}) %all-to-all-start) | async-done | bytes 1179680 | tf_op jit(solution)/shard_map/all_to_all | solution.py:377
  152.0 4.6 %all-to-all-start.4 = ((bf16[4,32,2304]{2,1,0:T(8,128)(2,1)}), bf16[4,32,2304]{2,1,0:T(8,128)(2,1)S(1)}, u32[]{:S(2)}, u32[]{:S(2)}) async-start(bf16[4,32,2304]{2,1,0:T(8,128)(2,1)} %copy-done.4), calls=%async_computation.4 | async-start | bytes 1179648 | tf_op jit(solution)/shard_map/all_to_all | solution.py:377
  156.6 1.1 copy-done.5
  157.7 1.2 copy-done.6
  158.9 2.2 copy-done.15
  161.1 0.8 copy-done.20
  161.9 0.8 copy-done.25
  162.6 18.2 %attend.8.refs_0_ = bf16[4,4,32,1152]{3,2,1,0:T(8,128)(2,1)} custom-call(s32[11]{0:T(128)S(1)} %concatenate.3.info, bf16[4,32,3072]{2,1,0:T(8,128)(2,1)} %collective-permute-done.6.refs_1_.refs_0_, bf16[4,32,3072]{2,1,0:T(8,128)(2,1)} %collective-permute-done.7.refs_2_.refs_1_, bf16[4,32,3072]{2,1,0:T(8,128)(2,1)} %collective-permute-done.8.refs_3_.refs_2_, ...), custom_call_target="tpu_custom_call" | custom-call | flops 12884901888 | bytes 3670016 | tf_op jit(solution)/shard_map/attend/pallas_call | solution.py:179
  180.8 5.8 %all-to-all-start.3 = ((bf16[4,4,32,1152]{3,2,1,0:T(8,128)(2,1)}), bf16[4,4,32,1152]{3,2,1,0:T(8,128)(2,1)S(1)}, u32[]{:S(2)}, u32[]{:S(2)}) async-start(bf16[4,4,32,1152]{3,2,1,0:T(8,128)(2,1)} %attend.8.refs_0_), calls=%async_computation.3 | async-start | bytes 2359296 | tf_op jit(solution)/shard_map/all_to_all | solution.py:377
  186.6 1.4 normalize.2.refs_5_
  188.1 2.2 copy-done.16
  190.2 6.3 %attend.9.refs_2_.refs_3_ = bf16[1,4,32,1152]{3,2,1,0:T(8,128)(2,1)S(1)} custom-call(s32[11]{0:T(128)S(1)} %concatenate.3.info, bf16[4,32,3072]{2,1,0:T(8,128)(2,1)S(1)} %copy-done.11, bf16[128,4096]{1,0:T(8,128)(2,1)S(1)} %copy-done.7, bf16[4096,512]{1,0:T(8,128)(2,1)S(1)} %copy-done.16, bf16[32,512]{1,0:T(8,128)(2,1)S(1)} %copy-done.21, ...), custom_call_target="tpu_custom_call" | custom-call | flops 4294967296 | bytes 2621440 | tf_op jit(solution)/shard_map/attend/pallas_call | solution.py:179
  196.5 1.3 all-to-all-done.3.refs_1_
  197.8 3.1 %merge.3.refs_0_ = bf16[4,32,2304]{2,1,0:T(8,128)(2,1)} custom-call(s32[11]{0:T(128)S(1)} %concatenate.3.info, bf16[4,4,32,1152]{3,2,1,0:T(8,128)(2,1)S(1)} %all-to-all-done.refs_0_, bf16[4,4,32,1152]{3,2,1,0:T(8,128)(2,1)S(1)} %all-to-all-done.3.refs_1_, bf16[1,4,32,1152]{3,2,1,0:T(8,128)(2,1)S(1)} %attend.9.refs_2_.refs_3_, ...), custom_call_target="tpu_custom_call" | custom-call | tf_op jit(solution)/shard_map/merge/pallas_call | solution.py:284
  201.0 4.8 %all-to-all-start.5 = ((bf16[4,32,2304]{2,1,0:T(8,128)(2,1)}), bf16[4,32,2304]{2,1,0:T(8,128)(2,1)S(1)}, u32[]{:S(2)}, u32[]{:S(2)}) async-start(bf16[4,32,2304]{2,1,0:T(8,128)(2,1)} %merge.3.refs_0_), calls=%async_computation.5 | async-start | bytes 1179648 | tf_op jit(solution)/shard_map/all_to_all | solution.py:377
  205.8 13.0 %all-to-all-done.5.got = bf16[4,32,2304]{2,1,0:T(8,128)(2,1)S(1)} async-done(((bf16[4,32,2304]{2,1,0:T(8,128)(2,1)}), bf16[4,32,2304]{2,1,0:T(8,128)(2,1)S(1)}, u32[]{:S(2)}, u32[]{:S(2)}) %all-to-all-start.5) | async-done | bytes 589856 | tf_op jit(solution)/shard_map/all_to_all | solution.py:377
  218.8 3.5 %all-to-all-start.8 = ((bf16[4,32,2048]{2,1,0:T(8,128)(2,1)}), bf16[4,32,2048]{2,1,0:T(8,128)(2,1)S(1)}, u32[]{:S(2)}, u32[]{:S(2)}) async-start(bf16[4,32,2048]{2,1,0:T(8,128)(2,1)} %normalize.2.refs_5_), calls=%async_computation.8 | async-start | bytes 1048576 | tf_op jit(solution)/shard_map/all_to_all | solution.py:377
  222.9 11.4 %all-to-all-done.8 = bf16[4,32,2048]{2,1,0:T(8,128)(2,1)S(1)} async-done(((bf16[4,32,2048]{2,1,0:T(8,128)(2,1)}), bf16[4,32,2048]{2,1,0:T(8,128)(2,1)S(1)}, u32[]{:S(2)}, u32[]{:S(2)}) %all-to-all-start.8) | async-done | bytes 524320 | tf_op jit(solution)/shard_map/all_to_all | solution.py:377
  234.3 15.5 %all_to_all.50 = bf16[4,32,2048]{2,1,0:T(8,128)(2,1)S(1)} all-to-all(bf16[4,32,2048]{2,1,0:T(8,128)(2,1)S(1)} %normalize.3), channel_id=1, replica_groups={{0,8,16,24},{2,10,18,26},{4,12,20,28},{6,14,22,30},{1,9,17,25},{3,11,19..., dimensions={0} | all-to-all | bytes 1048576 | tf_op jit(solution)/shard_map/all_to_all | solution.py:377
  250.1 26.7 %all_to_all.51.x_ref = bf16[4,4,32,2048]{3,2,1,0:T(8,128)(2,1)S(1)} all-to-all(bf16[4,4,32,2048]{3,2,1,0:T(8,128)(2,1)S(1)} %broadcast_in_dim.8), channel_id=1, replica_groups={{0,2,4,6},{8,10,12,14},{16,18,20,22},{24,26,28,30},{1,3,5,7},{9,11,13,1..., dimensions={0} | all-to-all | bytes 4194304 | tf_op jit(solution)/shard_map/all_to_all | solution.py:377
  276.8 1.6 broadcast_in_dim.7
  278.4 4.4 %all-to-all-start.7 = ((bf16[4,4,32,2048]{3,2,1,0:T(8,128)(2,1)}), bf16[4,4,32,2048]{3,2,1,0:T(8,128)(2,1)}, u32[]{:S(2)}, u32[]{:S(2)}) async-start(bf16[4,4,32,2048]{3,2,1,0:T(8,128)(2,1)} %broadcast_in_dim.7), calls=%async_computation.7 | async-start | bytes 4194304 | tf_op jit(solution)/shard_map/all_to_all | solution.py:377
  282.9 2.2 copy-done
  285.1 1.3 project.2.refs_0_
  286.4 18.9 %all-to-all-done.7.x_ref = bf16[4,4,32,2048]{3,2,1,0:T(8,128)(2,1)} async-done(((bf16[4,4,32,2048]{3,2,1,0:T(8,128)(2,1)}), bf16[4,4,32,2048]{3,2,1,0:T(8,128)(2,1)}, u32[]{:S(2)}, u32[]{:S(2)}) %all-to-all-start.7) | async-done | bytes 2097184 | tf_op jit(solution)/shard_map/all_to_all | solution.py:377
  305.2 2.2 copy-done.1
  307.4 2.9 project.3
  310.4 1.5 collective-permute-done.12
  311.9 0.8 add_convert_fusion
  (78 shorter events, 4.5 us)
Async XLA Ops:
  0.0 9.8 %slice-start = ((bf16[4096,512]{1,0:T(8,128)(2,1)}), bf16[4096,128]{1,0:T(8,128)(2,1)S(1)}, s32[]{:S(2)}) async-start(bf16[4096,512]{1,0:T(8,128)(2,1)} %param.10), calls=%async_computation.10 | async-start | bytes 2097152 | tf_op jit(solution)/shard_map/slice | solution.py:386
  0.9 10.9 %collective-permute-start.2 = (bf16[32,1024]{1,0:T(8,128)(2,1)S(1)}, bf16[32,1024]{1,0:T(8,128)(2,1)S(1)}, u32[]{:S(2)}, u32[]{:S(2)}) collective-permute-start(bf16[32,1024]{1,0:T(8,128)(2,1)S(1)} %get-tuple-element.17), channel_id=1, source_target_pairs={{0,24},{2,26},{4,28},{6,30},{8,16},{10,18},{12,20},{14,22},{16,8},... | collective-permute-start | bytes 196616 | tf_op jit(solution)/shard_map/ppermute | solution.py:347
  6.1 5.7 %collective-permute-start.1 = (bf16[32,1024]{1,0:T(8,128)(2,1)S(1)}, bf16[32,1024]{1,0:T(8,128)(2,1)S(1)}, u32[]{:S(2)}, u32[]{:S(2)}) collective-permute-start(bf16[32,1024]{1,0:T(8,128)(2,1)S(1)} %get-tuple-element.17), channel_id=1, source_target_pairs={{0,16},{2,18},{4,20},{6,22},{8,24},{10,26},{12,28},{14,30},{16,0},... | collective-permute-start | bytes 196616 | tf_op jit(solution)/shard_map/ppermute | solution.py:347
  6.1 5.7 %collective-permute-start = (bf16[32,1024]{1,0:T(8,128)(2,1)S(1)}, bf16[32,1024]{1,0:T(8,128)(2,1)S(1)}, u32[]{:S(2)}, u32[]{:S(2)}) collective-permute-start(bf16[32,1024]{1,0:T(8,128)(2,1)S(1)} %get-tuple-element.17), channel_id=1, source_target_pairs={{0,8},{2,10},{4,12},{6,14},{8,0},{10,2},{12,4},{14,6},{16,24},{18,... | collective-permute-start | bytes 196616 | tf_op jit(solution)/shard_map/ppermute | solution.py:347
  9.8 5.9 %copy-start.27 = (bf16[32,3072]{1,0:T(8,128)(2,1)}, bf16[32,3072]{1,0:T(8,128)(2,1)S(1)}, u32[]{:S(2)}) copy-start(bf16[32,3072]{1,0:T(8,128)(2,1)S(1)} %slice.18) | copy-start | bytes 589828
  11.9 17.7 %collective-permute-start.5 = (bf16[32,3072]{1,0:T(8,128)(2,1)S(1)}, bf16[32,3072]{1,0:T(8,128)(2,1)S(1)}, u32[]{:S(2)}, u32[]{:S(2)}) collective-permute-start(bf16[32,3072]{1,0:T(8,128)(2,1)S(1)} %slice.18), channel_id=1, source_target_pairs={{0,24},{2,26},{4,28},{6,30},{8,16},{10,18},{12,20},{14,22},{16,8},... | collective-permute-start | bytes 589832 | tf_op jit(solution)/shard_map/ppermute | solution.py:347
  15.7 15.8 %collective-permute-start.4 = (bf16[32,3072]{1,0:T(8,128)(2,1)S(1)}, bf16[32,3072]{1,0:T(8,128)(2,1)S(1)}, u32[]{:S(2)}, u32[]{:S(2)}) collective-permute-start(bf16[32,3072]{1,0:T(8,128)(2,1)S(1)} %slice.18), channel_id=1, source_target_pairs={{0,16},{2,18},{4,20},{6,22},{8,24},{10,26},{12,28},{14,30},{16,0},... | collective-permute-start | bytes 589832 | tf_op jit(solution)/shard_map/ppermute | solution.py:347
  15.7 15.8 %collective-permute-start.3 = (bf16[32,3072]{1,0:T(8,128)(2,1)S(1)}, bf16[32,3072]{1,0:T(8,128)(2,1)S(1)}, u32[]{:S(2)}, u32[]{:S(2)}) collective-permute-start(bf16[32,3072]{1,0:T(8,128)(2,1)S(1)} %slice.18), channel_id=1, source_target_pairs={{0,8},{2,10},{4,12},{6,14},{8,0},{10,2},{12,4},{14,6},{16,24},{18,... | collective-permute-start | bytes 589832 | tf_op jit(solution)/shard_map/ppermute | solution.py:347
  16.3 20.2 %collective-permute-start.9 = (bf16[4,32,1024]{2,1,0:T(8,128)(2,1)S(1)}, bf16[4,32,1024]{2,1,0:T(8,128)(2,1)S(1)}, u32[]{:S(2)}, u32[]{:S(2)}) collective-permute-start(bf16[4,32,1024]{2,1,0:T(8,128)(2,1)S(1)} %pad_maximum_fusion.1.refs_0_), channel_id=1, source_target_pairs={{0,2},{2,0},{4,6},{6,4},{8,10},{10,8},{12,14},{14,12},{16,18},{18,... | collective-permute-start | bytes 786440 | tf_op jit(solution)/shard_map/ppermute | solution.py:347
  18.0 19.1 %collective-permute-start.10 = (bf16[4,32,1024]{2,1,0:T(8,128)(2,1)S(1)}, bf16[4,32,1024]{2,1,0:T(8,128)(2,1)}, u32[]{:S(2)}, u32[]{:S(2)}) collective-permute-start(bf16[4,32,1024]{2,1,0:T(8,128)(2,1)S(1)} %pad_maximum_fusion.1.refs_0_), channel_id=1, source_target_pairs={{0,4},{2,6},{4,0},{6,2},{8,12},{10,14},{12,8},{14,10},{16,20},{18,... | collective-permute-start | bytes 786440 | tf_op jit(solution)/shard_map/ppermute | solution.py:347
  25.9 6.4 %copy-start.28 = (bf16[32,3072]{1,0:T(8,128)(2,1)S(1)}, bf16[32,3072]{1,0:T(8,128)(2,1)}, u32[]{:S(2)}) copy-start(bf16[32,3072]{1,0:T(8,128)(2,1)} %copy-done.27) | copy-start | bytes 589828
  25.9 12.1 %copy-start.12 = (bf16[4096,512]{1,0:T(8,128)(2,1)S(1)}, bf16[4096,512]{1,0:T(8,128)(2,1)}, u32[]{:S(2)}) copy-start(bf16[4096,512]{1,0:T(8,128)(2,1)} %refs_2_.1) | copy-start | bytes 12582916
  25.9 12.1 %copy-start.17 = (bf16[32,512]{1,0:T(8,128)(2,1)S(1)}, bf16[32,512]{1,0:T(8,128)(2,1)}, u32[]{:S(2)}) copy-start(bf16[32,512]{1,0:T(8,128)(2,1)} %refs_3_.1) | copy-start | bytes 98308
  25.9 12.1 %copy-start.22 = (bf16[32,512]{1,0:T(8,128)(2,1)S(1)}, bf16[32,512]{1,0:T(8,128)(2,1)}, u32[]{:S(2)}) copy-start(bf16[32,512]{1,0:T(8,128)(2,1)} %refs_4_.3) | copy-start | bytes 98308
  29.5 1.9 copy-start.29
  29.6 8.4 %collective-permute-start.11 = (bf16[4,32,1024]{2,1,0:T(8,128)(2,1)S(1)}, bf16[4,32,1024]{2,1,0:T(8,128)(2,1)S(1)}, u32[]{:S(2)}, u32[]{:S(2)}) collective-permute-start(bf16[4,32,1024]{2,1,0:T(8,128)(2,1)S(1)} %pad_maximum_fusion.1.refs_0_), channel_id=1, source_target_pairs={{0,6},{2,4},{4,2},{6,0},{8,14},{10,12},{12,10},{14,8},{16,22},{18,... | collective-permute-start | bytes 786440 | tf_op jit(solution)/shard_map/ppermute | solution.py:347
  31.5 0.7 copy-start.30
  31.5 0.8 copy-start.31
  33.5 40.7 %copy-start.9 = (bf16[4,32,3072]{2,1,0:T(8,128)(2,1)}, bf16[4,32,3072]{2,1,0:T(8,128)(2,1)S(1)}, u32[]{:S(2)}) copy-start(bf16[4,32,3072]{2,1,0:T(8,128)(2,1)S(1)} %pad_maximum_fusion.refs_8_.refs_0_) | copy-start | bytes 2359300
  33.5 34.2 %collective-permute-start.6 = (bf16[4,32,3072]{2,1,0:T(8,128)(2,1)S(1)}, bf16[4,32,3072]{2,1,0:T(8,128)(2,1)}, u32[]{:S(2)}, u32[]{:S(2)}) collective-permute-start(bf16[4,32,3072]{2,1,0:T(8,128)(2,1)S(1)} %pad_maximum_fusion.refs_8_.refs_0_), channel_id=1, source_target_pairs={{0,2},{2,0},{4,6},{6,4},{8,10},{10,8},{12,14},{14,12},{16,18},{18,... | collective-permute-start | bytes 2359304 | tf_op jit(solution)/shard_map/ppermute | solution.py:347
  35.0 39.2 %collective-permute-start.7 = (bf16[4,32,3072]{2,1,0:T(8,128)(2,1)S(1)}, bf16[4,32,3072]{2,1,0:T(8,128)(2,1)}, u32[]{:S(2)}, u32[]{:S(2)}) collective-permute-start(bf16[4,32,3072]{2,1,0:T(8,128)(2,1)S(1)} %pad_maximum_fusion.refs_8_.refs_0_), channel_id=1, source_target_pairs={{0,4},{2,6},{4,0},{6,2},{8,12},{10,14},{12,8},{14,10},{16,20},{18,... | collective-permute-start | bytes 2359304 | tf_op jit(solution)/shard_map/ppermute | solution.py:347
  36.5 37.6 %collective-permute-start.8 = (bf16[4,32,3072]{2,1,0:T(8,128)(2,1)S(1)}, bf16[4,32,3072]{2,1,0:T(8,128)(2,1)}, u32[]{:S(2)}, u32[]{:S(2)}) collective-permute-start(bf16[4,32,3072]{2,1,0:T(8,128)(2,1)S(1)} %pad_maximum_fusion.refs_8_.refs_0_), channel_id=1, source_target_pairs={{0,6},{2,4},{4,2},{6,0},{8,14},{10,12},{12,10},{14,8},{16,22},{18,... | collective-permute-start | bytes 2359304 | tf_op jit(solution)/shard_map/ppermute | solution.py:347
  60.4 13.8 %copy-start.18 = (bf16[32,512]{1,0:T(8,128)(2,1)S(1)}, bf16[32,512]{1,0:T(8,128)(2,1)}, u32[]{:S(2)}) copy-start(bf16[32,512]{1,0:T(8,128)(2,1)} %refs_3_.1) | copy-start | bytes 98308
  60.4 13.8 %copy-start.23 = (bf16[32,512]{1,0:T(8,128)(2,1)S(1)}, bf16[32,512]{1,0:T(8,128)(2,1)}, u32[]{:S(2)}) copy-start(bf16[32,512]{1,0:T(8,128)(2,1)} %refs_4_.3) | copy-start | bytes 98308
  60.4 38.5 %all-to-all-start.1 = ((bf16[4,4,32,1152]{3,2,1,0:T(8,128)(2,1)}), bf16[4,4,32,1152]{3,2,1,0:T(8,128)(2,1)S(1)}, u32[]{:S(2)}, u32[]{:S(2)}) async-start(bf16[4,4,32,1152]{3,2,1,0:T(8,128)(2,1)} %attend.5.refs_8_), calls=%async_computation.1 | async-start | bytes 2359296 | tf_op jit(solution)/shard_map/all_to_all | solution.py:377
  74.2 2.2 copy-start.13
  99.0 33.0 %all-to-all-start.2 = ((bf16[4,4,32,1152]{3,2,1,0:T(8,128)(2,1)}), bf16[4,4,32,1152]{3,2,1,0:T(8,128)(2,1)S(1)}, u32[]{:S(2)}, u32[]{:S(2)}) async-start(bf16[4,4,32,1152]{3,2,1,0:T(8,128)(2,1)} %attend.6.refs_8_), calls=%async_computation.2 | async-start | bytes 2359296 | tf_op jit(solution)/shard_map/all_to_all | solution.py:377
  103.3 1.2 copy-start.8
  104.6 1.1 copy-start.10
  105.7 2.2 copy-start.14
  107.9 0.8 copy-start.19
  108.6 0.8 copy-start.24
  130.9 1.0 copy-start.2
  132.0 20.0 %all-to-all-start = ((bf16[4,4,32,1152]{3,2,1,0:T(8,128)(2,1)}), bf16[4,4,32,1152]{3,2,1,0:T(8,128)(2,1)S(1)}, u32[]{:S(2)}, u32[]{:S(2)}) async-start(bf16[4,4,32,1152]{3,2,1,0:T(8,128)(2,1)} %copy-done.2), calls=%async_computation | async-start | bytes 2359296 | tf_op jit(solution)/shard_map/all_to_all | solution.py:377
  140.4 1.3 copy-start.3
  144.1 0.8 copy-start.4
  152.0 28.9 %all-to-all-start.4 = ((bf16[4,32,2304]{2,1,0:T(8,128)(2,1)}), bf16[4,32,2304]{2,1,0:T(8,128)(2,1)S(1)}, u32[]{:S(2)}, u32[]{:S(2)}) async-start(bf16[4,32,2304]{2,1,0:T(8,128)(2,1)} %copy-done.4), calls=%async_computation.4 | async-start | bytes 1179648 | tf_op jit(solution)/shard_map/all_to_all | solution.py:377
  156.6 1.1 copy-start.5
  157.7 1.2 copy-start.6
  158.9 2.2 copy-start.15
  161.1 0.8 copy-start.20
  161.9 0.8 copy-start.25
  180.8 7.2 %copy-start.21 = (bf16[32,512]{1,0:T(8,128)(2,1)S(1)}, bf16[32,512]{1,0:T(8,128)(2,1)}, u32[]{:S(2)}) copy-start(bf16[32,512]{1,0:T(8,128)(2,1)} %refs_3_.1) | copy-start | bytes 98308
  180.8 7.2 %copy-start.26 = (bf16[32,512]{1,0:T(8,128)(2,1)S(1)}, bf16[32,512]{1,0:T(8,128)(2,1)}, u32[]{:S(2)}) copy-start(bf16[32,512]{1,0:T(8,128)(2,1)} %refs_4_.3) | copy-start | bytes 98308
  180.8 17.0 %all-to-all-start.3 = ((bf16[4,4,32,1152]{3,2,1,0:T(8,128)(2,1)}), bf16[4,4,32,1152]{3,2,1,0:T(8,128)(2,1)S(1)}, u32[]{:S(2)}, u32[]{:S(2)}) async-start(bf16[4,4,32,1152]{3,2,1,0:T(8,128)(2,1)} %attend.8.refs_0_), calls=%async_computation.3 | async-start | bytes 2359296 | tf_op jit(solution)/shard_map/all_to_all | solution.py:377
  186.6 1.5 copy-start.7
  186.6 1.5 copy-start.11
  188.1 2.2 copy-start.16
  201.0 17.8 %all-to-all-start.5 = ((bf16[4,32,2304]{2,1,0:T(8,128)(2,1)}), bf16[4,32,2304]{2,1,0:T(8,128)(2,1)S(1)}, u32[]{:S(2)}, u32[]{:S(2)}) async-start(bf16[4,32,2304]{2,1,0:T(8,128)(2,1)} %merge.3.refs_0_), calls=%async_computation.5 | async-start | bytes 1179648 | tf_op jit(solution)/shard_map/all_to_all | solution.py:377
  218.8 15.6 %all-to-all-start.8 = ((bf16[4,32,2048]{2,1,0:T(8,128)(2,1)}), bf16[4,32,2048]{2,1,0:T(8,128)(2,1)S(1)}, u32[]{:S(2)}, u32[]{:S(2)}) async-start(bf16[4,32,2048]{2,1,0:T(8,128)(2,1)} %normalize.2.refs_5_), calls=%async_computation.8 | async-start | bytes 1048576 | tf_op jit(solution)/shard_map/all_to_all | solution.py:377
  278.4 26.8 %all-to-all-start.7 = ((bf16[4,4,32,2048]{3,2,1,0:T(8,128)(2,1)}), bf16[4,4,32,2048]{3,2,1,0:T(8,128)(2,1)}, u32[]{:S(2)}, u32[]{:S(2)}) async-start(bf16[4,4,32,2048]{3,2,1,0:T(8,128)(2,1)} %broadcast_in_dim.7), calls=%async_computation.7 | async-start | bytes 4194304 | tf_op jit(solution)/shard_map/all_to_all | solution.py:377
  282.9 2.2 copy-start
  305.2 2.2 copy-start.1
  310.3 1.6 collective-permute-start.12

commit v7 on v5

--- a/solution.py
+++ b/solution.py
@@ -29,7 +29,7 @@
     return parts[0]
 
 
-def attend_kernel(info, *refs, chosen, blocks, plane, rows, head, q_head, group_step, key_chunk, waits):
+def attend_kernel(info, *refs, chosen, blocks, plane, rows, group_step, key_chunk, waits):
     count = len(chosen)
     q_refs, refs = refs[:count], refs[count:]
     kt_ref, v_ref, ks_ref, vs_ref = refs[:4]
@@ -44,13 +44,11 @@
     steps = GROUP_QUERIES // group_step
     chunks = keys // key_chunk
     strip = math.gcd(tile_rows, 64)
-    own = slice(head * HEAD_SIZE, (head + 1) * HEAD_SIZE)
-    q_first = q_head * GROUP_QUERIES
 
     ks_pad[...] = jnp.zeros_like(ks_pad)
     vs_pad[...] = jnp.zeros_like(vs_pad)
-    ks_pad[0:rows, :] = ks_ref[:, own]
-    vs_pad[0:rows, :] = vs_ref[:, own]
+    ks_pad[0:rows, :] = ks_ref[...]
+    vs_pad[0:rows, :] = vs_ref[...]
     row = lax.broadcasted_iota(jnp.int32, (rows, LANES), 0)
     col = lax.broadcasted_iota(jnp.int32, (rows, LANES), 1)
     for i in range(group_step):
@@ -67,7 +65,7 @@
         slot, group = place(tile)
         parts = []
         for i in range(group_step):
-            cols = pl.ds(pl.multiple_of((q_first + group + i) * HEAD_SIZE, HEAD_SIZE), HEAD_SIZE)
+            cols = pl.ds(pl.multiple_of((group + i) * HEAD_SIZE, HEAD_SIZE), HEAD_SIZE)
             parts += [q[slot, :, cols] for q in q_refs]
         return jnp.concatenate(parts, axis=0)
 
@@ -118,7 +116,7 @@
                 weight_ref[part, c : c + LANES] = weights.astype(BF16)
 
     def apply_chunk(acc, j):
-        values = v_ref[j * key_chunk : (j + 1) * key_chunk, own]
+        values = v_ref[j * key_chunk : (j + 1) * key_chunk]
         return acc + jnp.dot(weight_refs[j % 2][...], values, preferred_element_type=F32)
 
     def step(now, later):
@@ -170,10 +168,11 @@
     plane, count = len(q_pieces), len(chosen)
     cols = GROUP_QUERIES * HEAD_SIZE
     key_count = values.shape[0]
-    group_step = min(GROUP_QUERIES, 2 * (plane // count))
+    group_step = min(GROUP_QUERIES, 4 * (plane // count))
     tile_rows = group_step * count * rows
     key_chunk = min(key_count, 512)
-    vmem, smem = pltpu.MemorySpace.VMEM, pltpu.MemorySpace.SMEM
+    vmem = pltpu.MemorySpace.VMEM
+    span_block = pl.BlockSpec((rows, HEAD_SIZE), lambda i, s: (0, head))
     scored = blocks * count * rows * GROUP_QUERIES * key_count
     return pl.pallas_call(
         functools.partial(
@@ -182,25 +181,32 @@
             blocks=blocks,
             plane=plane,
             rows=rows,
-            head=head,
-            q_head=q_head,
             group_step=group_step,
             key_chunk=key_chunk,
             waits=len(after),
         ),
-        in_specs=[pl.BlockSpec(memory_space=smem)]
-        + [pl.BlockSpec(memory_space=vmem)] * (count + 4)
-        + [pl.BlockSpec(memory_space=pl.ANY)] * len(after),
-        out_specs=[pl.BlockSpec(memory_space=vmem)] * count,
-        scratch_shapes=[vmem((tile_rows, key_chunk), BF16)] * 2
-        + [
-            vmem((tile_rows, key_count + LANES), F32),
-            vmem((tile_rows, LANES), F32),
-            vmem((count * rows, LANES), F32),
-            vmem((tile_rows, LANES), jnp.int32),
-            vmem((LANES, HEAD_SIZE), BF16),
-            vmem((LANES, HEAD_SIZE), BF16),
-        ],
+        grid_spec=pltpu.PrefetchScalarGridSpec(
+            num_scalar_prefetch=1,
+            grid=(1,),
+            in_specs=[pl.BlockSpec((blocks, rows, cols), lambda i, s: (0, 0, q_head))] * count
+            + [
+                pl.BlockSpec((HEAD_SIZE, key_count), lambda i, s: (head, 0)),
+                pl.BlockSpec((key_count, HEAD_SIZE), lambda i, s: (0, head)),
+                span_block,
+                span_block,
+            ]
+            + [pl.BlockSpec(memory_space=pl.ANY)] * len(after),
+            out_specs=[pl.BlockSpec((blocks, rows, cols + LANES), lambda i, s: (0, 0, 0))] * count,
+            scratch_shapes=[vmem((tile_rows, key_chunk), BF16)] * 2
+            + [
+                vmem((tile_rows, key_count + LANES), F32),
+                vmem((tile_rows, LANES), F32),
+                vmem((count * rows, LANES), F32),
+                vmem((tile_rows, LANES), jnp.int32),
+                vmem((LANES, HEAD_SIZE), BF16),
+                vmem((LANES, HEAD_SIZE), BF16),
+            ],
+        ),
         out_shape=[jax.ShapeDtypeStruct((blocks, rows, cols + LANES), BF16)] * count,
         compiler_params=pltpu.CompilerParams(vmem_limit_bytes=ATTEND_VMEM),
         cost_estimate=pl.CostEstimate(
@@ -294,19 +300,19 @@
     )(*pieces, *after)
 
 
-def project_kernel(info, *refs, chosen, blocks, rows, width):
+def project_kernel(info, *refs, order, chosen, rows, width):
     ins, (w_ref, *base_ref, out) = refs[: len(chosen)], refs[len(chosen) :]
     out[...] = base_ref[0][...].astype(out.dtype) if base_ref else jnp.zeros_like(out)
     for x_ref, b in zip(ins, chosen):
-        x = x_ref[...].reshape(blocks * rows, width)
+        x = x_ref[...].reshape(len(order) * rows, width)
         y = jnp.dot(x, w_ref[...], preferred_element_type=F32)
-        for a in range(blocks):
-            at = (info[3 + blocks + a], b ^ info[1])
-            part = y[a * rows : (a + 1) * rows]
+        for n, a in enumerate(order):
+            at = (info[3 + len(order) + a], b ^ info[1])
+            part = y[n * rows : (n + 1) * rows]
             out[at] = ((base_ref[0][at] + part) if base_ref else part).astype(out.dtype)
 
 
-def project(info, pieces, chosen, weight, group, base, dtype):
+def project(info, pieces, order, chosen, weight, group, base, dtype):
     plane = len(pieces)
     blocks, rows, width = pieces[0].shape
     out_cols = weight.shape[1]
@@ -314,7 +320,7 @@
     whole = pl.BlockSpec((blocks, rows, width), lambda i, s: (0, 0, 0))
     out_block = pl.BlockSpec((blocks, plane, rows, out_cols), lambda i, s: (0, 0, 0, 0))
     return pl.pallas_call(
-        functools.partial(project_kernel, chosen=chosen, blocks=blocks, rows=rows, width=width),
+        functools.partial(project_kernel, order=order, chosen=chosen, rows=rows, width=width),
         grid_spec=pltpu.PrefetchScalarGridSpec(
             num_scalar_prefetch=1,
             grid=(1,),
@@ -362,28 +368,39 @@
     def stack_blocks(x):
         return jnp.stack([x] + [exchange(x, "ctx", a * plane) for a in range(1, blocks)])
 
+    def doubled(column):
+        stack, order, distance = column
+        if not distance:
+            return column
+        stack = jnp.concatenate([stack, exchange(stack, "ctx", distance * plane)])
+        return stack, order + [a ^ distance for a in order], distance // 2
+
     def gather_plane(stack):
         return [stack] + [exchange(stack, "ctx", b) for b in range(1, plane)]
 
     first = stack_blocks(queries[:, :width])
     sources, stacks = [(gather_plane(first), 0)], []
     keys, _ = lax.optimization_barrier((context_keys, first))
-    keys_t = [
-        (keys if h else context_keys)[:, h * HEAD_SIZE : (h + 1) * HEAD_SIZE].T for h in range(heads)
-    ]
+    keys_t = keys.T
     if heads > 1:
-        stacks = [stack_blocks(queries[:, width:])]
+        held, _ = lax.optimization_barrier((queries[:, width:], first))
+        stacks = [stack_blocks(held)]
         pieces = gather_plane(stacks[0])
         sources += [(pieces, i) for i in range(heads - 1)]
 
     size = 2 if heads % 2 == 0 else 1
     attended, merged, rows_of = [], [], []
 
+    received = {}
+
+    def receive(h):
+        if h not in received:
+            received[h] = [exchange(x, "ctx", b) for b, x in zip(range(1, plane), attended[h][1 - plane :])]
+        return received[h]
+
     def merge(after):
         group = range(len(merged) * size, (len(merged) + 1) * size)
-        parts = [
-            [attended[h][0]] + [exchange(attended[h][b], "ctx", b) for b in range(1, plane)] for h in group
-        ]
+        parts = [[attended[h][0]] + receive(h) for h in group]
         merged.append(merge_pieces(parts, after))
         return [merged[-1][0]]
 
@@ -396,7 +413,7 @@
     def attend(h, chosen, after):
         pieces, q_head = sources[h]
         return attend_head(
-            info, pieces, chosen, q_head, keys_t[h], context_values, span_keys, span_values, h, after
+            info, pieces, chosen, q_head, keys_t, context_values, span_keys, span_values, h, after
         )
 
     latest = stacks
@@ -407,25 +424,38 @@
         if len(rows_of) < len(merged):
             latest = normalize(latest)
         if start:
-            attended[h] = attend(h, [0], latest) + attended[h]
+            before = receive(h - 1) if h else []
+            attended[h] = attend(h, [0], latest + before) + attended[h]
             latest = [attended[h][0]]
         if h >= (len(merged) + 1) * size:
             latest = merge(latest)
+    columns = []
+
+    def gather_round():
+        columns.extend((x[None], [0], blocks // 2) for x in rows_of[len(columns) :])
+        if len(merged) == heads // size and columns:
+            held, _ = lax.optimization_barrier(([column[0] for column in columns], merged[-1][0]))
+            columns[:] = [(x, *column[1:]) for x, column in zip(held, columns)]
+        columns[:] = [doubled(column) for column in columns]
+        return [column[0] for column in columns]
+
     while len(merged) < heads // size:
-        latest = merge(latest)
+        latest = merge(latest + gather_round())
     while len(rows_of) < heads // size:
-        latest = normalize(latest)
+        latest = normalize(latest + gather_round())
+    while any(distance for _, _, distance in columns) or len(columns) < len(rows_of):
+        gather_round()
 
     total = []
-    for g, rows_now in enumerate(rows_of):
+    for g, (stack, order, _) in enumerate(columns):
+        if g:
+            stack, _ = lax.optimization_barrier((stack, pieces))
+        pieces = gather_plane(stack)
         if g < len(rows_of) - 1:
-            rows_now, _ = lax.optimization_barrier((rows_now, attended[-1][0]))
-        pieces = gather_plane(stack_blocks(rows_now))
-        if g < len(rows_of) - 1:
-            total = [project(info, pieces, range(plane), out_weight, g, total, F32)]
+            total = [project(info, pieces, order, range(plane), out_weight, g, total, F32)]
         else:
-            total = [project(info, pieces, range(plane // 2), out_weight, g, total, F32)]
-            total = [project(info, pieces, range(plane // 2, plane), out_weight, g, total, BF16)]
+            total = [project(info, pieces, order, range(plane // 2), out_weight, g, total, F32)]
+            total = [project(info, pieces, order, range(plane // 2, plane), out_weight, g, total, BF16)]
     partial_out = total[0].reshape(ctx_count * rows, -1)
     share = partial_out.shape[0] // head_count
     total = lax.dynamic_slice_in_dim(partial_out, my_head * share, share, 0).astype(F32)

time: 251 us -> 257 us (1.024); the launches traced: 248 us -> 257 us
  Pallas kernels: 101 us -> 110 us
    pallas_call x5, Pallas kernels: 89.9 us -> 99.2 us  [attend_head(): pl.pallas_call(functools.partial(attend_kernel, chosen=chosen, blocks=blo...]
    unnamed x11 -> x17, local copies, waits for them, and re-layouts: 2.74 us -> 6.6 us
    ppermute x43 -> x41, waiting for transfers between devices: 51 us -> 49.3 us  [exchange(): return lax.ppermute(x, axis, [(i, i ^ distance) for i in range(count)])]
    ppermute x43 -> x41, starting transfers between devices: 76.1 us -> 77.7 us  [exchange(): return lax.ppermute(x, axis, [(i, i ^ distance) for i in range(count)])]
  transfers between devices with their start and end apart: 43 -> 41, of which waited for: 12 -> 16; matrix products, arithmetic and copies ran while one was open for 6% -> 4% of each run, Pallas kernels for 40% -> 40%
where the time goes in v7:
time: 257 us
  Pallas kernels  110 us (43%)
  starting transfers between devices  77.7 us (30%)
  waiting for transfers between devices  49.3 us (19%)
  local copies, waits for them, and re-layouts  16.2 us (6%)
  other arithmetic  3.28 us (1%)
    pallas_call x5, Pallas kernels, attend_head(): pl.pallas_call(functools.partial(attend_kernel, chosen=chosen, blocks=blo...  99.2 us
    ppermute x41, starting transfers between devices, exchange(): return lax.ppermute(x, axis, [(i, i ^ distance) for i in range(count)])  77.7 us
    ppermute x41, waiting for transfers between devices, exchange(): return lax.ppermute(x, axis, [(i, i ^ distance) for i in range(count)])  49.3 us
    pallas_call x3, Pallas kernels, project(): pl.pallas_call(functools.partial(project_kernel, order=order, chosen=chos...  6.68 us
    unnamed x17, local copies, waits for them, and re-layouts  6.6 us
    optimization_barrier x1, local copies, waits for them, and re-layouts, local(): keys, _ = lax.optimization_barrier((context_keys, first))  6.38 us
  transfers between devices with their start and end apart: 41, of which 16 were waited for; matrix products, arithmetic and copies ran while one was open for 4% of the time, Pallas kernels for 40%

profile of v7, /device:TPU:0, one launch (start us, length us, event | category | flops | bytes accessed | tf_op | source)
XLA Modules:
  0.0 257.2 jit_solution(12886318397741193973)
XLA Ops:
  0.0 0.8 slice_bitcast_fusion
  0.9 3.1 %collective-permute-start = (bf16[32,1024]{1,0:T(8,128)(2,1)S(1)}, bf16[32,1024]{1,0:T(8,128)(2,1)S(1)}, u32[]{:S(2)}, u32[]{:S(2)}) collective-permute-start(bf16[32,1024]{1,0:T(8,128)(2,1)S(1)} %get-tuple-element.70), channel_id=1, source_target_pairs={{0,8},{2,10},{4,12},{6,14},{8,0},{10,2},{12,4},{14,6},{16,24},{18,... | collective-permute-start | bytes 196616 | tf_op jit(solution)/shard_map/ppermute | solution.py:345
  3.9 2.6 %collective-permute-start.1 = (bf16[32,1024]{1,0:T(8,128)(2,1)S(1)}, bf16[32,1024]{1,0:T(8,128)(2,1)S(1)}, u32[]{:S(2)}, u32[]{:S(2)}) collective-permute-start(bf16[32,1024]{1,0:T(8,128)(2,1)S(1)} %get-tuple-element.70), channel_id=1, source_target_pairs={{0,16},{2,18},{4,20},{6,22},{8,24},{10,26},{12,28},{14,30},{16,0},... | collective-permute-start | bytes 196616 | tf_op jit(solution)/shard_map/ppermute | solution.py:345
  6.5 0.9 slice.7
  7.5 0.8 compare_reduce_fusion
  9.0 0.8 sort.17
  9.8 1.4 collective-permute-done.1
  11.2 1.4 collective-permute-done.2
  12.7 2.3 collective-permute-start.7
  15.1 2.0 collective-permute-start.8
  17.8 0.7 concatenate.15.info
  18.5 1.6 collective-permute-start.3
  20.0 1.5 collective-permute-start.4
  21.5 6.4 %copy.9 = bf16[4096,512]{0,1:T(8,128)(2,1)} copy(bf16[4096,512]{1,0:T(8,128)(2,1)} %param.10) | data formatting | bytes 8388608 | tf_op jit(solution)/shard_map/optimization_barrier | solution.py:383
  28.4 1.2 collective-permute-done.7
  29.7 1.6 collective-permute-start.12
  31.3 1.5 collective-permute-start.13
  33.3 4.8 %collective-permute-done.5.refs_3_ = bf16[4,32,1024]{2,1,0:T(8,128)(2,1)S(1)} collective-permute-done((bf16[4,32,1024]{2,1,0:T(8,128)(2,1)S(1)}, bf16[4,32,1024]{2,1,0:T(8,128)(2,1)S(1)}, u32[]{:S(2)}, u32[]{:S(2)}) %collective-permute-start.5) | collective-permute-done | bytes 262176 | tf_op jit(solution)/shard_map/ppermute | solution.py:345
  38.1 2.2 copy-done.2
  40.3 2.2 copy-done.4
  42.5 24.4 %attend.5 = (bf16[4,32,1152]{2,1,0:T(8,128)(2,1)S(1)}, bf16[4,32,1152]{2,1,0:T(8,128)(2,1)S(1)}, bf16[4,32,1152]{2,1,0:T(8,128)(2,1)S(1)}, bf16[4,32,1152]{2,1,0:T(8,128)(2,1)S(1)}) custom-call(s32[11]{0:T(128)S(1)} %concatenate.15.info, bf16[4,32,1024]{2,1,0:T(8,128)(2,1)S(1)} %pad_maximum_fusion.2.refs_0_, ...), custom_call_target="tpu_custom_call" | custom-call | flops 17179869184 | bytes 4194304 | tf_op jit(solution)/shard_map/attend/pallas_call | solution.py:177
  66.9 6.9 %collective-permute-start.10 = (bf16[4,32,1152]{2,1,0:T(8,128)(2,1)S(1)}, bf16[4,32,1152]{2,1,0:T(8,128)(2,1)S(1)}, u32[]{:S(2)}, u32[]{:S(2)}) collective-permute-start(bf16[4,32,1152]{2,1,0:T(8,128)(2,1)S(1)} %get-tuple-element.42), channel_id=1, source_target_pairs={{0,4},{2,6},{4,0},{6,2},{8,12},{10,14},{12,8},{14,10},{16,20},{18,... | collective-permute-start | bytes 884744 | tf_op jit(solution)/shard_map/ppermute | solution.py:345
  73.8 1.5 collective-permute-start.11
  75.3 24.8 %attend.6 = (bf16[4,32,1152]{2,1,0:T(8,128)(2,1)S(1)}, bf16[4,32,1152]{2,1,0:T(8,128)(2,1)S(1)}, bf16[4,32,1152]{2,1,0:T(8,128)(2,1)S(1)}, bf16[4,32,1152]{2,1,0:T(8,128)(2,1)S(1)}) custom-call(s32[11]{0:T(128)S(1)} %concatenate.15.info, bf16[4,32,3072]{2,1,0:T(8,128)(2,1)S(1)} %pad_maximum_fusion.refs_8_.refs_0_, ...), custom_call_target="tpu_custom_call" | custom-call | flops 17179869184 | bytes 4194304 | tf_op jit(solution)/shard_map/attend/pallas_call | solution.py:177
  100.2 8.4 %collective-permute-start.15 = (bf16[4,32,1152]{2,1,0:T(8,128)(2,1)S(1)}, bf16[4,32,1152]{2,1,0:T(8,128)(2,1)S(1)}, u32[]{:S(2)}, u32[]{:S(2)}) collective-permute-start(bf16[4,32,1152]{2,1,0:T(8,128)(2,1)S(1)} %get-tuple-element.45), channel_id=1, source_target_pairs={{0,2},{2,0},{4,6},{6,4},{8,10},{10,8},{12,14},{14,12},{16,18},{18,... | collective-permute-start | bytes 884744 | tf_op jit(solution)/shard_map/ppermute | solution.py:345
  108.6 1.5 collective-permute-start.17
  110.1 24.4 %attend.7 = (bf16[4,32,1152]{2,1,0:T(8,128)(2,1)S(1)}, bf16[4,32,1152]{2,1,0:T(8,128)(2,1)S(1)}, bf16[4,32,1152]{2,1,0:T(8,128)(2,1)S(1)}, bf16[4,32,1152]{2,1,0:T(8,128)(2,1)S(1)}) custom-call(s32[11]{0:T(128)S(1)} %concatenate.15.info, bf16[4,32,3072]{2,1,0:T(8,128)(2,1)S(1)} %pad_maximum_fusion.refs_8_.refs_0_, ...), custom_call_target="tpu_custom_call" | custom-call | flops 17179869184 | bytes 4194304 | tf_op jit(solution)/shard_map/attend/pallas_call | solution.py:177
  134.6 1.7 merge.2
  136.3 8.3 %collective-permute-start.22 = (bf16[4,32,1152]{2,1,0:T(8,128)(2,1)S(1)}, bf16[4,32,1152]{2,1,0:T(8,128)(2,1)S(1)}, u32[]{:S(2)}, u32[]{:S(2)}) collective-permute-start(bf16[4,32,1152]{2,1,0:T(8,128)(2,1)S(1)} %get-tuple-element.54), channel_id=1, source_target_pairs={{0,2},{2,0},{4,6},{6,4},{8,10},{10,8},{12,14},{14,12},{16,18},{18,... | collective-permute-start | bytes 884744 | tf_op jit(solution)/shard_map/ppermute | solution.py:345
  144.9 1.3 collective-permute-start.24
  146.2 2.1 collective-permute-start.19
  148.3 2.1 collective-permute-start.20
  150.4 19.2 %attend.8 = (bf16[4,32,1152]{2,1,0:T(8,128)(2,1)S(1)}, bf16[4,32,1152]{2,1,0:T(8,128)(2,1)S(1)}, bf16[4,32,1152]{2,1,0:T(8,128)(2,1)S(1)}) custom-call(s32[11]{0:T(128)S(1)} %concatenate.15.info, bf16[4,32,3072]{2,1,0:T(8,128)(2,1)S(1)} %collective-permute-done.12.refs_1_.refs_0_, bf16[4,32,3072]{2,1,0:T(8,128)(2,1)S(1)} %collective-permute-done.13.refs_2_.refs_1_, ...), custom_call_target="tpu_custom_call" | custom-call | flops 12884901888 | bytes 3670016 | tf_op jit(solution)/shard_map/attend/pallas_call | solution.py:177
  169.6 6.7 %collective-permute-start.25 = (bf16[4,32,1152]{2,1,0:T(8,128)(2,1)S(1)}, bf16[4,32,1152]{2,1,0:T(8,128)(2,1)S(1)}, u32[]{:S(2)}, u32[]{:S(2)}) collective-permute-start(bf16[4,32,1152]{2,1,0:T(8,128)(2,1)S(1)} %get-tuple-element.53.refs_4_), channel_id=1, source_target_pairs={{0,2},{2,0},{4,6},{6,4},{8,10},{10,8},{12,14},{14,12},{16,18},{18,... | collective-permute-start | bytes 884744 | tf_op jit(solution)/shard_map/ppermute | solution.py:345
  176.3 1.8 collective-permute-start.26
  178.7 1.4 collective-permute-start.27
  180.2 6.3 %attend.9.refs_4_.refs_8_ = bf16[4,32,1152]{2,1,0:T(8,128)(2,1)S(1)} custom-call(s32[11]{0:T(128)S(1)} %concatenate.15.info, bf16[4,32,3072]{2,1,0:T(8,128)(2,1)S(1)} %pad_maximum_fusion.refs_8_.refs_0_, bf16[512,4096]{1,0:T(8,128)(2,1)S(1)} %bitcast.22, bf16[4096,512]{1,0:T(8,128)(2,1)S(1)} %copy-done.5, bf16[32,512]{1,0:T(8,128)(2,1)S(1)} %copy-done.6, ...), custom_call_target="tpu_custom_call" | custom-call | flops 4294967296 | bytes 2621440 | tf_op jit(solution)/shard_map/attend/pallas_call | solution.py:177
  186.5 1.2 collective-permute-done.21
  187.8 1.7 merge.3
  189.5 2.0 collective-permute-start.29
  191.5 0.7 collective-permute-start.30
  192.2 1.8 collective-permute-start.31
  194.0 3.5 %collective-permute-done.28 = bf16[2,32,2048]{2,1,0:T(8,128)(2,1)S(1)} collective-permute-done((bf16[2,32,2048]{2,1,0:T(8,128)(2,1)S(1)}, bf16[2,32,2048]{2,1,0:T(8,128)(2,1)S(1)}, u32[]{:S(2)}, u32[]{:S(2)}) %collective-permute-start.28) | collective-permute-done | bytes 262176 | tf_op jit(solution)/shard_map/ppermute | solution.py:345
  197.5 2.2 collective-permute-done.29.refs_1_
  199.7 3.2 %collective-permute-done.30.refs_2_ = bf16[32,2304]{1,0:T(8,128)(2,1)S(1)} collective-permute-done((bf16[32,2304]{1,0:T(8,128)(2,1)S(1)}, bf16[32,2304]{1,0:T(8,128)(2,1)S(1)}, u32[]{:S(2)}, u32[]{:S(2)}) %collective-permute-start.30) | collective-permute-done | bytes 147488 | tf_op jit(solution)/shard_map/ppermute | solution.py:345
  203.5 2.7 %collective-permute-start.32 = (bf16[1,32,2048]{2,1,0:T(8,128)(2,1)S(1)}, bf16[1,32,2048]{2,1,0:T(8,128)(2,1)S(1)}, u32[]{:S(2)}, u32[]{:S(2)}) collective-permute-start(bf16[1,32,2048]{2,1,0:T(8,128)(2,1)S(1)} %bitcast.27), channel_id=1, source_target_pairs={{0,16},{2,18},{4,20},{6,22},{8,24},{10,26},{12,28},{14,30},{16,0},... | collective-permute-start | bytes 393224 | tf_op jit(solution)/shard_map/ppermute | solution.py:345
  206.2 3.9 %collective-permute-done.32 = bf16[1,32,2048]{2,1,0:T(8,128)(2,1)S(1)} collective-permute-done((bf16[1,32,2048]{2,1,0:T(8,128)(2,1)S(1)}, bf16[1,32,2048]{2,1,0:T(8,128)(2,1)S(1)}, u32[]{:S(2)}, u32[]{:S(2)}) %collective-permute-start.32) | collective-permute-done | bytes 131104 | tf_op jit(solution)/shard_map/ppermute | solution.py:345
  210.1 2.1 collective-permute-start.34
  212.3 1.6 collective-permute-start.35
  213.9 1.4 collective-permute-start.36
  215.3 1.6 collective-permute-start.33
  216.9 4.8 %collective-permute-done.33 = bf16[2,32,2048]{2,1,0:T(8,128)(2,1)S(1)} collective-permute-done((bf16[2,32,2048]{2,1,0:T(8,128)(2,1)S(1)}, bf16[2,32,2048]{2,1,0:T(8,128)(2,1)S(1)}, u32[]{:S(2)}, u32[]{:S(2)}) %collective-permute-start.33) | collective-permute-done | bytes 262176 | tf_op jit(solution)/shard_map/ppermute | solution.py:345
  221.7 1.6 collective-permute-done.34.refs_1_
  223.3 6.4 %collective-permute-done.35.refs_2_ = bf16[4,32,2048]{2,1,0:T(8,128)(2,1)S(1)} collective-permute-done((bf16[4,32,2048]{2,1,0:T(8,128)(2,1)S(1)}, bf16[4,32,2048]{2,1,0:T(8,128)(2,1)S(1)}, u32[]{:S(2)}, u32[]{:S(2)}) %collective-permute-start.35) | collective-permute-done | bytes 524320 | tf_op jit(solution)/shard_map/ppermute | solution.py:345
  229.7 4.9 %collective-permute-done.36.refs_3_ = bf16[4,32,2048]{2,1,0:T(8,128)(2,1)S(1)} collective-permute-done((bf16[4,32,2048]{2,1,0:T(8,128)(2,1)S(1)}, bf16[4,32,2048]{2,1,0:T(8,128)(2,1)S(1)}, u32[]{:S(2)}, u32[]{:S(2)}) %collective-permute-start.36) | collective-permute-done | bytes 524320 | tf_op jit(solution)/shard_map/ppermute | solution.py:345
  234.9 3.7 %collective-permute-start.37 = (bf16[4,32,2048]{2,1,0:T(8,128)(2,1)S(1)}, bf16[4,32,2048]{2,1,0:T(8,128)(2,1)S(1)}, u32[]{:S(2)}, u32[]{:S(2)}) collective-permute-start(bf16[4,32,2048]{2,1,0:T(8,128)(2,1)S(1)} %pad_maximum_fusion.1.refs_0_), channel_id=1, source_target_pairs={{0,4},{2,6},{4,0},{6,2},{8,12},{10,14},{12,8},{14,10},{16,20},{18,... | collective-permute-start | bytes 1572872 | tf_op jit(solution)/shard_map/ppermute | solution.py:345
  238.6 2.2 copy-done
  240.8 1.9 project.3.refs_3_
  242.7 2.8 %collective-permute-done.39.refs_1_ = bf16[4,32,2048]{2,1,0:T(8,128)(2,1)} collective-permute-done((bf16[4,32,2048]{2,1,0:T(8,128)(2,1)S(1)}, bf16[4,32,2048]{2,1,0:T(8,128)(2,1)}, u32[]{:S(2)}, u32[]{:S(2)}) %collective-permute-start.39) | collective-permute-done | bytes 524320 | tf_op jit(solution)/shard_map/ppermute | solution.py:345
  245.5 2.4 project.4.refs_3_
  247.9 4.5 %collective-permute-done.37.refs_0_ = bf16[4,32,2048]{2,1,0:T(8,128)(2,1)S(1)} collective-permute-done((bf16[4,32,2048]{2,1,0:T(8,128)(2,1)S(1)}, bf16[4,32,2048]{2,1,0:T(8,128)(2,1)S(1)}, u32[]{:S(2)}, u32[]{:S(2)}) %collective-permute-start.37) | collective-permute-done | bytes 524320 | tf_op jit(solution)/shard_map/ppermute | solution.py:345
  252.4 2.4 project.5
  254.9 1.5 collective-permute-done.40
  256.4 0.8 add_convert_fusion
  (68 shorter events, 4.8 us)
Async XLA Ops:
  0.9 8.9 %collective-permute-start = (bf16[32,1024]{1,0:T(8,128)(2,1)S(1)}, bf16[32,1024]{1,0:T(8,128)(2,1)S(1)}, u32[]{:S(2)}, u32[]{:S(2)}) collective-permute-start(bf16[32,1024]{1,0:T(8,128)(2,1)S(1)} %get-tuple-element.70), channel_id=1, source_target_pairs={{0,8},{2,10},{4,12},{6,14},{8,0},{10,2},{12,4},{14,6},{16,24},{18,... | collective-permute-start | bytes 196616 | tf_op jit(solution)/shard_map/ppermute | solution.py:345
  3.9 7.3 %collective-permute-start.1 = (bf16[32,1024]{1,0:T(8,128)(2,1)S(1)}, bf16[32,1024]{1,0:T(8,128)(2,1)S(1)}, u32[]{:S(2)}, u32[]{:S(2)}) collective-permute-start(bf16[32,1024]{1,0:T(8,128)(2,1)S(1)} %get-tuple-element.70), channel_id=1, source_target_pairs={{0,16},{2,18},{4,20},{6,22},{8,24},{10,26},{12,28},{14,30},{16,0},... | collective-permute-start | bytes 196616 | tf_op jit(solution)/shard_map/ppermute | solution.py:345
  6.5 6.1 %collective-permute-start.2 = (bf16[32,1024]{1,0:T(8,128)(2,1)S(1)}, bf16[32,1024]{1,0:T(8,128)(2,1)S(1)}, u32[]{:S(2)}, u32[]{:S(2)}) collective-permute-start(bf16[32,1024]{1,0:T(8,128)(2,1)S(1)} %get-tuple-element.70), channel_id=1, source_target_pairs={{0,24},{2,26},{4,28},{6,30},{8,16},{10,18},{12,20},{14,22},{16,8},... | collective-permute-start | bytes 196616 | tf_op jit(solution)/shard_map/ppermute | solution.py:345
  12.6 15.3 %collective-permute-start.6 = (bf16[32,3072]{1,0:T(8,128)(2,1)S(1)}, bf16[32,3072]{1,0:T(8,128)(2,1)S(1)}, u32[]{:S(2)}, u32[]{:S(2)}) collective-permute-start(bf16[32,3072]{1,0:T(8,128)(2,1)S(1)} %slice.7), channel_id=1, source_target_pairs={{0,8},{2,10},{4,12},{6,14},{8,0},{10,2},{12,4},{14,6},{16,24},{18,... | collective-permute-start | bytes 589832 | tf_op jit(solution)/shard_map/ppermute | solution.py:345
  12.7 16.9 %collective-permute-start.7 = (bf16[32,3072]{1,0:T(8,128)(2,1)S(1)}, bf16[32,3072]{1,0:T(8,128)(2,1)S(1)}, u32[]{:S(2)}, u32[]{:S(2)}) collective-permute-start(bf16[32,3072]{1,0:T(8,128)(2,1)S(1)} %slice.7), channel_id=1, source_target_pairs={{0,16},{2,18},{4,20},{6,22},{8,24},{10,26},{12,28},{14,30},{16,0},... | collective-permute-start | bytes 589832 | tf_op jit(solution)/shard_map/ppermute | solution.py:345
  15.1 14.5 %collective-permute-start.8 = (bf16[32,3072]{1,0:T(8,128)(2,1)S(1)}, bf16[32,3072]{1,0:T(8,128)(2,1)S(1)}, u32[]{:S(2)}, u32[]{:S(2)}) collective-permute-start(bf16[32,3072]{1,0:T(8,128)(2,1)S(1)} %slice.7), channel_id=1, source_target_pairs={{0,24},{2,26},{4,28},{6,30},{8,16},{10,18},{12,20},{14,22},{16,8},... | collective-permute-start | bytes 589832 | tf_op jit(solution)/shard_map/ppermute | solution.py:345
  18.5 19.6 %copy-start.6 = (bf16[32,512]{1,0:T(8,128)(2,1)S(1)}, bf16[32,512]{1,0:T(8,128)(2,1)}, u32[]{:S(2)}) copy-start(bf16[32,512]{1,0:T(8,128)(2,1)} %refs_3_.1) | copy-start | bytes 98308
  18.5 19.6 %copy-start.7 = (bf16[32,512]{1,0:T(8,128)(2,1)S(1)}, bf16[32,512]{1,0:T(8,128)(2,1)}, u32[]{:S(2)}) copy-start(bf16[32,512]{1,0:T(8,128)(2,1)} %refs_4_.4) | copy-start | bytes 98308
  18.5 14.3 %collective-permute-start.3 = (bf16[4,32,1024]{2,1,0:T(8,128)(2,1)S(1)}, bf16[4,32,1024]{2,1,0:T(8,128)(2,1)S(1)}, u32[]{:S(2)}, u32[]{:S(2)}) collective-permute-start(bf16[4,32,1024]{2,1,0:T(8,128)(2,1)S(1)} %pad_maximum_fusion.2.refs_0_), channel_id=1, source_target_pairs={{0,2},{2,0},{4,6},{6,4},{8,10},{10,8},{12,14},{14,12},{16,18},{18,... | collective-permute-start | bytes 786440 | tf_op jit(solution)/shard_map/ppermute | solution.py:345
  20.0 13.2 %collective-permute-start.4 = (bf16[4,32,1024]{2,1,0:T(8,128)(2,1)S(1)}, bf16[4,32,1024]{2,1,0:T(8,128)(2,1)S(1)}, u32[]{:S(2)}, u32[]{:S(2)}) collective-permute-start(bf16[4,32,1024]{2,1,0:T(8,128)(2,1)S(1)} %pad_maximum_fusion.2.refs_0_), channel_id=1, source_target_pairs={{0,4},{2,6},{4,0},{6,2},{8,12},{10,14},{12,8},{14,10},{16,20},{18,... | collective-permute-start | bytes 786440 | tf_op jit(solution)/shard_map/ppermute | solution.py:345
  27.9 10.1 %collective-permute-start.5 = (bf16[4,32,1024]{2,1,0:T(8,128)(2,1)S(1)}, bf16[4,32,1024]{2,1,0:T(8,128)(2,1)S(1)}, u32[]{:S(2)}, u32[]{:S(2)}) collective-permute-start(bf16[4,32,1024]{2,1,0:T(8,128)(2,1)S(1)} %pad_maximum_fusion.2.refs_0_), channel_id=1, source_target_pairs={{0,6},{2,4},{4,2},{6,0},{8,14},{10,12},{12,10},{14,8},{16,22},{18,... | collective-permute-start | bytes 786440 | tf_op jit(solution)/shard_map/ppermute | solution.py:345
  29.7 45.6 %collective-permute-start.12 = (bf16[4,32,3072]{2,1,0:T(8,128)(2,1)S(1)}, bf16[4,32,3072]{2,1,0:T(8,128)(2,1)S(1)}, u32[]{:S(2)}, u32[]{:S(2)}) collective-permute-start(bf16[4,32,3072]{2,1,0:T(8,128)(2,1)S(1)} %pad_maximum_fusion.refs_8_.refs_0_), channel_id=1, source_target_pairs={{0,2},{2,0},{4,6},{6,4},{8,10},{10,8},{12,14},{14,12},{16,18},{18,... | collective-permute-start | bytes 2359304 | tf_op jit(solution)/shard_map/ppermute | solution.py:345
  31.3 44.1 %collective-permute-start.13 = (bf16[4,32,3072]{2,1,0:T(8,128)(2,1)S(1)}, bf16[4,32,3072]{2,1,0:T(8,128)(2,1)S(1)}, u32[]{:S(2)}, u32[]{:S(2)}) collective-permute-start(bf16[4,32,3072]{2,1,0:T(8,128)(2,1)S(1)} %pad_maximum_fusion.refs_8_.refs_0_), channel_id=1, source_target_pairs={{0,4},{2,6},{4,0},{6,2},{8,12},{10,14},{12,8},{14,10},{16,20},{18,... | collective-permute-start | bytes 2359304 | tf_op jit(solution)/shard_map/ppermute | solution.py:345
  32.8 42.5 %collective-permute-start.14 = (bf16[4,32,3072]{2,1,0:T(8,128)(2,1)S(1)}, bf16[4,32,3072]{2,1,0:T(8,128)(2,1)S(1)}, u32[]{:S(2)}, u32[]{:S(2)}) collective-permute-start(bf16[4,32,3072]{2,1,0:T(8,128)(2,1)S(1)} %pad_maximum_fusion.refs_8_.refs_0_), channel_id=1, source_target_pairs={{0,6},{2,4},{4,2},{6,0},{8,14},{10,12},{12,10},{14,8},{16,22},{18,... | collective-permute-start | bytes 2359304 | tf_op jit(solution)/shard_map/ppermute | solution.py:345
  38.1 2.2 copy-start.2
  40.3 2.2 copy-start.4
  42.5 32.9 %copy-start.3 = (bf16[4096,512]{0,1:T(8,128)(2,1)S(1)}, bf16[4096,512]{0,1:T(8,128)(2,1)}, u32[]{:S(2)}) copy-start(bf16[4096,512]{0,1:T(8,128)(2,1)} %copy.9) | copy-start | bytes 12582916
  42.5 32.9 %copy-start.5 = (bf16[4096,512]{1,0:T(8,128)(2,1)S(1)}, bf16[4096,512]{1,0:T(8,128)(2,1)}, u32[]{:S(2)}) copy-start(bf16[4096,512]{1,0:T(8,128)(2,1)} %refs_2_.3) | copy-start | bytes 12582916
  66.9 41.7 %collective-permute-start.10 = (bf16[4,32,1152]{2,1,0:T(8,128)(2,1)S(1)}, bf16[4,32,1152]{2,1,0:T(8,128)(2,1)S(1)}, u32[]{:S(2)}, u32[]{:S(2)}) collective-permute-start(bf16[4,32,1152]{2,1,0:T(8,128)(2,1)S(1)} %get-tuple-element.42), channel_id=1, source_target_pairs={{0,4},{2,6},{4,0},{6,2},{8,12},{10,14},{12,8},{14,10},{16,20},{18,... | collective-permute-start | bytes 884744 | tf_op jit(solution)/shard_map/ppermute | solution.py:345
  73.8 60.8 %collective-permute-start.11 = (bf16[4,32,1152]{2,1,0:T(8,128)(2,1)S(1)}, bf16[4,32,1152]{2,1,0:T(8,128)(2,1)S(1)}, u32[]{:S(2)}, u32[]{:S(2)}) collective-permute-start(bf16[4,32,1152]{2,1,0:T(8,128)(2,1)S(1)} %get-tuple-element.43), channel_id=1, source_target_pairs={{0,6},{2,4},{4,2},{6,0},{8,14},{10,12},{12,10},{14,8},{16,22},{18,... | collective-permute-start | bytes 884744 | tf_op jit(solution)/shard_map/ppermute | solution.py:345
  75.3 59.3 %collective-permute-start.9 = (bf16[4,32,1152]{2,1,0:T(8,128)(2,1)S(1)}, bf16[4,32,1152]{2,1,0:T(8,128)(2,1)S(1)}, u32[]{:S(2)}, u32[]{:S(2)}) collective-permute-start(bf16[4,32,1152]{2,1,0:T(8,128)(2,1)S(1)} %get-tuple-element.41), channel_id=1, source_target_pairs={{0,2},{2,0},{4,6},{6,4},{8,10},{10,8},{12,14},{14,12},{16,18},{18,... | collective-permute-start | bytes 884744 | tf_op jit(solution)/shard_map/ppermute | solution.py:345
  100.2 34.4 %collective-permute-start.15 = (bf16[4,32,1152]{2,1,0:T(8,128)(2,1)S(1)}, bf16[4,32,1152]{2,1,0:T(8,128)(2,1)S(1)}, u32[]{:S(2)}, u32[]{:S(2)}) collective-permute-start(bf16[4,32,1152]{2,1,0:T(8,128)(2,1)S(1)} %get-tuple-element.45), channel_id=1, source_target_pairs={{0,2},{2,0},{4,6},{6,4},{8,10},{10,8},{12,14},{14,12},{16,18},{18,... | collective-permute-start | bytes 884744 | tf_op jit(solution)/shard_map/ppermute | solution.py:345
  108.5 26.0 %collective-permute-start.16 = (bf16[4,32,1152]{2,1,0:T(8,128)(2,1)S(1)}, bf16[4,32,1152]{2,1,0:T(8,128)(2,1)S(1)}, u32[]{:S(2)}, u32[]{:S(2)}) collective-permute-start(bf16[4,32,1152]{2,1,0:T(8,128)(2,1)S(1)} %get-tuple-element.46), channel_id=1, source_target_pairs={{0,4},{2,6},{4,0},{6,2},{8,12},{10,14},{12,8},{14,10},{16,20},{18,... | collective-permute-start | bytes 884744 | tf_op jit(solution)/shard_map/ppermute | solution.py:345
  108.6 26.0 %collective-permute-start.17 = (bf16[4,32,1152]{2,1,0:T(8,128)(2,1)S(1)}, bf16[4,32,1152]{2,1,0:T(8,128)(2,1)S(1)}, u32[]{:S(2)}, u32[]{:S(2)}) collective-permute-start(bf16[4,32,1152]{2,1,0:T(8,128)(2,1)S(1)} %get-tuple-element.47), channel_id=1, source_target_pairs={{0,6},{2,4},{4,2},{6,0},{8,14},{10,12},{12,10},{14,8},{16,22},{18,... | collective-permute-start | bytes 884744 | tf_op jit(solution)/shard_map/ppermute | solution.py:345
  136.2 12.1 %collective-permute-start.18 = (bf16[32,2304]{1,0:T(8,128)(2,1)S(1)}, bf16[32,2304]{1,0:T(8,128)(2,1)S(1)}, u32[]{:S(2)}, u32[]{:S(2)}) collective-permute-start(bf16[32,2304]{1,0:T(8,128)(2,1)S(1)} %get-tuple-element.50), channel_id=1, source_target_pairs={{0,8},{2,10},{4,12},{6,14},{8,0},{10,2},{12,4},{14,6},{16,24},{18,... | collective-permute-start | bytes 442376 | tf_op jit(solution)/shard_map/ppermute | solution.py:345
  136.3 42.4 %collective-permute-start.22 = (bf16[4,32,1152]{2,1,0:T(8,128)(2,1)S(1)}, bf16[4,32,1152]{2,1,0:T(8,128)(2,1)S(1)}, u32[]{:S(2)}, u32[]{:S(2)}) collective-permute-start(bf16[4,32,1152]{2,1,0:T(8,128)(2,1)S(1)} %get-tuple-element.54), channel_id=1, source_target_pairs={{0,2},{2,0},{4,6},{6,4},{8,10},{10,8},{12,14},{14,12},{16,18},{18,... | collective-permute-start | bytes 884744 | tf_op jit(solution)/shard_map/ppermute | solution.py:345
  144.6 35.6 %collective-permute-start.23 = (bf16[4,32,1152]{2,1,0:T(8,128)(2,1)S(1)}, bf16[4,32,1152]{2,1,0:T(8,128)(2,1)S(1)}, u32[]{:S(2)}, u32[]{:S(2)}) collective-permute-start(bf16[4,32,1152]{2,1,0:T(8,128)(2,1)S(1)} %get-tuple-element.55), channel_id=1, source_target_pairs={{0,4},{2,6},{4,0},{6,2},{8,12},{10,14},{12,8},{14,10},{16,20},{18,... | collective-permute-start | bytes 884744 | tf_op jit(solution)/shard_map/ppermute | solution.py:345
  144.9 35.3 %collective-permute-start.24 = (bf16[4,32,1152]{2,1,0:T(8,128)(2,1)S(1)}, bf16[4,32,1152]{2,1,0:T(8,128)(2,1)S(1)}, u32[]{:S(2)}, u32[]{:S(2)}) collective-permute-start(bf16[4,32,1152]{2,1,0:T(8,128)(2,1)S(1)} %get-tuple-element.56), channel_id=1, source_target_pairs={{0,6},{2,4},{4,2},{6,0},{8,14},{10,12},{12,10},{14,8},{16,22},{18,... | collective-permute-start | bytes 884744 | tf_op jit(solution)/shard_map/ppermute | solution.py:345
  146.2 23.4 %collective-permute-start.19 = (bf16[32,2304]{1,0:T(8,128)(2,1)S(1)}, bf16[32,2304]{1,0:T(8,128)(2,1)S(1)}, u32[]{:S(2)}, u32[]{:S(2)}) collective-permute-start(bf16[32,2304]{1,0:T(8,128)(2,1)S(1)} %get-tuple-element.51), channel_id=1, source_target_pairs={{0,16},{2,18},{4,20},{6,22},{8,24},{10,26},{12,28},{14,30},{16,0},... | collective-permute-start | bytes 442376 | tf_op jit(solution)/shard_map/ppermute | solution.py:345
  148.3 28.0 %collective-permute-start.20 = (bf16[32,2304]{1,0:T(8,128)(2,1)S(1)}, bf16[32,2304]{1,0:T(8,128)(2,1)S(1)}, u32[]{:S(2)}, u32[]{:S(2)}) collective-permute-start(bf16[32,2304]{1,0:T(8,128)(2,1)S(1)} %get-tuple-element.52), channel_id=1, source_target_pairs={{0,24},{2,26},{4,28},{6,30},{8,16},{10,18},{12,20},{14,22},{16,8},... | collective-permute-start | bytes 442376 | tf_op jit(solution)/shard_map/ppermute | solution.py:345
  169.6 18.1 %collective-permute-start.25 = (bf16[4,32,1152]{2,1,0:T(8,128)(2,1)S(1)}, bf16[4,32,1152]{2,1,0:T(8,128)(2,1)S(1)}, u32[]{:S(2)}, u32[]{:S(2)}) collective-permute-start(bf16[4,32,1152]{2,1,0:T(8,128)(2,1)S(1)} %get-tuple-element.53.refs_4_), channel_id=1, source_target_pairs={{0,2},{2,0},{4,6},{6,4},{8,10},{10,8},{12,14},{14,12},{16,18},{18,... | collective-permute-start | bytes 884744 | tf_op jit(solution)/shard_map/ppermute | solution.py:345
  176.3 11.4 %collective-permute-start.26 = (bf16[4,32,1152]{2,1,0:T(8,128)(2,1)S(1)}, bf16[4,32,1152]{2,1,0:T(8,128)(2,1)S(1)}, u32[]{:S(2)}, u32[]{:S(2)}) collective-permute-start(bf16[4,32,1152]{2,1,0:T(8,128)(2,1)S(1)} %get-tuple-element.57), channel_id=1, source_target_pairs={{0,4},{2,6},{4,0},{6,2},{8,12},{10,14},{12,8},{14,10},{16,20},{18,... | collective-permute-start | bytes 884744 | tf_op jit(solution)/shard_map/ppermute | solution.py:345
  178.7 9.0 %collective-permute-start.27 = (bf16[4,32,1152]{2,1,0:T(8,128)(2,1)S(1)}, bf16[4,32,1152]{2,1,0:T(8,128)(2,1)S(1)}, u32[]{:S(2)}, u32[]{:S(2)}) collective-permute-start(bf16[4,32,1152]{2,1,0:T(8,128)(2,1)S(1)} %get-tuple-element.58), channel_id=1, source_target_pairs={{0,6},{2,4},{4,2},{6,0},{8,14},{10,12},{12,10},{14,8},{16,22},{18,... | collective-permute-start | bytes 884744 | tf_op jit(solution)/shard_map/ppermute | solution.py:345
  180.2 7.5 %collective-permute-start.21 = (bf16[1,32,2048]{2,1,0:T(8,128)(2,1)S(1)}, bf16[1,32,2048]{2,1,0:T(8,128)(2,1)S(1)}, u32[]{:S(2)}, u32[]{:S(2)}) collective-permute-start(bf16[1,32,2048]{2,1,0:T(8,128)(2,1)S(1)} %bitcast.25), channel_id=1, source_target_pairs={{0,16},{2,18},{4,20},{6,22},{8,24},{10,26},{12,28},{14,30},{16,0},... | collective-permute-start | bytes 393224 | tf_op jit(solution)/shard_map/ppermute | solution.py:345
  189.4 8.1 %collective-permute-start.28 = (bf16[2,32,2048]{2,1,0:T(8,128)(2,1)S(1)}, bf16[2,32,2048]{2,1,0:T(8,128)(2,1)S(1)}, u32[]{:S(2)}, u32[]{:S(2)}) collective-permute-start(bf16[2,32,2048]{2,1,0:T(8,128)(2,1)S(1)} %pad_maximum_fusion.3.refs_9_), channel_id=1, source_target_pairs={{0,8},{2,10},{4,12},{6,14},{8,0},{10,2},{12,4},{14,6},{16,24},{18,... | collective-permute-start | bytes 786440 | tf_op jit(solution)/shard_map/ppermute | solution.py:345
  189.5 10.2 %collective-permute-start.29 = (bf16[32,2304]{1,0:T(8,128)(2,1)S(1)}, bf16[32,2304]{1,0:T(8,128)(2,1)S(1)}, u32[]{:S(2)}, u32[]{:S(2)}) collective-permute-start(bf16[32,2304]{1,0:T(8,128)(2,1)S(1)} %get-tuple-element.61), channel_id=1, source_target_pairs={{0,8},{2,10},{4,12},{6,14},{8,0},{10,2},{12,4},{14,6},{16,24},{18,... | collective-permute-start | bytes 442376 | tf_op jit(solution)/shard_map/ppermute | solution.py:345
  191.5 11.4 %collective-permute-start.30 = (bf16[32,2304]{1,0:T(8,128)(2,1)S(1)}, bf16[32,2304]{1,0:T(8,128)(2,1)S(1)}, u32[]{:S(2)}, u32[]{:S(2)}) collective-permute-start(bf16[32,2304]{1,0:T(8,128)(2,1)S(1)} %get-tuple-element.62), channel_id=1, source_target_pairs={{0,16},{2,18},{4,20},{6,22},{8,24},{10,26},{12,28},{14,30},{16,0},... | collective-permute-start | bytes 442376 | tf_op jit(solution)/shard_map/ppermute | solution.py:345
  192.2 10.7 %collective-permute-start.31 = (bf16[32,2304]{1,0:T(8,128)(2,1)S(1)}, bf16[32,2304]{1,0:T(8,128)(2,1)S(1)}, u32[]{:S(2)}, u32[]{:S(2)}) collective-permute-start(bf16[32,2304]{1,0:T(8,128)(2,1)S(1)} %get-tuple-element.63), channel_id=1, source_target_pairs={{0,24},{2,26},{4,28},{6,30},{8,16},{10,18},{12,20},{14,22},{16,8},... | collective-permute-start | bytes 442376 | tf_op jit(solution)/shard_map/ppermute | solution.py:345
  203.5 6.6 %collective-permute-start.32 = (bf16[1,32,2048]{2,1,0:T(8,128)(2,1)S(1)}, bf16[1,32,2048]{2,1,0:T(8,128)(2,1)S(1)}, u32[]{:S(2)}, u32[]{:S(2)}) collective-permute-start(bf16[1,32,2048]{2,1,0:T(8,128)(2,1)S(1)} %bitcast.27), channel_id=1, source_target_pairs={{0,16},{2,18},{4,20},{6,22},{8,24},{10,26},{12,28},{14,30},{16,0},... | collective-permute-start | bytes 393224 | tf_op jit(solution)/shard_map/ppermute | solution.py:345
  210.1 13.2 %collective-permute-start.34 = (bf16[4,32,2048]{2,1,0:T(8,128)(2,1)S(1)}, bf16[4,32,2048]{2,1,0:T(8,128)(2,1)S(1)}, u32[]{:S(2)}, u32[]{:S(2)}) collective-permute-start(bf16[4,32,2048]{2,1,0:T(8,128)(2,1)S(1)} %constant_dynamic-update-slice_fusion.refs_5_.refs_0_), channel_id=1, source_target_pairs={{0,2},{2,0},{4,6},{6,4},{8,10},{10,8},{12,14},{14,12},{16,18},{18,... | collective-permute-start | bytes 1572872 | tf_op jit(solution)/shard_map/ppermute | solution.py:345
  212.3 17.4 %collective-permute-start.35 = (bf16[4,32,2048]{2,1,0:T(8,128)(2,1)S(1)}, bf16[4,32,2048]{2,1,0:T(8,128)(2,1)S(1)}, u32[]{:S(2)}, u32[]{:S(2)}) collective-permute-start(bf16[4,32,2048]{2,1,0:T(8,128)(2,1)S(1)} %constant_dynamic-update-slice_fusion.refs_5_.refs_0_), channel_id=1, source_target_pairs={{0,4},{2,6},{4,0},{6,2},{8,12},{10,14},{12,8},{14,10},{16,20},{18,... | collective-permute-start | bytes 1572872 | tf_op jit(solution)/shard_map/ppermute | solution.py:345
  213.9 20.7 %collective-permute-start.36 = (bf16[4,32,2048]{2,1,0:T(8,128)(2,1)S(1)}, bf16[4,32,2048]{2,1,0:T(8,128)(2,1)S(1)}, u32[]{:S(2)}, u32[]{:S(2)}) collective-permute-start(bf16[4,32,2048]{2,1,0:T(8,128)(2,1)S(1)} %constant_dynamic-update-slice_fusion.refs_5_.refs_0_), channel_id=1, source_target_pairs={{0,6},{2,4},{4,2},{6,0},{8,14},{10,12},{12,10},{14,8},{16,22},{18,... | collective-permute-start | bytes 1572872 | tf_op jit(solution)/shard_map/ppermute | solution.py:345
  215.3 6.4 %collective-permute-start.33 = (bf16[2,32,2048]{2,1,0:T(8,128)(2,1)S(1)}, bf16[2,32,2048]{2,1,0:T(8,128)(2,1)S(1)}, u32[]{:S(2)}, u32[]{:S(2)}) collective-permute-start(bf16[2,32,2048]{2,1,0:T(8,128)(2,1)S(1)} %pad_maximum_fusion.4), channel_id=1, source_target_pairs={{0,8},{2,10},{4,12},{6,14},{8,0},{10,2},{12,4},{14,6},{16,24},{18,... | collective-permute-start | bytes 786440 | tf_op jit(solution)/shard_map/ppermute | solution.py:345
  234.6 10.9 %collective-permute-start.39 = (bf16[4,32,2048]{2,1,0:T(8,128)(2,1)S(1)}, bf16[4,32,2048]{2,1,0:T(8,128)(2,1)}, u32[]{:S(2)}, u32[]{:S(2)}) collective-permute-start(bf16[4,32,2048]{2,1,0:T(8,128)(2,1)S(1)} %pad_maximum_fusion.1.refs_0_), channel_id=1, source_target_pairs={{0,2},{2,0},{4,6},{6,4},{8,10},{10,8},{12,14},{14,12},{16,18},{18,... | collective-permute-start | bytes 1572872 | tf_op jit(solution)/shard_map/ppermute | solution.py:345
  234.9 17.5 %collective-permute-start.37 = (bf16[4,32,2048]{2,1,0:T(8,128)(2,1)S(1)}, bf16[4,32,2048]{2,1,0:T(8,128)(2,1)S(1)}, u32[]{:S(2)}, u32[]{:S(2)}) collective-permute-start(bf16[4,32,2048]{2,1,0:T(8,128)(2,1)S(1)} %pad_maximum_fusion.1.refs_0_), channel_id=1, source_target_pairs={{0,4},{2,6},{4,0},{6,2},{8,12},{10,14},{12,8},{14,10},{16,20},{18,... | collective-permute-start | bytes 1572872 | tf_op jit(solution)/shard_map/ppermute | solution.py:345
  238.6 13.8 %collective-permute-start.38 = (bf16[4,32,2048]{2,1,0:T(8,128)(2,1)S(1)}, bf16[4,32,2048]{2,1,0:T(8,128)(2,1)}, u32[]{:S(2)}, u32[]{:S(2)}) collective-permute-start(bf16[4,32,2048]{2,1,0:T(8,128)(2,1)S(1)} %pad_maximum_fusion.1.refs_0_), channel_id=1, source_target_pairs={{0,6},{2,4},{4,2},{6,0},{8,14},{10,12},{12,10},{14,8},{16,22},{18,... | collective-permute-start | bytes 1572872 | tf_op jit(solution)/shard_map/ppermute | solution.py:345
  238.6 2.2 copy-start
  240.8 4.7 %copy-start.1 = (bf16[4096,512]{1,0:T(8,128)(2,1)S(1)}, bf16[4096,512]{1,0:T(8,128)(2,1)}, u32[]{:S(2)}) copy-start(bf16[4096,512]{1,0:T(8,128)(2,1)} %refs_2_.5) | copy-start | bytes 12582916
  254.8 1.6 collective-permute-start.40

commit v8 on v7

--- a/solution.py
+++ b/solution.py
@@ -168,7 +168,7 @@
     plane, count = len(q_pieces), len(chosen)
     cols = GROUP_QUERIES * HEAD_SIZE
     key_count = values.shape[0]
-    group_step = min(GROUP_QUERIES, 4 * (plane // count))
+    group_step = min(GROUP_QUERIES, 2 * (plane // count))
     tile_rows = group_step * count * rows
     key_chunk = min(key_count, 512)
     vmem = pltpu.MemorySpace.VMEM
@@ -190,7 +190,7 @@
             grid=(1,),
             in_specs=[pl.BlockSpec((blocks, rows, cols), lambda i, s: (0, 0, q_head))] * count
             + [
-                pl.BlockSpec((HEAD_SIZE, key_count), lambda i, s: (head, 0)),
+                pl.BlockSpec((HEAD_SIZE, key_count), lambda i, s: (0, 0)),
                 pl.BlockSpec((key_count, HEAD_SIZE), lambda i, s: (0, head)),
                 span_block,
                 span_block,
@@ -365,9 +365,6 @@
         ]
     )
 
-    def stack_blocks(x):
-        return jnp.stack([x] + [exchange(x, "ctx", a * plane) for a in range(1, blocks)])
-
     def doubled(column):
         stack, order, distance = column
         if not distance:
@@ -375,13 +372,20 @@
         stack = jnp.concatenate([stack, exchange(stack, "ctx", distance * plane)])
         return stack, order + [a ^ distance for a in order], distance // 2
 
+    def stack_blocks(x):
+        return jnp.stack([x] + [exchange(x, "ctx", a * plane) for a in range(1, blocks)])
+
     def gather_plane(stack):
         return [stack] + [exchange(stack, "ctx", b) for b in range(1, plane)]
 
     first = stack_blocks(queries[:, :width])
     sources, stacks = [(gather_plane(first), 0)], []
-    keys, _ = lax.optimization_barrier((context_keys, first))
-    keys_t = keys.T
+    keys_t = []
+    for h in range(heads):
+        keys, _ = lax.optimization_barrier(
+            (context_keys[:, h * HEAD_SIZE : (h + 1) * HEAD_SIZE], sources[0][0][1] if h else info)
+        )
+        keys_t.append(keys.T)
     if heads > 1:
         held, _ = lax.optimization_barrier((queries[:, width:], first))
         stacks = [stack_blocks(held)]
@@ -413,7 +417,7 @@
     def attend(h, chosen, after):
         pieces, q_head = sources[h]
         return attend_head(
-            info, pieces, chosen, q_head, keys_t, context_values, span_keys, span_values, h, after
+            info, pieces, chosen, q_head, keys_t[h], context_values, span_keys, span_values, h, after
         )
 
     latest = stacks
@@ -434,15 +438,22 @@
     def gather_round():
         columns.extend((x[None], [0], blocks // 2) for x in rows_of[len(columns) :])
         if len(merged) == heads // size and columns:
-            held, _ = lax.optimization_barrier(([column[0] for column in columns], merged[-1][0]))
+            held, *_ = lax.optimization_barrier(
+                ([column[0] for column in columns], attended[-1][0], receive(heads - 1))
+            )
             columns[:] = [(x, *column[1:]) for x, column in zip(held, columns)]
         columns[:] = [doubled(column) for column in columns]
         return [column[0] for column in columns]
 
     while len(merged) < heads // size:
         latest = merge(latest + gather_round())
+    gathered = []
     while len(rows_of) < heads // size:
-        latest = normalize(latest + gather_round())
+        after = gather_round()
+        if columns and not columns[0][2]:
+            gathered = [gather_plane(after[0])]
+            after = [gathered[0][b] for b in (1, 2) if b < plane]
+        latest = normalize(latest + after)
     while any(distance for _, _, distance in columns) or len(columns) < len(rows_of):
         gather_round()
 
@@ -450,7 +461,7 @@
     for g, (stack, order, _) in enumerate(columns):
         if g:
             stack, _ = lax.optimization_barrier((stack, pieces))
-        pieces = gather_plane(stack)
+        pieces = gathered.pop() if gathered else gather_plane(stack)
         if g < len(rows_of) - 1:
             total = [project(info, pieces, order, range(plane), out_weight, g, total, F32)]
         else:

time: 257 us -> 244 us (0.949)
  starting transfers between devices: 77.7 us -> 65.4 us
  Pallas kernels: 110 us -> 98.2 us
  local copies, waits for them, and re-layouts: 16.2 us -> 22.2 us
  waiting for transfers between devices: 49.3 us -> 52.2 us
    pallas_call x5, Pallas kernels: 99.2 us -> 86.3 us  [attend_head(): pl.pallas_call(functools.partial(attend_kernel, chosen=chosen, blocks=blo...]
    ppermute x41, starting transfers between devices: 77.7 us -> 65.4 us  [exchange(): return lax.ppermute(x, axis, [(i, i ^ distance) for i in range(count)])]
    unnamed x17 -> x51, local copies, waits for them, and re-layouts: 6.6 us -> 10.5 us
    slice x0 -> x1, local copies, waits for them, and re-layouts: none -> 3.85 us  [local(): context_keys[:, h * HEAD_SIZE:(h + 1) * HEAD_SIZE]]
    ppermute x41, waiting for transfers between devices: 49.3 us -> 52.2 us  [exchange(): return lax.ppermute(x, axis, [(i, i ^ distance) for i in range(count)])]
    optimization_barrier x1 -> x4, local copies, waits for them, and re-layouts: 6.38 us -> 4.03 us  [local(): lax.optimization_barrier((context_keys[:, h * HEAD_SIZE:(h + 1) * HEAD_SI...]
  transfers between devices with their start and end apart: 41 -> 41, of which waited for: 16 -> 14; matrix products, arithmetic and copies ran while one was open for 4% -> 6% of each run, Pallas kernels for 40% -> 38%
where the time goes in v8:
time: 244 us; the launch traced here: 243 us
  Pallas kernels  98.2 us (40%)
  starting transfers between devices  65.4 us (27%)
  waiting for transfers between devices  52.2 us (21%)
  local copies, waits for them, and re-layouts  22.2 us (9%)
  other arithmetic  4.72 us (2%)
    pallas_call x5, Pallas kernels, attend_head(): pl.pallas_call(functools.partial(attend_kernel, chosen=chosen, blocks=blo...  86.3 us
    ppermute x41, starting transfers between devices, exchange(): return lax.ppermute(x, axis, [(i, i ^ distance) for i in range(count)])  65.4 us
    ppermute x41, waiting for transfers between devices, exchange(): return lax.ppermute(x, axis, [(i, i ^ distance) for i in range(count)])  52.2 us
    unnamed x51, local copies, waits for them, and re-layouts  10.5 us
    pallas_call x3, Pallas kernels, project(): pl.pallas_call(functools.partial(project_kernel, order=order, chosen=chos...  6.6 us
  transfers between devices with their start and end apart: 41, of which 14 were waited for; matrix products, arithmetic and copies ran while one was open for 6% of the time, Pallas kernels for 38%

profile of v8, /device:TPU:0, one launch (start us, length us, event | category | flops | bytes accessed | tf_op | source)
XLA Modules:
  0.0 243.3 jit_solution(1877030342970159691)
XLA Ops:
  0.0 0.8 slice_bitcast_fusion
  0.9 5.1 %collective-permute-start.2 = (bf16[32,1024]{1,0:T(8,128)(2,1)S(1)}, bf16[32,1024]{1,0:T(8,128)(2,1)S(1)}, u32[]{:S(2)}, u32[]{:S(2)}) collective-permute-start(bf16[32,1024]{1,0:T(8,128)(2,1)S(1)} %get-tuple-element.76), channel_id=1, source_target_pairs={{0,24},{2,26},{4,28},{6,30},{8,16},{10,18},{12,20},{14,22},{16,8},... | collective-permute-start | bytes 196616 | tf_op jit(solution)/shard_map/ppermute | solution.py:345
  6.6 1.6 slice.20
  8.3 3.8 %fusion.1 = (bf16[4096,128]{1,0:T(8,128)(2,1)}, bf16[4096,128]{1,0:T(8,128)(2,1)}, bf16[4096,128]{1,0:T(8,128)(2,1)S(1)}, bf16[4096,128]{1,0:T(8,128)(2,1)S(1)}) fusion(bf16[4096,512]{1,0:T(8,128)(2,1)} %param.10), kind=kLoop, calls=%fused_computation.17 | loop fusion | bytes 8388608 | tf_op jit(solution)/shard_map/slice | solution.py:386
  13.4 0.8 sort.17
  14.9 0.9 pad_maximum_fusion.2.refs_0_
  15.9 3.8 %collective-permute-start.8 = (bf16[32,3072]{1,0:T(8,128)(2,1)}, bf16[32,3072]{1,0:T(8,128)(2,1)}, u32[]{:S(2)}, u32[]{:S(2)}) collective-permute-start(bf16[32,3072]{1,0:T(8,128)(2,1)} %slice.20), channel_id=1, source_target_pairs={{0,24},{2,26},{4,28},{6,30},{8,16},{10,18},{12,20},{14,22},{16,8},... | collective-permute-start | bytes 589832 | tf_op jit(solution)/shard_map/ppermute | solution.py:345
  22.2 1.5 copy.18
  23.7 1.7 collective-permute-start.3
  25.4 1.5 collective-permute-start.4
  26.9 1.6 collective-permute-start.5
  28.6 7.3 %collective-permute-done.7 = bf16[32,3072]{1,0:T(8,128)(2,1)} collective-permute-done((bf16[32,3072]{1,0:T(8,128)(2,1)}, bf16[32,3072]{1,0:T(8,128)(2,1)}, u32[]{:S(2)}, u32[]{:S(2)}) %collective-permute-start.7) | collective-permute-done | bytes 196640 | tf_op jit(solution)/shard_map/ppermute | solution.py:345
  35.8 1.3 pad_maximum_fusion.refs_8_.refs_0_
  37.1 1.6 collective-permute-start.12
  38.7 1.5 collective-permute-start.13
  40.7 2.2 copy-done.4
  42.9 20.9 %attend.5 = (bf16[4,32,1152]{2,1,0:T(8,128)(2,1)S(1)}, bf16[4,32,1152]{2,1,0:T(8,128)(2,1)S(1)}, bf16[4,32,1152]{2,1,0:T(8,128)(2,1)S(1)}, bf16[4,32,1152]{2,1,0:T(8,128)(2,1)S(1)}) custom-call(s32[11]{0:T(128)S(1)} %concatenate.15.info, bf16[4,32,1024]{2,1,0:T(8,128)(2,1)S(1)} %pad_maximum_fusion.2.refs_0_, ...), custom_call_target="tpu_custom_call" | custom-call | flops 17179869184 | bytes 4194304 | tf_op jit(solution)/shard_map/attend/pallas_call | solution.py:177
  63.9 1.6 collective-permute-start.9
  65.4 1.5 collective-permute-start.10
  67.4 6.2 %collective-permute-done.13.refs_2_.refs_1_ = bf16[4,32,3072]{2,1,0:T(8,128)(2,1)S(1)} collective-permute-done((bf16[4,32,3072]{2,1,0:T(8,128)(2,1)S(1)}, bf16[4,32,3072]{2,1,0:T(8,128)(2,1)S(1)}, u32[]{:S(2)}, u32[]{:S(2)}) %collective-permute-start.13) | collective-permute-done | bytes 786464 | tf_op jit(solution)/shard_map/ppermute | solution.py:345
  73.6 1.9 collective-permute-done.14.refs_3_.refs_2_
  75.5 21.0 %attend.6 = (bf16[4,32,1152]{2,1,0:T(8,128)(2,1)S(1)}, bf16[4,32,1152]{2,1,0:T(8,128)(2,1)S(1)}, bf16[4,32,1152]{2,1,0:T(8,128)(2,1)S(1)}, bf16[4,32,1152]{2,1,0:T(8,128)(2,1)S(1)}) custom-call(s32[11]{0:T(128)S(1)} %concatenate.15.info, bf16[4,32,3072]{2,1,0:T(8,128)(2,1)S(1)} %pad_maximum_fusion.refs_8_.refs_0_, ...), custom_call_target="tpu_custom_call" | custom-call | flops 17179869184 | bytes 4194304 | tf_op jit(solution)/shard_map/attend/pallas_call | solution.py:177
  96.5 1.6 collective-permute-start.15
  98.6 1.5 collective-permute-start.17
  100.1 21.2 %attend.7 = (bf16[4,32,1152]{2,1,0:T(8,128)(2,1)S(1)}, bf16[4,32,1152]{2,1,0:T(8,128)(2,1)S(1)}, bf16[4,32,1152]{2,1,0:T(8,128)(2,1)S(1)}, bf16[4,32,1152]{2,1,0:T(8,128)(2,1)S(1)}) custom-call(s32[11]{0:T(128)S(1)} %concatenate.15.info, bf16[4,32,3072]{2,1,0:T(8,128)(2,1)S(1)} %pad_maximum_fusion.refs_8_.refs_0_, ...), custom_call_target="tpu_custom_call" | custom-call | flops 17179869184 | bytes 4194304 | tf_op jit(solution)/shard_map/attend/pallas_call | solution.py:177
  121.4 2.3 merge.2
  125.1 5.5 %collective-permute-start.18 = (bf16[32,2304]{1,0:T(8,128)(2,1)}, bf16[32,2304]{1,0:T(8,128)(2,1)S(1)}, u32[]{:S(2)}, u32[]{:S(2)}) collective-permute-start(bf16[32,2304]{1,0:T(8,128)(2,1)} %get-tuple-element.53), channel_id=1, source_target_pairs={{0,8},{2,10},{4,12},{6,14},{8,0},{10,2},{12,4},{14,6},{16,24},{18,... | collective-permute-start | bytes 442376 | tf_op jit(solution)/shard_map/ppermute | solution.py:345
  130.5 1.5 copy.19
  132.7 5.9 %collective-permute-start.23 = (bf16[4,32,1152]{2,1,0:T(8,128)(2,1)}, bf16[4,32,1152]{2,1,0:T(8,128)(2,1)S(1)}, u32[]{:S(2)}, u32[]{:S(2)}) collective-permute-start(bf16[4,32,1152]{2,1,0:T(8,128)(2,1)} %copy-done.13), channel_id=1, source_target_pairs={{0,4},{2,6},{4,0},{6,2},{8,12},{10,14},{12,8},{14,10},{16,20},{18,... | collective-permute-start | bytes 884744 | tf_op jit(solution)/shard_map/ppermute | solution.py:345
  138.6 1.4 collective-permute-start.24
  139.9 1.9 collective-permute-start.19
  141.8 2.9 %collective-permute-start.20 = (bf16[32,2304]{1,0:T(8,128)(2,1)}, bf16[32,2304]{1,0:T(8,128)(2,1)S(1)}, u32[]{:S(2)}, u32[]{:S(2)}) collective-permute-start(bf16[32,2304]{1,0:T(8,128)(2,1)} %copy-done.15), channel_id=1, source_target_pairs={{0,24},{2,26},{4,28},{6,30},{8,16},{10,18},{12,20},{14,22},{16,8},... | collective-permute-start | bytes 442376 | tf_op jit(solution)/shard_map/ppermute | solution.py:345
  144.7 2.2 copy-done.6
  146.9 1.1 copy-done.12
  148.8 16.6 %attend.8 = (bf16[4,32,1152]{2,1,0:T(8,128)(2,1)S(1)}, bf16[4,32,1152]{2,1,0:T(8,128)(2,1)S(1)}, bf16[4,32,1152]{2,1,0:T(8,128)(2,1)S(1)}) custom-call(s32[11]{0:T(128)S(1)} %concatenate.15.info, bf16[4,32,3072]{2,1,0:T(8,128)(2,1)S(1)} %copy-done.8, bf16[4,32,3072]{2,1,0:T(8,128)(2,1)S(1)} %copy-done.10, bf16[4,32,3072]{2,1,0:T(8,128)(2,1)S(1)} %copy-done.12, ...), custom_call_target="tpu_custom_call" | custom-call | flops 12884901888 | bytes 3670016 | tf_op jit(solution)/shard_map/attend/pallas_call | solution.py:177
  165.4 1.7 collective-permute-start.25
  168.1 1.6 collective-permute-start.27
  169.7 3.4 %collective-permute-start.21 = (bf16[1,32,2048]{2,1,0:T(8,128)(2,1)S(1)}, bf16[1,32,2048]{2,1,0:T(8,128)(2,1)S(1)}, u32[]{:S(2)}, u32[]{:S(2)}) collective-permute-start(bf16[1,32,2048]{2,1,0:T(8,128)(2,1)S(1)} %bitcast.28), channel_id=1, source_target_pairs={{0,16},{2,18},{4,20},{6,22},{8,24},{10,26},{12,28},{14,30},{16,0},... | collective-permute-start | bytes 393224 | tf_op jit(solution)/shard_map/ppermute | solution.py:345
  173.1 6.6 %attend.9.refs_4_.refs_8_ = bf16[4,32,1152]{2,1,0:T(8,128)(2,1)S(1)} custom-call(s32[11]{0:T(128)S(1)} %concatenate.15.info, bf16[4,32,3072]{2,1,0:T(8,128)(2,1)S(1)} %copy-done.3, bf16[128,4096]{1,0:T(8,128)(2,1)S(1)} %bitcast.27, bf16[4096,512]{1,0:T(8,128)(2,1)S(1)} %copy-done.6, bf16[32,512]{1,0:T(8,128)(2,1)S(1)} %copy-done.17, ...), custom_call_target="tpu_custom_call" | custom-call | flops 4294967296 | bytes 2621440 | tf_op jit(solution)/shard_map/attend/pallas_call | solution.py:177
  179.8 1.2 collective-permute-start.28
  181.0 8.3 %collective-permute-done.28 = bf16[2,32,2048]{2,1,0:T(8,128)(2,1)S(1)} collective-permute-done((bf16[2,32,2048]{2,1,0:T(8,128)(2,1)S(1)}, bf16[2,32,2048]{2,1,0:T(8,128)(2,1)S(1)}, u32[]{:S(2)}, u32[]{:S(2)}) %collective-permute-start.28) | collective-permute-done | bytes 262176 | tf_op jit(solution)/shard_map/ppermute | solution.py:345
  189.4 1.0 collective-permute-start.32
  190.3 1.2 collective-permute-start.33
  191.6 1.7 merge.3
  193.3 2.0 collective-permute-start.30
  195.4 2.3 collective-permute-start.31
  197.7 3.1 %collective-permute-done.29.refs_1_ = bf16[32,2304]{1,0:T(8,128)(2,1)S(1)} collective-permute-done((bf16[32,2304]{1,0:T(8,128)(2,1)S(1)}, bf16[32,2304]{1,0:T(8,128)(2,1)S(1)}, u32[]{:S(2)}, u32[]{:S(2)}) %collective-permute-start.29) | collective-permute-done | bytes 147488 | tf_op jit(solution)/shard_map/ppermute | solution.py:345
  200.8 1.0 collective-permute-done.30.refs_2_
  201.7 1.9 collective-permute-done.31.refs_3_
  203.6 1.5 collective-permute-done.33.refs_6_.refs_2_
  205.8 1.8 collective-permute-start.34
  207.6 1.3 collective-permute-start.36
  208.9 4.2 %collective-permute-done.34 = bf16[1,32,2048]{2,1,0:T(8,128)(2,1)S(1)} collective-permute-done((bf16[1,32,2048]{2,1,0:T(8,128)(2,1)S(1)}, bf16[1,32,2048]{2,1,0:T(8,128)(2,1)S(1)}, u32[]{:S(2)}, u32[]{:S(2)}) %collective-permute-start.34) | collective-permute-done | bytes 131104 | tf_op jit(solution)/shard_map/ppermute | solution.py:345
  213.2 6.4 %collective-permute-done.35 = bf16[2,32,2048]{2,1,0:T(8,128)(2,1)S(1)} collective-permute-done((bf16[2,32,2048]{2,1,0:T(8,128)(2,1)S(1)}, bf16[2,32,2048]{2,1,0:T(8,128)(2,1)S(1)}, u32[]{:S(2)}, u32[]{:S(2)}) %collective-permute-start.35) | collective-permute-done | bytes 262176 | tf_op jit(solution)/shard_map/ppermute | solution.py:345
  219.6 3.8 %collective-permute-done.36.refs_3_ = bf16[4,32,2048]{2,1,0:T(8,128)(2,1)S(1)} collective-permute-done((bf16[4,32,2048]{2,1,0:T(8,128)(2,1)S(1)}, bf16[4,32,2048]{2,1,0:T(8,128)(2,1)S(1)}, u32[]{:S(2)}, u32[]{:S(2)}) %collective-permute-start.36) | collective-permute-done | bytes 524320 | tf_op jit(solution)/shard_map/ppermute | solution.py:345
  223.7 1.6 collective-permute-start.37
  225.3 1.6 collective-permute-start.38
  227.0 2.2 copy-done
  229.2 1.8 project.3.refs_3_
  231.0 1.8 collective-permute-done.39.refs_1_
  232.8 2.4 project.4.refs_3_
  235.2 3.3 %collective-permute-done.37.refs_0_ = bf16[4,32,2048]{2,1,0:T(8,128)(2,1)S(1)} collective-permute-done((bf16[4,32,2048]{2,1,0:T(8,128)(2,1)S(1)}, bf16[4,32,2048]{2,1,0:T(8,128)(2,1)S(1)}, u32[]{:S(2)}, u32[]{:S(2)}) %collective-permute-start.37) | collective-permute-done | bytes 524320 | tf_op jit(solution)/shard_map/ppermute | solution.py:345
  238.5 2.4 project.5
  241.0 1.5 collective-permute-done.40
  (106 shorter events, 12.4 us)
Async XLA Ops:
  0.9 13.4 %collective-permute-start.2 = (bf16[32,1024]{1,0:T(8,128)(2,1)S(1)}, bf16[32,1024]{1,0:T(8,128)(2,1)S(1)}, u32[]{:S(2)}, u32[]{:S(2)}) collective-permute-start(bf16[32,1024]{1,0:T(8,128)(2,1)S(1)} %get-tuple-element.76), channel_id=1, source_target_pairs={{0,24},{2,26},{4,28},{6,30},{8,16},{10,18},{12,20},{14,22},{16,8},... | collective-permute-start | bytes 196616 | tf_op jit(solution)/shard_map/ppermute | solution.py:345
  6.0 8.3 %collective-permute-start.1 = (bf16[32,1024]{1,0:T(8,128)(2,1)S(1)}, bf16[32,1024]{1,0:T(8,128)(2,1)S(1)}, u32[]{:S(2)}, u32[]{:S(2)}) collective-permute-start(bf16[32,1024]{1,0:T(8,128)(2,1)S(1)} %get-tuple-element.76), channel_id=1, source_target_pairs={{0,16},{2,18},{4,20},{6,22},{8,24},{10,26},{12,28},{14,30},{16,0},... | collective-permute-start | bytes 196616 | tf_op jit(solution)/shard_map/ppermute | solution.py:345
  6.0 8.3 %collective-permute-start = (bf16[32,1024]{1,0:T(8,128)(2,1)S(1)}, bf16[32,1024]{1,0:T(8,128)(2,1)S(1)}, u32[]{:S(2)}, u32[]{:S(2)}) collective-permute-start(bf16[32,1024]{1,0:T(8,128)(2,1)S(1)} %get-tuple-element.76), channel_id=1, source_target_pairs={{0,8},{2,10},{4,12},{6,14},{8,0},{10,2},{12,4},{14,6},{16,24},{18,... | collective-permute-start | bytes 196616 | tf_op jit(solution)/shard_map/ppermute | solution.py:345
  8.2 3.9 %copy-start.24 = (s32[4,12]{1,0:T(4,128)S(1)}, s32[4,12]{1,0:T(4,128)}, u32[]{:S(2)}) copy-start(s32[4,12]{1,0:T(4,128)} %param.12) | copy-start | bytes 580
  12.9 27.8 %copy-start.17 = (bf16[32,512]{1,0:T(8,128)(2,1)S(1)}, bf16[32,512]{1,0:T(8,128)(2,1)}, u32[]{:S(2)}) copy-start(bf16[32,512]{1,0:T(8,128)(2,1)} %refs_3_.1) | copy-start | bytes 98308
  12.9 27.8 %copy-start.18 = (bf16[32,512]{1,0:T(8,128)(2,1)S(1)}, bf16[32,512]{1,0:T(8,128)(2,1)}, u32[]{:S(2)}) copy-start(bf16[32,512]{1,0:T(8,128)(2,1)} %refs_4_.4) | copy-start | bytes 98308
  14.3 0.7 copy-start.22
  15.9 11.0 %collective-permute-start.8 = (bf16[32,3072]{1,0:T(8,128)(2,1)}, bf16[32,3072]{1,0:T(8,128)(2,1)}, u32[]{:S(2)}, u32[]{:S(2)}) collective-permute-start(bf16[32,3072]{1,0:T(8,128)(2,1)} %slice.20), channel_id=1, source_target_pairs={{0,24},{2,26},{4,28},{6,30},{8,16},{10,18},{12,20},{14,22},{16,8},... | collective-permute-start | bytes 589832 | tf_op jit(solution)/shard_map/ppermute | solution.py:345
  19.7 16.1 %collective-permute-start.7 = (bf16[32,3072]{1,0:T(8,128)(2,1)}, bf16[32,3072]{1,0:T(8,128)(2,1)}, u32[]{:S(2)}, u32[]{:S(2)}) collective-permute-start(bf16[32,3072]{1,0:T(8,128)(2,1)} %slice.20), channel_id=1, source_target_pairs={{0,16},{2,18},{4,20},{6,22},{8,24},{10,26},{12,28},{14,30},{16,0},... | collective-permute-start | bytes 589832 | tf_op jit(solution)/shard_map/ppermute | solution.py:345
  19.7 16.1 %collective-permute-start.6 = (bf16[32,3072]{1,0:T(8,128)(2,1)}, bf16[32,3072]{1,0:T(8,128)(2,1)}, u32[]{:S(2)}, u32[]{:S(2)}) collective-permute-start(bf16[32,3072]{1,0:T(8,128)(2,1)} %slice.20), channel_id=1, source_target_pairs={{0,8},{2,10},{4,12},{6,14},{8,0},{10,2},{12,4},{14,6},{16,24},{18,... | collective-permute-start | bytes 589832 | tf_op jit(solution)/shard_map/ppermute | solution.py:345
  23.7 16.5 %collective-permute-start.3 = (bf16[4,32,1024]{2,1,0:T(8,128)(2,1)S(1)}, bf16[4,32,1024]{2,1,0:T(8,128)(2,1)S(1)}, u32[]{:S(2)}, u32[]{:S(2)}) collective-permute-start(bf16[4,32,1024]{2,1,0:T(8,128)(2,1)S(1)} %pad_maximum_fusion.2.refs_0_), channel_id=1, source_target_pairs={{0,2},{2,0},{4,6},{6,4},{8,10},{10,8},{12,14},{14,12},{16,18},{18,... | collective-permute-start | bytes 786440 | tf_op jit(solution)/shard_map/ppermute | solution.py:345
  25.4 15.3 %collective-permute-start.4 = (bf16[4,32,1024]{2,1,0:T(8,128)(2,1)S(1)}, bf16[4,32,1024]{2,1,0:T(8,128)(2,1)S(1)}, u32[]{:S(2)}, u32[]{:S(2)}) collective-permute-start(bf16[4,32,1024]{2,1,0:T(8,128)(2,1)S(1)} %pad_maximum_fusion.2.refs_0_), channel_id=1, source_target_pairs={{0,4},{2,6},{4,0},{6,2},{8,12},{10,14},{12,8},{14,10},{16,20},{18,... | collective-permute-start | bytes 786440 | tf_op jit(solution)/shard_map/ppermute | solution.py:345
  26.9 13.8 %collective-permute-start.5 = (bf16[4,32,1024]{2,1,0:T(8,128)(2,1)S(1)}, bf16[4,32,1024]{2,1,0:T(8,128)(2,1)S(1)}, u32[]{:S(2)}, u32[]{:S(2)}) collective-permute-start(bf16[4,32,1024]{2,1,0:T(8,128)(2,1)S(1)} %pad_maximum_fusion.2.refs_0_), channel_id=1, source_target_pairs={{0,6},{2,4},{4,2},{6,0},{8,14},{10,12},{12,10},{14,8},{16,22},{18,... | collective-permute-start | bytes 786440 | tf_op jit(solution)/shard_map/ppermute | solution.py:345
  37.1 63.0 %copy-start.2 = (bf16[4,32,3072]{2,1,0:T(8,128)(2,1)}, bf16[4,32,3072]{2,1,0:T(8,128)(2,1)S(1)}, u32[]{:S(2)}) copy-start(bf16[4,32,3072]{2,1,0:T(8,128)(2,1)S(1)} %pad_maximum_fusion.refs_8_.refs_0_) | copy-start | bytes 2359300
  37.1 29.8 %collective-permute-start.12 = (bf16[4,32,3072]{2,1,0:T(8,128)(2,1)S(1)}, bf16[4,32,3072]{2,1,0:T(8,128)(2,1)S(1)}, u32[]{:S(2)}, u32[]{:S(2)}) collective-permute-start(bf16[4,32,3072]{2,1,0:T(8,128)(2,1)S(1)} %pad_maximum_fusion.refs_8_.refs_0_), channel_id=1, source_target_pairs={{0,2},{2,0},{4,6},{6,4},{8,10},{10,8},{12,14},{14,12},{16,18},{18,... | collective-permute-start | bytes 2359304 | tf_op jit(solution)/shard_map/ppermute | solution.py:345
  38.7 34.9 %collective-permute-start.13 = (bf16[4,32,3072]{2,1,0:T(8,128)(2,1)S(1)}, bf16[4,32,3072]{2,1,0:T(8,128)(2,1)S(1)}, u32[]{:S(2)}, u32[]{:S(2)}) collective-permute-start(bf16[4,32,3072]{2,1,0:T(8,128)(2,1)S(1)} %pad_maximum_fusion.refs_8_.refs_0_), channel_id=1, source_target_pairs={{0,4},{2,6},{4,0},{6,2},{8,12},{10,14},{12,8},{14,10},{16,20},{18,... | collective-permute-start | bytes 2359304 | tf_op jit(solution)/shard_map/ppermute | solution.py:345
  40.2 35.3 %collective-permute-start.14 = (bf16[4,32,3072]{2,1,0:T(8,128)(2,1)S(1)}, bf16[4,32,3072]{2,1,0:T(8,128)(2,1)S(1)}, u32[]{:S(2)}, u32[]{:S(2)}) collective-permute-start(bf16[4,32,3072]{2,1,0:T(8,128)(2,1)S(1)} %pad_maximum_fusion.refs_8_.refs_0_), channel_id=1, source_target_pairs={{0,6},{2,4},{4,2},{6,0},{8,14},{10,12},{12,10},{14,8},{16,22},{18,... | collective-permute-start | bytes 2359304 | tf_op jit(solution)/shard_map/ppermute | solution.py:345
  40.7 2.2 copy-start.4
  42.9 32.6 %copy-start.5 = (bf16[4096,512]{1,0:T(8,128)(2,1)S(1)}, bf16[4096,512]{1,0:T(8,128)(2,1)}, u32[]{:S(2)}) copy-start(bf16[4096,512]{1,0:T(8,128)(2,1)} %refs_2_.3) | copy-start | bytes 12582916
  63.9 34.8 %collective-permute-start.9 = (bf16[4,32,1152]{2,1,0:T(8,128)(2,1)S(1)}, bf16[4,32,1152]{2,1,0:T(8,128)(2,1)S(1)}, u32[]{:S(2)}, u32[]{:S(2)}) collective-permute-start(bf16[4,32,1152]{2,1,0:T(8,128)(2,1)S(1)} %get-tuple-element.42), channel_id=1, source_target_pairs={{0,2},{2,0},{4,6},{6,4},{8,10},{10,8},{12,14},{14,12},{16,18},{18,... | collective-permute-start | bytes 884744 | tf_op jit(solution)/shard_map/ppermute | solution.py:345
  65.4 55.9 %collective-permute-start.10 = (bf16[4,32,1152]{2,1,0:T(8,128)(2,1)S(1)}, bf16[4,32,1152]{2,1,0:T(8,128)(2,1)S(1)}, u32[]{:S(2)}, u32[]{:S(2)}) collective-permute-start(bf16[4,32,1152]{2,1,0:T(8,128)(2,1)S(1)} %get-tuple-element.43), channel_id=1, source_target_pairs={{0,4},{2,6},{4,0},{6,2},{8,12},{10,14},{12,8},{14,10},{16,20},{18,... | collective-permute-start | bytes 884744 | tf_op jit(solution)/shard_map/ppermute | solution.py:345
  67.0 33.1 %copy-start.7 = (bf16[4,32,3072]{2,1,0:T(8,128)(2,1)}, bf16[4,32,3072]{2,1,0:T(8,128)(2,1)S(1)}, u32[]{:S(2)}) copy-start(bf16[4,32,3072]{2,1,0:T(8,128)(2,1)S(1)} %collective-permute-done.12.refs_1_.refs_0_) | copy-start | bytes 2359300
  67.0 54.4 %collective-permute-start.11 = (bf16[4,32,1152]{2,1,0:T(8,128)(2,1)S(1)}, bf16[4,32,1152]{2,1,0:T(8,128)(2,1)S(1)}, u32[]{:S(2)}, u32[]{:S(2)}) collective-permute-start(bf16[4,32,1152]{2,1,0:T(8,128)(2,1)S(1)} %get-tuple-element.44), channel_id=1, source_target_pairs={{0,6},{2,4},{4,2},{6,0},{8,14},{10,12},{12,10},{14,8},{16,22},{18,... | collective-permute-start | bytes 884744 | tf_op jit(solution)/shard_map/ppermute | solution.py:345
  73.6 26.5 %copy-start.9 = (bf16[4,32,3072]{2,1,0:T(8,128)(2,1)}, bf16[4,32,3072]{2,1,0:T(8,128)(2,1)S(1)}, u32[]{:S(2)}) copy-start(bf16[4,32,3072]{2,1,0:T(8,128)(2,1)S(1)} %collective-permute-done.13.refs_2_.refs_1_) | copy-start | bytes 2359300
  75.5 24.6 %copy-start.11 = (bf16[4,32,3072]{2,1,0:T(8,128)(2,1)}, bf16[4,32,3072]{2,1,0:T(8,128)(2,1)S(1)}, u32[]{:S(2)}) copy-start(bf16[4,32,3072]{2,1,0:T(8,128)(2,1)S(1)} %collective-permute-done.14.refs_3_.refs_2_) | copy-start | bytes 2359300
  96.5 24.8 %collective-permute-start.15 = (bf16[4,32,1152]{2,1,0:T(8,128)(2,1)S(1)}, bf16[4,32,1152]{2,1,0:T(8,128)(2,1)S(1)}, u32[]{:S(2)}, u32[]{:S(2)}) collective-permute-start(bf16[4,32,1152]{2,1,0:T(8,128)(2,1)S(1)} %get-tuple-element.47), channel_id=1, source_target_pairs={{0,2},{2,0},{4,6},{6,4},{8,10},{10,8},{12,14},{14,12},{16,18},{18,... | collective-permute-start | bytes 884744 | tf_op jit(solution)/shard_map/ppermute | solution.py:345
  98.1 23.3 %collective-permute-start.16 = (bf16[4,32,1152]{2,1,0:T(8,128)(2,1)S(1)}, bf16[4,32,1152]{2,1,0:T(8,128)(2,1)S(1)}, u32[]{:S(2)}, u32[]{:S(2)}) collective-permute-start(bf16[4,32,1152]{2,1,0:T(8,128)(2,1)S(1)} %get-tuple-element.48), channel_id=1, source_target_pairs={{0,4},{2,6},{4,0},{6,2},{8,12},{10,14},{12,8},{14,10},{16,20},{18,... | collective-permute-start | bytes 884744 | tf_op jit(solution)/shard_map/ppermute | solution.py:345
  98.6 22.8 %collective-permute-start.17 = (bf16[4,32,1152]{2,1,0:T(8,128)(2,1)S(1)}, bf16[4,32,1152]{2,1,0:T(8,128)(2,1)S(1)}, u32[]{:S(2)}, u32[]{:S(2)}) collective-permute-start(bf16[4,32,1152]{2,1,0:T(8,128)(2,1)S(1)} %get-tuple-element.49), channel_id=1, source_target_pairs={{0,6},{2,4},{4,2},{6,0},{8,14},{10,12},{12,10},{14,8},{16,22},{18,... | collective-permute-start | bytes 884744 | tf_op jit(solution)/shard_map/ppermute | solution.py:345
  121.3 9.2 %copy-start.13 = (bf16[4,32,1152]{2,1,0:T(8,128)(2,1)}, bf16[4,32,1152]{2,1,0:T(8,128)(2,1)S(1)}, u32[]{:S(2)}) copy-start(bf16[4,32,1152]{2,1,0:T(8,128)(2,1)S(1)} %get-tuple-element.59) | copy-start | bytes 884740
  121.3 9.2 %copy-start.14 = (bf16[4,32,1152]{2,1,0:T(8,128)(2,1)}, bf16[4,32,1152]{2,1,0:T(8,128)(2,1)S(1)}, u32[]{:S(2)}) copy-start(bf16[4,32,1152]{2,1,0:T(8,128)(2,1)S(1)} %get-tuple-element.58) | copy-start | bytes 884740
  121.3 23.4 %copy-start.8 = (bf16[4,32,3072]{2,1,0:T(8,128)(2,1)S(1)}, bf16[4,32,3072]{2,1,0:T(8,128)(2,1)}, u32[]{:S(2)}) copy-start(bf16[4,32,3072]{2,1,0:T(8,128)(2,1)} %copy-done.7) | copy-start | bytes 2359300
  121.3 23.3 %copy-start.10 = (bf16[4,32,3072]{2,1,0:T(8,128)(2,1)S(1)}, bf16[4,32,3072]{2,1,0:T(8,128)(2,1)}, u32[]{:S(2)}) copy-start(bf16[4,32,3072]{2,1,0:T(8,128)(2,1)} %copy-done.9) | copy-start | bytes 2359300
  123.7 0.7 copy-start.15
  124.4 0.7 copy-start.16
  125.1 16.8 %collective-permute-start.18 = (bf16[32,2304]{1,0:T(8,128)(2,1)}, bf16[32,2304]{1,0:T(8,128)(2,1)S(1)}, u32[]{:S(2)}, u32[]{:S(2)}) collective-permute-start(bf16[32,2304]{1,0:T(8,128)(2,1)} %get-tuple-element.53), channel_id=1, source_target_pairs={{0,8},{2,10},{4,12},{6,14},{8,0},{10,2},{12,4},{14,6},{16,24},{18,... | collective-permute-start | bytes 442376 | tf_op jit(solution)/shard_map/ppermute | solution.py:345
  132.0 36.1 %collective-permute-start.22 = (bf16[4,32,1152]{2,1,0:T(8,128)(2,1)}, bf16[4,32,1152]{2,1,0:T(8,128)(2,1)S(1)}, u32[]{:S(2)}, u32[]{:S(2)}) collective-permute-start(bf16[4,32,1152]{2,1,0:T(8,128)(2,1)} %copy-done.14), channel_id=1, source_target_pairs={{0,2},{2,0},{4,6},{6,4},{8,10},{10,8},{12,14},{14,12},{16,18},{18,... | collective-permute-start | bytes 884744 | tf_op jit(solution)/shard_map/ppermute | solution.py:345
  132.7 37.0 %collective-permute-start.23 = (bf16[4,32,1152]{2,1,0:T(8,128)(2,1)}, bf16[4,32,1152]{2,1,0:T(8,128)(2,1)S(1)}, u32[]{:S(2)}, u32[]{:S(2)}) collective-permute-start(bf16[4,32,1152]{2,1,0:T(8,128)(2,1)} %copy-done.13), channel_id=1, source_target_pairs={{0,4},{2,6},{4,0},{6,2},{8,12},{10,14},{12,8},{14,10},{16,20},{18,... | collective-permute-start | bytes 884744 | tf_op jit(solution)/shard_map/ppermute | solution.py:345
  138.6 34.5 %collective-permute-start.24 = (bf16[4,32,1152]{2,1,0:T(8,128)(2,1)S(1)}, bf16[4,32,1152]{2,1,0:T(8,128)(2,1)S(1)}, u32[]{:S(2)}, u32[]{:S(2)}) collective-permute-start(bf16[4,32,1152]{2,1,0:T(8,128)(2,1)S(1)} %get-tuple-element.60), channel_id=1, source_target_pairs={{0,6},{2,4},{4,2},{6,0},{8,14},{10,12},{12,10},{14,8},{16,22},{18,... | collective-permute-start | bytes 884744 | tf_op jit(solution)/shard_map/ppermute | solution.py:345
  139.9 25.4 %collective-permute-start.19 = (bf16[32,2304]{1,0:T(8,128)(2,1)}, bf16[32,2304]{1,0:T(8,128)(2,1)S(1)}, u32[]{:S(2)}, u32[]{:S(2)}) collective-permute-start(bf16[32,2304]{1,0:T(8,128)(2,1)} %copy-done.16), channel_id=1, source_target_pairs={{0,16},{2,18},{4,20},{6,22},{8,24},{10,26},{12,28},{14,30},{16,0},... | collective-permute-start | bytes 442376 | tf_op jit(solution)/shard_map/ppermute | solution.py:345
  141.8 25.3 %collective-permute-start.20 = (bf16[32,2304]{1,0:T(8,128)(2,1)}, bf16[32,2304]{1,0:T(8,128)(2,1)S(1)}, u32[]{:S(2)}, u32[]{:S(2)}) collective-permute-start(bf16[32,2304]{1,0:T(8,128)(2,1)} %copy-done.15), channel_id=1, source_target_pairs={{0,24},{2,26},{4,28},{6,30},{8,16},{10,18},{12,20},{14,22},{16,8},... | collective-permute-start | bytes 442376 | tf_op jit(solution)/shard_map/ppermute | solution.py:345
  144.7 2.2 copy-start.6
  146.9 1.1 copy-start.12
  148.0 0.8 copy-start.19
  148.8 24.3 %copy-start.3 = (bf16[4,32,3072]{2,1,0:T(8,128)(2,1)S(1)}, bf16[4,32,3072]{2,1,0:T(8,128)(2,1)}, u32[]{:S(2)}) copy-start(bf16[4,32,3072]{2,1,0:T(8,128)(2,1)} %copy-done.2) | copy-start | bytes 2359300
  148.8 24.3 %copy-start.20 = (bf16[32,512]{1,0:T(8,128)(2,1)S(1)}, bf16[32,512]{1,0:T(8,128)(2,1)}, u32[]{:S(2)}) copy-start(bf16[32,512]{1,0:T(8,128)(2,1)} %refs_4_.4) | copy-start | bytes 98308
  165.4 14.3 %collective-permute-start.25 = (bf16[4,32,1152]{2,1,0:T(8,128)(2,1)S(1)}, bf16[4,32,1152]{2,1,0:T(8,128)(2,1)S(1)}, u32[]{:S(2)}, u32[]{:S(2)}) collective-permute-start(bf16[4,32,1152]{2,1,0:T(8,128)(2,1)S(1)} %get-tuple-element.57.refs_4_), channel_id=1, source_target_pairs={{0,2},{2,0},{4,6},{6,4},{8,10},{10,8},{12,14},{14,12},{16,18},{18,... | collective-permute-start | bytes 884744 | tf_op jit(solution)/shard_map/ppermute | solution.py:345
  167.1 12.7 %collective-permute-start.26 = (bf16[4,32,1152]{2,1,0:T(8,128)(2,1)S(1)}, bf16[4,32,1152]{2,1,0:T(8,128)(2,1)S(1)}, u32[]{:S(2)}, u32[]{:S(2)}) collective-permute-start(bf16[4,32,1152]{2,1,0:T(8,128)(2,1)S(1)} %get-tuple-element.61), channel_id=1, source_target_pairs={{0,4},{2,6},{4,0},{6,2},{8,12},{10,14},{12,8},{14,10},{16,20},{18,... | collective-permute-start | bytes 884744 | tf_op jit(solution)/shard_map/ppermute | solution.py:345
  168.1 11.7 %collective-permute-start.27 = (bf16[4,32,1152]{2,1,0:T(8,128)(2,1)S(1)}, bf16[4,32,1152]{2,1,0:T(8,128)(2,1)S(1)}, u32[]{:S(2)}, u32[]{:S(2)}) collective-permute-start(bf16[4,32,1152]{2,1,0:T(8,128)(2,1)S(1)} %get-tuple-element.62), channel_id=1, source_target_pairs={{0,6},{2,4},{4,2},{6,0},{8,14},{10,12},{12,10},{14,8},{16,22},{18,... | collective-permute-start | bytes 884744 | tf_op jit(solution)/shard_map/ppermute | solution.py:345
  169.7 10.0 %collective-permute-start.21 = (bf16[1,32,2048]{2,1,0:T(8,128)(2,1)S(1)}, bf16[1,32,2048]{2,1,0:T(8,128)(2,1)S(1)}, u32[]{:S(2)}, u32[]{:S(2)}) collective-permute-start(bf16[1,32,2048]{2,1,0:T(8,128)(2,1)S(1)} %bitcast.28), channel_id=1, source_target_pairs={{0,16},{2,18},{4,20},{6,22},{8,24},{10,26},{12,28},{14,30},{16,0},... | collective-permute-start | bytes 393224 | tf_op jit(solution)/shard_map/ppermute | solution.py:345
  179.8 9.6 %collective-permute-start.28 = (bf16[2,32,2048]{2,1,0:T(8,128)(2,1)S(1)}, bf16[2,32,2048]{2,1,0:T(8,128)(2,1)S(1)}, u32[]{:S(2)}, u32[]{:S(2)}) collective-permute-start(bf16[2,32,2048]{2,1,0:T(8,128)(2,1)S(1)} %pad_maximum_fusion.3.refs_9_), channel_id=1, source_target_pairs={{0,8},{2,10},{4,12},{6,14},{8,0},{10,2},{12,4},{14,6},{16,24},{18,... | collective-permute-start | bytes 786440 | tf_op jit(solution)/shard_map/ppermute | solution.py:345
  189.4 14.3 %collective-permute-start.32 = (bf16[4,32,2048]{2,1,0:T(8,128)(2,1)S(1)}, bf16[4,32,2048]{2,1,0:T(8,128)(2,1)S(1)}, u32[]{:S(2)}, u32[]{:S(2)}) collective-permute-start(bf16[4,32,2048]{2,1,0:T(8,128)(2,1)S(1)} %constant_dynamic-update-slice_fusion.refs_0_), channel_id=1, source_target_pairs={{0,2},{2,0},{4,6},{6,4},{8,10},{10,8},{12,14},{14,12},{16,18},{18,... | collective-permute-start | bytes 1572872 | tf_op jit(solution)/shard_map/ppermute | solution.py:345
  190.3 14.8 %collective-permute-start.33 = (bf16[4,32,2048]{2,1,0:T(8,128)(2,1)S(1)}, bf16[4,32,2048]{2,1,0:T(8,128)(2,1)S(1)}, u32[]{:S(2)}, u32[]{:S(2)}) collective-permute-start(bf16[4,32,2048]{2,1,0:T(8,128)(2,1)S(1)} %constant_dynamic-update-slice_fusion.refs_0_), channel_id=1, source_target_pairs={{0,4},{2,6},{4,0},{6,2},{8,12},{10,14},{12,8},{14,10},{16,20},{18,... | collective-permute-start | bytes 1572872 | tf_op jit(solution)/shard_map/ppermute | solution.py:345
  193.3 7.5 %collective-permute-start.29 = (bf16[32,2304]{1,0:T(8,128)(2,1)S(1)}, bf16[32,2304]{1,0:T(8,128)(2,1)S(1)}, u32[]{:S(2)}, u32[]{:S(2)}) collective-permute-start(bf16[32,2304]{1,0:T(8,128)(2,1)S(1)} %get-tuple-element.65), channel_id=1, source_target_pairs={{0,8},{2,10},{4,12},{6,14},{8,0},{10,2},{12,4},{14,6},{16,24},{18,... | collective-permute-start | bytes 442376 | tf_op jit(solution)/shard_map/ppermute | solution.py:345
  193.3 8.4 %collective-permute-start.30 = (bf16[32,2304]{1,0:T(8,128)(2,1)S(1)}, bf16[32,2304]{1,0:T(8,128)(2,1)S(1)}, u32[]{:S(2)}, u32[]{:S(2)}) collective-permute-start(bf16[32,2304]{1,0:T(8,128)(2,1)S(1)} %get-tuple-element.66), channel_id=1, source_target_pairs={{0,16},{2,18},{4,20},{6,22},{8,24},{10,26},{12,28},{14,30},{16,0},... | collective-permute-start | bytes 442376 | tf_op jit(solution)/shard_map/ppermute | solution.py:345
  195.4 8.3 %collective-permute-start.31 = (bf16[32,2304]{1,0:T(8,128)(2,1)S(1)}, bf16[32,2304]{1,0:T(8,128)(2,1)S(1)}, u32[]{:S(2)}, u32[]{:S(2)}) collective-permute-start(bf16[32,2304]{1,0:T(8,128)(2,1)S(1)} %get-tuple-element.67), channel_id=1, source_target_pairs={{0,24},{2,26},{4,28},{6,30},{8,16},{10,18},{12,20},{14,22},{16,8},... | collective-permute-start | bytes 442376 | tf_op jit(solution)/shard_map/ppermute | solution.py:345
  205.8 7.3 %collective-permute-start.34 = (bf16[1,32,2048]{2,1,0:T(8,128)(2,1)S(1)}, bf16[1,32,2048]{2,1,0:T(8,128)(2,1)S(1)}, u32[]{:S(2)}, u32[]{:S(2)}) collective-permute-start(bf16[1,32,2048]{2,1,0:T(8,128)(2,1)S(1)} %bitcast.30), channel_id=1, source_target_pairs={{0,16},{2,18},{4,20},{6,22},{8,24},{10,26},{12,28},{14,30},{16,0},... | collective-permute-start | bytes 393224 | tf_op jit(solution)/shard_map/ppermute | solution.py:345
  207.6 15.9 %collective-permute-start.36 = (bf16[4,32,2048]{2,1,0:T(8,128)(2,1)S(1)}, bf16[4,32,2048]{2,1,0:T(8,128)(2,1)S(1)}, u32[]{:S(2)}, u32[]{:S(2)}) collective-permute-start(bf16[4,32,2048]{2,1,0:T(8,128)(2,1)S(1)} %constant_dynamic-update-slice_fusion.refs_0_), channel_id=1, source_target_pairs={{0,6},{2,4},{4,2},{6,0},{8,14},{10,12},{12,10},{14,8},{16,22},{18,... | collective-permute-start | bytes 1572872 | tf_op jit(solution)/shard_map/ppermute | solution.py:345
  213.1 6.4 %collective-permute-start.35 = (bf16[2,32,2048]{2,1,0:T(8,128)(2,1)S(1)}, bf16[2,32,2048]{2,1,0:T(8,128)(2,1)S(1)}, u32[]{:S(2)}, u32[]{:S(2)}) collective-permute-start(bf16[2,32,2048]{2,1,0:T(8,128)(2,1)S(1)} %pad_maximum_fusion.4), channel_id=1, source_target_pairs={{0,8},{2,10},{4,12},{6,14},{8,0},{10,2},{12,4},{14,6},{16,24},{18,... | collective-permute-start | bytes 786440 | tf_op jit(solution)/shard_map/ppermute | solution.py:345
  223.5 9.3 %collective-permute-start.39 = (bf16[4,32,2048]{2,1,0:T(8,128)(2,1)S(1)}, bf16[4,32,2048]{2,1,0:T(8,128)(2,1)}, u32[]{:S(2)}, u32[]{:S(2)}) collective-permute-start(bf16[4,32,2048]{2,1,0:T(8,128)(2,1)S(1)} %pad_maximum_fusion.1.refs_0_), channel_id=1, source_target_pairs={{0,2},{2,0},{4,6},{6,4},{8,10},{10,8},{12,14},{14,12},{16,18},{18,... | collective-permute-start | bytes 1572872 | tf_op jit(solution)/shard_map/ppermute | solution.py:345
  223.7 14.8 %collective-permute-start.37 = (bf16[4,32,2048]{2,1,0:T(8,128)(2,1)S(1)}, bf16[4,32,2048]{2,1,0:T(8,128)(2,1)S(1)}, u32[]{:S(2)}, u32[]{:S(2)}) collective-permute-start(bf16[4,32,2048]{2,1,0:T(8,128)(2,1)S(1)} %pad_maximum_fusion.1.refs_0_), channel_id=1, source_target_pairs={{0,4},{2,6},{4,0},{6,2},{8,12},{10,14},{12,8},{14,10},{16,20},{18,... | collective-permute-start | bytes 1572872 | tf_op jit(solution)/shard_map/ppermute | solution.py:345
  225.3 13.2 %collective-permute-start.38 = (bf16[4,32,2048]{2,1,0:T(8,128)(2,1)S(1)}, bf16[4,32,2048]{2,1,0:T(8,128)(2,1)}, u32[]{:S(2)}, u32[]{:S(2)}) collective-permute-start(bf16[4,32,2048]{2,1,0:T(8,128)(2,1)S(1)} %pad_maximum_fusion.1.refs_0_), channel_id=1, source_target_pairs={{0,6},{2,4},{4,2},{6,0},{8,14},{10,12},{12,10},{14,8},{16,22},{18,... | collective-permute-start | bytes 1572872 | tf_op jit(solution)/shard_map/ppermute | solution.py:345
  227.0 2.2 copy-start
  229.2 3.6 %copy-start.1 = (bf16[4096,512]{1,0:T(8,128)(2,1)S(1)}, bf16[4096,512]{1,0:T(8,128)(2,1)}, u32[]{:S(2)}) copy-start(bf16[4096,512]{1,0:T(8,128)(2,1)} %refs_2_.5) | copy-start | bytes 12582916
  240.9 1.6 collective-permute-start.40
  (2 other events, 1.3 us)

commit v9 on v8

--- a/solution.py
+++ b/solution.py
@@ -190,7 +190,7 @@
             grid=(1,),
             in_specs=[pl.BlockSpec((blocks, rows, cols), lambda i, s: (0, 0, q_head))] * count
             + [
-                pl.BlockSpec((HEAD_SIZE, key_count), lambda i, s: (0, 0)),
+                pl.BlockSpec((HEAD_SIZE, key_count), lambda i, s: (head, 0)),
                 pl.BlockSpec((key_count, HEAD_SIZE), lambda i, s: (0, head)),
                 span_block,
                 span_block,
@@ -216,6 +216,25 @@
         ),
         name="attend",
     )(info, *[q_pieces[b] for b in chosen], keys_t, values, span_keys, span_values, *after)
+
+
+def transpose_kernel(x_ref, *refs):
+    refs[-1][...] = x_ref[...].T
+
+
+def transpose_keys(keys, after):
+    count, cols = keys.shape
+    chunk = min(count, 1024)
+    return pl.pallas_call(
+        transpose_kernel,
+        grid=(count // chunk,),
+        in_specs=[pl.BlockSpec((chunk, cols), lambda i: (i, 0))] + [pl.BlockSpec(memory_space=pl.ANY)] * len(after),
+        out_specs=pl.BlockSpec((cols, chunk), lambda i: (0, i)),
+        out_shape=jax.ShapeDtypeStruct((cols, count), keys.dtype),
+        compiler_params=pltpu.CompilerParams(vmem_limit_bytes=SHORT_VMEM),
+        cost_estimate=pl.CostEstimate(flops=0, bytes_accessed=4 * keys.size, transcendentals=0),
+        name="transpose",
+    )(keys, *after)
 
 
 def combine(parts):
@@ -380,17 +399,16 @@
 
     first = stack_blocks(queries[:, :width])
     sources, stacks = [(gather_plane(first), 0)], []
-    keys_t = []
-    for h in range(heads):
-        keys, _ = lax.optimization_barrier(
-            (context_keys[:, h * HEAD_SIZE : (h + 1) * HEAD_SIZE], sources[0][0][1] if h else info)
-        )
-        keys_t.append(keys.T)
     if heads > 1:
         held, _ = lax.optimization_barrier((queries[:, width:], first))
-        stacks = [stack_blocks(held)]
+        early = [exchange(held, "ctx", a * plane) for a in range(1, blocks)]
+        keys_t = transpose_keys(context_keys, early[:1])
+        held, _ = lax.optimization_barrier((held, keys_t))
+        stacks = [jnp.stack([held] + early)]
         pieces = gather_plane(stacks[0])
         sources += [(pieces, i) for i in range(heads - 1)]
+    else:
+        keys_t = transpose_keys(context_keys, [])
 
     size = 2 if heads % 2 == 0 else 1
     attended, merged, rows_of = [], [], []
@@ -417,7 +435,7 @@
     def attend(h, chosen, after):
         pieces, q_head = sources[h]
         return attend_head(
-            info, pieces, chosen, q_head, keys_t[h], context_values, span_keys, span_values, h, after
+            info, pieces, chosen, q_head, keys_t, context_values, span_keys, span_values, h, after
         )
 
     latest = stacks

time: 244 us -> 232 us (0.951)
  starting transfers between devices: 65.4 us -> 84.8 us
  Pallas kernels: 98.2 us -> 82.1 us
  local copies, waits for them, and re-layouts: 22.2 us -> 7.59 us
    ppermute x41, starting transfers between devices: 65.4 us -> 84.8 us  [exchange(): return lax.ppermute(x, axis, [(i, i ^ distance) for i in range(count)])]
    pallas_call x5, Pallas kernels: 86.3 us -> 69.1 us  [attend_head(): pl.pallas_call(functools.partial(attend_kernel, chosen=chosen, blocks=blo...]
    unnamed x51 -> x13, local copies, waits for them, and re-layouts: 10.5 us -> 4.41 us
    optimization_barrier x4 -> x0, local copies, waits for them, and re-layouts: 4.03 us -> none  [local(): lax.optimization_barrier((context_keys[:, h * HEAD_SIZE:(h + 1) * HEAD_SI...]
    slice x1 -> x0, local copies, waits for them, and re-layouts: 3.85 us -> none  [local(): context_keys[:, h * HEAD_SIZE:(h + 1) * HEAD_SIZE]]
  transfers between devices with their start and end apart: 41 -> 41, of which waited for: 14 -> 13; matrix products, arithmetic and copies ran while one was open for 6% -> 2% of each run, Pallas kernels for 38% -> 33%
where the time goes in v9:
time: 232 us
  starting transfers between devices  84.8 us (37%)
  Pallas kernels  82.1 us (35%)
  waiting for transfers between devices  54.3 us (23%)
  local copies, waits for them, and re-layouts  7.59 us (3%)
  other arithmetic  3.26 us (1%)
    ppermute x41, starting transfers between devices, exchange(): return lax.ppermute(x, axis, [(i, i ^ distance) for i in range(count)])  84.8 us
    pallas_call x5, Pallas kernels, attend_head(): pl.pallas_call(functools.partial(attend_kernel, chosen=chosen, blocks=blo...  69.1 us
    ppermute x41, waiting for transfers between devices, exchange(): return lax.ppermute(x, axis, [(i, i ^ distance) for i in range(count)])  54.3 us
    pallas_call x3, Pallas kernels, project(): pl.pallas_call(functools.partial(project_kernel, order=order, chosen=chos...  6.72 us
  transfers between devices with their start and end apart: 41, of which 13 were waited for; matrix products, arithmetic and copies ran while one was open for 2% of the time, Pallas kernels for 33%

profile of v9, /device:TPU:0, one launch (start us, length us, event | category | flops | bytes accessed | tf_op | source)
XLA Modules:
  0.0 232.4 jit_solution(7965772736087655562)
XLA Ops:
  0.0 0.8 slice_bitcast_fusion
  0.9 3.1 %collective-permute-start = (bf16[32,1024]{1,0:T(8,128)(2,1)S(1)}, bf16[32,1024]{1,0:T(8,128)(2,1)S(1)}, u32[]{:S(2)}, u32[]{:S(2)}) collective-permute-start(bf16[32,1024]{1,0:T(8,128)(2,1)S(1)} %get-tuple-element.66), channel_id=1, source_target_pairs={{0,8},{2,10},{4,12},{6,14},{8,0},{10,2},{12,4},{14,6},{16,24},{18,... | collective-permute-start | bytes 196616 | tf_op jit(solution)/shard_map/ppermute | solution.py:364
  3.9 2.6 %collective-permute-start.1 = (bf16[32,1024]{1,0:T(8,128)(2,1)S(1)}, bf16[32,1024]{1,0:T(8,128)(2,1)S(1)}, u32[]{:S(2)}, u32[]{:S(2)}) collective-permute-start(bf16[32,1024]{1,0:T(8,128)(2,1)S(1)} %get-tuple-element.66), channel_id=1, source_target_pairs={{0,16},{2,18},{4,20},{6,22},{8,24},{10,26},{12,28},{14,30},{16,0},... | collective-permute-start | bytes 196616 | tf_op jit(solution)/shard_map/ppermute | solution.py:364
  6.5 0.9 slice.7
  7.5 0.8 compare_reduce_fusion
  9.0 0.8 sort.17
  9.7 1.5 collective-permute-done.1
  11.2 1.4 collective-permute-done.2
  12.7 2.3 %collective-permute-start.7 = (bf16[32,3072]{1,0:T(8,128)(2,1)S(1)}, bf16[32,3072]{1,0:T(8,128)(2,1)S(1)}, u32[]{:S(2)}, u32[]{:S(2)}) collective-permute-start(bf16[32,3072]{1,0:T(8,128)(2,1)S(1)} %slice.7), channel_id=1, source_target_pairs={{0,16},{2,18},{4,20},{6,22},{8,24},{10,26},{12,28},{14,30},{16,0},... | collective-permute-start | bytes 589832 | tf_op jit(solution)/shard_map/ppermute | solution.py:364
  15.1 2.0 collective-permute-start.8
  17.1 0.7 convert_reduce_fusion
  17.8 0.7 concatenate.15.info
  18.5 1.5 collective-permute-start.3
  20.0 1.5 collective-permute-start.4
  21.5 1.5 collective-permute-start.5
  23.0 2.2 copy-done.2
  25.2 1.7 transpose.8.refs_4_.refs_3_.refs_1_
  26.9 2.7 %collective-permute-done.7 = bf16[32,3072]{1,0:T(8,128)(2,1)S(1)} collective-permute-done((bf16[32,3072]{1,0:T(8,128)(2,1)S(1)}, bf16[32,3072]{1,0:T(8,128)(2,1)S(1)}, u32[]{:S(2)}, u32[]{:S(2)}) %collective-permute-start.7) | collective-permute-done | bytes 196640 | tf_op jit(solution)/shard_map/ppermute | solution.py:364
  29.7 1.6 collective-permute-start.12
  31.3 1.5 collective-permute-start.13
  33.3 16.6 %attend.5 = (bf16[4,32,1152]{2,1,0:T(8,128)(2,1)S(1)}, bf16[4,32,1152]{2,1,0:T(8,128)(2,1)S(1)}, bf16[4,32,1152]{2,1,0:T(8,128)(2,1)S(1)}, bf16[4,32,1152]{2,1,0:T(8,128)(2,1)S(1)}) custom-call(s32[11]{0:T(128)S(1)} %concatenate.15.info, bf16[4,32,1024]{2,1,0:T(8,128)(2,1)S(1)} %pad_maximum_fusion.2.refs_0_, ...), custom_call_target="tpu_custom_call" | custom-call | flops 17179869184 | bytes 4194304 | tf_op jit(solution)/shard_map/attend/pallas_call | solution.py:177
  49.9 6.0 %collective-permute-start.10 = (bf16[4,32,1152]{2,1,0:T(8,128)(2,1)S(1)}, bf16[4,32,1152]{2,1,0:T(8,128)(2,1)S(1)}, u32[]{:S(2)}, u32[]{:S(2)}) collective-permute-start(bf16[4,32,1152]{2,1,0:T(8,128)(2,1)S(1)} %get-tuple-element.40), channel_id=1, source_target_pairs={{0,4},{2,6},{4,0},{6,2},{8,12},{10,14},{12,8},{14,10},{16,20},{18,... | collective-permute-start | bytes 884744 | tf_op jit(solution)/shard_map/ppermute | solution.py:364
  55.8 1.5 collective-permute-start.9
  57.4 11.9 %collective-permute-done.13.refs_2_.refs_1_ = bf16[4,32,3072]{2,1,0:T(8,128)(2,1)S(1)} collective-permute-done((bf16[4,32,3072]{2,1,0:T(8,128)(2,1)S(1)}, bf16[4,32,3072]{2,1,0:T(8,128)(2,1)S(1)}, u32[]{:S(2)}, u32[]{:S(2)}) %collective-permute-start.13) | collective-permute-done | bytes 786464 | tf_op jit(solution)/shard_map/ppermute | solution.py:364
  69.3 16.6 %attend.6 = (bf16[4,32,1152]{2,1,0:T(8,128)(2,1)S(1)}, bf16[4,32,1152]{2,1,0:T(8,128)(2,1)S(1)}, bf16[4,32,1152]{2,1,0:T(8,128)(2,1)S(1)}, bf16[4,32,1152]{2,1,0:T(8,128)(2,1)S(1)}) custom-call(s32[11]{0:T(128)S(1)} %concatenate.15.info, bf16[4,32,3072]{2,1,0:T(8,128)(2,1)S(1)} %pad_maximum_fusion.refs_8_.refs_0_, ...), custom_call_target="tpu_custom_call" | custom-call | flops 17179869184 | bytes 4194304 | tf_op jit(solution)/shard_map/attend/pallas_call | solution.py:177
  85.9 4.1 %collective-permute-start.15 = (bf16[4,32,1152]{2,1,0:T(8,128)(2,1)S(1)}, bf16[4,32,1152]{2,1,0:T(8,128)(2,1)S(1)}, u32[]{:S(2)}, u32[]{:S(2)}) collective-permute-start(bf16[4,32,1152]{2,1,0:T(8,128)(2,1)S(1)} %get-tuple-element.43), channel_id=1, source_target_pairs={{0,2},{2,0},{4,6},{6,4},{8,10},{10,8},{12,14},{14,12},{16,18},{18,... | collective-permute-start | bytes 884744 | tf_op jit(solution)/shard_map/ppermute | solution.py:364
  90.0 3.3 %collective-permute-start.16 = (bf16[4,32,1152]{2,1,0:T(8,128)(2,1)S(1)}, bf16[4,32,1152]{2,1,0:T(8,128)(2,1)S(1)}, u32[]{:S(2)}, u32[]{:S(2)}) collective-permute-start(bf16[4,32,1152]{2,1,0:T(8,128)(2,1)S(1)} %get-tuple-element.44), channel_id=1, source_target_pairs={{0,4},{2,6},{4,0},{6,2},{8,12},{10,14},{12,8},{14,10},{16,20},{18,... | collective-permute-start | bytes 884744 | tf_op jit(solution)/shard_map/ppermute | solution.py:364
  93.4 1.4 collective-permute-start.17
  94.8 16.8 %attend.7 = (bf16[4,32,1152]{2,1,0:T(8,128)(2,1)S(1)}, bf16[4,32,1152]{2,1,0:T(8,128)(2,1)S(1)}, bf16[4,32,1152]{2,1,0:T(8,128)(2,1)S(1)}, bf16[4,32,1152]{2,1,0:T(8,128)(2,1)S(1)}) custom-call(s32[11]{0:T(128)S(1)} %concatenate.15.info, bf16[4,32,3072]{2,1,0:T(8,128)(2,1)S(1)} %pad_maximum_fusion.refs_8_.refs_0_, ...), custom_call_target="tpu_custom_call" | custom-call | flops 17179869184 | bytes 4194304 | tf_op jit(solution)/shard_map/attend/pallas_call | solution.py:177
  111.6 1.7 merge.2
  113.3 8.8 %collective-permute-start.18 = (bf16[32,2304]{1,0:T(8,128)(2,1)S(1)}, bf16[32,2304]{1,0:T(8,128)(2,1)S(1)}, u32[]{:S(2)}, u32[]{:S(2)}) collective-permute-start(bf16[32,2304]{1,0:T(8,128)(2,1)S(1)} %get-tuple-element.48), channel_id=1, source_target_pairs={{0,8},{2,10},{4,12},{6,14},{8,0},{10,2},{12,4},{14,6},{16,24},{18,... | collective-permute-start | bytes 442376 | tf_op jit(solution)/shard_map/ppermute | solution.py:364
  122.1 1.5 collective-permute-start.22
  123.6 6.4 %collective-permute-start.23 = (bf16[4,32,1152]{2,1,0:T(8,128)(2,1)S(1)}, bf16[4,32,1152]{2,1,0:T(8,128)(2,1)S(1)}, u32[]{:S(2)}, u32[]{:S(2)}) collective-permute-start(bf16[4,32,1152]{2,1,0:T(8,128)(2,1)S(1)} %get-tuple-element.53), channel_id=1, source_target_pairs={{0,4},{2,6},{4,0},{6,2},{8,12},{10,14},{12,8},{14,10},{16,20},{18,... | collective-permute-start | bytes 884744 | tf_op jit(solution)/shard_map/ppermute | solution.py:364
  130.0 6.4 %collective-permute-start.19 = (bf16[32,2304]{1,0:T(8,128)(2,1)S(1)}, bf16[32,2304]{1,0:T(8,128)(2,1)S(1)}, u32[]{:S(2)}, u32[]{:S(2)}) collective-permute-start(bf16[32,2304]{1,0:T(8,128)(2,1)S(1)} %get-tuple-element.49), channel_id=1, source_target_pairs={{0,16},{2,18},{4,20},{6,22},{8,24},{10,26},{12,28},{14,30},{16,0},... | collective-permute-start | bytes 442376 | tf_op jit(solution)/shard_map/ppermute | solution.py:364
  136.4 1.4 collective-permute-start.20
  137.8 13.6 %attend.8 = (bf16[4,32,1152]{2,1,0:T(8,128)(2,1)S(1)}, bf16[4,32,1152]{2,1,0:T(8,128)(2,1)S(1)}, bf16[4,32,1152]{2,1,0:T(8,128)(2,1)S(1)}) custom-call(s32[11]{0:T(128)S(1)} %concatenate.15.info, bf16[4,32,3072]{2,1,0:T(8,128)(2,1)S(1)} %collective-permute-done.12.refs_1_.refs_0_, bf16[4,32,3072]{2,1,0:T(8,128)(2,1)S(1)} %collective-permute-done.13.refs_2_.refs_1_, ...), custom_call_target="tpu_custom_call" | custom-call | flops 12884901888 | bytes 3670016 | tf_op jit(solution)/shard_map/attend/pallas_call | solution.py:177
  151.4 0.7 collective-permute-start.25
  152.1 4.5 %collective-permute-start.26 = (bf16[4,32,1152]{2,1,0:T(8,128)(2,1)S(1)}, bf16[4,32,1152]{2,1,0:T(8,128)(2,1)S(1)}, u32[]{:S(2)}, u32[]{:S(2)}) collective-permute-start(bf16[4,32,1152]{2,1,0:T(8,128)(2,1)S(1)} %get-tuple-element.55), channel_id=1, source_target_pairs={{0,4},{2,6},{4,0},{6,2},{8,12},{10,14},{12,8},{14,10},{16,20},{18,... | collective-permute-start | bytes 884744 | tf_op jit(solution)/shard_map/ppermute | solution.py:364
  157.2 1.4 collective-permute-start.27
  158.7 5.0 %collective-permute-start.21 = (bf16[1,32,2048]{2,1,0:T(8,128)(2,1)S(1)}, bf16[1,32,2048]{2,1,0:T(8,128)(2,1)S(1)}, u32[]{:S(2)}, u32[]{:S(2)}) collective-permute-start(bf16[1,32,2048]{2,1,0:T(8,128)(2,1)S(1)} %bitcast.20), channel_id=1, source_target_pairs={{0,16},{2,18},{4,20},{6,22},{8,24},{10,26},{12,28},{14,30},{16,0},... | collective-permute-start | bytes 393224 | tf_op jit(solution)/shard_map/ppermute | solution.py:364
  163.7 5.5 %attend.9.refs_4_.refs_8_ = bf16[4,32,1152]{2,1,0:T(8,128)(2,1)S(1)} custom-call(s32[11]{0:T(128)S(1)} %concatenate.15.info, bf16[4,32,3072]{2,1,0:T(8,128)(2,1)S(1)} %pad_maximum_fusion.refs_8_.refs_0_, bf16[512,4096]{1,0:T(8,128)(2,1)S(1)} %transpose.8.refs_4_.refs_3_.refs_1_, bf16[4096,512]{1,0:T(8,128)(2,1)S(1)} %copy-done.3, ...), custom_call_target="tpu_custom_call" | custom-call | flops 4294967296 | bytes 2621440 | tf_op jit(solution)/shard_map/attend/pallas_call | solution.py:177
  169.3 0.8 collective-permute-start.28
  170.2 8.6 %collective-permute-done.28 = bf16[2,32,2048]{2,1,0:T(8,128)(2,1)S(1)} collective-permute-done((bf16[2,32,2048]{2,1,0:T(8,128)(2,1)S(1)}, bf16[2,32,2048]{2,1,0:T(8,128)(2,1)S(1)}, u32[]{:S(2)}, u32[]{:S(2)}) %collective-permute-start.28) | collective-permute-done | bytes 262176 | tf_op jit(solution)/shard_map/ppermute | solution.py:364
  178.9 0.7 collective-permute-start.32
  179.9 1.7 merge.3
  181.6 1.2 collective-permute-start.29
  182.9 1.4 collective-permute-start.30
  184.2 1.8 collective-permute-start.31
  186.1 3.9 %collective-permute-done.29.refs_1_ = bf16[32,2304]{1,0:T(8,128)(2,1)S(1)} collective-permute-done((bf16[32,2304]{1,0:T(8,128)(2,1)S(1)}, bf16[32,2304]{1,0:T(8,128)(2,1)S(1)}, u32[]{:S(2)}, u32[]{:S(2)}) %collective-permute-start.29) | collective-permute-done | bytes 147488 | tf_op jit(solution)/shard_map/ppermute | solution.py:364
  190.0 3.8 %collective-permute-done.31.refs_3_ = bf16[32,2304]{1,0:T(8,128)(2,1)S(1)} collective-permute-done((bf16[32,2304]{1,0:T(8,128)(2,1)S(1)}, bf16[32,2304]{1,0:T(8,128)(2,1)S(1)}, u32[]{:S(2)}, u32[]{:S(2)}) %collective-permute-start.31) | collective-permute-done | bytes 147488 | tf_op jit(solution)/shard_map/ppermute | solution.py:364
  194.5 1.6 collective-permute-start.34
  196.1 2.5 %collective-permute-start.36 = (bf16[4,32,2048]{2,1,0:T(8,128)(2,1)S(1)}, bf16[4,32,2048]{2,1,0:T(8,128)(2,1)S(1)}, u32[]{:S(2)}, u32[]{:S(2)}) collective-permute-start(bf16[4,32,2048]{2,1,0:T(8,128)(2,1)S(1)} %constant_dynamic-update-slice_fusion.refs_0_), channel_id=1, source_target_pairs={{0,6},{2,4},{4,2},{6,0},{8,14},{10,12},{12,10},{14,8},{16,22},{18,... | collective-permute-start | bytes 1572872 | tf_op jit(solution)/shard_map/ppermute | solution.py:364
  198.6 2.9 %collective-permute-done.34 = bf16[1,32,2048]{2,1,0:T(8,128)(2,1)S(1)} collective-permute-done((bf16[1,32,2048]{2,1,0:T(8,128)(2,1)S(1)}, bf16[1,32,2048]{2,1,0:T(8,128)(2,1)S(1)}, u32[]{:S(2)}, u32[]{:S(2)}) %collective-permute-start.34) | collective-permute-done | bytes 131104 | tf_op jit(solution)/shard_map/ppermute | solution.py:364
  201.6 6.4 %collective-permute-done.35 = bf16[2,32,2048]{2,1,0:T(8,128)(2,1)S(1)} collective-permute-done((bf16[2,32,2048]{2,1,0:T(8,128)(2,1)S(1)}, bf16[2,32,2048]{2,1,0:T(8,128)(2,1)S(1)}, u32[]{:S(2)}, u32[]{:S(2)}) %collective-permute-start.35) | collective-permute-done | bytes 262176 | tf_op jit(solution)/shard_map/ppermute | solution.py:364
  208.0 3.7 %collective-permute-done.36.refs_3_ = bf16[4,32,2048]{2,1,0:T(8,128)(2,1)S(1)} collective-permute-done((bf16[4,32,2048]{2,1,0:T(8,128)(2,1)S(1)}, bf16[4,32,2048]{2,1,0:T(8,128)(2,1)S(1)}, u32[]{:S(2)}, u32[]{:S(2)}) %collective-permute-start.36) | collective-permute-done | bytes 524320 | tf_op jit(solution)/shard_map/ppermute | solution.py:364
  212.0 2.8 %collective-permute-start.37 = (bf16[4,32,2048]{2,1,0:T(8,128)(2,1)S(1)}, bf16[4,32,2048]{2,1,0:T(8,128)(2,1)S(1)}, u32[]{:S(2)}, u32[]{:S(2)}) collective-permute-start(bf16[4,32,2048]{2,1,0:T(8,128)(2,1)S(1)} %pad_maximum_fusion.1.refs_0_), channel_id=1, source_target_pairs={{0,4},{2,6},{4,0},{6,2},{8,12},{10,14},{12,8},{14,10},{16,20},{18,... | collective-permute-start | bytes 1572872 | tf_op jit(solution)/shard_map/ppermute | solution.py:364
  215.2 2.2 copy-done
  217.4 1.9 project.3.refs_3_
  219.3 1.7 collective-permute-done.39.refs_1_
  221.0 2.4 %project.4.refs_3_ = f32[4,4,32,512]{3,2,1,0:T(8,128)S(1)} custom-call(s32[11]{0:T(128)S(1)} %concatenate.15.info, bf16[4,32,2048]{2,1,0:T(8,128)(2,1)S(1)} %pad_maximum_fusion.1.refs_0_, bf16[4,32,2048]{2,1,0:T(8,128)(2,1)} %collective-permute-done.39.refs_1_, bf16[4096,512]{1,0:T(8,128)(2,1)S(1)} %copy-done.1, f32[4,4,32,512]{3,2,1,0:T(8,128)S(1)} %project.3.refs_3_), custom_call_target="tpu_custom_call" | custom-call | flops 536870912 | bytes 3145728 | tf_op jit(solution)/shard_map/project/pallas_call | solution.py:341
  223.4 4.2 %collective-permute-done.37.refs_0_ = bf16[4,32,2048]{2,1,0:T(8,128)(2,1)S(1)} collective-permute-done((bf16[4,32,2048]{2,1,0:T(8,128)(2,1)S(1)}, bf16[4,32,2048]{2,1,0:T(8,128)(2,1)S(1)}, u32[]{:S(2)}, u32[]{:S(2)}) %collective-permute-start.37) | collective-permute-done | bytes 524320 | tf_op jit(solution)/shard_map/ppermute | solution.py:364
  227.6 2.4 %project.5 = bf16[4,4,32,512]{3,2,1,0:T(8,128)(2,1)S(1)} custom-call(s32[11]{0:T(128)S(1)} %concatenate.15.info, bf16[4,32,2048]{2,1,0:T(8,128)(2,1)S(1)} %collective-permute-done.37.refs_0_, bf16[4,32,2048]{2,1,0:T(8,128)(2,1)} %collective-permute-done.38.refs_1_, bf16[4096,512]{1,0:T(8,128)(2,1)S(1)} %copy-done.1, f32[4,4,32,512]{3,2,1,0:T(8,128)S(1)} %project.4.refs_3_), custom_call_target="tpu_custom_call" | custom-call | flops 536870912 | bytes 3145728 | tf_op jit(solution)/shard_map/project/pallas_call | solution.py:341
  230.1 1.5 collective-permute-done.40
  231.7 0.8 add_convert_fusion
  (64 shorter events, 4.1 us)
Async XLA Ops:
  0.9 8.9 %collective-permute-start = (bf16[32,1024]{1,0:T(8,128)(2,1)S(1)}, bf16[32,1024]{1,0:T(8,128)(2,1)S(1)}, u32[]{:S(2)}, u32[]{:S(2)}) collective-permute-start(bf16[32,1024]{1,0:T(8,128)(2,1)S(1)} %get-tuple-element.66), channel_id=1, source_target_pairs={{0,8},{2,10},{4,12},{6,14},{8,0},{10,2},{12,4},{14,6},{16,24},{18,... | collective-permute-start | bytes 196616 | tf_op jit(solution)/shard_map/ppermute | solution.py:364
  3.9 7.3 %collective-permute-start.1 = (bf16[32,1024]{1,0:T(8,128)(2,1)S(1)}, bf16[32,1024]{1,0:T(8,128)(2,1)S(1)}, u32[]{:S(2)}, u32[]{:S(2)}) collective-permute-start(bf16[32,1024]{1,0:T(8,128)(2,1)S(1)} %get-tuple-element.66), channel_id=1, source_target_pairs={{0,16},{2,18},{4,20},{6,22},{8,24},{10,26},{12,28},{14,30},{16,0},... | collective-permute-start | bytes 196616 | tf_op jit(solution)/shard_map/ppermute | solution.py:364
  6.5 6.1 %collective-permute-start.2 = (bf16[32,1024]{1,0:T(8,128)(2,1)S(1)}, bf16[32,1024]{1,0:T(8,128)(2,1)S(1)}, u32[]{:S(2)}, u32[]{:S(2)}) collective-permute-start(bf16[32,1024]{1,0:T(8,128)(2,1)S(1)} %get-tuple-element.66), channel_id=1, source_target_pairs={{0,24},{2,26},{4,28},{6,30},{8,16},{10,18},{12,20},{14,22},{16,8},... | collective-permute-start | bytes 196616 | tf_op jit(solution)/shard_map/ppermute | solution.py:364
  12.6 8.8 %collective-permute-start.6 = (bf16[32,3072]{1,0:T(8,128)(2,1)S(1)}, bf16[32,3072]{1,0:T(8,128)(2,1)S(1)}, u32[]{:S(2)}, u32[]{:S(2)}) collective-permute-start(bf16[32,3072]{1,0:T(8,128)(2,1)S(1)} %slice.7), channel_id=1, source_target_pairs={{0,8},{2,10},{4,12},{6,14},{8,0},{10,2},{12,4},{14,6},{16,24},{18,... | collective-permute-start | bytes 589832 | tf_op jit(solution)/shard_map/ppermute | solution.py:364
  12.7 16.9 %collective-permute-start.7 = (bf16[32,3072]{1,0:T(8,128)(2,1)S(1)}, bf16[32,3072]{1,0:T(8,128)(2,1)S(1)}, u32[]{:S(2)}, u32[]{:S(2)}) collective-permute-start(bf16[32,3072]{1,0:T(8,128)(2,1)S(1)} %slice.7), channel_id=1, source_target_pairs={{0,16},{2,18},{4,20},{6,22},{8,24},{10,26},{12,28},{14,30},{16,0},... | collective-permute-start | bytes 589832 | tf_op jit(solution)/shard_map/ppermute | solution.py:364
  15.1 14.5 %collective-permute-start.8 = (bf16[32,3072]{1,0:T(8,128)(2,1)S(1)}, bf16[32,3072]{1,0:T(8,128)(2,1)S(1)}, u32[]{:S(2)}, u32[]{:S(2)}) collective-permute-start(bf16[32,3072]{1,0:T(8,128)(2,1)S(1)} %slice.7), channel_id=1, source_target_pairs={{0,24},{2,26},{4,28},{6,30},{8,16},{10,18},{12,20},{14,22},{16,8},... | collective-permute-start | bytes 589832 | tf_op jit(solution)/shard_map/ppermute | solution.py:364
  18.5 14.3 %collective-permute-start.3 = (bf16[4,32,1024]{2,1,0:T(8,128)(2,1)S(1)}, bf16[4,32,1024]{2,1,0:T(8,128)(2,1)S(1)}, u32[]{:S(2)}, u32[]{:S(2)}) collective-permute-start(bf16[4,32,1024]{2,1,0:T(8,128)(2,1)S(1)} %pad_maximum_fusion.2.refs_0_), channel_id=1, source_target_pairs={{0,2},{2,0},{4,6},{6,4},{8,10},{10,8},{12,14},{14,12},{16,18},{18,... | collective-permute-start | bytes 786440 | tf_op jit(solution)/shard_map/ppermute | solution.py:364
  20.0 13.3 %collective-permute-start.4 = (bf16[4,32,1024]{2,1,0:T(8,128)(2,1)S(1)}, bf16[4,32,1024]{2,1,0:T(8,128)(2,1)S(1)}, u32[]{:S(2)}, u32[]{:S(2)}) collective-permute-start(bf16[4,32,1024]{2,1,0:T(8,128)(2,1)S(1)} %pad_maximum_fusion.2.refs_0_), channel_id=1, source_target_pairs={{0,4},{2,6},{4,0},{6,2},{8,12},{10,14},{12,8},{14,10},{16,20},{18,... | collective-permute-start | bytes 786440 | tf_op jit(solution)/shard_map/ppermute | solution.py:364
  21.5 11.8 %collective-permute-start.5 = (bf16[4,32,1024]{2,1,0:T(8,128)(2,1)S(1)}, bf16[4,32,1024]{2,1,0:T(8,128)(2,1)S(1)}, u32[]{:S(2)}, u32[]{:S(2)}) collective-permute-start(bf16[4,32,1024]{2,1,0:T(8,128)(2,1)S(1)} %pad_maximum_fusion.2.refs_0_), channel_id=1, source_target_pairs={{0,6},{2,4},{4,2},{6,0},{8,14},{10,12},{12,10},{14,8},{16,22},{18,... | collective-permute-start | bytes 786440 | tf_op jit(solution)/shard_map/ppermute | solution.py:364
  23.0 2.2 copy-start.2
  25.2 8.1 %copy-start.3 = (bf16[4096,512]{1,0:T(8,128)(2,1)S(1)}, bf16[4096,512]{1,0:T(8,128)(2,1)}, u32[]{:S(2)}) copy-start(bf16[4096,512]{1,0:T(8,128)(2,1)} %refs_2_.3) | copy-start | bytes 12582916
  25.2 8.1 %copy-start.4 = (bf16[32,512]{1,0:T(8,128)(2,1)S(1)}, bf16[32,512]{1,0:T(8,128)(2,1)}, u32[]{:S(2)}) copy-start(bf16[32,512]{1,0:T(8,128)(2,1)} %refs_3_.1) | copy-start | bytes 98308
  25.2 8.1 %copy-start.5 = (bf16[32,512]{1,0:T(8,128)(2,1)S(1)}, bf16[32,512]{1,0:T(8,128)(2,1)}, u32[]{:S(2)}) copy-start(bf16[32,512]{1,0:T(8,128)(2,1)} %refs_4_.4) | copy-start | bytes 98308
  29.7 26.1 %collective-permute-start.12 = (bf16[4,32,3072]{2,1,0:T(8,128)(2,1)S(1)}, bf16[4,32,3072]{2,1,0:T(8,128)(2,1)S(1)}, u32[]{:S(2)}, u32[]{:S(2)}) collective-permute-start(bf16[4,32,3072]{2,1,0:T(8,128)(2,1)S(1)} %pad_maximum_fusion.refs_8_.refs_0_), channel_id=1, source_target_pairs={{0,2},{2,0},{4,6},{6,4},{8,10},{10,8},{12,14},{14,12},{16,18},{18,... | collective-permute-start | bytes 2359304 | tf_op jit(solution)/shard_map/ppermute | solution.py:364
  31.3 38.0 %collective-permute-start.13 = (bf16[4,32,3072]{2,1,0:T(8,128)(2,1)S(1)}, bf16[4,32,3072]{2,1,0:T(8,128)(2,1)S(1)}, u32[]{:S(2)}, u32[]{:S(2)}) collective-permute-start(bf16[4,32,3072]{2,1,0:T(8,128)(2,1)S(1)} %pad_maximum_fusion.refs_8_.refs_0_), channel_id=1, source_target_pairs={{0,4},{2,6},{4,0},{6,2},{8,12},{10,14},{12,8},{14,10},{16,20},{18,... | collective-permute-start | bytes 2359304 | tf_op jit(solution)/shard_map/ppermute | solution.py:364
  32.8 36.5 %collective-permute-start.14 = (bf16[4,32,3072]{2,1,0:T(8,128)(2,1)S(1)}, bf16[4,32,3072]{2,1,0:T(8,128)(2,1)S(1)}, u32[]{:S(2)}, u32[]{:S(2)}) collective-permute-start(bf16[4,32,3072]{2,1,0:T(8,128)(2,1)S(1)} %pad_maximum_fusion.refs_8_.refs_0_), channel_id=1, source_target_pairs={{0,6},{2,4},{4,2},{6,0},{8,14},{10,12},{12,10},{14,8},{16,22},{18,... | collective-permute-start | bytes 2359304 | tf_op jit(solution)/shard_map/ppermute | solution.py:364
  49.9 43.5 %collective-permute-start.10 = (bf16[4,32,1152]{2,1,0:T(8,128)(2,1)S(1)}, bf16[4,32,1152]{2,1,0:T(8,128)(2,1)S(1)}, u32[]{:S(2)}, u32[]{:S(2)}) collective-permute-start(bf16[4,32,1152]{2,1,0:T(8,128)(2,1)S(1)} %get-tuple-element.40), channel_id=1, source_target_pairs={{0,4},{2,6},{4,0},{6,2},{8,12},{10,14},{12,8},{14,10},{16,20},{18,... | collective-permute-start | bytes 884744 | tf_op jit(solution)/shard_map/ppermute | solution.py:364
  55.8 55.8 %collective-permute-start.11 = (bf16[4,32,1152]{2,1,0:T(8,128)(2,1)S(1)}, bf16[4,32,1152]{2,1,0:T(8,128)(2,1)S(1)}, u32[]{:S(2)}, u32[]{:S(2)}) collective-permute-start(bf16[4,32,1152]{2,1,0:T(8,128)(2,1)S(1)} %get-tuple-element.41), channel_id=1, source_target_pairs={{0,6},{2,4},{4,2},{6,0},{8,14},{10,12},{12,10},{14,8},{16,22},{18,... | collective-permute-start | bytes 884744 | tf_op jit(solution)/shard_map/ppermute | solution.py:364
  55.8 55.8 %collective-permute-start.9 = (bf16[4,32,1152]{2,1,0:T(8,128)(2,1)S(1)}, bf16[4,32,1152]{2,1,0:T(8,128)(2,1)S(1)}, u32[]{:S(2)}, u32[]{:S(2)}) collective-permute-start(bf16[4,32,1152]{2,1,0:T(8,128)(2,1)S(1)} %get-tuple-element.39), channel_id=1, source_target_pairs={{0,2},{2,0},{4,6},{6,4},{8,10},{10,8},{12,14},{14,12},{16,18},{18,... | collective-permute-start | bytes 884744 | tf_op jit(solution)/shard_map/ppermute | solution.py:364
  85.9 25.7 %collective-permute-start.15 = (bf16[4,32,1152]{2,1,0:T(8,128)(2,1)S(1)}, bf16[4,32,1152]{2,1,0:T(8,128)(2,1)S(1)}, u32[]{:S(2)}, u32[]{:S(2)}) collective-permute-start(bf16[4,32,1152]{2,1,0:T(8,128)(2,1)S(1)} %get-tuple-element.43), channel_id=1, source_target_pairs={{0,2},{2,0},{4,6},{6,4},{8,10},{10,8},{12,14},{14,12},{16,18},{18,... | collective-permute-start | bytes 884744 | tf_op jit(solution)/shard_map/ppermute | solution.py:364
  90.0 21.6 %collective-permute-start.16 = (bf16[4,32,1152]{2,1,0:T(8,128)(2,1)S(1)}, bf16[4,32,1152]{2,1,0:T(8,128)(2,1)S(1)}, u32[]{:S(2)}, u32[]{:S(2)}) collective-permute-start(bf16[4,32,1152]{2,1,0:T(8,128)(2,1)S(1)} %get-tuple-element.44), channel_id=1, source_target_pairs={{0,4},{2,6},{4,0},{6,2},{8,12},{10,14},{12,8},{14,10},{16,20},{18,... | collective-permute-start | bytes 884744 | tf_op jit(solution)/shard_map/ppermute | solution.py:364
  93.4 18.2 %collective-permute-start.17 = (bf16[4,32,1152]{2,1,0:T(8,128)(2,1)S(1)}, bf16[4,32,1152]{2,1,0:T(8,128)(2,1)S(1)}, u32[]{:S(2)}, u32[]{:S(2)}) collective-permute-start(bf16[4,32,1152]{2,1,0:T(8,128)(2,1)S(1)} %get-tuple-element.45), channel_id=1, source_target_pairs={{0,6},{2,4},{4,2},{6,0},{8,14},{10,12},{12,10},{14,8},{16,22},{18,... | collective-permute-start | bytes 884744 | tf_op jit(solution)/shard_map/ppermute | solution.py:364
  113.3 23.1 %collective-permute-start.18 = (bf16[32,2304]{1,0:T(8,128)(2,1)S(1)}, bf16[32,2304]{1,0:T(8,128)(2,1)S(1)}, u32[]{:S(2)}, u32[]{:S(2)}) collective-permute-start(bf16[32,2304]{1,0:T(8,128)(2,1)S(1)} %get-tuple-element.48), channel_id=1, source_target_pairs={{0,8},{2,10},{4,12},{6,14},{8,0},{10,2},{12,4},{14,6},{16,24},{18,... | collective-permute-start | bytes 442376 | tf_op jit(solution)/shard_map/ppermute | solution.py:364
  122.1 35.1 %collective-permute-start.22 = (bf16[4,32,1152]{2,1,0:T(8,128)(2,1)S(1)}, bf16[4,32,1152]{2,1,0:T(8,128)(2,1)S(1)}, u32[]{:S(2)}, u32[]{:S(2)}) collective-permute-start(bf16[4,32,1152]{2,1,0:T(8,128)(2,1)S(1)} %get-tuple-element.52), channel_id=1, source_target_pairs={{0,2},{2,0},{4,6},{6,4},{8,10},{10,8},{12,14},{14,12},{16,18},{18,... | collective-permute-start | bytes 884744 | tf_op jit(solution)/shard_map/ppermute | solution.py:364
  123.6 35.1 %collective-permute-start.23 = (bf16[4,32,1152]{2,1,0:T(8,128)(2,1)S(1)}, bf16[4,32,1152]{2,1,0:T(8,128)(2,1)S(1)}, u32[]{:S(2)}, u32[]{:S(2)}) collective-permute-start(bf16[4,32,1152]{2,1,0:T(8,128)(2,1)S(1)} %get-tuple-element.53), channel_id=1, source_target_pairs={{0,4},{2,6},{4,0},{6,2},{8,12},{10,14},{12,8},{14,10},{16,20},{18,... | collective-permute-start | bytes 884744 | tf_op jit(solution)/shard_map/ppermute | solution.py:364
  130.0 33.7 %collective-permute-start.24 = (bf16[4,32,1152]{2,1,0:T(8,128)(2,1)S(1)}, bf16[4,32,1152]{2,1,0:T(8,128)(2,1)S(1)}, u32[]{:S(2)}, u32[]{:S(2)}) collective-permute-start(bf16[4,32,1152]{2,1,0:T(8,128)(2,1)S(1)} %get-tuple-element.54), channel_id=1, source_target_pairs={{0,6},{2,4},{4,2},{6,0},{8,14},{10,12},{12,10},{14,8},{16,22},{18,... | collective-permute-start | bytes 884744 | tf_op jit(solution)/shard_map/ppermute | solution.py:364
  130.0 21.4 %collective-permute-start.19 = (bf16[32,2304]{1,0:T(8,128)(2,1)S(1)}, bf16[32,2304]{1,0:T(8,128)(2,1)S(1)}, u32[]{:S(2)}, u32[]{:S(2)}) collective-permute-start(bf16[32,2304]{1,0:T(8,128)(2,1)S(1)} %get-tuple-element.49), channel_id=1, source_target_pairs={{0,16},{2,18},{4,20},{6,22},{8,24},{10,26},{12,28},{14,30},{16,0},... | collective-permute-start | bytes 442376 | tf_op jit(solution)/shard_map/ppermute | solution.py:364
  136.4 15.7 %collective-permute-start.20 = (bf16[32,2304]{1,0:T(8,128)(2,1)S(1)}, bf16[32,2304]{1,0:T(8,128)(2,1)S(1)}, u32[]{:S(2)}, u32[]{:S(2)}) collective-permute-start(bf16[32,2304]{1,0:T(8,128)(2,1)S(1)} %get-tuple-element.50), channel_id=1, source_target_pairs={{0,24},{2,26},{4,28},{6,30},{8,16},{10,18},{12,20},{14,22},{16,8},... | collective-permute-start | bytes 442376 | tf_op jit(solution)/shard_map/ppermute | solution.py:364
  151.4 17.9 %collective-permute-start.25 = (bf16[4,32,1152]{2,1,0:T(8,128)(2,1)S(1)}, bf16[4,32,1152]{2,1,0:T(8,128)(2,1)S(1)}, u32[]{:S(2)}, u32[]{:S(2)}) collective-permute-start(bf16[4,32,1152]{2,1,0:T(8,128)(2,1)S(1)} %get-tuple-element.51.refs_4_), channel_id=1, source_target_pairs={{0,2},{2,0},{4,6},{6,4},{8,10},{10,8},{12,14},{14,12},{16,18},{18,... | collective-permute-start | bytes 884744 | tf_op jit(solution)/shard_map/ppermute | solution.py:364
  152.1 17.2 %collective-permute-start.26 = (bf16[4,32,1152]{2,1,0:T(8,128)(2,1)S(1)}, bf16[4,32,1152]{2,1,0:T(8,128)(2,1)S(1)}, u32[]{:S(2)}, u32[]{:S(2)}) collective-permute-start(bf16[4,32,1152]{2,1,0:T(8,128)(2,1)S(1)} %get-tuple-element.55), channel_id=1, source_target_pairs={{0,4},{2,6},{4,0},{6,2},{8,12},{10,14},{12,8},{14,10},{16,20},{18,... | collective-permute-start | bytes 884744 | tf_op jit(solution)/shard_map/ppermute | solution.py:364
  157.2 12.1 %collective-permute-start.27 = (bf16[4,32,1152]{2,1,0:T(8,128)(2,1)S(1)}, bf16[4,32,1152]{2,1,0:T(8,128)(2,1)S(1)}, u32[]{:S(2)}, u32[]{:S(2)}) collective-permute-start(bf16[4,32,1152]{2,1,0:T(8,128)(2,1)S(1)} %get-tuple-element.56), channel_id=1, source_target_pairs={{0,6},{2,4},{4,2},{6,0},{8,14},{10,12},{12,10},{14,8},{16,22},{18,... | collective-permute-start | bytes 884744 | tf_op jit(solution)/shard_map/ppermute | solution.py:364
  158.7 10.6 %collective-permute-start.21 = (bf16[1,32,2048]{2,1,0:T(8,128)(2,1)S(1)}, bf16[1,32,2048]{2,1,0:T(8,128)(2,1)S(1)}, u32[]{:S(2)}, u32[]{:S(2)}) collective-permute-start(bf16[1,32,2048]{2,1,0:T(8,128)(2,1)S(1)} %bitcast.20), channel_id=1, source_target_pairs={{0,16},{2,18},{4,20},{6,22},{8,24},{10,26},{12,28},{14,30},{16,0},... | collective-permute-start | bytes 393224 | tf_op jit(solution)/shard_map/ppermute | solution.py:364
  169.3 9.5 %collective-permute-start.28 = (bf16[2,32,2048]{2,1,0:T(8,128)(2,1)S(1)}, bf16[2,32,2048]{2,1,0:T(8,128)(2,1)S(1)}, u32[]{:S(2)}, u32[]{:S(2)}) collective-permute-start(bf16[2,32,2048]{2,1,0:T(8,128)(2,1)S(1)} %pad_maximum_fusion.3.refs_9_), channel_id=1, source_target_pairs={{0,8},{2,10},{4,12},{6,14},{8,0},{10,2},{12,4},{14,6},{16,24},{18,... | collective-permute-start | bytes 786440 | tf_op jit(solution)/shard_map/ppermute | solution.py:364
  178.9 15.0 %collective-permute-start.32 = (bf16[4,32,2048]{2,1,0:T(8,128)(2,1)S(1)}, bf16[4,32,2048]{2,1,0:T(8,128)(2,1)S(1)}, u32[]{:S(2)}, u32[]{:S(2)}) collective-permute-start(bf16[4,32,2048]{2,1,0:T(8,128)(2,1)S(1)} %constant_dynamic-update-slice_fusion.refs_0_), channel_id=1, source_target_pairs={{0,2},{2,0},{4,6},{6,4},{8,10},{10,8},{12,14},{14,12},{16,18},{18,... | collective-permute-start | bytes 1572872 | tf_op jit(solution)/shard_map/ppermute | solution.py:364
  179.6 14.3 %collective-permute-start.33 = (bf16[4,32,2048]{2,1,0:T(8,128)(2,1)S(1)}, bf16[4,32,2048]{2,1,0:T(8,128)(2,1)S(1)}, u32[]{:S(2)}, u32[]{:S(2)}) collective-permute-start(bf16[4,32,2048]{2,1,0:T(8,128)(2,1)S(1)} %constant_dynamic-update-slice_fusion.refs_0_), channel_id=1, source_target_pairs={{0,4},{2,6},{4,0},{6,2},{8,12},{10,14},{12,8},{14,10},{16,20},{18,... | collective-permute-start | bytes 1572872 | tf_op jit(solution)/shard_map/ppermute | solution.py:364
  181.6 8.4 %collective-permute-start.29 = (bf16[32,2304]{1,0:T(8,128)(2,1)S(1)}, bf16[32,2304]{1,0:T(8,128)(2,1)S(1)}, u32[]{:S(2)}, u32[]{:S(2)}) collective-permute-start(bf16[32,2304]{1,0:T(8,128)(2,1)S(1)} %get-tuple-element.59), channel_id=1, source_target_pairs={{0,8},{2,10},{4,12},{6,14},{8,0},{10,2},{12,4},{14,6},{16,24},{18,... | collective-permute-start | bytes 442376 | tf_op jit(solution)/shard_map/ppermute | solution.py:364
  182.9 7.1 %collective-permute-start.30 = (bf16[32,2304]{1,0:T(8,128)(2,1)S(1)}, bf16[32,2304]{1,0:T(8,128)(2,1)S(1)}, u32[]{:S(2)}, u32[]{:S(2)}) collective-permute-start(bf16[32,2304]{1,0:T(8,128)(2,1)S(1)} %get-tuple-element.60), channel_id=1, source_target_pairs={{0,16},{2,18},{4,20},{6,22},{8,24},{10,26},{12,28},{14,30},{16,0},... | collective-permute-start | bytes 442376 | tf_op jit(solution)/shard_map/ppermute | solution.py:364
  184.2 9.6 %collective-permute-start.31 = (bf16[32,2304]{1,0:T(8,128)(2,1)S(1)}, bf16[32,2304]{1,0:T(8,128)(2,1)S(1)}, u32[]{:S(2)}, u32[]{:S(2)}) collective-permute-start(bf16[32,2304]{1,0:T(8,128)(2,1)S(1)} %get-tuple-element.61), channel_id=1, source_target_pairs={{0,24},{2,26},{4,28},{6,30},{8,16},{10,18},{12,20},{14,22},{16,8},... | collective-permute-start | bytes 442376 | tf_op jit(solution)/shard_map/ppermute | solution.py:364
  194.5 7.0 %collective-permute-start.34 = (bf16[1,32,2048]{2,1,0:T(8,128)(2,1)S(1)}, bf16[1,32,2048]{2,1,0:T(8,128)(2,1)S(1)}, u32[]{:S(2)}, u32[]{:S(2)}) collective-permute-start(bf16[1,32,2048]{2,1,0:T(8,128)(2,1)S(1)} %bitcast.22), channel_id=1, source_target_pairs={{0,16},{2,18},{4,20},{6,22},{8,24},{10,26},{12,28},{14,30},{16,0},... | collective-permute-start | bytes 393224 | tf_op jit(solution)/shard_map/ppermute | solution.py:364
  196.1 15.6 %collective-permute-start.36 = (bf16[4,32,2048]{2,1,0:T(8,128)(2,1)S(1)}, bf16[4,32,2048]{2,1,0:T(8,128)(2,1)S(1)}, u32[]{:S(2)}, u32[]{:S(2)}) collective-permute-start(bf16[4,32,2048]{2,1,0:T(8,128)(2,1)S(1)} %constant_dynamic-update-slice_fusion.refs_0_), channel_id=1, source_target_pairs={{0,6},{2,4},{4,2},{6,0},{8,14},{10,12},{12,10},{14,8},{16,22},{18,... | collective-permute-start | bytes 1572872 | tf_op jit(solution)/shard_map/ppermute | solution.py:364
  201.5 6.4 %collective-permute-start.35 = (bf16[2,32,2048]{2,1,0:T(8,128)(2,1)S(1)}, bf16[2,32,2048]{2,1,0:T(8,128)(2,1)S(1)}, u32[]{:S(2)}, u32[]{:S(2)}) collective-permute-start(bf16[2,32,2048]{2,1,0:T(8,128)(2,1)S(1)} %pad_maximum_fusion.4), channel_id=1, source_target_pairs={{0,8},{2,10},{4,12},{6,14},{8,0},{10,2},{12,4},{14,6},{16,24},{18,... | collective-permute-start | bytes 786440 | tf_op jit(solution)/shard_map/ppermute | solution.py:364
  211.7 9.3 %collective-permute-start.39 = (bf16[4,32,2048]{2,1,0:T(8,128)(2,1)S(1)}, bf16[4,32,2048]{2,1,0:T(8,128)(2,1)}, u32[]{:S(2)}, u32[]{:S(2)}) collective-permute-start(bf16[4,32,2048]{2,1,0:T(8,128)(2,1)S(1)} %pad_maximum_fusion.1.refs_0_), channel_id=1, source_target_pairs={{0,2},{2,0},{4,6},{6,4},{8,10},{10,8},{12,14},{14,12},{16,18},{18,... | collective-permute-start | bytes 1572872 | tf_op jit(solution)/shard_map/ppermute | solution.py:364
  212.0 15.6 %collective-permute-start.37 = (bf16[4,32,2048]{2,1,0:T(8,128)(2,1)S(1)}, bf16[4,32,2048]{2,1,0:T(8,128)(2,1)S(1)}, u32[]{:S(2)}, u32[]{:S(2)}) collective-permute-start(bf16[4,32,2048]{2,1,0:T(8,128)(2,1)S(1)} %pad_maximum_fusion.1.refs_0_), channel_id=1, source_target_pairs={{0,4},{2,6},{4,0},{6,2},{8,12},{10,14},{12,8},{14,10},{16,20},{18,... | collective-permute-start | bytes 1572872 | tf_op jit(solution)/shard_map/ppermute | solution.py:364
  214.8 12.8 %collective-permute-start.38 = (bf16[4,32,2048]{2,1,0:T(8,128)(2,1)S(1)}, bf16[4,32,2048]{2,1,0:T(8,128)(2,1)}, u32[]{:S(2)}, u32[]{:S(2)}) collective-permute-start(bf16[4,32,2048]{2,1,0:T(8,128)(2,1)S(1)} %pad_maximum_fusion.1.refs_0_), channel_id=1, source_target_pairs={{0,6},{2,4},{4,2},{6,0},{8,14},{10,12},{12,10},{14,8},{16,22},{18,... | collective-permute-start | bytes 1572872 | tf_op jit(solution)/shard_map/ppermute | solution.py:364
  215.2 2.2 copy-start
  217.4 3.6 %copy-start.1 = (bf16[4096,512]{1,0:T(8,128)(2,1)S(1)}, bf16[4096,512]{1,0:T(8,128)(2,1)}, u32[]{:S(2)}) copy-start(bf16[4096,512]{1,0:T(8,128)(2,1)} %refs_2_.5) | copy-start | bytes 12582916
  230.1 1.6 collective-permute-start.40

commit v10 on v9

--- a/solution.py
+++ b/solution.py
@@ -170,7 +170,7 @@
     key_count = values.shape[0]
     group_step = min(GROUP_QUERIES, 2 * (plane // count))
     tile_rows = group_step * count * rows
-    key_chunk = min(key_count, 512)
+    key_chunk = min(key_count, 256)
     vmem = pltpu.MemorySpace.VMEM
     span_block = pl.BlockSpec((rows, HEAD_SIZE), lambda i, s: (0, head))
     scored = blocks * count * rows * GROUP_QUERIES * key_count
@@ -319,12 +319,17 @@
     )(*pieces, *after)
 
 
-def project_kernel(info, *refs, order, chosen, rows, width):
-    ins, (w_ref, *base_ref, out) = refs[: len(chosen)], refs[len(chosen) :]
+def project_kernel(info, *refs, order, chosen, parts, rows):
+    ins, (w_ref, *base_ref, out) = list(refs[: sum(parts)]), refs[sum(parts) :]
     out[...] = base_ref[0][...].astype(out.dtype) if base_ref else jnp.zeros_like(out)
-    for x_ref, b in zip(ins, chosen):
-        x = x_ref[...].reshape(len(order) * rows, width)
-        y = jnp.dot(x, w_ref[...], preferred_element_type=F32)
+    for b, count in zip(chosen, parts):
+        y, first = 0.0, 0
+        for _ in range(count):
+            x_ref = ins.pop(0)
+            width = x_ref.shape[-1]
+            x = x_ref[...].reshape(len(order) * rows, width)
+            y = y + jnp.dot(x, w_ref[first : first + width], preferred_element_type=F32)
+            first += width
         for n, a in enumerate(order):
             at = (info[3 + len(order) + a], b ^ info[1])
             part = y[n * rows : (n + 1) * rows]
@@ -333,17 +338,19 @@
 
 def project(info, pieces, order, chosen, weight, group, base, dtype):
     plane = len(pieces)
-    blocks, rows, width = pieces[0].shape
+    blocks, rows, width = pieces[0][0].shape
     out_cols = weight.shape[1]
     span = len(chosen) * blocks * rows
-    whole = pl.BlockSpec((blocks, rows, width), lambda i, s: (0, 0, 0))
+    arrays = [x for b in chosen for x in pieces[b]]
     out_block = pl.BlockSpec((blocks, plane, rows, out_cols), lambda i, s: (0, 0, 0, 0))
     return pl.pallas_call(
-        functools.partial(project_kernel, order=order, chosen=chosen, rows=rows, width=width),
+        functools.partial(
+            project_kernel, order=order, chosen=chosen, parts=[len(pieces[b]) for b in chosen], rows=rows
+        ),
         grid_spec=pltpu.PrefetchScalarGridSpec(
             num_scalar_prefetch=1,
             grid=(1,),
-            in_specs=[whole] * len(chosen)
+            in_specs=[pl.BlockSpec(x.shape, lambda i, s: (0, 0, 0)) for x in arrays]
             + [pl.BlockSpec((width, out_cols), lambda i, s: (group, 0))]
             + [out_block] * len(base),
             out_specs=out_block,
@@ -356,7 +363,7 @@
             transcendentals=0,
         ),
         name="project",
-    )(info, *[pieces[b] for b in chosen], weight, *base)
+    )(info, *arrays, weight, *base)
 
 
 def exchange(x, axis, distance):
@@ -396,6 +403,14 @@
 
     def gather_plane(stack):
         return [stack] + [exchange(stack, "ctx", b) for b in range(1, plane)]
+
+    def gather_rows(stack):
+        if plane != 4:
+            return [[x] for x in gather_plane(stack)]
+        near = [exchange(stack, "ctx", 1), exchange(stack, "ctx", 2)]
+        half = stack.shape[-1] // 2
+        far = [exchange(near[0][..., :half], "ctx", 2), exchange(near[1][..., half:], "ctx", 1)]
+        return [[stack], [near[0]], [near[1]], far]
 
     first = stack_blocks(queries[:, :width])
     sources, stacks = [(gather_plane(first), 0)], []
@@ -469,8 +484,8 @@
     while len(rows_of) < heads // size:
         after = gather_round()
         if columns and not columns[0][2]:
-            gathered = [gather_plane(after[0])]
-            after = [gathered[0][b] for b in (1, 2) if b < plane]
+            gathered = [gather_rows(after[0])]
+            after = [x for b in (1, 2) if b < plane for x in gathered[0][b]]
         latest = normalize(latest + after)
     while any(distance for _, _, distance in columns) or len(columns) < len(rows_of):
         gather_round()
@@ -479,12 +494,12 @@
     for g, (stack, order, _) in enumerate(columns):
         if g:
             stack, _ = lax.optimization_barrier((stack, pieces))
-        pieces = gathered.pop() if gathered else gather_plane(stack)
+        pieces = gathered.pop() if gathered else gather_rows(stack)
         if g < len(rows_of) - 1:
             total = [project(info, pieces, order, range(plane), out_weight, g, total, F32)]
         else:
-            total = [project(info, pieces, order, range(plane // 2), out_weight, g, total, F32)]
-            total = [project(info, pieces, order, range(plane // 2, plane), out_weight, g, total, BF16)]
+            total = [project(info, pieces, order, range(plane - 1), out_weight, g, total, F32)]
+            total = [project(info, pieces, order, range(plane - 1, plane), out_weight, g, total, BF16)]
     partial_out = total[0].reshape(ctx_count * rows, -1)
     share = partial_out.shape[0] // head_count
     total = lax.dynamic_slice_in_dim(partial_out, my_head * share, share, 0).astype(F32)

time: 232 us -> 236 us (1.017)
  starting transfers between devices: 84.8 us -> 90.3 us
  waiting for transfers between devices: 54.3 us -> 49.1 us
  local copies, waits for them, and re-layouts: 7.59 us -> 12.7 us
    ppermute x41 -> x43, starting transfers between devices: 84.8 us -> 90.3 us  [exchange(): return lax.ppermute(x, axis, [(i, i ^ distance) for i in range(count)])]
    ppermute x41 -> x43, waiting for transfers between devices: 54.3 us -> 49.1 us  [exchange(): return lax.ppermute(x, axis, [(i, i ^ distance) for i in range(count)])]
    unnamed x13 -> x21, local copies, waits for them, and re-layouts: 4.41 us -> 8.03 us
  transfers between devices with their start and end apart: 41 -> 43, of which waited for: 13 -> 14; matrix products, arithmetic and copies ran while one was open for 2% -> 3% of each run, Pallas kernels for 33% -> 32%
where the time goes in v10:
time: 236 us
  starting transfers between devices  90.3 us (38%)
  Pallas kernels  80.6 us (34%)
  waiting for transfers between devices  49.1 us (21%)
  local copies, waits for them, and re-layouts  12.7 us (5%)
  other arithmetic  3.34 us (1%)
    ppermute x43, starting transfers between devices, exchange(): return lax.ppermute(x, axis, [(i, i ^ distance) for i in range(count)])  90.3 us
    pallas_call x5, Pallas kernels, attend_head(): pl.pallas_call(functools.partial(attend_kernel, chosen=chosen, blocks=blo...  68.7 us
    ppermute x43, waiting for transfers between devices, exchange(): return lax.ppermute(x, axis, [(i, i ^ distance) for i in range(count)])  49.1 us
    unnamed x21, local copies, waits for them, and re-layouts  8.03 us
    pallas_call x3, Pallas kernels, project(): pl.pallas_call(functools.partial(project_kernel, order=order, chosen=chos...  5.52 us
  transfers between devices with their start and end apart: 43, of which 14 were waited for; matrix products, arithmetic and copies ran while one was open for 3% of the time, Pallas kernels for 32%

profile of v10, /device:TPU:0, one launch (start us, length us, event | category | flops | bytes accessed | tf_op | source)
XLA Modules:
  0.0 236.4 jit_solution(14665742182909634782)
XLA Ops:
  0.0 0.8 slice_bitcast_fusion
  0.9 3.1 %collective-permute-start = (bf16[32,1024]{1,0:T(8,128)(2,1)S(1)}, bf16[32,1024]{1,0:T(8,128)(2,1)S(1)}, u32[]{:S(2)}, u32[]{:S(2)}) collective-permute-start(bf16[32,1024]{1,0:T(8,128)(2,1)S(1)} %get-tuple-element.66), channel_id=1, source_target_pairs={{0,8},{2,10},{4,12},{6,14},{8,0},{10,2},{12,4},{14,6},{16,24},{18,... | collective-permute-start | bytes 196616 | tf_op jit(solution)/shard_map/ppermute | solution.py:371
  3.9 2.6 %collective-permute-start.1 = (bf16[32,1024]{1,0:T(8,128)(2,1)S(1)}, bf16[32,1024]{1,0:T(8,128)(2,1)S(1)}, u32[]{:S(2)}, u32[]{:S(2)}) collective-permute-start(bf16[32,1024]{1,0:T(8,128)(2,1)S(1)} %get-tuple-element.66), channel_id=1, source_target_pairs={{0,16},{2,18},{4,20},{6,22},{8,24},{10,26},{12,28},{14,30},{16,0},... | collective-permute-start | bytes 196616 | tf_op jit(solution)/shard_map/ppermute | solution.py:371
  6.5 0.9 slice.19
  7.5 0.8 compare_reduce_fusion
  8.3 0.6 gather_fusion
  9.0 0.8 sort.17
  9.8 1.4 collective-permute-done.1
  11.2 1.4 collective-permute-done.2
  12.7 2.3 collective-permute-start.7
  15.1 2.0 collective-permute-start.8
  17.1 0.7 convert_reduce_fusion
  17.8 0.7 concatenate.15.info
  18.5 1.5 collective-permute-start.3
  20.0 1.5 collective-permute-start.4
  21.5 1.5 collective-permute-start.5
  23.0 2.2 copy-done.2
  25.2 1.7 transpose.8.refs_4_.refs_3_.refs_1_
  26.9 2.7 %collective-permute-done.7 = bf16[32,3072]{1,0:T(8,128)(2,1)S(1)} collective-permute-done((bf16[32,3072]{1,0:T(8,128)(2,1)S(1)}, bf16[32,3072]{1,0:T(8,128)(2,1)S(1)}, u32[]{:S(2)}, u32[]{:S(2)}) %collective-permute-start.7) | collective-permute-done | bytes 196640 | tf_op jit(solution)/shard_map/ppermute | solution.py:371
  29.7 1.6 collective-permute-start.12
  31.3 1.5 collective-permute-start.13
  33.3 16.0 %attend.5 = (bf16[4,32,1152]{2,1,0:T(8,128)(2,1)S(1)}, bf16[4,32,1152]{2,1,0:T(8,128)(2,1)S(1)}, bf16[4,32,1152]{2,1,0:T(8,128)(2,1)S(1)}, bf16[4,32,1152]{2,1,0:T(8,128)(2,1)S(1)}) custom-call(s32[11]{0:T(128)S(1)} %concatenate.15.info, bf16[4,32,1024]{2,1,0:T(8,128)(2,1)S(1)} %pad_maximum_fusion.2.refs_0_, ...), custom_call_target="tpu_custom_call" | custom-call | flops 17179869184 | bytes 4194304 | tf_op jit(solution)/shard_map/attend/pallas_call | solution.py:177
  49.3 1.6 collective-permute-start.10
  50.9 9.2 %collective-permute-start.11 = (bf16[4,32,1152]{2,1,0:T(8,128)(2,1)S(1)}, bf16[4,32,1152]{2,1,0:T(8,128)(2,1)S(1)}, u32[]{:S(2)}, u32[]{:S(2)}) collective-permute-start(bf16[4,32,1152]{2,1,0:T(8,128)(2,1)S(1)} %get-tuple-element.41), channel_id=1, source_target_pairs={{0,6},{2,4},{4,2},{6,0},{8,14},{10,12},{12,10},{14,8},{16,22},{18,... | collective-permute-start | bytes 884744 | tf_op jit(solution)/shard_map/ppermute | solution.py:371
  60.7 12.2 %collective-permute-done.13.refs_2_.refs_1_ = bf16[4,32,3072]{2,1,0:T(8,128)(2,1)S(1)} collective-permute-done((bf16[4,32,3072]{2,1,0:T(8,128)(2,1)S(1)}, bf16[4,32,3072]{2,1,0:T(8,128)(2,1)S(1)}, u32[]{:S(2)}, u32[]{:S(2)}) %collective-permute-start.13) | collective-permute-done | bytes 786464 | tf_op jit(solution)/shard_map/ppermute | solution.py:371
  72.8 16.1 %attend.6 = (bf16[4,32,1152]{2,1,0:T(8,128)(2,1)S(1)}, bf16[4,32,1152]{2,1,0:T(8,128)(2,1)S(1)}, bf16[4,32,1152]{2,1,0:T(8,128)(2,1)S(1)}, bf16[4,32,1152]{2,1,0:T(8,128)(2,1)S(1)}) custom-call(s32[11]{0:T(128)S(1)} %concatenate.15.info, bf16[4,32,3072]{2,1,0:T(8,128)(2,1)S(1)} %pad_maximum_fusion.refs_8_.refs_0_, ...), custom_call_target="tpu_custom_call" | custom-call | flops 17179869184 | bytes 4194304 | tf_op jit(solution)/shard_map/attend/pallas_call | solution.py:177
  89.0 7.2 %collective-permute-start.16 = (bf16[4,32,1152]{2,1,0:T(8,128)(2,1)S(1)}, bf16[4,32,1152]{2,1,0:T(8,128)(2,1)S(1)}, u32[]{:S(2)}, u32[]{:S(2)}) collective-permute-start(bf16[4,32,1152]{2,1,0:T(8,128)(2,1)S(1)} %get-tuple-element.44), channel_id=1, source_target_pairs={{0,4},{2,6},{4,0},{6,2},{8,12},{10,14},{12,8},{14,10},{16,20},{18,... | collective-permute-start | bytes 884744 | tf_op jit(solution)/shard_map/ppermute | solution.py:371
  96.2 16.3 %attend.7 = (bf16[4,32,1152]{2,1,0:T(8,128)(2,1)S(1)}, bf16[4,32,1152]{2,1,0:T(8,128)(2,1)S(1)}, bf16[4,32,1152]{2,1,0:T(8,128)(2,1)S(1)}, bf16[4,32,1152]{2,1,0:T(8,128)(2,1)S(1)}) custom-call(s32[11]{0:T(128)S(1)} %concatenate.15.info, bf16[4,32,3072]{2,1,0:T(8,128)(2,1)S(1)} %pad_maximum_fusion.refs_8_.refs_0_, ...), custom_call_target="tpu_custom_call" | custom-call | flops 17179869184 | bytes 4194304 | tf_op jit(solution)/shard_map/attend/pallas_call | solution.py:177
  112.6 1.7 merge.2
  114.2 13.0 %collective-permute-start.18 = (bf16[32,2304]{1,0:T(8,128)(2,1)S(1)}, bf16[32,2304]{1,0:T(8,128)(2,1)S(1)}, u32[]{:S(2)}, u32[]{:S(2)}) collective-permute-start(bf16[32,2304]{1,0:T(8,128)(2,1)S(1)} %get-tuple-element.48), channel_id=1, source_target_pairs={{0,8},{2,10},{4,12},{6,14},{8,0},{10,2},{12,4},{14,6},{16,24},{18,... | collective-permute-start | bytes 442376 | tf_op jit(solution)/shard_map/ppermute | solution.py:371
  127.9 2.9 %collective-permute-start.24 = (bf16[4,32,1152]{2,1,0:T(8,128)(2,1)S(1)}, bf16[4,32,1152]{2,1,0:T(8,128)(2,1)S(1)}, u32[]{:S(2)}, u32[]{:S(2)}) collective-permute-start(bf16[4,32,1152]{2,1,0:T(8,128)(2,1)S(1)} %get-tuple-element.54), channel_id=1, source_target_pairs={{0,6},{2,4},{4,2},{6,0},{8,14},{10,12},{12,10},{14,8},{16,22},{18,... | collective-permute-start | bytes 884744 | tf_op jit(solution)/shard_map/ppermute | solution.py:371
  130.8 2.4 %collective-permute-start.20 = (bf16[32,2304]{1,0:T(8,128)(2,1)S(1)}, bf16[32,2304]{1,0:T(8,128)(2,1)S(1)}, u32[]{:S(2)}, u32[]{:S(2)}) collective-permute-start(bf16[32,2304]{1,0:T(8,128)(2,1)S(1)} %get-tuple-element.50), channel_id=1, source_target_pairs={{0,24},{2,26},{4,28},{6,30},{8,16},{10,18},{12,20},{14,22},{16,8},... | collective-permute-start | bytes 442376 | tf_op jit(solution)/shard_map/ppermute | solution.py:371
  133.2 14.9 %attend.8 = (bf16[4,32,1152]{2,1,0:T(8,128)(2,1)S(1)}, bf16[4,32,1152]{2,1,0:T(8,128)(2,1)S(1)}, bf16[4,32,1152]{2,1,0:T(8,128)(2,1)S(1)}) custom-call(s32[11]{0:T(128)S(1)} %concatenate.15.info, bf16[4,32,3072]{2,1,0:T(8,128)(2,1)S(1)} %collective-permute-done.12.refs_1_.refs_0_, bf16[4,32,3072]{2,1,0:T(8,128)(2,1)S(1)} %collective-permute-done.13.refs_2_.refs_1_, ...), custom_call_target="tpu_custom_call" | custom-call | flops 12884901888 | bytes 3670016 | tf_op jit(solution)/shard_map/attend/pallas_call | solution.py:177
  148.1 1.1 collective-permute-start.25
  149.2 9.1 %collective-permute-start.26 = (bf16[4,32,1152]{2,1,0:T(8,128)(2,1)S(1)}, bf16[4,32,1152]{2,1,0:T(8,128)(2,1)S(1)}, u32[]{:S(2)}, u32[]{:S(2)}) collective-permute-start(bf16[4,32,1152]{2,1,0:T(8,128)(2,1)S(1)} %get-tuple-element.55), channel_id=1, source_target_pairs={{0,4},{2,6},{4,0},{6,2},{8,12},{10,14},{12,8},{14,10},{16,20},{18,... | collective-permute-start | bytes 884744 | tf_op jit(solution)/shard_map/ppermute | solution.py:371
  159.1 1.5 collective-permute-start.21
  160.6 5.4 %attend.9.refs_4_.refs_8_ = bf16[4,32,1152]{2,1,0:T(8,128)(2,1)S(1)} custom-call(s32[11]{0:T(128)S(1)} %concatenate.15.info, bf16[4,32,3072]{2,1,0:T(8,128)(2,1)S(1)} %pad_maximum_fusion.refs_8_.refs_0_, bf16[512,4096]{1,0:T(8,128)(2,1)S(1)} %transpose.8.refs_4_.refs_3_.refs_1_, bf16[4096,512]{1,0:T(8,128)(2,1)S(1)} %copy-done.7, ...), custom_call_target="tpu_custom_call" | custom-call | flops 4294967296 | bytes 2621440 | tf_op jit(solution)/shard_map/attend/pallas_call | solution.py:177
  166.7 2.6 %collective-permute-start.28 = (bf16[2,32,2048]{2,1,0:T(8,128)(2,1)S(1)}, bf16[2,32,2048]{2,1,0:T(8,128)(2,1)S(1)}, u32[]{:S(2)}, u32[]{:S(2)}) collective-permute-start(bf16[2,32,2048]{2,1,0:T(8,128)(2,1)S(1)} %pad_maximum_fusion.3.refs_9_), channel_id=1, source_target_pairs={{0,8},{2,10},{4,12},{6,14},{8,0},{10,2},{12,4},{14,6},{16,24},{18,... | collective-permute-start | bytes 786440 | tf_op jit(solution)/shard_map/ppermute | solution.py:371
  169.4 6.9 %collective-permute-done.28 = bf16[2,32,2048]{2,1,0:T(8,128)(2,1)S(1)} collective-permute-done((bf16[2,32,2048]{2,1,0:T(8,128)(2,1)S(1)}, bf16[2,32,2048]{2,1,0:T(8,128)(2,1)S(1)}, u32[]{:S(2)}, u32[]{:S(2)}) %collective-permute-start.28) | collective-permute-done | bytes 262176 | tf_op jit(solution)/shard_map/ppermute | solution.py:371
  176.7 4.3 %collective-permute-start.33 = (bf16[4,32,2048]{2,1,0:T(8,128)(2,1)S(1)}, bf16[4,32,2048]{2,1,0:T(8,128)(2,1)S(1)}, u32[]{:S(2)}, u32[]{:S(2)}) collective-permute-start(bf16[4,32,2048]{2,1,0:T(8,128)(2,1)S(1)} %constant_dynamic-update-slice_fusion.refs_0_), channel_id=1, source_target_pairs={{0,4},{2,6},{4,0},{6,2},{8,12},{10,14},{12,8},{14,10},{16,20},{18,... | collective-permute-start | bytes 1572872 | tf_op jit(solution)/shard_map/ppermute | solution.py:371
  181.0 1.7 merge.3
  183.0 4.2 %collective-permute-start.31 = (bf16[32,2304]{1,0:T(8,128)(2,1)S(1)}, bf16[32,2304]{1,0:T(8,128)(2,1)S(1)}, u32[]{:S(2)}, u32[]{:S(2)}) collective-permute-start(bf16[32,2304]{1,0:T(8,128)(2,1)S(1)} %get-tuple-element.61), channel_id=1, source_target_pairs={{0,24},{2,26},{4,28},{6,30},{8,16},{10,18},{12,20},{14,22},{16,8},... | collective-permute-start | bytes 442376 | tf_op jit(solution)/shard_map/ppermute | solution.py:371
  187.1 2.8 %collective-permute-done.29.refs_1_ = bf16[32,2304]{1,0:T(8,128)(2,1)S(1)} collective-permute-done((bf16[32,2304]{1,0:T(8,128)(2,1)S(1)}, bf16[32,2304]{1,0:T(8,128)(2,1)S(1)}, u32[]{:S(2)}, u32[]{:S(2)}) %collective-permute-start.29) | collective-permute-done | bytes 147488 | tf_op jit(solution)/shard_map/ppermute | solution.py:371
  189.9 3.8 %collective-permute-done.31.refs_3_ = bf16[32,2304]{1,0:T(8,128)(2,1)S(1)} collective-permute-done((bf16[32,2304]{1,0:T(8,128)(2,1)S(1)}, bf16[32,2304]{1,0:T(8,128)(2,1)S(1)}, u32[]{:S(2)}, u32[]{:S(2)}) %collective-permute-start.31) | collective-permute-done | bytes 147488 | tf_op jit(solution)/shard_map/ppermute | solution.py:371
  194.4 6.3 %collective-permute-done.34 = bf16[1,32,2048]{2,1,0:T(8,128)(2,1)S(1)} collective-permute-done((bf16[1,32,2048]{2,1,0:T(8,128)(2,1)S(1)}, bf16[1,32,2048]{2,1,0:T(8,128)(2,1)S(1)}, u32[]{:S(2)}, u32[]{:S(2)}) %collective-permute-start.34) | collective-permute-done | bytes 131104 | tf_op jit(solution)/shard_map/ppermute | solution.py:371
  201.0 2.4 collective-permute-start.37
  203.3 3.9 %collective-permute-done.35 = bf16[2,32,2048]{2,1,0:T(8,128)(2,1)S(1)} collective-permute-done((bf16[2,32,2048]{2,1,0:T(8,128)(2,1)S(1)}, bf16[2,32,2048]{2,1,0:T(8,128)(2,1)S(1)}, u32[]{:S(2)}, u32[]{:S(2)}) %collective-permute-start.35) | collective-permute-done | bytes 262176 | tf_op jit(solution)/shard_map/ppermute | solution.py:371
  207.8 0.7 copy-done.3
  208.5 0.7 copy-done.5
  209.2 1.7 collective-permute-start.38
  210.9 2.5 %collective-permute-start.40 = (bf16[4,32,2048]{2,1,0:T(8,128)(2,1)S(1)}, bf16[4,32,2048]{2,1,0:T(8,128)(2,1)S(1)}, u32[]{:S(2)}, u32[]{:S(2)}) collective-permute-start(bf16[4,32,2048]{2,1,0:T(8,128)(2,1)S(1)} %pad_maximum_fusion.1.refs_0_), channel_id=1, source_target_pairs={{0,4},{2,6},{4,0},{6,2},{8,12},{10,14},{12,8},{14,10},{16,20},{18,... | collective-permute-start | bytes 1572872 | tf_op jit(solution)/shard_map/ppermute | solution.py:371
  213.4 5.0 %collective-permute-done.38.refs_1_ = bf16[4,32,2048]{2,1,0:T(8,128)(2,1)S(1)} collective-permute-done((bf16[4,32,2048]{2,1,0:T(8,128)(2,1)S(1)}, bf16[4,32,2048]{2,1,0:T(8,128)(2,1)S(1)}, u32[]{:S(2)}, u32[]{:S(2)}) %collective-permute-start.38) | collective-permute-done | bytes 524320 | tf_op jit(solution)/shard_map/ppermute | solution.py:371
  218.4 0.7 slice.28
  219.1 2.2 collective-permute-start.39
  221.3 0.7 slice.29
  222.0 2.0 collective-permute-start.41
  224.1 2.2 copy-done
  226.2 0.9 copy-done.4
  227.2 0.9 copy-done.6
  228.1 1.9 project.3.refs_4_
  230.3 1.6 project.4.refs_3_
  232.0 2.0 project.5
  234.1 1.5 collective-permute-done.42
  235.6 0.8 add_convert_fusion
  (80 shorter events, 6.0 us)
Async XLA Ops:
  0.9 8.9 %collective-permute-start = (bf16[32,1024]{1,0:T(8,128)(2,1)S(1)}, bf16[32,1024]{1,0:T(8,128)(2,1)S(1)}, u32[]{:S(2)}, u32[]{:S(2)}) collective-permute-start(bf16[32,1024]{1,0:T(8,128)(2,1)S(1)} %get-tuple-element.66), channel_id=1, source_target_pairs={{0,8},{2,10},{4,12},{6,14},{8,0},{10,2},{12,4},{14,6},{16,24},{18,... | collective-permute-start | bytes 196616 | tf_op jit(solution)/shard_map/ppermute | solution.py:371
  3.9 7.3 %collective-permute-start.1 = (bf16[32,1024]{1,0:T(8,128)(2,1)S(1)}, bf16[32,1024]{1,0:T(8,128)(2,1)S(1)}, u32[]{:S(2)}, u32[]{:S(2)}) collective-permute-start(bf16[32,1024]{1,0:T(8,128)(2,1)S(1)} %get-tuple-element.66), channel_id=1, source_target_pairs={{0,16},{2,18},{4,20},{6,22},{8,24},{10,26},{12,28},{14,30},{16,0},... | collective-permute-start | bytes 196616 | tf_op jit(solution)/shard_map/ppermute | solution.py:371
  6.5 6.1 %collective-permute-start.2 = (bf16[32,1024]{1,0:T(8,128)(2,1)S(1)}, bf16[32,1024]{1,0:T(8,128)(2,1)S(1)}, u32[]{:S(2)}, u32[]{:S(2)}) collective-permute-start(bf16[32,1024]{1,0:T(8,128)(2,1)S(1)} %get-tuple-element.66), channel_id=1, source_target_pairs={{0,24},{2,26},{4,28},{6,30},{8,16},{10,18},{12,20},{14,22},{16,8},... | collective-permute-start | bytes 196616 | tf_op jit(solution)/shard_map/ppermute | solution.py:371
  12.6 8.9 %collective-permute-start.6 = (bf16[32,3072]{1,0:T(8,128)(2,1)S(1)}, bf16[32,3072]{1,0:T(8,128)(2,1)S(1)}, u32[]{:S(2)}, u32[]{:S(2)}) collective-permute-start(bf16[32,3072]{1,0:T(8,128)(2,1)S(1)} %slice.19), channel_id=1, source_target_pairs={{0,8},{2,10},{4,12},{6,14},{8,0},{10,2},{12,4},{14,6},{16,24},{18,... | collective-permute-start | bytes 589832 | tf_op jit(solution)/shard_map/ppermute | solution.py:371
  12.7 16.9 %collective-permute-start.7 = (bf16[32,3072]{1,0:T(8,128)(2,1)S(1)}, bf16[32,3072]{1,0:T(8,128)(2,1)S(1)}, u32[]{:S(2)}, u32[]{:S(2)}) collective-permute-start(bf16[32,3072]{1,0:T(8,128)(2,1)S(1)} %slice.19), channel_id=1, source_target_pairs={{0,16},{2,18},{4,20},{6,22},{8,24},{10,26},{12,28},{14,30},{16,0},... | collective-permute-start | bytes 589832 | tf_op jit(solution)/shard_map/ppermute | solution.py:371
  15.1 14.5 %collective-permute-start.8 = (bf16[32,3072]{1,0:T(8,128)(2,1)S(1)}, bf16[32,3072]{1,0:T(8,128)(2,1)S(1)}, u32[]{:S(2)}, u32[]{:S(2)}) collective-permute-start(bf16[32,3072]{1,0:T(8,128)(2,1)S(1)} %slice.19), channel_id=1, source_target_pairs={{0,24},{2,26},{4,28},{6,30},{8,16},{10,18},{12,20},{14,22},{16,8},... | collective-permute-start | bytes 589832 | tf_op jit(solution)/shard_map/ppermute | solution.py:371
  18.5 14.3 %collective-permute-start.3 = (bf16[4,32,1024]{2,1,0:T(8,128)(2,1)S(1)}, bf16[4,32,1024]{2,1,0:T(8,128)(2,1)S(1)}, u32[]{:S(2)}, u32[]{:S(2)}) collective-permute-start(bf16[4,32,1024]{2,1,0:T(8,128)(2,1)S(1)} %pad_maximum_fusion.2.refs_0_), channel_id=1, source_target_pairs={{0,2},{2,0},{4,6},{6,4},{8,10},{10,8},{12,14},{14,12},{16,18},{18,... | collective-permute-start | bytes 786440 | tf_op jit(solution)/shard_map/ppermute | solution.py:371
  20.0 13.3 %collective-permute-start.4 = (bf16[4,32,1024]{2,1,0:T(8,128)(2,1)S(1)}, bf16[4,32,1024]{2,1,0:T(8,128)(2,1)S(1)}, u32[]{:S(2)}, u32[]{:S(2)}) collective-permute-start(bf16[4,32,1024]{2,1,0:T(8,128)(2,1)S(1)} %pad_maximum_fusion.2.refs_0_), channel_id=1, source_target_pairs={{0,4},{2,6},{4,0},{6,2},{8,12},{10,14},{12,8},{14,10},{16,20},{18,... | collective-permute-start | bytes 786440 | tf_op jit(solution)/shard_map/ppermute | solution.py:371
  21.5 11.7 %collective-permute-start.5 = (bf16[4,32,1024]{2,1,0:T(8,128)(2,1)S(1)}, bf16[4,32,1024]{2,1,0:T(8,128)(2,1)S(1)}, u32[]{:S(2)}, u32[]{:S(2)}) collective-permute-start(bf16[4,32,1024]{2,1,0:T(8,128)(2,1)S(1)} %pad_maximum_fusion.2.refs_0_), channel_id=1, source_target_pairs={{0,6},{2,4},{4,2},{6,0},{8,14},{10,12},{12,10},{14,8},{16,22},{18,... | collective-permute-start | bytes 786440 | tf_op jit(solution)/shard_map/ppermute | solution.py:371
  23.0 2.2 copy-start.2
  25.2 8.1 %copy-start.7 = (bf16[4096,512]{1,0:T(8,128)(2,1)S(1)}, bf16[4096,512]{1,0:T(8,128)(2,1)}, u32[]{:S(2)}) copy-start(bf16[4096,512]{1,0:T(8,128)(2,1)} %refs_2_.2) | copy-start | bytes 12582916
  25.2 8.1 %copy-start.8 = (bf16[32,512]{1,0:T(8,128)(2,1)S(1)}, bf16[32,512]{1,0:T(8,128)(2,1)}, u32[]{:S(2)}) copy-start(bf16[32,512]{1,0:T(8,128)(2,1)} %refs_3_.2) | copy-start | bytes 98308
  25.2 8.1 %copy-start.9 = (bf16[32,512]{1,0:T(8,128)(2,1)S(1)}, bf16[32,512]{1,0:T(8,128)(2,1)}, u32[]{:S(2)}) copy-start(bf16[32,512]{1,0:T(8,128)(2,1)} %refs_4_.3) | copy-start | bytes 98308
  29.7 30.5 %collective-permute-start.12 = (bf16[4,32,3072]{2,1,0:T(8,128)(2,1)S(1)}, bf16[4,32,3072]{2,1,0:T(8,128)(2,1)S(1)}, u32[]{:S(2)}, u32[]{:S(2)}) collective-permute-start(bf16[4,32,3072]{2,1,0:T(8,128)(2,1)S(1)} %pad_maximum_fusion.refs_8_.refs_0_), channel_id=1, source_target_pairs={{0,2},{2,0},{4,6},{6,4},{8,10},{10,8},{12,14},{14,12},{16,18},{18,... | collective-permute-start | bytes 2359304 | tf_op jit(solution)/shard_map/ppermute | solution.py:371
  31.3 41.6 %collective-permute-start.13 = (bf16[4,32,3072]{2,1,0:T(8,128)(2,1)S(1)}, bf16[4,32,3072]{2,1,0:T(8,128)(2,1)S(1)}, u32[]{:S(2)}, u32[]{:S(2)}) collective-permute-start(bf16[4,32,3072]{2,1,0:T(8,128)(2,1)S(1)} %pad_maximum_fusion.refs_8_.refs_0_), channel_id=1, source_target_pairs={{0,4},{2,6},{4,0},{6,2},{8,12},{10,14},{12,8},{14,10},{16,20},{18,... | collective-permute-start | bytes 2359304 | tf_op jit(solution)/shard_map/ppermute | solution.py:371
  32.8 40.0 %collective-permute-start.14 = (bf16[4,32,3072]{2,1,0:T(8,128)(2,1)S(1)}, bf16[4,32,3072]{2,1,0:T(8,128)(2,1)S(1)}, u32[]{:S(2)}, u32[]{:S(2)}) collective-permute-start(bf16[4,32,3072]{2,1,0:T(8,128)(2,1)S(1)} %pad_maximum_fusion.refs_8_.refs_0_), channel_id=1, source_target_pairs={{0,6},{2,4},{4,2},{6,0},{8,14},{10,12},{12,10},{14,8},{16,22},{18,... | collective-permute-start | bytes 2359304 | tf_op jit(solution)/shard_map/ppermute | solution.py:371
  49.3 46.9 %collective-permute-start.10 = (bf16[4,32,1152]{2,1,0:T(8,128)(2,1)S(1)}, bf16[4,32,1152]{2,1,0:T(8,128)(2,1)S(1)}, u32[]{:S(2)}, u32[]{:S(2)}) collective-permute-start(bf16[4,32,1152]{2,1,0:T(8,128)(2,1)S(1)} %get-tuple-element.40), channel_id=1, source_target_pairs={{0,4},{2,6},{4,0},{6,2},{8,12},{10,14},{12,8},{14,10},{16,20},{18,... | collective-permute-start | bytes 884744 | tf_op jit(solution)/shard_map/ppermute | solution.py:371
  50.9 61.6 %collective-permute-start.11 = (bf16[4,32,1152]{2,1,0:T(8,128)(2,1)S(1)}, bf16[4,32,1152]{2,1,0:T(8,128)(2,1)S(1)}, u32[]{:S(2)}, u32[]{:S(2)}) collective-permute-start(bf16[4,32,1152]{2,1,0:T(8,128)(2,1)S(1)} %get-tuple-element.41), channel_id=1, source_target_pairs={{0,6},{2,4},{4,2},{6,0},{8,14},{10,12},{12,10},{14,8},{16,22},{18,... | collective-permute-start | bytes 884744 | tf_op jit(solution)/shard_map/ppermute | solution.py:371
  60.2 52.3 %collective-permute-start.9 = (bf16[4,32,1152]{2,1,0:T(8,128)(2,1)S(1)}, bf16[4,32,1152]{2,1,0:T(8,128)(2,1)S(1)}, u32[]{:S(2)}, u32[]{:S(2)}) collective-permute-start(bf16[4,32,1152]{2,1,0:T(8,128)(2,1)S(1)} %get-tuple-element.39), channel_id=1, source_target_pairs={{0,2},{2,0},{4,6},{6,4},{8,10},{10,8},{12,14},{14,12},{16,18},{18,... | collective-permute-start | bytes 884744 | tf_op jit(solution)/shard_map/ppermute | solution.py:371
  88.9 23.6 %collective-permute-start.15 = (bf16[4,32,1152]{2,1,0:T(8,128)(2,1)S(1)}, bf16[4,32,1152]{2,1,0:T(8,128)(2,1)S(1)}, u32[]{:S(2)}, u32[]{:S(2)}) collective-permute-start(bf16[4,32,1152]{2,1,0:T(8,128)(2,1)S(1)} %get-tuple-element.43), channel_id=1, source_target_pairs={{0,2},{2,0},{4,6},{6,4},{8,10},{10,8},{12,14},{14,12},{16,18},{18,... | collective-permute-start | bytes 884744 | tf_op jit(solution)/shard_map/ppermute | solution.py:371
  89.0 23.5 %collective-permute-start.16 = (bf16[4,32,1152]{2,1,0:T(8,128)(2,1)S(1)}, bf16[4,32,1152]{2,1,0:T(8,128)(2,1)S(1)}, u32[]{:S(2)}, u32[]{:S(2)}) collective-permute-start(bf16[4,32,1152]{2,1,0:T(8,128)(2,1)S(1)} %get-tuple-element.44), channel_id=1, source_target_pairs={{0,4},{2,6},{4,0},{6,2},{8,12},{10,14},{12,8},{14,10},{16,20},{18,... | collective-permute-start | bytes 884744 | tf_op jit(solution)/shard_map/ppermute | solution.py:371
  96.2 16.3 %collective-permute-start.17 = (bf16[4,32,1152]{2,1,0:T(8,128)(2,1)S(1)}, bf16[4,32,1152]{2,1,0:T(8,128)(2,1)S(1)}, u32[]{:S(2)}, u32[]{:S(2)}) collective-permute-start(bf16[4,32,1152]{2,1,0:T(8,128)(2,1)S(1)} %get-tuple-element.45), channel_id=1, source_target_pairs={{0,6},{2,4},{4,2},{6,0},{8,14},{10,12},{12,10},{14,8},{16,22},{18,... | collective-permute-start | bytes 884744 | tf_op jit(solution)/shard_map/ppermute | solution.py:371
  114.2 16.5 %collective-permute-start.18 = (bf16[32,2304]{1,0:T(8,128)(2,1)S(1)}, bf16[32,2304]{1,0:T(8,128)(2,1)S(1)}, u32[]{:S(2)}, u32[]{:S(2)}) collective-permute-start(bf16[32,2304]{1,0:T(8,128)(2,1)S(1)} %get-tuple-element.48), channel_id=1, source_target_pairs={{0,8},{2,10},{4,12},{6,14},{8,0},{10,2},{12,4},{14,6},{16,24},{18,... | collective-permute-start | bytes 442376 | tf_op jit(solution)/shard_map/ppermute | solution.py:371
  127.3 31.7 %collective-permute-start.22 = (bf16[4,32,1152]{2,1,0:T(8,128)(2,1)S(1)}, bf16[4,32,1152]{2,1,0:T(8,128)(2,1)S(1)}, u32[]{:S(2)}, u32[]{:S(2)}) collective-permute-start(bf16[4,32,1152]{2,1,0:T(8,128)(2,1)S(1)} %get-tuple-element.52), channel_id=1, source_target_pairs={{0,2},{2,0},{4,6},{6,4},{8,10},{10,8},{12,14},{14,12},{16,18},{18,... | collective-permute-start | bytes 884744 | tf_op jit(solution)/shard_map/ppermute | solution.py:371
  127.3 31.8 %collective-permute-start.23 = (bf16[4,32,1152]{2,1,0:T(8,128)(2,1)S(1)}, bf16[4,32,1152]{2,1,0:T(8,128)(2,1)S(1)}, u32[]{:S(2)}, u32[]{:S(2)}) collective-permute-start(bf16[4,32,1152]{2,1,0:T(8,128)(2,1)S(1)} %get-tuple-element.53), channel_id=1, source_target_pairs={{0,4},{2,6},{4,0},{6,2},{8,12},{10,14},{12,8},{14,10},{16,20},{18,... | collective-permute-start | bytes 884744 | tf_op jit(solution)/shard_map/ppermute | solution.py:371
  127.9 32.7 %collective-permute-start.24 = (bf16[4,32,1152]{2,1,0:T(8,128)(2,1)S(1)}, bf16[4,32,1152]{2,1,0:T(8,128)(2,1)S(1)}, u32[]{:S(2)}, u32[]{:S(2)}) collective-permute-start(bf16[4,32,1152]{2,1,0:T(8,128)(2,1)S(1)} %get-tuple-element.54), channel_id=1, source_target_pairs={{0,6},{2,4},{4,2},{6,0},{8,14},{10,12},{12,10},{14,8},{16,22},{18,... | collective-permute-start | bytes 884744 | tf_op jit(solution)/shard_map/ppermute | solution.py:371
  130.7 17.4 %collective-permute-start.19 = (bf16[32,2304]{1,0:T(8,128)(2,1)S(1)}, bf16[32,2304]{1,0:T(8,128)(2,1)S(1)}, u32[]{:S(2)}, u32[]{:S(2)}) collective-permute-start(bf16[32,2304]{1,0:T(8,128)(2,1)S(1)} %get-tuple-element.49), channel_id=1, source_target_pairs={{0,16},{2,18},{4,20},{6,22},{8,24},{10,26},{12,28},{14,30},{16,0},... | collective-permute-start | bytes 442376 | tf_op jit(solution)/shard_map/ppermute | solution.py:371
  130.8 18.5 %collective-permute-start.20 = (bf16[32,2304]{1,0:T(8,128)(2,1)S(1)}, bf16[32,2304]{1,0:T(8,128)(2,1)S(1)}, u32[]{:S(2)}, u32[]{:S(2)}) collective-permute-start(bf16[32,2304]{1,0:T(8,128)(2,1)S(1)} %get-tuple-element.50), channel_id=1, source_target_pairs={{0,24},{2,26},{4,28},{6,30},{8,16},{10,18},{12,20},{14,22},{16,8},... | collective-permute-start | bytes 442376 | tf_op jit(solution)/shard_map/ppermute | solution.py:371
  148.1 18.3 %collective-permute-start.25 = (bf16[4,32,1152]{2,1,0:T(8,128)(2,1)S(1)}, bf16[4,32,1152]{2,1,0:T(8,128)(2,1)S(1)}, u32[]{:S(2)}, u32[]{:S(2)}) collective-permute-start(bf16[4,32,1152]{2,1,0:T(8,128)(2,1)S(1)} %get-tuple-element.51.refs_4_), channel_id=1, source_target_pairs={{0,2},{2,0},{4,6},{6,4},{8,10},{10,8},{12,14},{14,12},{16,18},{18,... | collective-permute-start | bytes 884744 | tf_op jit(solution)/shard_map/ppermute | solution.py:371
  149.2 17.2 %collective-permute-start.26 = (bf16[4,32,1152]{2,1,0:T(8,128)(2,1)S(1)}, bf16[4,32,1152]{2,1,0:T(8,128)(2,1)S(1)}, u32[]{:S(2)}, u32[]{:S(2)}) collective-permute-start(bf16[4,32,1152]{2,1,0:T(8,128)(2,1)S(1)} %get-tuple-element.55), channel_id=1, source_target_pairs={{0,4},{2,6},{4,0},{6,2},{8,12},{10,14},{12,8},{14,10},{16,20},{18,... | collective-permute-start | bytes 884744 | tf_op jit(solution)/shard_map/ppermute | solution.py:371
  159.0 7.7 %collective-permute-start.27 = (bf16[4,32,1152]{2,1,0:T(8,128)(2,1)S(1)}, bf16[4,32,1152]{2,1,0:T(8,128)(2,1)S(1)}, u32[]{:S(2)}, u32[]{:S(2)}) collective-permute-start(bf16[4,32,1152]{2,1,0:T(8,128)(2,1)S(1)} %get-tuple-element.56), channel_id=1, source_target_pairs={{0,6},{2,4},{4,2},{6,0},{8,14},{10,12},{12,10},{14,8},{16,22},{18,... | collective-permute-start | bytes 884744 | tf_op jit(solution)/shard_map/ppermute | solution.py:371
  159.1 7.3 %collective-permute-start.21 = (bf16[1,32,2048]{2,1,0:T(8,128)(2,1)S(1)}, bf16[1,32,2048]{2,1,0:T(8,128)(2,1)S(1)}, u32[]{:S(2)}, u32[]{:S(2)}) collective-permute-start(bf16[1,32,2048]{2,1,0:T(8,128)(2,1)S(1)} %bitcast.20), channel_id=1, source_target_pairs={{0,16},{2,18},{4,20},{6,22},{8,24},{10,26},{12,28},{14,30},{16,0},... | collective-permute-start | bytes 393224 | tf_op jit(solution)/shard_map/ppermute | solution.py:371
  166.7 9.6 %collective-permute-start.28 = (bf16[2,32,2048]{2,1,0:T(8,128)(2,1)S(1)}, bf16[2,32,2048]{2,1,0:T(8,128)(2,1)S(1)}, u32[]{:S(2)}, u32[]{:S(2)}) collective-permute-start(bf16[2,32,2048]{2,1,0:T(8,128)(2,1)S(1)} %pad_maximum_fusion.3.refs_9_), channel_id=1, source_target_pairs={{0,8},{2,10},{4,12},{6,14},{8,0},{10,2},{12,4},{14,6},{16,24},{18,... | collective-permute-start | bytes 786440 | tf_op jit(solution)/shard_map/ppermute | solution.py:371
  176.3 17.4 %collective-permute-start.32 = (bf16[4,32,2048]{2,1,0:T(8,128)(2,1)S(1)}, bf16[4,32,2048]{2,1,0:T(8,128)(2,1)S(1)}, u32[]{:S(2)}, u32[]{:S(2)}) collective-permute-start(bf16[4,32,2048]{2,1,0:T(8,128)(2,1)S(1)} %constant_dynamic-update-slice_fusion.refs_0_), channel_id=1, source_target_pairs={{0,2},{2,0},{4,6},{6,4},{8,10},{10,8},{12,14},{14,12},{16,18},{18,... | collective-permute-start | bytes 1572872 | tf_op jit(solution)/shard_map/ppermute | solution.py:371
  176.7 17.0 %collective-permute-start.33 = (bf16[4,32,2048]{2,1,0:T(8,128)(2,1)S(1)}, bf16[4,32,2048]{2,1,0:T(8,128)(2,1)S(1)}, u32[]{:S(2)}, u32[]{:S(2)}) collective-permute-start(bf16[4,32,2048]{2,1,0:T(8,128)(2,1)S(1)} %constant_dynamic-update-slice_fusion.refs_0_), channel_id=1, source_target_pairs={{0,4},{2,6},{4,0},{6,2},{8,12},{10,14},{12,8},{14,10},{16,20},{18,... | collective-permute-start | bytes 1572872 | tf_op jit(solution)/shard_map/ppermute | solution.py:371
  182.7 7.2 %collective-permute-start.29 = (bf16[32,2304]{1,0:T(8,128)(2,1)S(1)}, bf16[32,2304]{1,0:T(8,128)(2,1)S(1)}, u32[]{:S(2)}, u32[]{:S(2)}) collective-permute-start(bf16[32,2304]{1,0:T(8,128)(2,1)S(1)} %get-tuple-element.59), channel_id=1, source_target_pairs={{0,8},{2,10},{4,12},{6,14},{8,0},{10,2},{12,4},{14,6},{16,24},{18,... | collective-permute-start | bytes 442376 | tf_op jit(solution)/shard_map/ppermute | solution.py:371
  182.8 7.2 %collective-permute-start.30 = (bf16[32,2304]{1,0:T(8,128)(2,1)S(1)}, bf16[32,2304]{1,0:T(8,128)(2,1)S(1)}, u32[]{:S(2)}, u32[]{:S(2)}) collective-permute-start(bf16[32,2304]{1,0:T(8,128)(2,1)S(1)} %get-tuple-element.60), channel_id=1, source_target_pairs={{0,16},{2,18},{4,20},{6,22},{8,24},{10,26},{12,28},{14,30},{16,0},... | collective-permute-start | bytes 442376 | tf_op jit(solution)/shard_map/ppermute | solution.py:371
  183.0 10.8 %collective-permute-start.31 = (bf16[32,2304]{1,0:T(8,128)(2,1)S(1)}, bf16[32,2304]{1,0:T(8,128)(2,1)S(1)}, u32[]{:S(2)}, u32[]{:S(2)}) collective-permute-start(bf16[32,2304]{1,0:T(8,128)(2,1)S(1)} %get-tuple-element.61), channel_id=1, source_target_pairs={{0,24},{2,26},{4,28},{6,30},{8,16},{10,18},{12,20},{14,22},{16,8},... | collective-permute-start | bytes 442376 | tf_op jit(solution)/shard_map/ppermute | solution.py:371
  194.4 6.4 %collective-permute-start.34 = (bf16[1,32,2048]{2,1,0:T(8,128)(2,1)S(1)}, bf16[1,32,2048]{2,1,0:T(8,128)(2,1)S(1)}, u32[]{:S(2)}, u32[]{:S(2)}) collective-permute-start(bf16[1,32,2048]{2,1,0:T(8,128)(2,1)S(1)} %bitcast.22), channel_id=1, source_target_pairs={{0,16},{2,18},{4,20},{6,22},{8,24},{10,26},{12,28},{14,30},{16,0},... | collective-permute-start | bytes 393224 | tf_op jit(solution)/shard_map/ppermute | solution.py:371
  200.8 6.4 %collective-permute-start.35 = (bf16[2,32,2048]{2,1,0:T(8,128)(2,1)S(1)}, bf16[2,32,2048]{2,1,0:T(8,128)(2,1)S(1)}, u32[]{:S(2)}, u32[]{:S(2)}) collective-permute-start(bf16[2,32,2048]{2,1,0:T(8,128)(2,1)S(1)} %pad_maximum_fusion.4), channel_id=1, source_target_pairs={{0,8},{2,10},{4,12},{6,14},{8,0},{10,2},{12,4},{14,6},{16,24},{18,... | collective-permute-start | bytes 786440 | tf_op jit(solution)/shard_map/ppermute | solution.py:371
  200.9 6.9 %collective-permute-start.36 = (bf16[4,32,1024]{2,1,0:T(8,128)(2,1)S(1)}, bf16[4,32,1024]{2,1,0:T(8,128)(2,1)S(1)}, u32[]{:S(2)}, u32[]{:S(2)}) collective-permute-start(bf16[4,32,1024]{2,1,0:T(8,128)(2,1)S(1)} %slice.26), channel_id=1, source_target_pairs={{0,4},{2,6},{4,0},{6,2},{8,12},{10,14},{12,8},{14,10},{16,20},{18,... | collective-permute-start | bytes 786440 | tf_op jit(solution)/shard_map/ppermute | solution.py:371
  201.0 7.5 %collective-permute-start.37 = (bf16[4,32,1024]{2,1,0:T(8,128)(2,1)S(1)}, bf16[4,32,1024]{2,1,0:T(8,128)(2,1)S(1)}, u32[]{:S(2)}, u32[]{:S(2)}) collective-permute-start(bf16[4,32,1024]{2,1,0:T(8,128)(2,1)S(1)} %slice.27), channel_id=1, source_target_pairs={{0,2},{2,0},{4,6},{6,4},{8,10},{10,8},{12,14},{14,12},{16,18},{18,... | collective-permute-start | bytes 786440 | tf_op jit(solution)/shard_map/ppermute | solution.py:371
  207.8 0.7 copy-start.3
  208.5 0.7 copy-start.5
  209.2 9.2 %collective-permute-start.38 = (bf16[4,32,2048]{2,1,0:T(8,128)(2,1)S(1)}, bf16[4,32,2048]{2,1,0:T(8,128)(2,1)S(1)}, u32[]{:S(2)}, u32[]{:S(2)}) collective-permute-start(bf16[4,32,2048]{2,1,0:T(8,128)(2,1)S(1)} %pad_maximum_fusion.1.refs_0_), channel_id=1, source_target_pairs={{0,2},{2,0},{4,6},{6,4},{8,10},{10,8},{12,14},{14,12},{16,18},{18,... | collective-permute-start | bytes 1572872 | tf_op jit(solution)/shard_map/ppermute | solution.py:371
  210.9 10.4 %collective-permute-start.40 = (bf16[4,32,2048]{2,1,0:T(8,128)(2,1)S(1)}, bf16[4,32,2048]{2,1,0:T(8,128)(2,1)S(1)}, u32[]{:S(2)}, u32[]{:S(2)}) collective-permute-start(bf16[4,32,2048]{2,1,0:T(8,128)(2,1)S(1)} %pad_maximum_fusion.1.refs_0_), channel_id=1, source_target_pairs={{0,4},{2,6},{4,0},{6,2},{8,12},{10,14},{12,8},{14,10},{16,20},{18,... | collective-permute-start | bytes 1572872 | tf_op jit(solution)/shard_map/ppermute | solution.py:371
  219.1 12.9 %collective-permute-start.39 = (bf16[4,32,1024]{2,1,0:T(8,128)(2,1)}, bf16[4,32,1024]{2,1,0:T(8,128)(2,1)S(1)}, u32[]{:S(2)}, u32[]{:S(2)}) collective-permute-start(bf16[4,32,1024]{2,1,0:T(8,128)(2,1)} %slice.28), channel_id=1, source_target_pairs={{0,4},{2,6},{4,0},{6,2},{8,12},{10,14},{12,8},{14,10},{16,20},{18,... | collective-permute-start | bytes 786440 | tf_op jit(solution)/shard_map/ppermute | solution.py:371
  222.0 10.0 %collective-permute-start.41 = (bf16[4,32,1024]{2,1,0:T(8,128)(2,1)}, bf16[4,32,1024]{2,1,0:T(8,128)(2,1)}, u32[]{:S(2)}, u32[]{:S(2)}) collective-permute-start(bf16[4,32,1024]{2,1,0:T(8,128)(2,1)} %slice.29), channel_id=1, source_target_pairs={{0,2},{2,0},{4,6},{6,4},{8,10},{10,8},{12,14},{14,12},{16,18},{18,... | collective-permute-start | bytes 786440 | tf_op jit(solution)/shard_map/ppermute | solution.py:371
  224.0 2.2 copy-start
  226.2 0.9 copy-start.4
  227.2 0.9 copy-start.6
  228.1 2.2 copy-start.1
  234.0 1.6 collective-permute-start.42

commit v11 on v9

--- a/solution.py
+++ b/solution.py
@@ -146,11 +146,15 @@
             peak = score_chunk(q, peak, j)
         shift_ref[...] = shift_of(peak)
 
-        def body(t, _):
-            step(t, jnp.minimum(t + 1, tiles - 1))
+        unroll = 2 if steps % 2 == 0 and tile_rows % 256 == 0 else 1
+
+        def body(i, _):
+            for n in range(unroll):
+                t = i * unroll + n
+                step(t, jnp.minimum(t + 1, tiles - 1))
             return 0
 
-        lax.fori_loop(0, tiles, body, 0)
+        lax.fori_loop(0, lax.div(tiles, unroll), body, 0)
 
     def span_only(t, _):
         scores = span_scores(load_queries(t), t)
@@ -170,7 +174,7 @@
     key_count = values.shape[0]
     group_step = min(GROUP_QUERIES, 2 * (plane // count))
     tile_rows = group_step * count * rows
-    key_chunk = min(key_count, 512)
+    key_chunk = min(key_count, 256 if tile_rows % 256 == 0 else 512)
     vmem = pltpu.MemorySpace.VMEM
     span_block = pl.BlockSpec((rows, HEAD_SIZE), lambda i, s: (0, head))
     scored = blocks * count * rows * GROUP_QUERIES * key_count

time: 232 us -> 239 us (1.030)
  waiting for transfers between devices: 54.3 us -> 46.6 us
  starting transfers between devices: 84.8 us -> 92.1 us
  Pallas kernels: 82.1 us -> 88.7 us
    ppermute x41, waiting for transfers between devices: 54.3 us -> 46.6 us  [exchange(): return lax.ppermute(x, axis, [(i, i ^ distance) for i in range(count)])]
    ppermute x41, starting transfers between devices: 84.8 us -> 92.1 us  [exchange(): return lax.ppermute(x, axis, [(i, i ^ distance) for i in range(count)])]
    pallas_call x5, Pallas kernels: 69.1 us -> 75.7 us  [attend_head(): pl.pallas_call(functools.partial(attend_kernel, chosen=chosen, blocks=blo...]
  transfers between devices with their start and end apart: 41 -> 41, of which waited for: 13 -> 18; matrix products, arithmetic and copies ran while one was open for 2% -> 2% of each run, Pallas kernels for 33% -> 35%
where the time goes in v11:
time: 239 us
  starting transfers between devices  92.1 us (39%)
  Pallas kernels  88.7 us (37%)
  waiting for transfers between devices  46.6 us (19%)
  local copies, waits for them, and re-layouts  7.59 us (3%)
  other arithmetic  3.26 us (1%)
    ppermute x41, starting transfers between devices, exchange(): return lax.ppermute(x, axis, [(i, i ^ distance) for i in range(count)])  92.1 us
    pallas_call x5, Pallas kernels, attend_head(): pl.pallas_call(functools.partial(attend_kernel, chosen=chosen, blocks=blo...  75.7 us
    ppermute x41, waiting for transfers between devices, exchange(): return lax.ppermute(x, axis, [(i, i ^ distance) for i in range(count)])  46.6 us
    pallas_call x3, Pallas kernels, project(): pl.pallas_call(functools.partial(project_kernel, order=order, chosen=chos...  6.72 us
  transfers between devices with their start and end apart: 41, of which 18 were waited for; matrix products, arithmetic and copies ran while one was open for 2% of the time, Pallas kernels for 35%

profile of v11, /device:TPU:0, one launch (start us, length us, event | category | flops | bytes accessed | tf_op | source)
XLA Modules:
  0.0 238.6 jit_solution(10662797340591012053)
XLA Ops:
  0.0 0.8 slice_bitcast_fusion
  0.9 3.1 %collective-permute-start = (bf16[32,1024]{1,0:T(8,128)(2,1)S(1)}, bf16[32,1024]{1,0:T(8,128)(2,1)S(1)}, u32[]{:S(2)}, u32[]{:S(2)}) collective-permute-start(bf16[32,1024]{1,0:T(8,128)(2,1)S(1)} %get-tuple-element.66), channel_id=1, source_target_pairs={{0,8},{2,10},{4,12},{6,14},{8,0},{10,2},{12,4},{14,6},{16,24},{18,... | collective-permute-start | bytes 196616 | tf_op jit(solution)/shard_map/ppermute | solution.py:368
  3.9 2.6 %collective-permute-start.1 = (bf16[32,1024]{1,0:T(8,128)(2,1)S(1)}, bf16[32,1024]{1,0:T(8,128)(2,1)S(1)}, u32[]{:S(2)}, u32[]{:S(2)}) collective-permute-start(bf16[32,1024]{1,0:T(8,128)(2,1)S(1)} %get-tuple-element.66), channel_id=1, source_target_pairs={{0,16},{2,18},{4,20},{6,22},{8,24},{10,26},{12,28},{14,30},{16,0},... | collective-permute-start | bytes 196616 | tf_op jit(solution)/shard_map/ppermute | solution.py:368
  6.5 0.9 slice.7
  7.5 0.8 compare_reduce_fusion
  9.0 0.8 sort.17
  9.7 1.5 collective-permute-done.1
  11.2 1.4 collective-permute-done.2
  12.7 2.3 collective-permute-start.7
  15.1 2.0 collective-permute-start.8
  17.1 0.7 convert_reduce_fusion
  17.8 0.7 concatenate.15.info
  18.5 1.5 collective-permute-start.3
  20.0 1.5 collective-permute-start.4
  21.5 1.5 collective-permute-start.5
  23.0 2.2 copy-done.2
  25.2 1.7 transpose.8.refs_4_.refs_3_.refs_1_
  26.9 2.7 %collective-permute-done.7 = bf16[32,3072]{1,0:T(8,128)(2,1)S(1)} collective-permute-done((bf16[32,3072]{1,0:T(8,128)(2,1)S(1)}, bf16[32,3072]{1,0:T(8,128)(2,1)S(1)}, u32[]{:S(2)}, u32[]{:S(2)}) %collective-permute-start.7) | collective-permute-done | bytes 196640 | tf_op jit(solution)/shard_map/ppermute | solution.py:368
  29.7 1.6 collective-permute-start.12
  31.3 1.5 collective-permute-start.13
  33.3 18.8 %attend.5 = (bf16[4,32,1152]{2,1,0:T(8,128)(2,1)S(1)}, bf16[4,32,1152]{2,1,0:T(8,128)(2,1)S(1)}, bf16[4,32,1152]{2,1,0:T(8,128)(2,1)S(1)}, bf16[4,32,1152]{2,1,0:T(8,128)(2,1)S(1)}) custom-call(s32[11]{0:T(128)S(1)} %concatenate.15.info, bf16[4,32,1024]{2,1,0:T(8,128)(2,1)S(1)} %pad_maximum_fusion.2.refs_0_, ...), custom_call_target="tpu_custom_call" | custom-call | flops 17179869184 | bytes 4194304 | tf_op jit(solution)/shard_map/attend/pallas_call | solution.py:181
  52.1 7.1 %collective-permute-start.10 = (bf16[4,32,1152]{2,1,0:T(8,128)(2,1)S(1)}, bf16[4,32,1152]{2,1,0:T(8,128)(2,1)S(1)}, u32[]{:S(2)}, u32[]{:S(2)}) collective-permute-start(bf16[4,32,1152]{2,1,0:T(8,128)(2,1)S(1)} %get-tuple-element.40), channel_id=1, source_target_pairs={{0,4},{2,6},{4,0},{6,2},{8,12},{10,14},{12,8},{14,10},{16,20},{18,... | collective-permute-start | bytes 884744 | tf_op jit(solution)/shard_map/ppermute | solution.py:368
  59.1 6.9 %collective-permute-start.11 = (bf16[4,32,1152]{2,1,0:T(8,128)(2,1)S(1)}, bf16[4,32,1152]{2,1,0:T(8,128)(2,1)S(1)}, u32[]{:S(2)}, u32[]{:S(2)}) collective-permute-start(bf16[4,32,1152]{2,1,0:T(8,128)(2,1)S(1)} %get-tuple-element.41), channel_id=1, source_target_pairs={{0,6},{2,4},{4,2},{6,0},{8,14},{10,12},{12,10},{14,8},{16,22},{18,... | collective-permute-start | bytes 884744 | tf_op jit(solution)/shard_map/ppermute | solution.py:368
  66.1 3.2 %collective-permute-done.13.refs_2_.refs_1_ = bf16[4,32,3072]{2,1,0:T(8,128)(2,1)S(1)} collective-permute-done((bf16[4,32,3072]{2,1,0:T(8,128)(2,1)S(1)}, bf16[4,32,3072]{2,1,0:T(8,128)(2,1)S(1)}, u32[]{:S(2)}, u32[]{:S(2)}) %collective-permute-start.13) | collective-permute-done | bytes 786464 | tf_op jit(solution)/shard_map/ppermute | solution.py:368
  69.3 19.1 %attend.6 = (bf16[4,32,1152]{2,1,0:T(8,128)(2,1)S(1)}, bf16[4,32,1152]{2,1,0:T(8,128)(2,1)S(1)}, bf16[4,32,1152]{2,1,0:T(8,128)(2,1)S(1)}, bf16[4,32,1152]{2,1,0:T(8,128)(2,1)S(1)}) custom-call(s32[11]{0:T(128)S(1)} %concatenate.15.info, bf16[4,32,3072]{2,1,0:T(8,128)(2,1)S(1)} %pad_maximum_fusion.refs_8_.refs_0_, ...), custom_call_target="tpu_custom_call" | custom-call | flops 17179869184 | bytes 4194304 | tf_op jit(solution)/shard_map/attend/pallas_call | solution.py:181
  88.3 10.7 %collective-permute-start.15 = (bf16[4,32,1152]{2,1,0:T(8,128)(2,1)S(1)}, bf16[4,32,1152]{2,1,0:T(8,128)(2,1)S(1)}, u32[]{:S(2)}, u32[]{:S(2)}) collective-permute-start(bf16[4,32,1152]{2,1,0:T(8,128)(2,1)S(1)} %get-tuple-element.43), channel_id=1, source_target_pairs={{0,2},{2,0},{4,6},{6,4},{8,10},{10,8},{12,14},{14,12},{16,18},{18,... | collective-permute-start | bytes 884744 | tf_op jit(solution)/shard_map/ppermute | solution.py:368
  99.1 1.5 collective-permute-start.17
  100.6 18.9 %attend.7 = (bf16[4,32,1152]{2,1,0:T(8,128)(2,1)S(1)}, bf16[4,32,1152]{2,1,0:T(8,128)(2,1)S(1)}, bf16[4,32,1152]{2,1,0:T(8,128)(2,1)S(1)}, bf16[4,32,1152]{2,1,0:T(8,128)(2,1)S(1)}) custom-call(s32[11]{0:T(128)S(1)} %concatenate.15.info, bf16[4,32,3072]{2,1,0:T(8,128)(2,1)S(1)} %pad_maximum_fusion.refs_8_.refs_0_, ...), custom_call_target="tpu_custom_call" | custom-call | flops 17179869184 | bytes 4194304 | tf_op jit(solution)/shard_map/attend/pallas_call | solution.py:181
  119.6 1.7 merge.2
  121.2 17.0 %collective-permute-start.18 = (bf16[32,2304]{1,0:T(8,128)(2,1)S(1)}, bf16[32,2304]{1,0:T(8,128)(2,1)S(1)}, u32[]{:S(2)}, u32[]{:S(2)}) collective-permute-start(bf16[32,2304]{1,0:T(8,128)(2,1)S(1)} %get-tuple-element.48), channel_id=1, source_target_pairs={{0,8},{2,10},{4,12},{6,14},{8,0},{10,2},{12,4},{14,6},{16,24},{18,... | collective-permute-start | bytes 442376 | tf_op jit(solution)/shard_map/ppermute | solution.py:368
  138.8 1.5 collective-permute-start.23
  140.3 1.5 collective-permute-start.24
  142.0 2.2 collective-permute-start.20
  144.2 13.6 %attend.8 = (bf16[4,32,1152]{2,1,0:T(8,128)(2,1)S(1)}, bf16[4,32,1152]{2,1,0:T(8,128)(2,1)S(1)}, bf16[4,32,1152]{2,1,0:T(8,128)(2,1)S(1)}) custom-call(s32[11]{0:T(128)S(1)} %concatenate.15.info, bf16[4,32,3072]{2,1,0:T(8,128)(2,1)S(1)} %collective-permute-done.12.refs_1_.refs_0_, bf16[4,32,3072]{2,1,0:T(8,128)(2,1)S(1)} %collective-permute-done.13.refs_2_.refs_1_, ...), custom_call_target="tpu_custom_call" | custom-call | flops 12884901888 | bytes 3670016 | tf_op jit(solution)/shard_map/attend/pallas_call | solution.py:181
  157.8 6.6 %collective-permute-start.25 = (bf16[4,32,1152]{2,1,0:T(8,128)(2,1)S(1)}, bf16[4,32,1152]{2,1,0:T(8,128)(2,1)S(1)}, u32[]{:S(2)}, u32[]{:S(2)}) collective-permute-start(bf16[4,32,1152]{2,1,0:T(8,128)(2,1)S(1)} %get-tuple-element.51.refs_4_), channel_id=1, source_target_pairs={{0,2},{2,0},{4,6},{6,4},{8,10},{10,8},{12,14},{14,12},{16,18},{18,... | collective-permute-start | bytes 884744 | tf_op jit(solution)/shard_map/ppermute | solution.py:368
  165.1 1.6 collective-permute-start.27
  166.7 5.4 %attend.9.refs_4_.refs_8_ = bf16[4,32,1152]{2,1,0:T(8,128)(2,1)S(1)} custom-call(s32[11]{0:T(128)S(1)} %concatenate.15.info, bf16[4,32,3072]{2,1,0:T(8,128)(2,1)S(1)} %pad_maximum_fusion.refs_8_.refs_0_, bf16[512,4096]{1,0:T(8,128)(2,1)S(1)} %transpose.8.refs_4_.refs_3_.refs_1_, bf16[4096,512]{1,0:T(8,128)(2,1)S(1)} %copy-done.3, ...), custom_call_target="tpu_custom_call" | custom-call | flops 4294967296 | bytes 2621440 | tf_op jit(solution)/shard_map/attend/pallas_call | solution.py:181
  172.6 1.7 collective-permute-done.26.refs_6_
  174.3 2.4 %collective-permute-start.28 = (bf16[2,32,2048]{2,1,0:T(8,128)(2,1)S(1)}, bf16[2,32,2048]{2,1,0:T(8,128)(2,1)S(1)}, u32[]{:S(2)}, u32[]{:S(2)}) collective-permute-start(bf16[2,32,2048]{2,1,0:T(8,128)(2,1)S(1)} %pad_maximum_fusion.3.refs_9_), channel_id=1, source_target_pairs={{0,8},{2,10},{4,12},{6,14},{8,0},{10,2},{12,4},{14,6},{16,24},{18,... | collective-permute-start | bytes 786440 | tf_op jit(solution)/shard_map/ppermute | solution.py:368
  176.8 6.8 %collective-permute-done.28 = bf16[2,32,2048]{2,1,0:T(8,128)(2,1)S(1)} collective-permute-done((bf16[2,32,2048]{2,1,0:T(8,128)(2,1)S(1)}, bf16[2,32,2048]{2,1,0:T(8,128)(2,1)S(1)}, u32[]{:S(2)}, u32[]{:S(2)}) %collective-permute-start.28) | collective-permute-done | bytes 262176 | tf_op jit(solution)/shard_map/ppermute | solution.py:368
  183.6 2.1 collective-permute-start.32
  185.6 0.9 collective-permute-start.33
  186.5 1.7 merge.3
  188.2 1.8 collective-permute-start.29
  189.9 1.0 collective-permute-start.30
  191.0 1.7 collective-permute-start.31
  192.6 0.9 collective-permute-done.29.refs_1_
  193.6 4.1 %collective-permute-done.30.refs_2_ = bf16[32,2304]{1,0:T(8,128)(2,1)S(1)} collective-permute-done((bf16[32,2304]{1,0:T(8,128)(2,1)S(1)}, bf16[32,2304]{1,0:T(8,128)(2,1)S(1)}, u32[]{:S(2)}, u32[]{:S(2)}) %collective-permute-start.30) | collective-permute-done | bytes 147488 | tf_op jit(solution)/shard_map/ppermute | solution.py:368
  197.7 2.6 %collective-permute-done.31.refs_3_ = bf16[32,2304]{1,0:T(8,128)(2,1)S(1)} collective-permute-done((bf16[32,2304]{1,0:T(8,128)(2,1)S(1)}, bf16[32,2304]{1,0:T(8,128)(2,1)S(1)}, u32[]{:S(2)}, u32[]{:S(2)}) %collective-permute-start.31) | collective-permute-done | bytes 147488 | tf_op jit(solution)/shard_map/ppermute | solution.py:368
  201.1 1.8 collective-permute-start.34
  202.9 1.4 collective-permute-start.36
  204.2 4.2 %collective-permute-done.34 = bf16[1,32,2048]{2,1,0:T(8,128)(2,1)S(1)} collective-permute-done((bf16[1,32,2048]{2,1,0:T(8,128)(2,1)S(1)}, bf16[1,32,2048]{2,1,0:T(8,128)(2,1)S(1)}, u32[]{:S(2)}, u32[]{:S(2)}) %collective-permute-start.34) | collective-permute-done | bytes 131104 | tf_op jit(solution)/shard_map/ppermute | solution.py:368
  208.6 6.3 %collective-permute-done.35 = bf16[2,32,2048]{2,1,0:T(8,128)(2,1)S(1)} collective-permute-done((bf16[2,32,2048]{2,1,0:T(8,128)(2,1)S(1)}, bf16[2,32,2048]{2,1,0:T(8,128)(2,1)S(1)}, u32[]{:S(2)}, u32[]{:S(2)}) %collective-permute-start.35) | collective-permute-done | bytes 262176 | tf_op jit(solution)/shard_map/ppermute | solution.py:368
  214.9 3.8 %collective-permute-done.36.refs_3_ = bf16[4,32,2048]{2,1,0:T(8,128)(2,1)S(1)} collective-permute-done((bf16[4,32,2048]{2,1,0:T(8,128)(2,1)S(1)}, bf16[4,32,2048]{2,1,0:T(8,128)(2,1)S(1)}, u32[]{:S(2)}, u32[]{:S(2)}) %collective-permute-start.36) | collective-permute-done | bytes 524320 | tf_op jit(solution)/shard_map/ppermute | solution.py:368
  219.0 1.6 collective-permute-start.37
  220.5 1.7 collective-permute-start.38
  222.2 2.2 copy-done
  224.4 1.9 project.3.refs_3_
  226.3 1.7 collective-permute-done.39.refs_1_
  228.0 2.4 %project.4.refs_3_ = f32[4,4,32,512]{3,2,1,0:T(8,128)S(1)} custom-call(s32[11]{0:T(128)S(1)} %concatenate.15.info, bf16[4,32,2048]{2,1,0:T(8,128)(2,1)S(1)} %pad_maximum_fusion.1.refs_0_, bf16[4,32,2048]{2,1,0:T(8,128)(2,1)} %collective-permute-done.39.refs_1_, bf16[4096,512]{1,0:T(8,128)(2,1)S(1)} %copy-done.1, f32[4,4,32,512]{3,2,1,0:T(8,128)S(1)} %project.3.refs_3_), custom_call_target="tpu_custom_call" | custom-call | flops 536870912 | bytes 3145728 | tf_op jit(solution)/shard_map/project/pallas_call | solution.py:345
  230.4 3.3 %collective-permute-done.37.refs_0_ = bf16[4,32,2048]{2,1,0:T(8,128)(2,1)S(1)} collective-permute-done((bf16[4,32,2048]{2,1,0:T(8,128)(2,1)S(1)}, bf16[4,32,2048]{2,1,0:T(8,128)(2,1)S(1)}, u32[]{:S(2)}, u32[]{:S(2)}) %collective-permute-start.37) | collective-permute-done | bytes 524320 | tf_op jit(solution)/shard_map/ppermute | solution.py:368
  233.8 2.4 %project.5 = bf16[4,4,32,512]{3,2,1,0:T(8,128)(2,1)S(1)} custom-call(s32[11]{0:T(128)S(1)} %concatenate.15.info, bf16[4,32,2048]{2,1,0:T(8,128)(2,1)S(1)} %collective-permute-done.37.refs_0_, bf16[4,32,2048]{2,1,0:T(8,128)(2,1)} %collective-permute-done.38.refs_1_, bf16[4096,512]{1,0:T(8,128)(2,1)S(1)} %copy-done.1, f32[4,4,32,512]{3,2,1,0:T(8,128)S(1)} %project.4.refs_3_), custom_call_target="tpu_custom_call" | custom-call | flops 536870912 | bytes 3145728 | tf_op jit(solution)/shard_map/project/pallas_call | solution.py:345
  236.3 1.5 collective-permute-done.40
  237.8 0.8 add_convert_fusion
  (64 shorter events, 4.7 us)
Async XLA Ops:
  0.9 8.9 %collective-permute-start = (bf16[32,1024]{1,0:T(8,128)(2,1)S(1)}, bf16[32,1024]{1,0:T(8,128)(2,1)S(1)}, u32[]{:S(2)}, u32[]{:S(2)}) collective-permute-start(bf16[32,1024]{1,0:T(8,128)(2,1)S(1)} %get-tuple-element.66), channel_id=1, source_target_pairs={{0,8},{2,10},{4,12},{6,14},{8,0},{10,2},{12,4},{14,6},{16,24},{18,... | collective-permute-start | bytes 196616 | tf_op jit(solution)/shard_map/ppermute | solution.py:368
  3.9 7.3 %collective-permute-start.1 = (bf16[32,1024]{1,0:T(8,128)(2,1)S(1)}, bf16[32,1024]{1,0:T(8,128)(2,1)S(1)}, u32[]{:S(2)}, u32[]{:S(2)}) collective-permute-start(bf16[32,1024]{1,0:T(8,128)(2,1)S(1)} %get-tuple-element.66), channel_id=1, source_target_pairs={{0,16},{2,18},{4,20},{6,22},{8,24},{10,26},{12,28},{14,30},{16,0},... | collective-permute-start | bytes 196616 | tf_op jit(solution)/shard_map/ppermute | solution.py:368
  6.5 6.1 %collective-permute-start.2 = (bf16[32,1024]{1,0:T(8,128)(2,1)S(1)}, bf16[32,1024]{1,0:T(8,128)(2,1)S(1)}, u32[]{:S(2)}, u32[]{:S(2)}) collective-permute-start(bf16[32,1024]{1,0:T(8,128)(2,1)S(1)} %get-tuple-element.66), channel_id=1, source_target_pairs={{0,24},{2,26},{4,28},{6,30},{8,16},{10,18},{12,20},{14,22},{16,8},... | collective-permute-start | bytes 196616 | tf_op jit(solution)/shard_map/ppermute | solution.py:368
  12.6 8.8 %collective-permute-start.6 = (bf16[32,3072]{1,0:T(8,128)(2,1)S(1)}, bf16[32,3072]{1,0:T(8,128)(2,1)S(1)}, u32[]{:S(2)}, u32[]{:S(2)}) collective-permute-start(bf16[32,3072]{1,0:T(8,128)(2,1)S(1)} %slice.7), channel_id=1, source_target_pairs={{0,8},{2,10},{4,12},{6,14},{8,0},{10,2},{12,4},{14,6},{16,24},{18,... | collective-permute-start | bytes 589832 | tf_op jit(solution)/shard_map/ppermute | solution.py:368
  12.7 16.9 %collective-permute-start.7 = (bf16[32,3072]{1,0:T(8,128)(2,1)S(1)}, bf16[32,3072]{1,0:T(8,128)(2,1)S(1)}, u32[]{:S(2)}, u32[]{:S(2)}) collective-permute-start(bf16[32,3072]{1,0:T(8,128)(2,1)S(1)} %slice.7), channel_id=1, source_target_pairs={{0,16},{2,18},{4,20},{6,22},{8,24},{10,26},{12,28},{14,30},{16,0},... | collective-permute-start | bytes 589832 | tf_op jit(solution)/shard_map/ppermute | solution.py:368
  15.1 14.5 %collective-permute-start.8 = (bf16[32,3072]{1,0:T(8,128)(2,1)S(1)}, bf16[32,3072]{1,0:T(8,128)(2,1)S(1)}, u32[]{:S(2)}, u32[]{:S(2)}) collective-permute-start(bf16[32,3072]{1,0:T(8,128)(2,1)S(1)} %slice.7), channel_id=1, source_target_pairs={{0,24},{2,26},{4,28},{6,30},{8,16},{10,18},{12,20},{14,22},{16,8},... | collective-permute-start | bytes 589832 | tf_op jit(solution)/shard_map/ppermute | solution.py:368
  18.5 14.3 %collective-permute-start.3 = (bf16[4,32,1024]{2,1,0:T(8,128)(2,1)S(1)}, bf16[4,32,1024]{2,1,0:T(8,128)(2,1)S(1)}, u32[]{:S(2)}, u32[]{:S(2)}) collective-permute-start(bf16[4,32,1024]{2,1,0:T(8,128)(2,1)S(1)} %pad_maximum_fusion.2.refs_0_), channel_id=1, source_target_pairs={{0,2},{2,0},{4,6},{6,4},{8,10},{10,8},{12,14},{14,12},{16,18},{18,... | collective-permute-start | bytes 786440 | tf_op jit(solution)/shard_map/ppermute | solution.py:368
  20.0 13.3 %collective-permute-start.4 = (bf16[4,32,1024]{2,1,0:T(8,128)(2,1)S(1)}, bf16[4,32,1024]{2,1,0:T(8,128)(2,1)S(1)}, u32[]{:S(2)}, u32[]{:S(2)}) collective-permute-start(bf16[4,32,1024]{2,1,0:T(8,128)(2,1)S(1)} %pad_maximum_fusion.2.refs_0_), channel_id=1, source_target_pairs={{0,4},{2,6},{4,0},{6,2},{8,12},{10,14},{12,8},{14,10},{16,20},{18,... | collective-permute-start | bytes 786440 | tf_op jit(solution)/shard_map/ppermute | solution.py:368
  21.5 11.8 %collective-permute-start.5 = (bf16[4,32,1024]{2,1,0:T(8,128)(2,1)S(1)}, bf16[4,32,1024]{2,1,0:T(8,128)(2,1)S(1)}, u32[]{:S(2)}, u32[]{:S(2)}) collective-permute-start(bf16[4,32,1024]{2,1,0:T(8,128)(2,1)S(1)} %pad_maximum_fusion.2.refs_0_), channel_id=1, source_target_pairs={{0,6},{2,4},{4,2},{6,0},{8,14},{10,12},{12,10},{14,8},{16,22},{18,... | collective-permute-start | bytes 786440 | tf_op jit(solution)/shard_map/ppermute | solution.py:368
  23.0 2.2 copy-start.2
  25.2 8.1 %copy-start.3 = (bf16[4096,512]{1,0:T(8,128)(2,1)S(1)}, bf16[4096,512]{1,0:T(8,128)(2,1)}, u32[]{:S(2)}) copy-start(bf16[4096,512]{1,0:T(8,128)(2,1)} %refs_2_.3) | copy-start | bytes 12582916
  25.2 8.1 %copy-start.4 = (bf16[32,512]{1,0:T(8,128)(2,1)S(1)}, bf16[32,512]{1,0:T(8,128)(2,1)}, u32[]{:S(2)}) copy-start(bf16[32,512]{1,0:T(8,128)(2,1)} %refs_3_.1) | copy-start | bytes 98308
  25.2 8.1 %copy-start.5 = (bf16[32,512]{1,0:T(8,128)(2,1)S(1)}, bf16[32,512]{1,0:T(8,128)(2,1)}, u32[]{:S(2)}) copy-start(bf16[32,512]{1,0:T(8,128)(2,1)} %refs_4_.4) | copy-start | bytes 98308
  29.7 36.4 %collective-permute-start.12 = (bf16[4,32,3072]{2,1,0:T(8,128)(2,1)S(1)}, bf16[4,32,3072]{2,1,0:T(8,128)(2,1)S(1)}, u32[]{:S(2)}, u32[]{:S(2)}) collective-permute-start(bf16[4,32,3072]{2,1,0:T(8,128)(2,1)S(1)} %pad_maximum_fusion.refs_8_.refs_0_), channel_id=1, source_target_pairs={{0,2},{2,0},{4,6},{6,4},{8,10},{10,8},{12,14},{14,12},{16,18},{18,... | collective-permute-start | bytes 2359304 | tf_op jit(solution)/shard_map/ppermute | solution.py:368
  31.3 38.0 %collective-permute-start.13 = (bf16[4,32,3072]{2,1,0:T(8,128)(2,1)S(1)}, bf16[4,32,3072]{2,1,0:T(8,128)(2,1)S(1)}, u32[]{:S(2)}, u32[]{:S(2)}) collective-permute-start(bf16[4,32,3072]{2,1,0:T(8,128)(2,1)S(1)} %pad_maximum_fusion.refs_8_.refs_0_), channel_id=1, source_target_pairs={{0,4},{2,6},{4,0},{6,2},{8,12},{10,14},{12,8},{14,10},{16,20},{18,... | collective-permute-start | bytes 2359304 | tf_op jit(solution)/shard_map/ppermute | solution.py:368
  32.8 36.5 %collective-permute-start.14 = (bf16[4,32,3072]{2,1,0:T(8,128)(2,1)S(1)}, bf16[4,32,3072]{2,1,0:T(8,128)(2,1)S(1)}, u32[]{:S(2)}, u32[]{:S(2)}) collective-permute-start(bf16[4,32,3072]{2,1,0:T(8,128)(2,1)S(1)} %pad_maximum_fusion.refs_8_.refs_0_), channel_id=1, source_target_pairs={{0,6},{2,4},{4,2},{6,0},{8,14},{10,12},{12,10},{14,8},{16,22},{18,... | collective-permute-start | bytes 2359304 | tf_op jit(solution)/shard_map/ppermute | solution.py:368
  52.1 47.0 %collective-permute-start.10 = (bf16[4,32,1152]{2,1,0:T(8,128)(2,1)S(1)}, bf16[4,32,1152]{2,1,0:T(8,128)(2,1)S(1)}, u32[]{:S(2)}, u32[]{:S(2)}) collective-permute-start(bf16[4,32,1152]{2,1,0:T(8,128)(2,1)S(1)} %get-tuple-element.40), channel_id=1, source_target_pairs={{0,4},{2,6},{4,0},{6,2},{8,12},{10,14},{12,8},{14,10},{16,20},{18,... | collective-permute-start | bytes 884744 | tf_op jit(solution)/shard_map/ppermute | solution.py:368
  59.1 60.4 %collective-permute-start.11 = (bf16[4,32,1152]{2,1,0:T(8,128)(2,1)S(1)}, bf16[4,32,1152]{2,1,0:T(8,128)(2,1)S(1)}, u32[]{:S(2)}, u32[]{:S(2)}) collective-permute-start(bf16[4,32,1152]{2,1,0:T(8,128)(2,1)S(1)} %get-tuple-element.41), channel_id=1, source_target_pairs={{0,6},{2,4},{4,2},{6,0},{8,14},{10,12},{12,10},{14,8},{16,22},{18,... | collective-permute-start | bytes 884744 | tf_op jit(solution)/shard_map/ppermute | solution.py:368
  66.1 53.5 %collective-permute-start.9 = (bf16[4,32,1152]{2,1,0:T(8,128)(2,1)S(1)}, bf16[4,32,1152]{2,1,0:T(8,128)(2,1)S(1)}, u32[]{:S(2)}, u32[]{:S(2)}) collective-permute-start(bf16[4,32,1152]{2,1,0:T(8,128)(2,1)S(1)} %get-tuple-element.39), channel_id=1, source_target_pairs={{0,2},{2,0},{4,6},{6,4},{8,10},{10,8},{12,14},{14,12},{16,18},{18,... | collective-permute-start | bytes 884744 | tf_op jit(solution)/shard_map/ppermute | solution.py:368
  88.3 31.2 %collective-permute-start.15 = (bf16[4,32,1152]{2,1,0:T(8,128)(2,1)S(1)}, bf16[4,32,1152]{2,1,0:T(8,128)(2,1)S(1)}, u32[]{:S(2)}, u32[]{:S(2)}) collective-permute-start(bf16[4,32,1152]{2,1,0:T(8,128)(2,1)S(1)} %get-tuple-element.43), channel_id=1, source_target_pairs={{0,2},{2,0},{4,6},{6,4},{8,10},{10,8},{12,14},{14,12},{16,18},{18,... | collective-permute-start | bytes 884744 | tf_op jit(solution)/shard_map/ppermute | solution.py:368
  99.1 20.5 %collective-permute-start.16 = (bf16[4,32,1152]{2,1,0:T(8,128)(2,1)S(1)}, bf16[4,32,1152]{2,1,0:T(8,128)(2,1)S(1)}, u32[]{:S(2)}, u32[]{:S(2)}) collective-permute-start(bf16[4,32,1152]{2,1,0:T(8,128)(2,1)S(1)} %get-tuple-element.44), channel_id=1, source_target_pairs={{0,4},{2,6},{4,0},{6,2},{8,12},{10,14},{12,8},{14,10},{16,20},{18,... | collective-permute-start | bytes 884744 | tf_op jit(solution)/shard_map/ppermute | solution.py:368
  99.1 20.5 %collective-permute-start.17 = (bf16[4,32,1152]{2,1,0:T(8,128)(2,1)S(1)}, bf16[4,32,1152]{2,1,0:T(8,128)(2,1)S(1)}, u32[]{:S(2)}, u32[]{:S(2)}) collective-permute-start(bf16[4,32,1152]{2,1,0:T(8,128)(2,1)S(1)} %get-tuple-element.45), channel_id=1, source_target_pairs={{0,6},{2,4},{4,2},{6,0},{8,14},{10,12},{12,10},{14,8},{16,22},{18,... | collective-permute-start | bytes 884744 | tf_op jit(solution)/shard_map/ppermute | solution.py:368
  121.2 20.7 %collective-permute-start.18 = (bf16[32,2304]{1,0:T(8,128)(2,1)S(1)}, bf16[32,2304]{1,0:T(8,128)(2,1)S(1)}, u32[]{:S(2)}, u32[]{:S(2)}) collective-permute-start(bf16[32,2304]{1,0:T(8,128)(2,1)S(1)} %get-tuple-element.48), channel_id=1, source_target_pairs={{0,8},{2,10},{4,12},{6,14},{8,0},{10,2},{12,4},{14,6},{16,24},{18,... | collective-permute-start | bytes 442376 | tf_op jit(solution)/shard_map/ppermute | solution.py:368
  138.3 26.8 %collective-permute-start.22 = (bf16[4,32,1152]{2,1,0:T(8,128)(2,1)S(1)}, bf16[4,32,1152]{2,1,0:T(8,128)(2,1)S(1)}, u32[]{:S(2)}, u32[]{:S(2)}) collective-permute-start(bf16[4,32,1152]{2,1,0:T(8,128)(2,1)S(1)} %get-tuple-element.52), channel_id=1, source_target_pairs={{0,2},{2,0},{4,6},{6,4},{8,10},{10,8},{12,14},{14,12},{16,18},{18,... | collective-permute-start | bytes 884744 | tf_op jit(solution)/shard_map/ppermute | solution.py:368
  138.8 27.9 %collective-permute-start.23 = (bf16[4,32,1152]{2,1,0:T(8,128)(2,1)S(1)}, bf16[4,32,1152]{2,1,0:T(8,128)(2,1)S(1)}, u32[]{:S(2)}, u32[]{:S(2)}) collective-permute-start(bf16[4,32,1152]{2,1,0:T(8,128)(2,1)S(1)} %get-tuple-element.53), channel_id=1, source_target_pairs={{0,4},{2,6},{4,0},{6,2},{8,12},{10,14},{12,8},{14,10},{16,20},{18,... | collective-permute-start | bytes 884744 | tf_op jit(solution)/shard_map/ppermute | solution.py:368
  140.3 26.4 %collective-permute-start.24 = (bf16[4,32,1152]{2,1,0:T(8,128)(2,1)S(1)}, bf16[4,32,1152]{2,1,0:T(8,128)(2,1)S(1)}, u32[]{:S(2)}, u32[]{:S(2)}) collective-permute-start(bf16[4,32,1152]{2,1,0:T(8,128)(2,1)S(1)} %get-tuple-element.54), channel_id=1, source_target_pairs={{0,6},{2,4},{4,2},{6,0},{8,14},{10,12},{12,10},{14,8},{16,22},{18,... | collective-permute-start | bytes 884744 | tf_op jit(solution)/shard_map/ppermute | solution.py:368
  141.7 16.0 %collective-permute-start.19 = (bf16[32,2304]{1,0:T(8,128)(2,1)S(1)}, bf16[32,2304]{1,0:T(8,128)(2,1)S(1)}, u32[]{:S(2)}, u32[]{:S(2)}) collective-permute-start(bf16[32,2304]{1,0:T(8,128)(2,1)S(1)} %get-tuple-element.49), channel_id=1, source_target_pairs={{0,16},{2,18},{4,20},{6,22},{8,24},{10,26},{12,28},{14,30},{16,0},... | collective-permute-start | bytes 442376 | tf_op jit(solution)/shard_map/ppermute | solution.py:368
  142.0 22.5 %collective-permute-start.20 = (bf16[32,2304]{1,0:T(8,128)(2,1)S(1)}, bf16[32,2304]{1,0:T(8,128)(2,1)S(1)}, u32[]{:S(2)}, u32[]{:S(2)}) collective-permute-start(bf16[32,2304]{1,0:T(8,128)(2,1)S(1)} %get-tuple-element.50), channel_id=1, source_target_pairs={{0,24},{2,26},{4,28},{6,30},{8,16},{10,18},{12,20},{14,22},{16,8},... | collective-permute-start | bytes 442376 | tf_op jit(solution)/shard_map/ppermute | solution.py:368
  157.8 14.8 %collective-permute-start.25 = (bf16[4,32,1152]{2,1,0:T(8,128)(2,1)S(1)}, bf16[4,32,1152]{2,1,0:T(8,128)(2,1)S(1)}, u32[]{:S(2)}, u32[]{:S(2)}) collective-permute-start(bf16[4,32,1152]{2,1,0:T(8,128)(2,1)S(1)} %get-tuple-element.51.refs_4_), channel_id=1, source_target_pairs={{0,2},{2,0},{4,6},{6,4},{8,10},{10,8},{12,14},{14,12},{16,18},{18,... | collective-permute-start | bytes 884744 | tf_op jit(solution)/shard_map/ppermute | solution.py:368
  164.4 9.9 %collective-permute-start.26 = (bf16[4,32,1152]{2,1,0:T(8,128)(2,1)S(1)}, bf16[4,32,1152]{2,1,0:T(8,128)(2,1)S(1)}, u32[]{:S(2)}, u32[]{:S(2)}) collective-permute-start(bf16[4,32,1152]{2,1,0:T(8,128)(2,1)S(1)} %get-tuple-element.55), channel_id=1, source_target_pairs={{0,4},{2,6},{4,0},{6,2},{8,12},{10,14},{12,8},{14,10},{16,20},{18,... | collective-permute-start | bytes 884744 | tf_op jit(solution)/shard_map/ppermute | solution.py:368
  165.1 9.2 %collective-permute-start.27 = (bf16[4,32,1152]{2,1,0:T(8,128)(2,1)S(1)}, bf16[4,32,1152]{2,1,0:T(8,128)(2,1)S(1)}, u32[]{:S(2)}, u32[]{:S(2)}) collective-permute-start(bf16[4,32,1152]{2,1,0:T(8,128)(2,1)S(1)} %get-tuple-element.56), channel_id=1, source_target_pairs={{0,6},{2,4},{4,2},{6,0},{8,14},{10,12},{12,10},{14,8},{16,22},{18,... | collective-permute-start | bytes 884744 | tf_op jit(solution)/shard_map/ppermute | solution.py:368
  166.7 5.9 %collective-permute-start.21 = (bf16[1,32,2048]{2,1,0:T(8,128)(2,1)S(1)}, bf16[1,32,2048]{2,1,0:T(8,128)(2,1)S(1)}, u32[]{:S(2)}, u32[]{:S(2)}) collective-permute-start(bf16[1,32,2048]{2,1,0:T(8,128)(2,1)S(1)} %bitcast.20), channel_id=1, source_target_pairs={{0,16},{2,18},{4,20},{6,22},{8,24},{10,26},{12,28},{14,30},{16,0},... | collective-permute-start | bytes 393224 | tf_op jit(solution)/shard_map/ppermute | solution.py:368
  174.3 9.2 %collective-permute-start.28 = (bf16[2,32,2048]{2,1,0:T(8,128)(2,1)S(1)}, bf16[2,32,2048]{2,1,0:T(8,128)(2,1)S(1)}, u32[]{:S(2)}, u32[]{:S(2)}) collective-permute-start(bf16[2,32,2048]{2,1,0:T(8,128)(2,1)S(1)} %pad_maximum_fusion.3.refs_9_), channel_id=1, source_target_pairs={{0,8},{2,10},{4,12},{6,14},{8,0},{10,2},{12,4},{14,6},{16,24},{18,... | collective-permute-start | bytes 786440 | tf_op jit(solution)/shard_map/ppermute | solution.py:368
  183.6 16.7 %collective-permute-start.32 = (bf16[4,32,2048]{2,1,0:T(8,128)(2,1)S(1)}, bf16[4,32,2048]{2,1,0:T(8,128)(2,1)S(1)}, u32[]{:S(2)}, u32[]{:S(2)}) collective-permute-start(bf16[4,32,2048]{2,1,0:T(8,128)(2,1)S(1)} %constant_dynamic-update-slice_fusion.refs_0_), channel_id=1, source_target_pairs={{0,2},{2,0},{4,6},{6,4},{8,10},{10,8},{12,14},{14,12},{16,18},{18,... | collective-permute-start | bytes 1572872 | tf_op jit(solution)/shard_map/ppermute | solution.py:368
  185.6 14.8 %collective-permute-start.33 = (bf16[4,32,2048]{2,1,0:T(8,128)(2,1)S(1)}, bf16[4,32,2048]{2,1,0:T(8,128)(2,1)S(1)}, u32[]{:S(2)}, u32[]{:S(2)}) collective-permute-start(bf16[4,32,2048]{2,1,0:T(8,128)(2,1)S(1)} %constant_dynamic-update-slice_fusion.refs_0_), channel_id=1, source_target_pairs={{0,4},{2,6},{4,0},{6,2},{8,12},{10,14},{12,8},{14,10},{16,20},{18,... | collective-permute-start | bytes 1572872 | tf_op jit(solution)/shard_map/ppermute | solution.py:368
  188.2 5.4 %collective-permute-start.29 = (bf16[32,2304]{1,0:T(8,128)(2,1)S(1)}, bf16[32,2304]{1,0:T(8,128)(2,1)S(1)}, u32[]{:S(2)}, u32[]{:S(2)}) collective-permute-start(bf16[32,2304]{1,0:T(8,128)(2,1)S(1)} %get-tuple-element.59), channel_id=1, source_target_pairs={{0,8},{2,10},{4,12},{6,14},{8,0},{10,2},{12,4},{14,6},{16,24},{18,... | collective-permute-start | bytes 442376 | tf_op jit(solution)/shard_map/ppermute | solution.py:368
  189.9 7.7 %collective-permute-start.30 = (bf16[32,2304]{1,0:T(8,128)(2,1)S(1)}, bf16[32,2304]{1,0:T(8,128)(2,1)S(1)}, u32[]{:S(2)}, u32[]{:S(2)}) collective-permute-start(bf16[32,2304]{1,0:T(8,128)(2,1)S(1)} %get-tuple-element.60), channel_id=1, source_target_pairs={{0,16},{2,18},{4,20},{6,22},{8,24},{10,26},{12,28},{14,30},{16,0},... | collective-permute-start | bytes 442376 | tf_op jit(solution)/shard_map/ppermute | solution.py:368
  191.0 9.3 %collective-permute-start.31 = (bf16[32,2304]{1,0:T(8,128)(2,1)S(1)}, bf16[32,2304]{1,0:T(8,128)(2,1)S(1)}, u32[]{:S(2)}, u32[]{:S(2)}) collective-permute-start(bf16[32,2304]{1,0:T(8,128)(2,1)S(1)} %get-tuple-element.61), channel_id=1, source_target_pairs={{0,24},{2,26},{4,28},{6,30},{8,16},{10,18},{12,20},{14,22},{16,8},... | collective-permute-start | bytes 442376 | tf_op jit(solution)/shard_map/ppermute | solution.py:368
  201.1 7.3 %collective-permute-start.34 = (bf16[1,32,2048]{2,1,0:T(8,128)(2,1)S(1)}, bf16[1,32,2048]{2,1,0:T(8,128)(2,1)S(1)}, u32[]{:S(2)}, u32[]{:S(2)}) collective-permute-start(bf16[1,32,2048]{2,1,0:T(8,128)(2,1)S(1)} %bitcast.22), channel_id=1, source_target_pairs={{0,16},{2,18},{4,20},{6,22},{8,24},{10,26},{12,28},{14,30},{16,0},... | collective-permute-start | bytes 393224 | tf_op jit(solution)/shard_map/ppermute | solution.py:368
  202.9 15.9 %collective-permute-start.36 = (bf16[4,32,2048]{2,1,0:T(8,128)(2,1)S(1)}, bf16[4,32,2048]{2,1,0:T(8,128)(2,1)S(1)}, u32[]{:S(2)}, u32[]{:S(2)}) collective-permute-start(bf16[4,32,2048]{2,1,0:T(8,128)(2,1)S(1)} %constant_dynamic-update-slice_fusion.refs_0_), channel_id=1, source_target_pairs={{0,6},{2,4},{4,2},{6,0},{8,14},{10,12},{12,10},{14,8},{16,22},{18,... | collective-permute-start | bytes 1572872 | tf_op jit(solution)/shard_map/ppermute | solution.py:368
  208.5 6.4 %collective-permute-start.35 = (bf16[2,32,2048]{2,1,0:T(8,128)(2,1)S(1)}, bf16[2,32,2048]{2,1,0:T(8,128)(2,1)S(1)}, u32[]{:S(2)}, u32[]{:S(2)}) collective-permute-start(bf16[2,32,2048]{2,1,0:T(8,128)(2,1)S(1)} %pad_maximum_fusion.4), channel_id=1, source_target_pairs={{0,8},{2,10},{4,12},{6,14},{8,0},{10,2},{12,4},{14,6},{16,24},{18,... | collective-permute-start | bytes 786440 | tf_op jit(solution)/shard_map/ppermute | solution.py:368
  218.7 9.3 %collective-permute-start.39 = (bf16[4,32,2048]{2,1,0:T(8,128)(2,1)S(1)}, bf16[4,32,2048]{2,1,0:T(8,128)(2,1)}, u32[]{:S(2)}, u32[]{:S(2)}) collective-permute-start(bf16[4,32,2048]{2,1,0:T(8,128)(2,1)S(1)} %pad_maximum_fusion.1.refs_0_), channel_id=1, source_target_pairs={{0,2},{2,0},{4,6},{6,4},{8,10},{10,8},{12,14},{14,12},{16,18},{18,... | collective-permute-start | bytes 1572872 | tf_op jit(solution)/shard_map/ppermute | solution.py:368
  219.0 14.8 %collective-permute-start.37 = (bf16[4,32,2048]{2,1,0:T(8,128)(2,1)S(1)}, bf16[4,32,2048]{2,1,0:T(8,128)(2,1)S(1)}, u32[]{:S(2)}, u32[]{:S(2)}) collective-permute-start(bf16[4,32,2048]{2,1,0:T(8,128)(2,1)S(1)} %pad_maximum_fusion.1.refs_0_), channel_id=1, source_target_pairs={{0,4},{2,6},{4,0},{6,2},{8,12},{10,14},{12,8},{14,10},{16,20},{18,... | collective-permute-start | bytes 1572872 | tf_op jit(solution)/shard_map/ppermute | solution.py:368
  220.5 13.2 %collective-permute-start.38 = (bf16[4,32,2048]{2,1,0:T(8,128)(2,1)S(1)}, bf16[4,32,2048]{2,1,0:T(8,128)(2,1)}, u32[]{:S(2)}, u32[]{:S(2)}) collective-permute-start(bf16[4,32,2048]{2,1,0:T(8,128)(2,1)S(1)} %pad_maximum_fusion.1.refs_0_), channel_id=1, source_target_pairs={{0,6},{2,4},{4,2},{6,0},{8,14},{10,12},{12,10},{14,8},{16,22},{18,... | collective-permute-start | bytes 1572872 | tf_op jit(solution)/shard_map/ppermute | solution.py:368
  222.2 2.2 copy-start
  224.4 3.6 %copy-start.1 = (bf16[4096,512]{1,0:T(8,128)(2,1)S(1)}, bf16[4096,512]{1,0:T(8,128)(2,1)}, u32[]{:S(2)}) copy-start(bf16[4096,512]{1,0:T(8,128)(2,1)} %refs_2_.5) | copy-start | bytes 12582916
  236.2 1.6 collective-permute-start.40

commit v12 on v9

--- a/solution.py
+++ b/solution.py
@@ -170,7 +170,7 @@
     key_count = values.shape[0]
     group_step = min(GROUP_QUERIES, 2 * (plane // count))
     tile_rows = group_step * count * rows
-    key_chunk = min(key_count, 512)
+    key_chunk = min(key_count, 256 if tile_rows % 256 == 0 else 512)
     vmem = pltpu.MemorySpace.VMEM
     span_block = pl.BlockSpec((rows, HEAD_SIZE), lambda i, s: (0, head))
     scored = blocks * count * rows * GROUP_QUERIES * key_count

time: 232 us -> 230 us (level)
  starting transfers between devices: 84.8 us -> 53.2 us
  Pallas kernels: 82.1 us -> 113 us
  waiting for transfers between devices: 54.3 us -> 51.3 us
    ppermute x41, starting transfers between devices: 84.8 us -> 53.2 us  [exchange(): return lax.ppermute(x, axis, [(i, i ^ distance) for i in range(count)])]
    pallas_call x5, Pallas kernels: 69.1 us -> 100 us  [attend_head(): pl.pallas_call(functools.partial(attend_kernel, chosen=chosen, blocks=blo...]
    ppermute x41, waiting for transfers between devices: 54.3 us -> 51.3 us  [exchange(): return lax.ppermute(x, axis, [(i, i ^ distance) for i in range(count)])]
  transfers between devices with their start and end apart: 41 -> 41, of which waited for: 13 -> 15; matrix products, arithmetic and copies ran while one was open for 2% -> 2% of each run, Pallas kernels for 33% -> 47%
where the time goes in v12:
time: 230 us; the launch traced here: 229 us
  Pallas kernels  113 us (49%)
  starting transfers between devices  53.2 us (23%)
  waiting for transfers between devices  51.3 us (22%)
  local copies, waits for them, and re-layouts  7.59 us (3%)
  other arithmetic  3.26 us (1%)
    pallas_call x5, Pallas kernels, attend_head(): pl.pallas_call(functools.partial(attend_kernel, chosen=chosen, blocks=blo...  100 us
    ppermute x41, starting transfers between devices, exchange(): return lax.ppermute(x, axis, [(i, i ^ distance) for i in range(count)])  53.2 us
    ppermute x41, waiting for transfers between devices, exchange(): return lax.ppermute(x, axis, [(i, i ^ distance) for i in range(count)])  51.3 us
    pallas_call x3, Pallas kernels, project(): pl.pallas_call(functools.partial(project_kernel, order=order, chosen=chos...  6.72 us
  transfers between devices with their start and end apart: 41, of which 15 were waited for; matrix products, arithmetic and copies ran while one was open for 2% of the time, Pallas kernels for 47%

profile of v12, /device:TPU:0, one launch (start us, length us, event | category | flops | bytes accessed | tf_op | source)
XLA Modules:
  0.0 229.0 jit_solution(5379300149751935583)
XLA Ops:
  0.0 0.8 slice_bitcast_fusion
  0.9 3.1 %collective-permute-start = (bf16[32,1024]{1,0:T(8,128)(2,1)S(1)}, bf16[32,1024]{1,0:T(8,128)(2,1)S(1)}, u32[]{:S(2)}, u32[]{:S(2)}) collective-permute-start(bf16[32,1024]{1,0:T(8,128)(2,1)S(1)} %get-tuple-element.66), channel_id=1, source_target_pairs={{0,8},{2,10},{4,12},{6,14},{8,0},{10,2},{12,4},{14,6},{16,24},{18,... | collective-permute-start | bytes 196616 | tf_op jit(solution)/shard_map/ppermute | solution.py:364
  3.9 2.6 %collective-permute-start.1 = (bf16[32,1024]{1,0:T(8,128)(2,1)S(1)}, bf16[32,1024]{1,0:T(8,128)(2,1)S(1)}, u32[]{:S(2)}, u32[]{:S(2)}) collective-permute-start(bf16[32,1024]{1,0:T(8,128)(2,1)S(1)} %get-tuple-element.66), channel_id=1, source_target_pairs={{0,16},{2,18},{4,20},{6,22},{8,24},{10,26},{12,28},{14,30},{16,0},... | collective-permute-start | bytes 196616 | tf_op jit(solution)/shard_map/ppermute | solution.py:364
  6.5 0.9 slice.7
  7.5 0.8 compare_reduce_fusion
  8.3 0.6 gather_fusion
  9.0 0.8 sort.17
  9.7 1.5 collective-permute-done.1
  11.2 1.4 collective-permute-done.2
  12.7 2.3 %collective-permute-start.7 = (bf16[32,3072]{1,0:T(8,128)(2,1)S(1)}, bf16[32,3072]{1,0:T(8,128)(2,1)S(1)}, u32[]{:S(2)}, u32[]{:S(2)}) collective-permute-start(bf16[32,3072]{1,0:T(8,128)(2,1)S(1)} %slice.7), channel_id=1, source_target_pairs={{0,16},{2,18},{4,20},{6,22},{8,24},{10,26},{12,28},{14,30},{16,0},... | collective-permute-start | bytes 589832 | tf_op jit(solution)/shard_map/ppermute | solution.py:364
  15.1 2.0 collective-permute-start.8
  17.1 0.7 convert_reduce_fusion
  17.8 0.7 concatenate.15.info
  18.5 1.5 collective-permute-start.3
  20.0 1.5 collective-permute-start.4
  21.5 1.5 collective-permute-start.5
  23.0 2.2 copy-done.2
  25.2 1.7 transpose.8.refs_4_.refs_3_.refs_1_
  26.9 2.7 %collective-permute-done.7 = bf16[32,3072]{1,0:T(8,128)(2,1)S(1)} collective-permute-done((bf16[32,3072]{1,0:T(8,128)(2,1)S(1)}, bf16[32,3072]{1,0:T(8,128)(2,1)S(1)}, u32[]{:S(2)}, u32[]{:S(2)}) %collective-permute-start.7) | collective-permute-done | bytes 196640 | tf_op jit(solution)/shard_map/ppermute | solution.py:364
  29.7 1.6 collective-permute-start.12
  31.3 1.5 collective-permute-start.13
  32.8 0.5 collective-permute-start.14
  33.3 24.3 %attend.5 = (bf16[4,32,1152]{2,1,0:T(8,128)(2,1)S(1)}, bf16[4,32,1152]{2,1,0:T(8,128)(2,1)S(1)}, bf16[4,32,1152]{2,1,0:T(8,128)(2,1)S(1)}, bf16[4,32,1152]{2,1,0:T(8,128)(2,1)S(1)}) custom-call(s32[11]{0:T(128)S(1)} %concatenate.15.info, bf16[4,32,1024]{2,1,0:T(8,128)(2,1)S(1)} %pad_maximum_fusion.2.refs_0_, ...), custom_call_target="tpu_custom_call" | custom-call | flops 17179869184 | bytes 4194304 | tf_op jit(solution)/shard_map/attend/pallas_call | solution.py:177
  57.7 2.5 %collective-permute-start.11 = (bf16[4,32,1152]{2,1,0:T(8,128)(2,1)S(1)}, bf16[4,32,1152]{2,1,0:T(8,128)(2,1)S(1)}, u32[]{:S(2)}, u32[]{:S(2)}) collective-permute-start(bf16[4,32,1152]{2,1,0:T(8,128)(2,1)S(1)} %get-tuple-element.41), channel_id=1, source_target_pairs={{0,6},{2,4},{4,2},{6,0},{8,14},{10,12},{12,10},{14,8},{16,22},{18,... | collective-permute-start | bytes 884744 | tf_op jit(solution)/shard_map/ppermute | solution.py:364
  60.2 1.0 collective-permute-start.9
  61.1 8.1 %collective-permute-done.13.refs_2_.refs_1_ = bf16[4,32,3072]{2,1,0:T(8,128)(2,1)S(1)} collective-permute-done((bf16[4,32,3072]{2,1,0:T(8,128)(2,1)S(1)}, bf16[4,32,3072]{2,1,0:T(8,128)(2,1)S(1)}, u32[]{:S(2)}, u32[]{:S(2)}) %collective-permute-start.13) | collective-permute-done | bytes 786464 | tf_op jit(solution)/shard_map/ppermute | solution.py:364
  69.3 24.3 %attend.6 = (bf16[4,32,1152]{2,1,0:T(8,128)(2,1)S(1)}, bf16[4,32,1152]{2,1,0:T(8,128)(2,1)S(1)}, bf16[4,32,1152]{2,1,0:T(8,128)(2,1)S(1)}, bf16[4,32,1152]{2,1,0:T(8,128)(2,1)S(1)}) custom-call(s32[11]{0:T(128)S(1)} %concatenate.15.info, bf16[4,32,3072]{2,1,0:T(8,128)(2,1)S(1)} %pad_maximum_fusion.refs_8_.refs_0_, ...), custom_call_target="tpu_custom_call" | custom-call | flops 17179869184 | bytes 4194304 | tf_op jit(solution)/shard_map/attend/pallas_call | solution.py:177
  93.7 2.5 %collective-permute-start.16 = (bf16[4,32,1152]{2,1,0:T(8,128)(2,1)S(1)}, bf16[4,32,1152]{2,1,0:T(8,128)(2,1)S(1)}, u32[]{:S(2)}, u32[]{:S(2)}) collective-permute-start(bf16[4,32,1152]{2,1,0:T(8,128)(2,1)S(1)} %get-tuple-element.44), channel_id=1, source_target_pairs={{0,4},{2,6},{4,0},{6,2},{8,12},{10,14},{12,8},{14,10},{16,20},{18,... | collective-permute-start | bytes 884744 | tf_op jit(solution)/shard_map/ppermute | solution.py:364
  96.2 0.9 collective-permute-start.17
  97.2 24.5 %attend.7 = (bf16[4,32,1152]{2,1,0:T(8,128)(2,1)S(1)}, bf16[4,32,1152]{2,1,0:T(8,128)(2,1)S(1)}, bf16[4,32,1152]{2,1,0:T(8,128)(2,1)S(1)}, bf16[4,32,1152]{2,1,0:T(8,128)(2,1)S(1)}) custom-call(s32[11]{0:T(128)S(1)} %concatenate.15.info, bf16[4,32,3072]{2,1,0:T(8,128)(2,1)S(1)} %pad_maximum_fusion.refs_8_.refs_0_, ...), custom_call_target="tpu_custom_call" | custom-call | flops 17179869184 | bytes 4194304 | tf_op jit(solution)/shard_map/attend/pallas_call | solution.py:177
  121.7 1.7 merge.2
  123.6 2.5 %collective-permute-start.23 = (bf16[4,32,1152]{2,1,0:T(8,128)(2,1)S(1)}, bf16[4,32,1152]{2,1,0:T(8,128)(2,1)S(1)}, u32[]{:S(2)}, u32[]{:S(2)}) collective-permute-start(bf16[4,32,1152]{2,1,0:T(8,128)(2,1)S(1)} %get-tuple-element.53), channel_id=1, source_target_pairs={{0,4},{2,6},{4,0},{6,2},{8,12},{10,14},{12,8},{14,10},{16,20},{18,... | collective-permute-start | bytes 884744 | tf_op jit(solution)/shard_map/ppermute | solution.py:364
  126.1 0.9 collective-permute-start.24
  127.0 2.9 %collective-permute-start.19 = (bf16[32,2304]{1,0:T(8,128)(2,1)S(1)}, bf16[32,2304]{1,0:T(8,128)(2,1)S(1)}, u32[]{:S(2)}, u32[]{:S(2)}) collective-permute-start(bf16[32,2304]{1,0:T(8,128)(2,1)S(1)} %get-tuple-element.49), channel_id=1, source_target_pairs={{0,16},{2,18},{4,20},{6,22},{8,24},{10,26},{12,28},{14,30},{16,0},... | collective-permute-start | bytes 442376 | tf_op jit(solution)/shard_map/ppermute | solution.py:364
  130.2 1.2 collective-permute-start.20
  131.4 19.6 %attend.8 = (bf16[4,32,1152]{2,1,0:T(8,128)(2,1)S(1)}, bf16[4,32,1152]{2,1,0:T(8,128)(2,1)S(1)}, bf16[4,32,1152]{2,1,0:T(8,128)(2,1)S(1)}) custom-call(s32[11]{0:T(128)S(1)} %concatenate.15.info, bf16[4,32,3072]{2,1,0:T(8,128)(2,1)S(1)} %collective-permute-done.12.refs_1_.refs_0_, bf16[4,32,3072]{2,1,0:T(8,128)(2,1)S(1)} %collective-permute-done.13.refs_2_.refs_1_, ...), custom_call_target="tpu_custom_call" | custom-call | flops 12884901888 | bytes 3670016 | tf_op jit(solution)/shard_map/attend/pallas_call | solution.py:177
  151.1 4.4 %collective-permute-start.26 = (bf16[4,32,1152]{2,1,0:T(8,128)(2,1)S(1)}, bf16[4,32,1152]{2,1,0:T(8,128)(2,1)S(1)}, u32[]{:S(2)}, u32[]{:S(2)}) collective-permute-start(bf16[4,32,1152]{2,1,0:T(8,128)(2,1)S(1)} %get-tuple-element.55), channel_id=1, source_target_pairs={{0,4},{2,6},{4,0},{6,2},{8,12},{10,14},{12,8},{14,10},{16,20},{18,... | collective-permute-start | bytes 884744 | tf_op jit(solution)/shard_map/ppermute | solution.py:364
  155.5 0.6 normalize.2.refs_5_
  156.2 0.6 collective-permute-start.21
  156.8 7.5 %attend.9.refs_4_.refs_8_ = bf16[4,32,1152]{2,1,0:T(8,128)(2,1)S(1)} custom-call(s32[11]{0:T(128)S(1)} %concatenate.15.info, bf16[4,32,3072]{2,1,0:T(8,128)(2,1)S(1)} %pad_maximum_fusion.refs_8_.refs_0_, bf16[512,4096]{1,0:T(8,128)(2,1)S(1)} %transpose.8.refs_4_.refs_3_.refs_1_, bf16[4096,512]{1,0:T(8,128)(2,1)S(1)} %copy-done.3, ...), custom_call_target="tpu_custom_call" | custom-call | flops 4294967296 | bytes 2621440 | tf_op jit(solution)/shard_map/attend/pallas_call | solution.py:177
  164.3 0.5 collective-permute-start.28
  164.8 8.7 %collective-permute-done.28 = bf16[2,32,2048]{2,1,0:T(8,128)(2,1)S(1)} collective-permute-done((bf16[2,32,2048]{2,1,0:T(8,128)(2,1)S(1)}, bf16[2,32,2048]{2,1,0:T(8,128)(2,1)S(1)}, u32[]{:S(2)}, u32[]{:S(2)}) %collective-permute-start.28) | collective-permute-done | bytes 262176 | tf_op jit(solution)/shard_map/ppermute | solution.py:364
  173.5 0.9 collective-permute-start.32
  174.4 4.1 %collective-permute-start.33 = (bf16[4,32,2048]{2,1,0:T(8,128)(2,1)S(1)}, bf16[4,32,2048]{2,1,0:T(8,128)(2,1)S(1)}, u32[]{:S(2)}, u32[]{:S(2)}) collective-permute-start(bf16[4,32,2048]{2,1,0:T(8,128)(2,1)S(1)} %constant_dynamic-update-slice_fusion.refs_0_), channel_id=1, source_target_pairs={{0,4},{2,6},{4,0},{6,2},{8,12},{10,14},{12,8},{14,10},{16,20},{18,... | collective-permute-start | bytes 1572872 | tf_op jit(solution)/shard_map/ppermute | solution.py:364
  178.5 1.7 merge.3
  180.3 4.3 %collective-permute-start.31 = (bf16[32,2304]{1,0:T(8,128)(2,1)S(1)}, bf16[32,2304]{1,0:T(8,128)(2,1)S(1)}, u32[]{:S(2)}, u32[]{:S(2)}) collective-permute-start(bf16[32,2304]{1,0:T(8,128)(2,1)S(1)} %get-tuple-element.61), channel_id=1, source_target_pairs={{0,24},{2,26},{4,28},{6,30},{8,16},{10,18},{12,20},{14,22},{16,8},... | collective-permute-start | bytes 442376 | tf_op jit(solution)/shard_map/ppermute | solution.py:364
  184.6 3.4 %collective-permute-done.29.refs_1_ = bf16[32,2304]{1,0:T(8,128)(2,1)S(1)} collective-permute-done((bf16[32,2304]{1,0:T(8,128)(2,1)S(1)}, bf16[32,2304]{1,0:T(8,128)(2,1)S(1)}, u32[]{:S(2)}, u32[]{:S(2)}) %collective-permute-start.29) | collective-permute-done | bytes 147488 | tf_op jit(solution)/shard_map/ppermute | solution.py:364
  188.0 3.1 %collective-permute-done.31.refs_3_ = bf16[32,2304]{1,0:T(8,128)(2,1)S(1)} collective-permute-done((bf16[32,2304]{1,0:T(8,128)(2,1)S(1)}, bf16[32,2304]{1,0:T(8,128)(2,1)S(1)}, u32[]{:S(2)}, u32[]{:S(2)}) %collective-permute-start.31) | collective-permute-done | bytes 147488 | tf_op jit(solution)/shard_map/ppermute | solution.py:364
  191.3 0.6 normalize.3
  191.9 1.0 collective-permute-start.34
  192.9 0.7 collective-permute-start.36
  193.6 5.5 %collective-permute-done.34 = bf16[1,32,2048]{2,1,0:T(8,128)(2,1)S(1)} collective-permute-done((bf16[1,32,2048]{2,1,0:T(8,128)(2,1)S(1)}, bf16[1,32,2048]{2,1,0:T(8,128)(2,1)S(1)}, u32[]{:S(2)}, u32[]{:S(2)}) %collective-permute-start.34) | collective-permute-done | bytes 131104 | tf_op jit(solution)/shard_map/ppermute | solution.py:364
  199.2 6.4 %collective-permute-done.35 = bf16[2,32,2048]{2,1,0:T(8,128)(2,1)S(1)} collective-permute-done((bf16[2,32,2048]{2,1,0:T(8,128)(2,1)S(1)}, bf16[2,32,2048]{2,1,0:T(8,128)(2,1)S(1)}, u32[]{:S(2)}, u32[]{:S(2)}) %collective-permute-start.35) | collective-permute-done | bytes 262176 | tf_op jit(solution)/shard_map/ppermute | solution.py:364
  205.6 3.1 %collective-permute-done.36.refs_3_ = bf16[4,32,2048]{2,1,0:T(8,128)(2,1)S(1)} collective-permute-done((bf16[4,32,2048]{2,1,0:T(8,128)(2,1)S(1)}, bf16[4,32,2048]{2,1,0:T(8,128)(2,1)S(1)}, u32[]{:S(2)}, u32[]{:S(2)}) %collective-permute-start.36) | collective-permute-done | bytes 524320 | tf_op jit(solution)/shard_map/ppermute | solution.py:364
  208.8 1.1 collective-permute-start.37
  209.9 2.3 %collective-permute-start.38 = (bf16[4,32,2048]{2,1,0:T(8,128)(2,1)S(1)}, bf16[4,32,2048]{2,1,0:T(8,128)(2,1)}, u32[]{:S(2)}, u32[]{:S(2)}) collective-permute-start(bf16[4,32,2048]{2,1,0:T(8,128)(2,1)S(1)} %pad_maximum_fusion.1.refs_0_), channel_id=1, source_target_pairs={{0,6},{2,4},{4,2},{6,0},{8,14},{10,12},{12,10},{14,8},{16,22},{18,... | collective-permute-start | bytes 1572872 | tf_op jit(solution)/shard_map/ppermute | solution.py:364
  212.2 2.2 copy-done
  214.4 1.9 project.3.refs_3_
  216.3 1.7 collective-permute-done.39.refs_1_
  218.0 2.4 %project.4.refs_3_ = f32[4,4,32,512]{3,2,1,0:T(8,128)S(1)} custom-call(s32[11]{0:T(128)S(1)} %concatenate.15.info, bf16[4,32,2048]{2,1,0:T(8,128)(2,1)S(1)} %pad_maximum_fusion.1.refs_0_, bf16[4,32,2048]{2,1,0:T(8,128)(2,1)} %collective-permute-done.39.refs_1_, bf16[4096,512]{1,0:T(8,128)(2,1)S(1)} %copy-done.1, f32[4,4,32,512]{3,2,1,0:T(8,128)S(1)} %project.3.refs_3_), custom_call_target="tpu_custom_call" | custom-call | flops 536870912 | bytes 3145728 | tf_op jit(solution)/shard_map/project/pallas_call | solution.py:341
  220.5 3.7 %collective-permute-done.38.refs_1_ = bf16[4,32,2048]{2,1,0:T(8,128)(2,1)} collective-permute-done((bf16[4,32,2048]{2,1,0:T(8,128)(2,1)S(1)}, bf16[4,32,2048]{2,1,0:T(8,128)(2,1)}, u32[]{:S(2)}, u32[]{:S(2)}) %collective-permute-start.38) | collective-permute-done | bytes 524320 | tf_op jit(solution)/shard_map/ppermute | solution.py:364
  224.2 2.4 %project.5 = bf16[4,4,32,512]{3,2,1,0:T(8,128)(2,1)S(1)} custom-call(s32[11]{0:T(128)S(1)} %concatenate.15.info, bf16[4,32,2048]{2,1,0:T(8,128)(2,1)S(1)} %collective-permute-done.37.refs_0_, bf16[4,32,2048]{2,1,0:T(8,128)(2,1)} %collective-permute-done.38.refs_1_, bf16[4096,512]{1,0:T(8,128)(2,1)S(1)} %copy-done.1, f32[4,4,32,512]{3,2,1,0:T(8,128)S(1)} %project.4.refs_3_), custom_call_target="tpu_custom_call" | custom-call | flops 536870912 | bytes 3145728 | tf_op jit(solution)/shard_map/project/pallas_call | solution.py:341
  226.7 1.5 collective-permute-done.40
  228.2 0.8 add_convert_fusion
  (64 shorter events, 1.7 us)
Async XLA Ops:
  0.9 8.9 %collective-permute-start = (bf16[32,1024]{1,0:T(8,128)(2,1)S(1)}, bf16[32,1024]{1,0:T(8,128)(2,1)S(1)}, u32[]{:S(2)}, u32[]{:S(2)}) collective-permute-start(bf16[32,1024]{1,0:T(8,128)(2,1)S(1)} %get-tuple-element.66), channel_id=1, source_target_pairs={{0,8},{2,10},{4,12},{6,14},{8,0},{10,2},{12,4},{14,6},{16,24},{18,... | collective-permute-start | bytes 196616 | tf_op jit(solution)/shard_map/ppermute | solution.py:364
  3.9 7.3 %collective-permute-start.1 = (bf16[32,1024]{1,0:T(8,128)(2,1)S(1)}, bf16[32,1024]{1,0:T(8,128)(2,1)S(1)}, u32[]{:S(2)}, u32[]{:S(2)}) collective-permute-start(bf16[32,1024]{1,0:T(8,128)(2,1)S(1)} %get-tuple-element.66), channel_id=1, source_target_pairs={{0,16},{2,18},{4,20},{6,22},{8,24},{10,26},{12,28},{14,30},{16,0},... | collective-permute-start | bytes 196616 | tf_op jit(solution)/shard_map/ppermute | solution.py:364
  6.5 6.1 %collective-permute-start.2 = (bf16[32,1024]{1,0:T(8,128)(2,1)S(1)}, bf16[32,1024]{1,0:T(8,128)(2,1)S(1)}, u32[]{:S(2)}, u32[]{:S(2)}) collective-permute-start(bf16[32,1024]{1,0:T(8,128)(2,1)S(1)} %get-tuple-element.66), channel_id=1, source_target_pairs={{0,24},{2,26},{4,28},{6,30},{8,16},{10,18},{12,20},{14,22},{16,8},... | collective-permute-start | bytes 196616 | tf_op jit(solution)/shard_map/ppermute | solution.py:364
  12.6 8.8 %collective-permute-start.6 = (bf16[32,3072]{1,0:T(8,128)(2,1)S(1)}, bf16[32,3072]{1,0:T(8,128)(2,1)S(1)}, u32[]{:S(2)}, u32[]{:S(2)}) collective-permute-start(bf16[32,3072]{1,0:T(8,128)(2,1)S(1)} %slice.7), channel_id=1, source_target_pairs={{0,8},{2,10},{4,12},{6,14},{8,0},{10,2},{12,4},{14,6},{16,24},{18,... | collective-permute-start | bytes 589832 | tf_op jit(solution)/shard_map/ppermute | solution.py:364
  12.7 16.9 %collective-permute-start.7 = (bf16[32,3072]{1,0:T(8,128)(2,1)S(1)}, bf16[32,3072]{1,0:T(8,128)(2,1)S(1)}, u32[]{:S(2)}, u32[]{:S(2)}) collective-permute-start(bf16[32,3072]{1,0:T(8,128)(2,1)S(1)} %slice.7), channel_id=1, source_target_pairs={{0,16},{2,18},{4,20},{6,22},{8,24},{10,26},{12,28},{14,30},{16,0},... | collective-permute-start | bytes 589832 | tf_op jit(solution)/shard_map/ppermute | solution.py:364
  15.1 14.5 %collective-permute-start.8 = (bf16[32,3072]{1,0:T(8,128)(2,1)S(1)}, bf16[32,3072]{1,0:T(8,128)(2,1)S(1)}, u32[]{:S(2)}, u32[]{:S(2)}) collective-permute-start(bf16[32,3072]{1,0:T(8,128)(2,1)S(1)} %slice.7), channel_id=1, source_target_pairs={{0,24},{2,26},{4,28},{6,30},{8,16},{10,18},{12,20},{14,22},{16,8},... | collective-permute-start | bytes 589832 | tf_op jit(solution)/shard_map/ppermute | solution.py:364
  18.5 14.3 %collective-permute-start.3 = (bf16[4,32,1024]{2,1,0:T(8,128)(2,1)S(1)}, bf16[4,32,1024]{2,1,0:T(8,128)(2,1)S(1)}, u32[]{:S(2)}, u32[]{:S(2)}) collective-permute-start(bf16[4,32,1024]{2,1,0:T(8,128)(2,1)S(1)} %pad_maximum_fusion.2.refs_0_), channel_id=1, source_target_pairs={{0,2},{2,0},{4,6},{6,4},{8,10},{10,8},{12,14},{14,12},{16,18},{18,... | collective-permute-start | bytes 786440 | tf_op jit(solution)/shard_map/ppermute | solution.py:364
  20.0 13.3 %collective-permute-start.4 = (bf16[4,32,1024]{2,1,0:T(8,128)(2,1)S(1)}, bf16[4,32,1024]{2,1,0:T(8,128)(2,1)S(1)}, u32[]{:S(2)}, u32[]{:S(2)}) collective-permute-start(bf16[4,32,1024]{2,1,0:T(8,128)(2,1)S(1)} %pad_maximum_fusion.2.refs_0_), channel_id=1, source_target_pairs={{0,4},{2,6},{4,0},{6,2},{8,12},{10,14},{12,8},{14,10},{16,20},{18,... | collective-permute-start | bytes 786440 | tf_op jit(solution)/shard_map/ppermute | solution.py:364
  21.5 11.8 %collective-permute-start.5 = (bf16[4,32,1024]{2,1,0:T(8,128)(2,1)S(1)}, bf16[4,32,1024]{2,1,0:T(8,128)(2,1)S(1)}, u32[]{:S(2)}, u32[]{:S(2)}) collective-permute-start(bf16[4,32,1024]{2,1,0:T(8,128)(2,1)S(1)} %pad_maximum_fusion.2.refs_0_), channel_id=1, source_target_pairs={{0,6},{2,4},{4,2},{6,0},{8,14},{10,12},{12,10},{14,8},{16,22},{18,... | collective-permute-start | bytes 786440 | tf_op jit(solution)/shard_map/ppermute | solution.py:364
  23.0 2.2 copy-start.2
  25.2 8.1 %copy-start.3 = (bf16[4096,512]{1,0:T(8,128)(2,1)S(1)}, bf16[4096,512]{1,0:T(8,128)(2,1)}, u32[]{:S(2)}) copy-start(bf16[4096,512]{1,0:T(8,128)(2,1)} %refs_2_.3) | copy-start | bytes 12582916
  25.2 8.1 %copy-start.4 = (bf16[32,512]{1,0:T(8,128)(2,1)S(1)}, bf16[32,512]{1,0:T(8,128)(2,1)}, u32[]{:S(2)}) copy-start(bf16[32,512]{1,0:T(8,128)(2,1)} %refs_3_.1) | copy-start | bytes 98308
  25.2 8.1 %copy-start.5 = (bf16[32,512]{1,0:T(8,128)(2,1)S(1)}, bf16[32,512]{1,0:T(8,128)(2,1)}, u32[]{:S(2)}) copy-start(bf16[32,512]{1,0:T(8,128)(2,1)} %refs_4_.4) | copy-start | bytes 98308
  29.7 30.5 %collective-permute-start.12 = (bf16[4,32,3072]{2,1,0:T(8,128)(2,1)S(1)}, bf16[4,32,3072]{2,1,0:T(8,128)(2,1)S(1)}, u32[]{:S(2)}, u32[]{:S(2)}) collective-permute-start(bf16[4,32,3072]{2,1,0:T(8,128)(2,1)S(1)} %pad_maximum_fusion.refs_8_.refs_0_), channel_id=1, source_target_pairs={{0,2},{2,0},{4,6},{6,4},{8,10},{10,8},{12,14},{14,12},{16,18},{18,... | collective-permute-start | bytes 2359304 | tf_op jit(solution)/shard_map/ppermute | solution.py:364
  31.3 38.0 %collective-permute-start.13 = (bf16[4,32,3072]{2,1,0:T(8,128)(2,1)S(1)}, bf16[4,32,3072]{2,1,0:T(8,128)(2,1)S(1)}, u32[]{:S(2)}, u32[]{:S(2)}) collective-permute-start(bf16[4,32,3072]{2,1,0:T(8,128)(2,1)S(1)} %pad_maximum_fusion.refs_8_.refs_0_), channel_id=1, source_target_pairs={{0,4},{2,6},{4,0},{6,2},{8,12},{10,14},{12,8},{14,10},{16,20},{18,... | collective-permute-start | bytes 2359304 | tf_op jit(solution)/shard_map/ppermute | solution.py:364
  32.8 36.5 %collective-permute-start.14 = (bf16[4,32,3072]{2,1,0:T(8,128)(2,1)S(1)}, bf16[4,32,3072]{2,1,0:T(8,128)(2,1)S(1)}, u32[]{:S(2)}, u32[]{:S(2)}) collective-permute-start(bf16[4,32,3072]{2,1,0:T(8,128)(2,1)S(1)} %pad_maximum_fusion.refs_8_.refs_0_), channel_id=1, source_target_pairs={{0,6},{2,4},{4,2},{6,0},{8,14},{10,12},{12,10},{14,8},{16,22},{18,... | collective-permute-start | bytes 2359304 | tf_op jit(solution)/shard_map/ppermute | solution.py:364
  57.6 38.6 %collective-permute-start.10 = (bf16[4,32,1152]{2,1,0:T(8,128)(2,1)S(1)}, bf16[4,32,1152]{2,1,0:T(8,128)(2,1)S(1)}, u32[]{:S(2)}, u32[]{:S(2)}) collective-permute-start(bf16[4,32,1152]{2,1,0:T(8,128)(2,1)S(1)} %get-tuple-element.40), channel_id=1, source_target_pairs={{0,4},{2,6},{4,0},{6,2},{8,12},{10,14},{12,8},{14,10},{16,20},{18,... | collective-permute-start | bytes 884744 | tf_op jit(solution)/shard_map/ppermute | solution.py:364
  57.7 64.0 %collective-permute-start.11 = (bf16[4,32,1152]{2,1,0:T(8,128)(2,1)S(1)}, bf16[4,32,1152]{2,1,0:T(8,128)(2,1)S(1)}, u32[]{:S(2)}, u32[]{:S(2)}) collective-permute-start(bf16[4,32,1152]{2,1,0:T(8,128)(2,1)S(1)} %get-tuple-element.41), channel_id=1, source_target_pairs={{0,6},{2,4},{4,2},{6,0},{8,14},{10,12},{12,10},{14,8},{16,22},{18,... | collective-permute-start | bytes 884744 | tf_op jit(solution)/shard_map/ppermute | solution.py:364
  60.2 61.5 %collective-permute-start.9 = (bf16[4,32,1152]{2,1,0:T(8,128)(2,1)S(1)}, bf16[4,32,1152]{2,1,0:T(8,128)(2,1)S(1)}, u32[]{:S(2)}, u32[]{:S(2)}) collective-permute-start(bf16[4,32,1152]{2,1,0:T(8,128)(2,1)S(1)} %get-tuple-element.39), channel_id=1, source_target_pairs={{0,2},{2,0},{4,6},{6,4},{8,10},{10,8},{12,14},{14,12},{16,18},{18,... | collective-permute-start | bytes 884744 | tf_op jit(solution)/shard_map/ppermute | solution.py:364
  93.6 28.1 %collective-permute-start.15 = (bf16[4,32,1152]{2,1,0:T(8,128)(2,1)S(1)}, bf16[4,32,1152]{2,1,0:T(8,128)(2,1)S(1)}, u32[]{:S(2)}, u32[]{:S(2)}) collective-permute-start(bf16[4,32,1152]{2,1,0:T(8,128)(2,1)S(1)} %get-tuple-element.43), channel_id=1, source_target_pairs={{0,2},{2,0},{4,6},{6,4},{8,10},{10,8},{12,14},{14,12},{16,18},{18,... | collective-permute-start | bytes 884744 | tf_op jit(solution)/shard_map/ppermute | solution.py:364
  93.7 28.0 %collective-permute-start.16 = (bf16[4,32,1152]{2,1,0:T(8,128)(2,1)S(1)}, bf16[4,32,1152]{2,1,0:T(8,128)(2,1)S(1)}, u32[]{:S(2)}, u32[]{:S(2)}) collective-permute-start(bf16[4,32,1152]{2,1,0:T(8,128)(2,1)S(1)} %get-tuple-element.44), channel_id=1, source_target_pairs={{0,4},{2,6},{4,0},{6,2},{8,12},{10,14},{12,8},{14,10},{16,20},{18,... | collective-permute-start | bytes 884744 | tf_op jit(solution)/shard_map/ppermute | solution.py:364
  96.2 25.5 %collective-permute-start.17 = (bf16[4,32,1152]{2,1,0:T(8,128)(2,1)S(1)}, bf16[4,32,1152]{2,1,0:T(8,128)(2,1)S(1)}, u32[]{:S(2)}, u32[]{:S(2)}) collective-permute-start(bf16[4,32,1152]{2,1,0:T(8,128)(2,1)S(1)} %get-tuple-element.45), channel_id=1, source_target_pairs={{0,6},{2,4},{4,2},{6,0},{8,14},{10,12},{12,10},{14,8},{16,22},{18,... | collective-permute-start | bytes 884744 | tf_op jit(solution)/shard_map/ppermute | solution.py:364
  123.4 6.8 %collective-permute-start.18 = (bf16[32,2304]{1,0:T(8,128)(2,1)S(1)}, bf16[32,2304]{1,0:T(8,128)(2,1)S(1)}, u32[]{:S(2)}, u32[]{:S(2)}) collective-permute-start(bf16[32,2304]{1,0:T(8,128)(2,1)S(1)} %get-tuple-element.48), channel_id=1, source_target_pairs={{0,8},{2,10},{4,12},{6,14},{8,0},{10,2},{12,4},{14,6},{16,24},{18,... | collective-permute-start | bytes 442376 | tf_op jit(solution)/shard_map/ppermute | solution.py:364
  123.5 32.6 %collective-permute-start.22 = (bf16[4,32,1152]{2,1,0:T(8,128)(2,1)S(1)}, bf16[4,32,1152]{2,1,0:T(8,128)(2,1)S(1)}, u32[]{:S(2)}, u32[]{:S(2)}) collective-permute-start(bf16[4,32,1152]{2,1,0:T(8,128)(2,1)S(1)} %get-tuple-element.52), channel_id=1, source_target_pairs={{0,2},{2,0},{4,6},{6,4},{8,10},{10,8},{12,14},{14,12},{16,18},{18,... | collective-permute-start | bytes 884744 | tf_op jit(solution)/shard_map/ppermute | solution.py:364
  123.6 32.6 %collective-permute-start.23 = (bf16[4,32,1152]{2,1,0:T(8,128)(2,1)S(1)}, bf16[4,32,1152]{2,1,0:T(8,128)(2,1)S(1)}, u32[]{:S(2)}, u32[]{:S(2)}) collective-permute-start(bf16[4,32,1152]{2,1,0:T(8,128)(2,1)S(1)} %get-tuple-element.53), channel_id=1, source_target_pairs={{0,4},{2,6},{4,0},{6,2},{8,12},{10,14},{12,8},{14,10},{16,20},{18,... | collective-permute-start | bytes 884744 | tf_op jit(solution)/shard_map/ppermute | solution.py:364
  126.1 30.7 %collective-permute-start.24 = (bf16[4,32,1152]{2,1,0:T(8,128)(2,1)S(1)}, bf16[4,32,1152]{2,1,0:T(8,128)(2,1)S(1)}, u32[]{:S(2)}, u32[]{:S(2)}) collective-permute-start(bf16[4,32,1152]{2,1,0:T(8,128)(2,1)S(1)} %get-tuple-element.54), channel_id=1, source_target_pairs={{0,6},{2,4},{4,2},{6,0},{8,14},{10,12},{12,10},{14,8},{16,22},{18,... | collective-permute-start | bytes 884744 | tf_op jit(solution)/shard_map/ppermute | solution.py:364
  127.0 23.9 %collective-permute-start.19 = (bf16[32,2304]{1,0:T(8,128)(2,1)S(1)}, bf16[32,2304]{1,0:T(8,128)(2,1)S(1)}, u32[]{:S(2)}, u32[]{:S(2)}) collective-permute-start(bf16[32,2304]{1,0:T(8,128)(2,1)S(1)} %get-tuple-element.49), channel_id=1, source_target_pairs={{0,16},{2,18},{4,20},{6,22},{8,24},{10,26},{12,28},{14,30},{16,0},... | collective-permute-start | bytes 442376 | tf_op jit(solution)/shard_map/ppermute | solution.py:364
  130.2 20.9 %collective-permute-start.20 = (bf16[32,2304]{1,0:T(8,128)(2,1)S(1)}, bf16[32,2304]{1,0:T(8,128)(2,1)S(1)}, u32[]{:S(2)}, u32[]{:S(2)}) collective-permute-start(bf16[32,2304]{1,0:T(8,128)(2,1)S(1)} %get-tuple-element.50), channel_id=1, source_target_pairs={{0,24},{2,26},{4,28},{6,30},{8,16},{10,18},{12,20},{14,22},{16,8},... | collective-permute-start | bytes 442376 | tf_op jit(solution)/shard_map/ppermute | solution.py:364
  151.0 13.3 %collective-permute-start.25 = (bf16[4,32,1152]{2,1,0:T(8,128)(2,1)S(1)}, bf16[4,32,1152]{2,1,0:T(8,128)(2,1)S(1)}, u32[]{:S(2)}, u32[]{:S(2)}) collective-permute-start(bf16[4,32,1152]{2,1,0:T(8,128)(2,1)S(1)} %get-tuple-element.51.refs_4_), channel_id=1, source_target_pairs={{0,2},{2,0},{4,6},{6,4},{8,10},{10,8},{12,14},{14,12},{16,18},{18,... | collective-permute-start | bytes 884744 | tf_op jit(solution)/shard_map/ppermute | solution.py:364
  151.1 13.2 %collective-permute-start.26 = (bf16[4,32,1152]{2,1,0:T(8,128)(2,1)S(1)}, bf16[4,32,1152]{2,1,0:T(8,128)(2,1)S(1)}, u32[]{:S(2)}, u32[]{:S(2)}) collective-permute-start(bf16[4,32,1152]{2,1,0:T(8,128)(2,1)S(1)} %get-tuple-element.55), channel_id=1, source_target_pairs={{0,4},{2,6},{4,0},{6,2},{8,12},{10,14},{12,8},{14,10},{16,20},{18,... | collective-permute-start | bytes 884744 | tf_op jit(solution)/shard_map/ppermute | solution.py:364
  156.1 8.2 %collective-permute-start.27 = (bf16[4,32,1152]{2,1,0:T(8,128)(2,1)S(1)}, bf16[4,32,1152]{2,1,0:T(8,128)(2,1)S(1)}, u32[]{:S(2)}, u32[]{:S(2)}) collective-permute-start(bf16[4,32,1152]{2,1,0:T(8,128)(2,1)S(1)} %get-tuple-element.56), channel_id=1, source_target_pairs={{0,6},{2,4},{4,2},{6,0},{8,14},{10,12},{12,10},{14,8},{16,22},{18,... | collective-permute-start | bytes 884744 | tf_op jit(solution)/shard_map/ppermute | solution.py:364
  156.2 8.0 %collective-permute-start.21 = (bf16[1,32,2048]{2,1,0:T(8,128)(2,1)S(1)}, bf16[1,32,2048]{2,1,0:T(8,128)(2,1)S(1)}, u32[]{:S(2)}, u32[]{:S(2)}) collective-permute-start(bf16[1,32,2048]{2,1,0:T(8,128)(2,1)S(1)} %bitcast.20), channel_id=1, source_target_pairs={{0,16},{2,18},{4,20},{6,22},{8,24},{10,26},{12,28},{14,30},{16,0},... | collective-permute-start | bytes 393224 | tf_op jit(solution)/shard_map/ppermute | solution.py:364
  164.3 9.2 %collective-permute-start.28 = (bf16[2,32,2048]{2,1,0:T(8,128)(2,1)S(1)}, bf16[2,32,2048]{2,1,0:T(8,128)(2,1)S(1)}, u32[]{:S(2)}, u32[]{:S(2)}) collective-permute-start(bf16[2,32,2048]{2,1,0:T(8,128)(2,1)S(1)} %pad_maximum_fusion.3.refs_9_), channel_id=1, source_target_pairs={{0,8},{2,10},{4,12},{6,14},{8,0},{10,2},{12,4},{14,6},{16,24},{18,... | collective-permute-start | bytes 786440 | tf_op jit(solution)/shard_map/ppermute | solution.py:364
  173.5 17.6 %collective-permute-start.32 = (bf16[4,32,2048]{2,1,0:T(8,128)(2,1)S(1)}, bf16[4,32,2048]{2,1,0:T(8,128)(2,1)S(1)}, u32[]{:S(2)}, u32[]{:S(2)}) collective-permute-start(bf16[4,32,2048]{2,1,0:T(8,128)(2,1)S(1)} %constant_dynamic-update-slice_fusion.refs_0_), channel_id=1, source_target_pairs={{0,2},{2,0},{4,6},{6,4},{8,10},{10,8},{12,14},{14,12},{16,18},{18,... | collective-permute-start | bytes 1572872 | tf_op jit(solution)/shard_map/ppermute | solution.py:364
  174.4 16.9 %collective-permute-start.33 = (bf16[4,32,2048]{2,1,0:T(8,128)(2,1)S(1)}, bf16[4,32,2048]{2,1,0:T(8,128)(2,1)S(1)}, u32[]{:S(2)}, u32[]{:S(2)}) collective-permute-start(bf16[4,32,2048]{2,1,0:T(8,128)(2,1)S(1)} %constant_dynamic-update-slice_fusion.refs_0_), channel_id=1, source_target_pairs={{0,4},{2,6},{4,0},{6,2},{8,12},{10,14},{12,8},{14,10},{16,20},{18,... | collective-permute-start | bytes 1572872 | tf_op jit(solution)/shard_map/ppermute | solution.py:364
  180.2 7.8 %collective-permute-start.29 = (bf16[32,2304]{1,0:T(8,128)(2,1)S(1)}, bf16[32,2304]{1,0:T(8,128)(2,1)S(1)}, u32[]{:S(2)}, u32[]{:S(2)}) collective-permute-start(bf16[32,2304]{1,0:T(8,128)(2,1)S(1)} %get-tuple-element.59), channel_id=1, source_target_pairs={{0,8},{2,10},{4,12},{6,14},{8,0},{10,2},{12,4},{14,6},{16,24},{18,... | collective-permute-start | bytes 442376 | tf_op jit(solution)/shard_map/ppermute | solution.py:364
  180.3 7.7 %collective-permute-start.30 = (bf16[32,2304]{1,0:T(8,128)(2,1)S(1)}, bf16[32,2304]{1,0:T(8,128)(2,1)S(1)}, u32[]{:S(2)}, u32[]{:S(2)}) collective-permute-start(bf16[32,2304]{1,0:T(8,128)(2,1)S(1)} %get-tuple-element.60), channel_id=1, source_target_pairs={{0,16},{2,18},{4,20},{6,22},{8,24},{10,26},{12,28},{14,30},{16,0},... | collective-permute-start | bytes 442376 | tf_op jit(solution)/shard_map/ppermute | solution.py:364
  180.3 10.8 %collective-permute-start.31 = (bf16[32,2304]{1,0:T(8,128)(2,1)S(1)}, bf16[32,2304]{1,0:T(8,128)(2,1)S(1)}, u32[]{:S(2)}, u32[]{:S(2)}) collective-permute-start(bf16[32,2304]{1,0:T(8,128)(2,1)S(1)} %get-tuple-element.61), channel_id=1, source_target_pairs={{0,24},{2,26},{4,28},{6,30},{8,16},{10,18},{12,20},{14,22},{16,8},... | collective-permute-start | bytes 442376 | tf_op jit(solution)/shard_map/ppermute | solution.py:364
  191.9 7.2 %collective-permute-start.34 = (bf16[1,32,2048]{2,1,0:T(8,128)(2,1)S(1)}, bf16[1,32,2048]{2,1,0:T(8,128)(2,1)S(1)}, u32[]{:S(2)}, u32[]{:S(2)}) collective-permute-start(bf16[1,32,2048]{2,1,0:T(8,128)(2,1)S(1)} %bitcast.22), channel_id=1, source_target_pairs={{0,16},{2,18},{4,20},{6,22},{8,24},{10,26},{12,28},{14,30},{16,0},... | collective-permute-start | bytes 393224 | tf_op jit(solution)/shard_map/ppermute | solution.py:364
  192.9 15.9 %collective-permute-start.36 = (bf16[4,32,2048]{2,1,0:T(8,128)(2,1)S(1)}, bf16[4,32,2048]{2,1,0:T(8,128)(2,1)S(1)}, u32[]{:S(2)}, u32[]{:S(2)}) collective-permute-start(bf16[4,32,2048]{2,1,0:T(8,128)(2,1)S(1)} %constant_dynamic-update-slice_fusion.refs_0_), channel_id=1, source_target_pairs={{0,6},{2,4},{4,2},{6,0},{8,14},{10,12},{12,10},{14,8},{16,22},{18,... | collective-permute-start | bytes 1572872 | tf_op jit(solution)/shard_map/ppermute | solution.py:364
  199.2 6.4 %collective-permute-start.35 = (bf16[2,32,2048]{2,1,0:T(8,128)(2,1)S(1)}, bf16[2,32,2048]{2,1,0:T(8,128)(2,1)S(1)}, u32[]{:S(2)}, u32[]{:S(2)}) collective-permute-start(bf16[2,32,2048]{2,1,0:T(8,128)(2,1)S(1)} %pad_maximum_fusion.4), channel_id=1, source_target_pairs={{0,8},{2,10},{4,12},{6,14},{8,0},{10,2},{12,4},{14,6},{16,24},{18,... | collective-permute-start | bytes 786440 | tf_op jit(solution)/shard_map/ppermute | solution.py:364
  208.7 9.3 %collective-permute-start.39 = (bf16[4,32,2048]{2,1,0:T(8,128)(2,1)S(1)}, bf16[4,32,2048]{2,1,0:T(8,128)(2,1)}, u32[]{:S(2)}, u32[]{:S(2)}) collective-permute-start(bf16[4,32,2048]{2,1,0:T(8,128)(2,1)S(1)} %pad_maximum_fusion.1.refs_0_), channel_id=1, source_target_pairs={{0,2},{2,0},{4,6},{6,4},{8,10},{10,8},{12,14},{14,12},{16,18},{18,... | collective-permute-start | bytes 1572872 | tf_op jit(solution)/shard_map/ppermute | solution.py:364
  208.8 11.6 %collective-permute-start.37 = (bf16[4,32,2048]{2,1,0:T(8,128)(2,1)S(1)}, bf16[4,32,2048]{2,1,0:T(8,128)(2,1)S(1)}, u32[]{:S(2)}, u32[]{:S(2)}) collective-permute-start(bf16[4,32,2048]{2,1,0:T(8,128)(2,1)S(1)} %pad_maximum_fusion.1.refs_0_), channel_id=1, source_target_pairs={{0,4},{2,6},{4,0},{6,2},{8,12},{10,14},{12,8},{14,10},{16,20},{18,... | collective-permute-start | bytes 1572872 | tf_op jit(solution)/shard_map/ppermute | solution.py:364
  209.9 14.3 %collective-permute-start.38 = (bf16[4,32,2048]{2,1,0:T(8,128)(2,1)S(1)}, bf16[4,32,2048]{2,1,0:T(8,128)(2,1)}, u32[]{:S(2)}, u32[]{:S(2)}) collective-permute-start(bf16[4,32,2048]{2,1,0:T(8,128)(2,1)S(1)} %pad_maximum_fusion.1.refs_0_), channel_id=1, source_target_pairs={{0,6},{2,4},{4,2},{6,0},{8,14},{10,12},{12,10},{14,8},{16,22},{18,... | collective-permute-start | bytes 1572872 | tf_op jit(solution)/shard_map/ppermute | solution.py:364
  212.2 2.2 copy-start
  214.4 3.6 %copy-start.1 = (bf16[4096,512]{1,0:T(8,128)(2,1)S(1)}, bf16[4096,512]{1,0:T(8,128)(2,1)}, u32[]{:S(2)}) copy-start(bf16[4096,512]{1,0:T(8,128)(2,1)} %refs_2_.5) | copy-start | bytes 12582916
  226.6 1.6 collective-permute-start.40

commit v13 on v12

--- a/solution.py
+++ b/solution.py
@@ -373,6 +373,28 @@
     heads = context_keys.shape[1] // HEAD_SIZE
     width = GROUP_QUERIES * HEAD_SIZE
 
+    def doubled(column):
+        stack, order, distance = column
+        if not distance:
+            return column
+        stack = jnp.concatenate([stack, exchange(stack, "ctx", distance * plane)])
+        return stack, order + [a ^ distance for a in order], distance // 2
+
+    def gather_plane(stack):
+        return [stack] + [exchange(stack, "ctx", b) for b in range(1, plane)]
+
+    own = queries[:, :width]
+    near = [exchange(own, "ctx", a * plane) for a in range(1, blocks)]
+    first = jnp.stack([own] + near)
+    sources, stacks = [(gather_plane(first), 0)], []
+    if heads > 1:
+        held, _ = lax.optimization_barrier((queries[:, width:], near[0]))
+        early = [exchange(held, "ctx", a * plane) for a in range(1, blocks)]
+        keys_t = transpose_keys(context_keys, early[:1])
+        selected, _ = lax.optimization_barrier((selected, early[0]))
+    else:
+        keys_t = transpose_keys(context_keys, [])
+
     slot_block = lax.div(me, plane) ^ jnp.arange(blocks, dtype=jnp.int32)
     wanted = jnp.any(selected == me, axis=1)[slot_block]
     order = jnp.argsort(jnp.logical_not(wanted), stable=True).astype(jnp.int32)
@@ -384,31 +406,11 @@
         ]
     )
 
-    def doubled(column):
-        stack, order, distance = column
-        if not distance:
-            return column
-        stack = jnp.concatenate([stack, exchange(stack, "ctx", distance * plane)])
-        return stack, order + [a ^ distance for a in order], distance // 2
-
-    def stack_blocks(x):
-        return jnp.stack([x] + [exchange(x, "ctx", a * plane) for a in range(1, blocks)])
-
-    def gather_plane(stack):
-        return [stack] + [exchange(stack, "ctx", b) for b in range(1, plane)]
-
-    first = stack_blocks(queries[:, :width])
-    sources, stacks = [(gather_plane(first), 0)], []
     if heads > 1:
-        held, _ = lax.optimization_barrier((queries[:, width:], first))
-        early = [exchange(held, "ctx", a * plane) for a in range(1, blocks)]
-        keys_t = transpose_keys(context_keys, early[:1])
-        held, _ = lax.optimization_barrier((held, keys_t))
+        held, *_ = lax.optimization_barrier((held, keys_t, info))
         stacks = [jnp.stack([held] + early)]
         pieces = gather_plane(stacks[0])
         sources += [(pieces, i) for i in range(heads - 1)]
-    else:
-        keys_t = transpose_keys(context_keys, [])
 
     size = 2 if heads % 2 == 0 else 1
     attended, merged, rows_of = [], [], []

time: 230 us -> 228 us (level)
  starting transfers between devices: 53.2 us -> 70 us
  Pallas kernels: 113 us -> 96.8 us
    ppermute x41, starting transfers between devices: 53.2 us -> 70 us  [exchange(): return lax.ppermute(x, axis, [(i, i ^ distance) for i in range(count)])]
    pallas_call x5, Pallas kernels: 100 us -> 83.8 us  [attend_head(): pl.pallas_call(functools.partial(attend_kernel, chosen=chosen, blocks=blo...]
  transfers between devices with their start and end apart: 41 -> 41, of which waited for: 15 -> 12; matrix products, arithmetic and copies ran while one was open for 2% -> 2% of each run, Pallas kernels for 47% -> 40%
where the time goes in v13:
time: 228 us; the launch traced here: 227 us
  Pallas kernels  96.8 us (42%)
  starting transfers between devices  70 us (31%)
  waiting for transfers between devices  49.5 us (22%)
  local copies, waits for them, and re-layouts  7.6 us (3%)
  other arithmetic  3.26 us (1%)
    pallas_call x5, Pallas kernels, attend_head(): pl.pallas_call(functools.partial(attend_kernel, chosen=chosen, blocks=blo...  83.8 us
    ppermute x41, starting transfers between devices, exchange(): return lax.ppermute(x, axis, [(i, i ^ distance) for i in range(count)])  70 us
    ppermute x41, waiting for transfers between devices, exchange(): return lax.ppermute(x, axis, [(i, i ^ distance) for i in range(count)])  49.5 us
    pallas_call x3, Pallas kernels, project(): pl.pallas_call(functools.partial(project_kernel, order=order, chosen=chos...  6.71 us
  transfers between devices with their start and end apart: 41, of which 12 were waited for; matrix products, arithmetic and copies ran while one was open for 2% of the time, Pallas kernels for 40%

profile of v13, /device:TPU:0, one launch (start us, length us, event | category | flops | bytes accessed | tf_op | source)
XLA Modules:
  0.0 227.5 jit_solution(3836094808501859953)
XLA Ops:
  0.0 0.8 slice_bitcast_fusion
  0.9 3.1 %collective-permute-start = (bf16[32,1024]{1,0:T(8,128)(2,1)S(1)}, bf16[32,1024]{1,0:T(8,128)(2,1)S(1)}, u32[]{:S(2)}, u32[]{:S(2)}) collective-permute-start(bf16[32,1024]{1,0:T(8,128)(2,1)S(1)} %get-tuple-element.68), channel_id=1, source_target_pairs={{0,8},{2,10},{4,12},{6,14},{8,0},{10,2},{12,4},{14,6},{16,24},{18,... | collective-permute-start | bytes 196616 | tf_op jit(solution)/shard_map/ppermute | solution.py:364
  3.9 2.6 %collective-permute-start.2 = (bf16[32,1024]{1,0:T(8,128)(2,1)S(1)}, bf16[32,1024]{1,0:T(8,128)(2,1)S(1)}, u32[]{:S(2)}, u32[]{:S(2)}) collective-permute-start(bf16[32,1024]{1,0:T(8,128)(2,1)S(1)} %get-tuple-element.68), channel_id=1, source_target_pairs={{0,16},{2,18},{4,20},{6,22},{8,24},{10,26},{12,28},{14,30},{16,0},... | collective-permute-start | bytes 196616 | tf_op jit(solution)/shard_map/ppermute | solution.py:364
  6.5 0.9 slice.6
  7.5 1.0 collective-permute-start.1
  8.5 3.5 %collective-permute-start.7 = (bf16[32,3072]{1,0:T(8,128)(2,1)S(1)}, bf16[32,3072]{1,0:T(8,128)(2,1)S(1)}, u32[]{:S(2)}, u32[]{:S(2)}) collective-permute-start(bf16[32,3072]{1,0:T(8,128)(2,1)S(1)} %slice.6), channel_id=1, source_target_pairs={{0,16},{2,18},{4,20},{6,22},{8,24},{10,26},{12,28},{14,30},{16,0},... | collective-permute-start | bytes 589832 | tf_op jit(solution)/shard_map/ppermute | solution.py:364
  12.0 1.3 collective-permute-done.3
  13.3 1.6 collective-permute-start.4
  14.9 1.5 collective-permute-start.5
  16.4 2.6 %collective-permute-done.1.refs_0_ = bf16[32,3072]{1,0:T(8,128)(2,1)S(1)} collective-permute-done((bf16[32,3072]{1,0:T(8,128)(2,1)S(1)}, bf16[32,3072]{1,0:T(8,128)(2,1)S(1)}, u32[]{:S(2)}, u32[]{:S(2)}) %collective-permute-start.1) | collective-permute-done | bytes 196640 | tf_op jit(solution)/shard_map/ppermute | solution.py:364
  19.0 2.4 %collective-permute-start.6 = (bf16[4,32,1024]{2,1,0:T(8,128)(2,1)S(1)}, bf16[4,32,1024]{2,1,0:T(8,128)(2,1)S(1)}, u32[]{:S(2)}, u32[]{:S(2)}) collective-permute-start(bf16[4,32,1024]{2,1,0:T(8,128)(2,1)S(1)} %pad_maximum_fusion.2.refs_0_), channel_id=1, source_target_pairs={{0,6},{2,4},{4,2},{6,0},{8,14},{10,12},{12,10},{14,8},{16,22},{18,... | collective-permute-start | bytes 786440 | tf_op jit(solution)/shard_map/ppermute | solution.py:364
  21.4 0.8 compare_reduce_fusion
  22.2 0.6 gather_fusion
  22.9 0.8 sort.17
  23.6 0.7 convert_reduce_fusion
  24.3 0.7 concatenate.15.info
  25.0 2.2 copy-done.2
  27.2 1.7 transpose.8.refs_4_.refs_3_.refs_1_
  29.0 0.6 collective-permute-start.12
  30.2 2.4 %collective-permute-start.14 = (bf16[4,32,3072]{2,1,0:T(8,128)(2,1)S(1)}, bf16[4,32,3072]{2,1,0:T(8,128)(2,1)S(1)}, u32[]{:S(2)}, u32[]{:S(2)}) collective-permute-start(bf16[4,32,3072]{2,1,0:T(8,128)(2,1)S(1)} %pad_maximum_fusion.refs_8_.refs_0_), channel_id=1, source_target_pairs={{0,6},{2,4},{4,2},{6,0},{8,14},{10,12},{12,10},{14,8},{16,22},{18,... | collective-permute-start | bytes 2359304 | tf_op jit(solution)/shard_map/ppermute | solution.py:364
  32.6 20.2 %attend.5 = (bf16[4,32,1152]{2,1,0:T(8,128)(2,1)S(1)}, bf16[4,32,1152]{2,1,0:T(8,128)(2,1)S(1)}, bf16[4,32,1152]{2,1,0:T(8,128)(2,1)S(1)}, bf16[4,32,1152]{2,1,0:T(8,128)(2,1)S(1)}) custom-call(s32[11]{0:T(128)S(1)} %concatenate.15.info, bf16[4,32,1024]{2,1,0:T(8,128)(2,1)S(1)} %pad_maximum_fusion.2.refs_0_, ...), custom_call_target="tpu_custom_call" | custom-call | flops 17179869184 | bytes 4194304 | tf_op jit(solution)/shard_map/attend/pallas_call | solution.py:177
  52.8 4.7 %collective-permute-start.10 = (bf16[4,32,1152]{2,1,0:T(8,128)(2,1)S(1)}, bf16[4,32,1152]{2,1,0:T(8,128)(2,1)S(1)}, u32[]{:S(2)}, u32[]{:S(2)}) collective-permute-start(bf16[4,32,1152]{2,1,0:T(8,128)(2,1)S(1)} %get-tuple-element.42), channel_id=1, source_target_pairs={{0,4},{2,6},{4,0},{6,2},{8,12},{10,14},{12,8},{14,10},{16,20},{18,... | collective-permute-start | bytes 884744 | tf_op jit(solution)/shard_map/ppermute | solution.py:364
  57.5 1.5 collective-permute-start.9
  59.0 10.5 %collective-permute-done.13.refs_2_.refs_1_ = bf16[4,32,3072]{2,1,0:T(8,128)(2,1)S(1)} collective-permute-done((bf16[4,32,3072]{2,1,0:T(8,128)(2,1)S(1)}, bf16[4,32,3072]{2,1,0:T(8,128)(2,1)S(1)}, u32[]{:S(2)}, u32[]{:S(2)}) %collective-permute-start.13) | collective-permute-done | bytes 786464 | tf_op jit(solution)/shard_map/ppermute | solution.py:364
  69.5 20.2 %attend.6 = (bf16[4,32,1152]{2,1,0:T(8,128)(2,1)S(1)}, bf16[4,32,1152]{2,1,0:T(8,128)(2,1)S(1)}, bf16[4,32,1152]{2,1,0:T(8,128)(2,1)S(1)}, bf16[4,32,1152]{2,1,0:T(8,128)(2,1)S(1)}) custom-call(s32[11]{0:T(128)S(1)} %concatenate.15.info, bf16[4,32,3072]{2,1,0:T(8,128)(2,1)S(1)} %pad_maximum_fusion.refs_8_.refs_0_, ...), custom_call_target="tpu_custom_call" | custom-call | flops 17179869184 | bytes 4194304 | tf_op jit(solution)/shard_map/attend/pallas_call | solution.py:177
  89.7 4.0 %collective-permute-start.15 = (bf16[4,32,1152]{2,1,0:T(8,128)(2,1)S(1)}, bf16[4,32,1152]{2,1,0:T(8,128)(2,1)S(1)}, u32[]{:S(2)}, u32[]{:S(2)}) collective-permute-start(bf16[4,32,1152]{2,1,0:T(8,128)(2,1)S(1)} %get-tuple-element.45), channel_id=1, source_target_pairs={{0,2},{2,0},{4,6},{6,4},{8,10},{10,8},{12,14},{14,12},{16,18},{18,... | collective-permute-start | bytes 884744 | tf_op jit(solution)/shard_map/ppermute | solution.py:364
  93.7 1.5 collective-permute-start.17
  95.2 20.4 %attend.7 = (bf16[4,32,1152]{2,1,0:T(8,128)(2,1)S(1)}, bf16[4,32,1152]{2,1,0:T(8,128)(2,1)S(1)}, bf16[4,32,1152]{2,1,0:T(8,128)(2,1)S(1)}, bf16[4,32,1152]{2,1,0:T(8,128)(2,1)S(1)}) custom-call(s32[11]{0:T(128)S(1)} %concatenate.15.info, bf16[4,32,3072]{2,1,0:T(8,128)(2,1)S(1)} %pad_maximum_fusion.refs_8_.refs_0_, ...), custom_call_target="tpu_custom_call" | custom-call | flops 17179869184 | bytes 4194304 | tf_op jit(solution)/shard_map/attend/pallas_call | solution.py:177
  115.7 1.7 merge.2
  117.4 10.0 %collective-permute-start.18 = (bf16[32,2304]{1,0:T(8,128)(2,1)S(1)}, bf16[32,2304]{1,0:T(8,128)(2,1)S(1)}, u32[]{:S(2)}, u32[]{:S(2)}) collective-permute-start(bf16[32,2304]{1,0:T(8,128)(2,1)S(1)} %get-tuple-element.50), channel_id=1, source_target_pairs={{0,8},{2,10},{4,12},{6,14},{8,0},{10,2},{12,4},{14,6},{16,24},{18,... | collective-permute-start | bytes 442376 | tf_op jit(solution)/shard_map/ppermute | solution.py:364
  127.4 3.5 %collective-permute-start.24 = (bf16[4,32,1152]{2,1,0:T(8,128)(2,1)S(1)}, bf16[4,32,1152]{2,1,0:T(8,128)(2,1)S(1)}, u32[]{:S(2)}, u32[]{:S(2)}) collective-permute-start(bf16[4,32,1152]{2,1,0:T(8,128)(2,1)S(1)} %get-tuple-element.56), channel_id=1, source_target_pairs={{0,6},{2,4},{4,2},{6,0},{8,14},{10,12},{12,10},{14,8},{16,22},{18,... | collective-permute-start | bytes 884744 | tf_op jit(solution)/shard_map/ppermute | solution.py:364
  130.9 2.4 %collective-permute-start.20 = (bf16[32,2304]{1,0:T(8,128)(2,1)S(1)}, bf16[32,2304]{1,0:T(8,128)(2,1)S(1)}, u32[]{:S(2)}, u32[]{:S(2)}) collective-permute-start(bf16[32,2304]{1,0:T(8,128)(2,1)S(1)} %get-tuple-element.52), channel_id=1, source_target_pairs={{0,24},{2,26},{4,28},{6,30},{8,16},{10,18},{12,20},{14,22},{16,8},... | collective-permute-start | bytes 442376 | tf_op jit(solution)/shard_map/ppermute | solution.py:364
  133.3 16.6 %attend.8 = (bf16[4,32,1152]{2,1,0:T(8,128)(2,1)S(1)}, bf16[4,32,1152]{2,1,0:T(8,128)(2,1)S(1)}, bf16[4,32,1152]{2,1,0:T(8,128)(2,1)S(1)}) custom-call(s32[11]{0:T(128)S(1)} %concatenate.15.info, bf16[4,32,3072]{2,1,0:T(8,128)(2,1)S(1)} %collective-permute-done.12.refs_1_.refs_0_, bf16[4,32,3072]{2,1,0:T(8,128)(2,1)S(1)} %collective-permute-done.13.refs_2_.refs_1_, ...), custom_call_target="tpu_custom_call" | custom-call | flops 12884901888 | bytes 3670016 | tf_op jit(solution)/shard_map/attend/pallas_call | solution.py:177
  150.1 3.0 %collective-permute-start.26 = (bf16[4,32,1152]{2,1,0:T(8,128)(2,1)S(1)}, bf16[4,32,1152]{2,1,0:T(8,128)(2,1)S(1)}, u32[]{:S(2)}, u32[]{:S(2)}) collective-permute-start(bf16[4,32,1152]{2,1,0:T(8,128)(2,1)S(1)} %get-tuple-element.57), channel_id=1, source_target_pairs={{0,4},{2,6},{4,0},{6,2},{8,12},{10,14},{12,8},{14,10},{16,20},{18,... | collective-permute-start | bytes 884744 | tf_op jit(solution)/shard_map/ppermute | solution.py:364
  153.1 0.6 normalize.2.refs_5_
  153.7 1.4 collective-permute-start.27
  155.2 1.4 collective-permute-start.21
  156.6 6.4 %attend.9.refs_4_.refs_8_ = bf16[4,32,1152]{2,1,0:T(8,128)(2,1)S(1)} custom-call(s32[11]{0:T(128)S(1)} %concatenate.15.info, bf16[4,32,3072]{2,1,0:T(8,128)(2,1)S(1)} %pad_maximum_fusion.refs_8_.refs_0_, bf16[512,4096]{1,0:T(8,128)(2,1)S(1)} %transpose.8.refs_4_.refs_3_.refs_1_, bf16[4096,512]{1,0:T(8,128)(2,1)S(1)} %copy-done.3, ...), custom_call_target="tpu_custom_call" | custom-call | flops 4294967296 | bytes 2621440 | tf_op jit(solution)/shard_map/attend/pallas_call | solution.py:177
  163.1 3.6 %collective-permute-start.28 = (bf16[2,32,2048]{2,1,0:T(8,128)(2,1)S(1)}, bf16[2,32,2048]{2,1,0:T(8,128)(2,1)S(1)}, u32[]{:S(2)}, u32[]{:S(2)}) collective-permute-start(bf16[2,32,2048]{2,1,0:T(8,128)(2,1)S(1)} %pad_maximum_fusion.3.refs_9_), channel_id=1, source_target_pairs={{0,8},{2,10},{4,12},{6,14},{8,0},{10,2},{12,4},{14,6},{16,24},{18,... | collective-permute-start | bytes 786440 | tf_op jit(solution)/shard_map/ppermute | solution.py:364
  166.8 6.9 %collective-permute-done.28 = bf16[2,32,2048]{2,1,0:T(8,128)(2,1)S(1)} collective-permute-done((bf16[2,32,2048]{2,1,0:T(8,128)(2,1)S(1)}, bf16[2,32,2048]{2,1,0:T(8,128)(2,1)S(1)}, u32[]{:S(2)}, u32[]{:S(2)}) %collective-permute-start.28) | collective-permute-done | bytes 262176 | tf_op jit(solution)/shard_map/ppermute | solution.py:364
  173.8 2.2 collective-permute-start.33
  176.0 1.7 merge.3
  177.7 0.5 collective-permute-start.29
  178.2 0.8 collective-permute-start.30
  179.0 3.1 %collective-permute-start.31 = (bf16[32,2304]{1,0:T(8,128)(2,1)S(1)}, bf16[32,2304]{1,0:T(8,128)(2,1)S(1)}, u32[]{:S(2)}, u32[]{:S(2)}) collective-permute-start(bf16[32,2304]{1,0:T(8,128)(2,1)S(1)} %get-tuple-element.63), channel_id=1, source_target_pairs={{0,24},{2,26},{4,28},{6,30},{8,16},{10,18},{12,20},{14,22},{16,8},... | collective-permute-start | bytes 442376 | tf_op jit(solution)/shard_map/ppermute | solution.py:364
  182.1 3.9 %collective-permute-done.29.refs_1_ = bf16[32,2304]{1,0:T(8,128)(2,1)S(1)} collective-permute-done((bf16[32,2304]{1,0:T(8,128)(2,1)S(1)}, bf16[32,2304]{1,0:T(8,128)(2,1)S(1)}, u32[]{:S(2)}, u32[]{:S(2)}) %collective-permute-start.29) | collective-permute-done | bytes 147488 | tf_op jit(solution)/shard_map/ppermute | solution.py:364
  186.0 2.6 %collective-permute-done.31.refs_3_ = bf16[32,2304]{1,0:T(8,128)(2,1)S(1)} collective-permute-done((bf16[32,2304]{1,0:T(8,128)(2,1)S(1)}, bf16[32,2304]{1,0:T(8,128)(2,1)S(1)}, u32[]{:S(2)}, u32[]{:S(2)}) %collective-permute-start.31) | collective-permute-done | bytes 147488 | tf_op jit(solution)/shard_map/ppermute | solution.py:364
  188.6 0.6 normalize.3
  189.3 0.8 collective-permute-start.34
  190.1 2.3 %collective-permute-start.36 = (bf16[4,32,2048]{2,1,0:T(8,128)(2,1)S(1)}, bf16[4,32,2048]{2,1,0:T(8,128)(2,1)S(1)}, u32[]{:S(2)}, u32[]{:S(2)}) collective-permute-start(bf16[4,32,2048]{2,1,0:T(8,128)(2,1)S(1)} %constant_dynamic-update-slice_fusion.refs_0_), channel_id=1, source_target_pairs={{0,6},{2,4},{4,2},{6,0},{8,14},{10,12},{12,10},{14,8},{16,22},{18,... | collective-permute-start | bytes 1572872 | tf_op jit(solution)/shard_map/ppermute | solution.py:364
  192.4 4.2 %collective-permute-done.34 = bf16[1,32,2048]{2,1,0:T(8,128)(2,1)S(1)} collective-permute-done((bf16[1,32,2048]{2,1,0:T(8,128)(2,1)S(1)}, bf16[1,32,2048]{2,1,0:T(8,128)(2,1)S(1)}, u32[]{:S(2)}, u32[]{:S(2)}) %collective-permute-start.34) | collective-permute-done | bytes 131104 | tf_op jit(solution)/shard_map/ppermute | solution.py:364
  196.7 6.4 %collective-permute-done.35 = bf16[2,32,2048]{2,1,0:T(8,128)(2,1)S(1)} collective-permute-done((bf16[2,32,2048]{2,1,0:T(8,128)(2,1)S(1)}, bf16[2,32,2048]{2,1,0:T(8,128)(2,1)S(1)}, u32[]{:S(2)}, u32[]{:S(2)}) %collective-permute-start.35) | collective-permute-done | bytes 262176 | tf_op jit(solution)/shard_map/ppermute | solution.py:364
  203.1 2.8 %collective-permute-done.36.refs_3_ = bf16[4,32,2048]{2,1,0:T(8,128)(2,1)S(1)} collective-permute-done((bf16[4,32,2048]{2,1,0:T(8,128)(2,1)S(1)}, bf16[4,32,2048]{2,1,0:T(8,128)(2,1)S(1)}, u32[]{:S(2)}, u32[]{:S(2)}) %collective-permute-start.36) | collective-permute-done | bytes 524320 | tf_op jit(solution)/shard_map/ppermute | solution.py:364
  205.9 1.9 collective-permute-start.39
  207.9 0.8 collective-permute-start.37
  208.7 0.7 collective-permute-start.38
  209.4 2.2 copy-done
  211.6 1.9 project.3.refs_3_
  213.5 1.7 collective-permute-done.39.refs_1_
  215.2 2.4 %project.4.refs_3_ = f32[4,4,32,512]{3,2,1,0:T(8,128)S(1)} custom-call(s32[11]{0:T(128)S(1)} %concatenate.15.info, bf16[4,32,2048]{2,1,0:T(8,128)(2,1)S(1)} %pad_maximum_fusion.1.refs_0_, bf16[4,32,2048]{2,1,0:T(8,128)(2,1)} %collective-permute-done.39.refs_1_, bf16[4096,512]{1,0:T(8,128)(2,1)S(1)} %copy-done.1, f32[4,4,32,512]{3,2,1,0:T(8,128)S(1)} %project.3.refs_3_), custom_call_target="tpu_custom_call" | custom-call | flops 536870912 | bytes 3145728 | tf_op jit(solution)/shard_map/project/pallas_call | solution.py:341
  217.7 5.0 %collective-permute-done.37.refs_0_ = bf16[4,32,2048]{2,1,0:T(8,128)(2,1)S(1)} collective-permute-done((bf16[4,32,2048]{2,1,0:T(8,128)(2,1)S(1)}, bf16[4,32,2048]{2,1,0:T(8,128)(2,1)S(1)}, u32[]{:S(2)}, u32[]{:S(2)}) %collective-permute-start.37) | collective-permute-done | bytes 524320 | tf_op jit(solution)/shard_map/ppermute | solution.py:364
  222.7 2.4 %project.5 = bf16[4,4,32,512]{3,2,1,0:T(8,128)(2,1)S(1)} custom-call(s32[11]{0:T(128)S(1)} %concatenate.15.info, bf16[4,32,2048]{2,1,0:T(8,128)(2,1)S(1)} %collective-permute-done.37.refs_0_, bf16[4,32,2048]{2,1,0:T(8,128)(2,1)} %collective-permute-done.38.refs_1_, bf16[4096,512]{1,0:T(8,128)(2,1)S(1)} %copy-done.1, f32[4,4,32,512]{3,2,1,0:T(8,128)S(1)} %project.4.refs_3_), custom_call_target="tpu_custom_call" | custom-call | flops 536870912 | bytes 3145728 | tf_op jit(solution)/shard_map/project/pallas_call | solution.py:341
  225.2 1.5 collective-permute-done.40
  226.7 0.8 add_convert_fusion
  (64 shorter events, 1.3 us)
Async XLA Ops:
  0.9 6.7 %collective-permute-start = (bf16[32,1024]{1,0:T(8,128)(2,1)S(1)}, bf16[32,1024]{1,0:T(8,128)(2,1)S(1)}, u32[]{:S(2)}, u32[]{:S(2)}) collective-permute-start(bf16[32,1024]{1,0:T(8,128)(2,1)S(1)} %get-tuple-element.68), channel_id=1, source_target_pairs={{0,8},{2,10},{4,12},{6,14},{8,0},{10,2},{12,4},{14,6},{16,24},{18,... | collective-permute-start | bytes 196616 | tf_op jit(solution)/shard_map/ppermute | solution.py:364
  3.9 8.0 %collective-permute-start.2 = (bf16[32,1024]{1,0:T(8,128)(2,1)S(1)}, bf16[32,1024]{1,0:T(8,128)(2,1)S(1)}, u32[]{:S(2)}, u32[]{:S(2)}) collective-permute-start(bf16[32,1024]{1,0:T(8,128)(2,1)S(1)} %get-tuple-element.68), channel_id=1, source_target_pairs={{0,16},{2,18},{4,20},{6,22},{8,24},{10,26},{12,28},{14,30},{16,0},... | collective-permute-start | bytes 196616 | tf_op jit(solution)/shard_map/ppermute | solution.py:364
  6.5 6.8 %collective-permute-start.3 = (bf16[32,1024]{1,0:T(8,128)(2,1)S(1)}, bf16[32,1024]{1,0:T(8,128)(2,1)S(1)}, u32[]{:S(2)}, u32[]{:S(2)}) collective-permute-start(bf16[32,1024]{1,0:T(8,128)(2,1)S(1)} %get-tuple-element.68), channel_id=1, source_target_pairs={{0,24},{2,26},{4,28},{6,30},{8,16},{10,18},{12,20},{14,22},{16,8},... | collective-permute-start | bytes 196616 | tf_op jit(solution)/shard_map/ppermute | solution.py:364
  7.5 11.4 %collective-permute-start.1 = (bf16[32,3072]{1,0:T(8,128)(2,1)S(1)}, bf16[32,3072]{1,0:T(8,128)(2,1)S(1)}, u32[]{:S(2)}, u32[]{:S(2)}) collective-permute-start(bf16[32,3072]{1,0:T(8,128)(2,1)S(1)} %slice.6), channel_id=1, source_target_pairs={{0,8},{2,10},{4,12},{6,14},{8,0},{10,2},{12,4},{14,6},{16,24},{18,... | collective-permute-start | bytes 589832 | tf_op jit(solution)/shard_map/ppermute | solution.py:364
  8.5 20.4 %collective-permute-start.7 = (bf16[32,3072]{1,0:T(8,128)(2,1)S(1)}, bf16[32,3072]{1,0:T(8,128)(2,1)S(1)}, u32[]{:S(2)}, u32[]{:S(2)}) collective-permute-start(bf16[32,3072]{1,0:T(8,128)(2,1)S(1)} %slice.6), channel_id=1, source_target_pairs={{0,16},{2,18},{4,20},{6,22},{8,24},{10,26},{12,28},{14,30},{16,0},... | collective-permute-start | bytes 589832 | tf_op jit(solution)/shard_map/ppermute | solution.py:364
  12.0 17.0 %collective-permute-start.8 = (bf16[32,3072]{1,0:T(8,128)(2,1)S(1)}, bf16[32,3072]{1,0:T(8,128)(2,1)S(1)}, u32[]{:S(2)}, u32[]{:S(2)}) collective-permute-start(bf16[32,3072]{1,0:T(8,128)(2,1)S(1)} %slice.6), channel_id=1, source_target_pairs={{0,24},{2,26},{4,28},{6,30},{8,16},{10,18},{12,20},{14,22},{16,8},... | collective-permute-start | bytes 589832 | tf_op jit(solution)/shard_map/ppermute | solution.py:364
  13.3 16.8 %collective-permute-start.4 = (bf16[4,32,1024]{2,1,0:T(8,128)(2,1)S(1)}, bf16[4,32,1024]{2,1,0:T(8,128)(2,1)S(1)}, u32[]{:S(2)}, u32[]{:S(2)}) collective-permute-start(bf16[4,32,1024]{2,1,0:T(8,128)(2,1)S(1)} %pad_maximum_fusion.2.refs_0_), channel_id=1, source_target_pairs={{0,2},{2,0},{4,6},{6,4},{8,10},{10,8},{12,14},{14,12},{16,18},{18,... | collective-permute-start | bytes 786440 | tf_op jit(solution)/shard_map/ppermute | solution.py:364
  14.9 17.7 %collective-permute-start.5 = (bf16[4,32,1024]{2,1,0:T(8,128)(2,1)S(1)}, bf16[4,32,1024]{2,1,0:T(8,128)(2,1)S(1)}, u32[]{:S(2)}, u32[]{:S(2)}) collective-permute-start(bf16[4,32,1024]{2,1,0:T(8,128)(2,1)S(1)} %pad_maximum_fusion.2.refs_0_), channel_id=1, source_target_pairs={{0,4},{2,6},{4,0},{6,2},{8,12},{10,14},{12,8},{14,10},{16,20},{18,... | collective-permute-start | bytes 786440 | tf_op jit(solution)/shard_map/ppermute | solution.py:364
  19.0 13.6 %collective-permute-start.6 = (bf16[4,32,1024]{2,1,0:T(8,128)(2,1)S(1)}, bf16[4,32,1024]{2,1,0:T(8,128)(2,1)S(1)}, u32[]{:S(2)}, u32[]{:S(2)}) collective-permute-start(bf16[4,32,1024]{2,1,0:T(8,128)(2,1)S(1)} %pad_maximum_fusion.2.refs_0_), channel_id=1, source_target_pairs={{0,6},{2,4},{4,2},{6,0},{8,14},{10,12},{12,10},{14,8},{16,22},{18,... | collective-permute-start | bytes 786440 | tf_op jit(solution)/shard_map/ppermute | solution.py:364
  25.0 2.2 copy-start.2
  27.2 5.4 %copy-start.3 = (bf16[4096,512]{1,0:T(8,128)(2,1)S(1)}, bf16[4096,512]{1,0:T(8,128)(2,1)}, u32[]{:S(2)}) copy-start(bf16[4096,512]{1,0:T(8,128)(2,1)} %refs_2_.3) | copy-start | bytes 12582916
  27.2 5.4 %copy-start.4 = (bf16[32,512]{1,0:T(8,128)(2,1)S(1)}, bf16[32,512]{1,0:T(8,128)(2,1)}, u32[]{:S(2)}) copy-start(bf16[32,512]{1,0:T(8,128)(2,1)} %refs_3_.1) | copy-start | bytes 98308
  27.2 5.4 %copy-start.5 = (bf16[32,512]{1,0:T(8,128)(2,1)S(1)}, bf16[32,512]{1,0:T(8,128)(2,1)}, u32[]{:S(2)}) copy-start(bf16[32,512]{1,0:T(8,128)(2,1)} %refs_4_.4) | copy-start | bytes 98308
  29.0 28.5 %collective-permute-start.12 = (bf16[4,32,3072]{2,1,0:T(8,128)(2,1)S(1)}, bf16[4,32,3072]{2,1,0:T(8,128)(2,1)S(1)}, u32[]{:S(2)}, u32[]{:S(2)}) collective-permute-start(bf16[4,32,3072]{2,1,0:T(8,128)(2,1)S(1)} %pad_maximum_fusion.refs_8_.refs_0_), channel_id=1, source_target_pairs={{0,2},{2,0},{4,6},{6,4},{8,10},{10,8},{12,14},{14,12},{16,18},{18,... | collective-permute-start | bytes 2359304 | tf_op jit(solution)/shard_map/ppermute | solution.py:364
  29.6 39.9 %collective-permute-start.13 = (bf16[4,32,3072]{2,1,0:T(8,128)(2,1)S(1)}, bf16[4,32,3072]{2,1,0:T(8,128)(2,1)S(1)}, u32[]{:S(2)}, u32[]{:S(2)}) collective-permute-start(bf16[4,32,3072]{2,1,0:T(8,128)(2,1)S(1)} %pad_maximum_fusion.refs_8_.refs_0_), channel_id=1, source_target_pairs={{0,4},{2,6},{4,0},{6,2},{8,12},{10,14},{12,8},{14,10},{16,20},{18,... | collective-permute-start | bytes 2359304 | tf_op jit(solution)/shard_map/ppermute | solution.py:364
  30.2 39.4 %collective-permute-start.14 = (bf16[4,32,3072]{2,1,0:T(8,128)(2,1)S(1)}, bf16[4,32,3072]{2,1,0:T(8,128)(2,1)S(1)}, u32[]{:S(2)}, u32[]{:S(2)}) collective-permute-start(bf16[4,32,3072]{2,1,0:T(8,128)(2,1)S(1)} %pad_maximum_fusion.refs_8_.refs_0_), channel_id=1, source_target_pairs={{0,6},{2,4},{4,2},{6,0},{8,14},{10,12},{12,10},{14,8},{16,22},{18,... | collective-permute-start | bytes 2359304 | tf_op jit(solution)/shard_map/ppermute | solution.py:364
  52.8 40.9 %collective-permute-start.10 = (bf16[4,32,1152]{2,1,0:T(8,128)(2,1)S(1)}, bf16[4,32,1152]{2,1,0:T(8,128)(2,1)S(1)}, u32[]{:S(2)}, u32[]{:S(2)}) collective-permute-start(bf16[4,32,1152]{2,1,0:T(8,128)(2,1)S(1)} %get-tuple-element.42), channel_id=1, source_target_pairs={{0,4},{2,6},{4,0},{6,2},{8,12},{10,14},{12,8},{14,10},{16,20},{18,... | collective-permute-start | bytes 884744 | tf_op jit(solution)/shard_map/ppermute | solution.py:364
  57.5 58.1 %collective-permute-start.11 = (bf16[4,32,1152]{2,1,0:T(8,128)(2,1)S(1)}, bf16[4,32,1152]{2,1,0:T(8,128)(2,1)S(1)}, u32[]{:S(2)}, u32[]{:S(2)}) collective-permute-start(bf16[4,32,1152]{2,1,0:T(8,128)(2,1)S(1)} %get-tuple-element.43), channel_id=1, source_target_pairs={{0,6},{2,4},{4,2},{6,0},{8,14},{10,12},{12,10},{14,8},{16,22},{18,... | collective-permute-start | bytes 884744 | tf_op jit(solution)/shard_map/ppermute | solution.py:364
  57.5 58.2 %collective-permute-start.9 = (bf16[4,32,1152]{2,1,0:T(8,128)(2,1)S(1)}, bf16[4,32,1152]{2,1,0:T(8,128)(2,1)S(1)}, u32[]{:S(2)}, u32[]{:S(2)}) collective-permute-start(bf16[4,32,1152]{2,1,0:T(8,128)(2,1)S(1)} %get-tuple-element.41), channel_id=1, source_target_pairs={{0,2},{2,0},{4,6},{6,4},{8,10},{10,8},{12,14},{14,12},{16,18},{18,... | collective-permute-start | bytes 884744 | tf_op jit(solution)/shard_map/ppermute | solution.py:364
  89.7 25.9 %collective-permute-start.15 = (bf16[4,32,1152]{2,1,0:T(8,128)(2,1)S(1)}, bf16[4,32,1152]{2,1,0:T(8,128)(2,1)S(1)}, u32[]{:S(2)}, u32[]{:S(2)}) collective-permute-start(bf16[4,32,1152]{2,1,0:T(8,128)(2,1)S(1)} %get-tuple-element.45), channel_id=1, source_target_pairs={{0,2},{2,0},{4,6},{6,4},{8,10},{10,8},{12,14},{14,12},{16,18},{18,... | collective-permute-start | bytes 884744 | tf_op jit(solution)/shard_map/ppermute | solution.py:364
  93.7 22.0 %collective-permute-start.16 = (bf16[4,32,1152]{2,1,0:T(8,128)(2,1)S(1)}, bf16[4,32,1152]{2,1,0:T(8,128)(2,1)S(1)}, u32[]{:S(2)}, u32[]{:S(2)}) collective-permute-start(bf16[4,32,1152]{2,1,0:T(8,128)(2,1)S(1)} %get-tuple-element.46), channel_id=1, source_target_pairs={{0,4},{2,6},{4,0},{6,2},{8,12},{10,14},{12,8},{14,10},{16,20},{18,... | collective-permute-start | bytes 884744 | tf_op jit(solution)/shard_map/ppermute | solution.py:364
  93.7 22.0 %collective-permute-start.17 = (bf16[4,32,1152]{2,1,0:T(8,128)(2,1)S(1)}, bf16[4,32,1152]{2,1,0:T(8,128)(2,1)S(1)}, u32[]{:S(2)}, u32[]{:S(2)}) collective-permute-start(bf16[4,32,1152]{2,1,0:T(8,128)(2,1)S(1)} %get-tuple-element.47), channel_id=1, source_target_pairs={{0,6},{2,4},{4,2},{6,0},{8,14},{10,12},{12,10},{14,8},{16,22},{18,... | collective-permute-start | bytes 884744 | tf_op jit(solution)/shard_map/ppermute | solution.py:364
  117.4 13.5 %collective-permute-start.18 = (bf16[32,2304]{1,0:T(8,128)(2,1)S(1)}, bf16[32,2304]{1,0:T(8,128)(2,1)S(1)}, u32[]{:S(2)}, u32[]{:S(2)}) collective-permute-start(bf16[32,2304]{1,0:T(8,128)(2,1)S(1)} %get-tuple-element.50), channel_id=1, source_target_pairs={{0,8},{2,10},{4,12},{6,14},{8,0},{10,2},{12,4},{14,6},{16,24},{18,... | collective-permute-start | bytes 442376 | tf_op jit(solution)/shard_map/ppermute | solution.py:364
  127.4 26.4 %collective-permute-start.22 = (bf16[4,32,1152]{2,1,0:T(8,128)(2,1)S(1)}, bf16[4,32,1152]{2,1,0:T(8,128)(2,1)S(1)}, u32[]{:S(2)}, u32[]{:S(2)}) collective-permute-start(bf16[4,32,1152]{2,1,0:T(8,128)(2,1)S(1)} %get-tuple-element.54), channel_id=1, source_target_pairs={{0,2},{2,0},{4,6},{6,4},{8,10},{10,8},{12,14},{14,12},{16,18},{18,... | collective-permute-start | bytes 884744 | tf_op jit(solution)/shard_map/ppermute | solution.py:364
  127.4 27.8 %collective-permute-start.23 = (bf16[4,32,1152]{2,1,0:T(8,128)(2,1)S(1)}, bf16[4,32,1152]{2,1,0:T(8,128)(2,1)S(1)}, u32[]{:S(2)}, u32[]{:S(2)}) collective-permute-start(bf16[4,32,1152]{2,1,0:T(8,128)(2,1)S(1)} %get-tuple-element.55), channel_id=1, source_target_pairs={{0,4},{2,6},{4,0},{6,2},{8,12},{10,14},{12,8},{14,10},{16,20},{18,... | collective-permute-start | bytes 884744 | tf_op jit(solution)/shard_map/ppermute | solution.py:364
  127.4 29.3 %collective-permute-start.24 = (bf16[4,32,1152]{2,1,0:T(8,128)(2,1)S(1)}, bf16[4,32,1152]{2,1,0:T(8,128)(2,1)S(1)}, u32[]{:S(2)}, u32[]{:S(2)}) collective-permute-start(bf16[4,32,1152]{2,1,0:T(8,128)(2,1)S(1)} %get-tuple-element.56), channel_id=1, source_target_pairs={{0,6},{2,4},{4,2},{6,0},{8,14},{10,12},{12,10},{14,8},{16,22},{18,... | collective-permute-start | bytes 884744 | tf_op jit(solution)/shard_map/ppermute | solution.py:364
  130.8 19.1 %collective-permute-start.19 = (bf16[32,2304]{1,0:T(8,128)(2,1)S(1)}, bf16[32,2304]{1,0:T(8,128)(2,1)S(1)}, u32[]{:S(2)}, u32[]{:S(2)}) collective-permute-start(bf16[32,2304]{1,0:T(8,128)(2,1)S(1)} %get-tuple-element.51), channel_id=1, source_target_pairs={{0,16},{2,18},{4,20},{6,22},{8,24},{10,26},{12,28},{14,30},{16,0},... | collective-permute-start | bytes 442376 | tf_op jit(solution)/shard_map/ppermute | solution.py:364
  130.9 19.2 %collective-permute-start.20 = (bf16[32,2304]{1,0:T(8,128)(2,1)S(1)}, bf16[32,2304]{1,0:T(8,128)(2,1)S(1)}, u32[]{:S(2)}, u32[]{:S(2)}) collective-permute-start(bf16[32,2304]{1,0:T(8,128)(2,1)S(1)} %get-tuple-element.52), channel_id=1, source_target_pairs={{0,24},{2,26},{4,28},{6,30},{8,16},{10,18},{12,20},{14,22},{16,8},... | collective-permute-start | bytes 442376 | tf_op jit(solution)/shard_map/ppermute | solution.py:364
  149.9 13.2 %collective-permute-start.25 = (bf16[4,32,1152]{2,1,0:T(8,128)(2,1)S(1)}, bf16[4,32,1152]{2,1,0:T(8,128)(2,1)S(1)}, u32[]{:S(2)}, u32[]{:S(2)}) collective-permute-start(bf16[4,32,1152]{2,1,0:T(8,128)(2,1)S(1)} %get-tuple-element.53.refs_4_), channel_id=1, source_target_pairs={{0,2},{2,0},{4,6},{6,4},{8,10},{10,8},{12,14},{14,12},{16,18},{18,... | collective-permute-start | bytes 884744 | tf_op jit(solution)/shard_map/ppermute | solution.py:364
  150.1 13.1 %collective-permute-start.26 = (bf16[4,32,1152]{2,1,0:T(8,128)(2,1)S(1)}, bf16[4,32,1152]{2,1,0:T(8,128)(2,1)S(1)}, u32[]{:S(2)}, u32[]{:S(2)}) collective-permute-start(bf16[4,32,1152]{2,1,0:T(8,128)(2,1)S(1)} %get-tuple-element.57), channel_id=1, source_target_pairs={{0,4},{2,6},{4,0},{6,2},{8,12},{10,14},{12,8},{14,10},{16,20},{18,... | collective-permute-start | bytes 884744 | tf_op jit(solution)/shard_map/ppermute | solution.py:364
  153.7 9.4 %collective-permute-start.27 = (bf16[4,32,1152]{2,1,0:T(8,128)(2,1)S(1)}, bf16[4,32,1152]{2,1,0:T(8,128)(2,1)S(1)}, u32[]{:S(2)}, u32[]{:S(2)}) collective-permute-start(bf16[4,32,1152]{2,1,0:T(8,128)(2,1)S(1)} %get-tuple-element.58), channel_id=1, source_target_pairs={{0,6},{2,4},{4,2},{6,0},{8,14},{10,12},{12,10},{14,8},{16,22},{18,... | collective-permute-start | bytes 884744 | tf_op jit(solution)/shard_map/ppermute | solution.py:364
  155.2 7.9 %collective-permute-start.21 = (bf16[1,32,2048]{2,1,0:T(8,128)(2,1)S(1)}, bf16[1,32,2048]{2,1,0:T(8,128)(2,1)S(1)}, u32[]{:S(2)}, u32[]{:S(2)}) collective-permute-start(bf16[1,32,2048]{2,1,0:T(8,128)(2,1)S(1)} %bitcast.20), channel_id=1, source_target_pairs={{0,16},{2,18},{4,20},{6,22},{8,24},{10,26},{12,28},{14,30},{16,0},... | collective-permute-start | bytes 393224 | tf_op jit(solution)/shard_map/ppermute | solution.py:364
  163.1 10.6 %collective-permute-start.28 = (bf16[2,32,2048]{2,1,0:T(8,128)(2,1)S(1)}, bf16[2,32,2048]{2,1,0:T(8,128)(2,1)S(1)}, u32[]{:S(2)}, u32[]{:S(2)}) collective-permute-start(bf16[2,32,2048]{2,1,0:T(8,128)(2,1)S(1)} %pad_maximum_fusion.3.refs_9_), channel_id=1, source_target_pairs={{0,8},{2,10},{4,12},{6,14},{8,0},{10,2},{12,4},{14,6},{16,24},{18,... | collective-permute-start | bytes 786440 | tf_op jit(solution)/shard_map/ppermute | solution.py:364
  173.7 14.9 %collective-permute-start.32 = (bf16[4,32,2048]{2,1,0:T(8,128)(2,1)S(1)}, bf16[4,32,2048]{2,1,0:T(8,128)(2,1)S(1)}, u32[]{:S(2)}, u32[]{:S(2)}) collective-permute-start(bf16[4,32,2048]{2,1,0:T(8,128)(2,1)S(1)} %constant_dynamic-update-slice_fusion.refs_0_), channel_id=1, source_target_pairs={{0,2},{2,0},{4,6},{6,4},{8,10},{10,8},{12,14},{14,12},{16,18},{18,... | collective-permute-start | bytes 1572872 | tf_op jit(solution)/shard_map/ppermute | solution.py:364
  173.8 14.8 %collective-permute-start.33 = (bf16[4,32,2048]{2,1,0:T(8,128)(2,1)S(1)}, bf16[4,32,2048]{2,1,0:T(8,128)(2,1)S(1)}, u32[]{:S(2)}, u32[]{:S(2)}) collective-permute-start(bf16[4,32,2048]{2,1,0:T(8,128)(2,1)S(1)} %constant_dynamic-update-slice_fusion.refs_0_), channel_id=1, source_target_pairs={{0,4},{2,6},{4,0},{6,2},{8,12},{10,14},{12,8},{14,10},{16,20},{18,... | collective-permute-start | bytes 1572872 | tf_op jit(solution)/shard_map/ppermute | solution.py:364
  177.7 8.3 %collective-permute-start.29 = (bf16[32,2304]{1,0:T(8,128)(2,1)S(1)}, bf16[32,2304]{1,0:T(8,128)(2,1)S(1)}, u32[]{:S(2)}, u32[]{:S(2)}) collective-permute-start(bf16[32,2304]{1,0:T(8,128)(2,1)S(1)} %get-tuple-element.61), channel_id=1, source_target_pairs={{0,8},{2,10},{4,12},{6,14},{8,0},{10,2},{12,4},{14,6},{16,24},{18,... | collective-permute-start | bytes 442376 | tf_op jit(solution)/shard_map/ppermute | solution.py:364
  178.2 7.8 %collective-permute-start.30 = (bf16[32,2304]{1,0:T(8,128)(2,1)S(1)}, bf16[32,2304]{1,0:T(8,128)(2,1)S(1)}, u32[]{:S(2)}, u32[]{:S(2)}) collective-permute-start(bf16[32,2304]{1,0:T(8,128)(2,1)S(1)} %get-tuple-element.62), channel_id=1, source_target_pairs={{0,16},{2,18},{4,20},{6,22},{8,24},{10,26},{12,28},{14,30},{16,0},... | collective-permute-start | bytes 442376 | tf_op jit(solution)/shard_map/ppermute | solution.py:364
  179.0 9.6 %collective-permute-start.31 = (bf16[32,2304]{1,0:T(8,128)(2,1)S(1)}, bf16[32,2304]{1,0:T(8,128)(2,1)S(1)}, u32[]{:S(2)}, u32[]{:S(2)}) collective-permute-start(bf16[32,2304]{1,0:T(8,128)(2,1)S(1)} %get-tuple-element.63), channel_id=1, source_target_pairs={{0,24},{2,26},{4,28},{6,30},{8,16},{10,18},{12,20},{14,22},{16,8},... | collective-permute-start | bytes 442376 | tf_op jit(solution)/shard_map/ppermute | solution.py:364
  189.3 7.3 %collective-permute-start.34 = (bf16[1,32,2048]{2,1,0:T(8,128)(2,1)S(1)}, bf16[1,32,2048]{2,1,0:T(8,128)(2,1)S(1)}, u32[]{:S(2)}, u32[]{:S(2)}) collective-permute-start(bf16[1,32,2048]{2,1,0:T(8,128)(2,1)S(1)} %bitcast.22), channel_id=1, source_target_pairs={{0,16},{2,18},{4,20},{6,22},{8,24},{10,26},{12,28},{14,30},{16,0},... | collective-permute-start | bytes 393224 | tf_op jit(solution)/shard_map/ppermute | solution.py:364
  190.1 15.9 %collective-permute-start.36 = (bf16[4,32,2048]{2,1,0:T(8,128)(2,1)S(1)}, bf16[4,32,2048]{2,1,0:T(8,128)(2,1)S(1)}, u32[]{:S(2)}, u32[]{:S(2)}) collective-permute-start(bf16[4,32,2048]{2,1,0:T(8,128)(2,1)S(1)} %constant_dynamic-update-slice_fusion.refs_0_), channel_id=1, source_target_pairs={{0,6},{2,4},{4,2},{6,0},{8,14},{10,12},{12,10},{14,8},{16,22},{18,... | collective-permute-start | bytes 1572872 | tf_op jit(solution)/shard_map/ppermute | solution.py:364
  196.6 6.4 %collective-permute-start.35 = (bf16[2,32,2048]{2,1,0:T(8,128)(2,1)S(1)}, bf16[2,32,2048]{2,1,0:T(8,128)(2,1)S(1)}, u32[]{:S(2)}, u32[]{:S(2)}) collective-permute-start(bf16[2,32,2048]{2,1,0:T(8,128)(2,1)S(1)} %pad_maximum_fusion.4), channel_id=1, source_target_pairs={{0,8},{2,10},{4,12},{6,14},{8,0},{10,2},{12,4},{14,6},{16,24},{18,... | collective-permute-start | bytes 786440 | tf_op jit(solution)/shard_map/ppermute | solution.py:364
  205.9 9.3 %collective-permute-start.39 = (bf16[4,32,2048]{2,1,0:T(8,128)(2,1)S(1)}, bf16[4,32,2048]{2,1,0:T(8,128)(2,1)}, u32[]{:S(2)}, u32[]{:S(2)}) collective-permute-start(bf16[4,32,2048]{2,1,0:T(8,128)(2,1)S(1)} %pad_maximum_fusion.1.refs_0_), channel_id=1, source_target_pairs={{0,2},{2,0},{4,6},{6,4},{8,10},{10,8},{12,14},{14,12},{16,18},{18,... | collective-permute-start | bytes 1572872 | tf_op jit(solution)/shard_map/ppermute | solution.py:364
  207.9 14.8 %collective-permute-start.37 = (bf16[4,32,2048]{2,1,0:T(8,128)(2,1)S(1)}, bf16[4,32,2048]{2,1,0:T(8,128)(2,1)S(1)}, u32[]{:S(2)}, u32[]{:S(2)}) collective-permute-start(bf16[4,32,2048]{2,1,0:T(8,128)(2,1)S(1)} %pad_maximum_fusion.1.refs_0_), channel_id=1, source_target_pairs={{0,4},{2,6},{4,0},{6,2},{8,12},{10,14},{12,8},{14,10},{16,20},{18,... | collective-permute-start | bytes 1572872 | tf_op jit(solution)/shard_map/ppermute | solution.py:364
  208.7 14.0 %collective-permute-start.38 = (bf16[4,32,2048]{2,1,0:T(8,128)(2,1)S(1)}, bf16[4,32,2048]{2,1,0:T(8,128)(2,1)}, u32[]{:S(2)}, u32[]{:S(2)}) collective-permute-start(bf16[4,32,2048]{2,1,0:T(8,128)(2,1)S(1)} %pad_maximum_fusion.1.refs_0_), channel_id=1, source_target_pairs={{0,6},{2,4},{4,2},{6,0},{8,14},{10,12},{12,10},{14,8},{16,22},{18,... | collective-permute-start | bytes 1572872 | tf_op jit(solution)/shard_map/ppermute | solution.py:364
  209.4 2.2 copy-start
  211.6 3.6 %copy-start.1 = (bf16[4096,512]{1,0:T(8,128)(2,1)S(1)}, bf16[4096,512]{1,0:T(8,128)(2,1)}, u32[]{:S(2)}) copy-start(bf16[4096,512]{1,0:T(8,128)(2,1)} %refs_2_.5) | copy-start | bytes 12582916
  225.1 1.6 collective-permute-start.40

commit v14 on v13

--- a/solution.py
+++ b/solution.py
@@ -409,8 +409,10 @@
     if heads > 1:
         held, *_ = lax.optimization_barrier((held, keys_t, info))
         stacks = [jnp.stack([held] + early)]
-        pieces = gather_plane(stacks[0])
-        sources += [(pieces, i) for i in range(heads - 1)]
+        sources.append((gather_plane(stacks[0][..., :width]), 0))
+        if heads > 2:
+            pieces = gather_plane(stacks[0][..., width:])
+            sources += [(pieces, i) for i in range(heads - 2)]
 
     size = 2 if heads % 2 == 0 else 1
     attended, merged, rows_of = [], [], []

time: 228 us -> 222 us (0.974)
  starting transfers between devices: 70 us -> 53.6 us
  Pallas kernels: 96.8 us -> 113 us
  waiting for transfers between devices: 49.5 us -> 44.2 us
    ppermute x41 -> x44, starting transfers between devices: 70 us -> 53.6 us  [exchange(): return lax.ppermute(x, axis, [(i, i ^ distance) for i in range(count)])]
    pallas_call x5, Pallas kernels: 83.8 us -> 100 us  [attend_head(): pl.pallas_call(functools.partial(attend_kernel, chosen=chosen, blocks=blo...]
    ppermute x41 -> x44, waiting for transfers between devices: 49.5 us -> 44.2 us  [exchange(): return lax.ppermute(x, axis, [(i, i ^ distance) for i in range(count)])]
  transfers between devices with their start and end apart: 41 -> 44, of which waited for: 12 -> 12; matrix products, arithmetic and copies ran while one was open for 2% -> 2% of each run, Pallas kernels for 40% -> 49%
where the time goes in v14:
time: 222 us
  Pallas kernels  113 us (51%)
  starting transfers between devices  53.6 us (24%)
  waiting for transfers between devices  44.2 us (20%)
  local copies, waits for them, and re-layouts  7.64 us (3%)
  other arithmetic  3.23 us (1%)
    pallas_call x5, Pallas kernels, attend_head(): pl.pallas_call(functools.partial(attend_kernel, chosen=chosen, blocks=blo...  100 us
    ppermute x44, starting transfers between devices, exchange(): return lax.ppermute(x, axis, [(i, i ^ distance) for i in range(count)])  53.6 us
    ppermute x44, waiting for transfers between devices, exchange(): return lax.ppermute(x, axis, [(i, i ^ distance) for i in range(count)])  44.2 us
    pallas_call x3, Pallas kernels, project(): pl.pallas_call(functools.partial(project_kernel, order=order, chosen=chos...  6.71 us
  transfers between devices with their start and end apart: 44, of which 12 were waited for; matrix products, arithmetic and copies ran while one was open for 2% of the time, Pallas kernels for 49%

profile of v14, /device:TPU:0, one launch (start us, length us, event | category | flops | bytes accessed | tf_op | source)
XLA Modules:
  0.0 222.3 jit_solution(17938680451468129482)
XLA Ops:
  0.0 0.8 slice_bitcast_fusion
  0.9 3.1 %collective-permute-start = (bf16[32,1024]{1,0:T(8,128)(2,1)S(1)}, bf16[32,1024]{1,0:T(8,128)(2,1)S(1)}, u32[]{:S(2)}, u32[]{:S(2)}) collective-permute-start(bf16[32,1024]{1,0:T(8,128)(2,1)S(1)} %get-tuple-element.68), channel_id=1, source_target_pairs={{0,8},{2,10},{4,12},{6,14},{8,0},{10,2},{12,4},{14,6},{16,24},{18,... | collective-permute-start | bytes 196616 | tf_op jit(solution)/shard_map/ppermute | solution.py:364
  3.9 2.6 %collective-permute-start.2 = (bf16[32,1024]{1,0:T(8,128)(2,1)S(1)}, bf16[32,1024]{1,0:T(8,128)(2,1)S(1)}, u32[]{:S(2)}, u32[]{:S(2)}) collective-permute-start(bf16[32,1024]{1,0:T(8,128)(2,1)S(1)} %get-tuple-element.68), channel_id=1, source_target_pairs={{0,16},{2,18},{4,20},{6,22},{8,24},{10,26},{12,28},{14,30},{16,0},... | collective-permute-start | bytes 196616 | tf_op jit(solution)/shard_map/ppermute | solution.py:364
  6.5 0.9 slice.12
  7.5 1.0 collective-permute-start.1
  8.5 3.5 %collective-permute-start.7 = (bf16[32,3072]{1,0:T(8,128)(2,1)S(1)}, bf16[32,3072]{1,0:T(8,128)(2,1)S(1)}, u32[]{:S(2)}, u32[]{:S(2)}) collective-permute-start(bf16[32,3072]{1,0:T(8,128)(2,1)S(1)} %slice.12), channel_id=1, source_target_pairs={{0,16},{2,18},{4,20},{6,22},{8,24},{10,26},{12,28},{14,30},{16,0},... | collective-permute-start | bytes 589832 | tf_op jit(solution)/shard_map/ppermute | solution.py:364
  12.0 1.3 collective-permute-done.3
  13.3 1.6 collective-permute-start.4
  14.9 1.5 collective-permute-start.5
  16.4 2.6 %collective-permute-done.1.refs_0_ = bf16[32,3072]{1,0:T(8,128)(2,1)S(1)} collective-permute-done((bf16[32,3072]{1,0:T(8,128)(2,1)S(1)}, bf16[32,3072]{1,0:T(8,128)(2,1)S(1)}, u32[]{:S(2)}, u32[]{:S(2)}) %collective-permute-start.1) | collective-permute-done | bytes 196640 | tf_op jit(solution)/shard_map/ppermute | solution.py:364
  19.0 2.4 %collective-permute-start.6 = (bf16[4,32,1024]{2,1,0:T(8,128)(2,1)S(1)}, bf16[4,32,1024]{2,1,0:T(8,128)(2,1)S(1)}, u32[]{:S(2)}, u32[]{:S(2)}) collective-permute-start(bf16[4,32,1024]{2,1,0:T(8,128)(2,1)S(1)} %pad_maximum_fusion.2.refs_0_), channel_id=1, source_target_pairs={{0,6},{2,4},{4,2},{6,0},{8,14},{10,12},{12,10},{14,8},{16,22},{18,... | collective-permute-start | bytes 786440 | tf_op jit(solution)/shard_map/ppermute | solution.py:364
  21.4 0.8 compare_reduce_fusion
  22.2 0.6 gather_fusion
  22.9 0.8 sort.17
  23.6 0.6 convert_reduce_fusion
  24.3 0.7 concatenate.15.info
  25.0 2.2 copy-done.2
  27.2 1.7 transpose.8.refs_4_.refs_3_.refs_1_
  28.9 0.1 pad_maximum_fusion.refs_8_
  29.0 0.6 collective-permute-start.12
  29.6 0.5 collective-permute-start.13
  30.2 2.5 %collective-permute-start.14 = (bf16[4,32,1024]{2,1,0:T(8,128)(2,1)S(1)}, bf16[4,32,1024]{2,1,0:T(8,128)(2,1)S(1)}, u32[]{:S(2)}, u32[]{:S(2)}) collective-permute-start(bf16[4,32,1024]{2,1,0:T(8,128)(2,1)S(1)} %slice.18.refs_0_), channel_id=1, source_target_pairs={{0,6},{2,4},{4,2},{6,0},{8,14},{10,12},{12,10},{14,8},{16,22},{18,... | collective-permute-start | bytes 786440 | tf_op jit(solution)/shard_map/ppermute | solution.py:364
  32.7 0.5 collective-permute-start.18
  33.2 0.5 collective-permute-start.19
  33.7 24.3 %attend.5 = (bf16[4,32,1152]{2,1,0:T(8,128)(2,1)S(1)}, bf16[4,32,1152]{2,1,0:T(8,128)(2,1)S(1)}, bf16[4,32,1152]{2,1,0:T(8,128)(2,1)S(1)}, bf16[4,32,1152]{2,1,0:T(8,128)(2,1)S(1)}) custom-call(s32[11]{0:T(128)S(1)} %concatenate.15.info, bf16[4,32,1024]{2,1,0:T(8,128)(2,1)S(1)} %pad_maximum_fusion.2.refs_0_, ...), custom_call_target="tpu_custom_call" | custom-call | flops 17179869184 | bytes 4194304 | tf_op jit(solution)/shard_map/attend/pallas_call | solution.py:177
  58.2 2.9 %collective-permute-start.11 = (bf16[4,32,1152]{2,1,0:T(8,128)(2,1)S(1)}, bf16[4,32,1152]{2,1,0:T(8,128)(2,1)S(1)}, u32[]{:S(2)}, u32[]{:S(2)}) collective-permute-start(bf16[4,32,1152]{2,1,0:T(8,128)(2,1)S(1)} %get-tuple-element.43), channel_id=1, source_target_pairs={{0,6},{2,4},{4,2},{6,0},{8,14},{10,12},{12,10},{14,8},{16,22},{18,... | collective-permute-start | bytes 884744 | tf_op jit(solution)/shard_map/ppermute | solution.py:364
  61.1 24.3 %attend.6 = (bf16[4,32,1152]{2,1,0:T(8,128)(2,1)S(1)}, bf16[4,32,1152]{2,1,0:T(8,128)(2,1)S(1)}, bf16[4,32,1152]{2,1,0:T(8,128)(2,1)S(1)}, bf16[4,32,1152]{2,1,0:T(8,128)(2,1)S(1)}) custom-call(s32[11]{0:T(128)S(1)} %concatenate.15.info, bf16[4,32,1024]{2,1,0:T(8,128)(2,1)S(1)} %slice.18.refs_0_, bf16[4,32,1024]{2,1,0:T(8,128)(2,1)S(1)} %collective-permute-done.12.refs_1_, ...), custom_call_target="tpu_custom_call" | custom-call | flops 17179869184 | bytes 4194304 | tf_op jit(solution)/shard_map/attend/pallas_call | solution.py:177
  85.5 2.0 collective-permute-start.15
  87.5 1.5 collective-permute-start.17
  89.1 24.5 %attend.7 = (bf16[4,32,1152]{2,1,0:T(8,128)(2,1)S(1)}, bf16[4,32,1152]{2,1,0:T(8,128)(2,1)S(1)}, bf16[4,32,1152]{2,1,0:T(8,128)(2,1)S(1)}, bf16[4,32,1152]{2,1,0:T(8,128)(2,1)S(1)}) custom-call(s32[11]{0:T(128)S(1)} %concatenate.15.info, bf16[4,32,2048]{2,1,0:T(8,128)(2,1)S(1)} %slice.19.refs_0_, ...), custom_call_target="tpu_custom_call" | custom-call | flops 17179869184 | bytes 4194304 | tf_op jit(solution)/shard_map/attend/pallas_call | solution.py:177
  113.6 1.7 merge.2
  115.5 3.4 %collective-permute-start.27 = (bf16[4,32,1152]{2,1,0:T(8,128)(2,1)S(1)}, bf16[4,32,1152]{2,1,0:T(8,128)(2,1)S(1)}, u32[]{:S(2)}, u32[]{:S(2)}) collective-permute-start(bf16[4,32,1152]{2,1,0:T(8,128)(2,1)S(1)} %get-tuple-element.56), channel_id=1, source_target_pairs={{0,6},{2,4},{4,2},{6,0},{8,14},{10,12},{12,10},{14,8},{16,22},{18,... | collective-permute-start | bytes 884744 | tf_op jit(solution)/shard_map/ppermute | solution.py:364
  118.9 4.6 %collective-permute-start.22 = (bf16[32,2304]{1,0:T(8,128)(2,1)S(1)}, bf16[32,2304]{1,0:T(8,128)(2,1)S(1)}, u32[]{:S(2)}, u32[]{:S(2)}) collective-permute-start(bf16[32,2304]{1,0:T(8,128)(2,1)S(1)} %get-tuple-element.51), channel_id=1, source_target_pairs={{0,16},{2,18},{4,20},{6,22},{8,24},{10,26},{12,28},{14,30},{16,0},... | collective-permute-start | bytes 442376 | tf_op jit(solution)/shard_map/ppermute | solution.py:364
  123.5 1.7 collective-permute-start.23
  125.3 19.6 %attend.8 = (bf16[4,32,1152]{2,1,0:T(8,128)(2,1)S(1)}, bf16[4,32,1152]{2,1,0:T(8,128)(2,1)S(1)}, bf16[4,32,1152]{2,1,0:T(8,128)(2,1)S(1)}) custom-call(s32[11]{0:T(128)S(1)} %concatenate.15.info, bf16[4,32,2048]{2,1,0:T(8,128)(2,1)S(1)} %collective-permute-done.18.refs_1_.refs_0_, bf16[4,32,2048]{2,1,0:T(8,128)(2,1)S(1)} %collective-permute-done.19.refs_2_.refs_1_, ...), custom_call_target="tpu_custom_call" | custom-call | flops 12884901888 | bytes 3670016 | tf_op jit(solution)/shard_map/attend/pallas_call | solution.py:177
  145.1 0.6 normalize.2.refs_5_
  145.7 3.5 %collective-permute-start.30 = (bf16[4,32,1152]{2,1,0:T(8,128)(2,1)S(1)}, bf16[4,32,1152]{2,1,0:T(8,128)(2,1)S(1)}, u32[]{:S(2)}, u32[]{:S(2)}) collective-permute-start(bf16[4,32,1152]{2,1,0:T(8,128)(2,1)S(1)} %get-tuple-element.58), channel_id=1, source_target_pairs={{0,6},{2,4},{4,2},{6,0},{8,14},{10,12},{12,10},{14,8},{16,22},{18,... | collective-permute-start | bytes 884744 | tf_op jit(solution)/shard_map/ppermute | solution.py:364
  149.2 1.7 collective-permute-start.24
  150.9 7.5 %attend.9.refs_4_.refs_8_ = bf16[4,32,1152]{2,1,0:T(8,128)(2,1)S(1)} custom-call(s32[11]{0:T(128)S(1)} %concatenate.15.info, bf16[4,32,2048]{2,1,0:T(8,128)(2,1)S(1)} %slice.19.refs_0_, bf16[512,4096]{1,0:T(8,128)(2,1)S(1)} %transpose.8.refs_4_.refs_3_.refs_1_, bf16[4096,512]{1,0:T(8,128)(2,1)S(1)} %copy-done.3, bf16[32,512]{1,0:T(8,128)(2,1)S(1)} %copy-done.4, ...), custom_call_target="tpu_custom_call" | custom-call | flops 4294967296 | bytes 2621440 | tf_op jit(solution)/shard_map/attend/pallas_call | solution.py:177
  158.5 9.5 %collective-permute-done.31 = bf16[2,32,2048]{2,1,0:T(8,128)(2,1)S(1)} collective-permute-done((bf16[2,32,2048]{2,1,0:T(8,128)(2,1)S(1)}, bf16[2,32,2048]{2,1,0:T(8,128)(2,1)S(1)}, u32[]{:S(2)}, u32[]{:S(2)}) %collective-permute-start.31) | collective-permute-done | bytes 262176 | tf_op jit(solution)/shard_map/ppermute | solution.py:364
  168.0 0.3 collective-permute-start.35
  168.4 1.7 merge.3
  170.1 2.1 collective-permute-start.33
  172.2 2.3 %collective-permute-start.34 = (bf16[32,2304]{1,0:T(8,128)(2,1)S(1)}, bf16[32,2304]{1,0:T(8,128)(2,1)S(1)}, u32[]{:S(2)}, u32[]{:S(2)}) collective-permute-start(bf16[32,2304]{1,0:T(8,128)(2,1)S(1)} %get-tuple-element.63), channel_id=1, source_target_pairs={{0,24},{2,26},{4,28},{6,30},{8,16},{10,18},{12,20},{14,22},{16,8},... | collective-permute-start | bytes 442376 | tf_op jit(solution)/shard_map/ppermute | solution.py:364
  174.5 1.2 collective-permute-done.32.refs_1_
  175.7 6.2 %collective-permute-done.33.refs_2_ = bf16[32,2304]{1,0:T(8,128)(2,1)S(1)} collective-permute-done((bf16[32,2304]{1,0:T(8,128)(2,1)S(1)}, bf16[32,2304]{1,0:T(8,128)(2,1)S(1)}, u32[]{:S(2)}, u32[]{:S(2)}) %collective-permute-start.33) | collective-permute-done | bytes 147488 | tf_op jit(solution)/shard_map/ppermute | solution.py:364
  182.0 1.2 collective-permute-done.36.refs_6_.refs_2_
  183.2 0.6 normalize.3
  183.8 0.7 collective-permute-start.37
  184.5 2.3 %collective-permute-start.39 = (bf16[4,32,2048]{2,1,0:T(8,128)(2,1)S(1)}, bf16[4,32,2048]{2,1,0:T(8,128)(2,1)S(1)}, u32[]{:S(2)}, u32[]{:S(2)}) collective-permute-start(bf16[4,32,2048]{2,1,0:T(8,128)(2,1)S(1)} %constant_dynamic-update-slice_fusion.refs_0_), channel_id=1, source_target_pairs={{0,6},{2,4},{4,2},{6,0},{8,14},{10,12},{12,10},{14,8},{16,22},{18,... | collective-permute-start | bytes 1572872 | tf_op jit(solution)/shard_map/ppermute | solution.py:364
  186.8 4.4 %collective-permute-done.37 = bf16[1,32,2048]{2,1,0:T(8,128)(2,1)S(1)} collective-permute-done((bf16[1,32,2048]{2,1,0:T(8,128)(2,1)S(1)}, bf16[1,32,2048]{2,1,0:T(8,128)(2,1)S(1)}, u32[]{:S(2)}, u32[]{:S(2)}) %collective-permute-start.37) | collective-permute-done | bytes 131104 | tf_op jit(solution)/shard_map/ppermute | solution.py:364
  191.2 6.4 %collective-permute-done.38 = bf16[2,32,2048]{2,1,0:T(8,128)(2,1)S(1)} collective-permute-done((bf16[2,32,2048]{2,1,0:T(8,128)(2,1)S(1)}, bf16[2,32,2048]{2,1,0:T(8,128)(2,1)S(1)}, u32[]{:S(2)}, u32[]{:S(2)}) %collective-permute-start.38) | collective-permute-done | bytes 262176 | tf_op jit(solution)/shard_map/ppermute | solution.py:364
  197.6 2.7 %collective-permute-done.39.refs_3_ = bf16[4,32,2048]{2,1,0:T(8,128)(2,1)S(1)} collective-permute-done((bf16[4,32,2048]{2,1,0:T(8,128)(2,1)S(1)}, bf16[4,32,2048]{2,1,0:T(8,128)(2,1)S(1)}, u32[]{:S(2)}, u32[]{:S(2)}) %collective-permute-start.39) | collective-permute-done | bytes 524320 | tf_op jit(solution)/shard_map/ppermute | solution.py:364
  200.4 1.4 collective-permute-start.42
  201.7 1.4 collective-permute-start.40
  203.1 0.7 collective-permute-start.41
  203.8 2.2 copy-done
  206.0 1.9 project.3.refs_3_
  207.9 3.4 %collective-permute-done.42.refs_1_ = bf16[4,32,2048]{2,1,0:T(8,128)(2,1)} collective-permute-done((bf16[4,32,2048]{2,1,0:T(8,128)(2,1)S(1)}, bf16[4,32,2048]{2,1,0:T(8,128)(2,1)}, u32[]{:S(2)}, u32[]{:S(2)}) %collective-permute-start.42) | collective-permute-done | bytes 524320 | tf_op jit(solution)/shard_map/ppermute | solution.py:364
  211.4 2.4 %project.4.refs_3_ = f32[4,4,32,512]{3,2,1,0:T(8,128)S(1)} custom-call(s32[11]{0:T(128)S(1)} %concatenate.15.info, bf16[4,32,2048]{2,1,0:T(8,128)(2,1)S(1)} %pad_maximum_fusion.1.refs_0_, bf16[4,32,2048]{2,1,0:T(8,128)(2,1)} %collective-permute-done.42.refs_1_, bf16[4096,512]{1,0:T(8,128)(2,1)S(1)} %copy-done.1, f32[4,4,32,512]{3,2,1,0:T(8,128)S(1)} %project.3.refs_3_), custom_call_target="tpu_custom_call" | custom-call | flops 536870912 | bytes 3145728 | tf_op jit(solution)/shard_map/project/pallas_call | solution.py:341
  213.8 3.7 %collective-permute-done.40.refs_0_ = bf16[4,32,2048]{2,1,0:T(8,128)(2,1)S(1)} collective-permute-done((bf16[4,32,2048]{2,1,0:T(8,128)(2,1)S(1)}, bf16[4,32,2048]{2,1,0:T(8,128)(2,1)S(1)}, u32[]{:S(2)}, u32[]{:S(2)}) %collective-permute-start.40) | collective-permute-done | bytes 524320 | tf_op jit(solution)/shard_map/ppermute | solution.py:364
  217.5 2.4 %project.5 = bf16[4,4,32,512]{3,2,1,0:T(8,128)(2,1)S(1)} custom-call(s32[11]{0:T(128)S(1)} %concatenate.15.info, bf16[4,32,2048]{2,1,0:T(8,128)(2,1)S(1)} %collective-permute-done.40.refs_0_, bf16[4,32,2048]{2,1,0:T(8,128)(2,1)} %collective-permute-done.41.refs_1_, bf16[4096,512]{1,0:T(8,128)(2,1)S(1)} %copy-done.1, f32[4,4,32,512]{3,2,1,0:T(8,128)S(1)} %project.4.refs_3_), custom_call_target="tpu_custom_call" | custom-call | flops 536870912 | bytes 3145728 | tf_op jit(solution)/shard_map/project/pallas_call | solution.py:341
  220.0 1.5 collective-permute-done.43
  221.6 0.8 add_convert_fusion
  (72 shorter events, 1.2 us)
Async XLA Ops:
  0.9 6.7 %collective-permute-start = (bf16[32,1024]{1,0:T(8,128)(2,1)S(1)}, bf16[32,1024]{1,0:T(8,128)(2,1)S(1)}, u32[]{:S(2)}, u32[]{:S(2)}) collective-permute-start(bf16[32,1024]{1,0:T(8,128)(2,1)S(1)} %get-tuple-element.68), channel_id=1, source_target_pairs={{0,8},{2,10},{4,12},{6,14},{8,0},{10,2},{12,4},{14,6},{16,24},{18,... | collective-permute-start | bytes 196616 | tf_op jit(solution)/shard_map/ppermute | solution.py:364
  3.9 8.0 %collective-permute-start.2 = (bf16[32,1024]{1,0:T(8,128)(2,1)S(1)}, bf16[32,1024]{1,0:T(8,128)(2,1)S(1)}, u32[]{:S(2)}, u32[]{:S(2)}) collective-permute-start(bf16[32,1024]{1,0:T(8,128)(2,1)S(1)} %get-tuple-element.68), channel_id=1, source_target_pairs={{0,16},{2,18},{4,20},{6,22},{8,24},{10,26},{12,28},{14,30},{16,0},... | collective-permute-start | bytes 196616 | tf_op jit(solution)/shard_map/ppermute | solution.py:364
  6.5 6.8 %collective-permute-start.3 = (bf16[32,1024]{1,0:T(8,128)(2,1)S(1)}, bf16[32,1024]{1,0:T(8,128)(2,1)S(1)}, u32[]{:S(2)}, u32[]{:S(2)}) collective-permute-start(bf16[32,1024]{1,0:T(8,128)(2,1)S(1)} %get-tuple-element.68), channel_id=1, source_target_pairs={{0,24},{2,26},{4,28},{6,30},{8,16},{10,18},{12,20},{14,22},{16,8},... | collective-permute-start | bytes 196616 | tf_op jit(solution)/shard_map/ppermute | solution.py:364
  7.5 11.4 %collective-permute-start.1 = (bf16[32,3072]{1,0:T(8,128)(2,1)S(1)}, bf16[32,3072]{1,0:T(8,128)(2,1)S(1)}, u32[]{:S(2)}, u32[]{:S(2)}) collective-permute-start(bf16[32,3072]{1,0:T(8,128)(2,1)S(1)} %slice.12), channel_id=1, source_target_pairs={{0,8},{2,10},{4,12},{6,14},{8,0},{10,2},{12,4},{14,6},{16,24},{18,... | collective-permute-start | bytes 589832 | tf_op jit(solution)/shard_map/ppermute | solution.py:364
  8.5 20.4 %collective-permute-start.7 = (bf16[32,3072]{1,0:T(8,128)(2,1)S(1)}, bf16[32,3072]{1,0:T(8,128)(2,1)S(1)}, u32[]{:S(2)}, u32[]{:S(2)}) collective-permute-start(bf16[32,3072]{1,0:T(8,128)(2,1)S(1)} %slice.12), channel_id=1, source_target_pairs={{0,16},{2,18},{4,20},{6,22},{8,24},{10,26},{12,28},{14,30},{16,0},... | collective-permute-start | bytes 589832 | tf_op jit(solution)/shard_map/ppermute | solution.py:364
  12.0 16.9 %collective-permute-start.8 = (bf16[32,3072]{1,0:T(8,128)(2,1)S(1)}, bf16[32,3072]{1,0:T(8,128)(2,1)S(1)}, u32[]{:S(2)}, u32[]{:S(2)}) collective-permute-start(bf16[32,3072]{1,0:T(8,128)(2,1)S(1)} %slice.12), channel_id=1, source_target_pairs={{0,24},{2,26},{4,28},{6,30},{8,16},{10,18},{12,20},{14,22},{16,8},... | collective-permute-start | bytes 589832 | tf_op jit(solution)/shard_map/ppermute | solution.py:364
  13.3 16.8 %collective-permute-start.4 = (bf16[4,32,1024]{2,1,0:T(8,128)(2,1)S(1)}, bf16[4,32,1024]{2,1,0:T(8,128)(2,1)S(1)}, u32[]{:S(2)}, u32[]{:S(2)}) collective-permute-start(bf16[4,32,1024]{2,1,0:T(8,128)(2,1)S(1)} %pad_maximum_fusion.2.refs_0_), channel_id=1, source_target_pairs={{0,2},{2,0},{4,6},{6,4},{8,10},{10,8},{12,14},{14,12},{16,18},{18,... | collective-permute-start | bytes 786440 | tf_op jit(solution)/shard_map/ppermute | solution.py:364
  14.9 17.8 %collective-permute-start.5 = (bf16[4,32,1024]{2,1,0:T(8,128)(2,1)S(1)}, bf16[4,32,1024]{2,1,0:T(8,128)(2,1)S(1)}, u32[]{:S(2)}, u32[]{:S(2)}) collective-permute-start(bf16[4,32,1024]{2,1,0:T(8,128)(2,1)S(1)} %pad_maximum_fusion.2.refs_0_), channel_id=1, source_target_pairs={{0,4},{2,6},{4,0},{6,2},{8,12},{10,14},{12,8},{14,10},{16,20},{18,... | collective-permute-start | bytes 786440 | tf_op jit(solution)/shard_map/ppermute | solution.py:364
  19.0 14.3 %collective-permute-start.6 = (bf16[4,32,1024]{2,1,0:T(8,128)(2,1)S(1)}, bf16[4,32,1024]{2,1,0:T(8,128)(2,1)S(1)}, u32[]{:S(2)}, u32[]{:S(2)}) collective-permute-start(bf16[4,32,1024]{2,1,0:T(8,128)(2,1)S(1)} %pad_maximum_fusion.2.refs_0_), channel_id=1, source_target_pairs={{0,6},{2,4},{4,2},{6,0},{8,14},{10,12},{12,10},{14,8},{16,22},{18,... | collective-permute-start | bytes 786440 | tf_op jit(solution)/shard_map/ppermute | solution.py:364
  25.0 2.2 copy-start.2
  27.1 6.6 %copy-start.3 = (bf16[4096,512]{1,0:T(8,128)(2,1)S(1)}, bf16[4096,512]{1,0:T(8,128)(2,1)}, u32[]{:S(2)}) copy-start(bf16[4096,512]{1,0:T(8,128)(2,1)} %refs_2_.3) | copy-start | bytes 12582916
  27.2 6.6 %copy-start.4 = (bf16[32,512]{1,0:T(8,128)(2,1)S(1)}, bf16[32,512]{1,0:T(8,128)(2,1)}, u32[]{:S(2)}) copy-start(bf16[32,512]{1,0:T(8,128)(2,1)} %refs_3_.1) | copy-start | bytes 98308
  27.2 6.6 %copy-start.5 = (bf16[32,512]{1,0:T(8,128)(2,1)S(1)}, bf16[32,512]{1,0:T(8,128)(2,1)}, u32[]{:S(2)}) copy-start(bf16[32,512]{1,0:T(8,128)(2,1)} %refs_4_.4) | copy-start | bytes 98308
  29.0 29.0 %collective-permute-start.12 = (bf16[4,32,1024]{2,1,0:T(8,128)(2,1)S(1)}, bf16[4,32,1024]{2,1,0:T(8,128)(2,1)S(1)}, u32[]{:S(2)}, u32[]{:S(2)}) collective-permute-start(bf16[4,32,1024]{2,1,0:T(8,128)(2,1)S(1)} %slice.18.refs_0_), channel_id=1, source_target_pairs={{0,2},{2,0},{4,6},{6,4},{8,10},{10,8},{12,14},{14,12},{16,18},{18,... | collective-permute-start | bytes 786440 | tf_op jit(solution)/shard_map/ppermute | solution.py:364
  29.6 28.5 %collective-permute-start.13 = (bf16[4,32,1024]{2,1,0:T(8,128)(2,1)S(1)}, bf16[4,32,1024]{2,1,0:T(8,128)(2,1)S(1)}, u32[]{:S(2)}, u32[]{:S(2)}) collective-permute-start(bf16[4,32,1024]{2,1,0:T(8,128)(2,1)S(1)} %slice.18.refs_0_), channel_id=1, source_target_pairs={{0,4},{2,6},{4,0},{6,2},{8,12},{10,14},{12,8},{14,10},{16,20},{18,... | collective-permute-start | bytes 786440 | tf_op jit(solution)/shard_map/ppermute | solution.py:364
  30.2 28.0 %collective-permute-start.14 = (bf16[4,32,1024]{2,1,0:T(8,128)(2,1)S(1)}, bf16[4,32,1024]{2,1,0:T(8,128)(2,1)S(1)}, u32[]{:S(2)}, u32[]{:S(2)}) collective-permute-start(bf16[4,32,1024]{2,1,0:T(8,128)(2,1)S(1)} %slice.18.refs_0_), channel_id=1, source_target_pairs={{0,6},{2,4},{4,2},{6,0},{8,14},{10,12},{12,10},{14,8},{16,22},{18,... | collective-permute-start | bytes 786440 | tf_op jit(solution)/shard_map/ppermute | solution.py:364
  32.7 52.8 %collective-permute-start.18 = (bf16[4,32,2048]{2,1,0:T(8,128)(2,1)S(1)}, bf16[4,32,2048]{2,1,0:T(8,128)(2,1)S(1)}, u32[]{:S(2)}, u32[]{:S(2)}) collective-permute-start(bf16[4,32,2048]{2,1,0:T(8,128)(2,1)S(1)} %slice.19.refs_0_), channel_id=1, source_target_pairs={{0,2},{2,0},{4,6},{6,4},{8,10},{10,8},{12,14},{14,12},{16,18},{18,... | collective-permute-start | bytes 1572872 | tf_op jit(solution)/shard_map/ppermute | solution.py:364
  33.2 54.3 %collective-permute-start.19 = (bf16[4,32,2048]{2,1,0:T(8,128)(2,1)S(1)}, bf16[4,32,2048]{2,1,0:T(8,128)(2,1)S(1)}, u32[]{:S(2)}, u32[]{:S(2)}) collective-permute-start(bf16[4,32,2048]{2,1,0:T(8,128)(2,1)S(1)} %slice.19.refs_0_), channel_id=1, source_target_pairs={{0,4},{2,6},{4,0},{6,2},{8,12},{10,14},{12,8},{14,10},{16,20},{18,... | collective-permute-start | bytes 1572872 | tf_op jit(solution)/shard_map/ppermute | solution.py:364
  58.0 29.5 %collective-permute-start.20 = (bf16[4,32,2048]{2,1,0:T(8,128)(2,1)S(1)}, bf16[4,32,2048]{2,1,0:T(8,128)(2,1)S(1)}, u32[]{:S(2)}, u32[]{:S(2)}) collective-permute-start(bf16[4,32,2048]{2,1,0:T(8,128)(2,1)S(1)} %slice.19.refs_0_), channel_id=1, source_target_pairs={{0,6},{2,4},{4,2},{6,0},{8,14},{10,12},{12,10},{14,8},{16,22},{18,... | collective-permute-start | bytes 1572872 | tf_op jit(solution)/shard_map/ppermute | solution.py:364
  58.1 27.3 %collective-permute-start.10 = (bf16[4,32,1152]{2,1,0:T(8,128)(2,1)S(1)}, bf16[4,32,1152]{2,1,0:T(8,128)(2,1)S(1)}, u32[]{:S(2)}, u32[]{:S(2)}) collective-permute-start(bf16[4,32,1152]{2,1,0:T(8,128)(2,1)S(1)} %get-tuple-element.42), channel_id=1, source_target_pairs={{0,4},{2,6},{4,0},{6,2},{8,12},{10,14},{12,8},{14,10},{16,20},{18,... | collective-permute-start | bytes 884744 | tf_op jit(solution)/shard_map/ppermute | solution.py:364
  58.2 55.3 %collective-permute-start.11 = (bf16[4,32,1152]{2,1,0:T(8,128)(2,1)S(1)}, bf16[4,32,1152]{2,1,0:T(8,128)(2,1)S(1)}, u32[]{:S(2)}, u32[]{:S(2)}) collective-permute-start(bf16[4,32,1152]{2,1,0:T(8,128)(2,1)S(1)} %get-tuple-element.43), channel_id=1, source_target_pairs={{0,6},{2,4},{4,2},{6,0},{8,14},{10,12},{12,10},{14,8},{16,22},{18,... | collective-permute-start | bytes 884744 | tf_op jit(solution)/shard_map/ppermute | solution.py:364
  85.4 28.2 %collective-permute-start.9 = (bf16[4,32,1152]{2,1,0:T(8,128)(2,1)S(1)}, bf16[4,32,1152]{2,1,0:T(8,128)(2,1)S(1)}, u32[]{:S(2)}, u32[]{:S(2)}) collective-permute-start(bf16[4,32,1152]{2,1,0:T(8,128)(2,1)S(1)} %get-tuple-element.41), channel_id=1, source_target_pairs={{0,2},{2,0},{4,6},{6,4},{8,10},{10,8},{12,14},{14,12},{16,18},{18,... | collective-permute-start | bytes 884744 | tf_op jit(solution)/shard_map/ppermute | solution.py:364
  85.5 28.1 %collective-permute-start.15 = (bf16[4,32,1152]{2,1,0:T(8,128)(2,1)S(1)}, bf16[4,32,1152]{2,1,0:T(8,128)(2,1)S(1)}, u32[]{:S(2)}, u32[]{:S(2)}) collective-permute-start(bf16[4,32,1152]{2,1,0:T(8,128)(2,1)S(1)} %get-tuple-element.45), channel_id=1, source_target_pairs={{0,2},{2,0},{4,6},{6,4},{8,10},{10,8},{12,14},{14,12},{16,18},{18,... | collective-permute-start | bytes 884744 | tf_op jit(solution)/shard_map/ppermute | solution.py:364
  87.5 26.1 %collective-permute-start.16 = (bf16[4,32,1152]{2,1,0:T(8,128)(2,1)S(1)}, bf16[4,32,1152]{2,1,0:T(8,128)(2,1)S(1)}, u32[]{:S(2)}, u32[]{:S(2)}) collective-permute-start(bf16[4,32,1152]{2,1,0:T(8,128)(2,1)S(1)} %get-tuple-element.46), channel_id=1, source_target_pairs={{0,4},{2,6},{4,0},{6,2},{8,12},{10,14},{12,8},{14,10},{16,20},{18,... | collective-permute-start | bytes 884744 | tf_op jit(solution)/shard_map/ppermute | solution.py:364
  87.5 26.1 %collective-permute-start.17 = (bf16[4,32,1152]{2,1,0:T(8,128)(2,1)S(1)}, bf16[4,32,1152]{2,1,0:T(8,128)(2,1)S(1)}, u32[]{:S(2)}, u32[]{:S(2)}) collective-permute-start(bf16[4,32,1152]{2,1,0:T(8,128)(2,1)S(1)} %get-tuple-element.47), channel_id=1, source_target_pairs={{0,6},{2,4},{4,2},{6,0},{8,14},{10,12},{12,10},{14,8},{16,22},{18,... | collective-permute-start | bytes 884744 | tf_op jit(solution)/shard_map/ppermute | solution.py:364
  115.3 8.2 %collective-permute-start.21 = (bf16[32,2304]{1,0:T(8,128)(2,1)S(1)}, bf16[32,2304]{1,0:T(8,128)(2,1)S(1)}, u32[]{:S(2)}, u32[]{:S(2)}) collective-permute-start(bf16[32,2304]{1,0:T(8,128)(2,1)S(1)} %get-tuple-element.50), channel_id=1, source_target_pairs={{0,8},{2,10},{4,12},{6,14},{8,0},{10,2},{12,4},{14,6},{16,24},{18,... | collective-permute-start | bytes 442376 | tf_op jit(solution)/shard_map/ppermute | solution.py:364
  115.4 30.3 %collective-permute-start.25 = (bf16[4,32,1152]{2,1,0:T(8,128)(2,1)S(1)}, bf16[4,32,1152]{2,1,0:T(8,128)(2,1)S(1)}, u32[]{:S(2)}, u32[]{:S(2)}) collective-permute-start(bf16[4,32,1152]{2,1,0:T(8,128)(2,1)S(1)} %get-tuple-element.54), channel_id=1, source_target_pairs={{0,2},{2,0},{4,6},{6,4},{8,10},{10,8},{12,14},{14,12},{16,18},{18,... | collective-permute-start | bytes 884744 | tf_op jit(solution)/shard_map/ppermute | solution.py:364
  115.4 33.7 %collective-permute-start.26 = (bf16[4,32,1152]{2,1,0:T(8,128)(2,1)S(1)}, bf16[4,32,1152]{2,1,0:T(8,128)(2,1)S(1)}, u32[]{:S(2)}, u32[]{:S(2)}) collective-permute-start(bf16[4,32,1152]{2,1,0:T(8,128)(2,1)S(1)} %get-tuple-element.55), channel_id=1, source_target_pairs={{0,4},{2,6},{4,0},{6,2},{8,12},{10,14},{12,8},{14,10},{16,20},{18,... | collective-permute-start | bytes 884744 | tf_op jit(solution)/shard_map/ppermute | solution.py:364
  115.5 35.3 %collective-permute-start.27 = (bf16[4,32,1152]{2,1,0:T(8,128)(2,1)S(1)}, bf16[4,32,1152]{2,1,0:T(8,128)(2,1)S(1)}, u32[]{:S(2)}, u32[]{:S(2)}) collective-permute-start(bf16[4,32,1152]{2,1,0:T(8,128)(2,1)S(1)} %get-tuple-element.56), channel_id=1, source_target_pairs={{0,6},{2,4},{4,2},{6,0},{8,14},{10,12},{12,10},{14,8},{16,22},{18,... | collective-permute-start | bytes 884744 | tf_op jit(solution)/shard_map/ppermute | solution.py:364
  118.9 26.0 %collective-permute-start.22 = (bf16[32,2304]{1,0:T(8,128)(2,1)S(1)}, bf16[32,2304]{1,0:T(8,128)(2,1)S(1)}, u32[]{:S(2)}, u32[]{:S(2)}) collective-permute-start(bf16[32,2304]{1,0:T(8,128)(2,1)S(1)} %get-tuple-element.51), channel_id=1, source_target_pairs={{0,16},{2,18},{4,20},{6,22},{8,24},{10,26},{12,28},{14,30},{16,0},... | collective-permute-start | bytes 442376 | tf_op jit(solution)/shard_map/ppermute | solution.py:364
  123.5 21.4 %collective-permute-start.23 = (bf16[32,2304]{1,0:T(8,128)(2,1)S(1)}, bf16[32,2304]{1,0:T(8,128)(2,1)S(1)}, u32[]{:S(2)}, u32[]{:S(2)}) collective-permute-start(bf16[32,2304]{1,0:T(8,128)(2,1)S(1)} %get-tuple-element.52), channel_id=1, source_target_pairs={{0,24},{2,26},{4,28},{6,30},{8,16},{10,18},{12,20},{14,22},{16,8},... | collective-permute-start | bytes 442376 | tf_op jit(solution)/shard_map/ppermute | solution.py:364
  144.9 13.5 %collective-permute-start.28 = (bf16[4,32,1152]{2,1,0:T(8,128)(2,1)S(1)}, bf16[4,32,1152]{2,1,0:T(8,128)(2,1)S(1)}, u32[]{:S(2)}, u32[]{:S(2)}) collective-permute-start(bf16[4,32,1152]{2,1,0:T(8,128)(2,1)S(1)} %get-tuple-element.53.refs_4_), channel_id=1, source_target_pairs={{0,2},{2,0},{4,6},{6,4},{8,10},{10,8},{12,14},{14,12},{16,18},{18,... | collective-permute-start | bytes 884744 | tf_op jit(solution)/shard_map/ppermute | solution.py:364
  145.0 13.4 %collective-permute-start.29 = (bf16[4,32,1152]{2,1,0:T(8,128)(2,1)S(1)}, bf16[4,32,1152]{2,1,0:T(8,128)(2,1)S(1)}, u32[]{:S(2)}, u32[]{:S(2)}) collective-permute-start(bf16[4,32,1152]{2,1,0:T(8,128)(2,1)S(1)} %get-tuple-element.57), channel_id=1, source_target_pairs={{0,4},{2,6},{4,0},{6,2},{8,12},{10,14},{12,8},{14,10},{16,20},{18,... | collective-permute-start | bytes 884744 | tf_op jit(solution)/shard_map/ppermute | solution.py:364
  145.7 12.7 %collective-permute-start.30 = (bf16[4,32,1152]{2,1,0:T(8,128)(2,1)S(1)}, bf16[4,32,1152]{2,1,0:T(8,128)(2,1)S(1)}, u32[]{:S(2)}, u32[]{:S(2)}) collective-permute-start(bf16[4,32,1152]{2,1,0:T(8,128)(2,1)S(1)} %get-tuple-element.58), channel_id=1, source_target_pairs={{0,6},{2,4},{4,2},{6,0},{8,14},{10,12},{12,10},{14,8},{16,22},{18,... | collective-permute-start | bytes 884744 | tf_op jit(solution)/shard_map/ppermute | solution.py:364
  149.2 9.2 %collective-permute-start.24 = (bf16[1,32,2048]{2,1,0:T(8,128)(2,1)S(1)}, bf16[1,32,2048]{2,1,0:T(8,128)(2,1)S(1)}, u32[]{:S(2)}, u32[]{:S(2)}) collective-permute-start(bf16[1,32,2048]{2,1,0:T(8,128)(2,1)S(1)} %bitcast.20), channel_id=1, source_target_pairs={{0,16},{2,18},{4,20},{6,22},{8,24},{10,26},{12,28},{14,30},{16,0},... | collective-permute-start | bytes 393224 | tf_op jit(solution)/shard_map/ppermute | solution.py:364
  158.4 9.6 %collective-permute-start.31 = (bf16[2,32,2048]{2,1,0:T(8,128)(2,1)S(1)}, bf16[2,32,2048]{2,1,0:T(8,128)(2,1)S(1)}, u32[]{:S(2)}, u32[]{:S(2)}) collective-permute-start(bf16[2,32,2048]{2,1,0:T(8,128)(2,1)S(1)} %pad_maximum_fusion.3.refs_9_), channel_id=1, source_target_pairs={{0,8},{2,10},{4,12},{6,14},{8,0},{10,2},{12,4},{14,6},{16,24},{18,... | collective-permute-start | bytes 786440 | tf_op jit(solution)/shard_map/ppermute | solution.py:364
  168.0 13.9 %collective-permute-start.35 = (bf16[4,32,2048]{2,1,0:T(8,128)(2,1)S(1)}, bf16[4,32,2048]{2,1,0:T(8,128)(2,1)S(1)}, u32[]{:S(2)}, u32[]{:S(2)}) collective-permute-start(bf16[4,32,2048]{2,1,0:T(8,128)(2,1)S(1)} %constant_dynamic-update-slice_fusion.refs_0_), channel_id=1, source_target_pairs={{0,2},{2,0},{4,6},{6,4},{8,10},{10,8},{12,14},{14,12},{16,18},{18,... | collective-permute-start | bytes 1572872 | tf_op jit(solution)/shard_map/ppermute | solution.py:364
  168.4 14.8 %collective-permute-start.36 = (bf16[4,32,2048]{2,1,0:T(8,128)(2,1)S(1)}, bf16[4,32,2048]{2,1,0:T(8,128)(2,1)S(1)}, u32[]{:S(2)}, u32[]{:S(2)}) collective-permute-start(bf16[4,32,2048]{2,1,0:T(8,128)(2,1)S(1)} %constant_dynamic-update-slice_fusion.refs_0_), channel_id=1, source_target_pairs={{0,4},{2,6},{4,0},{6,2},{8,12},{10,14},{12,8},{14,10},{16,20},{18,... | collective-permute-start | bytes 1572872 | tf_op jit(solution)/shard_map/ppermute | solution.py:364
  170.0 5.7 %collective-permute-start.32 = (bf16[32,2304]{1,0:T(8,128)(2,1)S(1)}, bf16[32,2304]{1,0:T(8,128)(2,1)S(1)}, u32[]{:S(2)}, u32[]{:S(2)}) collective-permute-start(bf16[32,2304]{1,0:T(8,128)(2,1)S(1)} %get-tuple-element.61), channel_id=1, source_target_pairs={{0,8},{2,10},{4,12},{6,14},{8,0},{10,2},{12,4},{14,6},{16,24},{18,... | collective-permute-start | bytes 442376 | tf_op jit(solution)/shard_map/ppermute | solution.py:364
  170.1 11.8 %collective-permute-start.33 = (bf16[32,2304]{1,0:T(8,128)(2,1)S(1)}, bf16[32,2304]{1,0:T(8,128)(2,1)S(1)}, u32[]{:S(2)}, u32[]{:S(2)}) collective-permute-start(bf16[32,2304]{1,0:T(8,128)(2,1)S(1)} %get-tuple-element.62), channel_id=1, source_target_pairs={{0,16},{2,18},{4,20},{6,22},{8,24},{10,26},{12,28},{14,30},{16,0},... | collective-permute-start | bytes 442376 | tf_op jit(solution)/shard_map/ppermute | solution.py:364
  172.2 9.7 %collective-permute-start.34 = (bf16[32,2304]{1,0:T(8,128)(2,1)S(1)}, bf16[32,2304]{1,0:T(8,128)(2,1)S(1)}, u32[]{:S(2)}, u32[]{:S(2)}) collective-permute-start(bf16[32,2304]{1,0:T(8,128)(2,1)S(1)} %get-tuple-element.63), channel_id=1, source_target_pairs={{0,24},{2,26},{4,28},{6,30},{8,16},{10,18},{12,20},{14,22},{16,8},... | collective-permute-start | bytes 442376 | tf_op jit(solution)/shard_map/ppermute | solution.py:364
  183.8 7.3 %collective-permute-start.37 = (bf16[1,32,2048]{2,1,0:T(8,128)(2,1)S(1)}, bf16[1,32,2048]{2,1,0:T(8,128)(2,1)S(1)}, u32[]{:S(2)}, u32[]{:S(2)}) collective-permute-start(bf16[1,32,2048]{2,1,0:T(8,128)(2,1)S(1)} %bitcast.22), channel_id=1, source_target_pairs={{0,16},{2,18},{4,20},{6,22},{8,24},{10,26},{12,28},{14,30},{16,0},... | collective-permute-start | bytes 393224 | tf_op jit(solution)/shard_map/ppermute | solution.py:364
  184.5 15.9 %collective-permute-start.39 = (bf16[4,32,2048]{2,1,0:T(8,128)(2,1)S(1)}, bf16[4,32,2048]{2,1,0:T(8,128)(2,1)S(1)}, u32[]{:S(2)}, u32[]{:S(2)}) collective-permute-start(bf16[4,32,2048]{2,1,0:T(8,128)(2,1)S(1)} %constant_dynamic-update-slice_fusion.refs_0_), channel_id=1, source_target_pairs={{0,6},{2,4},{4,2},{6,0},{8,14},{10,12},{12,10},{14,8},{16,22},{18,... | collective-permute-start | bytes 1572872 | tf_op jit(solution)/shard_map/ppermute | solution.py:364
  191.2 6.4 %collective-permute-start.38 = (bf16[2,32,2048]{2,1,0:T(8,128)(2,1)S(1)}, bf16[2,32,2048]{2,1,0:T(8,128)(2,1)S(1)}, u32[]{:S(2)}, u32[]{:S(2)}) collective-permute-start(bf16[2,32,2048]{2,1,0:T(8,128)(2,1)S(1)} %pad_maximum_fusion.4), channel_id=1, source_target_pairs={{0,8},{2,10},{4,12},{6,14},{8,0},{10,2},{12,4},{14,6},{16,24},{18,... | collective-permute-start | bytes 786440 | tf_op jit(solution)/shard_map/ppermute | solution.py:364
  200.4 11.0 %collective-permute-start.42 = (bf16[4,32,2048]{2,1,0:T(8,128)(2,1)S(1)}, bf16[4,32,2048]{2,1,0:T(8,128)(2,1)}, u32[]{:S(2)}, u32[]{:S(2)}) collective-permute-start(bf16[4,32,2048]{2,1,0:T(8,128)(2,1)S(1)} %pad_maximum_fusion.1.refs_0_), channel_id=1, source_target_pairs={{0,2},{2,0},{4,6},{6,4},{8,10},{10,8},{12,14},{14,12},{16,18},{18,... | collective-permute-start | bytes 1572872 | tf_op jit(solution)/shard_map/ppermute | solution.py:364
  201.7 15.8 %collective-permute-start.40 = (bf16[4,32,2048]{2,1,0:T(8,128)(2,1)S(1)}, bf16[4,32,2048]{2,1,0:T(8,128)(2,1)S(1)}, u32[]{:S(2)}, u32[]{:S(2)}) collective-permute-start(bf16[4,32,2048]{2,1,0:T(8,128)(2,1)S(1)} %pad_maximum_fusion.1.refs_0_), channel_id=1, source_target_pairs={{0,4},{2,6},{4,0},{6,2},{8,12},{10,14},{12,8},{14,10},{16,20},{18,... | collective-permute-start | bytes 1572872 | tf_op jit(solution)/shard_map/ppermute | solution.py:364
  203.1 14.4 %collective-permute-start.41 = (bf16[4,32,2048]{2,1,0:T(8,128)(2,1)S(1)}, bf16[4,32,2048]{2,1,0:T(8,128)(2,1)}, u32[]{:S(2)}, u32[]{:S(2)}) collective-permute-start(bf16[4,32,2048]{2,1,0:T(8,128)(2,1)S(1)} %pad_maximum_fusion.1.refs_0_), channel_id=1, source_target_pairs={{0,6},{2,4},{4,2},{6,0},{8,14},{10,12},{12,10},{14,8},{16,22},{18,... | collective-permute-start | bytes 1572872 | tf_op jit(solution)/shard_map/ppermute | solution.py:364
  203.8 2.2 copy-start
  206.0 5.3 %copy-start.1 = (bf16[4096,512]{1,0:T(8,128)(2,1)S(1)}, bf16[4096,512]{1,0:T(8,128)(2,1)}, u32[]{:S(2)}) copy-start(bf16[4096,512]{1,0:T(8,128)(2,1)} %refs_2_.5) | copy-start | bytes 12582916
  220.0 1.6 collective-permute-start.43
